TPU v7x, 32 devices: a whole 2x2x4 slice. The times are simulated.
32 devices in a mesh: seq: 4 (over z), res: 8 (over y, x, core).
Axes of the slice: x: 2, y: 2, z: 4, core: 2. Of those that a mesh axis runs over, the one named last changes fastest.
Arguments:
- alignment_rows: bfloat16 [32, 512, 256], P('seq', 'res'), may hold values from -6 to 6
- pair_entries: bfloat16 [512, 512, 128], P('res', 'seq'), may hold values from -6 to 6
- combined_weight: bfloat16 [256, 1024], replicated, may hold values from -0.375 to 0.375
- output_weight: bfloat16 [256, 256], replicated, may hold values from -0.375 to 0.375
- pair_weight: float32 [128, 8], replicated, may hold values from -9 to 9
- updated_gradient: bfloat16 [32, 512, 256], P('seq', 'res'), may hold values from -6 to 6
Outputs:
- updated: bfloat16 [32, 512, 256], P('seq', 'res')
- alignment_gradient: bfloat16 [32, 512, 256], P('seq', 'res')
- pair_gradient: bfloat16 [512, 512, 128], P('res', 'seq')
- combined_weight_gradient: float32 [256, 1024], replicated
- output_weight_gradient: float32 [256, 256], replicated
- pair_weight_gradient: float32 [128, 8], replicated
All inputs are finite; a program needn't handle non-finite values.
Results may differ from a plain program's by a relative error of at most 0.011.
Values may be sent and summed in bfloat16 or wider, within the bound.
No kernel may reach another device: no remote copies, remote signals or barrier semaphores. Data moves between devices by JAX's collectives and lax.ppermute only.
A program may use at most 128 MiB of HBM per device.

v0:
```python
import math

import jax
import jax.numpy as jnp
from jax import lax
from jax.sharding import PartitionSpec as P

eps_norm = 1e-05


def layer_normalize(values):
    values = values.astype(jnp.float32)
    center = values - jnp.mean(values, axis=-1, keepdims=True)
    broadcast_pair = lax.rsqrt(jnp.mean(center * center, axis=-1, keepdims=True) + eps_norm)
    return (center * broadcast_pair, broadcast_pair)


def layer_norm_backward(normalized_gradient, normalized_rows, broadcast_pair):
    mean_grad = jnp.mean(normalized_gradient, axis=-1, keepdims=True)
    mean_cross = jnp.mean(normalized_gradient * normalized_rows, axis=-1, keepdims=True)
    return broadcast_pair * (normalized_gradient - mean_grad - normalized_rows * mean_cross)


def split_heads(tensor, head_count):
    return tensor.reshape(
        tensor.shape[0], tensor.shape[1], head_count, tensor.shape[2] // head_count
    )


def merge_heads(tensor):
    return tensor.reshape(tensor.shape[0], tensor.shape[1], tensor.shape[2] * tensor.shape[3])


def body(
    alignment_rows, pair_entries, combined_weight, output_weight, pair_weight, updated_gradient
):
    sequence_count, residue_count, alignment_width = alignment_rows.shape
    head_count = pair_weight.shape[1]
    query_width = output_weight.shape[0]
    head_dim = query_width // head_count
    column_count = pair_entries.shape[1]
    token_count = sequence_count * residue_count
    score_scale = 1.0 / math.sqrt(head_dim * sequence_count * lax.axis_size("seq"))
    normalized_rows, broadcast_pair = layer_normalize(alignment_rows)
    normalized_rows_backward = normalized_rows.astype(jnp.bfloat16).reshape(
        token_count, alignment_width
    )
    projected = jnp.dot(
        normalized_rows_backward, combined_weight, preferred_element_type=jnp.float32
    ).reshape(sequence_count, residue_count, 4 * query_width)
    queries = (projected[..., :query_width] * score_scale).astype(jnp.bfloat16)
    key_rows = projected[..., query_width : 2 * query_width].astype(jnp.bfloat16)
    value_rows = projected[..., 2 * query_width : 3 * query_width].astype(jnp.bfloat16)
    gate_open = jax.nn.sigmoid(projected[..., 3 * query_width :])
    all_keys, all_values = (
        lax.all_gather(key_rows, "res", axis=1, tiled=True),
        lax.all_gather(value_rows, "res", axis=1, tiled=True),
    )
    query_heads = split_heads(queries, head_count)
    key_heads = split_heads(all_keys, head_count)
    value_heads = split_heads(all_values, head_count)
    score_terms = jnp.einsum(
        "sihd,sjhd->hij", query_heads, key_heads, preferred_element_type=jnp.float32
    )
    pair_normed, pair_spread = layer_normalize(pair_entries)
    pair_bias = jnp.einsum("ijc,ch->hij", pair_normed, pair_weight, precision=lax.Precision.HIGHEST)
    col_start = lax.axis_index("seq") * column_count
    own_block = lax.dynamic_slice_in_dim(score_terms, col_start, column_count, 2) + pair_bias
    logits = lax.psum(lax.dynamic_update_slice_in_dim(score_terms, own_block, col_start, 2), "seq")
    row_top = jnp.max(logits, axis=-1, keepdims=True)
    lifted = jnp.exp(logits - row_top)
    softmax_out = lifted / jnp.sum(lifted, axis=-1, keepdims=True)
    softmax_low = softmax_out.astype(jnp.bfloat16)
    attended = merge_heads(
        jnp.einsum("hij,sjhd->sihd", softmax_low, value_heads, preferred_element_type=jnp.float32)
    )
    gated_out = (gate_open * attended).astype(jnp.bfloat16)
    flattened_gated = gated_out.reshape(token_count, query_width)
    updated = (
        jnp.dot(flattened_gated, output_weight, preferred_element_type=jnp.float32)
        .astype(jnp.bfloat16)
        .reshape(sequence_count, residue_count, alignment_width)
    )
    flattened_gradient = updated_gradient.reshape(token_count, alignment_width)
    grad_gated = jnp.dot(
        flattened_gradient, output_weight.T, preferred_element_type=jnp.float32
    ).reshape(sequence_count, residue_count, query_width)
    out_local = jnp.dot(flattened_gated.T, flattened_gradient, preferred_element_type=jnp.float32)
    grad_attended = (grad_gated * gate_open).astype(jnp.bfloat16)
    grad_gate_logit = grad_gated * attended * gate_open * (1.0 - gate_open)
    attended_grad_heads = split_heads(grad_attended, head_count)
    grad_terms = jnp.einsum(
        "sihd,sjhd->hij", attended_grad_heads, value_heads, preferred_element_type=jnp.float32
    )
    grad_probs = lax.psum(grad_terms, "seq")
    row_dot = jnp.sum(softmax_out * grad_probs, axis=-1, keepdims=True)
    grad_logits = softmax_out * (grad_probs - row_dot)
    grad_logits_b = grad_logits.astype(jnp.bfloat16)
    logit_share = lax.dynamic_slice_in_dim(grad_logits, col_start, column_count, 2)
    grad_query_heads = (
        jnp.einsum("hij,sjhd->sihd", grad_logits_b, key_heads, preferred_element_type=jnp.float32)
        * score_scale
    )
    key_part = jnp.einsum(
        "hij,sihd->jshd", grad_logits_b, query_heads, preferred_element_type=jnp.float32
    )
    value_part = jnp.einsum(
        "hij,sihd->jshd", softmax_low, attended_grad_heads, preferred_element_type=jnp.float32
    )
    summed = lax.psum_scatter(
        jnp.concatenate([merge_heads(key_part), merge_heads(value_part)], axis=-1),
        "res",
        scatter_dimension=0,
        tiled=True,
    )
    key_value_grads = jnp.transpose(summed, (1, 0, 2))
    projected_gradient = jnp.concatenate(
        [merge_heads(grad_query_heads), key_value_grads, grad_gate_logit], axis=-1
    )
    projected_gradient = projected_gradient.astype(jnp.bfloat16).reshape(
        token_count, 4 * query_width
    )
    qkvg_local = jnp.dot(
        normalized_rows_backward.T, projected_gradient, preferred_element_type=jnp.float32
    )
    normalized_gradient = jnp.dot(
        projected_gradient, combined_weight.T, preferred_element_type=jnp.float32
    ).reshape(sequence_count, residue_count, alignment_width)
    alignment_gradient = layer_norm_backward(
        normalized_gradient, normalized_rows, broadcast_pair
    ).astype(jnp.bfloat16)
    pair_w_local = jnp.einsum(
        "ijc,hij->ch", pair_normed, logit_share, precision=lax.Precision.HIGHEST
    )
    grad_pair_normed = jnp.einsum(
        "hij,ch->ijc", logit_share, pair_weight, precision=lax.Precision.HIGHEST
    )
    pair_gradient = layer_norm_backward(grad_pair_normed, pair_normed, pair_spread).astype(
        jnp.bfloat16
    )
    combined_weight_gradient, output_weight_gradient, pair_weight_gradient = lax.psum(
        (qkvg_local, out_local, pair_w_local), ("seq", "res")
    )
    return (
        updated,
        alignment_gradient,
        pair_gradient,
        combined_weight_gradient,
        output_weight_gradient,
        pair_weight_gradient,
    )


def solution(mesh):
    return jax.shard_map(
        body,
        mesh=mesh,
        in_specs=(
            P("seq", "res", None),
            P("res", "seq", None),
            P(),
            P(),
            P(),
            P("seq", "res", None),
        ),
        out_specs=(
            P("seq", "res", None),
            P("seq", "res", None),
            P("res", "seq", None),
            P(),
            P(),
            P(),
        ),
        check_vma=False,
    )
```

profile of v0, /device:TPU:0, one launch (start us, length us, event | category | flops | bytes accessed | tf_op | source)
XLA Modules:
  0.0 429.4 jit_solution(7661405447828870654)
XLA Ops:
  9.6 2.8 fusion.82
  14.1 3.2 copy.33
  22.4 2.6 fusion.7
  25.1 19.0 %all-gather.5.cloned.1.call-done = bf16[8,512,256]{2,1,0:T(8,128)(2,1)} async-done(((bf16[8,64,256]{2,1,0:T(8,128)(2,1)}), bf16[8,512,256]{2,1,0:T(8,128)(2,1)}) %all-gather.5.cloned.1.call-update) | async-done | bytes 2097168 | tf_op jit(solution)/shard_map/all_gather | solution.py:56
  44.1 3.9 copy.30
  48.0 3.1 convolution_bitcast_fusion.3
  51.1 23.4 %all-gather.3.cloned.1.call-done = bf16[8,512,256]{2,1,0:T(8,128)(2,1)} async-done(((bf16[8,64,256]{2,1,0:T(8,128)(2,1)}), bf16[8,512,256]{2,1,0:T(8,128)(2,1)}) %all-gather.3.cloned.1.call-update) | async-done | bytes 2097168 | tf_op jit(solution)/shard_map/all_gather | solution.py:57
  74.5 3.9 copy.28
  78.4 3.3 convolution_bitcast_fusion.2
  83.6 87.0 %all-reduce.7.cloned.1.call-done = (f32[8,64,512]{2,1,0:T(8,128)}, f32[8,64,512]{2,1,0:T(8,128)}) async-done(((f32[8,64,512]{2,1,0:T(8,128)}, f32[8,64,512]{2,1,0:T(8,128)}), (f32[8,64,512]{2,1,0:T(8,128)}, f32[8,64,512]{2,1,0:T(8,128)})) %all-reduce.7.cloned.1.call-update) | async-done | bytes 2097168 | tf_op jit(solution)/shard_map/psum | solution.py:69
  170.6 2.7 fusion.83
  173.3 4.6 %convolution_bitcast_fusion = f32[512,8,8,32]{0,3,1,2:T(8,128)} fusion(bf16[8,64,8,32]{1,3,2,0:T(8,128)(2,1)} %bitcast.91, f32[8,64]{1,0:T(8,128)S(1)} %get-tuple-element.35, f32[8,64,512]{2,1,0:T(8,128)} %get-tuple-element.24), kind=kOutput, calls=%fused_computation.15 | convolution fusion | flops 135005184 | bytes 5507072 | tf_op jit(solution)/shard_map/hij,sihd->jshd/dot_general | solution.py:107
  180.0 2.8 subtract_multiply_fusion
  185.2 5.3 %copy.49 = f32[512,8,256]{2,0,1:T(8,128)} copy(f32[512,8,256]{0,2,1:T(8,128)} %bitcast.81) | data formatting | bytes 8388608 | tf_op jit(solution)/shard_map/reshape | solution.py:31
  194.8 5.4 %copy.48 = f32[512,8,256]{2,0,1:T(8,128)} copy(f32[512,8,256]{0,2,1:T(8,128)} %bitcast.82) | data formatting | bytes 8388608 | tf_op jit(solution)/shard_map/reshape | solution.py:31
  200.2 7.9 %pad_maximum_fusion = f32[512,8,512]{2,0,1:T(8,128)} fusion(f32[512,8,256]{2,0,1:T(8,128)} %copy.49, f32[512,8,256]{2,0,1:T(8,128)} %copy.48), kind=kLoop, calls=%fused_computation.1 | loop fusion | flops 2097152 | bytes 16777216 | tf_op jit(solution)/shard_map/concatenate | solution.py:111
  208.4 4.1 fusion.23
  216.7 3.1 fusion.33
  223.6 4.2 fusion.79
  227.9 2.8 fusion.12
  230.7 4.1 copy.55
  234.8 4.6 %fusion.36 = f32[128,8]{0,1:T(8,128)S(1)} fusion(bf16[64,128,128]{1,2,0:T(8,128)(2,1)S(1)} %copy.33, f32[64,128]{1,0:T(8,128)S(1)} %add_rsqrt_fusion, f32[64,128]{1,0:T(8,128)S(1)} %broadcast_multiply_fusion.2, f32[8,64,128]{2,1,0:T(8,128)} %copy-done.3), kind=kOutput, calls=%fused_computation.36 | convolution fusion | flops 103809024 | bytes 2428928 | tf_op jit(solution)/shard_map/ijc,hij->ch/dot_general | solution.py:132
  239.3 39.7 %psum.39 = f32[128,8]{0,1:T(8,128)} all-reduce(f32[128,8]{0,1:T(8,128)S(1)} %fusion.36), channel_id=1, replica_groups=mesh['seq'=4,'res'=8] {'seq','res'}, use_global_device_ids=true, to_apply=%region_16.0 | all-reduce | flops 1024 | bytes 8192 | tf_op jit(solution)/shard_map/psum | solution.py:141
  288.9 130.1 %all-reduce.5.cloned.1.call-done = (f32[256,1024]{1,0:T(8,128)}, f32[256,256]{1,0:T(8,128)}) async-done(((f32[256,1024]{1,0:T(8,128)}, f32[256,256]{1,0:T(8,128)}), (f32[256,1024]{1,0:T(8,128)}, f32[256,256]{1,0:T(8,128)})) %all-reduce.5.cloned.1.call-update) | async-done | bytes 1310736 | tf_op jit(solution)/shard_map/psum | solution.py:141
  (58 shorter events, 41.7 us)
Async XLA Ops:
  7.2 2.5 copy-start
  7.2 36.9 %all-gather.5.cloned.1.call-start = ((), (), s32[]{:S(2)}) async-start(), calls=%async_computation.2 | async-start | bytes 2359296 | tf_op jit(solution)/shard_map/all_gather | solution.py:56
  9.6 7.8 %copy-start.5 = (bf16[256,256]{1,0:T(8,128)(2,1)S(1)}, bf16[256,256]{1,0:T(8,128)(2,1)}, u32[]{:S(2)}) copy-start(bf16[256,256]{1,0:T(8,128)(2,1)} %param.9) | copy-start | bytes 393220
  13.3 61.2 %all-gather.3.cloned.1.call-start = ((), (), s32[]{:S(2)}) async-start(), calls=%async_computation.1 | async-start | bytes 2359296 | tf_op jit(solution)/shard_map/all_gather | solution.py:57
  14.1 156.5 %all-reduce.7.cloned.1.call-start = ((), (), s32[]{:S(2)}) async-start(), calls=%async_computation.5 | async-start | bytes 4194304 | tf_op jit(solution)/shard_map/psum | solution.py:69
  17.4 5.0 %copy-start.6 = (f32[128,8]{0,1:T(8,128)S(1)}, f32[128,8]{0,1:T(8,128)}, u32[]{:S(2)}) copy-start(f32[128,8]{0,1:T(8,128)} %param.10) | copy-start | bytes 12292
  83.4 200.9 %reduce-scatter.2.cloned.1.call-start = ((), (), s32[]{:S(2)}) async-start(), calls=%async_computation.3 | async-start | bytes 9437184 | tf_op jit(solution)/shard_map/reduce_scatter | solution.py:110
  178.0 4.7 %copy-start.1 = (f32[512,8,8,32]{0,3,1,2:T(8,128)S(1)}, f32[512,8,8,32]{0,3,1,2:T(8,128)}, u32[]{:S(2)}) copy-start(f32[512,8,8,32]{0,3,1,2:T(8,128)} %convolution_bitcast_fusion) | copy-start | bytes 12582916
  208.1 210.8 %all-reduce.5.cloned.1.call-start = ((), (), s32[]{:S(2)}) async-start(), calls=%async_computation.4 | async-start | bytes 2621440 | tf_op jit(solution)/shard_map/psum | solution.py:141
  223.6 7.1 %copy-start.3 = (f32[8,64,128]{2,1,0:T(8,128)}, f32[8,64,128]{2,1,0:T(8,128)S(1)}, u32[]{:S(2)}) copy-start(f32[8,64,128]{2,1,0:T(8,128)S(1)} %constant_dynamic-slice_fusion) | copy-start | bytes 786436
  234.8 50.8 %copy-start.2 = (bf16[8,64,256]{2,1,0:T(8,128)(2,1)S(1)}, bf16[8,64,256]{2,1,0:T(8,128)(2,1)}, u32[]{:S(2)}) copy-start(bf16[8,64,256]{2,1,0:T(8,128)(2,1)} %param.6) | copy-start | bytes 786436
  239.3 46.2 %copy-start.4 = (bf16[8,64,256]{2,1,0:T(8,128)(2,1)S(1)}, bf16[8,64,256]{2,1,0:T(8,128)(2,1)}, u32[]{:S(2)}) copy-start(bf16[8,64,256]{2,1,0:T(8,128)(2,1)} %copy.51) | copy-start | bytes 786436
Sparse Core Ops, SparseCore 0:
  13.5 30.5 all-gather.4
  46.6 27.8 all-gather.2
  83.5 87.0 all-reduce.6
  208.2 71.3 reduce-scatter.1
  287.3 131.5 all-reduce.4
where the time goes:
time: 431 us; the launch traced here: 429 us
  waiting for transfers between devices  260 us (60%)
  local copies, waits for them, and re-layouts  44.8 us (10%)
  matrix products  42.7 us (10%)
  blocking collectives  39.7 us (9%)
  other arithmetic  27.3 us (6%)
  between operations  14 us (3%)
    psum x1, waiting for transfers between devices, body(): lax.psum((qkvg_local, out_local, pair_w_local), ('seq', 'res'))  130 us
    psum x1, waiting for transfers between devices, body(): lax.psum(lax.dynamic_update_slice_in_dim(score_terms, own_block, col_star...  87 us
    psum x1, blocking collectives, body(): lax.psum((qkvg_local, out_local, pair_w_local), ('seq', 'res'))  39.7 us
    all_gather x1, waiting for transfers between devices, body(): lax.all_gather(value_rows, 'res', axis=1, tiled=True)  23.4 us
    all_gather x1, waiting for transfers between devices, body(): lax.all_gather(key_rows, 'res', axis=1, tiled=True)  19 us
    reshape x3, local copies, waits for them, and re-layouts, merge_heads(): tensor.reshape(tensor.shape[0], tensor.shape[1], tensor.shape[2] * tensor...  12.5 us
    unnamed x18, local copies, waits for them, and re-layouts  11.3 us
  transfers between devices with their start and end apart: 5, of which 4 were waited for; matrix products, arithmetic and copies ran while one was open for 13% of the time, Pallas kernels for 0%

commit v1 on v0

--- a/solution.py
+++ b/solution.py
@@ -31,7 +31,7 @@
     return tensor.reshape(tensor.shape[0], tensor.shape[1], tensor.shape[2] * tensor.shape[3])
 
 
-def body(
+def gathered_body(
     alignment_rows, pair_entries, combined_weight, output_weight, pair_weight, updated_gradient
 ):
     sequence_count, residue_count, alignment_width = alignment_rows.shape
@@ -151,6 +151,186 @@
     )
 
 
+def shifted_rows(mine, axis_size, axis_name):
+    return [
+        lax.ppermute(mine[k], axis_name, [(a, (a + k) % axis_size) for a in range(axis_size)])
+        for k in range(1, axis_size)
+    ]
+
+
+def gathered(mine, seq_size, seq_index):
+    rows = jnp.zeros((seq_size,) + mine.shape, mine.dtype)
+    rows = lax.dynamic_update_index_in_dim(rows, mine, seq_index, 0)
+    for k, t in enumerate(shifted_rows([mine] * seq_size, seq_size, "seq"), 1):
+        rows = lax.dynamic_update_index_in_dim(rows, t, (seq_index - k) % seq_size, 0)
+    return rows
+
+
+def head_body(
+    alignment_rows, pair_entries, combined_weight, output_weight, pair_weight, updated_gradient
+):
+    sequence_count, residue_count, alignment_width = alignment_rows.shape
+    head_count = pair_weight.shape[1]
+    query_width = output_weight.shape[0]
+    head_dim = query_width // head_count
+    column_count = pair_entries.shape[1]
+    pair_width = pair_entries.shape[2]
+    token_count = sequence_count * residue_count
+    seq_size = lax.axis_size("seq")
+    seq_index = lax.axis_index("seq")
+    residue_total = residue_count * head_count
+    row_count = residue_total // seq_size
+    depth = sequence_count * head_dim
+    score_scale = 1.0 / math.sqrt(head_dim * sequence_count * seq_size)
+
+    normalized_rows, broadcast_pair = layer_normalize(alignment_rows)
+    normed_b = normalized_rows.astype(jnp.bfloat16).reshape(token_count, alignment_width)
+    projected = jnp.dot(normed_b, combined_weight, preferred_element_type=jnp.float32)
+    gate_open = jax.nn.sigmoid(projected[:, 3 * query_width :])
+    flattened_gradient = updated_gradient.reshape(token_count, alignment_width)
+    grad_gated = jnp.dot(flattened_gradient, output_weight.T, preferred_element_type=jnp.float32)
+
+    def to_heads(tensors):
+        blocks = jnp.stack(
+            [
+                t.astype(jnp.bfloat16).reshape(sequence_count, residue_count, head_count, head_dim)
+                for t in tensors
+            ]
+        )
+        blocks = jnp.transpose(blocks, (3, 0, 2, 1, 4)).reshape(
+            head_count, len(tensors), residue_count, depth
+        )
+        blocks = lax.all_to_all(blocks, "res", 0, 0, tiled=True)
+        return [
+            blocks[:, t].reshape(residue_total, depth) for t in range(len(tensors))
+        ]
+
+    queries, keys = to_heads(
+        [projected[:, :query_width] * score_scale, projected[:, query_width : 2 * query_width]]
+    )
+    values, grad_attended = to_heads(
+        [projected[:, 2 * query_width : 3 * query_width], grad_gated * gate_open]
+    )
+
+    pair_normed, pair_spread = layer_normalize(pair_entries)
+    pair_bias = jnp.einsum("ijc,ch->hij", pair_normed, pair_weight, precision=lax.Precision.HIGHEST)
+    bias = lax.all_to_all(pair_bias, "res", 0, 0, tiled=True).reshape(residue_total, column_count)
+
+    col_start = seq_index * column_count
+    score_terms = jnp.dot(queries, keys.T, preferred_element_type=jnp.float32)
+    own_block = lax.dynamic_slice_in_dim(score_terms, col_start, column_count, 1) + bias
+    score_terms = lax.dynamic_update_slice_in_dim(score_terms, own_block, col_start, 1)
+    grad_terms = jnp.dot(grad_attended, values.T, preferred_element_type=jnp.float32)
+
+    def row_sums(terms, kind):
+        blocks = terms.reshape(seq_size, row_count, residue_total)
+        pick = lambda k: lax.dynamic_index_in_dim(blocks, (seq_index + k) % seq_size, 0, False)
+        sent = [pick(k).astype(kind) for k in range(seq_size)]
+        return sum((t.astype(jnp.float32) for t in shifted_rows(sent, seq_size, "seq")), pick(0))
+
+    def all_rows(mine):
+        return gathered(mine, seq_size, seq_index).reshape(residue_total, residue_total)
+
+    logits = row_sums(score_terms, jnp.float32)
+    grad_probs = row_sums(grad_terms, jnp.bfloat16)
+    row_top = jnp.max(logits, axis=-1, keepdims=True)
+    lifted = jnp.exp(logits - row_top)
+    softmax_out = lifted / jnp.sum(lifted, axis=-1, keepdims=True)
+    probs = all_rows(softmax_out.astype(jnp.bfloat16))
+    row_dot = jnp.sum(softmax_out * grad_probs, axis=-1, keepdims=True)
+    grad_logits = all_rows((softmax_out * (grad_probs - row_dot)).astype(jnp.bfloat16))
+
+    def to_residues(tensors):
+        blocks = jnp.stack(
+            [t.astype(jnp.bfloat16).reshape(head_count, residue_count, depth) for t in tensors], 1
+        )
+        blocks = lax.all_to_all(blocks, "res", 0, 0, tiled=True)
+        blocks = blocks.reshape(
+            head_count, len(tensors), residue_count, sequence_count, head_dim
+        )
+        blocks = jnp.transpose(blocks, (1, 3, 2, 0, 4))
+        return [blocks[t].reshape(token_count, query_width) for t in range(len(tensors))]
+
+    attended, grad_values = to_residues(
+        [
+            jnp.dot(probs, values, preferred_element_type=jnp.float32),
+            jnp.dot(probs.T, grad_attended, preferred_element_type=jnp.float32),
+        ]
+    )
+    grad_queries, grad_keys = to_residues(
+        [
+            jnp.dot(grad_logits, keys, preferred_element_type=jnp.float32) * score_scale,
+            jnp.dot(grad_logits.T, queries, preferred_element_type=jnp.float32),
+        ]
+    )
+    logit_share = lax.dynamic_slice_in_dim(grad_logits, col_start, column_count, 1).reshape(
+        head_count, residue_count, column_count
+    )
+    logit_share = lax.all_to_all(logit_share, "res", 0, 0, tiled=True).astype(jnp.float32)
+
+    attended = attended.astype(jnp.float32)
+    gated_out = (gate_open * attended).astype(jnp.bfloat16)
+    updated = jnp.dot(gated_out, output_weight, preferred_element_type=jnp.float32).astype(
+        jnp.bfloat16
+    )
+    out_local = jnp.dot(gated_out.T, flattened_gradient, preferred_element_type=jnp.float32)
+    grad_gate_logit = grad_gated * attended * gate_open * (1.0 - gate_open)
+    projected_gradient = jnp.concatenate(
+        [grad_queries, grad_keys, grad_values, grad_gate_logit.astype(jnp.bfloat16)], axis=-1
+    )
+    qkvg_local = jnp.dot(normed_b.T, projected_gradient, preferred_element_type=jnp.float32)
+    normalized_gradient = jnp.dot(
+        projected_gradient, combined_weight.T, preferred_element_type=jnp.float32
+    ).reshape(alignment_rows.shape)
+    alignment_gradient = layer_norm_backward(
+        normalized_gradient, normalized_rows, broadcast_pair
+    ).astype(jnp.bfloat16)
+    pair_w_local = jnp.einsum(
+        "ijc,hij->hc", pair_normed, logit_share, precision=lax.Precision.HIGHEST
+    )
+
+    weight_rows = alignment_width // head_count
+    parts = jnp.concatenate(
+        [
+            qkvg_local.reshape(head_count, weight_rows, 4 * query_width),
+            out_local.reshape(head_count, weight_rows, alignment_width),
+            jnp.pad(pair_w_local[:, None, :], ((0, 0), (0, weight_rows - 1), (0, 0))),
+        ],
+        axis=-1,
+    ).astype(jnp.bfloat16)
+    part = jnp.sum(lax.all_to_all(parts, "res", 0, 0, tiled=True).astype(jnp.float32), axis=0)
+    sent = part.astype(jnp.bfloat16)
+    part = jnp.sum(gathered(sent, seq_size, seq_index).astype(jnp.float32), axis=0)
+    whole = lax.all_gather(part.astype(jnp.bfloat16), "res", axis=0).astype(jnp.float32)
+    wide = 4 * query_width + alignment_width
+    combined_weight_gradient = whole[:, :, : 4 * query_width].reshape(combined_weight.shape)
+    output_weight_gradient = whole[:, :, 4 * query_width : wide].reshape(output_weight.shape)
+    pair_weight_gradient = whole[:, 0, wide:].T
+
+    grad_pair_normed = jnp.einsum(
+        "hij,ch->ijc", logit_share, pair_weight, precision=lax.Precision.HIGHEST
+    )
+    pair_gradient = layer_norm_backward(grad_pair_normed, pair_normed, pair_spread).astype(
+        jnp.bfloat16
+    )
+    return (
+        updated.reshape(alignment_rows.shape),
+        alignment_gradient,
+        pair_gradient,
+        combined_weight_gradient,
+        output_weight_gradient,
+        pair_weight_gradient,
+    )
+
+
+def body(alignment_rows, pair_entries, combined_weight, output_weight, pair_weight, updated_gradient):
+    one_head = pair_weight.shape[1] == lax.axis_size("res")
+    chosen = head_body if one_head else gathered_body
+    return chosen(
+        alignment_rows, pair_entries, combined_weight, output_weight, pair_weight, updated_gradient
+    )
+
+
 def solution(mesh):
     return jax.shard_map(
         body,

time: 431 us -> 194 us (0.45)
  waiting for transfers between devices: 260 us -> 63.5 us
  starting transfers between devices: 0.6 us -> 53.9 us
  blocking collectives: 39.7 us -> 10.6 us
  matrix products: 42.7 us -> 16.6 us
  local copies, waits for them, and re-layouts: 44.8 us -> 28.2 us
  between operations: 14 us -> 1.35 us
  other arithmetic: 27.3 us -> 18.5 us
    psum x2 -> x0, waiting for transfers between devices: 217 us -> none  [the longest x1 130 us: body(): lax.psum((qkvg_local, out_local, pair_w_local), ('seq', 'res'))]
    all_gather x2 -> x0, waiting for transfers between devices: 42.4 us -> none  [the longest x1 23.4 us: body(): lax.all_gather(value_rows, 'res', axis=1, tiled=True)]
    ppermute x0 -> x15, waiting for transfers between devices: none -> 41.1 us  [shifted_rows(): lax.ppermute(mine[k], axis_name, [(a, (a + k) % axis_size) for a in range...]
    psum x1 -> x0, blocking collectives: 39.7 us -> none  [body(): lax.psum((qkvg_local, out_local, pair_w_local), ('seq', 'res'))]
    all_to_all x0 -> x7, starting transfers between devices: none -> 27.6 us  [the longest x2 8.67 us: to_heads(): blocks = lax.all_to_all(blocks, 'res', 0, 0, tiled=True)]
    ppermute x0 -> x15, starting transfers between devices: none -> 26.3 us  [shifted_rows(): lax.ppermute(mine[k], axis_name, [(a, (a + k) % axis_size) for a in range...]
    dot_general x15, matrix products: 42.7 us -> 16.6 us  [the longest x1 2.62 us: head_body(): jnp.einsum('ijc,ch->hij', pair_normed, pair_weight, precision=lax.Precisi...]
    all_to_all x0 -> x7, waiting for transfers between devices: none -> 22.5 us  [the longest x1 9.41 us: head_body(): lax.all_to_all(parts, 'res', 0, 0, tiled=True).astype(jnp.float32)]
  transfers between devices with their start and end apart: 5 -> 22, of which waited for: 4 -> 15; matrix products, arithmetic and copies ran while one was open for 13% -> 21% of each run, Pallas kernels for 0% -> 0%
where the time goes in v1:
time: 194 us; the launch traced here: 193 us
  waiting for transfers between devices  63.5 us (33%)
  starting transfers between devices  53.9 us (28%)
  local copies, waits for them, and re-layouts  28.2 us (15%)
  other arithmetic  18.5 us (10%)
  matrix products  16.6 us (9%)
  blocking collectives  10.6 us (5%)
    ppermute x15, waiting for transfers between devices, shifted_rows(): lax.ppermute(mine[k], axis_name, [(a, (a + k) % axis_size) for a in range...  41.1 us
    ppermute x15, starting transfers between devices, shifted_rows(): lax.ppermute(mine[k], axis_name, [(a, (a + k) % axis_size) for a in range...  26.3 us
    unnamed x36, local copies, waits for them, and re-layouts  10.9 us
    all_gather x1, blocking collectives, head_body(): lax.all_gather(part.astype(jnp.bfloat16), 'res', axis=0).astype(jnp.float32)  10.6 us
    all_to_all x1, waiting for transfers between devices, head_body(): lax.all_to_all(parts, 'res', 0, 0, tiled=True).astype(jnp.float32)  9.41 us
    all_to_all x2, starting transfers between devices, to_heads(): blocks = lax.all_to_all(blocks, 'res', 0, 0, tiled=True)  8.67 us
    all_to_all x2, starting transfers between devices, to_residues(): blocks = lax.all_to_all(blocks, 'res', 0, 0, tiled=True)  7.64 us
    all_to_all x1, waiting for transfers between devices, head_body(): lax.all_to_all(pair_bias, 'res', 0, 0, tiled=True)  6.11 us
  transfers between devices with their start and end apart: 22, of which 15 were waited for; matrix products, arithmetic and copies ran while one was open for 21% of the time, Pallas kernels for 0%

profile of v1, /device:TPU:0, one launch (start us, length us, event | category | flops | bytes accessed | tf_op | source)
XLA Modules:
  0.0 192.7 jit_solution(4978510799099241014)
XLA Ops:
  9.6 5.2 %all-to-all-start = ((bf16[8,2,64,256]{3,2,1,0:T(8,128)(2,1)}), bf16[8,2,64,256]{3,2,1,0:T(8,128)(2,1)S(1)}, u32[]{:S(2)}, u32[]{:S(2)}) async-start(bf16[8,2,64,256]{3,2,1,0:T(8,128)(2,1)} %copy.130), calls=%async_computation | async-start | bytes 1048576 | tf_op jit(solution)/shard_map/all_to_all | solution.py:203
  17.2 3.2 %copy.133 = bf16[64,128,128]{1,2,0:T(8,128)(2,1)S(1)} copy(bf16[64,128,128]{2,1,0:T(8,128)(2,1)} %param.7) | data formatting | bytes 4194304 | tf_op args[1]
  21.8 2.6 %fusion.19 = f32[8,64,128]{2,0,1:T(8,128)S(1)} fusion(bf16[64,128,128]{1,2,0:T(8,128)(2,1)S(1)} %copy.133, f32[64,128]{1,0:T(8,128)S(1)} %add_rsqrt_fusion, f32[64,128]{1,0:T(8,128)S(1)} %broadcast_multiply_fusion.2, f32[128,8]{0,1:T(8,128)S(1)} %copy-done.16), kind=kOutput, calls=%fused_computation.26 | convolution fusion | flops 103809024 | bytes 2428928 | tf_op jit(solution)/shard_map/ijc,ch->hij/dot_general | solution.py:216
  26.0 4.2 %all-to-all-start.1 = ((f32[8,64,128]{2,1,0:T(8,128)}), f32[8,64,128]{2,1,0:T(8,128)S(1)}, u32[]{:S(2)}, u32[]{:S(2)}) async-start(f32[8,64,128]{2,1,0:T(8,128)} %copy.135), calls=%async_computation.1 | async-start | bytes 524288 | tf_op jit(solution)/shard_map/all_to_all | solution.py:217
  31.0 6.1 %all-to-all-done.1 = f32[8,64,128]{2,1,0:T(8,128)S(1)} async-done(((f32[8,64,128]{2,1,0:T(8,128)}), f32[8,64,128]{2,1,0:T(8,128)S(1)}, u32[]{:S(2)}, u32[]{:S(2)}) %all-to-all-start.1) | async-done | bytes 262176 | tf_op jit(solution)/shard_map/all_to_all | solution.py:217
  37.9 3.5 %all-to-all-start.2 = ((bf16[8,2,64,256]{3,2,1,0:T(8,128)(2,1)}), bf16[8,2,64,256]{3,2,1,0:T(8,128)(2,1)S(1)}, u32[]{:S(2)}, u32[]{:S(2)}) async-start(bf16[8,2,64,256]{3,2,1,0:T(8,128)(2,1)} %copy.140), calls=%async_computation.2 | async-start | bytes 1048576 | tf_op jit(solution)/shard_map/all_to_all | solution.py:203
  47.2 2.6 %collective-permute-start.1 = (f32[128,512]{1,0:T(8,128)}, f32[128,512]{1,0:T(8,128)}, u32[]{:S(2)}, u32[]{:S(2)}) collective-permute-start(f32[128,512]{1,0:T(8,128)} %get-tuple-element.59), channel_id=1, source_target_pairs={{0,16},{8,24},{16,0},{24,8},{1,17},{9,25},{17,1},{25,9},{2,18},{10... | collective-permute-start | bytes 786440 | tf_op jit(solution)/shard_map/ppermute | solution.py:156
  53.1 2.6 %collective-permute-start.7 = (bf16[128,512]{1,0:T(8,128)(2,1)S(1)}, bf16[128,512]{1,0:T(8,128)(2,1)S(1)}, u32[]{:S(2)}, u32[]{:S(2)}) collective-permute-start(bf16[128,512]{1,0:T(8,128)(2,1)S(1)} %get-tuple-element.52), channel_id=1, source_target_pairs={{0,16},{8,24},{16,0},{24,8},{1,17},{9,25},{17,1},{25,9},{2,18},{10... | collective-permute-start | bytes 393224 | tf_op jit(solution)/shard_map/ppermute | solution.py:156
  58.9 9.4 %collective-permute-done.1 = f32[128,512]{1,0:T(8,128)} collective-permute-done((f32[128,512]{1,0:T(8,128)}, f32[128,512]{1,0:T(8,128)}, u32[]{:S(2)}, u32[]{:S(2)}) %collective-permute-start.1) | collective-permute-done | bytes 262176 | tf_op jit(solution)/shard_map/ppermute | solution.py:156
  71.0 10.8 %collective-permute-done.7 = bf16[128,512]{1,0:T(8,128)(2,1)S(1)} collective-permute-done((bf16[128,512]{1,0:T(8,128)(2,1)S(1)}, bf16[128,512]{1,0:T(8,128)(2,1)S(1)}, u32[]{:S(2)}, u32[]{:S(2)}) %collective-permute-start.7) | collective-permute-done | bytes 131104 | tf_op jit(solution)/shard_map/ppermute | solution.py:156
  82.2 3.4 %collective-permute-start.9 = (bf16[128,512]{1,0:T(8,128)(2,1)S(1)}, bf16[128,512]{1,0:T(8,128)(2,1)S(1)}, u32[]{:S(2)}, u32[]{:S(2)}) collective-permute-start(bf16[128,512]{1,0:T(8,128)(2,1)S(1)} %get-tuple-element.39), channel_id=1, source_target_pairs={{0,8},{8,16},{16,24},{24,0},{1,9},{9,17},{17,25},{25,1},{2,10},{10... | collective-permute-start | bytes 393224 | tf_op jit(solution)/shard_map/ppermute | solution.py:156
  92.1 8.1 %collective-permute-done.10 = bf16[128,512]{1,0:T(8,128)(2,1)S(1)} collective-permute-done((bf16[128,512]{1,0:T(8,128)(2,1)S(1)}, bf16[128,512]{1,0:T(8,128)(2,1)S(1)}, u32[]{:S(2)}, u32[]{:S(2)}) %collective-permute-start.10) | collective-permute-done | bytes 131104 | tf_op jit(solution)/shard_map/ppermute | solution.py:156
  101.7 5.1 %collective-permute-done.4 = bf16[128,512]{1,0:T(8,128)(2,1)S(1)} collective-permute-done((bf16[128,512]{1,0:T(8,128)(2,1)S(1)}, bf16[128,512]{1,0:T(8,128)(2,1)S(1)}, u32[]{:S(2)}, u32[]{:S(2)}) %collective-permute-start.4) | collective-permute-done | bytes 131104 | tf_op jit(solution)/shard_map/ppermute | solution.py:156
  108.9 3.5 %all-to-all-start.5 = ((bf16[8,64,128]{2,1,0:T(8,128)(2,1)}), bf16[8,64,128]{2,1,0:T(8,128)(2,1)S(1)}, u32[]{:S(2)}, u32[]{:S(2)}) async-start(bf16[8,64,128]{2,1,0:T(8,128)(2,1)} %bitcast.50), calls=%async_computation.5 | async-start | bytes 262144 | tf_op jit(solution)/shard_map/all_to_all | solution.py:269
  118.0 3.5 %all-to-all-start.4 = ((bf16[8,2,64,256]{3,2,1,0:T(8,128)(2,1)}), bf16[8,2,64,256]{3,2,1,0:T(8,128)(2,1)S(1)}, u32[]{:S(2)}, u32[]{:S(2)}) async-start(bf16[8,2,64,256]{3,2,1,0:T(8,128)(2,1)} %pad_maximum_fusion.2), calls=%async_computation.4 | async-start | bytes 1048576 | tf_op jit(solution)/shard_map/all_to_all | solution.py:247
  124.1 2.7 %fusion.11 = bf16[64,128,128]{1,2,0:T(8,128)(2,1)} fusion(bf16[64,128,128]{1,2,0:T(8,128)(2,1)S(1)} %copy.133, f32[64,128,128]{1,2,0:T(8,128)S(1)} %get-tuple-element.69, f32[64,128]{1,0:T(8,128)S(1)} %get-tuple-element.70, f32[64,128]{1,0:T(8,128)S(1)} %get-tuple-element.71, f32[64,128]{1,0:T(8,128)S(1)} %add_rsqrt_fusion, ...), kind=kLoop, calls=%fused_computation.11 | loop fusion | flops 8388608 | bytes 8519680 | tf_op jit(solution)/shard_map/convert_element_type | solution.py:313
  126.8 4.4 %all-to-all-done.4 = bf16[8,2,64,256]{3,2,1,0:T(8,128)(2,1)S(1)} async-done(((bf16[8,2,64,256]{3,2,1,0:T(8,128)(2,1)}), bf16[8,2,64,256]{3,2,1,0:T(8,128)(2,1)S(1)}, u32[]{:S(2)}, u32[]{:S(2)}) %all-to-all-start.4) | async-done | bytes 524320 | tf_op jit(solution)/shard_map/all_to_all | solution.py:247
  131.2 4.1 %all-to-all-start.3 = ((bf16[8,2,64,256]{3,2,1,0:T(8,128)(2,1)}), bf16[8,2,64,256]{3,2,1,0:T(8,128)(2,1)}, u32[]{:S(2)}, u32[]{:S(2)}) async-start(bf16[8,2,64,256]{3,2,1,0:T(8,128)(2,1)} %pad_maximum_fusion.1), calls=%async_computation.3 | async-start | bytes 1048576 | tf_op jit(solution)/shard_map/all_to_all | solution.py:247
  137.7 4.1 %copy.164 = bf16[64,128,128]{2,1,0:T(8,128)(2,1)} copy(bf16[64,128,128]{1,2,0:T(8,128)(2,1)} %fusion.11) | data formatting | bytes 4194304
  153.8 3.5 %all-to-all-start.6 = ((bf16[8,32,1408]{2,1,0:T(8,128)(2,1)}), bf16[8,32,1408]{2,1,0:T(8,128)(2,1)S(1)}, u32[]{:S(2)}, u32[]{:S(2)}) async-start(bf16[8,32,1408]{2,1,0:T(8,128)(2,1)} %fusion.32), calls=%async_computation.6 | async-start | bytes 1441792 | tf_op jit(solution)/shard_map/all_to_all | solution.py:301
  159.7 9.4 %all-to-all-done.6 = bf16[8,32,1408]{2,1,0:T(8,128)(2,1)S(1)} async-done(((bf16[8,32,1408]{2,1,0:T(8,128)(2,1)}), bf16[8,32,1408]{2,1,0:T(8,128)(2,1)S(1)}, u32[]{:S(2)}, u32[]{:S(2)}) %all-to-all-start.6) | async-done | bytes 720928 | tf_op jit(solution)/shard_map/all_to_all | solution.py:301
  169.3 2.6 %collective-permute-start.12 = (bf16[32,1408]{1,0:T(8,128)(2,1)S(1)}, bf16[32,1408]{1,0:T(8,128)(2,1)S(1)}, u32[]{:S(2)}, u32[]{:S(2)}) collective-permute-start(bf16[32,1408]{1,0:T(8,128)(2,1)S(1)} %reduce_sum.124), channel_id=1, source_target_pairs={{0,8},{8,16},{16,24},{24,0},{1,9},{9,17},{17,25},{25,1},{2,10},{10... | collective-permute-start | bytes 270344 | tf_op jit(solution)/shard_map/ppermute | solution.py:156
  171.9 2.7 %collective-permute-start.13 = (bf16[32,1408]{1,0:T(8,128)(2,1)S(1)}, bf16[32,1408]{1,0:T(8,128)(2,1)S(1)}, u32[]{:S(2)}, u32[]{:S(2)}) collective-permute-start(bf16[32,1408]{1,0:T(8,128)(2,1)S(1)} %reduce_sum.124), channel_id=1, source_target_pairs={{0,16},{8,24},{16,0},{24,8},{1,17},{9,25},{17,1},{25,9},{2,18},{10... | collective-permute-start | bytes 270344 | tf_op jit(solution)/shard_map/ppermute | solution.py:156
  179.7 10.6 %all-gather = bf16[256,1408]{1,0:T(8,128)(2,1)S(1)} all-gather(bf16[32,1408]{1,0:T(8,128)(2,1)S(1)} %reduce_sum.125), channel_id=2, replica_groups=mesh['seq'=4,'res'=8] {'res'}, dimensions={0}, use_global_device_ids=true | all-gather | bytes 811008 | tf_op jit(solution)/shard_map/all_gather | solution.py:304
  (156 shorter events, 73.4 us)
Async XLA Ops:
  9.6 16.5 %all-to-all-start = ((bf16[8,2,64,256]{3,2,1,0:T(8,128)(2,1)}), bf16[8,2,64,256]{3,2,1,0:T(8,128)(2,1)S(1)}, u32[]{:S(2)}, u32[]{:S(2)}) async-start(bf16[8,2,64,256]{3,2,1,0:T(8,128)(2,1)} %copy.130), calls=%async_computation | async-start | bytes 1048576 | tf_op jit(solution)/shard_map/all_to_all | solution.py:203
  26.0 11.1 %all-to-all-start.1 = ((f32[8,64,128]{2,1,0:T(8,128)}), f32[8,64,128]{2,1,0:T(8,128)S(1)}, u32[]{:S(2)}, u32[]{:S(2)}) async-start(f32[8,64,128]{2,1,0:T(8,128)} %copy.135), calls=%async_computation.1 | async-start | bytes 524288 | tf_op jit(solution)/shard_map/all_to_all | solution.py:217
  37.9 13.3 %all-to-all-start.2 = ((bf16[8,2,64,256]{3,2,1,0:T(8,128)(2,1)}), bf16[8,2,64,256]{3,2,1,0:T(8,128)(2,1)S(1)}, u32[]{:S(2)}, u32[]{:S(2)}) async-start(bf16[8,2,64,256]{3,2,1,0:T(8,128)(2,1)} %copy.140), calls=%async_computation.2 | async-start | bytes 1048576 | tf_op jit(solution)/shard_map/all_to_all | solution.py:203
  45.6 11.4 %collective-permute-start = (f32[128,512]{1,0:T(8,128)}, f32[128,512]{1,0:T(8,128)}, u32[]{:S(2)}, u32[]{:S(2)}) collective-permute-start(f32[128,512]{1,0:T(8,128)} %get-tuple-element.57), channel_id=1, source_target_pairs={{0,8},{8,16},{16,24},{24,0},{1,9},{9,17},{17,25},{25,1},{2,10},{10... | collective-permute-start | bytes 786440 | tf_op jit(solution)/shard_map/ppermute | solution.py:156
  47.2 21.1 %collective-permute-start.1 = (f32[128,512]{1,0:T(8,128)}, f32[128,512]{1,0:T(8,128)}, u32[]{:S(2)}, u32[]{:S(2)}) collective-permute-start(f32[128,512]{1,0:T(8,128)} %get-tuple-element.59), channel_id=1, source_target_pairs={{0,16},{8,24},{16,0},{24,8},{1,17},{9,25},{17,1},{25,9},{2,18},{10... | collective-permute-start | bytes 786440 | tf_op jit(solution)/shard_map/ppermute | solution.py:156
  49.8 18.5 %collective-permute-start.2 = (f32[128,512]{1,0:T(8,128)}, f32[128,512]{1,0:T(8,128)}, u32[]{:S(2)}, u32[]{:S(2)}) collective-permute-start(f32[128,512]{1,0:T(8,128)} %get-tuple-element.58), channel_id=1, source_target_pairs={{0,24},{8,0},{16,8},{24,16},{1,25},{9,1},{17,9},{25,17},{2,26},{10... | collective-permute-start | bytes 786440 | tf_op jit(solution)/shard_map/ppermute | solution.py:156
  51.6 19.4 %collective-permute-start.6 = (bf16[128,512]{1,0:T(8,128)(2,1)S(1)}, bf16[128,512]{1,0:T(8,128)(2,1)S(1)}, u32[]{:S(2)}, u32[]{:S(2)}) collective-permute-start(bf16[128,512]{1,0:T(8,128)(2,1)S(1)} %get-tuple-element.50), channel_id=1, source_target_pairs={{0,8},{8,16},{16,24},{24,0},{1,9},{9,17},{17,25},{25,1},{2,10},{10... | collective-permute-start | bytes 393224 | tf_op jit(solution)/shard_map/ppermute | solution.py:156
  53.1 28.6 %collective-permute-start.7 = (bf16[128,512]{1,0:T(8,128)(2,1)S(1)}, bf16[128,512]{1,0:T(8,128)(2,1)S(1)}, u32[]{:S(2)}, u32[]{:S(2)}) collective-permute-start(bf16[128,512]{1,0:T(8,128)(2,1)S(1)} %get-tuple-element.52), channel_id=1, source_target_pairs={{0,16},{8,24},{16,0},{24,8},{1,17},{9,25},{17,1},{25,9},{2,18},{10... | collective-permute-start | bytes 393224 | tf_op jit(solution)/shard_map/ppermute | solution.py:156
  57.0 24.7 %collective-permute-start.8 = (bf16[128,512]{1,0:T(8,128)(2,1)S(1)}, bf16[128,512]{1,0:T(8,128)(2,1)S(1)}, u32[]{:S(2)}, u32[]{:S(2)}) collective-permute-start(bf16[128,512]{1,0:T(8,128)(2,1)S(1)} %get-tuple-element.51), channel_id=1, source_target_pairs={{0,24},{8,0},{16,8},{24,16},{1,25},{9,1},{17,9},{25,17},{2,26},{10... | collective-permute-start | bytes 393224 | tf_op jit(solution)/shard_map/ppermute | solution.py:156
  69.8 30.5 %copy-start.6 = (bf16[8,1,64,256]{3,2,1,0:T(8,128)(2,1)S(1)}, bf16[8,1,64,256]{3,2,1,0:T(8,128)(2,1)}, u32[]{:S(2)}) copy-start(bf16[8,1,64,256]{3,2,1,0:T(8,128)(2,1)} %get-tuple-element.62) | copy-start | bytes 786436
  82.0 18.6 %copy-start.5 = (bf16[8,1,64,256]{3,2,1,0:T(8,128)(2,1)S(1)}, bf16[8,1,64,256]{3,2,1,0:T(8,128)(2,1)}, u32[]{:S(2)}) copy-start(bf16[8,1,64,256]{3,2,1,0:T(8,128)(2,1)} %get-tuple-element.63) | copy-start | bytes 786436
  82.2 8.8 %collective-permute-start.9 = (bf16[128,512]{1,0:T(8,128)(2,1)S(1)}, bf16[128,512]{1,0:T(8,128)(2,1)S(1)}, u32[]{:S(2)}, u32[]{:S(2)}) collective-permute-start(bf16[128,512]{1,0:T(8,128)(2,1)S(1)} %get-tuple-element.39), channel_id=1, source_target_pairs={{0,8},{8,16},{16,24},{24,0},{1,9},{9,17},{17,25},{25,1},{2,10},{10... | collective-permute-start | bytes 393224 | tf_op jit(solution)/shard_map/ppermute | solution.py:156
  85.5 14.7 %collective-permute-start.10 = (bf16[128,512]{1,0:T(8,128)(2,1)S(1)}, bf16[128,512]{1,0:T(8,128)(2,1)S(1)}, u32[]{:S(2)}, u32[]{:S(2)}) collective-permute-start(bf16[128,512]{1,0:T(8,128)(2,1)S(1)} %get-tuple-element.39), channel_id=1, source_target_pairs={{0,16},{8,24},{16,0},{24,8},{1,17},{9,25},{17,1},{25,9},{2,18},{10... | collective-permute-start | bytes 393224 | tf_op jit(solution)/shard_map/ppermute | solution.py:156
  87.1 13.2 %collective-permute-start.11 = (bf16[128,512]{1,0:T(8,128)(2,1)S(1)}, bf16[128,512]{1,0:T(8,128)(2,1)S(1)}, u32[]{:S(2)}, u32[]{:S(2)}) collective-permute-start(bf16[128,512]{1,0:T(8,128)(2,1)S(1)} %get-tuple-element.39), channel_id=1, source_target_pairs={{0,24},{8,0},{16,8},{24,16},{1,25},{9,1},{17,9},{25,17},{2,26},{10... | collective-permute-start | bytes 393224 | tf_op jit(solution)/shard_map/ppermute | solution.py:156
  88.2 13.5 %collective-permute-start.3 = (bf16[128,512]{1,0:T(8,128)(2,1)S(1)}, bf16[128,512]{1,0:T(8,128)(2,1)S(1)}, u32[]{:S(2)}, u32[]{:S(2)}) collective-permute-start(bf16[128,512]{1,0:T(8,128)(2,1)S(1)} %get-tuple-element.41), channel_id=1, source_target_pairs={{0,8},{8,16},{16,24},{24,0},{1,9},{9,17},{17,25},{25,1},{2,10},{10... | collective-permute-start | bytes 393224 | tf_op jit(solution)/shard_map/ppermute | solution.py:156
  89.4 17.5 %collective-permute-start.4 = (bf16[128,512]{1,0:T(8,128)(2,1)S(1)}, bf16[128,512]{1,0:T(8,128)(2,1)S(1)}, u32[]{:S(2)}, u32[]{:S(2)}) collective-permute-start(bf16[128,512]{1,0:T(8,128)(2,1)S(1)} %get-tuple-element.41), channel_id=1, source_target_pairs={{0,16},{8,24},{16,0},{24,8},{1,17},{9,25},{17,1},{25,9},{2,18},{10... | collective-permute-start | bytes 393224 | tf_op jit(solution)/shard_map/ppermute | solution.py:156
  91.0 16.5 %collective-permute-start.5 = (bf16[128,512]{1,0:T(8,128)(2,1)S(1)}, bf16[128,512]{1,0:T(8,128)(2,1)S(1)}, u32[]{:S(2)}, u32[]{:S(2)}) collective-permute-start(bf16[128,512]{1,0:T(8,128)(2,1)S(1)} %get-tuple-element.41), channel_id=1, source_target_pairs={{0,24},{8,0},{16,8},{24,16},{1,25},{9,1},{17,9},{25,17},{2,26},{10... | collective-permute-start | bytes 393224 | tf_op jit(solution)/shard_map/ppermute | solution.py:156
  108.9 9.1 %all-to-all-start.5 = ((bf16[8,64,128]{2,1,0:T(8,128)(2,1)}), bf16[8,64,128]{2,1,0:T(8,128)(2,1)S(1)}, u32[]{:S(2)}, u32[]{:S(2)}) async-start(bf16[8,64,128]{2,1,0:T(8,128)(2,1)} %bitcast.50), calls=%async_computation.5 | async-start | bytes 262144 | tf_op jit(solution)/shard_map/all_to_all | solution.py:269
  118.0 13.2 %all-to-all-start.4 = ((bf16[8,2,64,256]{3,2,1,0:T(8,128)(2,1)}), bf16[8,2,64,256]{3,2,1,0:T(8,128)(2,1)S(1)}, u32[]{:S(2)}, u32[]{:S(2)}) async-start(bf16[8,2,64,256]{3,2,1,0:T(8,128)(2,1)} %pad_maximum_fusion.2), calls=%async_computation.4 | async-start | bytes 1048576 | tf_op jit(solution)/shard_map/all_to_all | solution.py:247
  131.2 13.9 %all-to-all-start.3 = ((bf16[8,2,64,256]{3,2,1,0:T(8,128)(2,1)}), bf16[8,2,64,256]{3,2,1,0:T(8,128)(2,1)}, u32[]{:S(2)}, u32[]{:S(2)}) async-start(bf16[8,2,64,256]{3,2,1,0:T(8,128)(2,1)} %pad_maximum_fusion.1), calls=%async_computation.3 | async-start | bytes 1048576 | tf_op jit(solution)/shard_map/all_to_all | solution.py:247
  153.8 15.4 %all-to-all-start.6 = ((bf16[8,32,1408]{2,1,0:T(8,128)(2,1)}), bf16[8,32,1408]{2,1,0:T(8,128)(2,1)S(1)}, u32[]{:S(2)}, u32[]{:S(2)}) async-start(bf16[8,32,1408]{2,1,0:T(8,128)(2,1)} %fusion.32), calls=%async_computation.6 | async-start | bytes 1441792 | tf_op jit(solution)/shard_map/all_to_all | solution.py:301
  169.3 7.4 %collective-permute-start.12 = (bf16[32,1408]{1,0:T(8,128)(2,1)S(1)}, bf16[32,1408]{1,0:T(8,128)(2,1)S(1)}, u32[]{:S(2)}, u32[]{:S(2)}) collective-permute-start(bf16[32,1408]{1,0:T(8,128)(2,1)S(1)} %reduce_sum.124), channel_id=1, source_target_pairs={{0,8},{8,16},{16,24},{24,0},{1,9},{9,17},{17,25},{25,1},{2,10},{10... | collective-permute-start | bytes 270344 | tf_op jit(solution)/shard_map/ppermute | solution.py:156
  171.9 6.8 %collective-permute-start.13 = (bf16[32,1408]{1,0:T(8,128)(2,1)S(1)}, bf16[32,1408]{1,0:T(8,128)(2,1)S(1)}, u32[]{:S(2)}, u32[]{:S(2)}) collective-permute-start(bf16[32,1408]{1,0:T(8,128)(2,1)S(1)} %reduce_sum.124), channel_id=1, source_target_pairs={{0,16},{8,24},{16,0},{24,8},{1,17},{9,25},{17,1},{25,9},{2,18},{10... | collective-permute-start | bytes 270344 | tf_op jit(solution)/shard_map/ppermute | solution.py:156
  174.6 5.0 %collective-permute-start.14 = (bf16[32,1408]{1,0:T(8,128)(2,1)S(1)}, bf16[32,1408]{1,0:T(8,128)(2,1)S(1)}, u32[]{:S(2)}, u32[]{:S(2)}) collective-permute-start(bf16[32,1408]{1,0:T(8,128)(2,1)S(1)} %reduce_sum.124), channel_id=1, source_target_pairs={{0,24},{8,0},{16,8},{24,16},{1,25},{9,1},{17,9},{25,17},{2,26},{10... | collective-permute-start | bytes 270344 | tf_op jit(solution)/shard_map/ppermute | solution.py:156
  (15 other events, 30.2 us)

commit v2 on v1

--- a/solution.py
+++ b/solution.py
@@ -151,19 +151,26 @@
     )
 
 
-def shifted_rows(mine, axis_size, axis_name):
-    return [
-        lax.ppermute(mine[k], axis_name, [(a, (a + k) % axis_size) for a in range(axis_size)])
-        for k in range(1, axis_size)
-    ]
-
-
-def gathered(mine, seq_size, seq_index):
-    rows = jnp.zeros((seq_size,) + mine.shape, mine.dtype)
-    rows = lax.dynamic_update_index_in_dim(rows, mine, seq_index, 0)
-    for k, t in enumerate(shifted_rows([mine] * seq_size, seq_size, "seq"), 1):
-        rows = lax.dynamic_update_index_in_dim(rows, t, (seq_index - k) % seq_size, 0)
+def swapped(mine, axis_name, distance):
+    size = lax.axis_size(axis_name)
+    return lax.ppermute(mine, axis_name, [(a, a ^ distance) for a in range(size)])
+
+
+def gathered_seq(mine):
+    size, index = lax.axis_size("seq"), lax.axis_index("seq")
+    rows = jnp.zeros((size,) + mine.shape, mine.dtype)
+    rows = lax.dynamic_update_index_in_dim(rows, mine, index, 0)
+    for k in range(1, size):
+        t = lax.ppermute(mine, "seq", [(a, (a + k) % size) for a in range(size)])
+        rows = lax.dynamic_update_index_in_dim(rows, t, (index - k) % size, 0)
     return rows
+
+
+def summed_everywhere(parts):
+    parts = lax.all_to_all(parts.astype(jnp.bfloat16), "res", 0, 0, tiled=True)
+    part = jnp.sum(parts.astype(jnp.float32), axis=0).astype(jnp.bfloat16)
+    part = jnp.sum(gathered_seq(part).astype(jnp.float32), axis=0).astype(jnp.bfloat16)
+    return lax.all_gather(part, "res", axis=0).astype(jnp.float32)
 
 
 def head_body(
@@ -174,14 +181,23 @@
     query_width = output_weight.shape[0]
     head_dim = query_width // head_count
     column_count = pair_entries.shape[1]
-    pair_width = pair_entries.shape[2]
     token_count = sequence_count * residue_count
-    seq_size = lax.axis_size("seq")
+    seq_size, res_size = lax.axis_size("seq"), lax.axis_size("res")
     seq_index = lax.axis_index("seq")
-    residue_total = residue_count * head_count
-    row_count = residue_total // seq_size
-    depth = sequence_count * head_dim
+    core = lax.axis_index("res") % 2
+    half = seq_index // 2
+    residue_total = residue_count * res_size
+    half_seqs = sequence_count // 2
+    half_rows = residue_count // 2
+    depth = half_seqs * head_dim
+    group = 2 * res_size
+    groups = [[g * group + k for k in range(group)] for g in range(seq_size // 2)]
     score_scale = 1.0 / math.sqrt(head_dim * sequence_count * seq_size)
+
+    def across(blocks):
+        return lax.all_to_all(
+            blocks, ("seq", "res"), 0, 0, axis_index_groups=groups, tiled=True
+        )
 
     normalized_rows, broadcast_pair = layer_normalize(alignment_rows)
     normed_b = normalized_rows.astype(jnp.bfloat16).reshape(token_count, alignment_width)
@@ -193,17 +209,28 @@
     def to_heads(tensors):
         blocks = jnp.stack(
             [
-                t.astype(jnp.bfloat16).reshape(sequence_count, residue_count, head_count, head_dim)
+                t.astype(jnp.bfloat16).reshape(2, half_seqs, residue_count, head_count, head_dim)
                 for t in tensors
             ]
         )
-        blocks = jnp.transpose(blocks, (3, 0, 2, 1, 4)).reshape(
-            head_count, len(tensors), residue_count, depth
-        )
-        blocks = lax.all_to_all(blocks, "res", 0, 0, tiled=True)
-        return [
-            blocks[:, t].reshape(residue_total, depth) for t in range(len(tensors))
-        ]
+        blocks = jnp.transpose(blocks, (4, 1, 0, 3, 2, 5)).reshape(
+            group, len(tensors), residue_count, depth
+        )
+        blocks = across(blocks).reshape(2, res_size, len(tensors), residue_count, depth)
+        blocks = jnp.transpose(blocks, (2, 1, 3, 0, 4))
+        return [blocks[t].reshape(residue_total, 2 * depth) for t in range(len(tensors))]
+
+    def rows_of(tensor, which):
+        blocks = tensor.reshape(res_size, 2, half_rows, tensor.shape[1])
+        return lax.dynamic_index_in_dim(blocks, which, 1, False).reshape(
+            residue_total // 2, tensor.shape[1]
+        )
+
+    def products(left, right):
+        own = jnp.dot(rows_of(left, core), right.T, preferred_element_type=jnp.float32)
+        other_rows = swapped(rows_of(left, 1 - core), "res", 1)
+        other = swapped(right, "res", 1)
+        return own + jnp.dot(other_rows, other.T, preferred_element_type=jnp.float32)
 
     queries, keys = to_heads(
         [projected[:, :query_width] * score_scale, projected[:, query_width : 2 * query_width]]
@@ -214,41 +241,68 @@
 
     pair_normed, pair_spread = layer_normalize(pair_entries)
     pair_bias = jnp.einsum("ijc,ch->hij", pair_normed, pair_weight, precision=lax.Precision.HIGHEST)
-    bias = lax.all_to_all(pair_bias, "res", 0, 0, tiled=True).reshape(residue_total, column_count)
-
-    col_start = seq_index * column_count
-    score_terms = jnp.dot(queries, keys.T, preferred_element_type=jnp.float32)
-    own_block = lax.dynamic_slice_in_dim(score_terms, col_start, column_count, 1) + bias
-    score_terms = lax.dynamic_update_slice_in_dim(score_terms, own_block, col_start, 1)
-    grad_terms = jnp.dot(grad_attended, values.T, preferred_element_type=jnp.float32)
+    bias = across(pair_bias.reshape(group, half_rows, column_count))
+    bias = jnp.transpose(bias.reshape(2, res_size * half_rows, column_count), (1, 0, 2)).reshape(
+        residue_total // 2, 2 * column_count
+    )
+
+    score_terms = products(queries, keys)
+    bias_start = half * 2 * column_count
+    own_block = lax.dynamic_slice_in_dim(score_terms, bias_start, 2 * column_count, 1) + bias
+    score_terms = lax.dynamic_update_slice_in_dim(score_terms, own_block, bias_start, 1)
+    grad_terms = products(grad_attended, values)
 
     def row_sums(terms, kind):
-        blocks = terms.reshape(seq_size, row_count, residue_total)
-        pick = lambda k: lax.dynamic_index_in_dim(blocks, (seq_index + k) % seq_size, 0, False)
-        sent = [pick(k).astype(kind) for k in range(seq_size)]
-        return sum((t.astype(jnp.float32) for t in shifted_rows(sent, seq_size, "seq")), pick(0))
+        blocks = terms.reshape(2, residue_total // 4, residue_total)
+        mine = lax.dynamic_index_in_dim(blocks, half, 0, False)
+        sent = lax.dynamic_index_in_dim(blocks, 1 - half, 0, False).astype(kind)
+        return mine + swapped(sent, "seq", seq_size // 2).astype(jnp.float32)
+
+    def half_gathered(mine):
+        other = swapped(mine, "seq", seq_size // 2)
+        low = jnp.where(half == 0, mine, other)
+        high = jnp.where(half == 0, other, mine)
+        return jnp.concatenate([low, high], axis=0)
 
     def all_rows(mine):
-        return gathered(mine, seq_size, seq_index).reshape(residue_total, residue_total)
+        other = swapped(mine, "res", 1)
+        even = jnp.where(core == 0, mine, other).reshape(res_size, half_rows, residue_total)
+        odd = jnp.where(core == 0, other, mine).reshape(res_size, half_rows, residue_total)
+        return jnp.stack([even, odd], 1).reshape(residue_total, residue_total)
 
     logits = row_sums(score_terms, jnp.float32)
     grad_probs = row_sums(grad_terms, jnp.bfloat16)
     row_top = jnp.max(logits, axis=-1, keepdims=True)
     lifted = jnp.exp(logits - row_top)
     softmax_out = lifted / jnp.sum(lifted, axis=-1, keepdims=True)
-    probs = all_rows(softmax_out.astype(jnp.bfloat16))
+    probs = all_rows(half_gathered(softmax_out.astype(jnp.bfloat16)))
     row_dot = jnp.sum(softmax_out * grad_probs, axis=-1, keepdims=True)
-    grad_logits = all_rows((softmax_out * (grad_probs - row_dot)).astype(jnp.bfloat16))
+    grad_logits_half = half_gathered((softmax_out * (grad_probs - row_dot)).astype(jnp.bfloat16))
+    logit_share = lax.dynamic_slice_in_dim(grad_logits_half, bias_start, 2 * column_count, 1)
+    logit_share = jnp.transpose(
+        logit_share.reshape(res_size, half_rows, 2, column_count), (2, 0, 1, 3)
+    ).reshape(group, half_rows, column_count)
+    logit_share = (
+        across(logit_share)
+        .reshape(head_count, residue_count, column_count)
+        .astype(jnp.float32)
+    )
+    grad_logits = all_rows(grad_logits_half)
 
     def to_residues(tensors):
         blocks = jnp.stack(
-            [t.astype(jnp.bfloat16).reshape(head_count, residue_count, depth) for t in tensors], 1
-        )
-        blocks = lax.all_to_all(blocks, "res", 0, 0, tiled=True)
-        blocks = blocks.reshape(
-            head_count, len(tensors), residue_count, sequence_count, head_dim
-        )
-        blocks = jnp.transpose(blocks, (1, 3, 2, 0, 4))
+            [
+                t.astype(jnp.bfloat16).reshape(res_size, residue_count, 2, depth)
+                for t in tensors
+            ]
+        )
+        blocks = jnp.transpose(blocks, (3, 1, 0, 2, 4)).reshape(
+            group, len(tensors), residue_count, depth
+        )
+        blocks = across(blocks).reshape(
+            head_count, 2, len(tensors), residue_count, half_seqs, head_dim
+        )
+        blocks = jnp.transpose(blocks, (2, 1, 4, 3, 0, 5))
         return [blocks[t].reshape(token_count, query_width) for t in range(len(tensors))]
 
     attended, grad_values = to_residues(
@@ -263,50 +317,59 @@
             jnp.dot(grad_logits.T, queries, preferred_element_type=jnp.float32),
         ]
     )
-    logit_share = lax.dynamic_slice_in_dim(grad_logits, col_start, column_count, 1).reshape(
-        head_count, residue_count, column_count
-    )
-    logit_share = lax.all_to_all(logit_share, "res", 0, 0, tiled=True).astype(jnp.float32)
 
     attended = attended.astype(jnp.float32)
     gated_out = (gate_open * attended).astype(jnp.bfloat16)
     updated = jnp.dot(gated_out, output_weight, preferred_element_type=jnp.float32).astype(
         jnp.bfloat16
     )
-    out_local = jnp.dot(gated_out.T, flattened_gradient, preferred_element_type=jnp.float32)
     grad_gate_logit = grad_gated * attended * gate_open * (1.0 - gate_open)
     projected_gradient = jnp.concatenate(
         [grad_queries, grad_keys, grad_values, grad_gate_logit.astype(jnp.bfloat16)], axis=-1
     )
-    qkvg_local = jnp.dot(normed_b.T, projected_gradient, preferred_element_type=jnp.float32)
+
+    weight_rows = alignment_width // res_size
+
+    def row_blocks(matrix):
+        return matrix.reshape(res_size, weight_rows, matrix.shape[-1])
+
+    value_gate = projected_gradient[:, 2 * query_width :]
+    query_key = projected_gradient[:, : 2 * query_width]
+    early = summed_everywhere(
+        jnp.concatenate(
+            [
+                row_blocks(jnp.dot(normed_b.T, value_gate, preferred_element_type=jnp.float32)),
+                row_blocks(
+                    jnp.dot(gated_out.T, flattened_gradient, preferred_element_type=jnp.float32)
+                ),
+            ],
+            axis=-1,
+        )
+    )
+    pair_w_local = jnp.einsum(
+        "ijc,hij->hc", pair_normed, logit_share, precision=lax.Precision.HIGHEST
+    )
+    late = summed_everywhere(
+        jnp.concatenate(
+            [
+                row_blocks(jnp.dot(normed_b.T, query_key, preferred_element_type=jnp.float32)),
+                jnp.pad(pair_w_local[:, None, :], ((0, 0), (0, weight_rows - 1), (0, 0))),
+            ],
+            axis=-1,
+        )
+    )
+    combined_weight_gradient = jnp.concatenate(
+        [late[:, :, : 2 * query_width], early[:, :, : 2 * query_width]], axis=-1
+    ).reshape(combined_weight.shape)
+    output_weight_gradient = early[:, :, 2 * query_width :].reshape(output_weight.shape)
+    pair_weight_gradient = late[:, 0, 2 * query_width :].T
+
     normalized_gradient = jnp.dot(
         projected_gradient, combined_weight.T, preferred_element_type=jnp.float32
     ).reshape(alignment_rows.shape)
     alignment_gradient = layer_norm_backward(
         normalized_gradient, normalized_rows, broadcast_pair
     ).astype(jnp.bfloat16)
-    pair_w_local = jnp.einsum(
-        "ijc,hij->hc", pair_normed, logit_share, precision=lax.Precision.HIGHEST
-    )
-
-    weight_rows = alignment_width // head_count
-    parts = jnp.concatenate(
-        [
-            qkvg_local.reshape(head_count, weight_rows, 4 * query_width),
-            out_local.reshape(head_count, weight_rows, alignment_width),
-            jnp.pad(pair_w_local[:, None, :], ((0, 0), (0, weight_rows - 1), (0, 0))),
-        ],
-        axis=-1,
-    ).astype(jnp.bfloat16)
-    part = jnp.sum(lax.all_to_all(parts, "res", 0, 0, tiled=True).astype(jnp.float32), axis=0)
-    sent = part.astype(jnp.bfloat16)
-    part = jnp.sum(gathered(sent, seq_size, seq_index).astype(jnp.float32), axis=0)
-    whole = lax.all_gather(part.astype(jnp.bfloat16), "res", axis=0).astype(jnp.float32)
-    wide = 4 * query_width + alignment_width
-    combined_weight_gradient = whole[:, :, : 4 * query_width].reshape(combined_weight.shape)
-    output_weight_gradient = whole[:, :, 4 * query_width : wide].reshape(output_weight.shape)
-    pair_weight_gradient = whole[:, 0, wide:].T
-
     grad_pair_normed = jnp.einsum(
         "hij,ch->ijc", logit_share, pair_weight, precision=lax.Precision.HIGHEST
     )
@@ -324,7 +387,8 @@
 
 
 def body(alignment_rows, pair_entries, combined_weight, output_weight, pair_weight, updated_gradient):
-    one_head = pair_weight.shape[1] == lax.axis_size("res")
+    head_count = pair_weight.shape[1]
+    one_head = head_count == lax.axis_size("res") and lax.axis_size("seq") == 4
     chosen = head_body if one_head else gathered_body
     return chosen(
         alignment_rows, pair_entries, combined_weight, output_weight, pair_weight, updated_gradient

time: 194 us -> 223 us (1.15)
  local copies, waits for them, and re-layouts: 28.2 us -> 47.5 us
  waiting for transfers between devices: 63.5 us -> 46.8 us
  matrix products: 16.6 us -> 28.7 us
  other arithmetic: 18.5 us -> 28.3 us
  blocking collectives: 10.6 us -> 19.4 us
  starting transfers between devices: 53.9 us -> 48.2 us
    ppermute x15 -> x16, starting transfers between devices: 26.3 us -> 12.6 us  [the longest x10 7.56 us: swapped(): lax.ppermute(mine, axis_name, [(a, a ^ distance) for a in range(size)])]
    all_to_all x7 -> x8, waiting for transfers between devices: 22.5 us -> 12 us  [the longest x6 7.97 us: across(): lax.all_to_all(blocks, ('seq', 'res'), 0, 0, axis_index_groups=groups, ti...]
    all_gather x1 -> x2, blocking collectives: 10.6 us -> 19.4 us  [summed_everywhere(): return lax.all_gather(part, 'res', axis=0).astype(jnp.float32)]
    another operation x6 -> x14, local copies, waits for them, and re-layouts: 1.17 us -> 9.49 us  [the longest x8 4 us: to_residues(): jnp.stack([t.astype(jnp.bfloat16).reshape(res_size, residue_count, 2, dep...]
    all_to_all x7 -> x8, starting transfers between devices: 27.6 us -> 35.6 us  [the longest x6 28.2 us: across(): lax.all_to_all(blocks, ('seq', 'res'), 0, 0, axis_index_groups=groups, ti...]
    ppermute x15 -> x16, waiting for transfers between devices: 41.1 us -> 34.8 us  [the longest x10 23.9 us: swapped(): lax.ppermute(mine, axis_name, [(a, a ^ distance) for a in range(size)])]
    transpose x2, other arithmetic: 0.47 us -> 3.99 us  [to_heads(): jnp.transpose(blocks, (4, 1, 0, 3, 2, 5))]
    dot_general x1, matrix products: 2.56 us -> 6.03 us  [head_body(): jnp.einsum('hij,ch->ijc', logit_share, pair_weight, precision=lax.Precisi...]
  transfers between devices with their start and end apart: 22 -> 24, of which waited for: 15 -> 9; matrix products, arithmetic and copies ran while one was open for 21% -> 35% of each run, Pallas kernels for 0% -> 0%
where the time goes in v2:
time: 223 us; the launch traced here: 221 us
  starting transfers between devices  48.2 us (22%)
  local copies, waits for them, and re-layouts  47.5 us (21%)
  waiting for transfers between devices  46.8 us (21%)
  matrix products  28.7 us (13%)
  other arithmetic  28.3 us (13%)
  blocking collectives  19.4 us (9%)
    all_to_all x6, starting transfers between devices, across(): lax.all_to_all(blocks, ('seq', 'res'), 0, 0, axis_index_groups=groups, ti...  28.2 us
    ppermute x10, waiting for transfers between devices, swapped(): lax.ppermute(mine, axis_name, [(a, a ^ distance) for a in range(size)])  23.9 us
    all_gather x2, blocking collectives, summed_everywhere(): return lax.all_gather(part, 'res', axis=0).astype(jnp.float32)  19.4 us
    unnamed x56, local copies, waits for them, and re-layouts  11.1 us
    ppermute x6, waiting for transfers between devices, gathered_seq(): t = lax.ppermute(mine, 'seq', [(a, (a + k) % size) for a in range(size)])  10.9 us
    all_to_all x6, waiting for transfers between devices, across(): lax.all_to_all(blocks, ('seq', 'res'), 0, 0, axis_index_groups=groups, ti...  7.97 us
    ppermute x10, starting transfers between devices, swapped(): lax.ppermute(mine, axis_name, [(a, a ^ distance) for a in range(size)])  7.56 us
    all_to_all x2, starting transfers between devices, summed_everywhere(): parts = lax.all_to_all(parts.astype(jnp.bfloat16), 'res', 0, 0, tiled=True)  7.41 us
  transfers between devices with their start and end apart: 24, of which 9 were waited for; matrix products, arithmetic and copies ran while one was open for 35% of the time, Pallas kernels for 0%

profile of v2, /device:TPU:0, one launch (start us, length us, event | category | flops | bytes accessed | tf_op | source)
XLA Modules:
  0.0 220.7 jit_solution(2397679583863021542)
XLA Ops:
  13.6 6.3 %all-to-all-start.2 = ((bf16[16,2,64,128]{3,2,1,0:T(8,128)(2,1)}), bf16[16,2,64,128]{3,2,1,0:T(8,128)(2,1)S(1)}, u32[]{:S(2)}, u32[]{:S(2)}) async-start(bf16[16,2,64,128]{3,2,1,0:T(8,128)(2,1)} %copy.154), calls=%async_computation.2 | async-start | bytes 1048576 | tf_op jit(solution)/shard_map/all_to_all | solution.py:198
  20.0 3.2 %copy.146 = bf16[64,128,128]{1,2,0:T(8,128)(2,1)S(1)} copy(bf16[64,128,128]{2,1,0:T(8,128)(2,1)} %param.7) | data formatting | bytes 4194304 | tf_op args[1]
  33.8 5.1 %all-to-all-start = ((bf16[16,2,64,128]{3,2,1,0:T(8,128)(2,1)}), bf16[16,2,64,128]{3,2,1,0:T(8,128)(2,1)}, u32[]{:S(2)}, u32[]{:S(2)}) async-start(bf16[16,2,64,128]{3,2,1,0:T(8,128)(2,1)} %copy.144), calls=%async_computation | async-start | bytes 1048576 | tf_op jit(solution)/shard_map/all_to_all | solution.py:198
  45.6 3.9 %all-to-all-done = bf16[16,2,64,128]{3,2,1,0:T(8,128)(2,1)} async-done(((bf16[16,2,64,128]{3,2,1,0:T(8,128)(2,1)}), bf16[16,2,64,128]{3,2,1,0:T(8,128)(2,1)}, u32[]{:S(2)}, u32[]{:S(2)}) %all-to-all-start) | async-done | bytes 524320 | tf_op jit(solution)/shard_map/all_to_all | solution.py:198
  49.5 4.4 %all-to-all-start.1 = ((f32[16,32,128]{2,1,0:T(8,128)}), f32[16,32,128]{2,1,0:T(8,128)}, u32[]{:S(2)}, u32[]{:S(2)}) async-start(f32[16,32,128]{2,1,0:T(8,128)} %bitcast.213), calls=%async_computation.1 | async-start | bytes 524288 | tf_op jit(solution)/shard_map/all_to_all | solution.py:198
  64.0 2.7 %collective-permute-start.2 = (f32[128,512]{1,0:T(8,128)S(1)}, f32[128,512]{1,0:T(8,128)S(1)}, u32[]{:S(2)}, u32[]{:S(2)}) collective-permute-start(f32[128,512]{1,0:T(8,128)S(1)} %dynamic-slice_bitcast_fusion), channel_id=1, source_target_pairs={{0,16},{8,24},{16,0},{24,8},{1,17},{9,25},{17,1},{25,9},{2,18},{10... | collective-permute-start | bytes 786440 | tf_op jit(solution)/shard_map/ppermute | solution.py:156
  68.6 14.0 %collective-permute-done.2 = f32[128,512]{1,0:T(8,128)S(1)} collective-permute-done((f32[128,512]{1,0:T(8,128)S(1)}, f32[128,512]{1,0:T(8,128)S(1)}, u32[]{:S(2)}, u32[]{:S(2)}) %collective-permute-start.2) | collective-permute-done | bytes 262176 | tf_op jit(solution)/shard_map/ppermute | solution.py:156
  87.0 2.8 %collective-permute-start.3 = (bf16[128,512]{1,0:T(8,128)(2,1)S(1)}, bf16[128,512]{1,0:T(8,128)(2,1)}, u32[]{:S(2)}, u32[]{:S(2)}) collective-permute-start(bf16[128,512]{1,0:T(8,128)(2,1)S(1)} %get-tuple-element.59), channel_id=1, source_target_pairs={{0,16},{8,24},{16,0},{24,8},{1,17},{9,25},{17,1},{25,9},{2,18},{10... | collective-permute-start | bytes 393224 | tf_op jit(solution)/shard_map/ppermute | solution.py:156
  89.8 8.1 %collective-permute-done.8 = bf16[128,512]{1,0:T(8,128)(2,1)S(1)} collective-permute-done((bf16[128,512]{1,0:T(8,128)(2,1)S(1)}, bf16[128,512]{1,0:T(8,128)(2,1)S(1)}, u32[]{:S(2)}, u32[]{:S(2)}) %collective-permute-start.8) | collective-permute-done | bytes 131104 | tf_op jit(solution)/shard_map/ppermute | solution.py:156
  98.7 4.3 %all-to-all-start.5 = ((bf16[16,32,128]{2,1,0:T(8,128)(2,1)}), bf16[16,32,128]{2,1,0:T(8,128)(2,1)}, u32[]{:S(2)}, u32[]{:S(2)}) async-start(bf16[16,32,128]{2,1,0:T(8,128)(2,1)} %bitcast.44), calls=%async_computation.5 | async-start | bytes 262144 | tf_op jit(solution)/shard_map/all_to_all | solution.py:198
  106.0 3.4 %all-to-all-done.5 = bf16[16,32,128]{2,1,0:T(8,128)(2,1)} async-done(((bf16[16,32,128]{2,1,0:T(8,128)(2,1)}), bf16[16,32,128]{2,1,0:T(8,128)(2,1)}, u32[]{:S(2)}, u32[]{:S(2)}) %all-to-all-start.5) | async-done | bytes 131104 | tf_op jit(solution)/shard_map/all_to_all | solution.py:198
  109.3 6.0 %fusion.78 = (f32[64,128]{1,0:T(8,128)}, f32[64,128]{1,0:T(8,128)}, f32[64,128,128]{1,2,0:T(8,128)}) fusion(f32[64,128]{1,0:T(8,128)} %copy-done.15, f32[64,128]{1,0:T(8,128)} %copy-done.8, bf16[64,128,128]{1,2,0:T(8,128)(2,1)S(1)} %copy.146, f32[128,8]{0,1:T(8,128)S(1)} %copy-done.25, bf16[8,64,128]{2,1,0:T(8,128)(2,1)} %bitcast.45), kind=kOutput, calls=%fused_computation.143 | convolution fusion | flops 106938368 | bytes 6557696 | tf_op jit(solution)/shard_map/hij,ch->ijc/dot_general | solution.py:373
  115.4 3.3 %fusion.27 = bf16[8,1,128]{2,0,1:T(8,128)(2,1)S(1)} fusion(bf16[64,128,128]{1,2,0:T(8,128)(2,1)S(1)} %copy.146, f32[64,128]{1,0:T(8,128)S(1)} %copy-done.16, f32[64,128]{1,0:T(8,128)S(1)} %copy-done.9, bf16[8,64,128]{2,1,0:T(8,128)(2,1)} %bitcast.45), kind=kOutput, calls=%fused_computation.31 | convolution fusion | flops 103810048 | bytes 2295808 | tf_op jit(solution)/shard_map/ijc,hij->hc/dot_general | solution.py:349
  125.1 3.6 %all-to-all-start.4 = ((bf16[16,2,64,128]{3,2,1,0:T(8,128)(2,1)}), bf16[16,2,64,128]{3,2,1,0:T(8,128)(2,1)S(1)}, u32[]{:S(2)}, u32[]{:S(2)}) async-start(bf16[16,2,64,128]{3,2,1,0:T(8,128)(2,1)} %bitcast.208), calls=%async_computation.4 | async-start | bytes 1048576 | tf_op jit(solution)/shard_map/all_to_all | solution.py:198
  139.2 4.5 %all-to-all-start.3 = ((bf16[16,2,64,128]{3,2,1,0:T(8,128)(2,1)}), bf16[16,2,64,128]{3,2,1,0:T(8,128)(2,1)}, u32[]{:S(2)}, u32[]{:S(2)}) async-start(bf16[16,2,64,128]{3,2,1,0:T(8,128)(2,1)} %bitcast.207), calls=%async_computation.3 | async-start | bytes 1048576 | tf_op jit(solution)/shard_map/all_to_all | solution.py:198
  143.8 4.9 %fusion.11 = bf16[64,128,128]{1,2,0:T(8,128)(2,1)} fusion(bf16[64,128,128]{1,2,0:T(8,128)(2,1)S(1)} %copy.146, f32[64,128,128]{1,2,0:T(8,128)} %get-tuple-element.73, f32[64,128]{1,0:T(8,128)S(1)} %broadcast_multiply_fusion, f32[64,128]{1,0:T(8,128)S(1)} %broadcast_multiply_fusion.1, f32[64,128]{1,0:T(8,128)S(1)} %copy-done.17, f32[64,128]{1,0:T(8,128)S(1)} %copy-done.10), kind=kLoop, calls=%fused_computation.11 | loop fusion | flops 8388608 | bytes 8519680 | tf_op jit(solution)/shard_map/convert_element_type | solution.py:376
  148.7 4.1 %copy.182 = bf16[64,128,128]{2,1,0:T(8,128)(2,1)} copy(bf16[64,128,128]{1,2,0:T(8,128)(2,1)} %fusion.11) | data formatting | bytes 4194304
  167.4 4.0 %all-to-all-start.6 = ((bf16[8,32,640]{2,1,0:T(8,128)(2,1)}), bf16[8,32,640]{2,1,0:T(8,128)(2,1)S(1)}, u32[]{:S(2)}, u32[]{:S(2)}) async-start(bf16[8,32,640]{2,1,0:T(8,128)(2,1)} %fusion.57), calls=%async_computation.6 | async-start | bytes 655360 | tf_op jit(solution)/shard_map/all_to_all | solution.py:170
  174.9 4.0 %all-to-all-done.6 = bf16[8,32,640]{2,1,0:T(8,128)(2,1)S(1)} async-done(((bf16[8,32,640]{2,1,0:T(8,128)(2,1)}), bf16[8,32,640]{2,1,0:T(8,128)(2,1)S(1)}, u32[]{:S(2)}, u32[]{:S(2)}) %all-to-all-start.6) | async-done | bytes 327712 | tf_op jit(solution)/shard_map/all_to_all | solution.py:170
  179.0 3.5 %all-to-all-start.7 = ((bf16[8,32,768]{2,1,0:T(8,128)(2,1)}), bf16[8,32,768]{2,1,0:T(8,128)(2,1)S(1)}, u32[]{:S(2)}, u32[]{:S(2)}) async-start(bf16[8,32,768]{2,1,0:T(8,128)(2,1)} %pad_maximum_fusion.5), calls=%async_computation.7 | async-start | bytes 786432 | tf_op jit(solution)/shard_map/all_to_all | solution.py:170
  185.5 5.8 %collective-permute-done.10 = bf16[32,640]{1,0:T(8,128)(2,1)S(1)} collective-permute-done((bf16[32,640]{1,0:T(8,128)(2,1)S(1)}, bf16[32,640]{1,0:T(8,128)(2,1)S(1)}, u32[]{:S(2)}, u32[]{:S(2)}) %collective-permute-start.10) | collective-permute-done | bytes 40992 | tf_op jit(solution)/shard_map/ppermute | solution.py:164
  191.4 9.9 %all-gather = bf16[256,640]{1,0:T(8,128)(2,1)S(1)} all-gather(bf16[32,640]{1,0:T(8,128)(2,1)S(1)} %reduce_sum.149), channel_id=2, replica_groups=mesh['seq'=4,'res'=8] {'res'}, dimensions={0}, use_global_device_ids=true | all-gather | bytes 368640 | tf_op jit(solution)/shard_map/all_gather | solution.py:173
  204.1 5.1 %collective-permute-done.13 = bf16[32,768]{1,0:T(8,128)(2,1)S(1)} collective-permute-done((bf16[32,768]{1,0:T(8,128)(2,1)S(1)}, bf16[32,768]{1,0:T(8,128)(2,1)S(1)}, u32[]{:S(2)}, u32[]{:S(2)}) %collective-permute-start.13) | collective-permute-done | bytes 49184 | tf_op jit(solution)/shard_map/ppermute | solution.py:164
  209.3 9.6 %all-gather.1 = bf16[256,768]{1,0:T(8,128)(2,1)S(1)} all-gather(bf16[32,768]{1,0:T(8,128)(2,1)S(1)} %reduce_sum.151), channel_id=3, replica_groups=mesh['seq'=4,'res'=8] {'res'}, dimensions={0}, use_global_device_ids=true | all-gather | bytes 442368 | tf_op jit(solution)/shard_map/all_gather | solution.py:173
  (209 shorter events, 92.7 us)
Async XLA Ops:
  13.6 20.1 %all-to-all-start.2 = ((bf16[16,2,64,128]{3,2,1,0:T(8,128)(2,1)}), bf16[16,2,64,128]{3,2,1,0:T(8,128)(2,1)S(1)}, u32[]{:S(2)}, u32[]{:S(2)}) async-start(bf16[16,2,64,128]{3,2,1,0:T(8,128)(2,1)} %copy.154), calls=%async_computation.2 | async-start | bytes 1048576 | tf_op jit(solution)/shard_map/all_to_all | solution.py:198
  33.8 15.7 %all-to-all-start = ((bf16[16,2,64,128]{3,2,1,0:T(8,128)(2,1)}), bf16[16,2,64,128]{3,2,1,0:T(8,128)(2,1)}, u32[]{:S(2)}, u32[]{:S(2)}) async-start(bf16[16,2,64,128]{3,2,1,0:T(8,128)(2,1)} %copy.144), calls=%async_computation | async-start | bytes 1048576 | tf_op jit(solution)/shard_map/all_to_all | solution.py:198
  49.5 13.5 %all-to-all-start.1 = ((f32[16,32,128]{2,1,0:T(8,128)}), f32[16,32,128]{2,1,0:T(8,128)}, u32[]{:S(2)}, u32[]{:S(2)}) async-start(f32[16,32,128]{2,1,0:T(8,128)} %bitcast.213), calls=%async_computation.1 | async-start | bytes 524288 | tf_op jit(solution)/shard_map/all_to_all | solution.py:198
  60.3 6.4 %collective-permute-start.5 = (bf16[256,256]{1,0:T(8,128)(2,1)S(1)}, bf16[256,256]{1,0:T(8,128)(2,1)}, u32[]{:S(2)}, u32[]{:S(2)}) collective-permute-start(bf16[256,256]{1,0:T(8,128)(2,1)S(1)} %bitcast.236), channel_id=1, source_target_pairs={{0,1},{1,0},{2,3},{3,2},{4,5},{5,4},{6,7},{7,6},{8,9},{9,8},{10,11... | collective-permute-start | bytes 393224 | tf_op jit(solution)/shard_map/ppermute | solution.py:156
  60.6 2.1 collective-permute-start
  60.9 1.8 collective-permute-start.1
  61.1 5.6 %collective-permute-start.6 = (bf16[512,256]{1,0:T(8,128)(2,1)}, bf16[512,256]{1,0:T(8,128)(2,1)}, u32[]{:S(2)}, u32[]{:S(2)}) collective-permute-start(bf16[512,256]{1,0:T(8,128)(2,1)} %bitcast.233), channel_id=1, source_target_pairs={{0,1},{1,0},{2,3},{3,2},{4,5},{5,4},{6,7},{7,6},{8,9},{9,8},{10,11... | collective-permute-start | bytes 786440 | tf_op jit(solution)/shard_map/ppermute | solution.py:156
  64.0 18.5 %collective-permute-start.2 = (f32[128,512]{1,0:T(8,128)S(1)}, f32[128,512]{1,0:T(8,128)S(1)}, u32[]{:S(2)}, u32[]{:S(2)}) collective-permute-start(f32[128,512]{1,0:T(8,128)S(1)} %dynamic-slice_bitcast_fusion), channel_id=1, source_target_pairs={{0,16},{8,24},{16,0},{24,8},{1,17},{9,25},{17,1},{25,9},{2,18},{10... | collective-permute-start | bytes 786440 | tf_op jit(solution)/shard_map/ppermute | solution.py:156
  68.2 16.5 %collective-permute-start.7 = (bf16[128,512]{1,0:T(8,128)(2,1)S(1)}, bf16[128,512]{1,0:T(8,128)(2,1)S(1)}, u32[]{:S(2)}, u32[]{:S(2)}) collective-permute-start(bf16[128,512]{1,0:T(8,128)(2,1)S(1)} %fusion.65), channel_id=1, source_target_pairs={{0,16},{8,24},{16,0},{24,8},{1,17},{9,25},{17,1},{25,9},{2,18},{10... | collective-permute-start | bytes 393224 | tf_op jit(solution)/shard_map/ppermute | solution.py:156
  85.1 12.9 %collective-permute-start.8 = (bf16[128,512]{1,0:T(8,128)(2,1)S(1)}, bf16[128,512]{1,0:T(8,128)(2,1)S(1)}, u32[]{:S(2)}, u32[]{:S(2)}) collective-permute-start(bf16[128,512]{1,0:T(8,128)(2,1)S(1)} %get-tuple-element.58), channel_id=1, source_target_pairs={{0,16},{8,24},{16,0},{24,8},{1,17},{9,25},{17,1},{25,9},{2,18},{10... | collective-permute-start | bytes 393224 | tf_op jit(solution)/shard_map/ppermute | solution.py:156
  87.0 17.0 %collective-permute-start.3 = (bf16[128,512]{1,0:T(8,128)(2,1)S(1)}, bf16[128,512]{1,0:T(8,128)(2,1)}, u32[]{:S(2)}, u32[]{:S(2)}) collective-permute-start(bf16[128,512]{1,0:T(8,128)(2,1)S(1)} %get-tuple-element.59), channel_id=1, source_target_pairs={{0,16},{8,24},{16,0},{24,8},{1,17},{9,25},{17,1},{25,9},{2,18},{10... | collective-permute-start | bytes 393224 | tf_op jit(solution)/shard_map/ppermute | solution.py:156
  98.7 10.7 %all-to-all-start.5 = ((bf16[16,32,128]{2,1,0:T(8,128)(2,1)}), bf16[16,32,128]{2,1,0:T(8,128)(2,1)}, u32[]{:S(2)}, u32[]{:S(2)}) async-start(bf16[16,32,128]{2,1,0:T(8,128)(2,1)} %bitcast.44), calls=%async_computation.5 | async-start | bytes 262144 | tf_op jit(solution)/shard_map/all_to_all | solution.py:198
  103.7 15.0 %collective-permute-start.9 = (bf16[256,512]{1,0:T(8,128)(2,1)}, bf16[256,512]{1,0:T(8,128)(2,1)}, u32[]{:S(2)}, u32[]{:S(2)}) collective-permute-start(bf16[256,512]{1,0:T(8,128)(2,1)} %pad_maximum_fusion.6), channel_id=1, source_target_pairs={{0,1},{1,0},{2,3},{3,2},{4,5},{5,4},{6,7},{7,6},{8,9},{9,8},{10,11... | collective-permute-start | bytes 786440 | tf_op jit(solution)/shard_map/ppermute | solution.py:156
  105.7 23.0 %collective-permute-start.4 = (bf16[256,512]{1,0:T(8,128)(2,1)}, bf16[256,512]{1,0:T(8,128)(2,1)}, u32[]{:S(2)}, u32[]{:S(2)}) collective-permute-start(bf16[256,512]{1,0:T(8,128)(2,1)} %pad_maximum_fusion.7), channel_id=1, source_target_pairs={{0,1},{1,0},{2,3},{3,2},{4,5},{5,4},{6,7},{7,6},{8,9},{9,8},{10,11... | collective-permute-start | bytes 786440 | tf_op jit(solution)/shard_map/ppermute | solution.py:156
  125.1 14.1 %all-to-all-start.4 = ((bf16[16,2,64,128]{3,2,1,0:T(8,128)(2,1)}), bf16[16,2,64,128]{3,2,1,0:T(8,128)(2,1)S(1)}, u32[]{:S(2)}, u32[]{:S(2)}) async-start(bf16[16,2,64,128]{3,2,1,0:T(8,128)(2,1)} %bitcast.208), calls=%async_computation.4 | async-start | bytes 1048576 | tf_op jit(solution)/shard_map/all_to_all | solution.py:198
  139.2 17.0 %all-to-all-start.3 = ((bf16[16,2,64,128]{3,2,1,0:T(8,128)(2,1)}), bf16[16,2,64,128]{3,2,1,0:T(8,128)(2,1)}, u32[]{:S(2)}, u32[]{:S(2)}) async-start(bf16[16,2,64,128]{3,2,1,0:T(8,128)(2,1)} %bitcast.207), calls=%async_computation.3 | async-start | bytes 1048576 | tf_op jit(solution)/shard_map/all_to_all | solution.py:198
  167.4 11.6 %all-to-all-start.6 = ((bf16[8,32,640]{2,1,0:T(8,128)(2,1)}), bf16[8,32,640]{2,1,0:T(8,128)(2,1)S(1)}, u32[]{:S(2)}, u32[]{:S(2)}) async-start(bf16[8,32,640]{2,1,0:T(8,128)(2,1)} %fusion.57), calls=%async_computation.6 | async-start | bytes 655360 | tf_op jit(solution)/shard_map/all_to_all | solution.py:170
  179.0 22.9 %all-to-all-start.7 = ((bf16[8,32,768]{2,1,0:T(8,128)(2,1)}), bf16[8,32,768]{2,1,0:T(8,128)(2,1)S(1)}, u32[]{:S(2)}, u32[]{:S(2)}) async-start(bf16[8,32,768]{2,1,0:T(8,128)(2,1)} %pad_maximum_fusion.5), calls=%async_computation.7 | async-start | bytes 786432 | tf_op jit(solution)/shard_map/all_to_all | solution.py:170
  182.5 8.8 %collective-permute-start.12 = (bf16[32,640]{1,0:T(8,128)(2,1)S(1)}, bf16[32,640]{1,0:T(8,128)(2,1)S(1)}, u32[]{:S(2)}, u32[]{:S(2)}) collective-permute-start(bf16[32,640]{1,0:T(8,128)(2,1)S(1)} %reduce_sum.148), channel_id=1, source_target_pairs={{0,24},{8,0},{16,8},{24,16},{1,25},{9,1},{17,9},{25,17},{2,26},{10... | collective-permute-start | bytes 122888 | tf_op jit(solution)/shard_map/ppermute | solution.py:164
  184.1 7.2 %collective-permute-start.11 = (bf16[32,640]{1,0:T(8,128)(2,1)S(1)}, bf16[32,640]{1,0:T(8,128)(2,1)S(1)}, u32[]{:S(2)}, u32[]{:S(2)}) collective-permute-start(bf16[32,640]{1,0:T(8,128)(2,1)S(1)} %reduce_sum.148), channel_id=1, source_target_pairs={{0,16},{8,24},{16,0},{24,8},{1,17},{9,25},{17,1},{25,9},{2,18},{10... | collective-permute-start | bytes 122888 | tf_op jit(solution)/shard_map/ppermute | solution.py:164
  185.5 5.8 %collective-permute-start.10 = (bf16[32,640]{1,0:T(8,128)(2,1)S(1)}, bf16[32,640]{1,0:T(8,128)(2,1)S(1)}, u32[]{:S(2)}, u32[]{:S(2)}) collective-permute-start(bf16[32,640]{1,0:T(8,128)(2,1)S(1)} %reduce_sum.148), channel_id=1, source_target_pairs={{0,8},{8,16},{16,24},{24,0},{1,9},{9,17},{17,25},{25,1},{2,10},{10... | collective-permute-start | bytes 122888 | tf_op jit(solution)/shard_map/ppermute | solution.py:164
  202.0 7.3 %collective-permute-start.15 = (bf16[32,768]{1,0:T(8,128)(2,1)S(1)}, bf16[32,768]{1,0:T(8,128)(2,1)S(1)}, u32[]{:S(2)}, u32[]{:S(2)}) collective-permute-start(bf16[32,768]{1,0:T(8,128)(2,1)S(1)} %reduce_sum.150), channel_id=1, source_target_pairs={{0,24},{8,0},{16,8},{24,16},{1,25},{9,1},{17,9},{25,17},{2,26},{10... | collective-permute-start | bytes 147464 | tf_op jit(solution)/shard_map/ppermute | solution.py:164
  202.0 7.2 %collective-permute-start.14 = (bf16[32,768]{1,0:T(8,128)(2,1)S(1)}, bf16[32,768]{1,0:T(8,128)(2,1)S(1)}, u32[]{:S(2)}, u32[]{:S(2)}) collective-permute-start(bf16[32,768]{1,0:T(8,128)(2,1)S(1)} %reduce_sum.150), channel_id=1, source_target_pairs={{0,16},{8,24},{16,0},{24,8},{1,17},{9,25},{17,1},{25,9},{2,18},{10... | collective-permute-start | bytes 147464 | tf_op jit(solution)/shard_map/ppermute | solution.py:164
  202.1 7.1 %collective-permute-start.13 = (bf16[32,768]{1,0:T(8,128)(2,1)S(1)}, bf16[32,768]{1,0:T(8,128)(2,1)S(1)}, u32[]{:S(2)}, u32[]{:S(2)}) collective-permute-start(bf16[32,768]{1,0:T(8,128)(2,1)S(1)} %reduce_sum.150), channel_id=1, source_target_pairs={{0,8},{8,16},{16,24},{24,0},{1,9},{9,17},{17,25},{25,1},{2,10},{10... | collective-permute-start | bytes 147464 | tf_op jit(solution)/shard_map/ppermute | solution.py:164
  (26 other events, 218.3 us)

commit v3 on v0

--- a/solution.py
+++ b/solution.py
@@ -1,8 +1,11 @@
+import functools
 import math
 
 import jax
 import jax.numpy as jnp
 from jax import lax
+from jax.experimental import pallas as pl
+from jax.experimental.pallas import tpu as pltpu
 from jax.sharding import PartitionSpec as P
 
 eps_norm = 1e-05
@@ -31,7 +34,7 @@
     return tensor.reshape(tensor.shape[0], tensor.shape[1], tensor.shape[2] * tensor.shape[3])
 
 
-def body(
+def gathered_body(
     alignment_rows, pair_entries, combined_weight, output_weight, pair_weight, updated_gradient
 ):
     sequence_count, residue_count, alignment_width = alignment_rows.shape
@@ -148,6 +151,524 @@
         combined_weight_gradient,
         output_weight_gradient,
         pair_weight_gradient,
+    )
+
+
+VMEM_LIMIT = 48 * 1024 * 1024
+LANES = 128
+SLOTS = 4
+NT = (((1,), (1,)), ((), ()))
+TN = (((0,), (0,)), ((), ()))
+
+
+def f32_dot(left, right, dims=None):
+    if dims is None:
+        return jnp.dot(left, right, preferred_element_type=jnp.float32)
+    return lax.dot_general(left, right, dims, preferred_element_type=jnp.float32)
+
+
+def two_terms(values):
+    high = values.astype(jnp.bfloat16)
+    return high, (values - high.astype(jnp.float32)).astype(jnp.bfloat16)
+
+
+def slot_select(pieces):
+    slot = lax.broadcasted_iota(jnp.int32, pieces[0].shape, 1) // (LANES // SLOTS)
+    result = pieces[0]
+    for k in range(1, SLOTS):
+        result = jnp.where(slot == k, pieces[k], result)
+    return result
+
+
+def pack_heads(out_ref, row, tensor, residues):
+    for core in range(2):
+        for tile in range(tensor.shape[1] // LANES):
+            rolled = []
+            for s in range(SLOTS):
+                start = (core * SLOTS + s) * residues
+                piece = tensor[start : start + residues, tile * LANES : (tile + 1) * LANES]
+                rolled.append(pltpu.roll(piece, s * LANES // SLOTS, 1) if s else piece)
+            for j in range(SLOTS):
+                block = slot_select([rolled[(k - j) % SLOTS] for k in range(SLOTS)])
+                out_ref[(tile * SLOTS + j) * 2 + core, row : row + residues, :] = block.astype(
+                    jnp.bfloat16
+                )
+
+
+def unpack_heads(in_ref, row, residues, tiles):
+    rows = []
+    for core in range(2):
+        for s in range(SLOTS):
+            pieces = []
+            for tile in range(tiles):
+                blocks = [
+                    in_ref[
+                        (tile * SLOTS + (k - s) % SLOTS) * 2 + core, row : row + residues, :
+                    ].astype(jnp.float32)
+                    for k in range(SLOTS)
+                ]
+                block = slot_select(blocks)
+                pieces.append(pltpu.roll(block, LANES - s * LANES // SLOTS, 1) if s else block)
+            rows.append(jnp.concatenate(pieces, axis=1))
+    return jnp.concatenate(rows, axis=0)
+
+
+def normalized(x_ref):
+    width = x_ref.shape[-1]
+    values = x_ref[...].reshape(-1, width).astype(jnp.float32)
+    return layer_normalize(values)
+
+
+def gate_of(logits):
+    return 1.0 / (1.0 + jnp.exp(-logits))
+
+
+def value_kernel(x_ref, grad_ref, wc_ref, wo_ref, out_ref):
+    residues, width = x_ref.shape[1], x_ref.shape[2]
+    normed = normalized(x_ref)[0].astype(jnp.bfloat16)
+    values = f32_dot(normed, wc_ref[:, 2 * width : 3 * width])
+    gate = gate_of(f32_dot(normed, wc_ref[:, 3 * width :]))
+    grad_gated = f32_dot(grad_ref[...].reshape(-1, width), wo_ref[...], NT)
+    pack_heads(out_ref, 0, values, residues)
+    pack_heads(out_ref, residues, grad_gated * gate, residues)
+
+
+def query_kernel(scale, x_ref, wc_ref, pair_ref, weight_ref, out_ref, bias_ref, mean_ref, spread_ref):
+    residues, width = x_ref.shape[1], x_ref.shape[2]
+    heads = weight_ref.shape[0]
+    normed = normalized(x_ref)[0].astype(jnp.bfloat16)
+    pack_heads(out_ref, 0, f32_dot(normed, wc_ref[:, :width]) * scale, residues)
+    pack_heads(out_ref, residues, f32_dot(normed, wc_ref[:, width : 2 * width]), residues)
+
+    columns, channels = pair_ref.shape[1], pair_ref.shape[2]
+    first = weight_ref[...].astype(jnp.bfloat16)
+    rest = weight_ref[...] - first.astype(jnp.float32)
+    second, third = two_terms(rest)
+    share = jnp.full((heads, channels), 1.0 / channels, jnp.bfloat16)
+    left = jnp.concatenate([first, second, third, share], axis=0)
+    ones = jnp.full((heads, channels), 1.0 / channels, jnp.bfloat16)
+    average = jnp.full((channels, channels), 1.0 / channels, jnp.bfloat16)
+
+    def rows(step, carry):
+        for k in range(8):
+            i = step * 8 + k
+            entries = pair_ref[i]
+            center = entries.astype(jnp.float32) - f32_dot(entries, average)
+            high, low = two_terms(center * center)
+            variance = f32_dot(ones, high, NT) + f32_dot(ones, low, NT)
+            spread = lax.rsqrt(variance + eps_norm)
+            raw = f32_dot(left, entries, NT)
+            bias = spread * (raw[:heads] + raw[heads : 2 * heads] + raw[2 * heads : 3 * heads])
+            bias_ref[:, i, :] = bias
+            mean_ref[pl.ds(i, 1), :] = raw[3 * heads : 3 * heads + 1]
+            spread_ref[pl.ds(i, 1), :] = spread[:1]
+        return carry
+
+    lax.fori_loop(0, pair_ref.shape[0] // 8, rows, 0)
+    half = residues // 2
+    for h in range(heads):
+        for core in range(2):
+            high, low = two_terms(bias_ref[h, core * half : (core + 1) * half, :])
+            out_ref[h * 2 + core, 2 * residues : 2 * residues + half, :] = high
+            out_ref[h * 2 + core, 2 * residues + half : 3 * residues, :] = low
+
+
+def lanes_of(blocks_ref, row, residues):
+    count = blocks_ref.shape[0] // 2
+    planes = [
+        blocks_ref[p * count : (p + 1) * count, row : row + residues, :].reshape(-1, LANES)
+        for p in range(2)
+    ]
+    return jnp.concatenate(planes, axis=1)
+
+
+def score_kernel(
+    residues, left_row, right_row, with_bias, place_ref, own_ref, other_ref, mine_ref, sent_ref
+):
+    core, half = place_ref[0], place_ref[1]
+    count = own_ref.shape[0] // 2
+    part = residues // 2
+    right = jnp.concatenate(
+        [lanes_of(own_ref, right_row, residues), lanes_of(other_ref, right_row, residues)], axis=1
+    )
+    for which, ref in ((half, mine_ref), (1 - half, sent_ref)):
+        left = []
+        for k in range(count // 2):
+            block = which * (count // 2) + k
+            rows = pl.ds(pl.multiple_of(left_row + core * part, part), part)
+            left.append(
+                jnp.concatenate(
+                    [
+                        r[p * count + block, rows, :]
+                        for r in (own_ref, other_ref)
+                        for p in range(2)
+                    ],
+                    axis=1,
+                )
+            )
+        ref[...] = f32_dot(jnp.concatenate(left, axis=0), right, NT).astype(ref.dtype)
+        if with_bias:
+            for p in range(2):
+                columns = pl.ds(pl.multiple_of((half * 2 + p) * LANES, LANES), LANES)
+                for k in range(count // 2):
+                    block = p * count + which * (count // 2) + k
+                    high = own_ref[block, 2 * residues : 2 * residues + part, :]
+                    low = own_ref[block, 2 * residues + part : 3 * residues, :]
+                    bias = high.astype(jnp.float32) + low.astype(jnp.float32)
+                    ref[k * part : (k + 1) * part, columns] += bias
+
+
+def softmax_kernel(logit_ref, logit_other_ref, grad_ref, grad_other_ref, prob_ref, out_ref):
+    logits = logit_ref[...] + logit_other_ref[...]
+    lifted = jnp.exp(logits - jnp.max(logits, axis=-1, keepdims=True))
+    softmax_out = lifted / jnp.sum(lifted, axis=-1, keepdims=True)
+    prob_ref[...] = softmax_out.astype(jnp.bfloat16)
+    grad_probs = grad_ref[...] + grad_other_ref[...].astype(jnp.float32)
+    row_dot = jnp.sum(softmax_out * grad_probs, axis=-1, keepdims=True)
+    out_ref[...] = (softmax_out * (grad_probs - row_dot)).astype(jnp.bfloat16)
+
+
+def product_kernel(
+    residues, scale, first_row, second_row, with_share,
+    place_ref, own_ref, far_ref, near_ref, corner_ref, blocks_ref, out_ref, whole_ref,
+):
+    core, half = place_ref[0], place_ref[1]
+    count = blocks_ref.shape[0] // 2
+    part = residues // 2
+    quarters = (
+        (own_ref, core, half), (far_ref, core, 1 - half),
+        (near_ref, 1 - core, half), (corner_ref, 1 - core, 1 - half),
+    )
+    for ref, c, z in quarters:
+        for k in range(count // 2):
+            start = (z * (count // 2) + k) * residues + c * part
+            whole_ref[pl.ds(pl.multiple_of(start, part), part), :] = ref[k * part : (k + 1) * part, :]
+    whole = whole_ref[...]
+    if with_share:
+        for p in range(2):
+            columns = pl.ds(pl.multiple_of((half * 2 + p) * LANES, LANES), LANES)
+            for q in range(count):
+                rows = pl.ds(pl.multiple_of(q * residues + core * part, part), part)
+                out_ref[p * count + q, 2 * residues : 2 * residues + part, :] = whole_ref[rows, columns]
+    first = f32_dot(whole, lanes_of(blocks_ref, first_row, residues)) * scale
+    second = f32_dot(whole, lanes_of(blocks_ref, second_row, residues), TN)
+    for row, product in ((0, first), (residues, second)):
+        for p in range(2):
+            out_ref[p * count : (p + 1) * count, row : row + residues, :] = (
+                product[:, p * LANES : (p + 1) * LANES]
+                .astype(jnp.bfloat16)
+                .reshape(count, residues, LANES)
+            )
+
+
+def gate_kernel(x_ref, grad_ref, wc_ref, wo_ref, blocks_ref, updated_ref, value_gate_ref, weight_ref):
+    residues, width = x_ref.shape[1], x_ref.shape[2]
+    tiles = width // LANES
+    normed = normalized(x_ref)[0].astype(jnp.bfloat16)
+    gate = gate_of(f32_dot(normed, wc_ref[:, 3 * width :]))
+    grad = grad_ref[...].reshape(-1, width)
+    grad_gated = f32_dot(grad, wo_ref[...], NT)
+    attended = unpack_heads(blocks_ref, 0, residues, tiles)
+    gated = (gate * attended).astype(jnp.bfloat16)
+    updated_ref[...] = f32_dot(gated, wo_ref[...]).astype(jnp.bfloat16).reshape(updated_ref.shape)
+    value_gate_ref[:, :width] = unpack_heads(blocks_ref, residues, residues, tiles).astype(
+        jnp.bfloat16
+    )
+    value_gate_ref[:, width:] = (grad_gated * attended * gate * (1.0 - gate)).astype(jnp.bfloat16)
+    weight_ref[:, : 2 * width] = f32_dot(normed, value_gate_ref[...], TN).astype(jnp.bfloat16)
+    weight_ref[:, 2 * width :] = f32_dot(gated, grad, TN).astype(jnp.bfloat16)
+
+
+def share_of(blocks_ref, row, part, heads):
+    return jnp.concatenate(
+        [
+            blocks_ref[:, row : row + part, :]
+            .astype(jnp.float32)
+            .reshape(heads, 2 * part, LANES)
+        ],
+        axis=0,
+    )
+
+
+def weight_kernel(
+    x_ref, blocks_ref, pair_ref, mean_ref, spread_ref, query_key_ref, weight_ref, share_ref
+):
+    residues, width = x_ref.shape[1], x_ref.shape[2]
+    tiles = width // LANES
+    heads = share_ref.shape[0]
+    part = residues // 2
+    share_ref[...] = share_of(blocks_ref, 2 * residues, part, heads)
+
+    def rows(step, carry):
+        total, shift = carry
+        for k in range(8):
+            i = step * 8 + k
+            scaled = share_ref[:, i, :] * spread_ref[pl.ds(i, 1), :]
+            high, low = two_terms(scaled)
+            total += f32_dot(jnp.concatenate([high, low], axis=0), pair_ref[i])
+            shift += (high.astype(jnp.float32) + low.astype(jnp.float32)) * mean_ref[pl.ds(i, 1), :]
+        return total, shift
+
+    channels = pair_ref.shape[2]
+    total, shift = lax.fori_loop(
+        0,
+        pair_ref.shape[0] // 8,
+        rows,
+        (jnp.zeros((2 * heads, channels), jnp.float32), jnp.zeros((heads, LANES), jnp.float32)),
+    )
+    pair_weight = total[:heads] + total[heads:] - jnp.sum(shift, axis=1, keepdims=True)
+    normed = normalized(x_ref)[0].astype(jnp.bfloat16)
+    for t in range(2):
+        query_key_ref[:, t * width : (t + 1) * width] = unpack_heads(
+            blocks_ref, t * residues, residues, tiles
+        ).astype(jnp.bfloat16)
+    weight_ref[:, : 2 * width] = f32_dot(normed, query_key_ref[...], TN).astype(jnp.bfloat16)
+    rows_each = weight_ref.shape[0] // heads
+    first = lax.broadcasted_iota(jnp.int32, (rows_each, channels), 0) == 0
+    for h in range(heads):
+        row = jnp.broadcast_to(pair_weight[h : h + 1], (rows_each, channels))
+        weight_ref[h * rows_each : (h + 1) * rows_each, 2 * width :] = jnp.where(
+            first, row, 0.0
+        ).astype(jnp.bfloat16)
+
+
+def alignment_kernel(x_ref, wc_ref, query_key_ref, value_gate_ref, out_ref):
+    width = x_ref.shape[2]
+    normed, spread = normalized(x_ref)
+    gradient = f32_dot(query_key_ref[...], wc_ref[:, : 2 * width], NT) + f32_dot(
+        value_gate_ref[...], wc_ref[:, 2 * width :], NT
+    )
+    out_ref[...] = (
+        layer_norm_backward(gradient, normed, spread).astype(jnp.bfloat16).reshape(out_ref.shape)
+    )
+
+
+def pair_kernel(blocks_row, blocks_ref, pair_ref, weight_ref, bias_ref, mean_ref, spread_ref, out_ref, share_ref):
+    heads, channels = weight_ref.shape
+    part = pair_ref.shape[0] // 2
+    share_ref[...] = share_of(blocks_ref, blocks_row, part, heads)
+    first, second = two_terms(weight_ref[...])
+    zero = jnp.zeros((heads, channels), jnp.bfloat16)
+    top = lax.broadcasted_iota(jnp.int32, (heads, channels), 0) < 2
+    ones = jnp.where(top, 1.0, 0.0).astype(jnp.bfloat16)
+    right = jnp.concatenate(
+        [
+            jnp.concatenate([first, first, second, ones, zero], axis=0),
+            jnp.concatenate([zero, zero, zero, zero, ones], axis=0),
+        ],
+        axis=1,
+    )
+    row = lax.broadcasted_iota(jnp.int32, (heads, LANES), 0)
+
+    def rows_of_two(value):
+        high, low = two_terms(value)
+        high, low = high.astype(jnp.float32), low.astype(jnp.float32)
+        return jnp.where(row == 0, high, jnp.where(row == 1, low, 0.0)).astype(jnp.bfloat16)
+
+    def rows(step, carry):
+        for k in range(8):
+            i = step * 8 + k
+            gradient = share_ref[:, i, :]
+            spread = spread_ref[pl.ds(i, 1), :]
+            cross = jnp.sum(gradient * bias_ref[:, i, :], axis=0, keepdims=True) / channels
+            slope = spread * spread * cross
+            high, low = two_terms(gradient * spread)
+            left = jnp.concatenate(
+                [
+                    high, low, high,
+                    rows_of_two(jnp.broadcast_to(slope * mean_ref[pl.ds(i, 1), :], row.shape)),
+                    rows_of_two(jnp.broadcast_to(slope, row.shape)),
+                ],
+                axis=0,
+            )
+            terms = f32_dot(left, right, TN)
+            entries = pair_ref[i].astype(jnp.float32)
+            out_ref[i] = (terms[:, :channels] - terms[:, channels:] * entries).astype(jnp.bfloat16)
+        return carry
+
+    lax.fori_loop(0, pair_ref.shape[0] // 8, rows, 0)
+
+
+def call(kernel, outs, *args, scratch=(), place=None, flops=0):
+    whole = pl.BlockSpec(memory_space=pltpu.VMEM)
+    specs = [whole] * len(args)
+    if place is not None:
+        specs = [pl.BlockSpec(memory_space=pltpu.SMEM)] + specs
+        args = (place,) + args
+    shapes = [jax.ShapeDtypeStruct(*o) for o in outs]
+    moved = sum(math.prod(a.shape) * a.dtype.itemsize for a in list(args) + shapes)
+    result = pl.pallas_call(
+        kernel,
+        out_shape=shapes,
+        in_specs=specs,
+        out_specs=[whole] * len(shapes),
+        scratch_shapes=scratch,
+        compiler_params=pltpu.CompilerParams(vmem_limit_bytes=VMEM_LIMIT),
+        cost_estimate=pl.CostEstimate(flops=flops, bytes_accessed=moved, transcendentals=0),
+    )(*args)
+    return result
+
+
+def swapped(mine, axis_name, distance):
+    size = lax.axis_size(axis_name)
+    return lax.ppermute(mine, axis_name, [(a, a ^ distance) for a in range(size)])
+
+
+def gathered_seq(mine):
+    size, index = lax.axis_size("seq"), lax.axis_index("seq")
+    rows = jnp.zeros((size,) + mine.shape, mine.dtype)
+    rows = lax.dynamic_update_index_in_dim(rows, mine, index, 0)
+    for k in range(1, size):
+        t = lax.ppermute(mine, "seq", [(a, (a + k) % size) for a in range(size)])
+        rows = lax.dynamic_update_index_in_dim(rows, t, (index - k) % size, 0)
+    return rows
+
+
+def summed_everywhere(parts):
+    size = lax.axis_size("res")
+    rows, columns = parts.shape
+    parts = lax.all_to_all(parts.reshape(size, rows // size, columns), "res", 0, 0, tiled=True)
+    part = jnp.sum(parts.astype(jnp.float32), axis=0).astype(jnp.bfloat16)
+    part = jnp.sum(gathered_seq(part).astype(jnp.float32), axis=0).astype(jnp.bfloat16)
+    return lax.all_gather(part, "res", axis=0)
+
+
+def fits_heads(alignment_rows, pair_entries, pair_weight):
+    channels, heads = pair_weight.shape
+    return (
+        lax.axis_size("seq") == 4
+        and lax.axis_size("res") == heads == 8
+        and alignment_rows.shape[0] == 2 * SLOTS
+        and alignment_rows.shape[1] == pair_entries.shape[0] == 64
+        and alignment_rows.shape[2] == 2 * LANES
+        and pair_entries.shape[1] == channels == LANES
+    )
+
+
+def head_body(
+    alignment_rows, pair_entries, combined_weight, output_weight, pair_weight, updated_gradient
+):
+    sequences, residues, width = alignment_rows.shape
+    channels, heads = pair_weight.shape
+    tokens = sequences * residues
+    seq_size, res_size = lax.axis_size("seq"), lax.axis_size("res")
+    seq_half = seq_size // 2
+    total = residues * res_size
+    group = 2 * res_size
+    groups = [[g * group + k for k in range(group)] for g in range(seq_half)]
+    scale = 1.0 / math.sqrt(width // heads * sequences * seq_size)
+    place = jnp.stack([lax.axis_index("res") % 2, lax.axis_index("seq") // 2]).astype(jnp.int32)
+    bf16, f32 = jnp.bfloat16, jnp.float32
+
+    def across(blocks):
+        return lax.all_to_all(blocks, ("seq", "res"), 0, 0, axis_index_groups=groups, tiled=True)
+
+    def all_quarters(mine):
+        far = swapped(mine, "seq", seq_half)
+        return mine, far, swapped(mine, "res", 1), swapped(far, "res", 1)
+
+    x, grad, wc, wo = alignment_rows, updated_gradient, combined_weight, output_weight
+    (value_blocks,) = call(
+        value_kernel, [((group, 2 * residues, LANES), bf16)], x, grad, wc, wo,
+        flops=8 * tokens * width * width,
+    )
+    value_blocks = across(value_blocks)
+    centred = (pair_weight - jnp.mean(pair_weight, axis=0, keepdims=True)).T
+    query_blocks, bias, mean, spread = call(
+        functools.partial(query_kernel, scale),
+        [
+            ((group, 3 * residues, LANES), bf16),
+            ((heads, residues, LANES), f32),
+            ((residues, LANES), f32),
+            ((residues, LANES), f32),
+        ],
+        x, wc, pair_entries, centred,
+        flops=8 * tokens * width * width,
+    )
+    query_blocks = across(query_blocks)
+
+    def scores(blocks, left_row, right_row, with_bias, kind):
+        return call(
+            functools.partial(score_kernel, residues, left_row, right_row, with_bias),
+            [((total // 4, total), f32), ((total // 4, total), kind)],
+            blocks, swapped(blocks, "res", 1),
+            place=place, flops=2 * total * total * width,
+        )
+
+    grad_mine, grad_sent = scores(value_blocks, residues, 0, False, bf16)
+    grad_other = swapped(grad_sent, "seq", seq_half)
+    logit_mine, logit_sent = scores(query_blocks, 0, residues, True, f32)
+    logit_other = swapped(logit_sent, "seq", seq_half)
+    quarter = ((total // 4, total), bf16)
+    probs, grad_logits = call(
+        softmax_kernel, [quarter, quarter], logit_mine, logit_other, grad_mine, grad_other,
+        flops=total * total,
+    )
+
+    def products(quarters, blocks, first_row, second_row, with_share, factor):
+        rows = 2 * residues + (residues // 2 if with_share else 0)
+        (out,) = call(
+            functools.partial(
+                product_kernel, residues, factor, first_row, second_row, with_share
+            ),
+            [((group, rows, LANES), bf16)],
+            *quarters, blocks,
+            scratch=[pltpu.VMEM((total, total), bf16)],
+            place=place, flops=4 * total * total * width,
+        )
+        return across(out)
+
+    attended_blocks = products(all_quarters(probs), value_blocks, 0, residues, False, 1.0)
+    grad_blocks = products(all_quarters(grad_logits), query_blocks, residues, 0, True, scale)
+
+    updated, value_gate, early = call(
+        gate_kernel,
+        [(x.shape, bf16), ((tokens, 2 * width), bf16), ((width, 3 * width), bf16)],
+        x, grad, wc, wo, attended_blocks,
+        flops=12 * tokens * width * width,
+    )
+    early = summed_everywhere(early)
+    query_key, late = call(
+        weight_kernel,
+        [((tokens, 2 * width), bf16), ((width, 2 * width + channels), bf16)],
+        x, grad_blocks, pair_entries, mean, spread,
+        scratch=[pltpu.VMEM((heads, residues, LANES), f32)],
+        flops=4 * tokens * width * width,
+    )
+    late = summed_everywhere(late)
+    (alignment_gradient,) = call(
+        alignment_kernel, [(x.shape, bf16)], x, wc, query_key, value_gate,
+        flops=8 * tokens * width * width,
+    )
+    (pair_gradient,) = call(
+        functools.partial(pair_kernel, 2 * residues),
+        [(pair_entries.shape, bf16)],
+        grad_blocks, pair_entries, centred, bias, mean, spread,
+        scratch=[pltpu.VMEM((heads, residues, LANES), f32)],
+        flops=8 * tokens * width * width,
+    )
+
+    combined_weight_gradient = (
+        jnp.concatenate([late[:, :, : 2 * width], early[:, :, : 2 * width]], axis=-1)
+        .reshape(wc.shape)
+        .astype(f32)
+    )
+    output_weight_gradient = early[:, :, 2 * width :].reshape(wo.shape).astype(f32)
+    pair_weight_gradient = late[:, 0, 2 * width :].T.astype(f32)
+    return (
+        updated,
+        alignment_gradient,
+        pair_gradient,
+        combined_weight_gradient,
+        output_weight_gradient,
+        pair_weight_gradient,
+    )
+
+
+def body(alignment_rows, pair_entries, combined_weight, output_weight, pair_weight, updated_gradient):
+    chosen = head_body if fits_heads(alignment_rows, pair_entries, pair_weight) else gathered_body
+    return chosen(
+        alignment_rows, pair_entries, combined_weight, output_weight, pair_weight, updated_gradient
     )
 
 

time: 431 us -> 182 us (0.42)
  waiting for transfers between devices: 260 us -> 72.4 us
  matrix products: 42.7 us -> 0 us
  starting transfers between devices: 0.6 us -> 39.8 us
  local copies, waits for them, and re-layouts: 44.8 us -> 13.3 us
  Pallas kernels: 0 us -> 30.3 us
  other arithmetic: 27.3 us -> 5.3 us
  blocking collectives: 39.7 us -> 18.9 us
  between operations: 14 us -> 0.98 us
    psum x2 -> x0, waiting for transfers between devices: 217 us -> none  [the longest x1 130 us: body(): lax.psum((qkvg_local, out_local, pair_w_local), ('seq', 'res'))]
    ppermute x0 -> x16, waiting for transfers between devices: none -> 43.6 us  [the longest x10 36.7 us: swapped(): lax.ppermute(mine, axis_name, [(a, a ^ distance) for a in range(size)])]
    dot_general x15 -> x0, matrix products: 42.7 us -> none  [the longest x1 4.64 us: body(): jnp.einsum('hij,sihd->jshd', softmax_low, attended_grad_heads, preferred_...]
    all_gather x2 -> x0, waiting for transfers between devices: 42.4 us -> none  [the longest x1 23.4 us: body(): lax.all_gather(value_rows, 'res', axis=1, tiled=True)]
    psum x1 -> x0, blocking collectives: 39.7 us -> none  [body(): lax.psum((qkvg_local, out_local, pair_w_local), ('seq', 'res'))]
    pallas_call x0 -> x11, Pallas kernels: none -> 30.3 us  [call(): pl.pallas_call(kernel, out_shape=shapes, in_specs=specs, out_specs=[whole...]
    all_to_all x0 -> x6, waiting for transfers between devices: none -> 28.8 us  [the longest x4 28.8 us: across(): lax.all_to_all(blocks, ('seq', 'res'), 0, 0, axis_index_groups=groups, ti...]
    all_to_all x0 -> x6, starting transfers between devices: none -> 26.3 us  [the longest x4 18.2 us: across(): lax.all_to_all(blocks, ('seq', 'res'), 0, 0, axis_index_groups=groups, ti...]
  transfers between devices with their start and end apart: 5 -> 22, of which waited for: 4 -> 14; matrix products, arithmetic and copies ran while one was open for 13% -> 1% of each run, Pallas kernels for 0% -> 8%
where the time goes in v3:
time: 182 us; the launch traced here: 181 us
  waiting for transfers between devices  72.4 us (40%)
  starting transfers between devices  39.8 us (22%)
  Pallas kernels  30.3 us (17%)
  blocking collectives  18.9 us (10%)
  local copies, waits for them, and re-layouts  13.3 us (7%)
  other arithmetic  5.3 us (3%)
    ppermute x10, waiting for transfers between devices, swapped(): lax.ppermute(mine, axis_name, [(a, a ^ distance) for a in range(size)])  36.7 us
    pallas_call x11, Pallas kernels, call(): pl.pallas_call(kernel, out_shape=shapes, in_specs=specs, out_specs=[whole...  30.3 us
    all_to_all x4, waiting for transfers between devices, across(): lax.all_to_all(blocks, ('seq', 'res'), 0, 0, axis_index_groups=groups, ti...  28.8 us
    all_gather x2, blocking collectives, summed_everywhere(): return lax.all_gather(part, 'res', axis=0)  18.9 us
    all_to_all x4, starting transfers between devices, across(): lax.all_to_all(blocks, ('seq', 'res'), 0, 0, axis_index_groups=groups, ti...  18.2 us
    unnamed x44, local copies, waits for them, and re-layouts  13.2 us
    ppermute x6, starting transfers between devices, gathered_seq(): t = lax.ppermute(mine, 'seq', [(a, (a + k) % size) for a in range(size)])  9.14 us
    all_to_all x2, starting transfers between devices, summed_everywhere(): lax.all_to_all(parts.reshape(size, rows // size, columns), 'res', 0, 0, t...  8.12 us
  transfers between devices with their start and end apart: 22, of which 14 were waited for; matrix products, arithmetic and copies ran while one was open for 1% of the time, Pallas kernels for 8%

profile of v3, /device:TPU:0, one launch (start us, length us, event | category | flops | bytes accessed | tf_op | source)
XLA Modules:
  0.0 180.9 jit_solution(7634900324292267007)
XLA Ops:
  5.8 13.6 %shard_map.109 = (bf16[16,192,128]{2,1,0:T(8,128)(2,1)}, f32[8,64,128]{2,1,0:T(8,128)S(1)}, f32[64,128]{1,0:T(8,128)S(1)}, f32[64,128]{1,0:T(8,128)S(1)}) custom-call(bf16[8,64,256]{2,1,0:T(8,128)(2,1)S(1)} %copy-done.4, bf16[256,1024]{1,0:T(8,128)(2,1)S(1)} %copy-done.2, bf16[64,128,128]{2,1,0:T(8,128)(2,1)S(1)} %copy-done, ...), custom_call_target="tpu_custom_call" | custom-call | flops 268435456 | bytes 4001792 | tf_op jit(solution)/shard_map/pallas_call | solution.py:500
  21.4 6.3 %all-to-all-start = ((bf16[16,192,128]{2,1,0:T(8,128)(2,1)}), bf16[16,192,128]{2,1,0:T(8,128)(2,1)S(1)}, u32[]{:S(2)}, u32[]{:S(2)}) async-start(bf16[16,192,128]{2,1,0:T(8,128)(2,1)} %get-tuple-element.21), calls=%async_computation | async-start | bytes 1572864 | tf_op jit(solution)/shard_map/all_to_all | solution.py:564
  29.2 11.8 %all-to-all-done.own_ref.blocks_ref = bf16[16,192,128]{2,1,0:T(8,128)(2,1)S(1)} async-done(((bf16[16,192,128]{2,1,0:T(8,128)(2,1)}), bf16[16,192,128]{2,1,0:T(8,128)(2,1)S(1)}, u32[]{:S(2)}, u32[]{:S(2)}) %all-to-all-start) | async-done | bytes 786464 | tf_op jit(solution)/shard_map/all_to_all | solution.py:564
  41.0 3.6 %all-to-all-start.1 = ((bf16[16,128,128]{2,1,0:T(8,128)(2,1)}), bf16[16,128,128]{2,1,0:T(8,128)(2,1)S(1)}, u32[]{:S(2)}, u32[]{:S(2)}) async-start(bf16[16,128,128]{2,1,0:T(8,128)(2,1)} %shard_map.111), calls=%async_computation.1 | async-start | bytes 1048576 | tf_op jit(solution)/shard_map/all_to_all | solution.py:564
  44.9 10.2 %all-to-all-done.1.own_ref.blocks_ref = bf16[16,128,128]{2,1,0:T(8,128)(2,1)S(1)} async-done(((bf16[16,128,128]{2,1,0:T(8,128)(2,1)}), bf16[16,128,128]{2,1,0:T(8,128)(2,1)S(1)}, u32[]{:S(2)}, u32[]{:S(2)}) %all-to-all-start.1) | async-done | bytes 524320 | tf_op jit(solution)/shard_map/all_to_all | solution.py:564
  56.2 2.7 %collective-permute-start.1 = (f32[128,512]{1,0:T(8,128)S(1)}, f32[128,512]{1,0:T(8,128)S(1)}, u32[]{:S(2)}, u32[]{:S(2)}) collective-permute-start(f32[128,512]{1,0:T(8,128)S(1)} %get-tuple-element.23), channel_id=1, source_target_pairs={{0,16},{8,24},{16,0},{24,8},{1,17},{9,25},{17,1},{25,9},{2,18},{10... | collective-permute-start | bytes 786440 | tf_op jit(solution)/shard_map/ppermute | solution.py:514
  60.7 16.4 %collective-permute-done.3.grad_other_ref = bf16[128,512]{1,0:T(8,128)(2,1)S(1)} collective-permute-done((bf16[128,512]{1,0:T(8,128)(2,1)S(1)}, bf16[128,512]{1,0:T(8,128)(2,1)S(1)}, u32[]{:S(2)}, u32[]{:S(2)}) %collective-permute-start.3) | collective-permute-done | bytes 131104 | tf_op jit(solution)/shard_map/ppermute | solution.py:514
  77.7 8.6 %collective-permute-done.4.far_ref = bf16[128,512]{1,0:T(8,128)(2,1)S(1)} collective-permute-done((bf16[128,512]{1,0:T(8,128)(2,1)S(1)}, bf16[128,512]{1,0:T(8,128)(2,1)S(1)}, u32[]{:S(2)}, u32[]{:S(2)}) %collective-permute-start.4) | collective-permute-done | bytes 131104 | tf_op jit(solution)/shard_map/ppermute | solution.py:514
  87.7 1.8 %shard_map.114 = bf16[16,128,128]{2,1,0:T(8,128)(2,1)} custom-call(s32[2]{0:T(128)S(1)} %pad_add_fusion.place_ref, bf16[128,512]{1,0:T(8,128)(2,1)S(1)} %get-tuple-element.26.own_ref, bf16[128,512]{1,0:T(8,128)(2,1)S(1)} %collective-permute-done.4.far_ref, bf16[128,512]{1,0:T(8,128)(2,1)S(1)} %collective-permute-done.5.near_ref, ...), custom_call_target="tpu_custom_call" | custom-call | flops 268435456 | bytes 1572872 | tf_op jit(solution)/shard_map/pallas_call | solution.py:500
  89.5 3.6 %all-to-all-start.2 = ((bf16[16,128,128]{2,1,0:T(8,128)(2,1)}), bf16[16,128,128]{2,1,0:T(8,128)(2,1)S(1)}, u32[]{:S(2)}, u32[]{:S(2)}) async-start(bf16[16,128,128]{2,1,0:T(8,128)(2,1)} %shard_map.114), calls=%async_computation.2 | async-start | bytes 1048576 | tf_op jit(solution)/shard_map/all_to_all | solution.py:564
  93.4 8.9 %collective-permute-done.7.far_ref = bf16[128,512]{1,0:T(8,128)(2,1)S(1)} collective-permute-done((bf16[128,512]{1,0:T(8,128)(2,1)S(1)}, bf16[128,512]{1,0:T(8,128)(2,1)S(1)}, u32[]{:S(2)}, u32[]{:S(2)}) %collective-permute-start.7) | collective-permute-done | bytes 131104 | tf_op jit(solution)/shard_map/ppermute | solution.py:514
  107.2 4.7 %all-to-all-start.3 = ((bf16[16,160,128]{2,1,0:T(8,128)(2,1)}), bf16[16,160,128]{2,1,0:T(8,128)(2,1)S(1)}, u32[]{:S(2)}, u32[]{:S(2)}) async-start(bf16[16,160,128]{2,1,0:T(8,128)(2,1)} %copy-done.6), calls=%async_computation.3 | async-start | bytes 1310720 | tf_op jit(solution)/shard_map/all_to_all | solution.py:564
  117.9 6.0 %all-to-all-done.3.blocks_ref = bf16[16,160,128]{2,1,0:T(8,128)(2,1)S(1)} async-done(((bf16[16,160,128]{2,1,0:T(8,128)(2,1)}), bf16[16,160,128]{2,1,0:T(8,128)(2,1)S(1)}, u32[]{:S(2)}, u32[]{:S(2)}) %all-to-all-start.3) | async-done | bytes 655392 | tf_op jit(solution)/shard_map/all_to_all | solution.py:564
  123.9 4.1 %all-to-all-start.5 = ((bf16[8,32,768]{2,1,0:T(8,128)(2,1)}), bf16[8,32,768]{2,1,0:T(8,128)(2,1)}, u32[]{:S(2)}, u32[]{:S(2)}) async-start(bf16[8,32,768]{2,1,0:T(8,128)(2,1)} %bitcast.33), calls=%async_computation.5 | async-start | bytes 786432 | tf_op jit(solution)/shard_map/all_to_all | solution.py:530
  129.6 2.9 %shard_map.117 = (bf16[512,512]{1,0:T(8,128)(2,1)S(1)}, bf16[256,640]{1,0:T(8,128)(2,1)}) custom-call(bf16[8,64,256]{2,1,0:T(8,128)(2,1)S(1)} %copy-done.5, bf16[16,160,128]{2,1,0:T(8,128)(2,1)S(1)} %all-to-all-done.3.blocks_ref, bf16[64,128,128]{2,1,0:T(8,128)(2,1)S(1)} %copy-done.1, f32[64,128]{1,0:T(8,128)S(1)} %copy-done.19, f32[64,128]{1,0:T(8,128)S(1)} %copy-done.21), custom_call_target="tpu_custom_call" | custom-call | flops 134217728 | bytes 3932160 | tf_op jit(solution)/shard_map/pallas_call | solution.py:500
  133.8 4.2 %shard_map.119 = bf16[64,128,128]{2,1,0:T(8,128)(2,1)} custom-call(bf16[16,160,128]{2,1,0:T(8,128)(2,1)S(1)} %all-to-all-done.3.blocks_ref, bf16[64,128,128]{2,1,0:T(8,128)(2,1)S(1)} %copy-done.1, f32[8,128]{1,0:T(8,128)S(1)} %subtract_bitcast_fusion.weight_ref, f32[8,64,128]{2,1,0:T(8,128)S(1)} %copy-done.17, f32[64,128]{1,0:T(8,128)S(1)} %copy-done.19, ...), custom_call_target="tpu_custom_call" | custom-call | flops 268435456 | bytes 5181440 | tf_op jit(solution)/shard_map/pallas_call | solution.py:500
  138.1 4.0 %all-to-all-start.4 = ((bf16[8,32,640]{2,1,0:T(8,128)(2,1)}), bf16[8,32,640]{2,1,0:T(8,128)(2,1)S(1)}, u32[]{:S(2)}, u32[]{:S(2)}) async-start(bf16[8,32,640]{2,1,0:T(8,128)(2,1)} %bitcast.3), calls=%async_computation.4 | async-start | bytes 655360 | tf_op jit(solution)/shard_map/all_to_all | solution.py:530
  143.8 2.0 %collective-permute-start.14 = (bf16[32,768]{1,0:T(8,128)(2,1)S(1)}, bf16[32,768]{1,0:T(8,128)(2,1)S(1)}, u32[]{:S(2)}, u32[]{:S(2)}) collective-permute-start(bf16[32,768]{1,0:T(8,128)(2,1)S(1)} %reduce_sum.60), channel_id=1, source_target_pairs={{0,16},{8,24},{16,0},{24,8},{1,17},{9,25},{17,1},{25,9},{2,18},{10... | collective-permute-start | bytes 147464 | tf_op jit(solution)/shard_map/ppermute | solution.py:522
  145.8 2.4 %collective-permute-start.15 = (bf16[32,768]{1,0:T(8,128)(2,1)S(1)}, bf16[32,768]{1,0:T(8,128)(2,1)S(1)}, u32[]{:S(2)}, u32[]{:S(2)}) collective-permute-start(bf16[32,768]{1,0:T(8,128)(2,1)S(1)} %reduce_sum.60), channel_id=1, source_target_pairs={{0,24},{8,0},{16,8},{24,16},{1,25},{9,1},{17,9},{25,17},{2,26},{10... | collective-permute-start | bytes 147464 | tf_op jit(solution)/shard_map/ppermute | solution.py:522
  149.5 1.7 collective-permute-done.14
  151.2 9.5 %all-gather.1 = bf16[256,768]{1,0:T(8,128)(2,1)S(1)} all-gather(bf16[32,768]{1,0:T(8,128)(2,1)S(1)} %reduce_sum.61), channel_id=3, replica_groups=mesh['seq'=4,'res'=8] {'res'}, dimensions={0}, use_global_device_ids=true | all-gather | bytes 442368 | tf_op jit(solution)/shard_map/all_gather | solution.py:533
  163.0 2.6 %collective-permute-start.11 = (bf16[32,640]{1,0:T(8,128)(2,1)S(1)}, bf16[32,640]{1,0:T(8,128)(2,1)S(1)}, u32[]{:S(2)}, u32[]{:S(2)}) collective-permute-start(bf16[32,640]{1,0:T(8,128)(2,1)S(1)} %reduce_sum.58), channel_id=1, source_target_pairs={{0,16},{8,24},{16,0},{24,8},{1,17},{9,25},{17,1},{25,9},{2,18},{10... | collective-permute-start | bytes 122888 | tf_op jit(solution)/shard_map/ppermute | solution.py:522
  165.7 2.0 %collective-permute-done.10 = bf16[32,640]{1,0:T(8,128)(2,1)S(1)} collective-permute-done((bf16[32,640]{1,0:T(8,128)(2,1)S(1)}, bf16[32,640]{1,0:T(8,128)(2,1)S(1)}, u32[]{:S(2)}, u32[]{:S(2)}) %collective-permute-start.10) | collective-permute-done | bytes 40992 | tf_op jit(solution)/shard_map/ppermute | solution.py:522
  169.7 9.4 %all-gather = bf16[256,640]{1,0:T(8,128)(2,1)S(1)} all-gather(bf16[32,640]{1,0:T(8,128)(2,1)S(1)} %reduce_sum.59), channel_id=2, replica_groups=mesh['seq'=4,'res'=8] {'res'}, dimensions={0}, use_global_device_ids=true | all-gather | bytes 368640 | tf_op jit(solution)/shard_map/all_gather | solution.py:533
  (102 shorter events, 36.8 us)
Async XLA Ops:
  5.8 21.9 %copy-start.13 = (bf16[256,256]{1,0:T(8,128)(2,1)S(1)}, bf16[256,256]{1,0:T(8,128)(2,1)}, u32[]{:S(2)}) copy-start(bf16[256,256]{1,0:T(8,128)(2,1)} %wo_ref.3) | copy-start | bytes 393220
  21.4 19.7 %all-to-all-start = ((bf16[16,192,128]{2,1,0:T(8,128)(2,1)}), bf16[16,192,128]{2,1,0:T(8,128)(2,1)S(1)}, u32[]{:S(2)}, u32[]{:S(2)}) async-start(bf16[16,192,128]{2,1,0:T(8,128)(2,1)} %get-tuple-element.21), calls=%async_computation | async-start | bytes 1572864 | tf_op jit(solution)/shard_map/all_to_all | solution.py:564
  41.0 14.1 %all-to-all-start.1 = ((bf16[16,128,128]{2,1,0:T(8,128)(2,1)}), bf16[16,128,128]{2,1,0:T(8,128)(2,1)S(1)}, u32[]{:S(2)}, u32[]{:S(2)}) async-start(bf16[16,128,128]{2,1,0:T(8,128)(2,1)} %shard_map.111), calls=%async_computation.1 | async-start | bytes 1048576 | tf_op jit(solution)/shard_map/all_to_all | solution.py:564
  44.6 10.6 %collective-permute-start = (bf16[16,192,128]{2,1,0:T(8,128)(2,1)S(1)}, bf16[16,192,128]{2,1,0:T(8,128)(2,1)S(1)}, u32[]{:S(2)}, u32[]{:S(2)}) collective-permute-start(bf16[16,192,128]{2,1,0:T(8,128)(2,1)S(1)} %all-to-all-done.own_ref.blocks_ref), channel_id=1, source_target_pairs={{0,1},{1,0},{2,3},{3,2},{4,5},{5,4},{6,7},{7,6},{8,9},{9,8},{10,11... | collective-permute-start | bytes 2359304 | tf_op jit(solution)/shard_map/ppermute | solution.py:514
  55.1 3.8 %collective-permute-start.2 = (bf16[16,128,128]{2,1,0:T(8,128)(2,1)S(1)}, bf16[16,128,128]{2,1,0:T(8,128)(2,1)S(1)}, u32[]{:S(2)}, u32[]{:S(2)}) collective-permute-start(bf16[16,128,128]{2,1,0:T(8,128)(2,1)S(1)} %all-to-all-done.1.own_ref.blocks_ref), channel_id=1, source_target_pairs={{0,1},{1,0},{2,3},{3,2},{4,5},{5,4},{6,7},{7,6},{8,9},{9,8},{10,11... | collective-permute-start | bytes 1572872 | tf_op jit(solution)/shard_map/ppermute | solution.py:514
  56.2 20.9 %collective-permute-start.1 = (f32[128,512]{1,0:T(8,128)S(1)}, f32[128,512]{1,0:T(8,128)S(1)}, u32[]{:S(2)}, u32[]{:S(2)}) collective-permute-start(f32[128,512]{1,0:T(8,128)S(1)} %get-tuple-element.23), channel_id=1, source_target_pairs={{0,16},{8,24},{16,0},{24,8},{1,17},{9,25},{17,1},{25,9},{2,18},{10... | collective-permute-start | bytes 786440 | tf_op jit(solution)/shard_map/ppermute | solution.py:514
  59.9 17.2 %collective-permute-start.3 = (bf16[128,512]{1,0:T(8,128)(2,1)S(1)}, bf16[128,512]{1,0:T(8,128)(2,1)S(1)}, u32[]{:S(2)}, u32[]{:S(2)}) collective-permute-start(bf16[128,512]{1,0:T(8,128)(2,1)S(1)} %get-tuple-element.25), channel_id=1, source_target_pairs={{0,16},{8,24},{16,0},{24,8},{1,17},{9,25},{17,1},{25,9},{2,18},{10... | collective-permute-start | bytes 393224 | tf_op jit(solution)/shard_map/ppermute | solution.py:514
  77.4 8.9 %collective-permute-start.4 = (bf16[128,512]{1,0:T(8,128)(2,1)S(1)}, bf16[128,512]{1,0:T(8,128)(2,1)S(1)}, u32[]{:S(2)}, u32[]{:S(2)}) collective-permute-start(bf16[128,512]{1,0:T(8,128)(2,1)S(1)} %get-tuple-element.26.own_ref), channel_id=1, source_target_pairs={{0,16},{8,24},{16,0},{24,8},{1,17},{9,25},{17,1},{25,9},{2,18},{10... | collective-permute-start | bytes 393224 | tf_op jit(solution)/shard_map/ppermute | solution.py:514
  77.5 8.8 %collective-permute-start.5 = (bf16[128,512]{1,0:T(8,128)(2,1)S(1)}, bf16[128,512]{1,0:T(8,128)(2,1)S(1)}, u32[]{:S(2)}, u32[]{:S(2)}) collective-permute-start(bf16[128,512]{1,0:T(8,128)(2,1)S(1)} %get-tuple-element.26.own_ref), channel_id=1, source_target_pairs={{0,1},{1,0},{2,3},{3,2},{4,5},{5,4},{6,7},{7,6},{8,9},{9,8},{10,11... | collective-permute-start | bytes 393224 | tf_op jit(solution)/shard_map/ppermute | solution.py:514
  86.3 1.3 collective-permute-start.6
  89.5 16.9 %all-to-all-start.2 = ((bf16[16,128,128]{2,1,0:T(8,128)(2,1)}), bf16[16,128,128]{2,1,0:T(8,128)(2,1)S(1)}, u32[]{:S(2)}, u32[]{:S(2)}) async-start(bf16[16,128,128]{2,1,0:T(8,128)(2,1)} %shard_map.114), calls=%async_computation.2 | async-start | bytes 1048576 | tf_op jit(solution)/shard_map/all_to_all | solution.py:564
  93.1 9.3 %collective-permute-start.7 = (bf16[128,512]{1,0:T(8,128)(2,1)S(1)}, bf16[128,512]{1,0:T(8,128)(2,1)S(1)}, u32[]{:S(2)}, u32[]{:S(2)}) collective-permute-start(bf16[128,512]{1,0:T(8,128)(2,1)S(1)} %get-tuple-element.28.own_ref), channel_id=1, source_target_pairs={{0,16},{8,24},{16,0},{24,8},{1,17},{9,25},{17,1},{25,9},{2,18},{10... | collective-permute-start | bytes 393224 | tf_op jit(solution)/shard_map/ppermute | solution.py:514
  93.1 9.2 %collective-permute-start.8 = (bf16[128,512]{1,0:T(8,128)(2,1)S(1)}, bf16[128,512]{1,0:T(8,128)(2,1)S(1)}, u32[]{:S(2)}, u32[]{:S(2)}) collective-permute-start(bf16[128,512]{1,0:T(8,128)(2,1)S(1)} %get-tuple-element.28.own_ref), channel_id=1, source_target_pairs={{0,1},{1,0},{2,3},{3,2},{4,5},{5,4},{6,7},{7,6},{8,9},{9,8},{10,11... | collective-permute-start | bytes 393224 | tf_op jit(solution)/shard_map/ppermute | solution.py:514
  102.4 1.3 collective-permute-start.9
  105.6 22.4 %copy-start.1 = (bf16[64,128,128]{2,1,0:T(8,128)(2,1)S(1)}, bf16[64,128,128]{2,1,0:T(8,128)(2,1)}, u32[]{:S(2)}) copy-start(bf16[64,128,128]{2,1,0:T(8,128)(2,1)} %pair_ref.5) | copy-start | bytes 6291460
  107.2 16.7 %all-to-all-start.3 = ((bf16[16,160,128]{2,1,0:T(8,128)(2,1)}), bf16[16,160,128]{2,1,0:T(8,128)(2,1)S(1)}, u32[]{:S(2)}, u32[]{:S(2)}) async-start(bf16[16,160,128]{2,1,0:T(8,128)(2,1)} %copy-done.6), calls=%async_computation.3 | async-start | bytes 1310720 | tf_op jit(solution)/shard_map/all_to_all | solution.py:564
  123.9 14.2 %all-to-all-start.5 = ((bf16[8,32,768]{2,1,0:T(8,128)(2,1)}), bf16[8,32,768]{2,1,0:T(8,128)(2,1)}, u32[]{:S(2)}, u32[]{:S(2)}) async-start(bf16[8,32,768]{2,1,0:T(8,128)(2,1)} %bitcast.33), calls=%async_computation.5 | async-start | bytes 786432 | tf_op jit(solution)/shard_map/all_to_all | solution.py:530
  138.1 23.4 %all-to-all-start.4 = ((bf16[8,32,640]{2,1,0:T(8,128)(2,1)}), bf16[8,32,640]{2,1,0:T(8,128)(2,1)S(1)}, u32[]{:S(2)}, u32[]{:S(2)}) async-start(bf16[8,32,640]{2,1,0:T(8,128)(2,1)} %bitcast.3), calls=%async_computation.4 | async-start | bytes 655360 | tf_op jit(solution)/shard_map/all_to_all | solution.py:530
  143.2 6.3 %collective-permute-start.13 = (bf16[32,768]{1,0:T(8,128)(2,1)S(1)}, bf16[32,768]{1,0:T(8,128)(2,1)S(1)}, u32[]{:S(2)}, u32[]{:S(2)}) collective-permute-start(bf16[32,768]{1,0:T(8,128)(2,1)S(1)} %reduce_sum.60), channel_id=1, source_target_pairs={{0,8},{8,16},{16,24},{24,0},{1,9},{9,17},{17,25},{25,1},{2,10},{10... | collective-permute-start | bytes 147464 | tf_op jit(solution)/shard_map/ppermute | solution.py:522
  143.8 7.4 %collective-permute-start.14 = (bf16[32,768]{1,0:T(8,128)(2,1)S(1)}, bf16[32,768]{1,0:T(8,128)(2,1)S(1)}, u32[]{:S(2)}, u32[]{:S(2)}) collective-permute-start(bf16[32,768]{1,0:T(8,128)(2,1)S(1)} %reduce_sum.60), channel_id=1, source_target_pairs={{0,16},{8,24},{16,0},{24,8},{1,17},{9,25},{17,1},{25,9},{2,18},{10... | collective-permute-start | bytes 147464 | tf_op jit(solution)/shard_map/ppermute | solution.py:522
  145.8 5.4 %collective-permute-start.15 = (bf16[32,768]{1,0:T(8,128)(2,1)S(1)}, bf16[32,768]{1,0:T(8,128)(2,1)S(1)}, u32[]{:S(2)}, u32[]{:S(2)}) collective-permute-start(bf16[32,768]{1,0:T(8,128)(2,1)S(1)} %reduce_sum.60), channel_id=1, source_target_pairs={{0,24},{8,0},{16,8},{24,16},{1,25},{9,1},{17,9},{25,17},{2,26},{10... | collective-permute-start | bytes 147464 | tf_op jit(solution)/shard_map/ppermute | solution.py:522
  161.5 6.2 %collective-permute-start.10 = (bf16[32,640]{1,0:T(8,128)(2,1)S(1)}, bf16[32,640]{1,0:T(8,128)(2,1)S(1)}, u32[]{:S(2)}, u32[]{:S(2)}) collective-permute-start(bf16[32,640]{1,0:T(8,128)(2,1)S(1)} %reduce_sum.58), channel_id=1, source_target_pairs={{0,8},{8,16},{16,24},{24,0},{1,9},{9,17},{17,25},{25,1},{2,10},{10... | collective-permute-start | bytes 122888 | tf_op jit(solution)/shard_map/ppermute | solution.py:522
  163.0 6.0 %collective-permute-start.11 = (bf16[32,640]{1,0:T(8,128)(2,1)S(1)}, bf16[32,640]{1,0:T(8,128)(2,1)S(1)}, u32[]{:S(2)}, u32[]{:S(2)}) collective-permute-start(bf16[32,640]{1,0:T(8,128)(2,1)S(1)} %reduce_sum.58), channel_id=1, source_target_pairs={{0,16},{8,24},{16,0},{24,8},{1,17},{9,25},{17,1},{25,9},{2,18},{10... | collective-permute-start | bytes 122888 | tf_op jit(solution)/shard_map/ppermute | solution.py:522
  165.6 4.0 %collective-permute-start.12 = (bf16[32,640]{1,0:T(8,128)(2,1)S(1)}, bf16[32,640]{1,0:T(8,128)(2,1)S(1)}, u32[]{:S(2)}, u32[]{:S(2)}) collective-permute-start(bf16[32,640]{1,0:T(8,128)(2,1)S(1)} %reduce_sum.58), channel_id=1, source_target_pairs={{0,24},{8,0},{16,8},{24,16},{1,25},{9,1},{17,9},{25,17},{2,26},{10... | collective-permute-start | bytes 122888 | tf_op jit(solution)/shard_map/ppermute | solution.py:522
  (20 other events, 87.6 us)

commit v4 on v3

--- a/solution.py
+++ b/solution.py
@@ -223,9 +223,10 @@
     return 1.0 / (1.0 + jnp.exp(-logits))
 
 
-def value_kernel(x_ref, grad_ref, wc_ref, wo_ref, out_ref):
+def value_kernel(x_ref, grad_ref, wc_ref, wo_ref, out_ref, normed_ref):
     residues, width = x_ref.shape[1], x_ref.shape[2]
     normed = normalized(x_ref)[0].astype(jnp.bfloat16)
+    normed_ref[...] = normed.reshape(normed_ref.shape)
     values = f32_dot(normed, wc_ref[:, 2 * width : 3 * width])
     gate = gate_of(f32_dot(normed, wc_ref[:, 3 * width :]))
     grad_gated = f32_dot(grad_ref[...].reshape(-1, width), wo_ref[...], NT)
@@ -233,10 +234,10 @@
     pack_heads(out_ref, residues, grad_gated * gate, residues)
 
 
-def query_kernel(scale, x_ref, wc_ref, pair_ref, weight_ref, out_ref, bias_ref, mean_ref, spread_ref):
-    residues, width = x_ref.shape[1], x_ref.shape[2]
+def query_kernel(scale, normed_ref, wc_ref, pair_ref, weight_ref, out_ref, bias_ref, mean_ref, spread_ref):
+    residues, width = normed_ref.shape[1], normed_ref.shape[2]
     heads = weight_ref.shape[0]
-    normed = normalized(x_ref)[0].astype(jnp.bfloat16)
+    normed = normed_ref[...].reshape(-1, width)
     pack_heads(out_ref, 0, f32_dot(normed, wc_ref[:, :width]) * scale, residues)
     pack_heads(out_ref, residues, f32_dot(normed, wc_ref[:, width : 2 * width]), residues)
 
@@ -318,7 +319,15 @@
                     ref[k * part : (k + 1) * part, columns] += bias
 
 
-def softmax_kernel(logit_ref, logit_other_ref, grad_ref, grad_other_ref, prob_ref, out_ref):
+def split_kernel(place_ref, normed_ref, grad_ref, after_ref, keep_ref, send_ref):
+    core = place_ref[0]
+    for which, ref in ((core, keep_ref), (1 - core, send_ref)):
+        for s in range(SLOTS):
+            ref[0, s] = normed_ref[which * SLOTS + s]
+            ref[1, s] = grad_ref[which * SLOTS + s]
+
+
+def softmax_kernel(logit_ref, logit_other_ref, grad_ref, grad_other_ref, out_ref, prob_ref):
     logits = logit_ref[...] + logit_other_ref[...]
     lifted = jnp.exp(logits - jnp.max(logits, axis=-1, keepdims=True))
     softmax_out = lifted / jnp.sum(lifted, axis=-1, keepdims=True)
@@ -361,24 +370,6 @@
             )
 
 
-def gate_kernel(x_ref, grad_ref, wc_ref, wo_ref, blocks_ref, updated_ref, value_gate_ref, weight_ref):
-    residues, width = x_ref.shape[1], x_ref.shape[2]
-    tiles = width // LANES
-    normed = normalized(x_ref)[0].astype(jnp.bfloat16)
-    gate = gate_of(f32_dot(normed, wc_ref[:, 3 * width :]))
-    grad = grad_ref[...].reshape(-1, width)
-    grad_gated = f32_dot(grad, wo_ref[...], NT)
-    attended = unpack_heads(blocks_ref, 0, residues, tiles)
-    gated = (gate * attended).astype(jnp.bfloat16)
-    updated_ref[...] = f32_dot(gated, wo_ref[...]).astype(jnp.bfloat16).reshape(updated_ref.shape)
-    value_gate_ref[:, :width] = unpack_heads(blocks_ref, residues, residues, tiles).astype(
-        jnp.bfloat16
-    )
-    value_gate_ref[:, width:] = (grad_gated * attended * gate * (1.0 - gate)).astype(jnp.bfloat16)
-    weight_ref[:, : 2 * width] = f32_dot(normed, value_gate_ref[...], TN).astype(jnp.bfloat16)
-    weight_ref[:, 2 * width :] = f32_dot(gated, grad, TN).astype(jnp.bfloat16)
-
-
 def share_of(blocks_ref, row, part, heads):
     return jnp.concatenate(
         [
@@ -390,14 +381,83 @@
     )
 
 
-def weight_kernel(
-    x_ref, blocks_ref, pair_ref, mean_ref, spread_ref, query_key_ref, weight_ref, share_ref
-):
+def final_kernel(x_ref, grad_ref, wc_ref, wo_ref, attended_ref, blocks_ref, updated_ref, out_ref):
     residues, width = x_ref.shape[1], x_ref.shape[2]
     tiles = width // LANES
-    heads = share_ref.shape[0]
-    part = residues // 2
-    share_ref[...] = share_of(blocks_ref, 2 * residues, part, heads)
+    normed, spread = normalized(x_ref)
+    gate = gate_of(f32_dot(normed.astype(jnp.bfloat16), wc_ref[:, 3 * width :]))
+    grad_gated = f32_dot(grad_ref[...].reshape(-1, width), wo_ref[...], NT)
+    attended = unpack_heads(attended_ref, 0, residues, tiles)
+    gated = (gate * attended).astype(jnp.bfloat16)
+    updated_ref[...] = f32_dot(gated, wo_ref[...]).astype(jnp.bfloat16).reshape(updated_ref.shape)
+    parts = [
+        unpack_heads(blocks_ref, 0, residues, tiles),
+        unpack_heads(blocks_ref, residues, residues, tiles),
+        unpack_heads(attended_ref, residues, residues, tiles),
+        grad_gated * attended * gate * (1.0 - gate),
+    ]
+    gradient = f32_dot(
+        jnp.concatenate([p.astype(jnp.bfloat16) for p in parts], axis=1), wc_ref[...], NT
+    )
+    out_ref[...] = (
+        layer_norm_backward(gradient, normed, spread).astype(jnp.bfloat16).reshape(out_ref.shape)
+    )
+
+
+def head_weight_kernel(
+    place_ref, same_ref, cross_ref, gate_weight_ref, out_weight_ref, attended_ref, blocks_ref, sum_ref
+):
+    core, turn = place_ref[0], place_ref[2]
+    count, residues = blocks_ref.shape[0] // 2, same_ref.shape[3]
+    width = same_ref.shape[4]
+    slot = lax.broadcasted_iota(jnp.int32, (2 * count * residues, LANES), 1) // (LANES // SLOTS)
+
+    def tokens_of(t, s):
+        rows = []
+        for block in range(count):
+            a, b = same_ref[block, t, s], cross_ref[block, t, s]
+            rows += [jnp.where(core == 0, a, b), jnp.where(core == 0, b, a)]
+        return jnp.concatenate(rows, axis=0)
+
+    def tile_of(ref, row):
+        return ref[:, row : row + residues, :].reshape(-1, LANES)
+
+    attended = tile_of(attended_ref, 0).astype(jnp.float32)
+    sums = [jnp.zeros((width, LANES), jnp.float32)] * 5
+    for s in range(SLOTS):
+        chosen = slot == lax.rem(turn + s, SLOTS)
+        normed, grad = tokens_of(0, s), tokens_of(1, s)
+        gate = gate_of(f32_dot(normed, gate_weight_ref[...]))
+        grad_gated = f32_dot(grad, out_weight_ref[...], NT)
+        gated = (gate * attended).astype(jnp.bfloat16)
+        gate_logit = (grad_gated * attended * gate * (1.0 - gate)).astype(jnp.bfloat16)
+        pieces = [
+            tile_of(blocks_ref, 0),
+            tile_of(blocks_ref, residues),
+            tile_of(attended_ref, residues),
+            gate_logit,
+            gated,
+        ]
+        zero = jnp.zeros_like(gated)
+        pieces = [jnp.where(chosen, p, zero) for p in pieces]
+        products = f32_dot(normed, jnp.concatenate(pieces[:4], axis=1), TN)
+        for t in range(4):
+            sums[t] += products[:, t * LANES : (t + 1) * LANES]
+        sums[4] += f32_dot(grad, pieces[4], TN)
+    totals = []
+    for part in sums:
+        part = part + pltpu.roll(part, LANES // 2, 1)
+        totals.append(part + pltpu.roll(part, LANES // 4, 1))
+    sum_ref[:width, :] = slot_select(totals[:4])
+    quarter = width // SLOTS
+    sum_ref[width:, :] = slot_select(
+        [totals[4][k * quarter : (k + 1) * quarter] for k in range(SLOTS)]
+    )
+
+
+def pair_weight_kernel(blocks_ref, pair_ref, mean_ref, spread_ref, sums_ref, out_ref, share_ref):
+    heads, part = share_ref.shape[0], pair_ref.shape[0] // 2
+    share_ref[...] = share_of(blocks_ref, blocks_ref.shape[1] - part, part, heads)
 
     def rows(step, carry):
         total, shift = carry
@@ -416,31 +476,42 @@
         rows,
         (jnp.zeros((2 * heads, channels), jnp.float32), jnp.zeros((heads, LANES), jnp.float32)),
     )
-    pair_weight = total[:heads] + total[heads:] - jnp.sum(shift, axis=1, keepdims=True)
-    normed = normalized(x_ref)[0].astype(jnp.bfloat16)
-    for t in range(2):
-        query_key_ref[:, t * width : (t + 1) * width] = unpack_heads(
-            blocks_ref, t * residues, residues, tiles
-        ).astype(jnp.bfloat16)
-    weight_ref[:, : 2 * width] = f32_dot(normed, query_key_ref[...], TN).astype(jnp.bfloat16)
-    rows_each = weight_ref.shape[0] // heads
-    first = lax.broadcasted_iota(jnp.int32, (rows_each, channels), 0) == 0
+    count = sums_ref.shape[0]
+    out_ref[:count, :] = sums_ref[...]
+    out_ref[count:, :] = total[:heads] + total[heads:] - jnp.sum(shift, axis=1, keepdims=True)
+
+
+def add_kernel(mine_ref, other_ref, out_ref):
+    count = mine_ref.shape[0]
+    out_ref[:count, :] = (
+        mine_ref[...].astype(jnp.float32) + other_ref[:count, :].astype(jnp.float32)
+    ).astype(out_ref.dtype)
+    if out_ref.shape[0] > count:
+        out_ref[count:, :] = jnp.zeros((out_ref.shape[0] - count, LANES), out_ref.dtype)
+
+
+def spread_kernel(parts_ref, combined_ref, out_weight_ref, pair_weight_ref):
+    heads, width = parts_ref.shape[0], combined_ref.shape[0]
+    slot_lanes = LANES // SLOTS
+    quarter = width // SLOTS
+    for tile in range(heads // SLOTS):
+        parts = [parts_ref[tile * SLOTS + j, :width, :].astype(jnp.float32) for j in range(SLOTS)]
+        for t in range(4):
+            moved = []
+            for j in range(SLOTS):
+                shift = (j - t) % SLOTS * slot_lanes
+                moved.append(pltpu.roll(parts[j], shift, 1) if shift else parts[j])
+            start = t * width + tile * LANES
+            combined_ref[:, start : start + LANES] = slot_select(moved)
     for h in range(heads):
-        row = jnp.broadcast_to(pair_weight[h : h + 1], (rows_each, channels))
-        weight_ref[h * rows_each : (h + 1) * rows_each, 2 * width :] = jnp.where(
-            first, row, 0.0
-        ).astype(jnp.bfloat16)
-
-
-def alignment_kernel(x_ref, wc_ref, query_key_ref, value_gate_ref, out_ref):
-    width = x_ref.shape[2]
-    normed, spread = normalized(x_ref)
-    gradient = f32_dot(query_key_ref[...], wc_ref[:, : 2 * width], NT) + f32_dot(
-        value_gate_ref[...], wc_ref[:, 2 * width :], NT
-    )
-    out_ref[...] = (
-        layer_norm_backward(gradient, normed, spread).astype(jnp.bfloat16).reshape(out_ref.shape)
-    )
+        turned = parts_ref[h, width : width + quarter, :].astype(jnp.float32).T
+        out_weight_ref[h * slot_lanes : (h + 1) * slot_lanes, :] = jnp.concatenate(
+            [turned[k * slot_lanes : (k + 1) * slot_lanes, :] for k in range(SLOTS)], axis=1
+        )
+    total = jnp.zeros(pair_weight_ref.shape, jnp.float32)
+    for h in range(heads):
+        total += parts_ref[h, width + quarter :, :].astype(jnp.float32)[:heads]
+    pair_weight_ref[...] = total
 
 
 def pair_kernel(blocks_row, blocks_ref, pair_ref, weight_ref, bias_ref, mean_ref, spread_ref, out_ref, share_ref):
@@ -514,25 +585,6 @@
     return lax.ppermute(mine, axis_name, [(a, a ^ distance) for a in range(size)])
 
 
-def gathered_seq(mine):
-    size, index = lax.axis_size("seq"), lax.axis_index("seq")
-    rows = jnp.zeros((size,) + mine.shape, mine.dtype)
-    rows = lax.dynamic_update_index_in_dim(rows, mine, index, 0)
-    for k in range(1, size):
-        t = lax.ppermute(mine, "seq", [(a, (a + k) % size) for a in range(size)])
-        rows = lax.dynamic_update_index_in_dim(rows, t, (index - k) % size, 0)
-    return rows
-
-
-def summed_everywhere(parts):
-    size = lax.axis_size("res")
-    rows, columns = parts.shape
-    parts = lax.all_to_all(parts.reshape(size, rows // size, columns), "res", 0, 0, tiled=True)
-    part = jnp.sum(parts.astype(jnp.float32), axis=0).astype(jnp.bfloat16)
-    part = jnp.sum(gathered_seq(part).astype(jnp.float32), axis=0).astype(jnp.bfloat16)
-    return lax.all_gather(part, "res", axis=0)
-
-
 def fits_heads(alignment_rows, pair_entries, pair_weight):
     channels, heads = pair_weight.shape
     return (
@@ -557,19 +609,30 @@
     group = 2 * res_size
     groups = [[g * group + k for k in range(group)] for g in range(seq_half)]
     scale = 1.0 / math.sqrt(width // heads * sequences * seq_size)
-    place = jnp.stack([lax.axis_index("res") % 2, lax.axis_index("seq") // 2]).astype(jnp.int32)
+    res_index, seq_index = lax.axis_index("res"), lax.axis_index("seq")
+    head = seq_index % 2 * (res_size // 2) + res_index // 2
+    place = jnp.stack([res_index % 2, seq_index // 2, head % SLOTS]).astype(jnp.int32)
     bf16, f32 = jnp.bfloat16, jnp.float32
 
     def across(blocks):
         return lax.all_to_all(blocks, ("seq", "res"), 0, 0, axis_index_groups=groups, tiled=True)
+
+    core_groups = [
+        [g * group + 2 * k + core for k in range(res_size)]
+        for g in range(seq_half)
+        for core in range(2)
+    ]
+
+    def over_heads(mine):
+        return lax.all_gather(mine, ("seq", "res"), axis=0, axis_index_groups=core_groups)
 
     def all_quarters(mine):
         far = swapped(mine, "seq", seq_half)
         return mine, far, swapped(mine, "res", 1), swapped(far, "res", 1)
 
     x, grad, wc, wo = alignment_rows, updated_gradient, combined_weight, output_weight
-    (value_blocks,) = call(
-        value_kernel, [((group, 2 * residues, LANES), bf16)], x, grad, wc, wo,
+    value_blocks, normed = call(
+        value_kernel, [((group, 2 * residues, LANES), bf16), (x.shape, bf16)], x, grad, wc, wo,
         flops=8 * tokens * width * width,
     )
     value_blocks = across(value_blocks)
@@ -582,7 +645,7 @@
             ((residues, LANES), f32),
             ((residues, LANES), f32),
         ],
-        x, wc, pair_entries, centred,
+        normed, wc, pair_entries, centred,
         flops=8 * tokens * width * width,
     )
     query_blocks = across(query_blocks)
@@ -597,10 +660,16 @@
 
     grad_mine, grad_sent = scores(value_blocks, residues, 0, False, bf16)
     grad_other = swapped(grad_sent, "seq", seq_half)
+    half_tokens = ((2, sequences // 2, residues, width), bf16)
+    keep, send = call(
+        split_kernel, [half_tokens, half_tokens], normed, grad, grad_mine, place=place
+    )
+    same_tokens, cross_tokens = over_heads(keep), over_heads(swapped(send, "res", 1))
+
     logit_mine, logit_sent = scores(query_blocks, 0, residues, True, f32)
     logit_other = swapped(logit_sent, "seq", seq_half)
     quarter = ((total // 4, total), bf16)
-    probs, grad_logits = call(
+    grad_logits, probs = call(
         softmax_kernel, [quarter, quarter], logit_mine, logit_other, grad_mine, grad_other,
         flops=total * total,
     )
@@ -616,29 +685,44 @@
             scratch=[pltpu.VMEM((total, total), bf16)],
             place=place, flops=4 * total * total * width,
         )
-        return across(out)
-
-    attended_blocks = products(all_quarters(probs), value_blocks, 0, residues, False, 1.0)
-    grad_blocks = products(all_quarters(grad_logits), query_blocks, residues, 0, True, scale)
-
-    updated, value_gate, early = call(
-        gate_kernel,
-        [(x.shape, bf16), ((tokens, 2 * width), bf16), ((width, 3 * width), bf16)],
-        x, grad, wc, wo, attended_blocks,
-        flops=12 * tokens * width * width,
-    )
-    early = summed_everywhere(early)
-    query_key, late = call(
-        weight_kernel,
-        [((tokens, 2 * width), bf16), ((width, 2 * width + channels), bf16)],
-        x, grad_blocks, pair_entries, mean, spread,
+        return out
+
+    grad_sums = products(all_quarters(grad_logits), query_blocks, residues, 0, True, scale)
+    grad_blocks = across(grad_sums)
+    attended = products(all_quarters(probs), value_blocks, 0, residues, False, 1.0)
+    attended_blocks = across(attended)
+
+    head_dim = width // heads
+    gate_weight = jnp.tile(
+        lax.dynamic_slice_in_dim(wc, 3 * width + head * head_dim, head_dim, 1), (1, SLOTS)
+    )
+    out_weight = jnp.tile(
+        lax.dynamic_slice_in_dim(wo, head * head_dim, head_dim, 0), (SLOTS, 1)
+    )
+    rows = width + width // SLOTS
+    (sums,) = call(
+        head_weight_kernel, [((rows, LANES), f32)],
+        same_tokens, cross_tokens, gate_weight, out_weight, attended, grad_sums,
+        place=place, flops=20 * 4 * tokens * width * LANES,
+    )
+    (sums,) = call(
+        pair_weight_kernel, [((rows + heads, LANES), f32)],
+        grad_blocks, pair_entries, mean, spread, sums,
         scratch=[pltpu.VMEM((heads, residues, LANES), f32)],
         flops=4 * tokens * width * width,
     )
-    late = summed_everywhere(late)
-    (alignment_gradient,) = call(
-        alignment_kernel, [(x.shape, bf16)], x, wc, query_key, value_gate,
-        flops=8 * tokens * width * width,
+    wire = ((rows + 2 * heads, LANES), bf16)
+    (sums,) = call(add_kernel, [wire], sums, swapped(sums, "res", 1))
+    (sums,) = call(add_kernel, [wire], sums, swapped(sums, "seq", seq_half))
+    parts = over_heads(sums)
+    combined_weight_gradient, output_weight_gradient, pair_weight_gradient = call(
+        spread_kernel, [(wc.shape, f32), (wo.shape, f32), ((heads, channels), f32)], parts
+    )
+
+    updated, alignment_gradient = call(
+        final_kernel, [(x.shape, bf16), (x.shape, bf16)],
+        x, grad, wc, wo, attended_blocks, grad_blocks,
+        flops=14 * tokens * width * width,
     )
     (pair_gradient,) = call(
         functools.partial(pair_kernel, 2 * residues),
@@ -647,21 +731,13 @@
         scratch=[pltpu.VMEM((heads, residues, LANES), f32)],
         flops=8 * tokens * width * width,
     )
-
-    combined_weight_gradient = (
-        jnp.concatenate([late[:, :, : 2 * width], early[:, :, : 2 * width]], axis=-1)
-        .reshape(wc.shape)
-        .astype(f32)
-    )
-    output_weight_gradient = early[:, :, 2 * width :].reshape(wo.shape).astype(f32)
-    pair_weight_gradient = late[:, 0, 2 * width :].T.astype(f32)
     return (
         updated,
         alignment_gradient,
         pair_gradient,
         combined_weight_gradient,
         output_weight_gradient,
-        pair_weight_gradient,
+        pair_weight_gradient.T,
     )
 
 

time: 182 us -> 220 us (1.21)
  blocking collectives: 18.9 us -> 45.1 us
  starting transfers between devices: 39.8 us -> 22.1 us
  between operations: 0.98 us -> 14.4 us
  local copies, waits for them, and re-layouts: 13.3 us -> 23.3 us
  Pallas kernels: 30.3 us -> 35.9 us
  other arithmetic: 5.3 us -> 0.27 us
  waiting for transfers between devices: 72.4 us -> 77.4 us
    all_to_all x0 -> x1, blocking collectives: none -> 16.6 us  [across(): lax.all_to_all(blocks, ('seq', 'res'), 0, 0, axis_index_groups=groups, ti...]
    all_gather x0 -> x2, waiting for transfers between devices: none -> 13.2 us  [over_heads(): lax.all_gather(mine, ('seq', 'res'), axis=0, axis_index_groups=core_groups)]
    all_to_all x4 -> x3, waiting for transfers between devices: 28.8 us -> 15.8 us  [across(): lax.all_to_all(blocks, ('seq', 'res'), 0, 0, axis_index_groups=groups, ti...]
    ppermute x10 -> x13, waiting for transfers between devices: 36.7 us -> 48.4 us  [swapped(): lax.ppermute(mine, axis_name, [(a, a ^ distance) for a in range(size)])]
    all_gather x2 -> x1, blocking collectives: 18.9 us -> 28.5 us  [over_heads(): lax.all_gather(mine, ('seq', 'res'), axis=0, axis_index_groups=core_groups)]
    ppermute x6 -> x0, starting transfers between devices: 9.14 us -> none  [gathered_seq(): t = lax.ppermute(mine, 'seq', [(a, (a + k) % size) for a in range(size)])]
    unnamed x44 -> x68, local copies, waits for them, and re-layouts: 13.2 us -> 22.3 us
    all_to_all x2 -> x0, starting transfers between devices: 8.12 us -> none  [summed_everywhere(): lax.all_to_all(parts.reshape(size, rows // size, columns), 'res', 0, 0, t...]
  transfers between devices with their start and end apart: 22 -> 18, of which waited for: 14 -> 11; matrix products, arithmetic and copies ran while one was open for 1% -> 1% of each run, Pallas kernels for 8% -> 14%
where the time goes in v4:
time: 220 us; the launch traced here: 218 us
  waiting for transfers between devices  77.4 us (35%)
  blocking collectives  45.1 us (20%)
  Pallas kernels  35.9 us (16%)
  local copies, waits for them, and re-layouts  23.3 us (11%)
  starting transfers between devices  22.1 us (10%)
  between operations  14.4 us (7%)
    ppermute x13, waiting for transfers between devices, swapped(): lax.ppermute(mine, axis_name, [(a, a ^ distance) for a in range(size)])  48.4 us
    pallas_call x15, Pallas kernels, call(): pl.pallas_call(kernel, out_shape=shapes, in_specs=specs, out_specs=[whole...  35.9 us
    all_gather x1, blocking collectives, over_heads(): lax.all_gather(mine, ('seq', 'res'), axis=0, axis_index_groups=core_groups)  28.5 us
    unnamed x68, local copies, waits for them, and re-layouts  22.3 us
    all_to_all x1, blocking collectives, across(): lax.all_to_all(blocks, ('seq', 'res'), 0, 0, axis_index_groups=groups, ti...  16.6 us
    all_to_all x3, waiting for transfers between devices, across(): lax.all_to_all(blocks, ('seq', 'res'), 0, 0, axis_index_groups=groups, ti...  15.8 us
    all_to_all x3, starting transfers between devices, across(): lax.all_to_all(blocks, ('seq', 'res'), 0, 0, axis_index_groups=groups, ti...  14.7 us
    all_gather x2, waiting for transfers between devices, over_heads(): lax.all_gather(mine, ('seq', 'res'), axis=0, axis_index_groups=core_groups)  13.2 us
  transfers between devices with their start and end apart: 18, of which 11 were waited for; matrix products, arithmetic and copies ran while one was open for 1% of the time, Pallas kernels for 14%

profile of v4, /device:TPU:0, one launch (start us, length us, event | category | flops | bytes accessed | tf_op | source)
XLA Modules:
  0.0 218.5 jit_solution(16840654427829035062)
XLA Ops:
  12.6 16.6 %all_to_all.20.own_ref.blocks_ref = bf16[16,128,128]{2,1,0:T(8,128)(2,1)S(1)} all-to-all(bf16[16,128,128]{2,1,0:T(8,128)(2,1)S(1)} %get-tuple-element.29), channel_id=1, replica_groups={{0,1,2,3,4,5,6,7,8,9,10,11,12,13,14,15},{16,17,18,19,20,21,22,23,24,25,..., dimensions={0} | all-to-all | bytes 1048576 | tf_op jit(solution)/shard_map/all_to_all | solution.py:618
  29.3 2.0 collective-permute-done.2.other_ref
  31.3 1.5 shard_map.112
  37.7 12.5 %shard_map.110 = (bf16[16,192,128]{2,1,0:T(8,128)(2,1)S(1)}, f32[8,64,128]{2,1,0:T(8,128)S(1)}, f32[64,128]{1,0:T(8,128)S(1)}, f32[64,128]{1,0:T(8,128)S(1)}) custom-call(bf16[8,64,256]{2,1,0:T(8,128)(2,1)S(1)} %copy-done.18, bf16[256,1024]{1,0:T(8,128)(2,1)S(1)} %copy-done.2, bf16[64,128,128]{2,1,0:T(8,128)(2,1)S(1)} %copy-done, ...), custom_call_target="tpu_custom_call" | custom-call | flops 268435456 | bytes 4001792 | tf_op jit(solution)/shard_map/pallas_call | solution.py:571
  51.8 3.6 %all-to-all-start = ((bf16[16,192,128]{2,1,0:T(8,128)(2,1)}), bf16[16,192,128]{2,1,0:T(8,128)(2,1)S(1)}, u32[]{:S(2)}, u32[]{:S(2)}) async-start(bf16[16,192,128]{2,1,0:T(8,128)(2,1)} %copy-done.19), calls=%async_computation | async-start | bytes 1572864 | tf_op jit(solution)/shard_map/all_to_all | solution.py:618
  55.8 1.6 collective-permute-done.10
  57.5 15.8 %all-to-all-done.own_ref.blocks_ref = bf16[16,192,128]{2,1,0:T(8,128)(2,1)S(1)} async-done(((bf16[16,192,128]{2,1,0:T(8,128)(2,1)}), bf16[16,192,128]{2,1,0:T(8,128)(2,1)S(1)}, u32[]{:S(2)}, u32[]{:S(2)}) %all-to-all-start) | async-done | bytes 786464 | tf_op jit(solution)/shard_map/all_to_all | solution.py:618
  73.4 2.2 collective-permute-done.other_ref
  76.6 2.6 %collective-permute-start.1 = (f32[128,512]{1,0:T(8,128)S(1)}, f32[128,512]{1,0:T(8,128)S(1)}, u32[]{:S(2)}, u32[]{:S(2)}) collective-permute-start(f32[128,512]{1,0:T(8,128)S(1)} %get-tuple-element.28), channel_id=1, source_target_pairs={{0,16},{8,24},{16,0},{24,8},{1,17},{9,25},{17,1},{25,9},{2,18},{10... | collective-permute-start | bytes 786440 | tf_op jit(solution)/shard_map/ppermute | solution.py:585
  79.6 17.6 %collective-permute-done.3.grad_other_ref = bf16[128,512]{1,0:T(8,128)(2,1)S(1)} collective-permute-done((bf16[128,512]{1,0:T(8,128)(2,1)}, bf16[128,512]{1,0:T(8,128)(2,1)S(1)}, u32[]{:S(2)}, u32[]{:S(2)}) %collective-permute-start.3) | collective-permute-done | bytes 131104 | tf_op jit(solution)/shard_map/ppermute | solution.py:585
  99.1 8.0 %collective-permute-done.7.far_ref = bf16[128,512]{1,0:T(8,128)(2,1)S(1)} collective-permute-done((bf16[128,512]{1,0:T(8,128)(2,1)S(1)}, bf16[128,512]{1,0:T(8,128)(2,1)S(1)}, u32[]{:S(2)}, u32[]{:S(2)}) %collective-permute-start.7) | collective-permute-done | bytes 131104 | tf_op jit(solution)/shard_map/ppermute | solution.py:585
  108.4 1.9 shard_map.115.blocks_ref
  110.3 5.6 %all-to-all-start.3 = ((bf16[16,160,128]{2,1,0:T(8,128)(2,1)}), bf16[16,160,128]{2,1,0:T(8,128)(2,1)S(1)}, u32[]{:S(2)}, u32[]{:S(2)}) async-start(bf16[16,160,128]{2,1,0:T(8,128)(2,1)} %shard_map.115.blocks_ref), calls=%async_computation.3 | async-start | bytes 1310720 | tf_op jit(solution)/shard_map/all_to_all | solution.py:618
  117.3 13.1 %collective-permute-done.4.far_ref = bf16[128,512]{1,0:T(8,128)(2,1)S(1)} collective-permute-done((bf16[128,512]{1,0:T(8,128)(2,1)}, bf16[128,512]{1,0:T(8,128)(2,1)S(1)}, u32[]{:S(2)}, u32[]{:S(2)}) %collective-permute-start.4) | collective-permute-done | bytes 131104 | tf_op jit(solution)/shard_map/ppermute | solution.py:585
  135.5 5.4 %all-to-all-start.2 = ((bf16[16,128,128]{2,1,0:T(8,128)(2,1)}), bf16[16,128,128]{2,1,0:T(8,128)(2,1)}, u32[]{:S(2)}, u32[]{:S(2)}) async-start(bf16[16,128,128]{2,1,0:T(8,128)(2,1)} %copy-done.3), calls=%async_computation.2 | async-start | bytes 1048576 | tf_op jit(solution)/shard_map/all_to_all | solution.py:618
  142.0 13.2 %all-gather.8.cloned.1.call-done = bf16[16,4,64,256]{3,2,1,0:T(8,128)(2,1)} async-done(((bf16[2,4,64,256]{3,2,1,0:T(8,128)(2,1)}), bf16[16,4,64,256]{3,2,1,0:T(8,128)(2,1)}) %all-gather.8.cloned.1.call-update) | async-done | bytes 2097168 | tf_op jit(solution)/shard_map/all_gather | solution.py:627
  156.2 1.6 copy-done.10
  157.8 1.6 copy-done.11
  159.4 4.3 %shard_map.119.sums_ref = f32[320,128]{1,0:T(8,128)S(1)} custom-call(s32[3]{0:T(128)S(1)} %pad_add_fusion.place_ref, bf16[8,2,4,64,256]{4,3,2,1,0:T(8,128)(2,1)S(1)} %bitcast.12, bf16[8,2,4,64,256]{4,3,2,1,0:T(8,128)(2,1)S(1)} %bitcast.13, bf16[256,128]{1,0:T(8,128)(2,1)S(1)} %copy.15.gate_weight_ref, bf16[128,256]{1,0:T(8,128)(2,1)S(1)} %bitcast.14, ...), custom_call_target="tpu_custom_call" | custom-call | flops 1342177280 | bytes 5668876 | tf_op jit(solution)/shard_map/pallas_call | solution.py:571
  167.4 2.4 %collective-permute-start.12 = (bf16[336,128]{1,0:T(8,128)(2,1)}, bf16[336,128]{1,0:T(8,128)(2,1)}, u32[]{:S(2)}, u32[]{:S(2)}) collective-permute-start(bf16[336,128]{1,0:T(8,128)(2,1)} %shard_map.121.mine_ref), channel_id=1, source_target_pairs={{0,16},{8,24},{16,0},{24,8},{1,17},{9,25},{17,1},{25,9},{2,18},{10... | collective-permute-start | bytes 258056 | tf_op jit(solution)/shard_map/ppermute | solution.py:585
  171.3 4.2 %shard_map.117 = bf16[64,128,128]{2,1,0:T(8,128)(2,1)} custom-call(bf16[16,160,128]{2,1,0:T(8,128)(2,1)S(1)} %all-to-all-done.3.blocks_ref, bf16[64,128,128]{2,1,0:T(8,128)(2,1)S(1)} %copy-done, f32[8,128]{1,0:T(8,128)S(1)} %subtract_bitcast_fusion.weight_ref, f32[8,64,128]{2,1,0:T(8,128)S(1)} %copy-done.23, f32[64,128]{1,0:T(8,128)S(1)} %copy-done.26, ...), custom_call_target="tpu_custom_call" | custom-call | flops 268435456 | bytes 5181440 | tf_op jit(solution)/shard_map/pallas_call | solution.py:571
  177.4 3.1 %shard_map.116 = (bf16[8,64,256]{2,1,0:T(8,128)(2,1)}, bf16[8,64,256]{2,1,0:T(8,128)(2,1)}) custom-call(bf16[8,64,256]{2,1,0:T(8,128)(2,1)S(1)} %copy-done.13, bf16[8,64,256]{2,1,0:T(8,128)(2,1)S(1)} %copy-done.9, bf16[256,1024]{1,0:T(8,128)(2,1)S(1)} %copy-done.2, bf16[256,256]{1,0:T(8,128)(2,1)S(1)} %copy-done.21, ...), custom_call_target="tpu_custom_call" | custom-call | flops 469762048 | bytes 2883584 | tf_op jit(solution)/shard_map/pallas_call | solution.py:571
  181.5 28.5 %all-gather.2 = bf16[2688,128]{1,0:T(8,128)(2,1)S(1)} all-gather(bf16[336,128]{1,0:T(8,128)(2,1)S(1)} %shard_map.122), channel_id=4, replica_groups={{0,2,4,6,8,10,12,14},{1,3,5,7,9,11,13,15},{16,18,20,22,24,26,28,30},{17..., dimensions={0}, use_global_device_ids=true | all-gather | bytes 774144 | tf_op jit(solution)/shard_map/all_gather | solution.py:627
  210.0 1.6 shard_map.123
  (109 shorter events, 33.5 us)
Async XLA Ops:
  7.2 29.6 %copy-start = (bf16[64,128,128]{2,1,0:T(8,128)(2,1)S(1)}, bf16[64,128,128]{2,1,0:T(8,128)(2,1)}, u32[]{:S(2)}) copy-start(bf16[64,128,128]{2,1,0:T(8,128)(2,1)} %pair_ref.5) | copy-start | bytes 6291460
  7.2 134.8 %all-gather.6.cloned.1.call-start = ((), (), s32[]{:S(2)}) async-start(), calls=%async_computation.4 | async-start | bytes 2359296 | tf_op jit(solution)/shard_map/all_gather | solution.py:627
  11.2 22.2 %copy-start.8 = (bf16[8,64,256]{2,1,0:T(8,128)(2,1)S(1)}, bf16[8,64,256]{2,1,0:T(8,128)(2,1)}, u32[]{:S(2)}) copy-start(bf16[8,64,256]{2,1,0:T(8,128)(2,1)} %grad_ref.5) | copy-start | bytes 786436
  11.2 25.3 %copy-start.33 = (f32[128,8]{0,1:T(8,128)S(1)}, f32[128,8]{0,1:T(8,128)}, u32[]{:S(2)}) copy-start(f32[128,8]{0,1:T(8,128)} %param.10) | copy-start | bytes 12292
  11.2 25.5 %copy-start.2 = (bf16[256,1024]{1,0:T(8,128)(2,1)S(1)}, bf16[256,1024]{1,0:T(8,128)(2,1)}, u32[]{:S(2)}) copy-start(bf16[256,1024]{1,0:T(8,128)(2,1)} %wc_ref.5) | copy-start | bytes 1572868
  29.2 2.0 collective-permute-start.2
  51.8 112.0 %copy-start.25 = (f32[64,128]{1,0:T(8,128)}, f32[64,128]{1,0:T(8,128)S(1)}, u32[]{:S(2)}) copy-start(f32[64,128]{1,0:T(8,128)S(1)} %get-tuple-element.37.mean_ref) | copy-start | bytes 98308
  51.8 112.0 %copy-start.27 = (f32[64,128]{1,0:T(8,128)}, f32[64,128]{1,0:T(8,128)S(1)}, u32[]{:S(2)}) copy-start(f32[64,128]{1,0:T(8,128)S(1)} %get-tuple-element.38.spread_ref) | copy-start | bytes 98308
  51.8 21.4 %all-to-all-start = ((bf16[16,192,128]{2,1,0:T(8,128)(2,1)}), bf16[16,192,128]{2,1,0:T(8,128)(2,1)S(1)}, u32[]{:S(2)}, u32[]{:S(2)}) async-start(bf16[16,192,128]{2,1,0:T(8,128)(2,1)} %copy-done.19), calls=%async_computation | async-start | bytes 1572864 | tf_op jit(solution)/shard_map/all_to_all | solution.py:618
  55.4 99.8 %all-gather.8.cloned.1.call-start = ((), (), s32[]{:S(2)}) async-start(), calls=%async_computation.5 | async-start | bytes 2359296 | tf_op jit(solution)/shard_map/all_gather | solution.py:627
  55.5 1.9 collective-permute-start.10
  73.2 2.3 %collective-permute-start = (bf16[16,192,128]{2,1,0:T(8,128)(2,1)S(1)}, bf16[16,192,128]{2,1,0:T(8,128)(2,1)S(1)}, u32[]{:S(2)}, u32[]{:S(2)}) collective-permute-start(bf16[16,192,128]{2,1,0:T(8,128)(2,1)S(1)} %all-to-all-done.own_ref.blocks_ref), channel_id=1, source_target_pairs={{0,1},{1,0},{2,3},{3,2},{4,5},{5,4},{6,7},{7,6},{8,9},{9,8},{10,11... | collective-permute-start | bytes 2359304 | tf_op jit(solution)/shard_map/ppermute | solution.py:585
  76.6 20.6 %collective-permute-start.1 = (f32[128,512]{1,0:T(8,128)S(1)}, f32[128,512]{1,0:T(8,128)S(1)}, u32[]{:S(2)}, u32[]{:S(2)}) collective-permute-start(f32[128,512]{1,0:T(8,128)S(1)} %get-tuple-element.28), channel_id=1, source_target_pairs={{0,16},{8,24},{16,0},{24,8},{1,17},{9,25},{17,1},{25,9},{2,18},{10... | collective-permute-start | bytes 786440 | tf_op jit(solution)/shard_map/ppermute | solution.py:585
  79.2 18.0 %collective-permute-start.3 = (bf16[128,512]{1,0:T(8,128)(2,1)}, bf16[128,512]{1,0:T(8,128)(2,1)S(1)}, u32[]{:S(2)}, u32[]{:S(2)}) collective-permute-start(bf16[128,512]{1,0:T(8,128)(2,1)} %copy-done.32), channel_id=1, source_target_pairs={{0,16},{8,24},{16,0},{24,8},{1,17},{9,25},{17,1},{25,9},{2,18},{10... | collective-permute-start | bytes 393224 | tf_op jit(solution)/shard_map/ppermute | solution.py:585
  99.1 8.0 %collective-permute-start.7 = (bf16[128,512]{1,0:T(8,128)(2,1)S(1)}, bf16[128,512]{1,0:T(8,128)(2,1)S(1)}, u32[]{:S(2)}, u32[]{:S(2)}) collective-permute-start(bf16[128,512]{1,0:T(8,128)(2,1)S(1)} %get-tuple-element.33.own_ref), channel_id=1, source_target_pairs={{0,16},{8,24},{16,0},{24,8},{1,17},{9,25},{17,1},{25,9},{2,18},{10... | collective-permute-start | bytes 393224 | tf_op jit(solution)/shard_map/ppermute | solution.py:585
  99.1 8.0 %collective-permute-start.8 = (bf16[128,512]{1,0:T(8,128)(2,1)S(1)}, bf16[128,512]{1,0:T(8,128)(2,1)S(1)}, u32[]{:S(2)}, u32[]{:S(2)}) collective-permute-start(bf16[128,512]{1,0:T(8,128)(2,1)S(1)} %get-tuple-element.33.own_ref), channel_id=1, source_target_pairs={{0,1},{1,0},{2,3},{3,2},{4,5},{5,4},{6,7},{7,6},{8,9},{9,8},{10,11... | collective-permute-start | bytes 393224 | tf_op jit(solution)/shard_map/ppermute | solution.py:585
  107.1 1.3 collective-permute-start.9
  110.3 25.2 %all-to-all-start.3 = ((bf16[16,160,128]{2,1,0:T(8,128)(2,1)}), bf16[16,160,128]{2,1,0:T(8,128)(2,1)S(1)}, u32[]{:S(2)}, u32[]{:S(2)}) async-start(bf16[16,160,128]{2,1,0:T(8,128)(2,1)} %shard_map.115.blocks_ref), calls=%async_computation.3 | async-start | bytes 1310720 | tf_op jit(solution)/shard_map/all_to_all | solution.py:618
  115.9 14.4 %collective-permute-start.4 = (bf16[128,512]{1,0:T(8,128)(2,1)}, bf16[128,512]{1,0:T(8,128)(2,1)S(1)}, u32[]{:S(2)}, u32[]{:S(2)}) collective-permute-start(bf16[128,512]{1,0:T(8,128)(2,1)} %copy-done.29), channel_id=1, source_target_pairs={{0,16},{8,24},{16,0},{24,8},{1,17},{9,25},{17,1},{25,9},{2,18},{10... | collective-permute-start | bytes 393224 | tf_op jit(solution)/shard_map/ppermute | solution.py:585
  117.2 13.3 %collective-permute-start.5 = (bf16[128,512]{1,0:T(8,128)(2,1)}, bf16[128,512]{1,0:T(8,128)(2,1)S(1)}, u32[]{:S(2)}, u32[]{:S(2)}) collective-permute-start(bf16[128,512]{1,0:T(8,128)(2,1)} %copy-done.29), channel_id=1, source_target_pairs={{0,1},{1,0},{2,3},{3,2},{4,5},{5,4},{6,7},{7,6},{8,9},{9,8},{10,11... | collective-permute-start | bytes 393224 | tf_op jit(solution)/shard_map/ppermute | solution.py:585
  130.4 1.3 collective-permute-start.6
  135.5 40.0 %all-to-all-start.2 = ((bf16[16,128,128]{2,1,0:T(8,128)(2,1)}), bf16[16,128,128]{2,1,0:T(8,128)(2,1)}, u32[]{:S(2)}, u32[]{:S(2)}) async-start(bf16[16,128,128]{2,1,0:T(8,128)(2,1)} %copy-done.3), calls=%async_computation.2 | async-start | bytes 1048576 | tf_op jit(solution)/shard_map/all_to_all | solution.py:618
  165.3 1.5 collective-permute-start.11
  167.4 13.1 %collective-permute-start.12 = (bf16[336,128]{1,0:T(8,128)(2,1)}, bf16[336,128]{1,0:T(8,128)(2,1)}, u32[]{:S(2)}, u32[]{:S(2)}) collective-permute-start(bf16[336,128]{1,0:T(8,128)(2,1)} %shard_map.121.mine_ref), channel_id=1, source_target_pairs={{0,16},{8,24},{16,0},{24,8},{1,17},{9,25},{17,1},{25,9},{2,18},{10... | collective-permute-start | bytes 258056 | tf_op jit(solution)/shard_map/ppermute | solution.py:585
  (28 other events, 55.2 us)
Sparse Core Ops, SparseCore 0:
  36.7 55.5 all-gather.5
  93.8 61.3 all-gather.7

commit v5 on v4

--- a/solution.py
+++ b/solution.py
@@ -223,8 +223,11 @@
     return 1.0 / (1.0 + jnp.exp(-logits))
 
 
-def value_kernel(x_ref, grad_ref, wc_ref, wo_ref, out_ref, normed_ref):
+def value_kernel(
+    place_ref, x_ref, grad_ref, wc_ref, wo_ref, out_ref, normed_ref, keep_ref, send_ref
+):
     residues, width = x_ref.shape[1], x_ref.shape[2]
+    core = place_ref[0]
     normed = normalized(x_ref)[0].astype(jnp.bfloat16)
     normed_ref[...] = normed.reshape(normed_ref.shape)
     values = f32_dot(normed, wc_ref[:, 2 * width : 3 * width])
@@ -232,6 +235,17 @@
     grad_gated = f32_dot(grad_ref[...].reshape(-1, width), wo_ref[...], NT)
     pack_heads(out_ref, 0, values, residues)
     pack_heads(out_ref, residues, grad_gated * gate, residues)
+    for which, ref in ((core, keep_ref), (1 - core, send_ref)):
+        for s in range(SLOTS):
+            ref[0, s] = normed_ref[which * SLOTS + s]
+            ref[1, s] = grad_ref[which * SLOTS + s]
+
+
+def merge_kernel(place_ref, keep_ref, other_ref, normed_ref, grad_ref):
+    core = place_ref[0]
+    for t, ref in ((0, normed_ref), (1, grad_ref)):
+        ref[core] = keep_ref[t]
+        ref[1 - core] = other_ref[t]
 
 
 def query_kernel(scale, normed_ref, wc_ref, pair_ref, weight_ref, out_ref, bias_ref, mean_ref, spread_ref):
@@ -319,14 +333,6 @@
                     ref[k * part : (k + 1) * part, columns] += bias
 
 
-def split_kernel(place_ref, normed_ref, grad_ref, after_ref, keep_ref, send_ref):
-    core = place_ref[0]
-    for which, ref in ((core, keep_ref), (1 - core, send_ref)):
-        for s in range(SLOTS):
-            ref[0, s] = normed_ref[which * SLOTS + s]
-            ref[1, s] = grad_ref[which * SLOTS + s]
-
-
 def softmax_kernel(logit_ref, logit_other_ref, grad_ref, grad_other_ref, out_ref, prob_ref):
     logits = logit_ref[...] + logit_other_ref[...]
     lifted = jnp.exp(logits - jnp.max(logits, axis=-1, keepdims=True))
@@ -404,29 +410,29 @@
     )
 
 
-def head_weight_kernel(
-    place_ref, same_ref, cross_ref, gate_weight_ref, out_weight_ref, attended_ref, blocks_ref, sum_ref
-):
-    core, turn = place_ref[0], place_ref[2]
-    count, residues = blocks_ref.shape[0] // 2, same_ref.shape[3]
-    width = same_ref.shape[4]
-    slot = lax.broadcasted_iota(jnp.int32, (2 * count * residues, LANES), 1) // (LANES // SLOTS)
-
-    def tokens_of(t, s):
+def head_weight_kernel(place_ref, *refs):
+    turn, chip = place_ref[2], place_ref[3]
+    flips = (len(refs) - 5) // 2
+    normed_refs, grad_refs = refs[:flips], refs[flips : 2 * flips]
+    gate_weight_ref, out_weight_ref, attended_ref, blocks_ref, sum_ref = refs[2 * flips :]
+    residues, width = normed_refs[0].shape[2], normed_refs[0].shape[3]
+    slot = lax.broadcasted_iota(jnp.int32, (2 * flips * residues, LANES), 1) // (LANES // SLOTS)
+
+    def tokens_of(arrays, s):
+        return jnp.concatenate([r[c, s] for r in arrays for c in range(2)], axis=0)
+
+    def tile_of(ref, row):
         rows = []
-        for block in range(count):
-            a, b = same_ref[block, t, s], cross_ref[block, t, s]
-            rows += [jnp.where(core == 0, a, b), jnp.where(core == 0, b, a)]
+        for flip in range(flips):
+            block = jnp.bitwise_xor(chip, flip) * 2
+            rows += [ref[block + c, row : row + residues, :] for c in range(2)]
         return jnp.concatenate(rows, axis=0)
-
-    def tile_of(ref, row):
-        return ref[:, row : row + residues, :].reshape(-1, LANES)
 
     attended = tile_of(attended_ref, 0).astype(jnp.float32)
     sums = [jnp.zeros((width, LANES), jnp.float32)] * 5
     for s in range(SLOTS):
         chosen = slot == lax.rem(turn + s, SLOTS)
-        normed, grad = tokens_of(0, s), tokens_of(1, s)
+        normed, grad = tokens_of(normed_refs, s), tokens_of(grad_refs, s)
         gate = gate_of(f32_dot(normed, gate_weight_ref[...]))
         grad_gated = f32_dot(grad, out_weight_ref[...], NT)
         gated = (gate * attended).astype(jnp.bfloat16)
@@ -495,7 +501,7 @@
     slot_lanes = LANES // SLOTS
     quarter = width // SLOTS
     for tile in range(heads // SLOTS):
-        parts = [parts_ref[tile * SLOTS + j, :width, :].astype(jnp.float32) for j in range(SLOTS)]
+        parts = [parts_ref[2 * j + tile, :width, :].astype(jnp.float32) for j in range(SLOTS)]
         for t in range(4):
             moved = []
             for j in range(SLOTS):
@@ -504,7 +510,7 @@
             start = t * width + tile * LANES
             combined_ref[:, start : start + LANES] = slot_select(moved)
     for h in range(heads):
-        turned = parts_ref[h, width : width + quarter, :].astype(jnp.float32).T
+        turned = parts_ref[2 * (h % SLOTS) + h // SLOTS, width : width + quarter, :].astype(jnp.float32).T
         out_weight_ref[h * slot_lanes : (h + 1) * slot_lanes, :] = jnp.concatenate(
             [turned[k * slot_lanes : (k + 1) * slot_lanes, :] for k in range(SLOTS)], axis=1
         )
@@ -560,7 +566,7 @@
     lax.fori_loop(0, pair_ref.shape[0] // 8, rows, 0)
 
 
-def call(kernel, outs, *args, scratch=(), place=None, flops=0):
+def call(kernel, outs, *args, scratch=(), place=None, flops=0, after=()):
     whole = pl.BlockSpec(memory_space=pltpu.VMEM)
     specs = [whole] * len(args)
     if place is not None:
@@ -568,16 +574,16 @@
         args = (place,) + args
     shapes = [jax.ShapeDtypeStruct(*o) for o in outs]
     moved = sum(math.prod(a.shape) * a.dtype.itemsize for a in list(args) + shapes)
-    result = pl.pallas_call(
-        kernel,
+    first, last = len(args), len(args) + len(after)
+    return pl.pallas_call(
+        lambda *refs: kernel(*refs[:first], *refs[last:]),
         out_shape=shapes,
-        in_specs=specs,
+        in_specs=specs + [pl.BlockSpec(memory_space=pl.ANY)] * len(after),
         out_specs=[whole] * len(shapes),
         scratch_shapes=scratch,
         compiler_params=pltpu.CompilerParams(vmem_limit_bytes=VMEM_LIMIT),
         cost_estimate=pl.CostEstimate(flops=flops, bytes_accessed=moved, transcendentals=0),
-    )(*args)
-    return result
+    )(*args, *after)
 
 
 def swapped(mine, axis_name, distance):
@@ -611,29 +617,32 @@
     scale = 1.0 / math.sqrt(width // heads * sequences * seq_size)
     res_index, seq_index = lax.axis_index("res"), lax.axis_index("seq")
     head = seq_index % 2 * (res_size // 2) + res_index // 2
-    place = jnp.stack([res_index % 2, seq_index // 2, head % SLOTS]).astype(jnp.int32)
+    core, plane = res_index % 2, seq_index % 2
+    place = jnp.stack([core, seq_index // 2, head % SLOTS, head]).astype(jnp.int32)
     bf16, f32 = jnp.bfloat16, jnp.float32
 
     def across(blocks):
         return lax.all_to_all(blocks, ("seq", "res"), 0, 0, axis_index_groups=groups, tiled=True)
 
-    core_groups = [
-        [g * group + 2 * k + core for k in range(res_size)]
-        for g in range(seq_half)
-        for core in range(2)
-    ]
-
-    def over_heads(mine):
-        return lax.all_gather(mine, ("seq", "res"), axis=0, axis_index_groups=core_groups)
+    def doubled(mine, steps):
+        arrays = {0: mine}
+        for axis_name, distance, bit in steps:
+            arrays |= {
+                flip | bit: swapped(t, axis_name, distance) for flip, t in arrays.items()
+            }
+        return [arrays[flip] for flip in range(len(arrays))]
 
     def all_quarters(mine):
         far = swapped(mine, "seq", seq_half)
         return mine, far, swapped(mine, "res", 1), swapped(far, "res", 1)
 
     x, grad, wc, wo = alignment_rows, updated_gradient, combined_weight, output_weight
-    value_blocks, normed = call(
-        value_kernel, [((group, 2 * residues, LANES), bf16), (x.shape, bf16)], x, grad, wc, wo,
-        flops=8 * tokens * width * width,
+    half_tokens = ((2, sequences // 2, residues, width), bf16)
+    value_blocks, normed, keep, send = call(
+        value_kernel,
+        [((group, 2 * residues, LANES), bf16), (x.shape, bf16), half_tokens, half_tokens],
+        x, grad, wc, wo,
+        place=place, flops=8 * tokens * width * width,
     )
     value_blocks = across(value_blocks)
     centred = (pair_weight - jnp.mean(pair_weight, axis=0, keepdims=True)).T
@@ -650,21 +659,23 @@
     )
     query_blocks = across(query_blocks)
 
-    def scores(blocks, left_row, right_row, with_bias, kind):
+    def scores(blocks, left_row, right_row, with_bias, kind, after=()):
         return call(
             functools.partial(score_kernel, residues, left_row, right_row, with_bias),
             [((total // 4, total), f32), ((total // 4, total), kind)],
             blocks, swapped(blocks, "res", 1),
-            place=place, flops=2 * total * total * width,
+            place=place, flops=2 * total * total * width, after=after,
         )
 
-    grad_mine, grad_sent = scores(value_blocks, residues, 0, False, bf16)
+    grad_mine, grad_sent = scores(value_blocks, residues, 0, False, bf16, after=(mean,))
     grad_other = swapped(grad_sent, "seq", seq_half)
-    half_tokens = ((2, sequences // 2, residues, width), bf16)
-    keep, send = call(
-        split_kernel, [half_tokens, half_tokens], normed, grad, grad_mine, place=place
-    )
-    same_tokens, cross_tokens = over_heads(keep), over_heads(swapped(send, "res", 1))
+    normed_tokens, grad_tokens = call(
+        merge_kernel, [half_tokens, half_tokens], keep, swapped(send, "res", 1),
+        place=place, after=(mean,),
+    )
+    x_step, y_step, z_step = ("res", 2, 1), ("res", 4, 2), ("seq", 1, 4)
+    normed_tokens = doubled(normed_tokens, (x_step, y_step, z_step))
+    grad_tokens = doubled(grad_tokens, (y_step, z_step, x_step))
 
     logit_mine, logit_sent = scores(query_blocks, 0, residues, True, f32)
     logit_other = swapped(logit_sent, "seq", seq_half)
@@ -702,7 +713,7 @@
     rows = width + width // SLOTS
     (sums,) = call(
         head_weight_kernel, [((rows, LANES), f32)],
-        same_tokens, cross_tokens, gate_weight, out_weight, attended, grad_sums,
+        *normed_tokens, *grad_tokens, gate_weight, out_weight, attended, grad_sums,
         place=place, flops=20 * 4 * tokens * width * LANES,
     )
     (sums,) = call(
@@ -714,7 +725,8 @@
     wire = ((rows + 2 * heads, LANES), bf16)
     (sums,) = call(add_kernel, [wire], sums, swapped(sums, "res", 1))
     (sums,) = call(add_kernel, [wire], sums, swapped(sums, "seq", seq_half))
-    parts = over_heads(sums)
+    sums = jnp.where(plane == core, sums, swapped(sums, "seq", 1))
+    parts = lax.all_gather(sums, "res", axis=0)
     combined_weight_gradient, output_weight_gradient, pair_weight_gradient = call(
         spread_kernel, [(wc.shape, f32), (wo.shape, f32), ((heads, channels), f32)], parts
     )

time: 220 us -> 206 us (0.936)
  blocking collectives: 45.1 us -> 29.9 us
  starting transfers between devices: 22.1 us -> 36.6 us
  between operations: 14.4 us -> 1.01 us
  waiting for transfers between devices: 77.4 us -> 68.6 us
  local copies, waits for them, and re-layouts: 23.3 us -> 28.6 us
  other arithmetic: 0.27 us -> 2.54 us
    all_gather x1, blocking collectives: 28.5 us -> 10.4 us  [head_body(): parts = lax.all_gather(sums, 'res', axis=0)]
    ppermute x13 -> x28, starting transfers between devices: 7.31 us -> 24.9 us  [swapped(): lax.ppermute(mine, axis_name, [(a, a ^ distance) for a in range(size)])]
    all_gather x2 -> x0, waiting for transfers between devices: 13.2 us -> none  [over_heads(): lax.all_gather(mine, ('seq', 'res'), axis=0, axis_index_groups=core_groups)]
    ppermute x13 -> x28, waiting for transfers between devices: 48.4 us -> 58.4 us  [swapped(): lax.ppermute(mine, axis_name, [(a, a ^ distance) for a in range(size)])]
    all_to_all x3, waiting for transfers between devices: 15.8 us -> 10.2 us  [across(): lax.all_to_all(blocks, ('seq', 'res'), 0, 0, axis_index_groups=groups, ti...]
    unnamed x68 -> x84, local copies, waits for them, and re-layouts: 22.3 us -> 27.6 us
    all_to_all x3, starting transfers between devices: 14.7 us -> 11.7 us  [across(): lax.all_to_all(blocks, ('seq', 'res'), 0, 0, axis_index_groups=groups, ti...]
    all_to_all x1, blocking collectives: 16.6 us -> 19.4 us  [across(): lax.all_to_all(blocks, ('seq', 'res'), 0, 0, axis_index_groups=groups, ti...]
  transfers between devices with their start and end apart: 18 -> 31, of which waited for: 11 -> 14; matrix products, arithmetic and copies ran while one was open for 1% -> 1% of each run, Pallas kernels for 14% -> 9%
where the time goes in v5:
time: 206 us; the launch traced here: 205 us
  waiting for transfers between devices  68.6 us (33%)
  Pallas kernels  37.3 us (18%)
  starting transfers between devices  36.6 us (18%)
  blocking collectives  29.9 us (15%)
  local copies, waits for them, and re-layouts  28.6 us (14%)
  other arithmetic  2.54 us (1%)
    ppermute x28, waiting for transfers between devices, swapped(): lax.ppermute(mine, axis_name, [(a, a ^ distance) for a in range(size)])  58.4 us
    pallas_call x15, Pallas kernels, call(): pl.pallas_call(lambda *refs: kernel(*refs[:first], *refs[last:]), out_sha...  37.3 us
    unnamed x84, local copies, waits for them, and re-layouts  27.6 us
    ppermute x28, starting transfers between devices, swapped(): lax.ppermute(mine, axis_name, [(a, a ^ distance) for a in range(size)])  24.9 us
    all_to_all x1, blocking collectives, across(): lax.all_to_all(blocks, ('seq', 'res'), 0, 0, axis_index_groups=groups, ti...  19.4 us
    all_to_all x3, starting transfers between devices, across(): lax.all_to_all(blocks, ('seq', 'res'), 0, 0, axis_index_groups=groups, ti...  11.7 us
    all_gather x1, blocking collectives, head_body(): parts = lax.all_gather(sums, 'res', axis=0)  10.4 us
    all_to_all x3, waiting for transfers between devices, across(): lax.all_to_all(blocks, ('seq', 'res'), 0, 0, axis_index_groups=groups, ti...  10.2 us
  transfers between devices with their start and end apart: 31, of which 14 were waited for; matrix products, arithmetic and copies ran while one was open for 1% of the time, Pallas kernels for 9%

profile of v5, /device:TPU:0, one launch (start us, length us, event | category | flops | bytes accessed | tf_op | source)
XLA Modules:
  0.0 204.6 jit_solution(11615167516896033780)
XLA Ops:
  6.2 2.0 shard_map.109
  12.2 12.5 %shard_map.110 = (bf16[16,192,128]{2,1,0:T(8,128)(2,1)S(1)}, f32[8,64,128]{2,1,0:T(8,128)S(1)}, f32[64,128]{1,0:T(8,128)S(1)}, f32[64,128]{1,0:T(8,128)S(1)}) custom-call(bf16[8,64,256]{2,1,0:T(8,128)(2,1)S(1)} %get-tuple-element.27.refs_0_, bf16[256,1024]{1,0:T(8,128)(2,1)S(1)} %copy-done.3, bf16[64,128,128]{2,1,0:T(8,128)(2,1)S(1)} %copy-done, ...), custom_call_target="tpu_custom_call" | custom-call | flops 268435456 | bytes 4001792 | tf_op jit(solution)/shard_map/pallas_call | solution.py:578
  24.8 19.4 %all_to_all.20.refs_1_.refs_5_ = bf16[16,192,128]{2,1,0:T(8,128)(2,1)S(1)} all-to-all(bf16[16,192,128]{2,1,0:T(8,128)(2,1)S(1)} %get-tuple-element.28), channel_id=1, replica_groups={{0,1,2,3,4,5,6,7,8,9,10,11,12,13,14,15},{16,17,18,19,20,21,22,23,24,25,..., dimensions={0} | all-to-all | bytes 1572864 | tf_op jit(solution)/shard_map/all_to_all | solution.py:625
  44.2 3.6 %all-to-all-start.1 = ((bf16[16,128,128]{2,1,0:T(8,128)(2,1)}), bf16[16,128,128]{2,1,0:T(8,128)(2,1)S(1)}, u32[]{:S(2)}, u32[]{:S(2)}) async-start(bf16[16,128,128]{2,1,0:T(8,128)(2,1)} %get-tuple-element.31), calls=%async_computation.1 | async-start | bytes 1048576 | tf_op jit(solution)/shard_map/all_to_all | solution.py:625
  48.1 10.2 %all-to-all-done.1.refs_1_.refs_5_ = bf16[16,128,128]{2,1,0:T(8,128)(2,1)S(1)} async-done(((bf16[16,128,128]{2,1,0:T(8,128)(2,1)}), bf16[16,128,128]{2,1,0:T(8,128)(2,1)S(1)}, u32[]{:S(2)}, u32[]{:S(2)}) %all-to-all-start.1) | async-done | bytes 524320 | tf_op jit(solution)/shard_map/all_to_all | solution.py:625
  59.4 2.7 %collective-permute-start.1 = (f32[128,512]{1,0:T(8,128)S(1)}, f32[128,512]{1,0:T(8,128)S(1)}, u32[]{:S(2)}, u32[]{:S(2)}) collective-permute-start(f32[128,512]{1,0:T(8,128)S(1)} %get-tuple-element.30), channel_id=1, source_target_pairs={{0,16},{8,24},{16,0},{24,8},{1,17},{9,25},{17,1},{25,9},{2,18},{10... | collective-permute-start | bytes 786440 | tf_op jit(solution)/shard_map/ppermute | solution.py:591
  63.9 16.4 %collective-permute-done.3.refs_3_ = bf16[128,512]{1,0:T(8,128)(2,1)S(1)} collective-permute-done((bf16[128,512]{1,0:T(8,128)(2,1)S(1)}, bf16[128,512]{1,0:T(8,128)(2,1)S(1)}, u32[]{:S(2)}, u32[]{:S(2)}) %collective-permute-start.3) | collective-permute-done | bytes 131104 | tf_op jit(solution)/shard_map/ppermute | solution.py:591
  80.8 8.6 %collective-permute-done.7.refs_2_ = bf16[128,512]{1,0:T(8,128)(2,1)S(1)} collective-permute-done((bf16[128,512]{1,0:T(8,128)(2,1)S(1)}, bf16[128,512]{1,0:T(8,128)(2,1)S(1)}, u32[]{:S(2)}, u32[]{:S(2)}) %collective-permute-start.7) | collective-permute-done | bytes 131104 | tf_op jit(solution)/shard_map/ppermute | solution.py:591
  90.8 1.9 shard_map.115.refs_20_
  92.7 3.7 %all-to-all-start.3 = ((bf16[16,160,128]{2,1,0:T(8,128)(2,1)}), bf16[16,160,128]{2,1,0:T(8,128)(2,1)S(1)}, u32[]{:S(2)}, u32[]{:S(2)}) async-start(bf16[16,160,128]{2,1,0:T(8,128)(2,1)} %shard_map.115.refs_20_), calls=%async_computation.3 | async-start | bytes 1310720 | tf_op jit(solution)/shard_map/all_to_all | solution.py:625
  102.7 4.5 %collective-permute-done.4.refs_2_ = bf16[128,512]{1,0:T(8,128)(2,1)S(1)} collective-permute-done((bf16[128,512]{1,0:T(8,128)(2,1)S(1)}, bf16[128,512]{1,0:T(8,128)(2,1)S(1)}, u32[]{:S(2)}, u32[]{:S(2)}) %collective-permute-start.4) | collective-permute-done | bytes 131104 | tf_op jit(solution)/shard_map/ppermute | solution.py:591
  107.1 2.2 %collective-permute-start.21 = (bf16[2,4,64,256]{3,2,1,0:T(8,128)(2,1)S(1)}, bf16[2,4,64,256]{3,2,1,0:T(8,128)(2,1)S(1)}, u32[]{:S(2)}, u32[]{:S(2)}) collective-permute-start(bf16[2,4,64,256]{3,2,1,0:T(8,128)(2,1)S(1)} %get-tuple-element.44.refs_9_), channel_id=1, source_target_pairs={{0,8},{8,0},{16,24},{24,16},{1,9},{9,1},{17,25},{25,17},{2,10},{10... | collective-permute-start | bytes 786440 | tf_op jit(solution)/shard_map/ppermute | solution.py:591
  110.7 1.8 shard_map.114.refs_19_
  112.6 4.4 %all-to-all-start.2 = ((bf16[16,128,128]{2,1,0:T(8,128)(2,1)}), bf16[16,128,128]{2,1,0:T(8,128)(2,1)}, u32[]{:S(2)}, u32[]{:S(2)}) async-start(bf16[16,128,128]{2,1,0:T(8,128)(2,1)} %shard_map.114.refs_19_), calls=%async_computation.2 | async-start | bytes 1048576 | tf_op jit(solution)/shard_map/all_to_all | solution.py:625
  123.7 7.8 %collective-permute-done.14.refs_5_ = bf16[2,4,64,256]{3,2,1,0:T(8,128)(2,1)S(1)} collective-permute-done((bf16[2,4,64,256]{3,2,1,0:T(8,128)(2,1)S(1)}, bf16[2,4,64,256]{3,2,1,0:T(8,128)(2,1)S(1)}, u32[]{:S(2)}, u32[]{:S(2)}) %collective-permute-start.14) | collective-permute-done | bytes 262176 | tf_op jit(solution)/shard_map/ppermute | solution.py:591
  138.4 4.4 %collective-permute-done.15.refs_6_ = bf16[2,4,64,256]{3,2,1,0:T(8,128)(2,1)S(1)} collective-permute-done((bf16[2,4,64,256]{3,2,1,0:T(8,128)(2,1)S(1)}, bf16[2,4,64,256]{3,2,1,0:T(8,128)(2,1)S(1)}, u32[]{:S(2)}, u32[]{:S(2)}) %collective-permute-start.15) | collective-permute-done | bytes 262176 | tf_op jit(solution)/shard_map/ppermute | solution.py:591
  146.0 2.4 %collective-permute-done.16.refs_7_ = bf16[2,4,64,256]{3,2,1,0:T(8,128)(2,1)S(1)} collective-permute-done((bf16[2,4,64,256]{3,2,1,0:T(8,128)(2,1)S(1)}, bf16[2,4,64,256]{3,2,1,0:T(8,128)(2,1)S(1)}, u32[]{:S(2)}, u32[]{:S(2)}) %collective-permute-start.16) | collective-permute-done | bytes 262176 | tf_op jit(solution)/shard_map/ppermute | solution.py:591
  149.8 3.8 %collective-permute-done.17.refs_8_ = bf16[2,4,64,256]{3,2,1,0:T(8,128)(2,1)} collective-permute-done((bf16[2,4,64,256]{3,2,1,0:T(8,128)(2,1)}, bf16[2,4,64,256]{3,2,1,0:T(8,128)(2,1)}, u32[]{:S(2)}, u32[]{:S(2)}) %collective-permute-start.17) | collective-permute-done | bytes 262176 | tf_op jit(solution)/shard_map/ppermute | solution.py:591
  164.1 5.0 %shard_map.119.refs_4_ = f32[320,128]{1,0:T(8,128)S(1)} custom-call(s32[4]{0:T(128)S(1)} %pad_add_fusion.refs_0_, bf16[2,4,64,256]{3,2,1,0:T(8,128)(2,1)S(1)} %copy-done.16, bf16[2,4,64,256]{3,2,1,0:T(8,128)(2,1)S(1)} %copy-done.20, bf16[2,4,64,256]{3,2,1,0:T(8,128)(2,1)S(1)} %copy-done.24, bf16[2,4,64,256]{3,2,1,0:T(8,128)(2,1)} %collective-permute-done.13.refs_4_, ...), custom_call_target="tpu_custom_call" | custom-call | flops 1342177280 | bytes 5668880 | tf_op jit(solution)/shard_map/pallas_call | solution.py:578
  172.1 2.5 %collective-permute-start.26 = (bf16[336,128]{1,0:T(8,128)(2,1)S(1)}, bf16[336,128]{1,0:T(8,128)(2,1)S(1)}, u32[]{:S(2)}, u32[]{:S(2)}) collective-permute-start(bf16[336,128]{1,0:T(8,128)(2,1)S(1)} %shard_map.121.refs_0_), channel_id=1, source_target_pairs={{0,16},{8,24},{16,0},{24,8},{1,17},{9,25},{17,1},{25,9},{2,18},{10... | collective-permute-start | bytes 258056 | tf_op jit(solution)/shard_map/ppermute | solution.py:591
  174.6 4.6 %collective-permute-done.26.refs_1_ = bf16[336,128]{1,0:T(8,128)(2,1)S(1)} collective-permute-done((bf16[336,128]{1,0:T(8,128)(2,1)S(1)}, bf16[336,128]{1,0:T(8,128)(2,1)S(1)}, u32[]{:S(2)}, u32[]{:S(2)}) %collective-permute-start.26) | collective-permute-done | bytes 86048 | tf_op jit(solution)/shard_map/ppermute | solution.py:591
  182.4 4.2 %shard_map.117 = bf16[64,128,128]{2,1,0:T(8,128)(2,1)} custom-call(bf16[16,160,128]{2,1,0:T(8,128)(2,1)S(1)} %all-to-all-done.3.refs_5_.refs_0_, bf16[64,128,128]{2,1,0:T(8,128)(2,1)S(1)} %copy-done.1, f32[8,128]{1,0:T(8,128)S(1)} %subtract_bitcast_fusion.refs_3_.refs_2_, f32[8,64,128]{2,1,0:T(8,128)S(1)} %copy-done.14, f32[64,128]{1,0:T(8,128)S(1)} %copy-done.12, ...), custom_call_target="tpu_custom_call" | custom-call | flops 268435456 | bytes 5181440 | tf_op jit(solution)/shard_map/pallas_call | solution.py:578
  188.5 3.1 %shard_map.116 = (bf16[8,64,256]{2,1,0:T(8,128)(2,1)}, bf16[8,64,256]{2,1,0:T(8,128)(2,1)}) custom-call(bf16[8,64,256]{2,1,0:T(8,128)(2,1)S(1)} %copy-done.6, bf16[8,64,256]{2,1,0:T(8,128)(2,1)S(1)} %copy-done.8, bf16[256,1024]{1,0:T(8,128)(2,1)S(1)} %copy-done.4, bf16[256,256]{1,0:T(8,128)(2,1)S(1)} %copy-done.10, ...), custom_call_target="tpu_custom_call" | custom-call | flops 469762048 | bytes 2883584 | tf_op jit(solution)/shard_map/pallas_call | solution.py:578
  192.5 10.4 %all-gather = bf16[2688,128]{1,0:T(8,128)(2,1)S(1)} all-gather(bf16[336,128]{1,0:T(8,128)(2,1)S(1)} %broadcast_select_fusion), channel_id=2, replica_groups=mesh['seq'=4,'res'=8] {'res'}, dimensions={0}, use_global_device_ids=true | all-gather | bytes 774144 | tf_op jit(solution)/shard_map/all_gather | solution.py:729
  (150 shorter events, 61.3 us)
Async XLA Ops:
  44.2 14.1 %all-to-all-start.1 = ((bf16[16,128,128]{2,1,0:T(8,128)(2,1)}), bf16[16,128,128]{2,1,0:T(8,128)(2,1)S(1)}, u32[]{:S(2)}, u32[]{:S(2)}) async-start(bf16[16,128,128]{2,1,0:T(8,128)(2,1)} %get-tuple-element.31), calls=%async_computation.1 | async-start | bytes 1048576 | tf_op jit(solution)/shard_map/all_to_all | solution.py:625
  47.8 10.5 %collective-permute-start = (bf16[16,192,128]{2,1,0:T(8,128)(2,1)S(1)}, bf16[16,192,128]{2,1,0:T(8,128)(2,1)S(1)}, u32[]{:S(2)}, u32[]{:S(2)}) collective-permute-start(bf16[16,192,128]{2,1,0:T(8,128)(2,1)S(1)} %all_to_all.20.refs_1_.refs_5_), channel_id=1, source_target_pairs={{0,1},{1,0},{2,3},{3,2},{4,5},{5,4},{6,7},{7,6},{8,9},{9,8},{10,11... | collective-permute-start | bytes 2359304 | tf_op jit(solution)/shard_map/ppermute | solution.py:591
  59.4 20.9 %collective-permute-start.1 = (f32[128,512]{1,0:T(8,128)S(1)}, f32[128,512]{1,0:T(8,128)S(1)}, u32[]{:S(2)}, u32[]{:S(2)}) collective-permute-start(f32[128,512]{1,0:T(8,128)S(1)} %get-tuple-element.30), channel_id=1, source_target_pairs={{0,16},{8,24},{16,0},{24,8},{1,17},{9,25},{17,1},{25,9},{2,18},{10... | collective-permute-start | bytes 786440 | tf_op jit(solution)/shard_map/ppermute | solution.py:591
  63.0 17.2 %collective-permute-start.3 = (bf16[128,512]{1,0:T(8,128)(2,1)S(1)}, bf16[128,512]{1,0:T(8,128)(2,1)S(1)}, u32[]{:S(2)}, u32[]{:S(2)}) collective-permute-start(bf16[128,512]{1,0:T(8,128)(2,1)S(1)} %get-tuple-element.34), channel_id=1, source_target_pairs={{0,16},{8,24},{16,0},{24,8},{1,17},{9,25},{17,1},{25,9},{2,18},{10... | collective-permute-start | bytes 393224 | tf_op jit(solution)/shard_map/ppermute | solution.py:591
  80.6 8.9 %collective-permute-start.7 = (bf16[128,512]{1,0:T(8,128)(2,1)S(1)}, bf16[128,512]{1,0:T(8,128)(2,1)S(1)}, u32[]{:S(2)}, u32[]{:S(2)}) collective-permute-start(bf16[128,512]{1,0:T(8,128)(2,1)S(1)} %get-tuple-element.36.refs_1_), channel_id=1, source_target_pairs={{0,16},{8,24},{16,0},{24,8},{1,17},{9,25},{17,1},{25,9},{2,18},{10... | collective-permute-start | bytes 393224 | tf_op jit(solution)/shard_map/ppermute | solution.py:591
  92.7 19.9 %all-to-all-start.3 = ((bf16[16,160,128]{2,1,0:T(8,128)(2,1)}), bf16[16,160,128]{2,1,0:T(8,128)(2,1)S(1)}, u32[]{:S(2)}, u32[]{:S(2)}) async-start(bf16[16,160,128]{2,1,0:T(8,128)(2,1)} %shard_map.115.refs_20_), calls=%async_computation.3 | async-start | bytes 1310720 | tf_op jit(solution)/shard_map/all_to_all | solution.py:625
  96.7 10.4 %collective-permute-start.4 = (bf16[128,512]{1,0:T(8,128)(2,1)S(1)}, bf16[128,512]{1,0:T(8,128)(2,1)S(1)}, u32[]{:S(2)}, u32[]{:S(2)}) collective-permute-start(bf16[128,512]{1,0:T(8,128)(2,1)S(1)} %get-tuple-element.35.refs_1_), channel_id=1, source_target_pairs={{0,16},{8,24},{16,0},{24,8},{1,17},{9,25},{17,1},{25,9},{2,18},{10... | collective-permute-start | bytes 393224 | tf_op jit(solution)/shard_map/ppermute | solution.py:591
  96.7 12.6 %collective-permute-start.5 = (bf16[128,512]{1,0:T(8,128)(2,1)S(1)}, bf16[128,512]{1,0:T(8,128)(2,1)S(1)}, u32[]{:S(2)}, u32[]{:S(2)}) collective-permute-start(bf16[128,512]{1,0:T(8,128)(2,1)S(1)} %get-tuple-element.35.refs_1_), channel_id=1, source_target_pairs={{0,1},{1,0},{2,3},{3,2},{4,5},{5,4},{6,7},{7,6},{8,9},{9,8},{10,11... | collective-permute-start | bytes 393224 | tf_op jit(solution)/shard_map/ppermute | solution.py:591
  98.8 19.8 %collective-permute-start.11 = (bf16[2,4,64,256]{3,2,1,0:T(8,128)(2,1)S(1)}, bf16[2,4,64,256]{3,2,1,0:T(8,128)(2,1)S(1)}, u32[]{:S(2)}, u32[]{:S(2)}) collective-permute-start(bf16[2,4,64,256]{3,2,1,0:T(8,128)(2,1)S(1)} %get-tuple-element.43.refs_1_), channel_id=1, source_target_pairs={{0,2},{1,3},{2,0},{3,1},{4,6},{5,7},{6,4},{7,5},{8,10},{9,11},{10,... | collective-permute-start | bytes 786440 | tf_op jit(solution)/shard_map/ppermute | solution.py:591
  100.7 19.5 %collective-permute-start.19 = (bf16[2,4,64,256]{3,2,1,0:T(8,128)(2,1)S(1)}, bf16[2,4,64,256]{3,2,1,0:T(8,128)(2,1)S(1)}, u32[]{:S(2)}, u32[]{:S(2)}) collective-permute-start(bf16[2,4,64,256]{3,2,1,0:T(8,128)(2,1)S(1)} %get-tuple-element.44.refs_9_), channel_id=1, source_target_pairs={{0,4},{1,5},{2,6},{3,7},{4,0},{5,1},{6,2},{7,3},{8,12},{9,13},{10,... | collective-permute-start | bytes 786440 | tf_op jit(solution)/shard_map/ppermute | solution.py:591
  102.1 19.5 %collective-permute-start.12 = (bf16[2,4,64,256]{3,2,1,0:T(8,128)(2,1)S(1)}, bf16[2,4,64,256]{3,2,1,0:T(8,128)(2,1)S(1)}, u32[]{:S(2)}, u32[]{:S(2)}) collective-permute-start(bf16[2,4,64,256]{3,2,1,0:T(8,128)(2,1)S(1)} %get-tuple-element.43.refs_1_), channel_id=1, source_target_pairs={{0,4},{1,5},{2,6},{3,7},{4,0},{5,1},{6,2},{7,3},{8,12},{9,13},{10,... | collective-permute-start | bytes 786440 | tf_op jit(solution)/shard_map/ppermute | solution.py:591
  107.1 15.0 %collective-permute-start.21 = (bf16[2,4,64,256]{3,2,1,0:T(8,128)(2,1)S(1)}, bf16[2,4,64,256]{3,2,1,0:T(8,128)(2,1)S(1)}, u32[]{:S(2)}, u32[]{:S(2)}) collective-permute-start(bf16[2,4,64,256]{3,2,1,0:T(8,128)(2,1)S(1)} %get-tuple-element.44.refs_9_), channel_id=1, source_target_pairs={{0,8},{8,0},{16,24},{24,16},{1,9},{9,1},{17,25},{25,17},{2,10},{10... | collective-permute-start | bytes 786440 | tf_op jit(solution)/shard_map/ppermute | solution.py:591
  112.6 74.0 %all-to-all-start.2 = ((bf16[16,128,128]{2,1,0:T(8,128)(2,1)}), bf16[16,128,128]{2,1,0:T(8,128)(2,1)}, u32[]{:S(2)}, u32[]{:S(2)}) async-start(bf16[16,128,128]{2,1,0:T(8,128)(2,1)} %shard_map.114.refs_19_), calls=%async_computation.2 | async-start | bytes 1048576 | tf_op jit(solution)/shard_map/all_to_all | solution.py:625
  117.0 14.5 %collective-permute-start.14 = (bf16[2,4,64,256]{3,2,1,0:T(8,128)(2,1)S(1)}, bf16[2,4,64,256]{3,2,1,0:T(8,128)(2,1)S(1)}, u32[]{:S(2)}, u32[]{:S(2)}) collective-permute-start(bf16[2,4,64,256]{3,2,1,0:T(8,128)(2,1)S(1)} %get-tuple-element.43.refs_1_), channel_id=1, source_target_pairs={{0,8},{8,0},{16,24},{24,16},{1,9},{9,1},{17,25},{25,17},{2,10},{10... | collective-permute-start | bytes 786440 | tf_op jit(solution)/shard_map/ppermute | solution.py:591
  118.7 15.0 %collective-permute-start.18 = (bf16[2,4,64,256]{3,2,1,0:T(8,128)(2,1)S(1)}, bf16[2,4,64,256]{3,2,1,0:T(8,128)(2,1)S(1)}, u32[]{:S(2)}, u32[]{:S(2)}) collective-permute-start(bf16[2,4,64,256]{3,2,1,0:T(8,128)(2,1)S(1)} %get-tuple-element.44.refs_9_), channel_id=1, source_target_pairs={{0,2},{1,3},{2,0},{3,1},{4,6},{5,7},{6,4},{7,5},{8,10},{9,11},{10,... | collective-permute-start | bytes 786440 | tf_op jit(solution)/shard_map/ppermute | solution.py:591
  120.2 15.5 %collective-permute-start.13 = (bf16[2,4,64,256]{3,2,1,0:T(8,128)(2,1)S(1)}, bf16[2,4,64,256]{3,2,1,0:T(8,128)(2,1)}, u32[]{:S(2)}, u32[]{:S(2)}) collective-permute-start(bf16[2,4,64,256]{3,2,1,0:T(8,128)(2,1)S(1)} %collective-permute-done.11.refs_2_), channel_id=1, source_target_pairs={{0,4},{1,5},{2,6},{3,7},{4,0},{5,1},{6,2},{7,3},{8,12},{9,13},{10,... | collective-permute-start | bytes 786440 | tf_op jit(solution)/shard_map/ppermute | solution.py:591
  121.7 15.6 %collective-permute-start.23 = (bf16[2,4,64,256]{3,2,1,0:T(8,128)(2,1)S(1)}, bf16[2,4,64,256]{3,2,1,0:T(8,128)(2,1)}, u32[]{:S(2)}, u32[]{:S(2)}) collective-permute-start(bf16[2,4,64,256]{3,2,1,0:T(8,128)(2,1)S(1)} %collective-permute-done.19.refs_11_), channel_id=1, source_target_pairs={{0,8},{8,0},{16,24},{24,16},{1,9},{9,1},{17,25},{25,17},{2,10},{10... | collective-permute-start | bytes 786440 | tf_op jit(solution)/shard_map/ppermute | solution.py:591
  122.2 20.6 %collective-permute-start.15 = (bf16[2,4,64,256]{3,2,1,0:T(8,128)(2,1)S(1)}, bf16[2,4,64,256]{3,2,1,0:T(8,128)(2,1)S(1)}, u32[]{:S(2)}, u32[]{:S(2)}) collective-permute-start(bf16[2,4,64,256]{3,2,1,0:T(8,128)(2,1)S(1)} %collective-permute-done.11.refs_2_), channel_id=1, source_target_pairs={{0,8},{8,0},{16,24},{24,16},{1,9},{9,1},{17,25},{25,17},{2,10},{10... | collective-permute-start | bytes 786440 | tf_op jit(solution)/shard_map/ppermute | solution.py:591
  132.2 16.9 %collective-permute-start.20 = (bf16[2,4,64,256]{3,2,1,0:T(8,128)(2,1)S(1)}, bf16[2,4,64,256]{3,2,1,0:T(8,128)(2,1)S(1)}, u32[]{:S(2)}, u32[]{:S(2)}) collective-permute-start(bf16[2,4,64,256]{3,2,1,0:T(8,128)(2,1)S(1)} %collective-permute-done.19.refs_11_), channel_id=1, source_target_pairs={{0,2},{1,3},{2,0},{3,1},{4,6},{5,7},{6,4},{7,5},{8,10},{9,11},{10,... | collective-permute-start | bytes 786440 | tf_op jit(solution)/shard_map/ppermute | solution.py:591
  134.4 14.0 %collective-permute-start.16 = (bf16[2,4,64,256]{3,2,1,0:T(8,128)(2,1)S(1)}, bf16[2,4,64,256]{3,2,1,0:T(8,128)(2,1)S(1)}, u32[]{:S(2)}, u32[]{:S(2)}) collective-permute-start(bf16[2,4,64,256]{3,2,1,0:T(8,128)(2,1)S(1)} %collective-permute-done.12.refs_3_), channel_id=1, source_target_pairs={{0,8},{8,0},{16,24},{24,16},{1,9},{9,1},{17,25},{25,17},{2,10},{10... | collective-permute-start | bytes 786440 | tf_op jit(solution)/shard_map/ppermute | solution.py:591
  135.6 14.2 %collective-permute-start.22 = (bf16[2,4,64,256]{3,2,1,0:T(8,128)(2,1)S(1)}, bf16[2,4,64,256]{3,2,1,0:T(8,128)(2,1)}, u32[]{:S(2)}, u32[]{:S(2)}) collective-permute-start(bf16[2,4,64,256]{3,2,1,0:T(8,128)(2,1)S(1)} %collective-permute-done.21.refs_13_), channel_id=1, source_target_pairs={{0,2},{1,3},{2,0},{3,1},{4,6},{5,7},{6,4},{7,5},{8,10},{9,11},{10,... | collective-permute-start | bytes 786440 | tf_op jit(solution)/shard_map/ppermute | solution.py:591
  137.3 16.4 %collective-permute-start.17 = (bf16[2,4,64,256]{3,2,1,0:T(8,128)(2,1)}, bf16[2,4,64,256]{3,2,1,0:T(8,128)(2,1)}, u32[]{:S(2)}, u32[]{:S(2)}) collective-permute-start(bf16[2,4,64,256]{3,2,1,0:T(8,128)(2,1)} %collective-permute-done.13.refs_4_), channel_id=1, source_target_pairs={{0,8},{8,0},{16,24},{24,16},{1,9},{9,1},{17,25},{25,17},{2,10},{10... | collective-permute-start | bytes 786440 | tf_op jit(solution)/shard_map/ppermute | solution.py:591
  143.5 10.2 %collective-permute-start.24 = (bf16[2,4,64,256]{3,2,1,0:T(8,128)(2,1)}, bf16[2,4,64,256]{3,2,1,0:T(8,128)(2,1)}, u32[]{:S(2)}, u32[]{:S(2)}) collective-permute-start(bf16[2,4,64,256]{3,2,1,0:T(8,128)(2,1)} %collective-permute-done.23.refs_15_), channel_id=1, source_target_pairs={{0,2},{1,3},{2,0},{3,1},{4,6},{5,7},{6,4},{7,5},{8,10},{9,11},{10,... | collective-permute-start | bytes 786440 | tf_op jit(solution)/shard_map/ppermute | solution.py:591
  179.9 11.7 %collective-permute-start.27 = (bf16[336,128]{1,0:T(8,128)(2,1)}, bf16[336,128]{1,0:T(8,128)(2,1)}, u32[]{:S(2)}, u32[]{:S(2)}) collective-permute-start(bf16[336,128]{1,0:T(8,128)(2,1)} %shard_map.122), channel_id=1, source_target_pairs={{0,8},{8,0},{16,24},{24,16},{1,9},{9,1},{17,25},{25,17},{2,10},{10... | collective-permute-start | bytes 258056 | tf_op jit(solution)/shard_map/ppermute | solution.py:591
  (49 other events, 619.0 us)

commit v6 on v5

--- a/solution.py
+++ b/solution.py
@@ -154,7 +154,7 @@
     )
 
 
-VMEM_LIMIT = 48 * 1024 * 1024
+VMEM_LIMIT = 20 * 1024 * 1024
 LANES = 128
 SLOTS = 4
 NT = (((1,), (1,)), ((), ()))
@@ -224,7 +224,7 @@
 
 
 def value_kernel(
-    place_ref, x_ref, grad_ref, wc_ref, wo_ref, out_ref, normed_ref, keep_ref, send_ref
+    place_ref, x_ref, grad_ref, wc_ref, wo_ref, out_ref, keep_ref, send_ref, normed_ref
 ):
     residues, width = x_ref.shape[1], x_ref.shape[2]
     core = place_ref[0]
@@ -248,38 +248,43 @@
         ref[1 - core] = other_ref[t]
 
 
-def query_kernel(scale, normed_ref, wc_ref, pair_ref, weight_ref, out_ref, bias_ref, mean_ref, spread_ref):
-    residues, width = normed_ref.shape[1], normed_ref.shape[2]
+def centred(weight):
+    return weight - jnp.mean(weight, axis=1, keepdims=True)
+
+
+def query_kernel(scale, x_ref, wc_ref, pair_ref, weight_ref, out_ref, bias_ref, mean_ref, spread_ref):
+    residues, width = x_ref.shape[1], x_ref.shape[2]
     heads = weight_ref.shape[0]
-    normed = normed_ref[...].reshape(-1, width)
+    normed = normalized(x_ref)[0].astype(jnp.bfloat16)
     pack_heads(out_ref, 0, f32_dot(normed, wc_ref[:, :width]) * scale, residues)
     pack_heads(out_ref, residues, f32_dot(normed, wc_ref[:, width : 2 * width]), residues)
 
     columns, channels = pair_ref.shape[1], pair_ref.shape[2]
-    first = weight_ref[...].astype(jnp.bfloat16)
-    rest = weight_ref[...] - first.astype(jnp.float32)
-    second, third = two_terms(rest)
+    weight = centred(weight_ref[...])
+    first = weight.astype(jnp.bfloat16)
+    second, third = two_terms(weight - first.astype(jnp.float32))
     share = jnp.full((heads, channels), 1.0 / channels, jnp.bfloat16)
     left = jnp.concatenate([first, second, third, share], axis=0)
-    ones = jnp.full((heads, channels), 1.0 / channels, jnp.bfloat16)
     average = jnp.full((channels, channels), 1.0 / channels, jnp.bfloat16)
+    step_rows = 8
 
     def rows(step, carry):
-        for k in range(8):
-            i = step * 8 + k
-            entries = pair_ref[i]
-            center = entries.astype(jnp.float32) - f32_dot(entries, average)
-            high, low = two_terms(center * center)
-            variance = f32_dot(ones, high, NT) + f32_dot(ones, low, NT)
-            spread = lax.rsqrt(variance + eps_norm)
-            raw = f32_dot(left, entries, NT)
-            bias = spread * (raw[:heads] + raw[heads : 2 * heads] + raw[2 * heads : 3 * heads])
-            bias_ref[:, i, :] = bias
-            mean_ref[pl.ds(i, 1), :] = raw[3 * heads : 3 * heads + 1]
-            spread_ref[pl.ds(i, 1), :] = spread[:1]
+        start = pl.multiple_of(step * step_rows, step_rows)
+        entries = pair_ref[pl.ds(start, step_rows)].reshape(step_rows * columns, channels)
+        center = entries.astype(jnp.float32) - f32_dot(entries, average)
+        high, low = two_terms(center * center)
+        variance = f32_dot(share, high, NT) + f32_dot(share, low, NT)
+        spread = lax.rsqrt(variance + eps_norm)
+        raw = f32_dot(left, entries, NT)
+        bias = spread * (raw[:heads] + raw[heads : 2 * heads] + raw[2 * heads : 3 * heads])
+        for k in range(step_rows):
+            lanes = slice(k * columns, (k + 1) * columns)
+            bias_ref[:, start + k, :] = bias[:, lanes]
+            mean_ref[pl.ds(start + k, 1), :] = raw[3 * heads : 3 * heads + 1, lanes]
+            spread_ref[pl.ds(start + k, 1), :] = spread[:1, lanes]
         return carry
 
-    lax.fori_loop(0, pair_ref.shape[0] // 8, rows, 0)
+    lax.fori_loop(0, pair_ref.shape[0] // step_rows, rows, 0)
     half = residues // 2
     for h in range(heads):
         for core in range(2):
@@ -524,7 +529,7 @@
     heads, channels = weight_ref.shape
     part = pair_ref.shape[0] // 2
     share_ref[...] = share_of(blocks_ref, blocks_row, part, heads)
-    first, second = two_terms(weight_ref[...])
+    first, second = two_terms(centred(weight_ref[...]))
     zero = jnp.zeros((heads, channels), jnp.bfloat16)
     top = lax.broadcasted_iota(jnp.int32, (heads, channels), 0) < 2
     ones = jnp.where(top, 1.0, 0.0).astype(jnp.bfloat16)
@@ -638,14 +643,14 @@
 
     x, grad, wc, wo = alignment_rows, updated_gradient, combined_weight, output_weight
     half_tokens = ((2, sequences // 2, residues, width), bf16)
-    value_blocks, normed, keep, send = call(
+    value_blocks, keep, send = call(
         value_kernel,
-        [((group, 2 * residues, LANES), bf16), (x.shape, bf16), half_tokens, half_tokens],
+        [((group, 2 * residues, LANES), bf16), half_tokens, half_tokens],
         x, grad, wc, wo,
+        scratch=[pltpu.VMEM(x.shape, bf16)],
         place=place, flops=8 * tokens * width * width,
     )
     value_blocks = across(value_blocks)
-    centred = (pair_weight - jnp.mean(pair_weight, axis=0, keepdims=True)).T
     query_blocks, bias, mean, spread = call(
         functools.partial(query_kernel, scale),
         [
@@ -654,7 +659,7 @@
             ((residues, LANES), f32),
             ((residues, LANES), f32),
         ],
-        normed, wc, pair_entries, centred,
+        x, wc, pair_entries, pair_weight.T,
         flops=8 * tokens * width * width,
     )
     query_blocks = across(query_blocks)
@@ -671,21 +676,24 @@
     grad_other = swapped(grad_sent, "seq", seq_half)
     normed_tokens, grad_tokens = call(
         merge_kernel, [half_tokens, half_tokens], keep, swapped(send, "res", 1),
-        place=place, after=(mean,),
+        place=place,
     )
     x_step, y_step, z_step = ("res", 2, 1), ("res", 4, 2), ("seq", 1, 4)
     normed_tokens = doubled(normed_tokens, (x_step, y_step, z_step))
     grad_tokens = doubled(grad_tokens, (y_step, z_step, x_step))
 
-    logit_mine, logit_sent = scores(query_blocks, 0, residues, True, f32)
+    logit_mine, logit_sent = scores(
+        query_blocks, 0, residues, True, f32, after=(normed_tokens[1], grad_tokens[2])
+    )
     logit_other = swapped(logit_sent, "seq", seq_half)
     quarter = ((total // 4, total), bf16)
     grad_logits, probs = call(
         softmax_kernel, [quarter, quarter], logit_mine, logit_other, grad_mine, grad_other,
         flops=total * total,
-    )
-
-    def products(quarters, blocks, first_row, second_row, with_share, factor):
+        after=(normed_tokens[2], normed_tokens[3], grad_tokens[4], grad_tokens[6]),
+    )
+
+    def products(quarters, blocks, first_row, second_row, with_share, factor, after=()):
         rows = 2 * residues + (residues // 2 if with_share else 0)
         (out,) = call(
             functools.partial(
@@ -694,13 +702,16 @@
             [((group, rows, LANES), bf16)],
             *quarters, blocks,
             scratch=[pltpu.VMEM((total, total), bf16)],
-            place=place, flops=4 * total * total * width,
+            place=place, flops=4 * total * total * width, after=after,
         )
         return out
 
     grad_sums = products(all_quarters(grad_logits), query_blocks, residues, 0, True, scale)
     grad_blocks = across(grad_sums)
-    attended = products(all_quarters(probs), value_blocks, 0, residues, False, 1.0)
+    attended = products(
+        all_quarters(probs), value_blocks, 0, residues, False, 1.0,
+        after=(*normed_tokens[4:], *grad_tokens[1::2]),
+    )
     attended_blocks = across(attended)
 
     head_dim = width // heads
@@ -739,7 +750,7 @@
     (pair_gradient,) = call(
         functools.partial(pair_kernel, 2 * residues),
         [(pair_entries.shape, bf16)],
-        grad_blocks, pair_entries, centred, bias, mean, spread,
+        grad_blocks, pair_entries, pair_weight.T, bias, mean, spread,
         scratch=[pltpu.VMEM((heads, residues, LANES), f32)],
         flops=8 * tokens * width * width,
     )

time: 206 us -> 203 us (0.985)
  blocking collectives: 29.9 us -> 10.3 us
  waiting for transfers between devices: 68.6 us -> 84.9 us
  local copies, waits for them, and re-layouts: 28.6 us -> 35 us
  Pallas kernels: 37.3 us -> 31.1 us
    all_to_all x1 -> x0, blocking collectives: 19.4 us -> none  [across(): lax.all_to_all(blocks, ('seq', 'res'), 0, 0, axis_index_groups=groups, ti...]
    all_to_all x3 -> x4, waiting for transfers between devices: 10.2 us -> 21.1 us  [across(): lax.all_to_all(blocks, ('seq', 'res'), 0, 0, axis_index_groups=groups, ti...]
    pallas_call x15, Pallas kernels: 37.3 us -> 31.1 us  [call(): pl.pallas_call(lambda *refs: kernel(*refs[:first], *refs[last:]), out_sha...]
    all_to_all x3 -> x4, starting transfers between devices: 11.7 us -> 17.9 us  [across(): lax.all_to_all(blocks, ('seq', 'res'), 0, 0, axis_index_groups=groups, ti...]
    unnamed x84 -> x110, local copies, waits for them, and re-layouts: 27.6 us -> 33.3 us
    ppermute x28, waiting for transfers between devices: 58.4 us -> 63.8 us  [swapped(): lax.ppermute(mine, axis_name, [(a, a ^ distance) for a in range(size)])]
    ppermute x28, starting transfers between devices: 24.9 us -> 20.6 us  [swapped(): lax.ppermute(mine, axis_name, [(a, a ^ distance) for a in range(size)])]
  transfers between devices with their start and end apart: 31 -> 32, of which waited for: 14 -> 14; matrix products, arithmetic and copies ran while one was open for 1% -> 1% of each run, Pallas kernels for 9% -> 11%
where the time goes in v6:
time: 203 us; the launch traced here: 202 us
  waiting for transfers between devices  84.9 us (42%)
  starting transfers between devices  38.5 us (19%)
  local copies, waits for them, and re-layouts  35 us (17%)
  Pallas kernels  31.1 us (15%)
  blocking collectives  10.3 us (5%)
    ppermute x28, waiting for transfers between devices, swapped(): lax.ppermute(mine, axis_name, [(a, a ^ distance) for a in range(size)])  63.8 us
    unnamed x110, local copies, waits for them, and re-layouts  33.3 us
    pallas_call x15, Pallas kernels, call(): pl.pallas_call(lambda *refs: kernel(*refs[:first], *refs[last:]), out_sha...  31.1 us
    all_to_all x4, waiting for transfers between devices, across(): lax.all_to_all(blocks, ('seq', 'res'), 0, 0, axis_index_groups=groups, ti...  21.1 us
    ppermute x28, starting transfers between devices, swapped(): lax.ppermute(mine, axis_name, [(a, a ^ distance) for a in range(size)])  20.6 us
    all_to_all x4, starting transfers between devices, across(): lax.all_to_all(blocks, ('seq', 'res'), 0, 0, axis_index_groups=groups, ti...  17.9 us
    all_gather x1, blocking collectives, head_body(): parts = lax.all_gather(sums, 'res', axis=0)  10.3 us
  transfers between devices with their start and end apart: 32, of which 14 were waited for; matrix products, arithmetic and copies ran while one was open for 1% of the time, Pallas kernels for 11%

profile of v6, /device:TPU:0, one launch (start us, length us, event | category | flops | bytes accessed | tf_op | source)
XLA Modules:
  0.0 201.8 jit_solution(13423938061967664504)
XLA Ops:
  4.9 6.0 %shard_map.109 = (bf16[16,192,128]{2,1,0:T(8,128)(2,1)}, f32[8,64,128]{2,1,0:T(8,128)S(1)}, f32[64,128]{1,0:T(8,128)S(1)}, f32[64,128]{1,0:T(8,128)S(1)}) custom-call(bf16[8,64,256]{2,1,0:T(8,128)(2,1)S(1)} %copy-done.4, bf16[256,1024]{1,0:T(8,128)(2,1)S(1)} %copy-done.2, bf16[64,128,128]{2,1,0:T(8,128)(2,1)S(1)} %copy-done, f32[8,128]{1,0:T(8,128)S(1)} %bitcast.11), custom_call_target="tpu_custom_call" | custom-call | flops 268435456 | bytes 4001792 | tf_op jit(solution)/shard_map/pallas_call | solution.py:583
  11.7 6.3 %all-to-all-start = ((bf16[16,192,128]{2,1,0:T(8,128)(2,1)}), bf16[16,192,128]{2,1,0:T(8,128)(2,1)S(1)}, u32[]{:S(2)}, u32[]{:S(2)}) async-start(bf16[16,192,128]{2,1,0:T(8,128)(2,1)} %get-tuple-element.26), calls=%async_computation | async-start | bytes 1572864 | tf_op jit(solution)/shard_map/all_to_all | solution.py:630
  18.1 2.0 %shard_map.110 = (bf16[16,128,128]{2,1,0:T(8,128)(2,1)}, bf16[2,4,64,256]{3,2,1,0:T(8,128)(2,1)S(1)}, bf16[2,4,64,256]{3,2,1,0:T(8,128)(2,1)S(1)}) custom-call(s32[4]{0:T(128)S(1)} %pad_add_fusion.refs_0_, bf16[8,64,256]{2,1,0:T(8,128)(2,1)S(1)} %copy-done.5, bf16[8,64,256]{2,1,0:T(8,128)(2,1)S(1)} %copy-done.18, bf16[256,1024]{1,0:T(8,128)(2,1)S(1)} %copy-done.3, ...), custom_call_target="tpu_custom_call" | custom-call | flops 268435456 | bytes 2228240 | tf_op jit(solution)/shard_map/pallas_call | solution.py:583
  20.1 11.2 %all-to-all-done.refs_1_.refs_5_ = bf16[16,192,128]{2,1,0:T(8,128)(2,1)S(1)} async-done(((bf16[16,192,128]{2,1,0:T(8,128)(2,1)}), bf16[16,192,128]{2,1,0:T(8,128)(2,1)S(1)}, u32[]{:S(2)}, u32[]{:S(2)}) %all-to-all-start) | async-done | bytes 786464 | tf_op jit(solution)/shard_map/all_to_all | solution.py:630
  31.3 3.6 %all-to-all-start.1 = ((bf16[16,128,128]{2,1,0:T(8,128)(2,1)}), bf16[16,128,128]{2,1,0:T(8,128)(2,1)S(1)}, u32[]{:S(2)}, u32[]{:S(2)}) async-start(bf16[16,128,128]{2,1,0:T(8,128)(2,1)} %get-tuple-element.33), calls=%async_computation.1 | async-start | bytes 1048576 | tf_op jit(solution)/shard_map/all_to_all | solution.py:630
  35.5 9.9 %all-to-all-done.1.refs_1_.refs_5_ = bf16[16,128,128]{2,1,0:T(8,128)(2,1)S(1)} async-done(((bf16[16,128,128]{2,1,0:T(8,128)(2,1)}), bf16[16,128,128]{2,1,0:T(8,128)(2,1)S(1)}, u32[]{:S(2)}, u32[]{:S(2)}) %all-to-all-start.1) | async-done | bytes 524320 | tf_op jit(solution)/shard_map/all_to_all | solution.py:630
  48.2 6.6 %collective-permute-done.2.refs_3_.refs_2_ = bf16[2,4,64,256]{3,2,1,0:T(8,128)(2,1)S(1)} collective-permute-done((bf16[2,4,64,256]{3,2,1,0:T(8,128)(2,1)S(1)}, bf16[2,4,64,256]{3,2,1,0:T(8,128)(2,1)S(1)}, u32[]{:S(2)}, u32[]{:S(2)}) %collective-permute-start.2) | collective-permute-done | bytes 262176 | tf_op jit(solution)/shard_map/ppermute | solution.py:596
  58.6 2.7 %collective-permute-start.4 = (f32[128,512]{1,0:T(8,128)S(1)}, f32[128,512]{1,0:T(8,128)S(1)}, u32[]{:S(2)}, u32[]{:S(2)}) collective-permute-start(f32[128,512]{1,0:T(8,128)S(1)} %get-tuple-element.32), channel_id=1, source_target_pairs={{0,16},{8,24},{16,0},{24,8},{1,17},{9,25},{17,1},{25,9},{2,18},{10... | collective-permute-start | bytes 786440 | tf_op jit(solution)/shard_map/ppermute | solution.py:596
  63.5 9.0 %collective-permute-done.9.refs_6_.refs_13_ = bf16[2,4,64,256]{3,2,1,0:T(8,128)(2,1)S(1)} collective-permute-done((bf16[2,4,64,256]{3,2,1,0:T(8,128)(2,1)S(1)}, bf16[2,4,64,256]{3,2,1,0:T(8,128)(2,1)S(1)}, u32[]{:S(2)}, u32[]{:S(2)}) %collective-permute-start.9) | collective-permute-done | bytes 262176 | tf_op jit(solution)/shard_map/ppermute | solution.py:596
  72.5 4.3 %collective-permute-done.10.refs_7_.refs_15_ = bf16[2,4,64,256]{3,2,1,0:T(8,128)(2,1)S(1)} collective-permute-done((bf16[2,4,64,256]{3,2,1,0:T(8,128)(2,1)S(1)}, bf16[2,4,64,256]{3,2,1,0:T(8,128)(2,1)S(1)}, u32[]{:S(2)}, u32[]{:S(2)}) %collective-permute-start.10) | collective-permute-done | bytes 262176 | tf_op jit(solution)/shard_map/ppermute | solution.py:596
  79.3 7.2 %collective-permute-done.22.refs_2_ = bf16[128,512]{1,0:T(8,128)(2,1)S(1)} collective-permute-done((bf16[128,512]{1,0:T(8,128)(2,1)S(1)}, bf16[128,512]{1,0:T(8,128)(2,1)S(1)}, u32[]{:S(2)}, u32[]{:S(2)}) %collective-permute-start.22) | collective-permute-done | bytes 131104 | tf_op jit(solution)/shard_map/ppermute | solution.py:596
  87.9 1.9 shard_map.116.refs_20_
  89.7 3.6 %all-to-all-start.3 = ((bf16[16,160,128]{2,1,0:T(8,128)(2,1)}), bf16[16,160,128]{2,1,0:T(8,128)(2,1)S(1)}, u32[]{:S(2)}, u32[]{:S(2)}) async-start(bf16[16,160,128]{2,1,0:T(8,128)(2,1)} %shard_map.116.refs_20_), calls=%async_computation.3 | async-start | bytes 1310720 | tf_op jit(solution)/shard_map/all_to_all | solution.py:630
  93.3 1.9 collective-permute-start.14
  99.3 10.2 %collective-permute-done.14.refs_6_.refs_5_ = bf16[2,4,64,256]{3,2,1,0:T(8,128)(2,1)S(1)} collective-permute-done((bf16[2,4,64,256]{3,2,1,0:T(8,128)(2,1)}, bf16[2,4,64,256]{3,2,1,0:T(8,128)(2,1)S(1)}, u32[]{:S(2)}, u32[]{:S(2)}) %collective-permute-start.14) | collective-permute-done | bytes 262176 | tf_op jit(solution)/shard_map/ppermute | solution.py:596
  111.5 3.6 %collective-permute-done.15.refs_7_.refs_6_ = bf16[2,4,64,256]{3,2,1,0:T(8,128)(2,1)S(1)} collective-permute-done((bf16[2,4,64,256]{3,2,1,0:T(8,128)(2,1)S(1)}, bf16[2,4,64,256]{3,2,1,0:T(8,128)(2,1)S(1)}, u32[]{:S(2)}, u32[]{:S(2)}) %collective-permute-start.15) | collective-permute-done | bytes 262176 | tf_op jit(solution)/shard_map/ppermute | solution.py:596
  116.6 4.1 %collective-permute-done.16.refs_8_.refs_7_ = bf16[2,4,64,256]{3,2,1,0:T(8,128)(2,1)S(1)} collective-permute-done((bf16[2,4,64,256]{3,2,1,0:T(8,128)(2,1)S(1)}, bf16[2,4,64,256]{3,2,1,0:T(8,128)(2,1)S(1)}, u32[]{:S(2)}, u32[]{:S(2)}) %collective-permute-start.16) | collective-permute-done | bytes 262176 | tf_op jit(solution)/shard_map/ppermute | solution.py:596
  122.0 7.6 %collective-permute-done.11.refs_2_ = bf16[128,512]{1,0:T(8,128)(2,1)S(1)} collective-permute-done((bf16[128,512]{1,0:T(8,128)(2,1)}, bf16[128,512]{1,0:T(8,128)(2,1)S(1)}, u32[]{:S(2)}, u32[]{:S(2)}) %collective-permute-start.11) | collective-permute-done | bytes 131104 | tf_op jit(solution)/shard_map/ppermute | solution.py:596
  139.4 4.4 %all-to-all-start.2 = ((bf16[16,128,128]{2,1,0:T(8,128)(2,1)}), bf16[16,128,128]{2,1,0:T(8,128)(2,1)}, u32[]{:S(2)}, u32[]{:S(2)}) async-start(bf16[16,128,128]{2,1,0:T(8,128)(2,1)} %shard_map.115.refs_19_), calls=%async_computation.2 | async-start | bytes 1048576 | tf_op jit(solution)/shard_map/all_to_all | solution.py:630
  161.6 4.6 %shard_map.119.refs_4_ = f32[320,128]{1,0:T(8,128)S(1)} custom-call(s32[4]{0:T(128)S(1)} %pad_add_fusion.refs_0_, bf16[2,4,64,256]{3,2,1,0:T(8,128)(2,1)S(1)} %copy-done.45, bf16[2,4,64,256]{3,2,1,0:T(8,128)(2,1)S(1)} %copy-done.7, bf16[2,4,64,256]{3,2,1,0:T(8,128)(2,1)S(1)} %copy-done.11, bf16[2,4,64,256]{3,2,1,0:T(8,128)(2,1)S(1)} %copy-done.17, ...), custom_call_target="tpu_custom_call" | custom-call | flops 1342177280 | bytes 5668880 | tf_op jit(solution)/shard_map/pallas_call | solution.py:583
  169.5 7.0 %collective-permute-done.26.refs_1_ = bf16[336,128]{1,0:T(8,128)(2,1)S(1)} collective-permute-done((bf16[336,128]{1,0:T(8,128)(2,1)S(1)}, bf16[336,128]{1,0:T(8,128)(2,1)S(1)}, u32[]{:S(2)}, u32[]{:S(2)}) %collective-permute-start.26) | collective-permute-done | bytes 86048 | tf_op jit(solution)/shard_map/ppermute | solution.py:596
  179.7 4.3 %shard_map.118 = bf16[64,128,128]{2,1,0:T(8,128)(2,1)} custom-call(bf16[16,160,128]{2,1,0:T(8,128)(2,1)S(1)} %all-to-all-done.3.refs_5_.refs_0_, bf16[64,128,128]{2,1,0:T(8,128)(2,1)S(1)} %copy-done.1, f32[8,128]{1,0:T(8,128)S(1)} %bitcast.12, f32[8,64,128]{2,1,0:T(8,128)S(1)} %copy-done.43, f32[64,128]{1,0:T(8,128)S(1)} %copy-done.40, f32[64,128]{1,0:T(8,128)S(1)} %copy-done.50), custom_call_target="tpu_custom_call" | custom-call | flops 268435456 | bytes 5181440 | tf_op jit(solution)/shard_map/pallas_call | solution.py:583
  185.8 3.1 %shard_map.117 = (bf16[8,64,256]{2,1,0:T(8,128)(2,1)}, bf16[8,64,256]{2,1,0:T(8,128)(2,1)}) custom-call(bf16[8,64,256]{2,1,0:T(8,128)(2,1)S(1)} %copy-done.5, bf16[8,64,256]{2,1,0:T(8,128)(2,1)S(1)} %copy-done.19, bf16[256,1024]{1,0:T(8,128)(2,1)S(1)} %copy-done.3, bf16[256,256]{1,0:T(8,128)(2,1)S(1)} %copy-done.37, ...), custom_call_target="tpu_custom_call" | custom-call | flops 469762048 | bytes 2883584 | tf_op jit(solution)/shard_map/pallas_call | solution.py:583
  189.9 10.3 %all-gather = bf16[2688,128]{1,0:T(8,128)(2,1)S(1)} all-gather(bf16[336,128]{1,0:T(8,128)(2,1)S(1)} %broadcast_select_fusion), channel_id=2, replica_groups=mesh['seq'=4,'res'=8] {'res'}, dimensions={0}, use_global_device_ids=true | all-gather | bytes 774144 | tf_op jit(solution)/shard_map/all_gather | solution.py:740
  (174 shorter events, 65.2 us)
Async XLA Ops:
  11.7 19.7 %all-to-all-start = ((bf16[16,192,128]{2,1,0:T(8,128)(2,1)}), bf16[16,192,128]{2,1,0:T(8,128)(2,1)S(1)}, u32[]{:S(2)}, u32[]{:S(2)}) async-start(bf16[16,192,128]{2,1,0:T(8,128)(2,1)} %get-tuple-element.26), calls=%async_computation | async-start | bytes 1572864 | tf_op jit(solution)/shard_map/all_to_all | solution.py:630
  31.3 14.1 %all-to-all-start.1 = ((bf16[16,128,128]{2,1,0:T(8,128)(2,1)}), bf16[16,128,128]{2,1,0:T(8,128)(2,1)S(1)}, u32[]{:S(2)}, u32[]{:S(2)}) async-start(bf16[16,128,128]{2,1,0:T(8,128)(2,1)} %get-tuple-element.33), calls=%async_computation.1 | async-start | bytes 1048576 | tf_op jit(solution)/shard_map/all_to_all | solution.py:630
  34.9 22.0 %collective-permute-start = (bf16[16,192,128]{2,1,0:T(8,128)(2,1)S(1)}, bf16[16,192,128]{2,1,0:T(8,128)(2,1)}, u32[]{:S(2)}, u32[]{:S(2)}) collective-permute-start(bf16[16,192,128]{2,1,0:T(8,128)(2,1)S(1)} %all-to-all-done.refs_1_.refs_5_), channel_id=1, source_target_pairs={{0,1},{1,0},{2,3},{3,2},{4,5},{5,4},{6,7},{7,6},{8,9},{9,8},{10,11... | collective-permute-start | bytes 2359304 | tf_op jit(solution)/shard_map/ppermute | solution.py:596
  35.2 10.2 %collective-permute-start.1 = (bf16[2,4,64,256]{3,2,1,0:T(8,128)(2,1)S(1)}, bf16[2,4,64,256]{3,2,1,0:T(8,128)(2,1)S(1)}, u32[]{:S(2)}, u32[]{:S(2)}) collective-permute-start(bf16[2,4,64,256]{3,2,1,0:T(8,128)(2,1)S(1)} %get-tuple-element.28), channel_id=1, source_target_pairs={{0,1},{1,0},{2,3},{3,2},{4,5},{5,4},{6,7},{7,6},{8,9},{9,8},{10,11... | collective-permute-start | bytes 786440 | tf_op jit(solution)/shard_map/ppermute | solution.py:596
  45.4 13.2 %collective-permute-start.5 = (bf16[16,128,128]{2,1,0:T(8,128)(2,1)S(1)}, bf16[16,128,128]{2,1,0:T(8,128)(2,1)S(1)}, u32[]{:S(2)}, u32[]{:S(2)}) collective-permute-start(bf16[16,128,128]{2,1,0:T(8,128)(2,1)S(1)} %all-to-all-done.1.refs_1_.refs_5_), channel_id=1, source_target_pairs={{0,1},{1,0},{2,3},{3,2},{4,5},{5,4},{6,7},{7,6},{8,9},{9,8},{10,11... | collective-permute-start | bytes 1572872 | tf_op jit(solution)/shard_map/ppermute | solution.py:596
  46.1 9.3 %collective-permute-start.3 = (bf16[2,4,64,256]{3,2,1,0:T(8,128)(2,1)S(1)}, bf16[2,4,64,256]{3,2,1,0:T(8,128)(2,1)S(1)}, u32[]{:S(2)}, u32[]{:S(2)}) collective-permute-start(bf16[2,4,64,256]{3,2,1,0:T(8,128)(2,1)S(1)} %get-tuple-element.30.refs_9_), channel_id=1, source_target_pairs={{0,4},{1,5},{2,6},{3,7},{4,0},{5,1},{6,2},{7,3},{8,12},{9,13},{10,... | collective-permute-start | bytes 786440 | tf_op jit(solution)/shard_map/ppermute | solution.py:596
  47.4 15.0 %collective-permute-start.7 = (bf16[2,4,64,256]{3,2,1,0:T(8,128)(2,1)S(1)}, bf16[2,4,64,256]{3,2,1,0:T(8,128)(2,1)S(1)}, u32[]{:S(2)}, u32[]{:S(2)}) collective-permute-start(bf16[2,4,64,256]{3,2,1,0:T(8,128)(2,1)S(1)} %get-tuple-element.29.refs_1_), channel_id=1, source_target_pairs={{0,4},{1,5},{2,6},{3,7},{4,0},{5,1},{6,2},{7,3},{8,12},{9,13},{10,... | collective-permute-start | bytes 786440 | tf_op jit(solution)/shard_map/ppermute | solution.py:596
  54.8 17.6 %collective-permute-start.9 = (bf16[2,4,64,256]{3,2,1,0:T(8,128)(2,1)S(1)}, bf16[2,4,64,256]{3,2,1,0:T(8,128)(2,1)S(1)}, u32[]{:S(2)}, u32[]{:S(2)}) collective-permute-start(bf16[2,4,64,256]{3,2,1,0:T(8,128)(2,1)S(1)} %get-tuple-element.30.refs_9_), channel_id=1, source_target_pairs={{0,8},{8,0},{16,24},{24,16},{1,9},{9,1},{17,25},{25,17},{2,10},{10... | collective-permute-start | bytes 786440 | tf_op jit(solution)/shard_map/ppermute | solution.py:596
  55.4 21.4 %collective-permute-start.10 = (bf16[2,4,64,256]{3,2,1,0:T(8,128)(2,1)S(1)}, bf16[2,4,64,256]{3,2,1,0:T(8,128)(2,1)S(1)}, u32[]{:S(2)}, u32[]{:S(2)}) collective-permute-start(bf16[2,4,64,256]{3,2,1,0:T(8,128)(2,1)S(1)} %collective-permute-done.3.refs_4_.refs_11_), channel_id=1, source_target_pairs={{0,8},{8,0},{16,24},{24,16},{1,9},{9,1},{17,25},{25,17},{2,10},{10... | collective-permute-start | bytes 786440 | tf_op jit(solution)/shard_map/ppermute | solution.py:596
  56.9 20.0 %collective-permute-start.8 = (bf16[2,4,64,256]{3,2,1,0:T(8,128)(2,1)S(1)}, bf16[2,4,64,256]{3,2,1,0:T(8,128)(2,1)S(1)}, u32[]{:S(2)}, u32[]{:S(2)}) collective-permute-start(bf16[2,4,64,256]{3,2,1,0:T(8,128)(2,1)S(1)} %collective-permute-done.2.refs_3_.refs_2_), channel_id=1, source_target_pairs={{0,4},{1,5},{2,6},{3,7},{4,0},{5,1},{6,2},{7,3},{8,12},{9,13},{10,... | collective-permute-start | bytes 786440 | tf_op jit(solution)/shard_map/ppermute | solution.py:596
  58.6 18.2 %collective-permute-start.4 = (f32[128,512]{1,0:T(8,128)S(1)}, f32[128,512]{1,0:T(8,128)S(1)}, u32[]{:S(2)}, u32[]{:S(2)}) collective-permute-start(f32[128,512]{1,0:T(8,128)S(1)} %get-tuple-element.32), channel_id=1, source_target_pairs={{0,16},{8,24},{16,0},{24,8},{1,17},{9,25},{17,1},{25,9},{2,18},{10... | collective-permute-start | bytes 786440 | tf_op jit(solution)/shard_map/ppermute | solution.py:596
  62.3 14.5 %collective-permute-start.6 = (bf16[128,512]{1,0:T(8,128)(2,1)S(1)}, bf16[128,512]{1,0:T(8,128)(2,1)S(1)}, u32[]{:S(2)}, u32[]{:S(2)}) collective-permute-start(bf16[128,512]{1,0:T(8,128)(2,1)S(1)} %get-tuple-element.36), channel_id=1, source_target_pairs={{0,16},{8,24},{16,0},{24,8},{1,17},{9,25},{17,1},{25,9},{2,18},{10... | collective-permute-start | bytes 393224 | tf_op jit(solution)/shard_map/ppermute | solution.py:596
  89.7 49.6 %all-to-all-start.3 = ((bf16[16,160,128]{2,1,0:T(8,128)(2,1)}), bf16[16,160,128]{2,1,0:T(8,128)(2,1)S(1)}, u32[]{:S(2)}, u32[]{:S(2)}) async-start(bf16[16,160,128]{2,1,0:T(8,128)(2,1)} %shard_map.116.refs_20_), calls=%async_computation.3 | async-start | bytes 1310720 | tf_op jit(solution)/shard_map/all_to_all | solution.py:630
  93.3 16.2 %collective-permute-start.14 = (bf16[2,4,64,256]{3,2,1,0:T(8,128)(2,1)}, bf16[2,4,64,256]{3,2,1,0:T(8,128)(2,1)S(1)}, u32[]{:S(2)}, u32[]{:S(2)}) collective-permute-start(bf16[2,4,64,256]{3,2,1,0:T(8,128)(2,1)} %copy-done.44), channel_id=1, source_target_pairs={{0,8},{8,0},{16,24},{24,16},{1,9},{9,1},{17,25},{25,17},{2,10},{10... | collective-permute-start | bytes 786440 | tf_op jit(solution)/shard_map/ppermute | solution.py:596
  95.2 15.8 %collective-permute-start.18 = (bf16[2,4,64,256]{3,2,1,0:T(8,128)(2,1)}, bf16[2,4,64,256]{3,2,1,0:T(8,128)(2,1)S(1)}, u32[]{:S(2)}, u32[]{:S(2)}) collective-permute-start(bf16[2,4,64,256]{3,2,1,0:T(8,128)(2,1)} %copy-done.46), channel_id=1, source_target_pairs={{0,2},{1,3},{2,0},{3,1},{4,6},{5,7},{6,4},{7,5},{8,10},{9,11},{10,... | collective-permute-start | bytes 786440 | tf_op jit(solution)/shard_map/ppermute | solution.py:596
  96.7 18.4 %collective-permute-start.15 = (bf16[2,4,64,256]{3,2,1,0:T(8,128)(2,1)S(1)}, bf16[2,4,64,256]{3,2,1,0:T(8,128)(2,1)S(1)}, u32[]{:S(2)}, u32[]{:S(2)}) collective-permute-start(bf16[2,4,64,256]{3,2,1,0:T(8,128)(2,1)S(1)} %collective-permute-done.2.refs_3_.refs_2_), channel_id=1, source_target_pairs={{0,8},{8,0},{16,24},{24,16},{1,9},{9,1},{17,25},{25,17},{2,10},{10... | collective-permute-start | bytes 786440 | tf_op jit(solution)/shard_map/ppermute | solution.py:596
  97.2 23.6 %collective-permute-start.16 = (bf16[2,4,64,256]{3,2,1,0:T(8,128)(2,1)S(1)}, bf16[2,4,64,256]{3,2,1,0:T(8,128)(2,1)S(1)}, u32[]{:S(2)}, u32[]{:S(2)}) collective-permute-start(bf16[2,4,64,256]{3,2,1,0:T(8,128)(2,1)S(1)} %collective-permute-done.7.refs_4_.refs_3_), channel_id=1, source_target_pairs={{0,8},{8,0},{16,24},{24,16},{1,9},{9,1},{17,25},{25,17},{2,10},{10... | collective-permute-start | bytes 786440 | tf_op jit(solution)/shard_map/ppermute | solution.py:596
  98.7 23.3 %collective-permute-start.19 = (bf16[2,4,64,256]{3,2,1,0:T(8,128)(2,1)S(1)}, bf16[2,4,64,256]{3,2,1,0:T(8,128)(2,1)S(1)}, u32[]{:S(2)}, u32[]{:S(2)}) collective-permute-start(bf16[2,4,64,256]{3,2,1,0:T(8,128)(2,1)S(1)} %collective-permute-done.3.refs_4_.refs_11_), channel_id=1, source_target_pairs={{0,2},{1,3},{2,0},{3,1},{4,6},{5,7},{6,4},{7,5},{8,10},{9,11},{10,... | collective-permute-start | bytes 786440 | tf_op jit(solution)/shard_map/ppermute | solution.py:596
  109.5 20.1 %collective-permute-start.20 = (bf16[2,4,64,256]{3,2,1,0:T(8,128)(2,1)}, bf16[2,4,64,256]{3,2,1,0:T(8,128)(2,1)S(1)}, u32[]{:S(2)}, u32[]{:S(2)}) collective-permute-start(bf16[2,4,64,256]{3,2,1,0:T(8,128)(2,1)} %copy-done.12), channel_id=1, source_target_pairs={{0,2},{1,3},{2,0},{3,1},{4,6},{5,7},{6,4},{7,5},{8,10},{9,11},{10,... | collective-permute-start | bytes 786440 | tf_op jit(solution)/shard_map/ppermute | solution.py:596
  111.0 18.7 %collective-permute-start.17 = (bf16[2,4,64,256]{3,2,1,0:T(8,128)(2,1)}, bf16[2,4,64,256]{3,2,1,0:T(8,128)(2,1)S(1)}, u32[]{:S(2)}, u32[]{:S(2)}) collective-permute-start(bf16[2,4,64,256]{3,2,1,0:T(8,128)(2,1)} %copy-done.16), channel_id=1, source_target_pairs={{0,8},{8,0},{16,24},{24,16},{1,9},{9,1},{17,25},{25,17},{2,10},{10... | collective-permute-start | bytes 786440 | tf_op jit(solution)/shard_map/ppermute | solution.py:596
  115.1 14.5 %collective-permute-start.21 = (bf16[2,4,64,256]{3,2,1,0:T(8,128)(2,1)}, bf16[2,4,64,256]{3,2,1,0:T(8,128)(2,1)S(1)}, u32[]{:S(2)}, u32[]{:S(2)}) collective-permute-start(bf16[2,4,64,256]{3,2,1,0:T(8,128)(2,1)} %copy-done.14), channel_id=1, source_target_pairs={{0,2},{1,3},{2,0},{3,1},{4,6},{5,7},{6,4},{7,5},{8,10},{9,11},{10,... | collective-permute-start | bytes 786440 | tf_op jit(solution)/shard_map/ppermute | solution.py:596
  120.7 8.9 %collective-permute-start.11 = (bf16[128,512]{1,0:T(8,128)(2,1)}, bf16[128,512]{1,0:T(8,128)(2,1)S(1)}, u32[]{:S(2)}, u32[]{:S(2)}) collective-permute-start(bf16[128,512]{1,0:T(8,128)(2,1)} %copy-done.51), channel_id=1, source_target_pairs={{0,16},{8,24},{16,0},{24,8},{1,17},{9,25},{17,1},{25,9},{2,18},{10... | collective-permute-start | bytes 393224 | tf_op jit(solution)/shard_map/ppermute | solution.py:596
  139.4 44.6 %all-to-all-start.2 = ((bf16[16,128,128]{2,1,0:T(8,128)(2,1)}), bf16[16,128,128]{2,1,0:T(8,128)(2,1)}, u32[]{:S(2)}, u32[]{:S(2)}) async-start(bf16[16,128,128]{2,1,0:T(8,128)(2,1)} %shard_map.115.refs_19_), calls=%async_computation.2 | async-start | bytes 1048576 | tf_op jit(solution)/shard_map/all_to_all | solution.py:630
  177.2 11.8 %collective-permute-start.27 = (bf16[336,128]{1,0:T(8,128)(2,1)}, bf16[336,128]{1,0:T(8,128)(2,1)}, u32[]{:S(2)}, u32[]{:S(2)}) collective-permute-start(bf16[336,128]{1,0:T(8,128)(2,1)} %shard_map.122), channel_id=1, source_target_pairs={{0,8},{8,0},{16,24},{24,16},{1,9},{9,1},{17,25},{25,17},{2,10},{10... | collective-permute-start | bytes 258056 | tf_op jit(solution)/shard_map/ppermute | solution.py:596
  (63 other events, 449.9 us)

commit v7 on v3

--- a/solution.py
+++ b/solution.py
@@ -154,7 +154,7 @@
     )
 
 
-VMEM_LIMIT = 48 * 1024 * 1024
+VMEM_LIMIT = 20 * 1024 * 1024
 LANES = 128
 SLOTS = 4
 NT = (((1,), (1,)), ((), ()))
@@ -233,6 +233,10 @@
     pack_heads(out_ref, residues, grad_gated * gate, residues)
 
 
+def centred(weight):
+    return weight - jnp.mean(weight, axis=1, keepdims=True)
+
+
 def query_kernel(scale, x_ref, wc_ref, pair_ref, weight_ref, out_ref, bias_ref, mean_ref, spread_ref):
     residues, width = x_ref.shape[1], x_ref.shape[2]
     heads = weight_ref.shape[0]
@@ -241,30 +245,31 @@
     pack_heads(out_ref, residues, f32_dot(normed, wc_ref[:, width : 2 * width]), residues)
 
     columns, channels = pair_ref.shape[1], pair_ref.shape[2]
-    first = weight_ref[...].astype(jnp.bfloat16)
-    rest = weight_ref[...] - first.astype(jnp.float32)
-    second, third = two_terms(rest)
+    weight = centred(weight_ref[...])
+    first = weight.astype(jnp.bfloat16)
+    second, third = two_terms(weight - first.astype(jnp.float32))
     share = jnp.full((heads, channels), 1.0 / channels, jnp.bfloat16)
     left = jnp.concatenate([first, second, third, share], axis=0)
-    ones = jnp.full((heads, channels), 1.0 / channels, jnp.bfloat16)
     average = jnp.full((channels, channels), 1.0 / channels, jnp.bfloat16)
+    step_rows = 8
 
     def rows(step, carry):
-        for k in range(8):
-            i = step * 8 + k
-            entries = pair_ref[i]
-            center = entries.astype(jnp.float32) - f32_dot(entries, average)
-            high, low = two_terms(center * center)
-            variance = f32_dot(ones, high, NT) + f32_dot(ones, low, NT)
-            spread = lax.rsqrt(variance + eps_norm)
-            raw = f32_dot(left, entries, NT)
-            bias = spread * (raw[:heads] + raw[heads : 2 * heads] + raw[2 * heads : 3 * heads])
-            bias_ref[:, i, :] = bias
-            mean_ref[pl.ds(i, 1), :] = raw[3 * heads : 3 * heads + 1]
-            spread_ref[pl.ds(i, 1), :] = spread[:1]
+        start = pl.multiple_of(step * step_rows, step_rows)
+        entries = pair_ref[pl.ds(start, step_rows)].reshape(step_rows * columns, channels)
+        center = entries.astype(jnp.float32) - f32_dot(entries, average)
+        high, low = two_terms(center * center)
+        variance = f32_dot(share, high, NT) + f32_dot(share, low, NT)
+        spread = lax.rsqrt(variance + eps_norm)
+        raw = f32_dot(left, entries, NT)
+        bias = spread * (raw[:heads] + raw[heads : 2 * heads] + raw[2 * heads : 3 * heads])
+        for k in range(step_rows):
+            lanes = slice(k * columns, (k + 1) * columns)
+            bias_ref[:, start + k, :] = bias[:, lanes]
+            mean_ref[pl.ds(start + k, 1), :] = raw[3 * heads : 3 * heads + 1, lanes]
+            spread_ref[pl.ds(start + k, 1), :] = spread[:1, lanes]
         return carry
 
-    lax.fori_loop(0, pair_ref.shape[0] // 8, rows, 0)
+    lax.fori_loop(0, pair_ref.shape[0] // step_rows, rows, 0)
     half = residues // 2
     for h in range(heads):
         for core in range(2):
@@ -318,7 +323,7 @@
                     ref[k * part : (k + 1) * part, columns] += bias
 
 
-def softmax_kernel(logit_ref, logit_other_ref, grad_ref, grad_other_ref, prob_ref, out_ref):
+def softmax_kernel(logit_ref, logit_other_ref, grad_ref, grad_other_ref, out_ref, prob_ref):
     logits = logit_ref[...] + logit_other_ref[...]
     lifted = jnp.exp(logits - jnp.max(logits, axis=-1, keepdims=True))
     softmax_out = lifted / jnp.sum(lifted, axis=-1, keepdims=True)
@@ -361,24 +366,6 @@
             )
 
 
-def gate_kernel(x_ref, grad_ref, wc_ref, wo_ref, blocks_ref, updated_ref, value_gate_ref, weight_ref):
-    residues, width = x_ref.shape[1], x_ref.shape[2]
-    tiles = width // LANES
-    normed = normalized(x_ref)[0].astype(jnp.bfloat16)
-    gate = gate_of(f32_dot(normed, wc_ref[:, 3 * width :]))
-    grad = grad_ref[...].reshape(-1, width)
-    grad_gated = f32_dot(grad, wo_ref[...], NT)
-    attended = unpack_heads(blocks_ref, 0, residues, tiles)
-    gated = (gate * attended).astype(jnp.bfloat16)
-    updated_ref[...] = f32_dot(gated, wo_ref[...]).astype(jnp.bfloat16).reshape(updated_ref.shape)
-    value_gate_ref[:, :width] = unpack_heads(blocks_ref, residues, residues, tiles).astype(
-        jnp.bfloat16
-    )
-    value_gate_ref[:, width:] = (grad_gated * attended * gate * (1.0 - gate)).astype(jnp.bfloat16)
-    weight_ref[:, : 2 * width] = f32_dot(normed, value_gate_ref[...], TN).astype(jnp.bfloat16)
-    weight_ref[:, 2 * width :] = f32_dot(gated, grad, TN).astype(jnp.bfloat16)
-
-
 def share_of(blocks_ref, row, part, heads):
     return jnp.concatenate(
         [
@@ -391,13 +378,46 @@
 
 
 def weight_kernel(
-    x_ref, blocks_ref, pair_ref, mean_ref, spread_ref, query_key_ref, weight_ref, share_ref
+    place_ref, x_ref, grad_ref, wc_ref, wo_ref, attended_ref, blocks_ref, pair_weight_ref,
+    updated_ref, projected_ref, keep_ref, send_ref, sums_ref,
 ):
     residues, width = x_ref.shape[1], x_ref.shape[2]
     tiles = width // LANES
-    heads = share_ref.shape[0]
-    part = residues // 2
-    share_ref[...] = share_of(blocks_ref, 2 * residues, part, heads)
+    core = place_ref[0]
+    normed = normalized(x_ref)[0].astype(jnp.bfloat16)
+    gate = gate_of(f32_dot(normed, wc_ref[:, 3 * width :]))
+    grad = grad_ref[...].reshape(-1, width)
+    grad_gated = f32_dot(grad, wo_ref[...], NT)
+    attended = unpack_heads(attended_ref, 0, residues, tiles)
+    gated = (gate * attended).astype(jnp.bfloat16)
+    updated_ref[...] = f32_dot(gated, wo_ref[...]).astype(jnp.bfloat16).reshape(updated_ref.shape)
+    parts = [
+        unpack_heads(blocks_ref, 0, residues, tiles),
+        unpack_heads(blocks_ref, residues, residues, tiles),
+        unpack_heads(attended_ref, residues, residues, tiles),
+        grad_gated * attended * gate * (1.0 - gate),
+    ]
+    for t in range(4):
+        projected_ref[:, t * width : (t + 1) * width] = parts[t].astype(jnp.bfloat16)
+    sums_ref[:, : 4 * width] = f32_dot(normed, projected_ref[...], TN).astype(jnp.bfloat16)
+    sums_ref[:, 4 * width : 5 * width] = f32_dot(gated, grad, TN).astype(jnp.bfloat16)
+    heads, channels = pair_weight_ref.shape
+    rows = sums_ref.shape[0] // heads
+    first = lax.broadcasted_iota(jnp.int32, (rows, channels), 0) == 0
+    for h in range(heads):
+        row = jnp.broadcast_to(pair_weight_ref[h : h + 1], (rows, channels))
+        sums_ref[h * rows : (h + 1) * rows, 5 * width :] = jnp.where(first, row, 0.0).astype(
+            jnp.bfloat16
+        )
+    for which, ref in ((core, keep_ref), (1 - core, send_ref)):
+        for block in range(heads // 2):
+            start = pl.multiple_of((2 * block + which) * rows, rows)
+            ref[block] = sums_ref[pl.ds(start, rows), :]
+
+
+def pair_weight_kernel(blocks_ref, pair_ref, mean_ref, spread_ref, out_ref, share_ref):
+    heads, part = share_ref.shape[0], pair_ref.shape[0] // 2
+    share_ref[...] = share_of(blocks_ref, blocks_ref.shape[1] - part, part, heads)
 
     def rows(step, carry):
         total, shift = carry
@@ -416,28 +436,12 @@
         rows,
         (jnp.zeros((2 * heads, channels), jnp.float32), jnp.zeros((heads, LANES), jnp.float32)),
     )
-    pair_weight = total[:heads] + total[heads:] - jnp.sum(shift, axis=1, keepdims=True)
-    normed = normalized(x_ref)[0].astype(jnp.bfloat16)
-    for t in range(2):
-        query_key_ref[:, t * width : (t + 1) * width] = unpack_heads(
-            blocks_ref, t * residues, residues, tiles
-        ).astype(jnp.bfloat16)
-    weight_ref[:, : 2 * width] = f32_dot(normed, query_key_ref[...], TN).astype(jnp.bfloat16)
-    rows_each = weight_ref.shape[0] // heads
-    first = lax.broadcasted_iota(jnp.int32, (rows_each, channels), 0) == 0
-    for h in range(heads):
-        row = jnp.broadcast_to(pair_weight[h : h + 1], (rows_each, channels))
-        weight_ref[h * rows_each : (h + 1) * rows_each, 2 * width :] = jnp.where(
-            first, row, 0.0
-        ).astype(jnp.bfloat16)
-
-
-def alignment_kernel(x_ref, wc_ref, query_key_ref, value_gate_ref, out_ref):
-    width = x_ref.shape[2]
+    out_ref[...] = total[:heads] + total[heads:] - jnp.sum(shift, axis=1, keepdims=True)
+
+
+def alignment_kernel(x_ref, wc_ref, projected_ref, out_ref):
     normed, spread = normalized(x_ref)
-    gradient = f32_dot(query_key_ref[...], wc_ref[:, : 2 * width], NT) + f32_dot(
-        value_gate_ref[...], wc_ref[:, 2 * width :], NT
-    )
+    gradient = f32_dot(projected_ref[...], wc_ref[...], NT)
     out_ref[...] = (
         layer_norm_backward(gradient, normed, spread).astype(jnp.bfloat16).reshape(out_ref.shape)
     )
@@ -447,7 +451,7 @@
     heads, channels = weight_ref.shape
     part = pair_ref.shape[0] // 2
     share_ref[...] = share_of(blocks_ref, blocks_row, part, heads)
-    first, second = two_terms(weight_ref[...])
+    first, second = two_terms(centred(weight_ref[...]))
     zero = jnp.zeros((heads, channels), jnp.bfloat16)
     top = lax.broadcasted_iota(jnp.int32, (heads, channels), 0) < 2
     ones = jnp.where(top, 1.0, 0.0).astype(jnp.bfloat16)
@@ -489,7 +493,7 @@
     lax.fori_loop(0, pair_ref.shape[0] // 8, rows, 0)
 
 
-def call(kernel, outs, *args, scratch=(), place=None, flops=0):
+def call(kernel, outs, *args, scratch=(), place=None, flops=0, after=()):
     whole = pl.BlockSpec(memory_space=pltpu.VMEM)
     specs = [whole] * len(args)
     if place is not None:
@@ -497,40 +501,21 @@
         args = (place,) + args
     shapes = [jax.ShapeDtypeStruct(*o) for o in outs]
     moved = sum(math.prod(a.shape) * a.dtype.itemsize for a in list(args) + shapes)
-    result = pl.pallas_call(
-        kernel,
+    first, last = len(args), len(args) + len(after)
+    return pl.pallas_call(
+        lambda *refs: kernel(*refs[:first], *refs[last:]),
         out_shape=shapes,
-        in_specs=specs,
+        in_specs=specs + [pl.BlockSpec(memory_space=pl.ANY)] * len(after),
         out_specs=[whole] * len(shapes),
         scratch_shapes=scratch,
         compiler_params=pltpu.CompilerParams(vmem_limit_bytes=VMEM_LIMIT),
         cost_estimate=pl.CostEstimate(flops=flops, bytes_accessed=moved, transcendentals=0),
-    )(*args)
-    return result
+    )(*args, *after)
 
 
 def swapped(mine, axis_name, distance):
     size = lax.axis_size(axis_name)
     return lax.ppermute(mine, axis_name, [(a, a ^ distance) for a in range(size)])
-
-
-def gathered_seq(mine):
-    size, index = lax.axis_size("seq"), lax.axis_index("seq")
-    rows = jnp.zeros((size,) + mine.shape, mine.dtype)
-    rows = lax.dynamic_update_index_in_dim(rows, mine, index, 0)
-    for k in range(1, size):
-        t = lax.ppermute(mine, "seq", [(a, (a + k) % size) for a in range(size)])
-        rows = lax.dynamic_update_index_in_dim(rows, t, (index - k) % size, 0)
-    return rows
-
-
-def summed_everywhere(parts):
-    size = lax.axis_size("res")
-    rows, columns = parts.shape
-    parts = lax.all_to_all(parts.reshape(size, rows // size, columns), "res", 0, 0, tiled=True)
-    part = jnp.sum(parts.astype(jnp.float32), axis=0).astype(jnp.bfloat16)
-    part = jnp.sum(gathered_seq(part).astype(jnp.float32), axis=0).astype(jnp.bfloat16)
-    return lax.all_gather(part, "res", axis=0)
 
 
 def fits_heads(alignment_rows, pair_entries, pair_weight):
@@ -557,7 +542,8 @@
     group = 2 * res_size
     groups = [[g * group + k for k in range(group)] for g in range(seq_half)]
     scale = 1.0 / math.sqrt(width // heads * sequences * seq_size)
-    place = jnp.stack([lax.axis_index("res") % 2, lax.axis_index("seq") // 2]).astype(jnp.int32)
+    res_index, seq_index = lax.axis_index("res"), lax.axis_index("seq")
+    place = jnp.stack([res_index % 2, seq_index // 2]).astype(jnp.int32)
     bf16, f32 = jnp.bfloat16, jnp.float32
 
     def across(blocks):
@@ -568,12 +554,6 @@
         return mine, far, swapped(mine, "res", 1), swapped(far, "res", 1)
 
     x, grad, wc, wo = alignment_rows, updated_gradient, combined_weight, output_weight
-    (value_blocks,) = call(
-        value_kernel, [((group, 2 * residues, LANES), bf16)], x, grad, wc, wo,
-        flops=8 * tokens * width * width,
-    )
-    value_blocks = across(value_blocks)
-    centred = (pair_weight - jnp.mean(pair_weight, axis=0, keepdims=True)).T
     query_blocks, bias, mean, spread = call(
         functools.partial(query_kernel, scale),
         [
@@ -582,25 +562,30 @@
             ((residues, LANES), f32),
             ((residues, LANES), f32),
         ],
-        x, wc, pair_entries, centred,
+        x, wc, pair_entries, pair_weight.T,
         flops=8 * tokens * width * width,
     )
     query_blocks = across(query_blocks)
-
-    def scores(blocks, left_row, right_row, with_bias, kind):
+    (value_blocks,) = call(
+        value_kernel, [((group, 2 * residues, LANES), bf16)], x, grad, wc, wo,
+        flops=8 * tokens * width * width,
+    )
+    value_blocks = across(value_blocks)
+
+    def scores(blocks, left_row, right_row, with_bias, kind, after=()):
         return call(
             functools.partial(score_kernel, residues, left_row, right_row, with_bias),
             [((total // 4, total), f32), ((total // 4, total), kind)],
             blocks, swapped(blocks, "res", 1),
-            place=place, flops=2 * total * total * width,
+            place=place, flops=2 * total * total * width, after=after,
         )
 
-    grad_mine, grad_sent = scores(value_blocks, residues, 0, False, bf16)
-    grad_other = swapped(grad_sent, "seq", seq_half)
     logit_mine, logit_sent = scores(query_blocks, 0, residues, True, f32)
     logit_other = swapped(logit_sent, "seq", seq_half)
+    grad_mine, grad_sent = scores(value_blocks, residues, 0, False, bf16, after=(logit_mine,))
+    grad_other = swapped(grad_sent, "seq", seq_half)
     quarter = ((total // 4, total), bf16)
-    probs, grad_logits = call(
+    grad_logits, probs = call(
         softmax_kernel, [quarter, quarter], logit_mine, logit_other, grad_mine, grad_other,
         flops=total * total,
     )
@@ -618,50 +603,53 @@
         )
         return across(out)
 
+    grad_blocks = products(all_quarters(grad_logits), query_blocks, residues, 0, True, scale)
     attended_blocks = products(all_quarters(probs), value_blocks, 0, residues, False, 1.0)
-    grad_blocks = products(all_quarters(grad_logits), query_blocks, residues, 0, True, scale)
-
-    updated, value_gate, early = call(
-        gate_kernel,
-        [(x.shape, bf16), ((tokens, 2 * width), bf16), ((width, 3 * width), bf16)],
-        x, grad, wc, wo, attended_blocks,
-        flops=12 * tokens * width * width,
-    )
-    early = summed_everywhere(early)
-    query_key, late = call(
-        weight_kernel,
-        [((tokens, 2 * width), bf16), ((width, 2 * width + channels), bf16)],
-        x, grad_blocks, pair_entries, mean, spread,
-        scratch=[pltpu.VMEM((heads, residues, LANES), f32)],
-        flops=4 * tokens * width * width,
-    )
-    late = summed_everywhere(late)
-    (alignment_gradient,) = call(
-        alignment_kernel, [(x.shape, bf16)], x, wc, query_key, value_gate,
-        flops=8 * tokens * width * width,
+
+    share = pltpu.VMEM((heads, residues, LANES), f32)
+    (pair_weight_part,) = call(
+        pair_weight_kernel, [((heads, channels), f32)],
+        grad_blocks, pair_entries, mean, spread,
+        scratch=[share], flops=4 * tokens * width * width,
     )
     (pair_gradient,) = call(
         functools.partial(pair_kernel, 2 * residues),
         [(pair_entries.shape, bf16)],
-        grad_blocks, pair_entries, centred, bias, mean, spread,
-        scratch=[pltpu.VMEM((heads, residues, LANES), f32)],
+        grad_blocks, pair_entries, pair_weight.T, bias, mean, spread,
+        scratch=[share], flops=8 * tokens * width * width,
+    )
+    columns = 5 * width + channels
+    rows = width // res_size
+    part_rows = ((res_size // 2, rows, columns), bf16)
+    updated, projected, keep, send = call(
+        weight_kernel,
+        [(x.shape, bf16), ((tokens, 4 * width), bf16), part_rows, part_rows],
+        x, grad, wc, wo, attended_blocks, grad_blocks, pair_weight_part,
+        scratch=[pltpu.VMEM((width, columns), bf16)],
+        place=place, flops=24 * tokens * width * width,
+    )
+    (alignment_gradient,) = call(
+        alignment_kernel, [(x.shape, bf16)], x, wc, projected,
         flops=8 * tokens * width * width,
     )
 
-    combined_weight_gradient = (
-        jnp.concatenate([late[:, :, : 2 * width], early[:, :, : 2 * width]], axis=-1)
-        .reshape(wc.shape)
-        .astype(f32)
-    )
-    output_weight_gradient = early[:, :, 2 * width :].reshape(wo.shape).astype(f32)
-    pair_weight_gradient = late[:, 0, 2 * width :].T.astype(f32)
+    def added(mine, other):
+        return (mine.astype(f32) + other.astype(f32)).astype(bf16)
+
+    parts = added(keep, swapped(send, "res", 1))
+    chips = [[2 * k + core for k in range(res_size // 2)] for core in range(2)]
+    parts = lax.all_to_all(parts, "res", 0, 0, axis_index_groups=chips, tiled=True)
+    part = jnp.sum(parts.astype(f32), axis=0).astype(bf16)
+    part = added(part, swapped(part, "seq", 1))
+    part = added(part, swapped(part, "seq", seq_half))
+    whole = lax.all_gather(part, "res", axis=0)
     return (
         updated,
         alignment_gradient,
         pair_gradient,
-        combined_weight_gradient,
-        output_weight_gradient,
-        pair_weight_gradient,
+        whole[:, :, : 4 * width].reshape(wc.shape).astype(f32),
+        whole[:, :, 4 * width : 5 * width].reshape(wo.shape).astype(f32),
+        whole[:, 0, 5 * width :].T.astype(f32),
     )
 
 

time: 182 us -> 165 us (0.907)
  starting transfers between devices: 39.8 us -> 26.1 us
  Pallas kernels: 30.3 us -> 21.8 us
  waiting for transfers between devices: 72.4 us -> 75.1 us
    all_to_all x0 -> x1, blocking collectives: none -> 10.5 us  [head_body(): lax.all_to_all(parts, 'res', 0, 0, axis_index_groups=chips, tiled=True)]
    all_gather x2 -> x1, blocking collectives: 18.9 us -> 9.59 us  [head_body(): whole = lax.all_gather(part, 'res', axis=0)]
    ppermute x6 -> x0, starting transfers between devices: 9.14 us -> none  [gathered_seq(): t = lax.ppermute(mine, 'seq', [(a, (a + k) % size) for a in range(size)])]
    pallas_call x11, Pallas kernels: 30.3 us -> 21.8 us  [call(): pl.pallas_call(lambda *refs: kernel(*refs[:first], *refs[last:]), out_sha...]
    all_to_all x2 -> x0, starting transfers between devices: 8.12 us -> none  [summed_everywhere(): lax.all_to_all(parts.reshape(size, rows // size, columns), 'res', 0, 0, t...]
    ppermute x10 -> x13, waiting for transfers between devices: 36.7 us -> 43.9 us  [swapped(): lax.ppermute(mine, axis_name, [(a, a ^ distance) for a in range(size)])]
    ppermute x6 -> x0, waiting for transfers between devices: 6.85 us -> none  [gathered_seq(): t = lax.ppermute(mine, 'seq', [(a, (a + k) % size) for a in range(size)])]
    ppermute x10 -> x13, starting transfers between devices: 4.33 us -> 7.05 us  [swapped(): lax.ppermute(mine, axis_name, [(a, a ^ distance) for a in range(size)])]
  transfers between devices with their start and end apart: 22 -> 17, of which waited for: 14 -> 10; matrix products, arithmetic and copies ran while one was open for 1% -> 0% of each run, Pallas kernels for 8% -> 7%
where the time goes in v7:
time: 165 us; the launch traced here: 164 us
  waiting for transfers between devices  75.1 us (46%)
  starting transfers between devices  26.1 us (16%)
  Pallas kernels  21.8 us (13%)
  blocking collectives  20.1 us (12%)
  local copies, waits for them, and re-layouts  15.1 us (9%)
  other arithmetic  4.59 us (3%)
    ppermute x13, waiting for transfers between devices, swapped(): lax.ppermute(mine, axis_name, [(a, a ^ distance) for a in range(size)])  43.9 us
    all_to_all x4, waiting for transfers between devices, across(): lax.all_to_all(blocks, ('seq', 'res'), 0, 0, axis_index_groups=groups, ti...  31.2 us
    pallas_call x11, Pallas kernels, call(): pl.pallas_call(lambda *refs: kernel(*refs[:first], *refs[last:]), out_sha...  21.8 us
    all_to_all x4, starting transfers between devices, across(): lax.all_to_all(blocks, ('seq', 'res'), 0, 0, axis_index_groups=groups, ti...  19 us
    unnamed x48, local copies, waits for them, and re-layouts  15.1 us
    all_to_all x1, blocking collectives, head_body(): lax.all_to_all(parts, 'res', 0, 0, axis_index_groups=chips, tiled=True)  10.5 us
    all_gather x1, blocking collectives, head_body(): whole = lax.all_gather(part, 'res', axis=0)  9.59 us
    ppermute x13, starting transfers between devices, swapped(): lax.ppermute(mine, axis_name, [(a, a ^ distance) for a in range(size)])  7.05 us
  transfers between devices with their start and end apart: 17, of which 10 were waited for; matrix products, arithmetic and copies ran while one was open for 0% of the time, Pallas kernels for 7%

profile of v7, /device:TPU:0, one launch (start us, length us, event | category | flops | bytes accessed | tf_op | source)
XLA Modules:
  0.0 163.6 jit_solution(4085447311407757690)
XLA Ops:
  0.6 1.6 copy-done
  4.9 6.0 %shard_map.109 = (bf16[16,192,128]{2,1,0:T(8,128)(2,1)}, f32[8,64,128]{2,1,0:T(8,128)S(1)}, f32[64,128]{1,0:T(8,128)S(1)}, f32[64,128]{1,0:T(8,128)S(1)}) custom-call(bf16[8,64,256]{2,1,0:T(8,128)(2,1)S(1)} %copy-done.6, bf16[256,1024]{1,0:T(8,128)(2,1)S(1)} %copy-done.2, bf16[64,128,128]{2,1,0:T(8,128)(2,1)S(1)} %copy-done, f32[8,128]{1,0:T(8,128)S(1)} %bitcast.13), custom_call_target="tpu_custom_call" | custom-call | flops 268435456 | bytes 4001792 | tf_op jit(solution)/shard_map/pallas_call | solution.py:505
  11.7 6.3 %all-to-all-start = ((bf16[16,192,128]{2,1,0:T(8,128)(2,1)}), bf16[16,192,128]{2,1,0:T(8,128)(2,1)S(1)}, u32[]{:S(2)}, u32[]{:S(2)}) async-start(bf16[16,192,128]{2,1,0:T(8,128)(2,1)} %get-tuple-element.20), calls=%async_computation | async-start | bytes 1572864 | tf_op jit(solution)/shard_map/all_to_all | solution.py:550
  18.0 1.5 shard_map.111
  19.5 11.8 %all-to-all-done.refs_1_.refs_5_ = bf16[16,192,128]{2,1,0:T(8,128)(2,1)S(1)} async-done(((bf16[16,192,128]{2,1,0:T(8,128)(2,1)}), bf16[16,192,128]{2,1,0:T(8,128)(2,1)S(1)}, u32[]{:S(2)}, u32[]{:S(2)}) %all-to-all-start) | async-done | bytes 786464 | tf_op jit(solution)/shard_map/all_to_all | solution.py:550
  31.3 3.6 %all-to-all-start.1 = ((bf16[16,128,128]{2,1,0:T(8,128)(2,1)}), bf16[16,128,128]{2,1,0:T(8,128)(2,1)S(1)}, u32[]{:S(2)}, u32[]{:S(2)}) async-start(bf16[16,128,128]{2,1,0:T(8,128)(2,1)} %shard_map.111), calls=%async_computation.1 | async-start | bytes 1048576 | tf_op jit(solution)/shard_map/all_to_all | solution.py:550
  35.2 10.2 %all-to-all-done.1.refs_1_.refs_5_ = bf16[16,128,128]{2,1,0:T(8,128)(2,1)S(1)} async-done(((bf16[16,128,128]{2,1,0:T(8,128)(2,1)}), bf16[16,128,128]{2,1,0:T(8,128)(2,1)S(1)}, u32[]{:S(2)}, u32[]{:S(2)}) %all-to-all-start.1) | async-done | bytes 524320 | tf_op jit(solution)/shard_map/all_to_all | solution.py:550
  46.5 2.7 %collective-permute-start.1 = (f32[128,512]{1,0:T(8,128)S(1)}, f32[128,512]{1,0:T(8,128)S(1)}, u32[]{:S(2)}, u32[]{:S(2)}) collective-permute-start(f32[128,512]{1,0:T(8,128)S(1)} %get-tuple-element.22), channel_id=1, source_target_pairs={{0,16},{8,24},{16,0},{24,8},{1,17},{9,25},{17,1},{25,9},{2,18},{10... | collective-permute-start | bytes 786440 | tf_op jit(solution)/shard_map/ppermute | solution.py:518
  51.0 16.4 %collective-permute-done.3.refs_3_ = bf16[128,512]{1,0:T(8,128)(2,1)S(1)} collective-permute-done((bf16[128,512]{1,0:T(8,128)(2,1)S(1)}, bf16[128,512]{1,0:T(8,128)(2,1)S(1)}, u32[]{:S(2)}, u32[]{:S(2)}) %collective-permute-start.3) | collective-permute-done | bytes 131104 | tf_op jit(solution)/shard_map/ppermute | solution.py:518
  68.5 8.7 %collective-permute-done.7.refs_2_ = bf16[128,512]{1,0:T(8,128)(2,1)S(1)} collective-permute-done((bf16[128,512]{1,0:T(8,128)(2,1)S(1)}, bf16[128,512]{1,0:T(8,128)(2,1)S(1)}, u32[]{:S(2)}, u32[]{:S(2)}) %collective-permute-start.7) | collective-permute-done | bytes 131104 | tf_op jit(solution)/shard_map/ppermute | solution.py:518
  77.2 1.3 collective-permute-done.9.refs_4_
  80.4 3.7 %all-to-all-start.3 = ((bf16[16,160,128]{2,1,0:T(8,128)(2,1)}), bf16[16,160,128]{2,1,0:T(8,128)(2,1)S(1)}, u32[]{:S(2)}, u32[]{:S(2)}) async-start(bf16[16,160,128]{2,1,0:T(8,128)(2,1)} %copy-done.5), calls=%async_computation.3 | async-start | bytes 1310720 | tf_op jit(solution)/shard_map/all_to_all | solution.py:550
  84.5 10.5 %collective-permute-done.4.refs_2_ = bf16[128,512]{1,0:T(8,128)(2,1)S(1)} collective-permute-done((bf16[128,512]{1,0:T(8,128)(2,1)}, bf16[128,512]{1,0:T(8,128)(2,1)S(1)}, u32[]{:S(2)}, u32[]{:S(2)}) %collective-permute-start.4) | collective-permute-done | bytes 131104 | tf_op jit(solution)/shard_map/ppermute | solution.py:518
  95.0 1.3 collective-permute-done.6.refs_4_
  99.1 5.4 %all-to-all-start.2 = ((bf16[16,128,128]{2,1,0:T(8,128)(2,1)}), bf16[16,128,128]{2,1,0:T(8,128)(2,1)}, u32[]{:S(2)}, u32[]{:S(2)}) async-start(bf16[16,128,128]{2,1,0:T(8,128)(2,1)} %copy-done.10), calls=%async_computation.2 | async-start | bytes 1048576 | tf_op jit(solution)/shard_map/all_to_all | solution.py:550
  104.5 1.5 shard_map.116.refs_7_
  106.0 9.1 %all-to-all-done.2.refs_5_ = bf16[16,128,128]{2,1,0:T(8,128)(2,1)} async-done(((bf16[16,128,128]{2,1,0:T(8,128)(2,1)}), bf16[16,128,128]{2,1,0:T(8,128)(2,1)}, u32[]{:S(2)}, u32[]{:S(2)}) %all-to-all-start.2) | async-done | bytes 524320 | tf_op jit(solution)/shard_map/all_to_all | solution.py:550
  117.9 2.8 %shard_map.117 = (bf16[8,64,256]{2,1,0:T(8,128)(2,1)}, bf16[512,1024]{1,0:T(8,128)(2,1)S(1)}, bf16[4,32,1408]{2,1,0:T(8,128)(2,1)S(1)}, bf16[4,32,1408]{2,1,0:T(8,128)(2,1)S(1)}) custom-call(s32[2]{0:T(128)S(1)} %pad_add_fusion.refs_0_, bf16[8,64,256]{2,1,0:T(8,128)(2,1)S(1)} %copy-done.8, bf16[8,64,256]{2,1,0:T(8,128)(2,1)S(1)} %copy-done.16, ...), custom_call_target="tpu_custom_call" | custom-call | flops 805306368 | bytes 4395016 | tf_op jit(solution)/shard_map/pallas_call | solution.py:505
  121.7 1.7 %collective-permute-done.10 = bf16[4,32,1408]{2,1,0:T(8,128)(2,1)S(1)} collective-permute-done((bf16[4,32,1408]{2,1,0:T(8,128)(2,1)S(1)}, bf16[4,32,1408]{2,1,0:T(8,128)(2,1)S(1)}, u32[]{:S(2)}, u32[]{:S(2)}) %collective-permute-start.10) | collective-permute-done | bytes 360480 | tf_op jit(solution)/shard_map/ppermute | solution.py:518
  123.5 10.5 %all_to_all.25 = bf16[4,32,1408]{2,1,0:T(8,128)(2,1)} all-to-all(bf16[4,32,1408]{2,1,0:T(8,128)(2,1)S(1)} %add_convert_fusion), channel_id=1, replica_groups={{0,2,4,6},{1,3,5,7},{8,10,12,14},{9,11,13,15},{16,18,20,22},{17,19,21,2..., dimensions={0} | all-to-all | bytes 720896 | tf_op jit(solution)/shard_map/all_to_all | solution.py:641
  135.7 4.0 %collective-permute-done.11 = bf16[32,1408]{1,0:T(8,128)(2,1)S(1)} collective-permute-done((bf16[32,1408]{1,0:T(8,128)(2,1)S(1)}, bf16[32,1408]{1,0:T(8,128)(2,1)S(1)}, u32[]{:S(2)}, u32[]{:S(2)}) %collective-permute-start.11) | collective-permute-done | bytes 90144 | tf_op jit(solution)/shard_map/ppermute | solution.py:518
  140.5 2.2 %collective-permute-start.12 = (bf16[32,1408]{1,0:T(8,128)(2,1)S(1)}, bf16[32,1408]{1,0:T(8,128)(2,1)S(1)}, u32[]{:S(2)}, u32[]{:S(2)}) collective-permute-start(bf16[32,1408]{1,0:T(8,128)(2,1)S(1)} %add_convert_fusion.2), channel_id=1, source_target_pairs={{0,16},{8,24},{16,0},{24,8},{1,17},{9,25},{17,1},{25,9},{2,18},{10... | collective-permute-start | bytes 270344 | tf_op jit(solution)/shard_map/ppermute | solution.py:518
  147.2 4.3 %shard_map.119 = bf16[64,128,128]{2,1,0:T(8,128)(2,1)} custom-call(bf16[16,160,128]{2,1,0:T(8,128)(2,1)S(1)} %all-to-all-done.3.refs_0_.refs_6_, bf16[64,128,128]{2,1,0:T(8,128)(2,1)S(1)} %copy-done.1, f32[8,128]{1,0:T(8,128)S(1)} %bitcast.14, f32[8,64,128]{2,1,0:T(8,128)S(1)} %copy-done.14, f32[64,128]{1,0:T(8,128)S(1)} %get-tuple-element.27.refs_2_.refs_4_, ...), custom_call_target="tpu_custom_call" | custom-call | flops 268435456 | bytes 5181440 | tf_op jit(solution)/shard_map/pallas_call | solution.py:505
  151.5 9.6 %all-gather = bf16[256,1408]{1,0:T(8,128)(2,1)S(1)} all-gather(bf16[32,1408]{1,0:T(8,128)(2,1)S(1)} %add_convert_fusion.1), channel_id=2, replica_groups=mesh['seq'=4,'res'=8] {'res'}, dimensions={0}, use_global_device_ids=true | all-gather | bytes 811008 | tf_op jit(solution)/shard_map/all_gather | solution.py:645
  (81 shorter events, 26.0 us)
Async XLA Ops:
  4.9 13.0 %copy-start.3 = (bf16[256,1024]{1,0:T(8,128)(2,1)S(1)}, bf16[256,1024]{1,0:T(8,128)(2,1)}, u32[]{:S(2)}) copy-start(bf16[256,1024]{1,0:T(8,128)(2,1)} %refs_1_.10) | copy-start | bytes 1572868
  4.9 13.1 %copy-start.7 = (bf16[8,64,256]{2,1,0:T(8,128)(2,1)S(1)}, bf16[8,64,256]{2,1,0:T(8,128)(2,1)}, u32[]{:S(2)}) copy-start(bf16[8,64,256]{2,1,0:T(8,128)(2,1)} %refs_0_.5) | copy-start | bytes 786436
  4.9 13.1 %copy-start.15 = (bf16[8,64,256]{2,1,0:T(8,128)(2,1)S(1)}, bf16[8,64,256]{2,1,0:T(8,128)(2,1)}, u32[]{:S(2)}) copy-start(bf16[8,64,256]{2,1,0:T(8,128)(2,1)} %refs_2_.5) | copy-start | bytes 786436
  4.9 13.1 %copy-start.19 = (bf16[256,256]{1,0:T(8,128)(2,1)S(1)}, bf16[256,256]{1,0:T(8,128)(2,1)}, u32[]{:S(2)}) copy-start(bf16[256,256]{1,0:T(8,128)(2,1)} %refs_4_.1) | copy-start | bytes 393220
  11.7 19.6 %all-to-all-start = ((bf16[16,192,128]{2,1,0:T(8,128)(2,1)}), bf16[16,192,128]{2,1,0:T(8,128)(2,1)S(1)}, u32[]{:S(2)}, u32[]{:S(2)}) async-start(bf16[16,192,128]{2,1,0:T(8,128)(2,1)} %get-tuple-element.20), calls=%async_computation | async-start | bytes 1572864 | tf_op jit(solution)/shard_map/all_to_all | solution.py:550
  31.3 14.1 %all-to-all-start.1 = ((bf16[16,128,128]{2,1,0:T(8,128)(2,1)}), bf16[16,128,128]{2,1,0:T(8,128)(2,1)S(1)}, u32[]{:S(2)}, u32[]{:S(2)}) async-start(bf16[16,128,128]{2,1,0:T(8,128)(2,1)} %shard_map.111), calls=%async_computation.1 | async-start | bytes 1048576 | tf_op jit(solution)/shard_map/all_to_all | solution.py:550
  34.9 10.6 %collective-permute-start = (bf16[16,192,128]{2,1,0:T(8,128)(2,1)S(1)}, bf16[16,192,128]{2,1,0:T(8,128)(2,1)S(1)}, u32[]{:S(2)}, u32[]{:S(2)}) collective-permute-start(bf16[16,192,128]{2,1,0:T(8,128)(2,1)S(1)} %all-to-all-done.refs_1_.refs_5_), channel_id=1, source_target_pairs={{0,1},{1,0},{2,3},{3,2},{4,5},{5,4},{6,7},{7,6},{8,9},{9,8},{10,11... | collective-permute-start | bytes 2359304 | tf_op jit(solution)/shard_map/ppermute | solution.py:518
  45.4 3.8 %collective-permute-start.2 = (bf16[16,128,128]{2,1,0:T(8,128)(2,1)S(1)}, bf16[16,128,128]{2,1,0:T(8,128)(2,1)S(1)}, u32[]{:S(2)}, u32[]{:S(2)}) collective-permute-start(bf16[16,128,128]{2,1,0:T(8,128)(2,1)S(1)} %all-to-all-done.1.refs_1_.refs_5_), channel_id=1, source_target_pairs={{0,1},{1,0},{2,3},{3,2},{4,5},{5,4},{6,7},{7,6},{8,9},{9,8},{10,11... | collective-permute-start | bytes 1572872 | tf_op jit(solution)/shard_map/ppermute | solution.py:518
  46.5 20.9 %collective-permute-start.1 = (f32[128,512]{1,0:T(8,128)S(1)}, f32[128,512]{1,0:T(8,128)S(1)}, u32[]{:S(2)}, u32[]{:S(2)}) collective-permute-start(f32[128,512]{1,0:T(8,128)S(1)} %get-tuple-element.22), channel_id=1, source_target_pairs={{0,16},{8,24},{16,0},{24,8},{1,17},{9,25},{17,1},{25,9},{2,18},{10... | collective-permute-start | bytes 786440 | tf_op jit(solution)/shard_map/ppermute | solution.py:518
  50.2 17.2 %collective-permute-start.3 = (bf16[128,512]{1,0:T(8,128)(2,1)S(1)}, bf16[128,512]{1,0:T(8,128)(2,1)S(1)}, u32[]{:S(2)}, u32[]{:S(2)}) collective-permute-start(bf16[128,512]{1,0:T(8,128)(2,1)S(1)} %get-tuple-element.24), channel_id=1, source_target_pairs={{0,16},{8,24},{16,0},{24,8},{1,17},{9,25},{17,1},{25,9},{2,18},{10... | collective-permute-start | bytes 393224 | tf_op jit(solution)/shard_map/ppermute | solution.py:518
  68.4 8.8 %collective-permute-start.7 = (bf16[128,512]{1,0:T(8,128)(2,1)S(1)}, bf16[128,512]{1,0:T(8,128)(2,1)S(1)}, u32[]{:S(2)}, u32[]{:S(2)}) collective-permute-start(bf16[128,512]{1,0:T(8,128)(2,1)S(1)} %get-tuple-element.26.refs_1_), channel_id=1, source_target_pairs={{0,16},{8,24},{16,0},{24,8},{1,17},{9,25},{17,1},{25,9},{2,18},{10... | collective-permute-start | bytes 393224 | tf_op jit(solution)/shard_map/ppermute | solution.py:518
  68.4 8.8 %collective-permute-start.8 = (bf16[128,512]{1,0:T(8,128)(2,1)S(1)}, bf16[128,512]{1,0:T(8,128)(2,1)S(1)}, u32[]{:S(2)}, u32[]{:S(2)}) collective-permute-start(bf16[128,512]{1,0:T(8,128)(2,1)S(1)} %get-tuple-element.26.refs_1_), channel_id=1, source_target_pairs={{0,1},{1,0},{2,3},{3,2},{4,5},{5,4},{6,7},{7,6},{8,9},{9,8},{10,11... | collective-permute-start | bytes 393224 | tf_op jit(solution)/shard_map/ppermute | solution.py:518
  77.2 1.3 collective-permute-start.9
  80.4 24.1 %copy-start.1 = (bf16[64,128,128]{2,1,0:T(8,128)(2,1)S(1)}, bf16[64,128,128]{2,1,0:T(8,128)(2,1)}, u32[]{:S(2)}) copy-start(bf16[64,128,128]{2,1,0:T(8,128)(2,1)} %refs_1_.11) | copy-start | bytes 6291460
  80.4 18.6 %all-to-all-start.3 = ((bf16[16,160,128]{2,1,0:T(8,128)(2,1)}), bf16[16,160,128]{2,1,0:T(8,128)(2,1)S(1)}, u32[]{:S(2)}, u32[]{:S(2)}) async-start(bf16[16,160,128]{2,1,0:T(8,128)(2,1)} %copy-done.5), calls=%async_computation.3 | async-start | bytes 1310720 | tf_op jit(solution)/shard_map/all_to_all | solution.py:550
  84.1 10.8 %collective-permute-start.4 = (bf16[128,512]{1,0:T(8,128)(2,1)}, bf16[128,512]{1,0:T(8,128)(2,1)S(1)}, u32[]{:S(2)}, u32[]{:S(2)}) collective-permute-start(bf16[128,512]{1,0:T(8,128)(2,1)} %copy-done.17), channel_id=1, source_target_pairs={{0,16},{8,24},{16,0},{24,8},{1,17},{9,25},{17,1},{25,9},{2,18},{10... | collective-permute-start | bytes 393224 | tf_op jit(solution)/shard_map/ppermute | solution.py:518
  84.2 10.8 %collective-permute-start.5 = (bf16[128,512]{1,0:T(8,128)(2,1)}, bf16[128,512]{1,0:T(8,128)(2,1)S(1)}, u32[]{:S(2)}, u32[]{:S(2)}) collective-permute-start(bf16[128,512]{1,0:T(8,128)(2,1)} %copy-done.17), channel_id=1, source_target_pairs={{0,1},{1,0},{2,3},{3,2},{4,5},{5,4},{6,7},{7,6},{8,9},{9,8},{10,11... | collective-permute-start | bytes 393224 | tf_op jit(solution)/shard_map/ppermute | solution.py:518
  95.0 1.3 collective-permute-start.6
  99.0 16.1 %copy-start.4 = (bf16[256,1024]{1,0:T(8,128)(2,1)S(1)}, bf16[256,1024]{1,0:T(8,128)(2,1)}, u32[]{:S(2)}) copy-start(bf16[256,1024]{1,0:T(8,128)(2,1)} %refs_1_.10) | copy-start | bytes 1572868
  99.1 16.1 %all-to-all-start.2 = ((bf16[16,128,128]{2,1,0:T(8,128)(2,1)}), bf16[16,128,128]{2,1,0:T(8,128)(2,1)}, u32[]{:S(2)}, u32[]{:S(2)}) async-start(bf16[16,128,128]{2,1,0:T(8,128)(2,1)} %copy-done.10), calls=%async_computation.2 | async-start | bytes 1048576 | tf_op jit(solution)/shard_map/all_to_all | solution.py:550
  121.7 1.7 %collective-permute-start.10 = (bf16[4,32,1408]{2,1,0:T(8,128)(2,1)S(1)}, bf16[4,32,1408]{2,1,0:T(8,128)(2,1)S(1)}, u32[]{:S(2)}, u32[]{:S(2)}) collective-permute-start(bf16[4,32,1408]{2,1,0:T(8,128)(2,1)S(1)} %get-tuple-element.33), channel_id=1, source_target_pairs={{0,1},{1,0},{2,3},{3,2},{4,5},{5,4},{6,7},{7,6},{8,9},{9,8},{10,11... | collective-permute-start | bytes 1081352 | tf_op jit(solution)/shard_map/ppermute | solution.py:518
  123.4 22.8 %copy-start.22 = (f32[128,8]{0,1:T(8,128)S(1)}, f32[128,8]{0,1:T(8,128)}, u32[]{:S(2)}) copy-start(f32[128,8]{0,1:T(8,128)} %param.10) | copy-start | bytes 12292
  135.0 4.6 %collective-permute-start.11 = (bf16[32,1408]{1,0:T(8,128)(2,1)S(1)}, bf16[32,1408]{1,0:T(8,128)(2,1)S(1)}, u32[]{:S(2)}, u32[]{:S(2)}) collective-permute-start(bf16[32,1408]{1,0:T(8,128)(2,1)S(1)} %reduce_sum.12), channel_id=1, source_target_pairs={{0,8},{8,0},{16,24},{24,16},{1,9},{9,1},{17,25},{25,17},{2,10},{10... | collective-permute-start | bytes 270344 | tf_op jit(solution)/shard_map/ppermute | solution.py:518
  140.5 11.0 %collective-permute-start.12 = (bf16[32,1408]{1,0:T(8,128)(2,1)S(1)}, bf16[32,1408]{1,0:T(8,128)(2,1)S(1)}, u32[]{:S(2)}, u32[]{:S(2)}) collective-permute-start(bf16[32,1408]{1,0:T(8,128)(2,1)S(1)} %add_convert_fusion.2), channel_id=1, source_target_pairs={{0,16},{8,24},{16,0},{24,8},{1,17},{9,25},{17,1},{25,9},{2,18},{10... | collective-permute-start | bytes 270344 | tf_op jit(solution)/shard_map/ppermute | solution.py:518
  (17 other events, 15.7 us)

commit v8 on v7

--- a/solution.py
+++ b/solution.py
@@ -155,6 +155,7 @@
 
 
 VMEM_LIMIT = 20 * 1024 * 1024
+ARGUMENT_VMEM_LIMIT = 56 * 1024 * 1024
 LANES = 128
 SLOTS = 4
 NT = (((1,), (1,)), ((), ()))
@@ -237,13 +238,16 @@
     return weight - jnp.mean(weight, axis=1, keepdims=True)
 
 
-def query_kernel(scale, x_ref, wc_ref, pair_ref, weight_ref, out_ref, bias_ref, mean_ref, spread_ref):
+def query_kernel(
+    scale, arrive, x_ref, wc_ref, pair_ref, weight_ref, out_ref, bias_ref, mean_ref, spread_ref
+):
     residues, width = x_ref.shape[1], x_ref.shape[2]
     heads = weight_ref.shape[0]
     normed = normalized(x_ref)[0].astype(jnp.bfloat16)
     pack_heads(out_ref, 0, f32_dot(normed, wc_ref[:, :width]) * scale, residues)
     pack_heads(out_ref, residues, f32_dot(normed, wc_ref[:, width : 2 * width]), residues)
 
+    arrive()
     columns, channels = pair_ref.shape[1], pair_ref.shape[2]
     weight = centred(weight_ref[...])
     first = weight.astype(jnp.bfloat16)
@@ -323,12 +327,17 @@
                     ref[k * part : (k + 1) * part, columns] += bias
 
 
-def softmax_kernel(logit_ref, logit_other_ref, grad_ref, grad_other_ref, out_ref, prob_ref):
-    logits = logit_ref[...] + logit_other_ref[...]
+def softmax_kernel(logit_ref, other_ref, out_ref, low_ref):
+    logits = logit_ref[...] + other_ref[...]
     lifted = jnp.exp(logits - jnp.max(logits, axis=-1, keepdims=True))
     softmax_out = lifted / jnp.sum(lifted, axis=-1, keepdims=True)
-    prob_ref[...] = softmax_out.astype(jnp.bfloat16)
-    grad_probs = grad_ref[...] + grad_other_ref[...].astype(jnp.float32)
+    out_ref[...] = softmax_out
+    low_ref[...] = softmax_out.astype(jnp.bfloat16)
+
+
+def softmax_gradient_kernel(softmax_ref, grad_ref, other_ref, out_ref):
+    softmax_out = softmax_ref[...]
+    grad_probs = grad_ref[...] + other_ref[...].astype(jnp.float32)
     row_dot = jnp.sum(softmax_out * grad_probs, axis=-1, keepdims=True)
     out_ref[...] = (softmax_out * (grad_probs - row_dot)).astype(jnp.bfloat16)
 
@@ -493,24 +502,51 @@
     lax.fori_loop(0, pair_ref.shape[0] // 8, rows, 0)
 
 
-def call(kernel, outs, *args, scratch=(), place=None, flops=0, after=()):
-    whole = pl.BlockSpec(memory_space=pltpu.VMEM)
-    specs = [whole] * len(args)
-    if place is not None:
-        specs = [pl.BlockSpec(memory_space=pltpu.SMEM)] + specs
-        args = (place,) + args
+def call(kernel, outs, *args, scratch=(), place=None, flops=0, after=(), outside=0, late=0):
+    whole, anywhere = pl.BlockSpec(memory_space=pltpu.VMEM), pl.BlockSpec(memory_space=pl.ANY)
+    specs = [anywhere] * outside + [whole] * (len(args) - outside)
+    ahead = () if place is None else (place,)
     shapes = [jax.ShapeDtypeStruct(*o) for o in outs]
     moved = sum(math.prod(a.shape) * a.dtype.itemsize for a in list(args) + shapes)
-    first, last = len(args), len(args) + len(after)
+    first = len(ahead) + len(args)
+    last = first + len(after)
+
+    def wrapped(*refs):
+        given, rest = list(refs[:first]), refs[last:]
+        if outside:
+            *rest, arrived = rest
+            held = rest[len(rest) - outside :]
+            rest = rest[: len(rest) - outside]
+            copies = []
+            for k in range(outside):
+                copies.append(
+                    pltpu.make_async_copy(given[len(ahead) + k], held[k], arrived.at[k])
+                )
+                given[len(ahead) + k] = held[k]
+            for copy in copies:
+                copy.start()
+            for copy in copies[: outside - late]:
+                copy.wait()
+            if late:
+                given.insert(0, lambda: [copy.wait() for copy in copies[outside - late :]])
+        kernel(*given, *rest)
+
+    held = [pltpu.VMEM(a.shape, a.dtype) for a in args[:outside]]
+    if outside:
+        held.append(pltpu.SemaphoreType.DMA((outside,)))
     return pl.pallas_call(
-        lambda *refs: kernel(*refs[:first], *refs[last:]),
+        wrapped,
         out_shape=shapes,
-        in_specs=specs + [pl.BlockSpec(memory_space=pl.ANY)] * len(after),
+        in_specs=[pl.BlockSpec(memory_space=pltpu.SMEM)] * len(ahead)
+        + specs
+        + [anywhere] * len(after),
         out_specs=[whole] * len(shapes),
-        scratch_shapes=scratch,
-        compiler_params=pltpu.CompilerParams(vmem_limit_bytes=VMEM_LIMIT),
+        scratch_shapes=[*scratch, *held],
+        compiler_params=pltpu.CompilerParams(
+            vmem_limit_bytes=ARGUMENT_VMEM_LIMIT if outside else VMEM_LIMIT
+        ),
         cost_estimate=pl.CostEstimate(flops=flops, bytes_accessed=moved, transcendentals=0),
-    )(*args, *after)
+    )(*ahead, *args, *after)
 
 
 def swapped(mine, axis_name, distance):
@@ -563,33 +599,31 @@
             ((residues, LANES), f32),
         ],
         x, wc, pair_entries, pair_weight.T,
-        flops=8 * tokens * width * width,
+        flops=8 * tokens * width * width, outside=3, late=1,
     )
     query_blocks = across(query_blocks)
-    (value_blocks,) = call(
-        value_kernel, [((group, 2 * residues, LANES), bf16)], x, grad, wc, wo,
-        flops=8 * tokens * width * width,
-    )
-    value_blocks = across(value_blocks)
-
-    def scores(blocks, left_row, right_row, with_bias, kind, after=()):
+    def scores(blocks, left_row, right_row, with_bias, kind):
         return call(
             functools.partial(score_kernel, residues, left_row, right_row, with_bias),
             [((total // 4, total), f32), ((total // 4, total), kind)],
             blocks, swapped(blocks, "res", 1),
-            place=place, flops=2 * total * total * width, after=after,
+            place=place, flops=2 * total * total * width,
         )
 
     logit_mine, logit_sent = scores(query_blocks, 0, residues, True, f32)
     logit_other = swapped(logit_sent, "seq", seq_half)
-    grad_mine, grad_sent = scores(value_blocks, residues, 0, False, bf16, after=(logit_mine,))
-    grad_other = swapped(grad_sent, "seq", seq_half)
-    quarter = ((total // 4, total), bf16)
-    grad_logits, probs = call(
-        softmax_kernel, [quarter, quarter], logit_mine, logit_other, grad_mine, grad_other,
+    (value_blocks,) = call(
+        value_kernel, [((group, 2 * residues, LANES), bf16)], x, grad, wc, wo,
+        flops=8 * tokens * width * width, outside=4, after=(logit_sent,),
+    )
+    value_blocks = across(value_blocks)
+
+    quarter = (total // 4, total)
+    softmax_out, probs = call(
+        softmax_kernel, [(quarter, f32), (quarter, bf16)], logit_mine, logit_other,
         flops=total * total,
     )
-
+    value_blocks, probs = lax.optimization_barrier((value_blocks, probs))
     def products(quarters, blocks, first_row, second_row, with_share, factor):
         rows = 2 * residues + (residues // 2 if with_share else 0)
         (out,) = call(
@@ -601,10 +635,21 @@
             scratch=[pltpu.VMEM((total, total), bf16)],
             place=place, flops=4 * total * total * width,
         )
-        return across(out)
-
-    grad_blocks = products(all_quarters(grad_logits), query_blocks, residues, 0, True, scale)
-    attended_blocks = products(all_quarters(probs), value_blocks, 0, residues, False, 1.0)
+        return out
+
+    grad_mine, grad_sent = scores(value_blocks, residues, 0, False, bf16)
+    grad_other = swapped(grad_sent, "seq", seq_half)
+    attended = products(all_quarters(probs), value_blocks, 0, residues, False, 1.0)
+    attended, grad_other = lax.optimization_barrier((attended, grad_other))
+    attended_blocks = across(attended)
+    (grad_logits,) = call(
+        softmax_gradient_kernel, [(quarter, bf16)], softmax_out, grad_mine, grad_other,
+        flops=total * total,
+    )
+
+    grad_blocks = across(
+        products(all_quarters(grad_logits), query_blocks, residues, 0, True, scale)
+    )
 
     share = pltpu.VMEM((heads, residues, LANES), f32)
     (pair_weight_part,) = call(
@@ -626,7 +671,7 @@
         [(x.shape, bf16), ((tokens, 4 * width), bf16), part_rows, part_rows],
         x, grad, wc, wo, attended_blocks, grad_blocks, pair_weight_part,
         scratch=[pltpu.VMEM((width, columns), bf16)],
-        place=place, flops=24 * tokens * width * width,
+        place=place, flops=24 * tokens * width * width, outside=4,
     )
     (alignment_gradient,) = call(
         alignment_kernel, [(x.shape, bf16)], x, wc, projected,

time: 165 us -> 161 us (0.976)
  blocking collectives: 20.1 us -> 54.3 us
  waiting for transfers between devices: 75.1 us -> 55.7 us
  starting transfers between devices: 26.1 us -> 12.5 us
  local copies, waits for them, and re-layouts: 15.1 us -> 2.68 us
  Pallas kernels: 21.8 us -> 27.9 us
  other arithmetic: 4.59 us -> 6.3 us
    all_to_all x0 -> x2, blocking collectives: none -> 34.2 us  [across(): lax.all_to_all(blocks, ('seq', 'res'), 0, 0, axis_index_groups=groups, ti...]
    all_to_all x4 -> x2, waiting for transfers between devices: 31.2 us -> 12.1 us  [across(): lax.all_to_all(blocks, ('seq', 'res'), 0, 0, axis_index_groups=groups, ti...]
    unnamed x48 -> x32, local copies, waits for them, and re-layouts: 15.1 us -> 2.62 us
    all_to_all x4 -> x2, starting transfers between devices: 19 us -> 7.82 us  [across(): lax.all_to_all(blocks, ('seq', 'res'), 0, 0, axis_index_groups=groups, ti...]
    pallas_call x11 -> x12, Pallas kernels: 21.8 us -> 27.9 us  [call(): pl.pallas_call(wrapped, out_shape=shapes, in_specs=[pl.BlockSpec(memory_s...]
    ppermute x13, starting transfers between devices: 7.05 us -> 4.63 us  [swapped(): lax.ppermute(mine, axis_name, [(a, a ^ distance) for a in range(size)])]
  transfers between devices with their start and end apart: 17 -> 15, of which waited for: 10 -> 11; matrix products, arithmetic and copies ran while one was open for 0% -> 0% of each run, Pallas kernels for 7% -> 6%
where the time goes in v8:
time: 161 us; the launch traced here: 160 us
  waiting for transfers between devices  55.7 us (35%)
  blocking collectives  54.3 us (34%)
  Pallas kernels  27.9 us (17%)
  starting transfers between devices  12.5 us (8%)
  other arithmetic  6.3 us (4%)
  local copies, waits for them, and re-layouts  2.68 us (2%)
    ppermute x13, waiting for transfers between devices, swapped(): lax.ppermute(mine, axis_name, [(a, a ^ distance) for a in range(size)])  43.5 us
    all_to_all x2, blocking collectives, across(): lax.all_to_all(blocks, ('seq', 'res'), 0, 0, axis_index_groups=groups, ti...  34.2 us
    pallas_call x12, Pallas kernels, call(): pl.pallas_call(wrapped, out_shape=shapes, in_specs=[pl.BlockSpec(memory_s...  27.9 us
    all_to_all x2, waiting for transfers between devices, across(): lax.all_to_all(blocks, ('seq', 'res'), 0, 0, axis_index_groups=groups, ti...  12.1 us
    all_to_all x1, blocking collectives, head_body(): lax.all_to_all(parts, 'res', 0, 0, axis_index_groups=chips, tiled=True)  10.5 us
    all_gather x1, blocking collectives, head_body(): whole = lax.all_gather(part, 'res', axis=0)  9.59 us
    all_to_all x2, starting transfers between devices, across(): lax.all_to_all(blocks, ('seq', 'res'), 0, 0, axis_index_groups=groups, ti...  7.82 us
    ppermute x13, starting transfers between devices, swapped(): lax.ppermute(mine, axis_name, [(a, a ^ distance) for a in range(size)])  4.63 us
  transfers between devices with their start and end apart: 15, of which 11 were waited for; matrix products, arithmetic and copies ran while one was open for 0% of the time, Pallas kernels for 6%

profile of v8, /device:TPU:0, one launch (start us, length us, event | category | flops | bytes accessed | tf_op | source)
XLA Modules:
  0.0 160.2 jit_solution(1099309446968704721)
XLA Ops:
  0.6 8.1 %shard_map.109 = (bf16[16,192,128]{2,1,0:T(8,128)(2,1)}, f32[8,64,128]{2,1,0:T(8,128)}, f32[64,128]{1,0:T(8,128)}, f32[64,128]{1,0:T(8,128)}) custom-call(bf16[8,64,256]{2,1,0:T(8,128)(2,1)} %refs_0_.5, bf16[256,1024]{1,0:T(8,128)(2,1)} %refs_1_.10, bf16[64,128,128]{2,1,0:T(8,128)(2,1)} %refs_1_.11, f32[8,128]{1,0:T(8,128)} %bitcast.13), custom_call_target="tpu_custom_call" | custom-call | flops 268435456 | bytes 4001792 | tf_op jit(solution)/shard_map/pallas_call | solution.py:537
  8.7 19.7 %all_to_all.25.refs_1_.refs_5_ = bf16[16,192,128]{2,1,0:T(8,128)(2,1)S(1)} all-to-all(bf16[16,192,128]{2,1,0:T(8,128)(2,1)} %get-tuple-element.24), channel_id=1, replica_groups={{0,1,2,3,4,5,6,7,8,9,10,11,12,13,14,15},{16,17,18,19,20,21,22,23,24,25,..., dimensions={0} | all-to-all | bytes 1572864 | tf_op jit(solution)/shard_map/all_to_all | solution.py:586
  28.4 2.2 %collective-permute-done.refs_2_ = bf16[16,192,128]{2,1,0:T(8,128)(2,1)S(1)} collective-permute-done((bf16[16,192,128]{2,1,0:T(8,128)(2,1)S(1)}, bf16[16,192,128]{2,1,0:T(8,128)(2,1)S(1)}, u32[]{:S(2)}, u32[]{:S(2)}) %collective-permute-start) | collective-permute-done | bytes 786464 | tf_op jit(solution)/shard_map/ppermute | solution.py:554
  32.4 2.8 %shard_map.111 = bf16[16,128,128]{2,1,0:T(8,128)(2,1)} custom-call(bf16[8,64,256]{2,1,0:T(8,128)(2,1)} %refs_0_.5, bf16[8,64,256]{2,1,0:T(8,128)(2,1)} %refs_2_.5, bf16[256,1024]{1,0:T(8,128)(2,1)} %refs_1_.10, bf16[256,256]{1,0:T(8,128)(2,1)} %refs_4_.1, f32[128,512]{1,0:T(8,128)} %copy-done.7), custom_call_target="tpu_custom_call" | custom-call | flops 268435456 | bytes 1703936 | tf_op jit(solution)/shard_map/pallas_call | solution.py:537
  35.2 3.6 %all-to-all-start.1 = ((bf16[16,128,128]{2,1,0:T(8,128)(2,1)}), bf16[16,128,128]{2,1,0:T(8,128)(2,1)S(1)}, u32[]{:S(2)}, u32[]{:S(2)}) async-start(bf16[16,128,128]{2,1,0:T(8,128)(2,1)} %shard_map.111), calls=%async_computation.1 | async-start | bytes 1048576 | tf_op jit(solution)/shard_map/all_to_all | solution.py:586
  38.8 2.7 %collective-permute-start.1 = (f32[128,512]{1,0:T(8,128)S(1)}, f32[128,512]{1,0:T(8,128)S(1)}, u32[]{:S(2)}, u32[]{:S(2)}) collective-permute-start(f32[128,512]{1,0:T(8,128)S(1)} %copy-done.8), channel_id=1, source_target_pairs={{0,16},{8,24},{16,0},{24,8},{1,17},{9,25},{17,1},{25,9},{2,18},{10... | collective-permute-start | bytes 786440 | tf_op jit(solution)/shard_map/ppermute | solution.py:554
  41.4 9.5 %collective-permute-done.1.refs_1_ = f32[128,512]{1,0:T(8,128)S(1)} collective-permute-done((f32[128,512]{1,0:T(8,128)S(1)}, f32[128,512]{1,0:T(8,128)S(1)}, u32[]{:S(2)}, u32[]{:S(2)}) %collective-permute-start.1) | collective-permute-done | bytes 262176 | tf_op jit(solution)/shard_map/ppermute | solution.py:554
  51.1 3.7 %all-to-all-done.1.refs_5_.refs_1_ = bf16[16,128,128]{2,1,0:T(8,128)(2,1)S(1)} async-done(((bf16[16,128,128]{2,1,0:T(8,128)(2,1)}), bf16[16,128,128]{2,1,0:T(8,128)(2,1)S(1)}, u32[]{:S(2)}, u32[]{:S(2)}) %all-to-all-start.1) | async-done | bytes 524320 | tf_op jit(solution)/shard_map/all_to_all | solution.py:586
  55.4 9.1 %collective-permute-done.2.refs_2_ = bf16[128,512]{1,0:T(8,128)(2,1)S(1)} collective-permute-done((bf16[128,512]{1,0:T(8,128)(2,1)S(1)}, bf16[128,512]{1,0:T(8,128)(2,1)S(1)}, u32[]{:S(2)}, u32[]{:S(2)}) %collective-permute-start.2) | collective-permute-done | bytes 131104 | tf_op jit(solution)/shard_map/ppermute | solution.py:554
  65.9 1.8 %shard_map.113 = bf16[16,128,128]{2,1,0:T(8,128)(2,1)} custom-call(s32[2]{0:T(128)S(1)} %pad_add_fusion.refs_0_, bf16[128,512]{1,0:T(8,128)(2,1)S(1)} %get-tuple-element.28.refs_1_, bf16[128,512]{1,0:T(8,128)(2,1)S(1)} %collective-permute-done.2.refs_2_, bf16[128,512]{1,0:T(8,128)(2,1)S(1)} %collective-permute-done.3.refs_3_, ...), custom_call_target="tpu_custom_call" | custom-call | flops 268435456 | bytes 1572864 | tf_op jit(solution)/shard_map/pallas_call | solution.py:537
  67.7 6.1 %collective-permute-done.6.refs_2_ = bf16[128,512]{1,0:T(8,128)(2,1)S(1)} collective-permute-done((bf16[128,512]{1,0:T(8,128)(2,1)S(1)}, bf16[128,512]{1,0:T(8,128)(2,1)S(1)}, u32[]{:S(2)}, u32[]{:S(2)}) %collective-permute-start.6) | collective-permute-done | bytes 131104 | tf_op jit(solution)/shard_map/ppermute | solution.py:554
  74.1 9.0 %collective-permute-done.7.refs_2_ = bf16[128,512]{1,0:T(8,128)(2,1)S(1)} collective-permute-done((bf16[128,512]{1,0:T(8,128)(2,1)S(1)}, bf16[128,512]{1,0:T(8,128)(2,1)S(1)}, u32[]{:S(2)}, u32[]{:S(2)}) %collective-permute-start.7) | collective-permute-done | bytes 131104 | tf_op jit(solution)/shard_map/ppermute | solution.py:554
  83.2 1.3 collective-permute-done.9.refs_4_
  85.6 14.5 %all_to_all.26.refs_0_.refs_6_ = bf16[16,160,128]{2,1,0:T(8,128)(2,1)S(1)} all-to-all(bf16[16,160,128]{2,1,0:T(8,128)(2,1)S(1)} %shard_map.116), channel_id=1, replica_groups={{0,1,2,3,4,5,6,7,8,9,10,11,12,13,14,15},{16,17,18,19,20,21,22,23,24,25,..., dimensions={0} | all-to-all | bytes 1310720 | tf_op jit(solution)/shard_map/all_to_all | solution.py:586
  100.1 4.2 %all-to-all-start.2 = ((bf16[16,128,128]{2,1,0:T(8,128)(2,1)}), bf16[16,128,128]{2,1,0:T(8,128)(2,1)}, u32[]{:S(2)}, u32[]{:S(2)}) async-start(bf16[16,128,128]{2,1,0:T(8,128)(2,1)} %shard_map.113), calls=%async_computation.2 | async-start | bytes 1048576 | tf_op jit(solution)/shard_map/all_to_all | solution.py:586
  104.4 1.5 shard_map.117.refs_7_
  106.5 8.4 %all-to-all-done.2.refs_5_ = bf16[16,128,128]{2,1,0:T(8,128)(2,1)} async-done(((bf16[16,128,128]{2,1,0:T(8,128)(2,1)}), bf16[16,128,128]{2,1,0:T(8,128)(2,1)}, u32[]{:S(2)}, u32[]{:S(2)}) %all-to-all-start.2) | async-done | bytes 524320 | tf_op jit(solution)/shard_map/all_to_all | solution.py:586
  114.9 4.7 %shard_map.118 = (bf16[8,64,256]{2,1,0:T(8,128)(2,1)}, bf16[512,1024]{1,0:T(8,128)(2,1)}, bf16[4,32,1408]{2,1,0:T(8,128)(2,1)}, bf16[4,32,1408]{2,1,0:T(8,128)(2,1)}) custom-call(s32[2]{0:T(128)} %copy-done.14, bf16[8,64,256]{2,1,0:T(8,128)(2,1)} %refs_0_.5, bf16[8,64,256]{2,1,0:T(8,128)(2,1)} %refs_2_.5, bf16[256,1024]{1,0:T(8,128)(2,1)} %refs_1_.10, ...), custom_call_target="tpu_custom_call" | custom-call | flops 805306368 | bytes 4395008 | tf_op jit(solution)/shard_map/pallas_call | solution.py:537
  119.8 1.9 %collective-permute-done.10 = bf16[4,32,1408]{2,1,0:T(8,128)(2,1)S(1)} collective-permute-done((bf16[4,32,1408]{2,1,0:T(8,128)(2,1)}, bf16[4,32,1408]{2,1,0:T(8,128)(2,1)S(1)}, u32[]{:S(2)}, u32[]{:S(2)}) %collective-permute-start.10) | collective-permute-done | bytes 360480 | tf_op jit(solution)/shard_map/ppermute | solution.py:554
  122.8 10.5 %all_to_all.27 = bf16[4,32,1408]{2,1,0:T(8,128)(2,1)} all-to-all(bf16[4,32,1408]{2,1,0:T(8,128)(2,1)S(1)} %add_convert_fusion), channel_id=1, replica_groups={{0,2,4,6},{1,3,5,7},{8,10,12,14},{9,11,13,15},{16,18,20,22},{17,19,21,2..., dimensions={0} | all-to-all | bytes 720896 | tf_op jit(solution)/shard_map/all_to_all | solution.py:686
  133.3 1.7 %reduce_sum.12 = bf16[32,1408]{1,0:T(8,128)(2,1)} reduce(bf16[4,32,1408]{2,1,0:T(8,128)(2,1)} %all_to_all.27, bf16[]{:T(256)} %constant.34.clone.1), dimensions={0}, to_apply=%region_0.1 | reduce | flops 135168 | bytes 450562 | tf_op jit(solution)/shard_map/reduce_sum | solution.py:687
  135.5 4.2 %collective-permute-done.11 = bf16[32,1408]{1,0:T(8,128)(2,1)S(1)} collective-permute-done((bf16[32,1408]{1,0:T(8,128)(2,1)}, bf16[32,1408]{1,0:T(8,128)(2,1)S(1)}, u32[]{:S(2)}, u32[]{:S(2)}) %collective-permute-start.11) | collective-permute-done | bytes 90144 | tf_op jit(solution)/shard_map/ppermute | solution.py:554
  143.7 4.3 %shard_map.120 = bf16[64,128,128]{2,1,0:T(8,128)(2,1)} custom-call(bf16[16,160,128]{2,1,0:T(8,128)(2,1)S(1)} %copy-done.2, bf16[64,128,128]{2,1,0:T(8,128)(2,1)S(1)} %copy-done, f32[8,128]{1,0:T(8,128)S(1)} %bitcast.14, f32[8,64,128]{2,1,0:T(8,128)S(1)} %copy-done.6, f32[64,128]{1,0:T(8,128)S(1)} %copy-done.10, f32[64,128]{1,0:T(8,128)S(1)} %copy-done.12), custom_call_target="tpu_custom_call" | custom-call | flops 268435456 | bytes 5181440 | tf_op jit(solution)/shard_map/pallas_call | solution.py:537
  148.1 9.6 %all-gather = bf16[256,1408]{1,0:T(8,128)(2,1)S(1)} all-gather(bf16[32,1408]{1,0:T(8,128)(2,1)S(1)} %add_convert_fusion.1), channel_id=2, replica_groups=mesh['seq'=4,'res'=8] {'res'}, dimensions={0}, use_global_device_ids=true | all-gather | bytes 811008 | tf_op jit(solution)/shard_map/all_gather | solution.py:690
  (64 shorter events, 14.2 us)
Async XLA Ops:
  28.4 2.3 %collective-permute-start = (bf16[16,192,128]{2,1,0:T(8,128)(2,1)S(1)}, bf16[16,192,128]{2,1,0:T(8,128)(2,1)S(1)}, u32[]{:S(2)}, u32[]{:S(2)}) collective-permute-start(bf16[16,192,128]{2,1,0:T(8,128)(2,1)S(1)} %all_to_all.25.refs_1_.refs_5_), channel_id=1, source_target_pairs={{0,1},{1,0},{2,3},{3,2},{4,5},{5,4},{6,7},{7,6},{8,9},{9,8},{10,11... | collective-permute-start | bytes 2359304 | tf_op jit(solution)/shard_map/ppermute | solution.py:554
  28.4 56.1 %copy-start.14 = (s32[2]{0:T(128)}, s32[2]{0:T(128)S(1)}, u32[]{:S(2)}) copy-start(s32[2]{0:T(128)S(1)} %pad_add_fusion.refs_0_) | copy-start | bytes 28
  35.2 19.7 %all-to-all-start.1 = ((bf16[16,128,128]{2,1,0:T(8,128)(2,1)}), bf16[16,128,128]{2,1,0:T(8,128)(2,1)S(1)}, u32[]{:S(2)}, u32[]{:S(2)}) async-start(bf16[16,128,128]{2,1,0:T(8,128)(2,1)} %shard_map.111), calls=%async_computation.1 | async-start | bytes 1048576 | tf_op jit(solution)/shard_map/all_to_all | solution.py:586
  38.8 12.2 %collective-permute-start.1 = (f32[128,512]{1,0:T(8,128)S(1)}, f32[128,512]{1,0:T(8,128)S(1)}, u32[]{:S(2)}, u32[]{:S(2)}) collective-permute-start(f32[128,512]{1,0:T(8,128)S(1)} %copy-done.8), channel_id=1, source_target_pairs={{0,16},{8,24},{16,0},{24,8},{1,17},{9,25},{17,1},{25,9},{2,18},{10... | collective-permute-start | bytes 786440 | tf_op jit(solution)/shard_map/ppermute | solution.py:554
  54.9 9.6 %collective-permute-start.5 = (bf16[16,128,128]{2,1,0:T(8,128)(2,1)S(1)}, bf16[16,128,128]{2,1,0:T(8,128)(2,1)S(1)}, u32[]{:S(2)}, u32[]{:S(2)}) collective-permute-start(bf16[16,128,128]{2,1,0:T(8,128)(2,1)S(1)} %all-to-all-done.1.refs_5_.refs_1_), channel_id=1, source_target_pairs={{0,1},{1,0},{2,3},{3,2},{4,5},{5,4},{6,7},{7,6},{8,9},{9,8},{10,11... | collective-permute-start | bytes 1572872 | tf_op jit(solution)/shard_map/ppermute | solution.py:554
  54.9 9.6 %collective-permute-start.2 = (bf16[128,512]{1,0:T(8,128)(2,1)S(1)}, bf16[128,512]{1,0:T(8,128)(2,1)S(1)}, u32[]{:S(2)}, u32[]{:S(2)}) collective-permute-start(bf16[128,512]{1,0:T(8,128)(2,1)S(1)} %get-tuple-element.28.refs_1_), channel_id=1, source_target_pairs={{0,16},{8,24},{16,0},{24,8},{1,17},{9,25},{17,1},{25,9},{2,18},{10... | collective-permute-start | bytes 393224 | tf_op jit(solution)/shard_map/ppermute | solution.py:554
  54.9 10.7 %collective-permute-start.3 = (bf16[128,512]{1,0:T(8,128)(2,1)S(1)}, bf16[128,512]{1,0:T(8,128)(2,1)S(1)}, u32[]{:S(2)}, u32[]{:S(2)}) collective-permute-start(bf16[128,512]{1,0:T(8,128)(2,1)S(1)} %get-tuple-element.28.refs_1_), channel_id=1, source_target_pairs={{0,1},{1,0},{2,3},{3,2},{4,5},{5,4},{6,7},{7,6},{8,9},{9,8},{10,11... | collective-permute-start | bytes 393224 | tf_op jit(solution)/shard_map/ppermute | solution.py:554
  64.5 1.3 collective-permute-start.4
  65.5 8.2 %collective-permute-start.6 = (bf16[128,512]{1,0:T(8,128)(2,1)S(1)}, bf16[128,512]{1,0:T(8,128)(2,1)S(1)}, u32[]{:S(2)}, u32[]{:S(2)}) collective-permute-start(bf16[128,512]{1,0:T(8,128)(2,1)S(1)} %get-tuple-element.30), channel_id=1, source_target_pairs={{0,16},{8,24},{16,0},{24,8},{1,17},{9,25},{17,1},{25,9},{2,18},{10... | collective-permute-start | bytes 393224 | tf_op jit(solution)/shard_map/ppermute | solution.py:554
  73.9 30.5 %copy-start = (bf16[64,128,128]{2,1,0:T(8,128)(2,1)S(1)}, bf16[64,128,128]{2,1,0:T(8,128)(2,1)}, u32[]{:S(2)}) copy-start(bf16[64,128,128]{2,1,0:T(8,128)(2,1)} %refs_1_.11) | copy-start | bytes 6291460
  73.9 30.5 %copy-start.9 = (f32[64,128]{1,0:T(8,128)S(1)}, f32[64,128]{1,0:T(8,128)}, u32[]{:S(2)}) copy-start(f32[64,128]{1,0:T(8,128)} %get-tuple-element.35.refs_2_.refs_4_) | copy-start | bytes 98308
  73.9 30.5 %copy-start.11 = (f32[64,128]{1,0:T(8,128)S(1)}, f32[64,128]{1,0:T(8,128)}, u32[]{:S(2)}) copy-start(f32[64,128]{1,0:T(8,128)} %get-tuple-element.36.refs_3_.refs_5_) | copy-start | bytes 98308
  73.9 9.2 %collective-permute-start.7 = (bf16[128,512]{1,0:T(8,128)(2,1)S(1)}, bf16[128,512]{1,0:T(8,128)(2,1)S(1)}, u32[]{:S(2)}, u32[]{:S(2)}) collective-permute-start(bf16[128,512]{1,0:T(8,128)(2,1)S(1)} %shard_map.115.refs_1_), channel_id=1, source_target_pairs={{0,16},{8,24},{16,0},{24,8},{1,17},{9,25},{17,1},{25,9},{2,18},{10... | collective-permute-start | bytes 393224 | tf_op jit(solution)/shard_map/ppermute | solution.py:554
  74.0 9.2 %collective-permute-start.8 = (bf16[128,512]{1,0:T(8,128)(2,1)S(1)}, bf16[128,512]{1,0:T(8,128)(2,1)S(1)}, u32[]{:S(2)}, u32[]{:S(2)}) collective-permute-start(bf16[128,512]{1,0:T(8,128)(2,1)S(1)} %shard_map.115.refs_1_), channel_id=1, source_target_pairs={{0,1},{1,0},{2,3},{3,2},{4,5},{5,4},{6,7},{7,6},{8,9},{9,8},{10,11... | collective-permute-start | bytes 393224 | tf_op jit(solution)/shard_map/ppermute | solution.py:554
  83.2 1.3 collective-permute-start.9
  100.1 14.8 %copy-start.1 = (bf16[16,160,128]{2,1,0:T(8,128)(2,1)}, bf16[16,160,128]{2,1,0:T(8,128)(2,1)S(1)}, u32[]{:S(2)}) copy-start(bf16[16,160,128]{2,1,0:T(8,128)(2,1)S(1)} %all_to_all.26.refs_0_.refs_6_) | copy-start | bytes 1966084
  100.1 14.8 %all-to-all-start.2 = ((bf16[16,128,128]{2,1,0:T(8,128)(2,1)}), bf16[16,128,128]{2,1,0:T(8,128)(2,1)}, u32[]{:S(2)}, u32[]{:S(2)}) async-start(bf16[16,128,128]{2,1,0:T(8,128)(2,1)} %shard_map.113), calls=%async_computation.2 | async-start | bytes 1048576 | tf_op jit(solution)/shard_map/all_to_all | solution.py:586
  106.5 34.7 %copy-start.3 = (bf16[256,1024]{1,0:T(8,128)(2,1)S(1)}, bf16[256,1024]{1,0:T(8,128)(2,1)}, u32[]{:S(2)}) copy-start(bf16[256,1024]{1,0:T(8,128)(2,1)} %refs_1_.10) | copy-start | bytes 1572868
  106.5 34.7 %copy-start.4 = (bf16[8,64,256]{2,1,0:T(8,128)(2,1)S(1)}, bf16[8,64,256]{2,1,0:T(8,128)(2,1)}, u32[]{:S(2)}) copy-start(bf16[8,64,256]{2,1,0:T(8,128)(2,1)} %refs_0_.5) | copy-start | bytes 786436
  119.7 2.0 %collective-permute-start.10 = (bf16[4,32,1408]{2,1,0:T(8,128)(2,1)}, bf16[4,32,1408]{2,1,0:T(8,128)(2,1)S(1)}, u32[]{:S(2)}, u32[]{:S(2)}) collective-permute-start(bf16[4,32,1408]{2,1,0:T(8,128)(2,1)} %get-tuple-element.41), channel_id=1, source_target_pairs={{0,1},{1,0},{2,3},{3,2},{4,5},{5,4},{6,7},{7,6},{8,9},{9,8},{10,11... | collective-permute-start | bytes 1081352 | tf_op jit(solution)/shard_map/ppermute | solution.py:554
  121.6 22.1 %copy-start.2 = (bf16[16,160,128]{2,1,0:T(8,128)(2,1)S(1)}, bf16[16,160,128]{2,1,0:T(8,128)(2,1)}, u32[]{:S(2)}) copy-start(bf16[16,160,128]{2,1,0:T(8,128)(2,1)} %copy-done.1) | copy-start | bytes 1966084
  121.6 22.1 %copy-start.13 = (f32[128,8]{0,1:T(8,128)S(1)}, f32[128,8]{0,1:T(8,128)}, u32[]{:S(2)}) copy-start(f32[128,8]{0,1:T(8,128)} %param.10) | copy-start | bytes 12292
  135.0 4.7 %collective-permute-start.11 = (bf16[32,1408]{1,0:T(8,128)(2,1)}, bf16[32,1408]{1,0:T(8,128)(2,1)S(1)}, u32[]{:S(2)}, u32[]{:S(2)}) collective-permute-start(bf16[32,1408]{1,0:T(8,128)(2,1)} %reduce_sum.12), channel_id=1, source_target_pairs={{0,8},{8,0},{16,24},{24,16},{1,9},{9,1},{17,25},{25,17},{2,10},{10... | collective-permute-start | bytes 270344 | tf_op jit(solution)/shard_map/ppermute | solution.py:554
  140.6 7.4 %collective-permute-start.12 = (bf16[32,1408]{1,0:T(8,128)(2,1)S(1)}, bf16[32,1408]{1,0:T(8,128)(2,1)S(1)}, u32[]{:S(2)}, u32[]{:S(2)}) collective-permute-start(bf16[32,1408]{1,0:T(8,128)(2,1)S(1)} %add_convert_fusion.2), channel_id=1, source_target_pairs={{0,16},{8,24},{16,0},{24,8},{1,17},{9,25},{17,1},{25,9},{2,18},{10... | collective-permute-start | bytes 270344 | tf_op jit(solution)/shard_map/ppermute | solution.py:554
  (7 other events, 20.3 us)

commit v9 on v8

--- a/solution.py
+++ b/solution.py
@@ -386,30 +386,42 @@
     )
 
 
-def weight_kernel(
-    place_ref, x_ref, grad_ref, wc_ref, wo_ref, attended_ref, blocks_ref, pair_weight_ref,
-    updated_ref, projected_ref, keep_ref, send_ref, sums_ref,
+def attended_weight_kernel(
+    x_ref, grad_ref, wc_ref, wo_ref, blocks_ref, updated_ref, projected_ref, normed_ref, sums_ref
 ):
     residues, width = x_ref.shape[1], x_ref.shape[2]
     tiles = width // LANES
-    core = place_ref[0]
     normed = normalized(x_ref)[0].astype(jnp.bfloat16)
+    normed_ref[...] = normed
     gate = gate_of(f32_dot(normed, wc_ref[:, 3 * width :]))
     grad = grad_ref[...].reshape(-1, width)
     grad_gated = f32_dot(grad, wo_ref[...], NT)
-    attended = unpack_heads(attended_ref, 0, residues, tiles)
+    attended = unpack_heads(blocks_ref, 0, residues, tiles)
     gated = (gate * attended).astype(jnp.bfloat16)
     updated_ref[...] = f32_dot(gated, wo_ref[...]).astype(jnp.bfloat16).reshape(updated_ref.shape)
-    parts = [
-        unpack_heads(blocks_ref, 0, residues, tiles),
-        unpack_heads(blocks_ref, residues, residues, tiles),
-        unpack_heads(attended_ref, residues, residues, tiles),
-        grad_gated * attended * gate * (1.0 - gate),
-    ]
-    for t in range(4):
-        projected_ref[:, t * width : (t + 1) * width] = parts[t].astype(jnp.bfloat16)
-    sums_ref[:, : 4 * width] = f32_dot(normed, projected_ref[...], TN).astype(jnp.bfloat16)
-    sums_ref[:, 4 * width : 5 * width] = f32_dot(gated, grad, TN).astype(jnp.bfloat16)
+    projected_ref[:, :width] = unpack_heads(blocks_ref, residues, residues, tiles).astype(
+        jnp.bfloat16
+    )
+    projected_ref[:, width:] = (grad_gated * attended * gate * (1.0 - gate)).astype(jnp.bfloat16)
+    sums_ref[:, : 2 * width] = f32_dot(normed, projected_ref[...], TN).astype(jnp.bfloat16)
+    sums_ref[:, 2 * width :] = f32_dot(gated, grad, TN).astype(jnp.bfloat16)
+
+
+def query_weight_kernel(
+    place_ref, normed_ref, blocks_ref, pair_weight_ref, attended_sums_ref,
+    projected_ref, keep_ref, send_ref, sums_ref,
+):
+    width = normed_ref.shape[1]
+    tiles, residues = width // LANES, (blocks_ref.shape[1] * 2) // 5
+    core = place_ref[0]
+    for t in range(2):
+        projected_ref[:, t * width : (t + 1) * width] = unpack_heads(
+            blocks_ref, t * residues, residues, tiles
+        ).astype(jnp.bfloat16)
+    sums_ref[:, : 2 * width] = f32_dot(normed_ref[...], projected_ref[...], TN).astype(
+        jnp.bfloat16
+    )
+    sums_ref[:, 2 * width : 5 * width] = attended_sums_ref[...]
     heads, channels = pair_weight_ref.shape
     rows = sums_ref.shape[0] // heads
     first = lax.broadcasted_iota(jnp.int32, (rows, channels), 0) == 0
@@ -424,6 +436,21 @@
             ref[block] = sums_ref[pl.ds(start, rows), :]
 
 
+def core_sum_kernel(place_ref, keep_ref, other_ref, own_ref, *send_refs):
+    chip = place_ref[2]
+    for flip, ref in enumerate((own_ref, *send_refs)):
+        block = jnp.bitwise_xor(chip, flip)
+        total = keep_ref[block].astype(jnp.float32) + other_ref[block].astype(jnp.float32)
+        ref[...] = total.astype(ref.dtype)
+
+
+def plane_sum_kernel(own_ref, *refs):
+    total = own_ref[...]
+    for ref in refs[:-1]:
+        total += ref[...].astype(jnp.float32)
+    refs[-1][...] = total.astype(refs[-1].dtype)
+
+
 def pair_weight_kernel(blocks_ref, pair_ref, mean_ref, spread_ref, out_ref, share_ref):
     heads, part = share_ref.shape[0], pair_ref.shape[0] // 2
     share_ref[...] = share_of(blocks_ref, blocks_ref.shape[1] - part, part, heads)
@@ -448,9 +475,12 @@
     out_ref[...] = total[:heads] + total[heads:] - jnp.sum(shift, axis=1, keepdims=True)
 
 
-def alignment_kernel(x_ref, wc_ref, projected_ref, out_ref):
+def alignment_kernel(x_ref, wc_ref, query_key_ref, value_gate_ref, out_ref):
     normed, spread = normalized(x_ref)
-    gradient = f32_dot(projected_ref[...], wc_ref[...], NT)
+    width = x_ref.shape[2]
+    gradient = f32_dot(query_key_ref[...], wc_ref[:, : 2 * width], NT) + f32_dot(
+        value_gate_ref[...], wc_ref[:, 2 * width :], NT
+    )
     out_ref[...] = (
         layer_norm_backward(gradient, normed, spread).astype(jnp.bfloat16).reshape(out_ref.shape)
     )
@@ -579,15 +609,11 @@
     groups = [[g * group + k for k in range(group)] for g in range(seq_half)]
     scale = 1.0 / math.sqrt(width // heads * sequences * seq_size)
     res_index, seq_index = lax.axis_index("res"), lax.axis_index("seq")
-    place = jnp.stack([res_index % 2, seq_index // 2]).astype(jnp.int32)
+    place = jnp.stack([res_index % 2, seq_index // 2, res_index // 2]).astype(jnp.int32)
     bf16, f32 = jnp.bfloat16, jnp.float32
 
     def across(blocks):
         return lax.all_to_all(blocks, ("seq", "res"), 0, 0, axis_index_groups=groups, tiled=True)
-
-    def all_quarters(mine):
-        far = swapped(mine, "seq", seq_half)
-        return mine, far, swapped(mine, "res", 1), swapped(far, "res", 1)
 
     x, grad, wc, wo = alignment_rows, updated_gradient, combined_weight, output_weight
     query_blocks, bias, mean, spread = call(
@@ -610,20 +636,24 @@
             place=place, flops=2 * total * total * width,
         )
 
-    logit_mine, logit_sent = scores(query_blocks, 0, residues, True, f32)
-    logit_other = swapped(logit_sent, "seq", seq_half)
     (value_blocks,) = call(
         value_kernel, [((group, 2 * residues, LANES), bf16)], x, grad, wc, wo,
-        flops=8 * tokens * width * width, outside=4, after=(logit_sent,),
-    )
+        flops=8 * tokens * width * width, outside=4,
+    )
+    logit_mine, logit_sent = scores(query_blocks, 0, residues, True, f32)
+    value_blocks, logit_sent = lax.optimization_barrier((value_blocks, logit_sent))
+    logit_other = swapped(logit_sent, "seq", seq_half)
     value_blocks = across(value_blocks)
-
     quarter = (total // 4, total)
     softmax_out, probs = call(
         softmax_kernel, [(quarter, f32), (quarter, bf16)], logit_mine, logit_other,
         flops=total * total,
     )
-    value_blocks, probs = lax.optimization_barrier((value_blocks, probs))
+    probs_far = swapped(probs, "seq", seq_half)
+    value_blocks, probs_far = lax.optimization_barrier((value_blocks, probs_far))
+    grad_mine, grad_sent = scores(value_blocks, residues, 0, False, bf16)
+    grad_other = swapped(grad_sent, "seq", seq_half)
+
     def products(quarters, blocks, first_row, second_row, with_share, factor):
         rows = 2 * residues + (residues // 2 if with_share else 0)
         (out,) = call(
@@ -637,54 +667,69 @@
         )
         return out
 
-    grad_mine, grad_sent = scores(value_blocks, residues, 0, False, bf16)
-    grad_other = swapped(grad_sent, "seq", seq_half)
-    attended = products(all_quarters(probs), value_blocks, 0, residues, False, 1.0)
+    def with_near(mine, far):
+        return mine, far, swapped(mine, "res", 1), swapped(far, "res", 1)
+
+    attended = products(with_near(probs, probs_far), value_blocks, 0, residues, False, 1.0)
     attended, grad_other = lax.optimization_barrier((attended, grad_other))
     attended_blocks = across(attended)
     (grad_logits,) = call(
         softmax_gradient_kernel, [(quarter, bf16)], softmax_out, grad_mine, grad_other,
         flops=total * total,
     )
-
-    grad_blocks = across(
-        products(all_quarters(grad_logits), query_blocks, residues, 0, True, scale)
-    )
-
+    grad_quarters = with_near(grad_logits, swapped(grad_logits, "seq", seq_half))
+    grad_quarters, attended_blocks = lax.optimization_barrier((grad_quarters, attended_blocks))
+    grad_blocks = across(products(grad_quarters, query_blocks, residues, 0, True, scale))
+
+    updated, value_gate, normed, attended_sums = call(
+        attended_weight_kernel,
+        [
+            (x.shape, bf16),
+            ((tokens, 2 * width), bf16),
+            ((tokens, width), bf16),
+            ((width, 3 * width), bf16),
+        ],
+        x, grad, wc, wo, attended_blocks,
+        flops=14 * tokens * width * width, outside=4,
+    )
     share = pltpu.VMEM((heads, residues, LANES), f32)
     (pair_weight_part,) = call(
         pair_weight_kernel, [((heads, channels), f32)],
         grad_blocks, pair_entries, mean, spread,
         scratch=[share], flops=4 * tokens * width * width,
     )
+    columns = 5 * width + channels
+    rows = width // res_size
+    part_rows = ((res_size // 2, rows, columns), bf16)
+    query_key, keep, send = call(
+        query_weight_kernel,
+        [((tokens, 2 * width), bf16), part_rows, part_rows],
+        normed, grad_blocks, pair_weight_part, attended_sums,
+        scratch=[pltpu.VMEM((width, columns), bf16)],
+        place=place, flops=4 * tokens * width * width,
+    )
+    own, *sent = call(
+        core_sum_kernel,
+        [((rows, columns), f32)] + [((rows, columns), bf16)] * 3,
+        keep, swapped(send, "res", 1), place=place,
+    )
+    received = [swapped(t, "res", 2 * flip) for flip, t in enumerate(sent, 1)]
     (pair_gradient,) = call(
         functools.partial(pair_kernel, 2 * residues),
         [(pair_entries.shape, bf16)],
         grad_blocks, pair_entries, pair_weight.T, bias, mean, spread,
         scratch=[share], flops=8 * tokens * width * width,
     )
-    columns = 5 * width + channels
-    rows = width // res_size
-    part_rows = ((res_size // 2, rows, columns), bf16)
-    updated, projected, keep, send = call(
-        weight_kernel,
-        [(x.shape, bf16), ((tokens, 4 * width), bf16), part_rows, part_rows],
-        x, grad, wc, wo, attended_blocks, grad_blocks, pair_weight_part,
-        scratch=[pltpu.VMEM((width, columns), bf16)],
-        place=place, flops=24 * tokens * width * width, outside=4,
-    )
+    received, pair_gradient = lax.optimization_barrier((received, pair_gradient))
+    (part,) = call(plane_sum_kernel, [((rows, columns), bf16)], own, *received)
     (alignment_gradient,) = call(
-        alignment_kernel, [(x.shape, bf16)], x, wc, projected,
+        alignment_kernel, [(x.shape, bf16)], x, wc, query_key, value_gate,
         flops=8 * tokens * width * width,
     )
 
     def added(mine, other):
         return (mine.astype(f32) + other.astype(f32)).astype(bf16)
 
-    parts = added(keep, swapped(send, "res", 1))
-    chips = [[2 * k + core for k in range(res_size // 2)] for core in range(2)]
-    parts = lax.all_to_all(parts, "res", 0, 0, axis_index_groups=chips, tiled=True)
-    part = jnp.sum(parts.astype(f32), axis=0).astype(bf16)
     part = added(part, swapped(part, "seq", 1))
     part = added(part, swapped(part, "seq", seq_half))
     whole = lax.all_gather(part, "res", axis=0)

time: 161 us -> 141 us (0.88)
  blocking collectives: 54.3 us -> 28.9 us
  starting transfers between devices: 12.5 us -> 33 us
  waiting for transfers between devices: 55.7 us -> 45.3 us
  other arithmetic: 6.3 us -> 2.57 us
  local copies, waits for them, and re-layouts: 2.68 us -> 0.17 us
  Pallas kernels: 27.9 us -> 29.8 us
    all_to_all x2 -> x1, blocking collectives: 34.2 us -> 19.7 us  [across(): lax.all_to_all(blocks, ('seq', 'res'), 0, 0, axis_index_groups=groups, ti...]
    ppermute x13 -> x16, starting transfers between devices: 4.63 us -> 16.7 us  [swapped(): lax.ppermute(mine, axis_name, [(a, a ^ distance) for a in range(size)])]
    all_to_all x1 -> x0, blocking collectives: 10.5 us -> none  [head_body(): lax.all_to_all(parts, 'res', 0, 0, axis_index_groups=chips, tiled=True)]
    ppermute x13 -> x16, waiting for transfers between devices: 43.5 us -> 34.7 us  [swapped(): lax.ppermute(mine, axis_name, [(a, a ^ distance) for a in range(size)])]
    all_to_all x2 -> x3, starting transfers between devices: 7.82 us -> 16.4 us  [across(): lax.all_to_all(blocks, ('seq', 'res'), 0, 0, axis_index_groups=groups, ti...]
    unnamed x32 -> x20, local copies, waits for them, and re-layouts: 2.62 us -> 0.1 us
    convert_element_type x3 -> x2, other arithmetic: 2.08 us -> 0.05 us  [added(): return (mine.astype(f32) + other.astype(f32)).astype(bf16)]
    pallas_call x12 -> x15, Pallas kernels: 27.9 us -> 29.8 us  [call(): pl.pallas_call(wrapped, out_shape=shapes, in_specs=[pl.BlockSpec(memory_s...]
  transfers between devices with their start and end apart: 15 -> 19, of which waited for: 11 -> 11; matrix products, arithmetic and copies ran while one was open for 0% -> 0% of each run, Pallas kernels for 6% -> 11%
where the time goes in v9:
time: 141 us
  waiting for transfers between devices  45.3 us (32%)
  starting transfers between devices  33 us (23%)
  Pallas kernels  29.8 us (21%)
  blocking collectives  28.9 us (20%)
  other arithmetic  2.57 us (2%)
    ppermute x16, waiting for transfers between devices, swapped(): lax.ppermute(mine, axis_name, [(a, a ^ distance) for a in range(size)])  34.7 us
    pallas_call x15, Pallas kernels, call(): pl.pallas_call(wrapped, out_shape=shapes, in_specs=[pl.BlockSpec(memory_s...  29.8 us
    all_to_all x1, blocking collectives, across(): lax.all_to_all(blocks, ('seq', 'res'), 0, 0, axis_index_groups=groups, ti...  19.7 us
    ppermute x16, starting transfers between devices, swapped(): lax.ppermute(mine, axis_name, [(a, a ^ distance) for a in range(size)])  16.7 us
    all_to_all x3, starting transfers between devices, across(): lax.all_to_all(blocks, ('seq', 'res'), 0, 0, axis_index_groups=groups, ti...  16.4 us
    all_to_all x3, waiting for transfers between devices, across(): lax.all_to_all(blocks, ('seq', 'res'), 0, 0, axis_index_groups=groups, ti...  10.5 us
    all_gather x1, blocking collectives, head_body(): whole = lax.all_gather(part, 'res', axis=0)  9.25 us
  transfers between devices with their start and end apart: 19, of which 11 were waited for; matrix products, arithmetic and copies ran while one was open for 0% of the time, Pallas kernels for 11%

profile of v9, /device:TPU:0, one launch (start us, length us, event | category | flops | bytes accessed | tf_op | source)
XLA Modules:
  0.0 140.6 jit_solution(15852069394633611474)
XLA Ops:
  0.6 8.1 %shard_map.109 = (bf16[16,192,128]{2,1,0:T(8,128)(2,1)}, f32[8,64,128]{2,1,0:T(8,128)}, f32[64,128]{1,0:T(8,128)}, f32[64,128]{1,0:T(8,128)}) custom-call(bf16[8,64,256]{2,1,0:T(8,128)(2,1)} %refs_0_.7, bf16[256,1024]{1,0:T(8,128)(2,1)} %refs_1_.10, bf16[64,128,128]{2,1,0:T(8,128)(2,1)} %refs_1_.11, f32[8,128]{1,0:T(8,128)} %bitcast.18), custom_call_target="tpu_custom_call" | custom-call | flops 268435456 | bytes 4001792 | tf_op jit(solution)/shard_map/pallas_call | solution.py:567
  8.7 19.7 %all_to_all.20.refs_1_.refs_5_ = bf16[16,192,128]{2,1,0:T(8,128)(2,1)S(1)} all-to-all(bf16[16,192,128]{2,1,0:T(8,128)(2,1)} %get-tuple-element.42), channel_id=1, replica_groups={{0,1,2,3,4,5,6,7,8,9,10,11,12,13,14,15},{16,17,18,19,20,21,22,23,24,25,..., dimensions={0} | all-to-all | bytes 1572864 | tf_op jit(solution)/shard_map/all_to_all | solution.py:616
  28.4 2.7 %shard_map.111 = bf16[16,128,128]{2,1,0:T(8,128)(2,1)} custom-call(bf16[8,64,256]{2,1,0:T(8,128)(2,1)} %refs_0_.7, bf16[8,64,256]{2,1,0:T(8,128)(2,1)} %refs_1_.8, bf16[256,1024]{1,0:T(8,128)(2,1)} %refs_1_.10, bf16[256,256]{1,0:T(8,128)(2,1)} %refs_3_.3), custom_call_target="tpu_custom_call" | custom-call | flops 268435456 | bytes 1703936 | tf_op jit(solution)/shard_map/pallas_call | solution.py:567
  32.2 3.6 %all-to-all-start.1 = ((bf16[16,128,128]{2,1,0:T(8,128)(2,1)}), bf16[16,128,128]{2,1,0:T(8,128)(2,1)S(1)}, u32[]{:S(2)}, u32[]{:S(2)}) async-start(bf16[16,128,128]{2,1,0:T(8,128)(2,1)} %shard_map.111), calls=%async_computation.1 | async-start | bytes 1048576 | tf_op jit(solution)/shard_map/all_to_all | solution.py:616
  35.8 2.7 %collective-permute-start.1 = (f32[128,512]{1,0:T(8,128)S(1)}, f32[128,512]{1,0:T(8,128)S(1)}, u32[]{:S(2)}, u32[]{:S(2)}) collective-permute-start(f32[128,512]{1,0:T(8,128)S(1)} %get-tuple-element.45), channel_id=1, source_target_pairs={{0,16},{8,24},{16,0},{24,8},{1,17},{9,25},{17,1},{25,9},{2,18},{10... | collective-permute-start | bytes 786440 | tf_op jit(solution)/shard_map/ppermute | solution.py:584
  38.5 9.5 %collective-permute-done.1.refs_1_ = f32[128,512]{1,0:T(8,128)S(1)} collective-permute-done((f32[128,512]{1,0:T(8,128)S(1)}, f32[128,512]{1,0:T(8,128)S(1)}, u32[]{:S(2)}, u32[]{:S(2)}) %collective-permute-start.1) | collective-permute-done | bytes 262176 | tf_op jit(solution)/shard_map/ppermute | solution.py:584
  48.2 3.5 %collective-permute-start.2 = (bf16[128,512]{1,0:T(8,128)(2,1)S(1)}, bf16[128,512]{1,0:T(8,128)(2,1)S(1)}, u32[]{:S(2)}, u32[]{:S(2)}) collective-permute-start(bf16[128,512]{1,0:T(8,128)(2,1)S(1)} %get-tuple-element.48.refs_1_), channel_id=1, source_target_pairs={{0,16},{8,24},{16,0},{24,8},{1,17},{9,25},{17,1},{25,9},{2,18},{10... | collective-permute-start | bytes 393224 | tf_op jit(solution)/shard_map/ppermute | solution.py:584
  51.7 3.4 %collective-permute-done.2.refs_2_ = bf16[128,512]{1,0:T(8,128)(2,1)S(1)} collective-permute-done((bf16[128,512]{1,0:T(8,128)(2,1)S(1)}, bf16[128,512]{1,0:T(8,128)(2,1)S(1)}, u32[]{:S(2)}, u32[]{:S(2)}) %collective-permute-start.2) | collective-permute-done | bytes 131104 | tf_op jit(solution)/shard_map/ppermute | solution.py:584
  58.1 2.8 %collective-permute-start.6 = (bf16[128,512]{1,0:T(8,128)(2,1)S(1)}, bf16[128,512]{1,0:T(8,128)(2,1)S(1)}, u32[]{:S(2)}, u32[]{:S(2)}) collective-permute-start(bf16[128,512]{1,0:T(8,128)(2,1)S(1)} %get-tuple-element.52), channel_id=1, source_target_pairs={{0,16},{8,24},{16,0},{24,8},{1,17},{9,25},{17,1},{25,9},{2,18},{10... | collective-permute-start | bytes 393224 | tf_op jit(solution)/shard_map/ppermute | solution.py:584
  60.9 1.8 %shard_map.114 = bf16[16,128,128]{2,1,0:T(8,128)(2,1)} custom-call(s32[3]{0:T(128)S(1)} %pad_add_fusion.refs_0_, bf16[128,512]{1,0:T(8,128)(2,1)S(1)} %get-tuple-element.48.refs_1_, bf16[128,512]{1,0:T(8,128)(2,1)S(1)} %collective-permute-done.2.refs_2_, bf16[128,512]{1,0:T(8,128)(2,1)S(1)} %collective-permute-done.4.refs_3_, ...), custom_call_target="tpu_custom_call" | custom-call | flops 268435456 | bytes 1572864 | tf_op jit(solution)/shard_map/pallas_call | solution.py:567
  62.7 2.0 %collective-permute-done.6.refs_2_ = bf16[128,512]{1,0:T(8,128)(2,1)S(1)} collective-permute-done((bf16[128,512]{1,0:T(8,128)(2,1)S(1)}, bf16[128,512]{1,0:T(8,128)(2,1)S(1)}, u32[]{:S(2)}, u32[]{:S(2)}) %collective-permute-start.6) | collective-permute-done | bytes 131104 | tf_op jit(solution)/shard_map/ppermute | solution.py:584
  64.7 7.4 %all-to-all-start.2 = ((bf16[16,128,128]{2,1,0:T(8,128)(2,1)}), bf16[16,128,128]{2,1,0:T(8,128)(2,1)}, u32[]{:S(2)}, u32[]{:S(2)}) async-start(bf16[16,128,128]{2,1,0:T(8,128)(2,1)} %shard_map.114), calls=%async_computation.2 | async-start | bytes 1048576 | tf_op jit(solution)/shard_map/all_to_all | solution.py:616
  72.3 2.8 %collective-permute-start.7 = (bf16[128,512]{1,0:T(8,128)(2,1)S(1)}, bf16[128,512]{1,0:T(8,128)(2,1)S(1)}, u32[]{:S(2)}, u32[]{:S(2)}) collective-permute-start(bf16[128,512]{1,0:T(8,128)(2,1)S(1)} %shard_map.115.refs_1_), channel_id=1, source_target_pairs={{0,16},{8,24},{16,0},{24,8},{1,17},{9,25},{17,1},{25,9},{2,18},{10... | collective-permute-start | bytes 393224 | tf_op jit(solution)/shard_map/ppermute | solution.py:584
  75.2 6.4 %collective-permute-done.7.refs_2_ = bf16[128,512]{1,0:T(8,128)(2,1)S(1)} collective-permute-done((bf16[128,512]{1,0:T(8,128)(2,1)S(1)}, bf16[128,512]{1,0:T(8,128)(2,1)S(1)}, u32[]{:S(2)}, u32[]{:S(2)}) %collective-permute-start.7) | collective-permute-done | bytes 131104 | tf_op jit(solution)/shard_map/ppermute | solution.py:584
  82.9 2.7 %all-to-all-done.2.refs_4_ = bf16[16,128,128]{2,1,0:T(8,128)(2,1)} async-done(((bf16[16,128,128]{2,1,0:T(8,128)(2,1)}), bf16[16,128,128]{2,1,0:T(8,128)(2,1)}, u32[]{:S(2)}, u32[]{:S(2)}) %all-to-all-start.2) | async-done | bytes 524320 | tf_op jit(solution)/shard_map/all_to_all | solution.py:616
  85.5 1.9 %shard_map.117 = bf16[16,160,128]{2,1,0:T(8,128)(2,1)} custom-call(s32[3]{0:T(128)S(1)} %pad_add_fusion.refs_0_, bf16[128,512]{1,0:T(8,128)(2,1)S(1)} %shard_map.115.refs_1_, bf16[128,512]{1,0:T(8,128)(2,1)S(1)} %collective-permute-done.7.refs_2_, bf16[128,512]{1,0:T(8,128)(2,1)S(1)} %collective-permute-done.8.refs_3_, ...), custom_call_target="tpu_custom_call" | custom-call | flops 268435456 | bytes 1966080 | tf_op jit(solution)/shard_map/pallas_call | solution.py:567
  87.4 5.4 %all-to-all-start.3 = ((bf16[16,160,128]{2,1,0:T(8,128)(2,1)}), bf16[16,160,128]{2,1,0:T(8,128)(2,1)S(1)}, u32[]{:S(2)}, u32[]{:S(2)}) async-start(bf16[16,160,128]{2,1,0:T(8,128)(2,1)} %shard_map.117), calls=%async_computation.3 | async-start | bytes 1310720 | tf_op jit(solution)/shard_map/all_to_all | solution.py:616
  92.8 4.1 %shard_map.116 = (bf16[8,64,256]{2,1,0:T(8,128)(2,1)}, bf16[512,512]{1,0:T(8,128)(2,1)}, bf16[512,256]{1,0:T(8,128)(2,1)}, bf16[256,768]{1,0:T(8,128)(2,1)}) custom-call(bf16[8,64,256]{2,1,0:T(8,128)(2,1)} %refs_0_.7, bf16[8,64,256]{2,1,0:T(8,128)(2,1)} %refs_1_.8, bf16[256,1024]{1,0:T(8,128)(2,1)} %refs_1_.10, bf16[256,256]{1,0:T(8,128)(2,1)} %refs_3_.3, ...), custom_call_target="tpu_custom_call" | custom-call | flops 469762048 | bytes 3145728 | tf_op jit(solution)/shard_map/pallas_call | solution.py:567
  96.9 7.9 %all-to-all-done.3.refs_0_.refs_2_ = bf16[16,160,128]{2,1,0:T(8,128)(2,1)S(1)} async-done(((bf16[16,160,128]{2,1,0:T(8,128)(2,1)}), bf16[16,160,128]{2,1,0:T(8,128)(2,1)S(1)}, u32[]{:S(2)}, u32[]{:S(2)}) %all-to-all-start.3) | async-done | bytes 655392 | tf_op jit(solution)/shard_map/all_to_all | solution.py:616
  110.9 2.5 %collective-permute-start.13 = (bf16[32,1408]{1,0:T(8,128)(2,1)S(1)}, bf16[32,1408]{1,0:T(8,128)(2,1)S(1)}, u32[]{:S(2)}, u32[]{:S(2)}) collective-permute-start(bf16[32,1408]{1,0:T(8,128)(2,1)S(1)} %get-tuple-element.71), channel_id=1, source_target_pairs={{0,6},{1,7},{2,4},{3,5},{4,2},{5,3},{6,0},{7,1},{8,14},{9,15},{10,... | collective-permute-start | bytes 270344 | tf_op jit(solution)/shard_map/ppermute | solution.py:584
  113.4 4.3 %shard_map.122 = bf16[64,128,128]{2,1,0:T(8,128)(2,1)} custom-call(bf16[16,160,128]{2,1,0:T(8,128)(2,1)S(1)} %all-to-all-done.3.refs_0_.refs_2_, bf16[64,128,128]{2,1,0:T(8,128)(2,1)S(1)} %copy-done, f32[8,128]{1,0:T(8,128)S(1)} %bitcast.19, f32[8,64,128]{2,1,0:T(8,128)S(1)} %copy-done.5, f32[64,128]{1,0:T(8,128)S(1)} %copy-done.7, f32[64,128]{1,0:T(8,128)S(1)} %copy-done.8), custom_call_target="tpu_custom_call" | custom-call | flops 268435456 | bytes 5181440 | tf_op jit(solution)/shard_map/pallas_call | solution.py:567
  118.4 4.0 %collective-permute-done.14 = bf16[32,1408]{1,0:T(8,128)(2,1)S(1)} collective-permute-done((bf16[32,1408]{1,0:T(8,128)(2,1)S(1)}, bf16[32,1408]{1,0:T(8,128)(2,1)S(1)}, u32[]{:S(2)}, u32[]{:S(2)}) %collective-permute-start.14) | collective-permute-done | bytes 90144 | tf_op jit(solution)/shard_map/ppermute | solution.py:584
  123.8 5.1 %collective-permute-done.15 = bf16[32,1408]{1,0:T(8,128)(2,1)S(1)} collective-permute-done((bf16[32,1408]{1,0:T(8,128)(2,1)S(1)}, bf16[32,1408]{1,0:T(8,128)(2,1)S(1)}, u32[]{:S(2)}, u32[]{:S(2)}) %collective-permute-start.15) | collective-permute-done | bytes 90144 | tf_op jit(solution)/shard_map/ppermute | solution.py:584
  128.9 9.3 %all-gather = bf16[256,1408]{1,0:T(8,128)(2,1)S(1)} all-gather(bf16[32,1408]{1,0:T(8,128)(2,1)S(1)} %add_convert_fusion), channel_id=2, replica_groups=mesh['seq'=4,'res'=8] {'res'}, dimensions={0}, use_global_device_ids=true | all-gather | bytes 811008 | tf_op jit(solution)/shard_map/all_gather | solution.py:735
  (60 shorter events, 16.5 us)
Async XLA Ops:
  28.4 2.8 %collective-permute-start = (bf16[16,192,128]{2,1,0:T(8,128)(2,1)S(1)}, bf16[16,192,128]{2,1,0:T(8,128)(2,1)S(1)}, u32[]{:S(2)}, u32[]{:S(2)}) collective-permute-start(bf16[16,192,128]{2,1,0:T(8,128)(2,1)S(1)} %all_to_all.20.refs_1_.refs_5_), channel_id=1, source_target_pairs={{0,1},{1,0},{2,3},{3,2},{4,5},{5,4},{6,7},{7,6},{8,9},{9,8},{10,11... | collective-permute-start | bytes 2359304 | tf_op jit(solution)/shard_map/ppermute | solution.py:584
  32.2 22.9 %all-to-all-start.1 = ((bf16[16,128,128]{2,1,0:T(8,128)(2,1)}), bf16[16,128,128]{2,1,0:T(8,128)(2,1)S(1)}, u32[]{:S(2)}, u32[]{:S(2)}) async-start(bf16[16,128,128]{2,1,0:T(8,128)(2,1)} %shard_map.111), calls=%async_computation.1 | async-start | bytes 1048576 | tf_op jit(solution)/shard_map/all_to_all | solution.py:616
  35.8 12.2 %collective-permute-start.1 = (f32[128,512]{1,0:T(8,128)S(1)}, f32[128,512]{1,0:T(8,128)S(1)}, u32[]{:S(2)}, u32[]{:S(2)}) collective-permute-start(f32[128,512]{1,0:T(8,128)S(1)} %get-tuple-element.45), channel_id=1, source_target_pairs={{0,16},{8,24},{16,0},{24,8},{1,17},{9,25},{17,1},{25,9},{2,18},{10... | collective-permute-start | bytes 786440 | tf_op jit(solution)/shard_map/ppermute | solution.py:584
  48.2 6.9 %collective-permute-start.2 = (bf16[128,512]{1,0:T(8,128)(2,1)S(1)}, bf16[128,512]{1,0:T(8,128)(2,1)S(1)}, u32[]{:S(2)}, u32[]{:S(2)}) collective-permute-start(bf16[128,512]{1,0:T(8,128)(2,1)S(1)} %get-tuple-element.48.refs_1_), channel_id=1, source_target_pairs={{0,16},{8,24},{16,0},{24,8},{1,17},{9,25},{17,1},{25,9},{2,18},{10... | collective-permute-start | bytes 393224 | tf_op jit(solution)/shard_map/ppermute | solution.py:584
  55.2 1.9 %collective-permute-start.3 = (bf16[16,128,128]{2,1,0:T(8,128)(2,1)S(1)}, bf16[16,128,128]{2,1,0:T(8,128)(2,1)S(1)}, u32[]{:S(2)}, u32[]{:S(2)}) collective-permute-start(bf16[16,128,128]{2,1,0:T(8,128)(2,1)S(1)} %all-to-all-done.1.refs_1_.refs_5_), channel_id=1, source_target_pairs={{0,1},{1,0},{2,3},{3,2},{4,5},{5,4},{6,7},{7,6},{8,9},{9,8},{10,11... | collective-permute-start | bytes 1572872 | tf_op jit(solution)/shard_map/ppermute | solution.py:584
  55.2 5.7 %collective-permute-start.4 = (bf16[128,512]{1,0:T(8,128)(2,1)S(1)}, bf16[128,512]{1,0:T(8,128)(2,1)S(1)}, u32[]{:S(2)}, u32[]{:S(2)}) collective-permute-start(bf16[128,512]{1,0:T(8,128)(2,1)S(1)} %get-tuple-element.48.refs_1_), channel_id=1, source_target_pairs={{0,1},{1,0},{2,3},{3,2},{4,5},{5,4},{6,7},{7,6},{8,9},{9,8},{10,11... | collective-permute-start | bytes 393224 | tf_op jit(solution)/shard_map/ppermute | solution.py:584
  55.7 5.2 %collective-permute-start.5 = (bf16[128,512]{1,0:T(8,128)(2,1)S(1)}, bf16[128,512]{1,0:T(8,128)(2,1)S(1)}, u32[]{:S(2)}, u32[]{:S(2)}) collective-permute-start(bf16[128,512]{1,0:T(8,128)(2,1)S(1)} %collective-permute-done.2.refs_2_), channel_id=1, source_target_pairs={{0,1},{1,0},{2,3},{3,2},{4,5},{5,4},{6,7},{7,6},{8,9},{9,8},{10,11... | collective-permute-start | bytes 393224 | tf_op jit(solution)/shard_map/ppermute | solution.py:584
  58.1 6.6 %collective-permute-start.6 = (bf16[128,512]{1,0:T(8,128)(2,1)S(1)}, bf16[128,512]{1,0:T(8,128)(2,1)S(1)}, u32[]{:S(2)}, u32[]{:S(2)}) collective-permute-start(bf16[128,512]{1,0:T(8,128)(2,1)S(1)} %get-tuple-element.52), channel_id=1, source_target_pairs={{0,16},{8,24},{16,0},{24,8},{1,17},{9,25},{17,1},{25,9},{2,18},{10... | collective-permute-start | bytes 393224 | tf_op jit(solution)/shard_map/ppermute | solution.py:584
  64.7 20.9 %all-to-all-start.2 = ((bf16[16,128,128]{2,1,0:T(8,128)(2,1)}), bf16[16,128,128]{2,1,0:T(8,128)(2,1)}, u32[]{:S(2)}, u32[]{:S(2)}) async-start(bf16[16,128,128]{2,1,0:T(8,128)(2,1)} %shard_map.114), calls=%async_computation.2 | async-start | bytes 1048576 | tf_op jit(solution)/shard_map/all_to_all | solution.py:616
  72.2 32.5 %copy-start = (bf16[64,128,128]{2,1,0:T(8,128)(2,1)S(1)}, bf16[64,128,128]{2,1,0:T(8,128)(2,1)}, u32[]{:S(2)}) copy-start(bf16[64,128,128]{2,1,0:T(8,128)(2,1)} %refs_1_.11) | copy-start | bytes 6291460
  72.3 32.5 %copy-start.7 = (f32[64,128]{1,0:T(8,128)S(1)}, f32[64,128]{1,0:T(8,128)}, u32[]{:S(2)}) copy-start(f32[64,128]{1,0:T(8,128)} %get-tuple-element.62.refs_2_.refs_4_) | copy-start | bytes 98308
  72.3 32.5 %copy-start.8 = (f32[64,128]{1,0:T(8,128)S(1)}, f32[64,128]{1,0:T(8,128)}, u32[]{:S(2)}) copy-start(f32[64,128]{1,0:T(8,128)} %get-tuple-element.63.refs_3_.refs_5_) | copy-start | bytes 98308
  72.3 9.2 %collective-permute-start.7 = (bf16[128,512]{1,0:T(8,128)(2,1)S(1)}, bf16[128,512]{1,0:T(8,128)(2,1)S(1)}, u32[]{:S(2)}, u32[]{:S(2)}) collective-permute-start(bf16[128,512]{1,0:T(8,128)(2,1)S(1)} %shard_map.115.refs_1_), channel_id=1, source_target_pairs={{0,16},{8,24},{16,0},{24,8},{1,17},{9,25},{17,1},{25,9},{2,18},{10... | collective-permute-start | bytes 393224 | tf_op jit(solution)/shard_map/ppermute | solution.py:584
  75.1 6.4 %collective-permute-start.8 = (bf16[128,512]{1,0:T(8,128)(2,1)S(1)}, bf16[128,512]{1,0:T(8,128)(2,1)S(1)}, u32[]{:S(2)}, u32[]{:S(2)}) collective-permute-start(bf16[128,512]{1,0:T(8,128)(2,1)S(1)} %shard_map.115.refs_1_), channel_id=1, source_target_pairs={{0,1},{1,0},{2,3},{3,2},{4,5},{5,4},{6,7},{7,6},{8,9},{9,8},{10,11... | collective-permute-start | bytes 393224 | tf_op jit(solution)/shard_map/ppermute | solution.py:584
  81.5 1.3 collective-permute-start.9
  87.4 17.3 %all-to-all-start.3 = ((bf16[16,160,128]{2,1,0:T(8,128)(2,1)}), bf16[16,160,128]{2,1,0:T(8,128)(2,1)S(1)}, u32[]{:S(2)}, u32[]{:S(2)}) async-start(bf16[16,160,128]{2,1,0:T(8,128)(2,1)} %shard_map.117), calls=%async_computation.3 | async-start | bytes 1310720 | tf_op jit(solution)/shard_map/all_to_all | solution.py:616
  96.9 9.4 %copy-start.4 = (bf16[256,768]{1,0:T(8,128)(2,1)S(1)}, bf16[256,768]{1,0:T(8,128)(2,1)}, u32[]{:S(2)}) copy-start(bf16[256,768]{1,0:T(8,128)(2,1)} %get-tuple-element.64.refs_4_) | copy-start | bytes 1179652
  96.9 9.4 %copy-start.6 = (bf16[512,256]{1,0:T(8,128)(2,1)S(1)}, bf16[512,256]{1,0:T(8,128)(2,1)}, u32[]{:S(2)}) copy-start(bf16[512,256]{1,0:T(8,128)(2,1)} %get-tuple-element.57.refs_1_) | copy-start | bytes 786436
  107.4 1.7 %collective-permute-start.10 = (bf16[4,32,1408]{2,1,0:T(8,128)(2,1)S(1)}, bf16[4,32,1408]{2,1,0:T(8,128)(2,1)S(1)}, u32[]{:S(2)}, u32[]{:S(2)}) collective-permute-start(bf16[4,32,1408]{2,1,0:T(8,128)(2,1)S(1)} %get-tuple-element.68), channel_id=1, source_target_pairs={{0,1},{1,0},{2,3},{3,2},{4,5},{5,4},{6,7},{7,6},{8,9},{9,8},{10,11... | collective-permute-start | bytes 1081352 | tf_op jit(solution)/shard_map/ppermute | solution.py:584
  109.8 7.9 %collective-permute-start.11 = (bf16[32,1408]{1,0:T(8,128)(2,1)S(1)}, bf16[32,1408]{1,0:T(8,128)(2,1)S(1)}, u32[]{:S(2)}, u32[]{:S(2)}) collective-permute-start(bf16[32,1408]{1,0:T(8,128)(2,1)S(1)} %get-tuple-element.69), channel_id=1, source_target_pairs={{0,2},{1,3},{2,0},{3,1},{4,6},{5,7},{6,4},{7,5},{8,10},{9,11},{10,... | collective-permute-start | bytes 270344 | tf_op jit(solution)/shard_map/ppermute | solution.py:584
  109.9 7.8 %collective-permute-start.12 = (bf16[32,1408]{1,0:T(8,128)(2,1)S(1)}, bf16[32,1408]{1,0:T(8,128)(2,1)S(1)}, u32[]{:S(2)}, u32[]{:S(2)}) collective-permute-start(bf16[32,1408]{1,0:T(8,128)(2,1)S(1)} %get-tuple-element.70), channel_id=1, source_target_pairs={{0,4},{1,5},{2,6},{3,7},{4,0},{5,1},{6,2},{7,3},{8,12},{9,13},{10,... | collective-permute-start | bytes 270344 | tf_op jit(solution)/shard_map/ppermute | solution.py:584
  110.9 6.8 %collective-permute-start.13 = (bf16[32,1408]{1,0:T(8,128)(2,1)S(1)}, bf16[32,1408]{1,0:T(8,128)(2,1)S(1)}, u32[]{:S(2)}, u32[]{:S(2)}) collective-permute-start(bf16[32,1408]{1,0:T(8,128)(2,1)S(1)} %get-tuple-element.71), channel_id=1, source_target_pairs={{0,6},{1,7},{2,4},{3,5},{4,2},{5,3},{6,0},{7,1},{8,14},{9,15},{10,... | collective-permute-start | bytes 270344 | tf_op jit(solution)/shard_map/ppermute | solution.py:584
  117.7 4.6 %collective-permute-start.14 = (bf16[32,1408]{1,0:T(8,128)(2,1)S(1)}, bf16[32,1408]{1,0:T(8,128)(2,1)S(1)}, u32[]{:S(2)}, u32[]{:S(2)}) collective-permute-start(bf16[32,1408]{1,0:T(8,128)(2,1)S(1)} %shard_map.123), channel_id=1, source_target_pairs={{0,8},{8,0},{16,24},{24,16},{1,9},{9,1},{17,25},{25,17},{2,10},{10... | collective-permute-start | bytes 270344 | tf_op jit(solution)/shard_map/ppermute | solution.py:584
  122.4 6.5 %collective-permute-start.15 = (bf16[32,1408]{1,0:T(8,128)(2,1)S(1)}, bf16[32,1408]{1,0:T(8,128)(2,1)S(1)}, u32[]{:S(2)}, u32[]{:S(2)}) collective-permute-start(bf16[32,1408]{1,0:T(8,128)(2,1)S(1)} %add_convert_fusion.1), channel_id=1, source_target_pairs={{0,16},{8,24},{16,0},{24,8},{1,17},{9,25},{17,1},{25,9},{2,18},{10... | collective-permute-start | bytes 270344 | tf_op jit(solution)/shard_map/ppermute | solution.py:584
  (5 other events, 44.5 us)

commit v10 on v9

--- a/solution.py
+++ b/solution.py
@@ -238,31 +238,32 @@
     return weight - jnp.mean(weight, axis=1, keepdims=True)
 
 
-def query_kernel(
-    scale, arrive, x_ref, wc_ref, pair_ref, weight_ref, out_ref, bias_ref, mean_ref, spread_ref
-):
+def query_kernel(scale, x_ref, wc_ref, out_ref):
     residues, width = x_ref.shape[1], x_ref.shape[2]
-    heads = weight_ref.shape[0]
     normed = normalized(x_ref)[0].astype(jnp.bfloat16)
     pack_heads(out_ref, 0, f32_dot(normed, wc_ref[:, :width]) * scale, residues)
     pack_heads(out_ref, residues, f32_dot(normed, wc_ref[:, width : 2 * width]), residues)
 
-    arrive()
-    columns, channels = pair_ref.shape[1], pair_ref.shape[2]
+
+def bias_kernel(pair_ref, weight_ref, out_ref, bias_ref, mean_ref, spread_ref):
+    heads = weight_ref.shape[0]
+    residues, columns, channels = pair_ref.shape
     weight = centred(weight_ref[...])
     first = weight.astype(jnp.bfloat16)
     second, third = two_terms(weight - first.astype(jnp.float32))
     share = jnp.full((heads, channels), 1.0 / channels, jnp.bfloat16)
     left = jnp.concatenate([first, second, third, share], axis=0)
-    average = jnp.full((channels, channels), 1.0 / channels, jnp.bfloat16)
+    shares = jnp.concatenate([share, share], axis=1)
+    row = lax.broadcasted_iota(jnp.int32, (channels, channels), 0)
+    column = lax.broadcasted_iota(jnp.int32, (channels, channels), 1)
+    less_mean = (jnp.where(row == column, 1.0, 0.0) - 1.0 / channels).astype(jnp.bfloat16)
     step_rows = 8
 
     def rows(step, carry):
         start = pl.multiple_of(step * step_rows, step_rows)
         entries = pair_ref[pl.ds(start, step_rows)].reshape(step_rows * columns, channels)
-        center = entries.astype(jnp.float32) - f32_dot(entries, average)
-        high, low = two_terms(center * center)
-        variance = f32_dot(share, high, NT) + f32_dot(share, low, NT)
+        center = f32_dot(entries, less_mean)
+        variance = f32_dot(shares, jnp.concatenate(two_terms(center * center), axis=1), NT)
         spread = lax.rsqrt(variance + eps_norm)
         raw = f32_dot(left, entries, NT)
         bias = spread * (raw[:heads] + raw[heads : 2 * heads] + raw[2 * heads : 3 * heads])
@@ -273,13 +274,13 @@
             spread_ref[pl.ds(start + k, 1), :] = spread[:1, lanes]
         return carry
 
-    lax.fori_loop(0, pair_ref.shape[0] // step_rows, rows, 0)
+    lax.fori_loop(0, residues // step_rows, rows, 0)
     half = residues // 2
     for h in range(heads):
         for core in range(2):
             high, low = two_terms(bias_ref[h, core * half : (core + 1) * half, :])
-            out_ref[h * 2 + core, 2 * residues : 2 * residues + half, :] = high
-            out_ref[h * 2 + core, 2 * residues + half : 3 * residues, :] = low
+            out_ref[h * 2 + core, :half, :] = high
+            out_ref[h * 2 + core, half:, :] = low
 
 
 def lanes_of(blocks_ref, row, residues):
@@ -292,7 +293,7 @@
 
 
 def score_kernel(
-    residues, left_row, right_row, with_bias, place_ref, own_ref, other_ref, mine_ref, sent_ref
+    residues, left_row, right_row, place_ref, own_ref, other_ref, mine_ref, sent_ref
 ):
     core, half = place_ref[0], place_ref[1]
     count = own_ref.shape[0] // 2
@@ -316,19 +317,30 @@
                 )
             )
         ref[...] = f32_dot(jnp.concatenate(left, axis=0), right, NT).astype(ref.dtype)
-        if with_bias:
-            for p in range(2):
-                columns = pl.ds(pl.multiple_of((half * 2 + p) * LANES, LANES), LANES)
-                for k in range(count // 2):
-                    block = p * count + which * (count // 2) + k
-                    high = own_ref[block, 2 * residues : 2 * residues + part, :]
-                    low = own_ref[block, 2 * residues + part : 3 * residues, :]
-                    bias = high.astype(jnp.float32) + low.astype(jnp.float32)
-                    ref[k * part : (k + 1) * part, columns] += bias
-
-
-def softmax_kernel(logit_ref, other_ref, out_ref, low_ref):
-    logits = logit_ref[...] + other_ref[...]
+
+
+def add_bias(place_ref, blocks_ref, which, ref):
+    half = place_ref[1]
+    count, part = blocks_ref.shape[0] // 2, blocks_ref.shape[1] // 2
+    for p in range(2):
+        columns = pl.ds(pl.multiple_of((half * 2 + p) * LANES, LANES), LANES)
+        for k in range(count // 2):
+            block = p * count + which * (count // 2) + k
+            bias = blocks_ref[block, :part, :].astype(jnp.float32) + blocks_ref[
+                block, part:, :
+            ].astype(jnp.float32)
+            ref[k * part : (k + 1) * part, columns] += bias
+
+
+def sent_bias_kernel(place_ref, blocks_ref, sent_ref, out_ref):
+    out_ref[...] = sent_ref[...]
+    add_bias(place_ref, blocks_ref, 1 - place_ref[1], out_ref)
+
+
+def softmax_kernel(place_ref, blocks_ref, logit_ref, other_ref, out_ref, low_ref):
+    out_ref[...] = logit_ref[...] + other_ref[...]
+    add_bias(place_ref, blocks_ref, place_ref[1], out_ref)
+    logits = out_ref[...]
     lifted = jnp.exp(logits - jnp.max(logits, axis=-1, keepdims=True))
     softmax_out = lifted / jnp.sum(lifted, axis=-1, keepdims=True)
     out_ref[...] = softmax_out
@@ -532,7 +544,7 @@
     lax.fori_loop(0, pair_ref.shape[0] // 8, rows, 0)
 
 
-def call(kernel, outs, *args, scratch=(), place=None, flops=0, after=(), outside=0, late=0):
+def call(kernel, outs, *args, scratch=(), place=None, flops=0, after=(), outside=0):
     whole, anywhere = pl.BlockSpec(memory_space=pltpu.VMEM), pl.BlockSpec(memory_space=pl.ANY)
     specs = [anywhere] * outside + [whole] * (len(args) - outside)
     ahead = () if place is None else (place,)
@@ -555,10 +567,8 @@
                 given[len(ahead) + k] = held[k]
             for copy in copies:
                 copy.start()
-            for copy in copies[: outside - late]:
+            for copy in copies:
                 copy.wait()
-            if late:
-                given.insert(0, lambda: [copy.wait() for copy in copies[outside - late :]])
         kernel(*given, *rest)
 
     held = [pltpu.VMEM(a.shape, a.dtype) for a in args[:outside]]
@@ -616,42 +626,56 @@
         return lax.all_to_all(blocks, ("seq", "res"), 0, 0, axis_index_groups=groups, tiled=True)
 
     x, grad, wc, wo = alignment_rows, updated_gradient, combined_weight, output_weight
-    query_blocks, bias, mean, spread = call(
-        functools.partial(query_kernel, scale),
+    (query_blocks,) = call(
+        functools.partial(query_kernel, scale), [((group, 2 * residues, LANES), bf16)], x, wc,
+        flops=8 * tokens * width * width, outside=2,
+    )
+    query_blocks = across(query_blocks)
+    bias_blocks, bias, mean, spread = call(
+        bias_kernel,
         [
-            ((group, 3 * residues, LANES), bf16),
+            ((group, residues, LANES), bf16),
             ((heads, residues, LANES), f32),
             ((residues, LANES), f32),
             ((residues, LANES), f32),
         ],
-        x, wc, pair_entries, pair_weight.T,
-        flops=8 * tokens * width * width, outside=3, late=1,
-    )
-    query_blocks = across(query_blocks)
-    def scores(blocks, left_row, right_row, with_bias, kind):
+        pair_entries, pair_weight.T,
+        flops=8 * tokens * width * width, outside=1,
+    )
+    (value_blocks,) = call(
+        value_kernel, [((group, 2 * residues, LANES), bf16)], x, grad, wc, wo,
+        flops=8 * tokens * width * width, outside=4,
+    )
+    query_blocks, bias_blocks, value_blocks = lax.optimization_barrier(
+        (query_blocks, bias_blocks, value_blocks)
+    )
+    bias_blocks = across(bias_blocks)
+
+    def scores(blocks, left_row, right_row, kind):
         return call(
-            functools.partial(score_kernel, residues, left_row, right_row, with_bias),
+            functools.partial(score_kernel, residues, left_row, right_row),
             [((total // 4, total), f32), ((total // 4, total), kind)],
             blocks, swapped(blocks, "res", 1),
             place=place, flops=2 * total * total * width,
         )
 
-    (value_blocks,) = call(
-        value_kernel, [((group, 2 * residues, LANES), bf16)], x, grad, wc, wo,
-        flops=8 * tokens * width * width, outside=4,
-    )
-    logit_mine, logit_sent = scores(query_blocks, 0, residues, True, f32)
+    logit_mine, logit_sent = scores(query_blocks, 0, residues, f32)
+    logit_sent, bias_blocks = lax.optimization_barrier((logit_sent, bias_blocks))
+    quarter = (total // 4, total)
+    (logit_sent,) = call(
+        sent_bias_kernel, [(quarter, f32)], bias_blocks, logit_sent, place=place,
+        flops=total * total,
+    )
     value_blocks, logit_sent = lax.optimization_barrier((value_blocks, logit_sent))
     logit_other = swapped(logit_sent, "seq", seq_half)
     value_blocks = across(value_blocks)
-    quarter = (total // 4, total)
     softmax_out, probs = call(
-        softmax_kernel, [(quarter, f32), (quarter, bf16)], logit_mine, logit_other,
-        flops=total * total,
+        softmax_kernel, [(quarter, f32), (quarter, bf16)], bias_blocks, logit_mine, logit_other,
+        place=place, flops=total * total,
     )
     probs_far = swapped(probs, "seq", seq_half)
     value_blocks, probs_far = lax.optimization_barrier((value_blocks, probs_far))
-    grad_mine, grad_sent = scores(value_blocks, residues, 0, False, bf16)
+    grad_mine, grad_sent = scores(value_blocks, residues, 0, bf16)
     grad_other = swapped(grad_sent, "seq", seq_half)
 
     def products(quarters, blocks, first_row, second_row, with_share, factor):
@@ -671,8 +695,8 @@
         return mine, far, swapped(mine, "res", 1), swapped(far, "res", 1)
 
     attended = products(with_near(probs, probs_far), value_blocks, 0, residues, False, 1.0)
-    attended, grad_other = lax.optimization_barrier((attended, grad_other))
     attended_blocks = across(attended)
+    grad_other = lax.optimization_barrier((attended, grad_other))[1]
     (grad_logits,) = call(
         softmax_gradient_kernel, [(quarter, bf16)], softmax_out, grad_mine, grad_other,
         flops=total * total,

time: 141 us -> 143 us (1.014)
  blocking collectives: 28.9 us -> 9.32 us
  starting transfers between devices: 33 us -> 49 us
  Pallas kernels: 29.8 us -> 32.8 us
  waiting for transfers between devices: 45.3 us -> 47.8 us
    all_to_all x1 -> x0, blocking collectives: 19.7 us -> none  [across(): lax.all_to_all(blocks, ('seq', 'res'), 0, 0, axis_index_groups=groups, ti...]
    all_to_all x3 -> x5, starting transfers between devices: 16.4 us -> 29.2 us  [across(): lax.all_to_all(blocks, ('seq', 'res'), 0, 0, axis_index_groups=groups, ti...]
    all_to_all x3 -> x5, waiting for transfers between devices: 10.5 us -> 15 us  [across(): lax.all_to_all(blocks, ('seq', 'res'), 0, 0, axis_index_groups=groups, ti...]
    ppermute x16, starting transfers between devices: 16.7 us -> 19.8 us  [swapped(): lax.ppermute(mine, axis_name, [(a, a ^ distance) for a in range(size)])]
    pallas_call x15 -> x17, Pallas kernels: 29.8 us -> 32.8 us  [call(): pl.pallas_call(wrapped, out_shape=shapes, in_specs=[pl.BlockSpec(memory_s...]
    ppermute x16, waiting for transfers between devices: 34.7 us -> 32.8 us  [swapped(): lax.ppermute(mine, axis_name, [(a, a ^ distance) for a in range(size)])]
  transfers between devices with their start and end apart: 19 -> 21, of which waited for: 11 -> 13; matrix products, arithmetic and copies ran while one was open for 0% -> 0% of each run, Pallas kernels for 11% -> 16%
where the time goes in v10:
time: 143 us
  starting transfers between devices  49 us (34%)
  waiting for transfers between devices  47.8 us (33%)
  Pallas kernels  32.8 us (23%)
  blocking collectives  9.32 us (7%)
  other arithmetic  2.57 us (2%)
    ppermute x16, waiting for transfers between devices, swapped(): lax.ppermute(mine, axis_name, [(a, a ^ distance) for a in range(size)])  32.8 us
    pallas_call x17, Pallas kernels, call(): pl.pallas_call(wrapped, out_shape=shapes, in_specs=[pl.BlockSpec(memory_s...  32.8 us
    all_to_all x5, starting transfers between devices, across(): lax.all_to_all(blocks, ('seq', 'res'), 0, 0, axis_index_groups=groups, ti...  29.2 us
    ppermute x16, starting transfers between devices, swapped(): lax.ppermute(mine, axis_name, [(a, a ^ distance) for a in range(size)])  19.8 us
    all_to_all x5, waiting for transfers between devices, across(): lax.all_to_all(blocks, ('seq', 'res'), 0, 0, axis_index_groups=groups, ti...  15 us
    all_gather x1, blocking collectives, head_body(): whole = lax.all_gather(part, 'res', axis=0)  9.32 us
  transfers between devices with their start and end apart: 21, of which 13 were waited for; matrix products, arithmetic and copies ran while one was open for 0% of the time, Pallas kernels for 16%

profile of v10, /device:TPU:0, one launch (start us, length us, event | category | flops | bytes accessed | tf_op | source)
XLA Modules:
  0.0 142.5 jit_solution(16978996367405793116)
XLA Ops:
  0.6 2.6 %shard_map.109 = bf16[16,128,128]{2,1,0:T(8,128)(2,1)} custom-call(bf16[8,64,256]{2,1,0:T(8,128)(2,1)} %refs_0_.9, bf16[256,1024]{1,0:T(8,128)(2,1)} %refs_1_.10), custom_call_target="tpu_custom_call" | custom-call | flops 268435456 | bytes 1310720 | tf_op jit(solution)/shard_map/pallas_call | solution.py:577
  3.3 6.3 %all-to-all-start = ((bf16[16,128,128]{2,1,0:T(8,128)(2,1)}), bf16[16,128,128]{2,1,0:T(8,128)(2,1)S(1)}, u32[]{:S(2)}, u32[]{:S(2)}) async-start(bf16[16,128,128]{2,1,0:T(8,128)(2,1)} %shard_map.109), calls=%async_computation | async-start | bytes 1048576 | tf_op jit(solution)/shard_map/all_to_all | solution.py:626
  9.6 2.7 %shard_map.111 = bf16[16,128,128]{2,1,0:T(8,128)(2,1)} custom-call(bf16[8,64,256]{2,1,0:T(8,128)(2,1)} %refs_0_.9, bf16[8,64,256]{2,1,0:T(8,128)(2,1)} %refs_1_.8, bf16[256,1024]{1,0:T(8,128)(2,1)} %refs_1_.10, bf16[256,256]{1,0:T(8,128)(2,1)} %refs_3_.3), custom_call_target="tpu_custom_call" | custom-call | flops 268435456 | bytes 1703936 | tf_op jit(solution)/shard_map/pallas_call | solution.py:577
  12.3 7.3 %shard_map.110 = (bf16[16,64,128]{2,1,0:T(8,128)(2,1)}, f32[8,64,128]{2,1,0:T(8,128)}, f32[64,128]{1,0:T(8,128)}, f32[64,128]{1,0:T(8,128)}) custom-call(bf16[64,128,128]{2,1,0:T(8,128)(2,1)} %refs_1_.11, f32[8,128]{1,0:T(8,128)} %bitcast.18), custom_call_target="tpu_custom_call" | custom-call | flops 268435456 | bytes 2691072 | tf_op jit(solution)/shard_map/pallas_call | solution.py:577
  20.1 4.8 %all-to-all-start.1 = ((bf16[16,64,128]{2,1,0:T(8,128)(2,1)}), bf16[16,64,128]{2,1,0:T(8,128)(2,1)S(1)}, u32[]{:S(2)}, u32[]{:S(2)}) async-start(bf16[16,64,128]{2,1,0:T(8,128)(2,1)} %get-tuple-element.49), calls=%async_computation.1 | async-start | bytes 524288 | tf_op jit(solution)/shard_map/all_to_all | solution.py:626
  26.1 6.6 %all-to-all-done.1.refs_1_ = bf16[16,64,128]{2,1,0:T(8,128)(2,1)S(1)} async-done(((bf16[16,64,128]{2,1,0:T(8,128)(2,1)}), bf16[16,64,128]{2,1,0:T(8,128)(2,1)S(1)}, u32[]{:S(2)}, u32[]{:S(2)}) %all-to-all-start.1) | async-done | bytes 262176 | tf_op jit(solution)/shard_map/all_to_all | solution.py:626
  33.3 3.6 %all-to-all-start.2 = ((bf16[16,128,128]{2,1,0:T(8,128)(2,1)}), bf16[16,128,128]{2,1,0:T(8,128)(2,1)S(1)}, u32[]{:S(2)}, u32[]{:S(2)}) async-start(bf16[16,128,128]{2,1,0:T(8,128)(2,1)} %shard_map.111), calls=%async_computation.2 | async-start | bytes 1048576 | tf_op jit(solution)/shard_map/all_to_all | solution.py:626
  36.9 2.6 %collective-permute-start.1 = (f32[128,512]{1,0:T(8,128)S(1)}, f32[128,512]{1,0:T(8,128)S(1)}, u32[]{:S(2)}, u32[]{:S(2)}) collective-permute-start(f32[128,512]{1,0:T(8,128)S(1)} %shard_map.113), channel_id=1, source_target_pairs={{0,16},{8,24},{16,0},{24,8},{1,17},{9,25},{17,1},{25,9},{2,18},{10... | collective-permute-start | bytes 786440 | tf_op jit(solution)/shard_map/ppermute | solution.py:594
  39.5 9.5 %collective-permute-done.1.refs_3_ = f32[128,512]{1,0:T(8,128)S(1)} collective-permute-done((f32[128,512]{1,0:T(8,128)S(1)}, f32[128,512]{1,0:T(8,128)S(1)}, u32[]{:S(2)}, u32[]{:S(2)}) %collective-permute-start.1) | collective-permute-done | bytes 262176 | tf_op jit(solution)/shard_map/ppermute | solution.py:594
  49.8 3.5 %collective-permute-start.2 = (bf16[128,512]{1,0:T(8,128)(2,1)S(1)}, bf16[128,512]{1,0:T(8,128)(2,1)S(1)}, u32[]{:S(2)}, u32[]{:S(2)}) collective-permute-start(bf16[128,512]{1,0:T(8,128)(2,1)S(1)} %get-tuple-element.57.refs_1_), channel_id=1, source_target_pairs={{0,16},{8,24},{16,0},{24,8},{1,17},{9,25},{17,1},{25,9},{2,18},{10... | collective-permute-start | bytes 393224 | tf_op jit(solution)/shard_map/ppermute | solution.py:594
  53.3 3.4 %collective-permute-done.2.refs_2_ = bf16[128,512]{1,0:T(8,128)(2,1)S(1)} collective-permute-done((bf16[128,512]{1,0:T(8,128)(2,1)S(1)}, bf16[128,512]{1,0:T(8,128)(2,1)S(1)}, u32[]{:S(2)}, u32[]{:S(2)}) %collective-permute-start.2) | collective-permute-done | bytes 131104 | tf_op jit(solution)/shard_map/ppermute | solution.py:594
  59.9 7.1 %all-to-all-start.3 = ((bf16[16,128,128]{2,1,0:T(8,128)(2,1)}), bf16[16,128,128]{2,1,0:T(8,128)(2,1)}, u32[]{:S(2)}, u32[]{:S(2)}) async-start(bf16[16,128,128]{2,1,0:T(8,128)(2,1)} %shard_map.116), calls=%async_computation.3 | async-start | bytes 1048576 | tf_op jit(solution)/shard_map/all_to_all | solution.py:626
  70.0 3.2 %collective-permute-start.6 = (bf16[128,512]{1,0:T(8,128)(2,1)S(1)}, bf16[128,512]{1,0:T(8,128)(2,1)S(1)}, u32[]{:S(2)}, u32[]{:S(2)}) collective-permute-start(bf16[128,512]{1,0:T(8,128)(2,1)S(1)} %get-tuple-element.61), channel_id=1, source_target_pairs={{0,16},{8,24},{16,0},{24,8},{1,17},{9,25},{17,1},{25,9},{2,18},{10... | collective-permute-start | bytes 393224 | tf_op jit(solution)/shard_map/ppermute | solution.py:594
  73.2 4.1 %collective-permute-done.6.refs_2_ = bf16[128,512]{1,0:T(8,128)(2,1)S(1)} collective-permute-done((bf16[128,512]{1,0:T(8,128)(2,1)S(1)}, bf16[128,512]{1,0:T(8,128)(2,1)S(1)}, u32[]{:S(2)}, u32[]{:S(2)}) %collective-permute-start.6) | collective-permute-done | bytes 131104 | tf_op jit(solution)/shard_map/ppermute | solution.py:594
  77.4 2.7 %collective-permute-start.7 = (bf16[128,512]{1,0:T(8,128)(2,1)S(1)}, bf16[128,512]{1,0:T(8,128)(2,1)S(1)}, u32[]{:S(2)}, u32[]{:S(2)}) collective-permute-start(bf16[128,512]{1,0:T(8,128)(2,1)S(1)} %shard_map.117.refs_1_), channel_id=1, source_target_pairs={{0,16},{8,24},{16,0},{24,8},{1,17},{9,25},{17,1},{25,9},{2,18},{10... | collective-permute-start | bytes 393224 | tf_op jit(solution)/shard_map/ppermute | solution.py:594
  80.1 3.8 %collective-permute-done.7.refs_2_ = bf16[128,512]{1,0:T(8,128)(2,1)S(1)} collective-permute-done((bf16[128,512]{1,0:T(8,128)(2,1)S(1)}, bf16[128,512]{1,0:T(8,128)(2,1)S(1)}, u32[]{:S(2)}, u32[]{:S(2)}) %collective-permute-start.7) | collective-permute-done | bytes 131104 | tf_op jit(solution)/shard_map/ppermute | solution.py:594
  87.1 7.5 %all-to-all-start.4 = ((bf16[16,160,128]{2,1,0:T(8,128)(2,1)}), bf16[16,160,128]{2,1,0:T(8,128)(2,1)S(1)}, u32[]{:S(2)}, u32[]{:S(2)}) async-start(bf16[16,160,128]{2,1,0:T(8,128)(2,1)} %shard_map.119), calls=%async_computation.4 | async-start | bytes 1310720 | tf_op jit(solution)/shard_map/all_to_all | solution.py:626
  94.6 4.1 %shard_map.118 = (bf16[8,64,256]{2,1,0:T(8,128)(2,1)}, bf16[512,512]{1,0:T(8,128)(2,1)}, bf16[512,256]{1,0:T(8,128)(2,1)}, bf16[256,768]{1,0:T(8,128)(2,1)}) custom-call(bf16[8,64,256]{2,1,0:T(8,128)(2,1)} %refs_0_.9, bf16[8,64,256]{2,1,0:T(8,128)(2,1)} %refs_1_.8, bf16[256,1024]{1,0:T(8,128)(2,1)} %refs_1_.10, bf16[256,256]{1,0:T(8,128)(2,1)} %refs_3_.3, ...), custom_call_target="tpu_custom_call" | custom-call | flops 469762048 | bytes 3145728 | tf_op jit(solution)/shard_map/pallas_call | solution.py:577
  98.7 7.9 %all-to-all-done.4.refs_0_.refs_2_ = bf16[16,160,128]{2,1,0:T(8,128)(2,1)S(1)} async-done(((bf16[16,160,128]{2,1,0:T(8,128)(2,1)}), bf16[16,160,128]{2,1,0:T(8,128)(2,1)S(1)}, u32[]{:S(2)}, u32[]{:S(2)}) %all-to-all-start.4) | async-done | bytes 655392 | tf_op jit(solution)/shard_map/all_to_all | solution.py:626
  112.7 2.5 %collective-permute-start.13 = (bf16[32,1408]{1,0:T(8,128)(2,1)S(1)}, bf16[32,1408]{1,0:T(8,128)(2,1)S(1)}, u32[]{:S(2)}, u32[]{:S(2)}) collective-permute-start(bf16[32,1408]{1,0:T(8,128)(2,1)S(1)} %get-tuple-element.79), channel_id=1, source_target_pairs={{0,6},{1,7},{2,4},{3,5},{4,2},{5,3},{6,0},{7,1},{8,14},{9,15},{10,... | collective-permute-start | bytes 270344 | tf_op jit(solution)/shard_map/ppermute | solution.py:594
  115.2 4.3 %shard_map.124 = bf16[64,128,128]{2,1,0:T(8,128)(2,1)} custom-call(bf16[16,160,128]{2,1,0:T(8,128)(2,1)S(1)} %all-to-all-done.4.refs_0_.refs_2_, bf16[64,128,128]{2,1,0:T(8,128)(2,1)S(1)} %copy-done, f32[8,128]{1,0:T(8,128)S(1)} %bitcast.19, f32[8,64,128]{2,1,0:T(8,128)S(1)} %copy-done.5, f32[64,128]{1,0:T(8,128)S(1)} %copy-done.7, f32[64,128]{1,0:T(8,128)S(1)} %copy-done.8), custom_call_target="tpu_custom_call" | custom-call | flops 268435456 | bytes 5181440 | tf_op jit(solution)/shard_map/pallas_call | solution.py:577
  120.2 4.0 %collective-permute-done.14 = bf16[32,1408]{1,0:T(8,128)(2,1)S(1)} collective-permute-done((bf16[32,1408]{1,0:T(8,128)(2,1)S(1)}, bf16[32,1408]{1,0:T(8,128)(2,1)S(1)}, u32[]{:S(2)}, u32[]{:S(2)}) %collective-permute-start.14) | collective-permute-done | bytes 90144 | tf_op jit(solution)/shard_map/ppermute | solution.py:594
  124.2 3.1 %collective-permute-start.15 = (bf16[32,1408]{1,0:T(8,128)(2,1)S(1)}, bf16[32,1408]{1,0:T(8,128)(2,1)S(1)}, u32[]{:S(2)}, u32[]{:S(2)}) collective-permute-start(bf16[32,1408]{1,0:T(8,128)(2,1)S(1)} %add_convert_fusion.1), channel_id=1, source_target_pairs={{0,16},{8,24},{16,0},{24,8},{1,17},{9,25},{17,1},{25,9},{2,18},{10... | collective-permute-start | bytes 270344 | tf_op jit(solution)/shard_map/ppermute | solution.py:594
  130.7 9.3 %all-gather = bf16[256,1408]{1,0:T(8,128)(2,1)S(1)} all-gather(bf16[32,1408]{1,0:T(8,128)(2,1)S(1)} %add_convert_fusion), channel_id=2, replica_groups=mesh['seq'=4,'res'=8] {'res'}, dimensions={0}, use_global_device_ids=true | all-gather | bytes 811008 | tf_op jit(solution)/shard_map/all_gather | solution.py:759
  (65 shorter events, 25.3 us)
Async XLA Ops:
  3.3 16.9 %all-to-all-start = ((bf16[16,128,128]{2,1,0:T(8,128)(2,1)}), bf16[16,128,128]{2,1,0:T(8,128)(2,1)S(1)}, u32[]{:S(2)}, u32[]{:S(2)}) async-start(bf16[16,128,128]{2,1,0:T(8,128)(2,1)} %shard_map.109), calls=%async_computation | async-start | bytes 1048576 | tf_op jit(solution)/shard_map/all_to_all | solution.py:626
  20.1 4.9 %collective-permute-start = (bf16[16,128,128]{2,1,0:T(8,128)(2,1)S(1)}, bf16[16,128,128]{2,1,0:T(8,128)(2,1)S(1)}, u32[]{:S(2)}, u32[]{:S(2)}) collective-permute-start(bf16[16,128,128]{2,1,0:T(8,128)(2,1)S(1)} %all-to-all-done.refs_1_.refs_5_), channel_id=1, source_target_pairs={{0,1},{1,0},{2,3},{3,2},{4,5},{5,4},{6,7},{7,6},{8,9},{9,8},{10,11... | collective-permute-start | bytes 1572872 | tf_op jit(solution)/shard_map/ppermute | solution.py:594
  20.1 12.5 %all-to-all-start.1 = ((bf16[16,64,128]{2,1,0:T(8,128)(2,1)}), bf16[16,64,128]{2,1,0:T(8,128)(2,1)S(1)}, u32[]{:S(2)}, u32[]{:S(2)}) async-start(bf16[16,64,128]{2,1,0:T(8,128)(2,1)} %get-tuple-element.49), calls=%async_computation.1 | async-start | bytes 524288 | tf_op jit(solution)/shard_map/all_to_all | solution.py:626
  33.3 23.5 %all-to-all-start.2 = ((bf16[16,128,128]{2,1,0:T(8,128)(2,1)}), bf16[16,128,128]{2,1,0:T(8,128)(2,1)S(1)}, u32[]{:S(2)}, u32[]{:S(2)}) async-start(bf16[16,128,128]{2,1,0:T(8,128)(2,1)} %shard_map.111), calls=%async_computation.2 | async-start | bytes 1048576 | tf_op jit(solution)/shard_map/all_to_all | solution.py:626
  36.9 12.2 %collective-permute-start.1 = (f32[128,512]{1,0:T(8,128)S(1)}, f32[128,512]{1,0:T(8,128)S(1)}, u32[]{:S(2)}, u32[]{:S(2)}) collective-permute-start(f32[128,512]{1,0:T(8,128)S(1)} %shard_map.113), channel_id=1, source_target_pairs={{0,16},{8,24},{16,0},{24,8},{1,17},{9,25},{17,1},{25,9},{2,18},{10... | collective-permute-start | bytes 786440 | tf_op jit(solution)/shard_map/ppermute | solution.py:594
  49.8 6.9 %collective-permute-start.2 = (bf16[128,512]{1,0:T(8,128)(2,1)S(1)}, bf16[128,512]{1,0:T(8,128)(2,1)S(1)}, u32[]{:S(2)}, u32[]{:S(2)}) collective-permute-start(bf16[128,512]{1,0:T(8,128)(2,1)S(1)} %get-tuple-element.57.refs_1_), channel_id=1, source_target_pairs={{0,16},{8,24},{16,0},{24,8},{1,17},{9,25},{17,1},{25,9},{2,18},{10... | collective-permute-start | bytes 393224 | tf_op jit(solution)/shard_map/ppermute | solution.py:594
  53.3 3.4 %collective-permute-start.4 = (bf16[128,512]{1,0:T(8,128)(2,1)S(1)}, bf16[128,512]{1,0:T(8,128)(2,1)S(1)}, u32[]{:S(2)}, u32[]{:S(2)}) collective-permute-start(bf16[128,512]{1,0:T(8,128)(2,1)S(1)} %get-tuple-element.57.refs_1_), channel_id=1, source_target_pairs={{0,1},{1,0},{2,3},{3,2},{4,5},{5,4},{6,7},{7,6},{8,9},{9,8},{10,11... | collective-permute-start | bytes 393224 | tf_op jit(solution)/shard_map/ppermute | solution.py:594
  56.7 1.3 collective-permute-start.5
  59.9 25.3 %all-to-all-start.3 = ((bf16[16,128,128]{2,1,0:T(8,128)(2,1)}), bf16[16,128,128]{2,1,0:T(8,128)(2,1)}, u32[]{:S(2)}, u32[]{:S(2)}) async-start(bf16[16,128,128]{2,1,0:T(8,128)(2,1)} %shard_map.116), calls=%async_computation.3 | async-start | bytes 1048576 | tf_op jit(solution)/shard_map/all_to_all | solution.py:626
  67.0 2.0 %collective-permute-start.3 = (bf16[16,128,128]{2,1,0:T(8,128)(2,1)S(1)}, bf16[16,128,128]{2,1,0:T(8,128)(2,1)S(1)}, u32[]{:S(2)}, u32[]{:S(2)}) collective-permute-start(bf16[16,128,128]{2,1,0:T(8,128)(2,1)S(1)} %all-to-all-done.2.refs_1_.refs_5_), channel_id=1, source_target_pairs={{0,1},{1,0},{2,3},{3,2},{4,5},{5,4},{6,7},{7,6},{8,9},{9,8},{10,11... | collective-permute-start | bytes 1572872 | tf_op jit(solution)/shard_map/ppermute | solution.py:594
  70.0 7.3 %collective-permute-start.6 = (bf16[128,512]{1,0:T(8,128)(2,1)S(1)}, bf16[128,512]{1,0:T(8,128)(2,1)S(1)}, u32[]{:S(2)}, u32[]{:S(2)}) collective-permute-start(bf16[128,512]{1,0:T(8,128)(2,1)S(1)} %get-tuple-element.61), channel_id=1, source_target_pairs={{0,16},{8,24},{16,0},{24,8},{1,17},{9,25},{17,1},{25,9},{2,18},{10... | collective-permute-start | bytes 393224 | tf_op jit(solution)/shard_map/ppermute | solution.py:594
  77.4 29.2 %copy-start = (bf16[64,128,128]{2,1,0:T(8,128)(2,1)S(1)}, bf16[64,128,128]{2,1,0:T(8,128)(2,1)}, u32[]{:S(2)}) copy-start(bf16[64,128,128]{2,1,0:T(8,128)(2,1)} %refs_1_.11) | copy-start | bytes 6291460
  77.4 29.2 %copy-start.7 = (f32[64,128]{1,0:T(8,128)S(1)}, f32[64,128]{1,0:T(8,128)}, u32[]{:S(2)}) copy-start(f32[64,128]{1,0:T(8,128)} %get-tuple-element.70.refs_2_.refs_4_) | copy-start | bytes 98308
  77.4 29.2 %copy-start.8 = (f32[64,128]{1,0:T(8,128)S(1)}, f32[64,128]{1,0:T(8,128)}, u32[]{:S(2)}) copy-start(f32[64,128]{1,0:T(8,128)} %get-tuple-element.71.refs_3_.refs_5_) | copy-start | bytes 98308
  77.4 6.5 %collective-permute-start.7 = (bf16[128,512]{1,0:T(8,128)(2,1)S(1)}, bf16[128,512]{1,0:T(8,128)(2,1)S(1)}, u32[]{:S(2)}, u32[]{:S(2)}) collective-permute-start(bf16[128,512]{1,0:T(8,128)(2,1)S(1)} %shard_map.117.refs_1_), channel_id=1, source_target_pairs={{0,16},{8,24},{16,0},{24,8},{1,17},{9,25},{17,1},{25,9},{2,18},{10... | collective-permute-start | bytes 393224 | tf_op jit(solution)/shard_map/ppermute | solution.py:594
  80.1 3.8 %collective-permute-start.8 = (bf16[128,512]{1,0:T(8,128)(2,1)S(1)}, bf16[128,512]{1,0:T(8,128)(2,1)S(1)}, u32[]{:S(2)}, u32[]{:S(2)}) collective-permute-start(bf16[128,512]{1,0:T(8,128)(2,1)S(1)} %shard_map.117.refs_1_), channel_id=1, source_target_pairs={{0,1},{1,0},{2,3},{3,2},{4,5},{5,4},{6,7},{7,6},{8,9},{9,8},{10,11... | collective-permute-start | bytes 393224 | tf_op jit(solution)/shard_map/ppermute | solution.py:594
  83.9 1.3 collective-permute-start.9
  87.1 19.4 %all-to-all-start.4 = ((bf16[16,160,128]{2,1,0:T(8,128)(2,1)}), bf16[16,160,128]{2,1,0:T(8,128)(2,1)S(1)}, u32[]{:S(2)}, u32[]{:S(2)}) async-start(bf16[16,160,128]{2,1,0:T(8,128)(2,1)} %shard_map.119), calls=%async_computation.4 | async-start | bytes 1310720 | tf_op jit(solution)/shard_map/all_to_all | solution.py:626
  109.2 1.7 %collective-permute-start.10 = (bf16[4,32,1408]{2,1,0:T(8,128)(2,1)S(1)}, bf16[4,32,1408]{2,1,0:T(8,128)(2,1)S(1)}, u32[]{:S(2)}, u32[]{:S(2)}) collective-permute-start(bf16[4,32,1408]{2,1,0:T(8,128)(2,1)S(1)} %get-tuple-element.76), channel_id=1, source_target_pairs={{0,1},{1,0},{2,3},{3,2},{4,5},{5,4},{6,7},{7,6},{8,9},{9,8},{10,11... | collective-permute-start | bytes 1081352 | tf_op jit(solution)/shard_map/ppermute | solution.py:594
  111.6 7.9 %collective-permute-start.11 = (bf16[32,1408]{1,0:T(8,128)(2,1)S(1)}, bf16[32,1408]{1,0:T(8,128)(2,1)S(1)}, u32[]{:S(2)}, u32[]{:S(2)}) collective-permute-start(bf16[32,1408]{1,0:T(8,128)(2,1)S(1)} %get-tuple-element.77), channel_id=1, source_target_pairs={{0,2},{1,3},{2,0},{3,1},{4,6},{5,7},{6,4},{7,5},{8,10},{9,11},{10,... | collective-permute-start | bytes 270344 | tf_op jit(solution)/shard_map/ppermute | solution.py:594
  111.7 7.8 %collective-permute-start.12 = (bf16[32,1408]{1,0:T(8,128)(2,1)S(1)}, bf16[32,1408]{1,0:T(8,128)(2,1)S(1)}, u32[]{:S(2)}, u32[]{:S(2)}) collective-permute-start(bf16[32,1408]{1,0:T(8,128)(2,1)S(1)} %get-tuple-element.78), channel_id=1, source_target_pairs={{0,4},{1,5},{2,6},{3,7},{4,0},{5,1},{6,2},{7,3},{8,12},{9,13},{10,... | collective-permute-start | bytes 270344 | tf_op jit(solution)/shard_map/ppermute | solution.py:594
  112.7 6.8 %collective-permute-start.13 = (bf16[32,1408]{1,0:T(8,128)(2,1)S(1)}, bf16[32,1408]{1,0:T(8,128)(2,1)S(1)}, u32[]{:S(2)}, u32[]{:S(2)}) collective-permute-start(bf16[32,1408]{1,0:T(8,128)(2,1)S(1)} %get-tuple-element.79), channel_id=1, source_target_pairs={{0,6},{1,7},{2,4},{3,5},{4,2},{5,3},{6,0},{7,1},{8,14},{9,15},{10,... | collective-permute-start | bytes 270344 | tf_op jit(solution)/shard_map/ppermute | solution.py:594
  119.6 4.6 %collective-permute-start.14 = (bf16[32,1408]{1,0:T(8,128)(2,1)S(1)}, bf16[32,1408]{1,0:T(8,128)(2,1)S(1)}, u32[]{:S(2)}, u32[]{:S(2)}) collective-permute-start(bf16[32,1408]{1,0:T(8,128)(2,1)S(1)} %shard_map.125), channel_id=1, source_target_pairs={{0,8},{8,0},{16,24},{24,16},{1,9},{9,1},{17,25},{25,17},{2,10},{10... | collective-permute-start | bytes 270344 | tf_op jit(solution)/shard_map/ppermute | solution.py:594
  124.2 6.5 %collective-permute-start.15 = (bf16[32,1408]{1,0:T(8,128)(2,1)S(1)}, bf16[32,1408]{1,0:T(8,128)(2,1)S(1)}, u32[]{:S(2)}, u32[]{:S(2)}) collective-permute-start(bf16[32,1408]{1,0:T(8,128)(2,1)S(1)} %add_convert_fusion.1), channel_id=1, source_target_pairs={{0,16},{8,24},{16,0},{24,8},{1,17},{9,25},{17,1},{25,9},{2,18},{10... | collective-permute-start | bytes 270344 | tf_op jit(solution)/shard_map/ppermute | solution.py:594
  (7 other events, 72.3 us)

commit v11 on v9

--- a/solution.py
+++ b/solution.py
@@ -327,17 +327,12 @@
                     ref[k * part : (k + 1) * part, columns] += bias
 
 
-def softmax_kernel(logit_ref, other_ref, out_ref, low_ref):
-    logits = logit_ref[...] + other_ref[...]
+def softmax_kernel(logit_ref, logit_other_ref, grad_ref, grad_other_ref, out_ref, low_ref):
+    logits = logit_ref[...] + logit_other_ref[...]
     lifted = jnp.exp(logits - jnp.max(logits, axis=-1, keepdims=True))
     softmax_out = lifted / jnp.sum(lifted, axis=-1, keepdims=True)
-    out_ref[...] = softmax_out
     low_ref[...] = softmax_out.astype(jnp.bfloat16)
-
-
-def softmax_gradient_kernel(softmax_ref, grad_ref, other_ref, out_ref):
-    softmax_out = softmax_ref[...]
-    grad_probs = grad_ref[...] + other_ref[...].astype(jnp.float32)
+    grad_probs = grad_ref[...] + grad_other_ref[...].astype(jnp.float32)
     row_dot = jnp.sum(softmax_out * grad_probs, axis=-1, keepdims=True)
     out_ref[...] = (softmax_out * (grad_probs - row_dot)).astype(jnp.bfloat16)
 
@@ -386,13 +381,33 @@
     )
 
 
+def query_weight_kernel(x_ref, blocks_ref, pair_weight_ref, projected_ref, sums_ref):
+    residues, width = x_ref.shape[1], x_ref.shape[2]
+    tiles = width // LANES
+    normed = normalized(x_ref)[0].astype(jnp.bfloat16)
+    for t in range(2):
+        projected_ref[:, t * width : (t + 1) * width] = unpack_heads(
+            blocks_ref, t * residues, residues, tiles
+        ).astype(jnp.bfloat16)
+    sums_ref[:, : 2 * width] = f32_dot(normed, projected_ref[...], TN).astype(jnp.bfloat16)
+    heads, channels = pair_weight_ref.shape
+    rows = sums_ref.shape[0] // heads
+    first = lax.broadcasted_iota(jnp.int32, (rows, channels), 0) == 0
+    for h in range(heads):
+        row = jnp.broadcast_to(pair_weight_ref[h : h + 1], (rows, channels))
+        sums_ref[h * rows : (h + 1) * rows, 2 * width :] = jnp.where(first, row, 0.0).astype(
+            jnp.bfloat16
+        )
+
+
 def attended_weight_kernel(
-    x_ref, grad_ref, wc_ref, wo_ref, blocks_ref, updated_ref, projected_ref, normed_ref, sums_ref
+    place_ref, x_ref, grad_ref, wc_ref, wo_ref, query_sums_ref, blocks_ref,
+    updated_ref, projected_ref, keep_ref, send_ref, sums_ref,
 ):
     residues, width = x_ref.shape[1], x_ref.shape[2]
     tiles = width // LANES
+    core = place_ref[0]
     normed = normalized(x_ref)[0].astype(jnp.bfloat16)
-    normed_ref[...] = normed
     gate = gate_of(f32_dot(normed, wc_ref[:, 3 * width :]))
     grad = grad_ref[...].reshape(-1, width)
     grad_gated = f32_dot(grad, wo_ref[...], NT)
@@ -404,34 +419,11 @@
     )
     projected_ref[:, width:] = (grad_gated * attended * gate * (1.0 - gate)).astype(jnp.bfloat16)
     sums_ref[:, : 2 * width] = f32_dot(normed, projected_ref[...], TN).astype(jnp.bfloat16)
-    sums_ref[:, 2 * width :] = f32_dot(gated, grad, TN).astype(jnp.bfloat16)
-
-
-def query_weight_kernel(
-    place_ref, normed_ref, blocks_ref, pair_weight_ref, attended_sums_ref,
-    projected_ref, keep_ref, send_ref, sums_ref,
-):
-    width = normed_ref.shape[1]
-    tiles, residues = width // LANES, (blocks_ref.shape[1] * 2) // 5
-    core = place_ref[0]
-    for t in range(2):
-        projected_ref[:, t * width : (t + 1) * width] = unpack_heads(
-            blocks_ref, t * residues, residues, tiles
-        ).astype(jnp.bfloat16)
-    sums_ref[:, : 2 * width] = f32_dot(normed_ref[...], projected_ref[...], TN).astype(
-        jnp.bfloat16
-    )
-    sums_ref[:, 2 * width : 5 * width] = attended_sums_ref[...]
-    heads, channels = pair_weight_ref.shape
-    rows = sums_ref.shape[0] // heads
-    first = lax.broadcasted_iota(jnp.int32, (rows, channels), 0) == 0
-    for h in range(heads):
-        row = jnp.broadcast_to(pair_weight_ref[h : h + 1], (rows, channels))
-        sums_ref[h * rows : (h + 1) * rows, 5 * width :] = jnp.where(first, row, 0.0).astype(
-            jnp.bfloat16
-        )
+    sums_ref[:, 2 * width : 3 * width] = f32_dot(gated, grad, TN).astype(jnp.bfloat16)
+    sums_ref[:, 3 * width :] = query_sums_ref[...]
+    rows = keep_ref.shape[1]
     for which, ref in ((core, keep_ref), (1 - core, send_ref)):
-        for block in range(heads // 2):
+        for block in range(keep_ref.shape[0]):
             start = pl.multiple_of((2 * block + which) * rows, rows)
             ref[block] = sums_ref[pl.ds(start, rows), :]
 
@@ -532,6 +524,18 @@
     lax.fori_loop(0, pair_ref.shape[0] // 8, rows, 0)
 
 
+def output_kernel(parts_ref, combined_ref, out_weight_ref, pair_weight_ref):
+    width = combined_ref.shape[0]
+    rows = parts_ref.shape[1]
+    for h in range(parts_ref.shape[0]):
+        block = slice(h * rows, (h + 1) * rows)
+        part = parts_ref[h].astype(jnp.float32)
+        combined_ref[block, 2 * width :] = part[:, : 2 * width]
+        out_weight_ref[block, :] = part[:, 2 * width : 3 * width]
+        combined_ref[block, : 2 * width] = part[:, 3 * width : 5 * width]
+        pair_weight_ref[h : h + 1, :] = part[:1, 5 * width :]
+
+
 def call(kernel, outs, *args, scratch=(), place=None, flops=0, after=(), outside=0, late=0):
     whole, anywhere = pl.BlockSpec(memory_space=pltpu.VMEM), pl.BlockSpec(memory_space=pl.ANY)
     specs = [anywhere] * outside + [whole] * (len(args) - outside)
@@ -616,6 +620,11 @@
         return lax.all_to_all(blocks, ("seq", "res"), 0, 0, axis_index_groups=groups, tiled=True)
 
     x, grad, wc, wo = alignment_rows, updated_gradient, combined_weight, output_weight
+    (value_blocks,) = call(
+        value_kernel, [((group, 2 * residues, LANES), bf16)], x, grad, wc, wo,
+        flops=8 * tokens * width * width, outside=4,
+    )
+    value_blocks = across(value_blocks)
     query_blocks, bias, mean, spread = call(
         functools.partial(query_kernel, scale),
         [
@@ -627,7 +636,9 @@
         x, wc, pair_entries, pair_weight.T,
         flops=8 * tokens * width * width, outside=3, late=1,
     )
+    value_blocks, query_blocks = lax.optimization_barrier((value_blocks, query_blocks))
     query_blocks = across(query_blocks)
+
     def scores(blocks, left_row, right_row, with_bias, kind):
         return call(
             functools.partial(score_kernel, residues, left_row, right_row, with_bias),
@@ -636,110 +647,102 @@
             place=place, flops=2 * total * total * width,
         )
 
-    (value_blocks,) = call(
-        value_kernel, [((group, 2 * residues, LANES), bf16)], x, grad, wc, wo,
-        flops=8 * tokens * width * width, outside=4,
-    )
-    logit_mine, logit_sent = scores(query_blocks, 0, residues, True, f32)
-    value_blocks, logit_sent = lax.optimization_barrier((value_blocks, logit_sent))
-    logit_other = swapped(logit_sent, "seq", seq_half)
-    value_blocks = across(value_blocks)
-    quarter = (total // 4, total)
-    softmax_out, probs = call(
-        softmax_kernel, [(quarter, f32), (quarter, bf16)], logit_mine, logit_other,
-        flops=total * total,
-    )
-    probs_far = swapped(probs, "seq", seq_half)
-    value_blocks, probs_far = lax.optimization_barrier((value_blocks, probs_far))
     grad_mine, grad_sent = scores(value_blocks, residues, 0, False, bf16)
     grad_other = swapped(grad_sent, "seq", seq_half)
-
-    def products(quarters, blocks, first_row, second_row, with_share, factor):
+    query_blocks, grad_other = lax.optimization_barrier((query_blocks, grad_other))
+    logit_mine, logit_sent = scores(query_blocks, 0, residues, True, f32)
+    quarter = ((total // 4, total), bf16)
+    grad_logits, probs = call(
+        softmax_kernel, [quarter, quarter],
+        logit_mine, swapped(logit_sent, "seq", seq_half), grad_mine, grad_other,
+        flops=total * total,
+    )
+
+    def products(mine, far, blocks, first_row, second_row, with_share, factor):
         rows = 2 * residues + (residues // 2 if with_share else 0)
         (out,) = call(
             functools.partial(
                 product_kernel, residues, factor, first_row, second_row, with_share
             ),
             [((group, rows, LANES), bf16)],
-            *quarters, blocks,
+            mine, far, swapped(mine, "res", 1), swapped(far, "res", 1), blocks,
             scratch=[pltpu.VMEM((total, total), bf16)],
             place=place, flops=4 * total * total * width,
         )
         return out
 
-    def with_near(mine, far):
-        return mine, far, swapped(mine, "res", 1), swapped(far, "res", 1)
-
-    attended = products(with_near(probs, probs_far), value_blocks, 0, residues, False, 1.0)
-    attended, grad_other = lax.optimization_barrier((attended, grad_other))
+    grad_far = swapped(grad_logits, "seq", seq_half)
+    grad_far, probs = lax.optimization_barrier((grad_far, probs))
+    grad_blocks = across(
+        products(grad_logits, grad_far, query_blocks, residues, 0, True, scale)
+    )
+    attended = products(
+        probs, swapped(probs, "seq", seq_half), value_blocks, 0, residues, False, 1.0
+    )
+    grad_blocks, attended = lax.optimization_barrier((grad_blocks, attended))
     attended_blocks = across(attended)
-    (grad_logits,) = call(
-        softmax_gradient_kernel, [(quarter, bf16)], softmax_out, grad_mine, grad_other,
-        flops=total * total,
-    )
-    grad_quarters = with_near(grad_logits, swapped(grad_logits, "seq", seq_half))
-    grad_quarters, attended_blocks = lax.optimization_barrier((grad_quarters, attended_blocks))
-    grad_blocks = across(products(grad_quarters, query_blocks, residues, 0, True, scale))
-
-    updated, value_gate, normed, attended_sums = call(
-        attended_weight_kernel,
-        [
-            (x.shape, bf16),
-            ((tokens, 2 * width), bf16),
-            ((tokens, width), bf16),
-            ((width, 3 * width), bf16),
-        ],
-        x, grad, wc, wo, attended_blocks,
-        flops=14 * tokens * width * width, outside=4,
-    )
+
     share = pltpu.VMEM((heads, residues, LANES), f32)
     (pair_weight_part,) = call(
         pair_weight_kernel, [((heads, channels), f32)],
         grad_blocks, pair_entries, mean, spread,
         scratch=[share], flops=4 * tokens * width * width,
     )
-    columns = 5 * width + channels
-    rows = width // res_size
-    part_rows = ((res_size // 2, rows, columns), bf16)
-    query_key, keep, send = call(
+    query_key, query_sums = call(
         query_weight_kernel,
-        [((tokens, 2 * width), bf16), part_rows, part_rows],
-        normed, grad_blocks, pair_weight_part, attended_sums,
-        scratch=[pltpu.VMEM((width, columns), bf16)],
-        place=place, flops=4 * tokens * width * width,
-    )
-    own, *sent = call(
-        core_sum_kernel,
-        [((rows, columns), f32)] + [((rows, columns), bf16)] * 3,
-        keep, swapped(send, "res", 1), place=place,
-    )
-    received = [swapped(t, "res", 2 * flip) for flip, t in enumerate(sent, 1)]
+        [((tokens, 2 * width), bf16), ((width, 2 * width + channels), bf16)],
+        x, grad_blocks, pair_weight_part,
+        flops=4 * tokens * width * width, outside=1,
+    )
     (pair_gradient,) = call(
         functools.partial(pair_kernel, 2 * residues),
         [(pair_entries.shape, bf16)],
         grad_blocks, pair_entries, pair_weight.T, bias, mean, spread,
         scratch=[share], flops=8 * tokens * width * width,
     )
-    received, pair_gradient = lax.optimization_barrier((received, pair_gradient))
-    (part,) = call(plane_sum_kernel, [((rows, columns), bf16)], own, *received)
+    attended_blocks, query_sums, pair_gradient = lax.optimization_barrier(
+        (attended_blocks, query_sums, pair_gradient)
+    )
+    columns = 5 * width + channels
+    rows = width // res_size
+    part_rows = ((res_size // 2, rows, columns), bf16)
+    updated, value_gate, keep, send = call(
+        attended_weight_kernel,
+        [(x.shape, bf16), ((tokens, 2 * width), bf16), part_rows, part_rows],
+        x, grad, wc, wo, query_sums, attended_blocks,
+        scratch=[pltpu.VMEM((width, columns), bf16)],
+        place=place, flops=14 * tokens * width * width, outside=5,
+    )
+    own, *sent = call(
+        core_sum_kernel,
+        [((rows, columns), f32)] + [((rows, columns), bf16)] * 3,
+        keep, swapped(send, "res", 1), place=place,
+    )
+    received = [swapped(t, "res", 2 * flip) for flip, t in enumerate(sent, 1)]
     (alignment_gradient,) = call(
         alignment_kernel, [(x.shape, bf16)], x, wc, query_key, value_gate,
-        flops=8 * tokens * width * width,
-    )
+        flops=8 * tokens * width * width, outside=4,
+    )
+    received, alignment_gradient = lax.optimization_barrier((received, alignment_gradient))
+    (part,) = call(plane_sum_kernel, [((rows, columns), bf16)], own, *received)
 
     def added(mine, other):
         return (mine.astype(f32) + other.astype(f32)).astype(bf16)
 
     part = added(part, swapped(part, "seq", 1))
     part = added(part, swapped(part, "seq", seq_half))
-    whole = lax.all_gather(part, "res", axis=0)
+    combined_gradient, output_gradient, pair_weight_gradient = call(
+        output_kernel,
+        [(wc.shape, f32), (wo.shape, f32), ((heads, channels), f32)],
+        lax.all_gather(part, "res", axis=0),
+    )
     return (
         updated,
         alignment_gradient,
         pair_gradient,
-        whole[:, :, : 4 * width].reshape(wc.shape).astype(f32),
-        whole[:, :, 4 * width : 5 * width].reshape(wo.shape).astype(f32),
-        whole[:, 0, 5 * width :].T.astype(f32),
+        combined_gradient,
+        output_gradient,
+        pair_weight_gradient.T,
     )
 
 

time: 141 us -> 143 us (1.014)
  blocking collectives: 28.9 us -> 9.8 us
  waiting for transfers between devices: 45.3 us -> 63.6 us
  local copies, waits for them, and re-layouts: 0.17 us -> 4.34 us
  Pallas kernels: 29.8 us -> 33.2 us
  starting transfers between devices: 33 us -> 30.3 us
  other arithmetic: 2.57 us -> 0.12 us
    ppermute x16, waiting for transfers between devices: 34.7 us -> 56.3 us  [swapped(): lax.ppermute(mine, axis_name, [(a, a ^ distance) for a in range(size)])]
    all_to_all x1 -> x0, blocking collectives: 19.7 us -> none  [across(): lax.all_to_all(blocks, ('seq', 'res'), 0, 0, axis_index_groups=groups, ti...]
    ppermute x16, starting transfers between devices: 16.7 us -> 11.2 us  [swapped(): lax.ppermute(mine, axis_name, [(a, a ^ distance) for a in range(size)])]
    unnamed x20 -> x26, local copies, waits for them, and re-layouts: 0.1 us -> 4.34 us
    pallas_call x15, Pallas kernels: 29.8 us -> 33.2 us  [call(): pl.pallas_call(wrapped, out_shape=shapes, in_specs=[pl.BlockSpec(memory_s...]
    all_to_all x3 -> x4, waiting for transfers between devices: 10.5 us -> 7.3 us  [across(): lax.all_to_all(blocks, ('seq', 'res'), 0, 0, axis_index_groups=groups, ti...]
    all_to_all x3 -> x4, starting transfers between devices: 16.4 us -> 19.1 us  [across(): lax.all_to_all(blocks, ('seq', 'res'), 0, 0, axis_index_groups=groups, ti...]
    convert_element_type x3 -> x0, other arithmetic: 2.45 us -> none  [the longest x1 1.12 us: head_body(): whole[:, :, :4 * width].reshape(wc.shape).astype(f32)]
  transfers between devices with their start and end apart: 19 -> 20, of which waited for: 11 -> 16; matrix products, arithmetic and copies ran while one was open for 0% -> 0% of each run, Pallas kernels for 11% -> 16%
where the time goes in v11:
time: 143 us; the launch traced here: 142 us
  waiting for transfers between devices  63.6 us (44%)
  Pallas kernels  33.2 us (23%)
  starting transfers between devices  30.3 us (21%)
  blocking collectives  9.8 us (7%)
  local copies, waits for them, and re-layouts  4.34 us (3%)
    ppermute x16, waiting for transfers between devices, swapped(): lax.ppermute(mine, axis_name, [(a, a ^ distance) for a in range(size)])  56.3 us
    pallas_call x15, Pallas kernels, call(): pl.pallas_call(wrapped, out_shape=shapes, in_specs=[pl.BlockSpec(memory_s...  33.2 us
    all_to_all x4, starting transfers between devices, across(): lax.all_to_all(blocks, ('seq', 'res'), 0, 0, axis_index_groups=groups, ti...  19.1 us
    ppermute x16, starting transfers between devices, swapped(): lax.ppermute(mine, axis_name, [(a, a ^ distance) for a in range(size)])  11.2 us
    all_gather x1, blocking collectives, head_body(): lax.all_gather(part, 'res', axis=0)  9.8 us
    all_to_all x4, waiting for transfers between devices, across(): lax.all_to_all(blocks, ('seq', 'res'), 0, 0, axis_index_groups=groups, ti...  7.3 us
    unnamed x26, local copies, waits for them, and re-layouts  4.34 us
  transfers between devices with their start and end apart: 20, of which 16 were waited for; matrix products, arithmetic and copies ran while one was open for 0% of the time, Pallas kernels for 16%

profile of v11, /device:TPU:0, one launch (start us, length us, event | category | flops | bytes accessed | tf_op | source)
XLA Modules:
  0.0 142.3 jit_solution(13282262424336418256)
XLA Ops:
  0.6 2.7 %shard_map.109 = bf16[16,128,128]{2,1,0:T(8,128)(2,1)} custom-call(bf16[8,64,256]{2,1,0:T(8,128)(2,1)} %refs_0_.7, bf16[8,64,256]{2,1,0:T(8,128)(2,1)} %refs_2_.5, bf16[256,1024]{1,0:T(8,128)(2,1)} %refs_1_.11, bf16[256,256]{1,0:T(8,128)(2,1)} %refs_4_.1), custom_call_target="tpu_custom_call" | custom-call | flops 268435456 | bytes 1703936 | tf_op jit(solution)/shard_map/pallas_call | solution.py:571
  3.4 6.3 %all-to-all-start = ((bf16[16,128,128]{2,1,0:T(8,128)(2,1)}), bf16[16,128,128]{2,1,0:T(8,128)(2,1)S(1)}, u32[]{:S(2)}, u32[]{:S(2)}) async-start(bf16[16,128,128]{2,1,0:T(8,128)(2,1)} %shard_map.109), calls=%async_computation | async-start | bytes 1048576 | tf_op jit(solution)/shard_map/all_to_all | solution.py:620
  9.7 8.1 %shard_map.110 = (bf16[16,192,128]{2,1,0:T(8,128)(2,1)}, f32[8,64,128]{2,1,0:T(8,128)}, f32[64,128]{1,0:T(8,128)}, f32[64,128]{1,0:T(8,128)}) custom-call(bf16[8,64,256]{2,1,0:T(8,128)(2,1)} %refs_0_.7, bf16[256,1024]{1,0:T(8,128)(2,1)} %refs_1_.11, bf16[64,128,128]{2,1,0:T(8,128)(2,1)} %refs_1_.9, f32[8,128]{1,0:T(8,128)} %bitcast.7), custom_call_target="tpu_custom_call" | custom-call | flops 268435456 | bytes 4001792 | tf_op jit(solution)/shard_map/pallas_call | solution.py:571
  17.7 2.5 %all-to-all-done.refs_1_.refs_5_ = bf16[16,128,128]{2,1,0:T(8,128)(2,1)S(1)} async-done(((bf16[16,128,128]{2,1,0:T(8,128)(2,1)}), bf16[16,128,128]{2,1,0:T(8,128)(2,1)S(1)}, u32[]{:S(2)}, u32[]{:S(2)}) %all-to-all-start) | async-done | bytes 524320 | tf_op jit(solution)/shard_map/all_to_all | solution.py:620
  20.2 3.6 %all-to-all-start.1 = ((bf16[16,192,128]{2,1,0:T(8,128)(2,1)}), bf16[16,192,128]{2,1,0:T(8,128)(2,1)S(1)}, u32[]{:S(2)}, u32[]{:S(2)}) async-start(bf16[16,192,128]{2,1,0:T(8,128)(2,1)} %get-tuple-element.45), calls=%async_computation.1 | async-start | bytes 1572864 | tf_op jit(solution)/shard_map/all_to_all | solution.py:620
  24.2 1.6 %collective-permute-done.refs_2_ = bf16[16,128,128]{2,1,0:T(8,128)(2,1)S(1)} collective-permute-done((bf16[16,128,128]{2,1,0:T(8,128)(2,1)S(1)}, bf16[16,128,128]{2,1,0:T(8,128)(2,1)S(1)}, u32[]{:S(2)}, u32[]{:S(2)}) %collective-permute-start) | collective-permute-done | bytes 524320 | tf_op jit(solution)/shard_map/ppermute | solution.py:588
  26.8 2.7 %collective-permute-start.1 = (bf16[128,512]{1,0:T(8,128)(2,1)S(1)}, bf16[128,512]{1,0:T(8,128)(2,1)S(1)}, u32[]{:S(2)}, u32[]{:S(2)}) collective-permute-start(bf16[128,512]{1,0:T(8,128)(2,1)S(1)} %get-tuple-element.47), channel_id=1, source_target_pairs={{0,16},{8,24},{16,0},{24,8},{1,17},{9,25},{17,1},{25,9},{2,18},{10... | collective-permute-start | bytes 393224 | tf_op jit(solution)/shard_map/ppermute | solution.py:588
  29.5 6.5 %collective-permute-done.1.refs_3_ = bf16[128,512]{1,0:T(8,128)(2,1)S(1)} collective-permute-done((bf16[128,512]{1,0:T(8,128)(2,1)S(1)}, bf16[128,512]{1,0:T(8,128)(2,1)S(1)}, u32[]{:S(2)}, u32[]{:S(2)}) %collective-permute-start.1) | collective-permute-done | bytes 131104 | tf_op jit(solution)/shard_map/ppermute | solution.py:588
  36.0 4.0 %all-to-all-done.1.refs_1_.refs_5_ = bf16[16,192,128]{2,1,0:T(8,128)(2,1)S(1)} async-done(((bf16[16,192,128]{2,1,0:T(8,128)(2,1)}), bf16[16,192,128]{2,1,0:T(8,128)(2,1)S(1)}, u32[]{:S(2)}, u32[]{:S(2)}) %all-to-all-start.1) | async-done | bytes 786464 | tf_op jit(solution)/shard_map/all_to_all | solution.py:620
  40.0 2.3 %collective-permute-done.2.refs_2_ = bf16[16,192,128]{2,1,0:T(8,128)(2,1)S(1)} collective-permute-done((bf16[16,192,128]{2,1,0:T(8,128)(2,1)S(1)}, bf16[16,192,128]{2,1,0:T(8,128)(2,1)S(1)}, u32[]{:S(2)}, u32[]{:S(2)}) %collective-permute-start.2) | collective-permute-done | bytes 786464 | tf_op jit(solution)/shard_map/ppermute | solution.py:588
  43.6 14.6 %collective-permute-done.3.refs_1_ = f32[128,512]{1,0:T(8,128)S(1)} collective-permute-done((f32[128,512]{1,0:T(8,128)S(1)}, f32[128,512]{1,0:T(8,128)S(1)}, u32[]{:S(2)}, u32[]{:S(2)}) %collective-permute-start.3) | collective-permute-done | bytes 262176 | tf_op jit(solution)/shard_map/ppermute | solution.py:588
  58.7 7.6 %collective-permute-done.4.refs_2_ = bf16[128,512]{1,0:T(8,128)(2,1)S(1)} collective-permute-done((bf16[128,512]{1,0:T(8,128)(2,1)S(1)}, bf16[128,512]{1,0:T(8,128)(2,1)S(1)}, u32[]{:S(2)}, u32[]{:S(2)}) %collective-permute-start.4) | collective-permute-done | bytes 131104 | tf_op jit(solution)/shard_map/ppermute | solution.py:588
  69.5 3.7 %all-to-all-start.2 = ((bf16[16,160,128]{2,1,0:T(8,128)(2,1)}), bf16[16,160,128]{2,1,0:T(8,128)(2,1)S(1)}, u32[]{:S(2)}, u32[]{:S(2)}) async-start(bf16[16,160,128]{2,1,0:T(8,128)(2,1)} %copy-done.3), calls=%async_computation.2 | async-start | bytes 1310720 | tf_op jit(solution)/shard_map/all_to_all | solution.py:620
  74.2 9.8 %collective-permute-done.7.refs_2_ = bf16[128,512]{1,0:T(8,128)(2,1)S(1)} collective-permute-done((bf16[128,512]{1,0:T(8,128)(2,1)S(1)}, bf16[128,512]{1,0:T(8,128)(2,1)S(1)}, u32[]{:S(2)}, u32[]{:S(2)}) %collective-permute-start.7) | collective-permute-done | bytes 131104 | tf_op jit(solution)/shard_map/ppermute | solution.py:588
  88.0 5.4 %all-to-all-start.3 = ((bf16[16,128,128]{2,1,0:T(8,128)(2,1)}), bf16[16,128,128]{2,1,0:T(8,128)(2,1)}, u32[]{:S(2)}, u32[]{:S(2)}) async-start(bf16[16,128,128]{2,1,0:T(8,128)(2,1)} %copy-done.4), calls=%async_computation.3 | async-start | bytes 1048576 | tf_op jit(solution)/shard_map/all_to_all | solution.py:620
  95.6 3.5 %shard_map.117 = (bf16[512,512]{1,0:T(8,128)(2,1)}, bf16[256,640]{1,0:T(8,128)(2,1)}) custom-call(bf16[8,64,256]{2,1,0:T(8,128)(2,1)} %refs_0_.7, bf16[16,160,128]{2,1,0:T(8,128)(2,1)} %copy-done.1, f32[8,128]{1,0:T(8,128)} %copy-done.11), custom_call_target="tpu_custom_call" | custom-call | flops 134217728 | bytes 1773568 | tf_op jit(solution)/shard_map/pallas_call | solution.py:571
  100.2 4.3 %shard_map.118 = bf16[64,128,128]{2,1,0:T(8,128)(2,1)} custom-call(bf16[16,160,128]{2,1,0:T(8,128)(2,1)S(1)} %copy-done.2, bf16[64,128,128]{2,1,0:T(8,128)(2,1)S(1)} %copy-done, f32[8,128]{1,0:T(8,128)S(1)} %bitcast.8, f32[8,64,128]{2,1,0:T(8,128)S(1)} %copy-done.6, f32[64,128]{1,0:T(8,128)S(1)} %copy-done.7, f32[64,128]{1,0:T(8,128)S(1)} %copy-done.8), custom_call_target="tpu_custom_call" | custom-call | flops 268435456 | bytes 5181440 | tf_op jit(solution)/shard_map/pallas_call | solution.py:571
  104.5 4.3 %shard_map.119 = (bf16[8,64,256]{2,1,0:T(8,128)(2,1)}, bf16[512,512]{1,0:T(8,128)(2,1)}, bf16[4,32,1408]{2,1,0:T(8,128)(2,1)}, bf16[4,32,1408]{2,1,0:T(8,128)(2,1)}) custom-call(s32[3]{0:T(128)} %copy-done.9, bf16[8,64,256]{2,1,0:T(8,128)(2,1)} %refs_0_.7, bf16[8,64,256]{2,1,0:T(8,128)(2,1)} %refs_2_.5, bf16[256,1024]{1,0:T(8,128)(2,1)} %refs_1_.11, ...), custom_call_target="tpu_custom_call" | custom-call | flops 469762048 | bytes 3538944 | tf_op jit(solution)/shard_map/pallas_call | solution.py:571
  109.2 1.5 %collective-permute-done.10.refs_2_ = bf16[4,32,1408]{2,1,0:T(8,128)(2,1)S(1)} collective-permute-done((bf16[4,32,1408]{2,1,0:T(8,128)(2,1)}, bf16[4,32,1408]{2,1,0:T(8,128)(2,1)S(1)}, u32[]{:S(2)}, u32[]{:S(2)}) %collective-permute-start.10) | collective-permute-done | bytes 360480 | tf_op jit(solution)/shard_map/ppermute | solution.py:588
  112.4 1.9 %collective-permute-start.11 = (bf16[32,1408]{1,0:T(8,128)(2,1)S(1)}, bf16[32,1408]{1,0:T(8,128)(2,1)S(1)}, u32[]{:S(2)}, u32[]{:S(2)}) collective-permute-start(bf16[32,1408]{1,0:T(8,128)(2,1)S(1)} %get-tuple-element.68), channel_id=1, source_target_pairs={{0,2},{1,3},{2,0},{3,1},{4,6},{5,7},{6,4},{7,5},{8,10},{9,11},{10,... | collective-permute-start | bytes 270344 | tf_op jit(solution)/shard_map/ppermute | solution.py:588
  115.9 2.7 %shard_map.121 = bf16[8,64,256]{2,1,0:T(8,128)(2,1)} custom-call(bf16[8,64,256]{2,1,0:T(8,128)(2,1)} %refs_0_.7, bf16[256,1024]{1,0:T(8,128)(2,1)} %refs_1_.11, bf16[512,512]{1,0:T(8,128)(2,1)} %get-tuple-element.71.refs_2_, bf16[512,512]{1,0:T(8,128)(2,1)} %get-tuple-element.72.refs_3_), custom_call_target="tpu_custom_call" | custom-call | flops 268435456 | bytes 2097152 | tf_op jit(solution)/shard_map/pallas_call | solution.py:571
  122.8 3.1 %collective-permute-done.14 = bf16[32,1408]{1,0:T(8,128)(2,1)S(1)} collective-permute-done((bf16[32,1408]{1,0:T(8,128)(2,1)S(1)}, bf16[32,1408]{1,0:T(8,128)(2,1)S(1)}, u32[]{:S(2)}, u32[]{:S(2)}) %collective-permute-start.14) | collective-permute-done | bytes 90144 | tf_op jit(solution)/shard_map/ppermute | solution.py:588
  127.2 4.2 %collective-permute-done.15 = bf16[32,1408]{1,0:T(8,128)(2,1)S(1)} collective-permute-done((bf16[32,1408]{1,0:T(8,128)(2,1)S(1)}, bf16[32,1408]{1,0:T(8,128)(2,1)S(1)}, u32[]{:S(2)}, u32[]{:S(2)}) %collective-permute-start.15) | collective-permute-done | bytes 90144 | tf_op jit(solution)/shard_map/ppermute | solution.py:588
  131.4 9.8 %all-gather = bf16[256,1408]{1,0:T(8,128)(2,1)S(1)} all-gather(bf16[32,1408]{1,0:T(8,128)(2,1)S(1)} %add_convert_fusion), channel_id=2, replica_groups=mesh['seq'=4,'res'=8] {'res'}, dimensions={0}, use_global_device_ids=true | all-gather | bytes 811008 | tf_op jit(solution)/shard_map/all_gather | solution.py:737
  (61 shorter events, 24.7 us)
Async XLA Ops:
  3.4 16.9 %all-to-all-start = ((bf16[16,128,128]{2,1,0:T(8,128)(2,1)}), bf16[16,128,128]{2,1,0:T(8,128)(2,1)S(1)}, u32[]{:S(2)}, u32[]{:S(2)}) async-start(bf16[16,128,128]{2,1,0:T(8,128)(2,1)} %shard_map.109), calls=%async_computation | async-start | bytes 1048576 | tf_op jit(solution)/shard_map/all_to_all | solution.py:620
  20.2 19.8 %all-to-all-start.1 = ((bf16[16,192,128]{2,1,0:T(8,128)(2,1)}), bf16[16,192,128]{2,1,0:T(8,128)(2,1)S(1)}, u32[]{:S(2)}, u32[]{:S(2)}) async-start(bf16[16,192,128]{2,1,0:T(8,128)(2,1)} %get-tuple-element.45), calls=%async_computation.1 | async-start | bytes 1572864 | tf_op jit(solution)/shard_map/all_to_all | solution.py:620
  23.8 2.0 %collective-permute-start = (bf16[16,128,128]{2,1,0:T(8,128)(2,1)S(1)}, bf16[16,128,128]{2,1,0:T(8,128)(2,1)S(1)}, u32[]{:S(2)}, u32[]{:S(2)}) collective-permute-start(bf16[16,128,128]{2,1,0:T(8,128)(2,1)S(1)} %all-to-all-done.refs_1_.refs_5_), channel_id=1, source_target_pairs={{0,1},{1,0},{2,3},{3,2},{4,5},{5,4},{6,7},{7,6},{8,9},{9,8},{10,11... | collective-permute-start | bytes 1572872 | tf_op jit(solution)/shard_map/ppermute | solution.py:588
  24.2 61.1 %copy-start.9 = (s32[3]{0:T(128)}, s32[3]{0:T(128)S(1)}, u32[]{:S(2)}) copy-start(s32[3]{0:T(128)S(1)} %pad_add_fusion.refs_0_) | copy-start | bytes 40
  26.8 9.1 %collective-permute-start.1 = (bf16[128,512]{1,0:T(8,128)(2,1)S(1)}, bf16[128,512]{1,0:T(8,128)(2,1)S(1)}, u32[]{:S(2)}, u32[]{:S(2)}) collective-permute-start(bf16[128,512]{1,0:T(8,128)(2,1)S(1)} %get-tuple-element.47), channel_id=1, source_target_pairs={{0,16},{8,24},{16,0},{24,8},{1,17},{9,25},{17,1},{25,9},{2,18},{10... | collective-permute-start | bytes 393224 | tf_op jit(solution)/shard_map/ppermute | solution.py:588
  40.0 2.3 %collective-permute-start.2 = (bf16[16,192,128]{2,1,0:T(8,128)(2,1)S(1)}, bf16[16,192,128]{2,1,0:T(8,128)(2,1)S(1)}, u32[]{:S(2)}, u32[]{:S(2)}) collective-permute-start(bf16[16,192,128]{2,1,0:T(8,128)(2,1)S(1)} %all-to-all-done.1.refs_1_.refs_5_), channel_id=1, source_target_pairs={{0,1},{1,0},{2,3},{3,2},{4,5},{5,4},{6,7},{7,6},{8,9},{9,8},{10,11... | collective-permute-start | bytes 2359304 | tf_op jit(solution)/shard_map/ppermute | solution.py:588
  43.3 14.9 %collective-permute-start.3 = (f32[128,512]{1,0:T(8,128)S(1)}, f32[128,512]{1,0:T(8,128)S(1)}, u32[]{:S(2)}, u32[]{:S(2)}) collective-permute-start(f32[128,512]{1,0:T(8,128)S(1)} %get-tuple-element.50), channel_id=1, source_target_pairs={{0,16},{8,24},{16,0},{24,8},{1,17},{9,25},{17,1},{25,9},{2,18},{10... | collective-permute-start | bytes 786440 | tf_op jit(solution)/shard_map/ppermute | solution.py:588
  58.5 7.8 %collective-permute-start.4 = (bf16[128,512]{1,0:T(8,128)(2,1)S(1)}, bf16[128,512]{1,0:T(8,128)(2,1)S(1)}, u32[]{:S(2)}, u32[]{:S(2)}) collective-permute-start(bf16[128,512]{1,0:T(8,128)(2,1)S(1)} %get-tuple-element.53.refs_1_), channel_id=1, source_target_pairs={{0,16},{8,24},{16,0},{24,8},{1,17},{9,25},{17,1},{25,9},{2,18},{10... | collective-permute-start | bytes 393224 | tf_op jit(solution)/shard_map/ppermute | solution.py:588
  58.6 7.7 %collective-permute-start.5 = (bf16[128,512]{1,0:T(8,128)(2,1)S(1)}, bf16[128,512]{1,0:T(8,128)(2,1)S(1)}, u32[]{:S(2)}, u32[]{:S(2)}) collective-permute-start(bf16[128,512]{1,0:T(8,128)(2,1)S(1)} %get-tuple-element.53.refs_1_), channel_id=1, source_target_pairs={{0,1},{1,0},{2,3},{3,2},{4,5},{5,4},{6,7},{7,6},{8,9},{9,8},{10,11... | collective-permute-start | bytes 393224 | tf_op jit(solution)/shard_map/ppermute | solution.py:588
  66.3 1.3 collective-permute-start.6
  69.5 23.9 %copy-start = (bf16[64,128,128]{2,1,0:T(8,128)(2,1)S(1)}, bf16[64,128,128]{2,1,0:T(8,128)(2,1)}, u32[]{:S(2)}) copy-start(bf16[64,128,128]{2,1,0:T(8,128)(2,1)} %refs_1_.9) | copy-start | bytes 6291460
  69.5 23.9 %copy-start.7 = (f32[64,128]{1,0:T(8,128)S(1)}, f32[64,128]{1,0:T(8,128)}, u32[]{:S(2)}) copy-start(f32[64,128]{1,0:T(8,128)} %get-tuple-element.59.refs_2_.refs_4_) | copy-start | bytes 98308
  69.5 24.0 %copy-start.8 = (f32[64,128]{1,0:T(8,128)S(1)}, f32[64,128]{1,0:T(8,128)}, u32[]{:S(2)}) copy-start(f32[64,128]{1,0:T(8,128)} %get-tuple-element.60.refs_3_.refs_5_) | copy-start | bytes 98308
  69.5 18.5 %all-to-all-start.2 = ((bf16[16,160,128]{2,1,0:T(8,128)(2,1)}), bf16[16,160,128]{2,1,0:T(8,128)(2,1)S(1)}, u32[]{:S(2)}, u32[]{:S(2)}) async-start(bf16[16,160,128]{2,1,0:T(8,128)(2,1)} %copy-done.3), calls=%async_computation.2 | async-start | bytes 1310720 | tf_op jit(solution)/shard_map/all_to_all | solution.py:620
  73.3 10.7 %collective-permute-start.7 = (bf16[128,512]{1,0:T(8,128)(2,1)S(1)}, bf16[128,512]{1,0:T(8,128)(2,1)S(1)}, u32[]{:S(2)}, u32[]{:S(2)}) collective-permute-start(bf16[128,512]{1,0:T(8,128)(2,1)S(1)} %get-tuple-element.56.refs_1_), channel_id=1, source_target_pairs={{0,16},{8,24},{16,0},{24,8},{1,17},{9,25},{17,1},{25,9},{2,18},{10... | collective-permute-start | bytes 393224 | tf_op jit(solution)/shard_map/ppermute | solution.py:588
  74.1 9.9 %collective-permute-start.8 = (bf16[128,512]{1,0:T(8,128)(2,1)S(1)}, bf16[128,512]{1,0:T(8,128)(2,1)S(1)}, u32[]{:S(2)}, u32[]{:S(2)}) collective-permute-start(bf16[128,512]{1,0:T(8,128)(2,1)S(1)} %get-tuple-element.56.refs_1_), channel_id=1, source_target_pairs={{0,1},{1,0},{2,3},{3,2},{4,5},{5,4},{6,7},{7,6},{8,9},{9,8},{10,11... | collective-permute-start | bytes 393224 | tf_op jit(solution)/shard_map/ppermute | solution.py:588
  84.0 1.3 collective-permute-start.9
  88.0 16.5 %all-to-all-start.3 = ((bf16[16,128,128]{2,1,0:T(8,128)(2,1)}), bf16[16,128,128]{2,1,0:T(8,128)(2,1)}, u32[]{:S(2)}, u32[]{:S(2)}) async-start(bf16[16,128,128]{2,1,0:T(8,128)(2,1)} %copy-done.4), calls=%async_computation.3 | async-start | bytes 1048576 | tf_op jit(solution)/shard_map/all_to_all | solution.py:620
  108.8 2.0 %collective-permute-start.10 = (bf16[4,32,1408]{2,1,0:T(8,128)(2,1)}, bf16[4,32,1408]{2,1,0:T(8,128)(2,1)S(1)}, u32[]{:S(2)}, u32[]{:S(2)}) collective-permute-start(bf16[4,32,1408]{2,1,0:T(8,128)(2,1)} %get-tuple-element.67), channel_id=1, source_target_pairs={{0,1},{1,0},{2,3},{3,2},{4,5},{5,4},{6,7},{7,6},{8,9},{9,8},{10,11... | collective-permute-start | bytes 1081352 | tf_op jit(solution)/shard_map/ppermute | solution.py:588
  112.4 6.3 %collective-permute-start.11 = (bf16[32,1408]{1,0:T(8,128)(2,1)S(1)}, bf16[32,1408]{1,0:T(8,128)(2,1)S(1)}, u32[]{:S(2)}, u32[]{:S(2)}) collective-permute-start(bf16[32,1408]{1,0:T(8,128)(2,1)S(1)} %get-tuple-element.68), channel_id=1, source_target_pairs={{0,2},{1,3},{2,0},{3,1},{4,6},{5,7},{6,4},{7,5},{8,10},{9,11},{10,... | collective-permute-start | bytes 270344 | tf_op jit(solution)/shard_map/ppermute | solution.py:588
  114.3 5.5 %collective-permute-start.12 = (bf16[32,1408]{1,0:T(8,128)(2,1)S(1)}, bf16[32,1408]{1,0:T(8,128)(2,1)S(1)}, u32[]{:S(2)}, u32[]{:S(2)}) collective-permute-start(bf16[32,1408]{1,0:T(8,128)(2,1)S(1)} %get-tuple-element.69), channel_id=1, source_target_pairs={{0,4},{1,5},{2,6},{3,7},{4,0},{5,1},{6,2},{7,3},{8,12},{9,13},{10,... | collective-permute-start | bytes 270344 | tf_op jit(solution)/shard_map/ppermute | solution.py:588
  115.8 5.4 %collective-permute-start.13 = (bf16[32,1408]{1,0:T(8,128)(2,1)S(1)}, bf16[32,1408]{1,0:T(8,128)(2,1)S(1)}, u32[]{:S(2)}, u32[]{:S(2)}) collective-permute-start(bf16[32,1408]{1,0:T(8,128)(2,1)S(1)} %get-tuple-element.70), channel_id=1, source_target_pairs={{0,6},{1,7},{2,4},{3,5},{4,2},{5,3},{6,0},{7,1},{8,14},{9,15},{10,... | collective-permute-start | bytes 270344 | tf_op jit(solution)/shard_map/ppermute | solution.py:588
  121.2 4.6 %collective-permute-start.14 = (bf16[32,1408]{1,0:T(8,128)(2,1)S(1)}, bf16[32,1408]{1,0:T(8,128)(2,1)S(1)}, u32[]{:S(2)}, u32[]{:S(2)}) collective-permute-start(bf16[32,1408]{1,0:T(8,128)(2,1)S(1)} %shard_map.122), channel_id=1, source_target_pairs={{0,8},{8,0},{16,24},{24,16},{1,9},{9,1},{17,25},{25,17},{2,10},{10... | collective-permute-start | bytes 270344 | tf_op jit(solution)/shard_map/ppermute | solution.py:588
  125.9 5.5 %collective-permute-start.15 = (bf16[32,1408]{1,0:T(8,128)(2,1)S(1)}, bf16[32,1408]{1,0:T(8,128)(2,1)S(1)}, u32[]{:S(2)}, u32[]{:S(2)}) collective-permute-start(bf16[32,1408]{1,0:T(8,128)(2,1)S(1)} %add_convert_fusion.1), channel_id=1, source_target_pairs={{0,16},{8,24},{16,0},{24,8},{1,17},{9,25},{17,1},{25,9},{2,18},{10... | collective-permute-start | bytes 270344 | tf_op jit(solution)/shard_map/ppermute | solution.py:588
  (9 other events, 33.2 us)

commit v12 on v9

--- a/solution.py
+++ b/solution.py
@@ -224,28 +224,29 @@
     return 1.0 / (1.0 + jnp.exp(-logits))
 
 
-def value_kernel(x_ref, grad_ref, wc_ref, wo_ref, out_ref):
+def query_kernel(scale, x_ref, wc_ref, out_ref):
     residues, width = x_ref.shape[1], x_ref.shape[2]
+    normed = normalized(x_ref)[0].astype(jnp.bfloat16)
+    pack_heads(out_ref, 0, f32_dot(normed, wc_ref[:, :width]) * scale, residues)
+    pack_heads(out_ref, residues, f32_dot(normed, wc_ref[:, width : 2 * width]), residues)
+
+
+def centred(weight):
+    return weight - jnp.mean(weight, axis=1, keepdims=True)
+
+
+def value_kernel(
+    arrive, x_ref, grad_ref, wc_ref, wo_ref, pair_ref, weight_ref,
+    out_ref, bias_ref, mean_ref, spread_ref,
+):
+    residues, width = x_ref.shape[1], x_ref.shape[2]
+    heads = weight_ref.shape[0]
     normed = normalized(x_ref)[0].astype(jnp.bfloat16)
     values = f32_dot(normed, wc_ref[:, 2 * width : 3 * width])
     gate = gate_of(f32_dot(normed, wc_ref[:, 3 * width :]))
     grad_gated = f32_dot(grad_ref[...].reshape(-1, width), wo_ref[...], NT)
     pack_heads(out_ref, 0, values, residues)
     pack_heads(out_ref, residues, grad_gated * gate, residues)
-
-
-def centred(weight):
-    return weight - jnp.mean(weight, axis=1, keepdims=True)
-
-
-def query_kernel(
-    scale, arrive, x_ref, wc_ref, pair_ref, weight_ref, out_ref, bias_ref, mean_ref, spread_ref
-):
-    residues, width = x_ref.shape[1], x_ref.shape[2]
-    heads = weight_ref.shape[0]
-    normed = normalized(x_ref)[0].astype(jnp.bfloat16)
-    pack_heads(out_ref, 0, f32_dot(normed, wc_ref[:, :width]) * scale, residues)
-    pack_heads(out_ref, residues, f32_dot(normed, wc_ref[:, width : 2 * width]), residues)
 
     arrive()
     columns, channels = pair_ref.shape[1], pair_ref.shape[2]
@@ -292,7 +293,7 @@
 
 
 def score_kernel(
-    residues, left_row, right_row, with_bias, place_ref, own_ref, other_ref, mine_ref, sent_ref
+    residues, left_row, right_row, place_ref, own_ref, other_ref, mine_ref, sent_ref
 ):
     core, half = place_ref[0], place_ref[1]
     count = own_ref.shape[0] // 2
@@ -316,19 +317,32 @@
                 )
             )
         ref[...] = f32_dot(jnp.concatenate(left, axis=0), right, NT).astype(ref.dtype)
-        if with_bias:
-            for p in range(2):
-                columns = pl.ds(pl.multiple_of((half * 2 + p) * LANES, LANES), LANES)
-                for k in range(count // 2):
-                    block = p * count + which * (count // 2) + k
-                    high = own_ref[block, 2 * residues : 2 * residues + part, :]
-                    low = own_ref[block, 2 * residues + part : 3 * residues, :]
-                    bias = high.astype(jnp.float32) + low.astype(jnp.float32)
-                    ref[k * part : (k + 1) * part, columns] += bias
-
-
-def softmax_kernel(logit_ref, other_ref, out_ref, low_ref):
-    logits = logit_ref[...] + other_ref[...]
+
+
+def bias_kernel(row, place_ref, blocks_ref, mine_ref, sent_ref):
+    half = place_ref[1]
+    count = blocks_ref.shape[0] // 2
+    for which, ref in ((half, mine_ref), (1 - half, sent_ref)):
+        for p in range(2):
+            for k in range(count // 2):
+                block = p * count + which * (count // 2) + k
+                ref[p * (count // 2) + k] = blocks_ref[block, row:, :]
+
+
+def softmax_kernel(
+    place_ref, logit_ref, other_ref, bias_ref, bias_other_ref, out_ref, low_ref
+):
+    half = place_ref[1]
+    count, part = bias_ref.shape[0] // 2, bias_ref.shape[1] // 2
+    out_ref[...] = logit_ref[...] + other_ref[...]
+    for which, ref in ((half, bias_ref), (1 - half, bias_other_ref)):
+        for p in range(2):
+            columns = pl.ds(pl.multiple_of((which * 2 + p) * LANES, LANES), LANES)
+            for k in range(count):
+                high = ref[p * count + k, :part, :].astype(jnp.float32)
+                low = ref[p * count + k, part:, :].astype(jnp.float32)
+                out_ref[k * part : (k + 1) * part, columns] += high + low
+    logits = out_ref[...]
     lifted = jnp.exp(logits - jnp.max(logits, axis=-1, keepdims=True))
     softmax_out = lifted / jnp.sum(lifted, axis=-1, keepdims=True)
     out_ref[...] = softmax_out
@@ -532,6 +546,17 @@
     lax.fori_loop(0, pair_ref.shape[0] // 8, rows, 0)
 
 
+def output_kernel(parts_ref, combined_ref, out_weight_ref, pair_weight_ref):
+    width = combined_ref.shape[0]
+    rows = parts_ref.shape[1]
+    for h in range(parts_ref.shape[0]):
+        block = slice(h * rows, (h + 1) * rows)
+        part = parts_ref[h].astype(jnp.float32)
+        combined_ref[block, :] = part[:, : 4 * width]
+        out_weight_ref[block, :] = part[:, 4 * width : 5 * width]
+        pair_weight_ref[h : h + 1, :] = part[:1, 5 * width :]
+
+
 def call(kernel, outs, *args, scratch=(), place=None, flops=0, after=(), outside=0, late=0):
     whole, anywhere = pl.BlockSpec(memory_space=pltpu.VMEM), pl.BlockSpec(memory_space=pl.ANY)
     specs = [anywhere] * outside + [whole] * (len(args) - outside)
@@ -616,70 +641,76 @@
         return lax.all_to_all(blocks, ("seq", "res"), 0, 0, axis_index_groups=groups, tiled=True)
 
     x, grad, wc, wo = alignment_rows, updated_gradient, combined_weight, output_weight
-    query_blocks, bias, mean, spread = call(
-        functools.partial(query_kernel, scale),
+    (query_blocks,) = call(
+        functools.partial(query_kernel, scale), [((group, 2 * residues, LANES), bf16)], x, wc,
+        flops=8 * tokens * width * width, outside=2,
+    )
+    query_blocks = across(query_blocks)
+    value_blocks, bias, mean, spread = call(
+        value_kernel,
         [
             ((group, 3 * residues, LANES), bf16),
             ((heads, residues, LANES), f32),
             ((residues, LANES), f32),
             ((residues, LANES), f32),
         ],
-        x, wc, pair_entries, pair_weight.T,
-        flops=8 * tokens * width * width, outside=3, late=1,
-    )
-    query_blocks = across(query_blocks)
-    def scores(blocks, left_row, right_row, with_bias, kind):
+        x, grad, wc, wo, pair_entries, pair_weight.T,
+        flops=8 * tokens * width * width, outside=5, late=1,
+    )
+    query_blocks, value_blocks = lax.optimization_barrier((query_blocks, value_blocks))
+    value_blocks = across(value_blocks)
+
+    def scores(blocks, left_row, right_row, kind):
         return call(
-            functools.partial(score_kernel, residues, left_row, right_row, with_bias),
+            functools.partial(score_kernel, residues, left_row, right_row),
             [((total // 4, total), f32), ((total // 4, total), kind)],
             blocks, swapped(blocks, "res", 1),
             place=place, flops=2 * total * total * width,
         )
 
-    (value_blocks,) = call(
-        value_kernel, [((group, 2 * residues, LANES), bf16)], x, grad, wc, wo,
-        flops=8 * tokens * width * width, outside=4,
-    )
-    logit_mine, logit_sent = scores(query_blocks, 0, residues, True, f32)
-    value_blocks, logit_sent = lax.optimization_barrier((value_blocks, logit_sent))
+    logit_mine, logit_sent = scores(query_blocks, 0, residues, f32)
     logit_other = swapped(logit_sent, "seq", seq_half)
-    value_blocks = across(value_blocks)
+    value_blocks, logit_other = lax.optimization_barrier((value_blocks, logit_other))
     quarter = (total // 4, total)
+    bias_half = ((group // 2, residues, LANES), bf16)
+    bias_mine, bias_sent = call(
+        functools.partial(bias_kernel, 2 * residues), [bias_half, bias_half], value_blocks,
+        place=place,
+    )
+    bias_other = swapped(bias_sent, "seq", seq_half)
+    grad_mine, grad_sent = scores(value_blocks, residues, 0, bf16)
+    grad_other = swapped(grad_sent, "seq", seq_half)
+    bias_other, grad_mine = lax.optimization_barrier((bias_other, grad_mine))
     softmax_out, probs = call(
-        softmax_kernel, [(quarter, f32), (quarter, bf16)], logit_mine, logit_other,
-        flops=total * total,
-    )
-    probs_far = swapped(probs, "seq", seq_half)
-    value_blocks, probs_far = lax.optimization_barrier((value_blocks, probs_far))
-    grad_mine, grad_sent = scores(value_blocks, residues, 0, False, bf16)
-    grad_other = swapped(grad_sent, "seq", seq_half)
-
-    def products(quarters, blocks, first_row, second_row, with_share, factor):
+        softmax_kernel, [(quarter, f32), (quarter, bf16)],
+        logit_mine, logit_other, bias_mine, bias_other,
+        place=place, flops=total * total,
+    )
+
+    def products(mine, blocks, first_row, second_row, with_share, factor):
         rows = 2 * residues + (residues // 2 if with_share else 0)
+        far = swapped(mine, "seq", seq_half)
         (out,) = call(
             functools.partial(
                 product_kernel, residues, factor, first_row, second_row, with_share
             ),
             [((group, rows, LANES), bf16)],
-            *quarters, blocks,
+            mine, far, swapped(mine, "res", 1), swapped(far, "res", 1), blocks,
             scratch=[pltpu.VMEM((total, total), bf16)],
             place=place, flops=4 * total * total * width,
         )
         return out
 
-    def with_near(mine, far):
-        return mine, far, swapped(mine, "res", 1), swapped(far, "res", 1)
-
-    attended = products(with_near(probs, probs_far), value_blocks, 0, residues, False, 1.0)
-    attended, grad_other = lax.optimization_barrier((attended, grad_other))
-    attended_blocks = across(attended)
+    attended = products(probs, value_blocks, 0, residues, False, 1.0)
     (grad_logits,) = call(
         softmax_gradient_kernel, [(quarter, bf16)], softmax_out, grad_mine, grad_other,
         flops=total * total,
     )
-    grad_quarters = with_near(grad_logits, swapped(grad_logits, "seq", seq_half))
-    grad_quarters, attended_blocks = lax.optimization_barrier((grad_quarters, attended_blocks))
-    grad_blocks = across(products(grad_quarters, query_blocks, residues, 0, True, scale))
+    attended, grad_logits = lax.optimization_barrier((attended, grad_logits))
+    attended_blocks = across(attended)
+    grad_sums = products(grad_logits, query_blocks, residues, 0, True, scale)
+    grad_sums, attended_blocks = lax.optimization_barrier((grad_sums, attended_blocks))
+    grad_blocks = across(grad_sums)
 
     updated, value_gate, normed, attended_sums = call(
         attended_weight_kernel,
@@ -732,14 +763,18 @@
 
     part = added(part, swapped(part, "seq", 1))
     part = added(part, swapped(part, "seq", seq_half))
-    whole = lax.all_gather(part, "res", axis=0)
+    combined_gradient, output_gradient, pair_weight_gradient = call(
+        output_kernel,
+        [(wc.shape, f32), (wo.shape, f32), ((heads, channels), f32)],
+        lax.all_gather(part, "res", axis=0),
+    )
     return (
         updated,
         alignment_gradient,
         pair_gradient,
-        whole[:, :, : 4 * width].reshape(wc.shape).astype(f32),
-        whole[:, :, 4 * width : 5 * width].reshape(wo.shape).astype(f32),
-        whole[:, 0, 5 * width :].T.astype(f32),
+        combined_gradient,
+        output_gradient,
+        pair_weight_gradient.T,
     )
 
 

time: 141 us -> 139 us (0.986)
  blocking collectives: 28.9 us -> 9.25 us
  waiting for transfers between devices: 45.3 us -> 64 us
  other arithmetic: 2.57 us -> 0.12 us
  Pallas kernels: 29.8 us -> 32.1 us
  starting transfers between devices: 33 us -> 31.4 us
    all_to_all x1 -> x0, blocking collectives: 19.7 us -> none  [across(): lax.all_to_all(blocks, ('seq', 'res'), 0, 0, axis_index_groups=groups, ti...]
    ppermute x16 -> x17, waiting for transfers between devices: 34.7 us -> 49.1 us  [swapped(): lax.ppermute(mine, axis_name, [(a, a ^ distance) for a in range(size)])]
    all_to_all x3 -> x4, waiting for transfers between devices: 10.5 us -> 14.9 us  [across(): lax.all_to_all(blocks, ('seq', 'res'), 0, 0, axis_index_groups=groups, ti...]
    ppermute x16 -> x17, starting transfers between devices: 16.7 us -> 12.5 us  [swapped(): lax.ppermute(mine, axis_name, [(a, a ^ distance) for a in range(size)])]
    all_to_all x3 -> x4, starting transfers between devices: 16.4 us -> 18.9 us  [across(): lax.all_to_all(blocks, ('seq', 'res'), 0, 0, axis_index_groups=groups, ti...]
    convert_element_type x3 -> x0, other arithmetic: 2.45 us -> none  [the longest x1 1.12 us: head_body(): whole[:, :, :4 * width].reshape(wc.shape).astype(f32)]
    pallas_call x15 -> x17, Pallas kernels: 29.8 us -> 32.1 us  [call(): pl.pallas_call(wrapped, out_shape=shapes, in_specs=[pl.BlockSpec(memory_s...]
  transfers between devices with their start and end apart: 19 -> 21, of which waited for: 11 -> 15; matrix products, arithmetic and copies ran while one was open for 0% -> 0% of each run, Pallas kernels for 11% -> 16%
where the time goes in v12:
time: 139 us; the launch traced here: 138 us
  waiting for transfers between devices  64 us (46%)
  Pallas kernels  32.1 us (23%)
  starting transfers between devices  31.4 us (23%)
  blocking collectives  9.25 us (7%)
    ppermute x17, waiting for transfers between devices, swapped(): lax.ppermute(mine, axis_name, [(a, a ^ distance) for a in range(size)])  49.1 us
    pallas_call x17, Pallas kernels, call(): pl.pallas_call(wrapped, out_shape=shapes, in_specs=[pl.BlockSpec(memory_s...  32.1 us
    all_to_all x4, starting transfers between devices, across(): lax.all_to_all(blocks, ('seq', 'res'), 0, 0, axis_index_groups=groups, ti...  18.9 us
    all_to_all x4, waiting for transfers between devices, across(): lax.all_to_all(blocks, ('seq', 'res'), 0, 0, axis_index_groups=groups, ti...  14.9 us
    ppermute x17, starting transfers between devices, swapped(): lax.ppermute(mine, axis_name, [(a, a ^ distance) for a in range(size)])  12.5 us
    all_gather x1, blocking collectives, head_body(): lax.all_gather(part, 'res', axis=0)  9.25 us
  transfers between devices with their start and end apart: 21, of which 15 were waited for; matrix products, arithmetic and copies ran while one was open for 0% of the time, Pallas kernels for 16%

profile of v12, /device:TPU:0, one launch (start us, length us, event | category | flops | bytes accessed | tf_op | source)
XLA Modules:
  0.0 137.9 jit_solution(6519134066200477689)
XLA Ops:
  0.6 2.6 %shard_map.109 = bf16[16,128,128]{2,1,0:T(8,128)(2,1)} custom-call(bf16[8,64,256]{2,1,0:T(8,128)(2,1)} %refs_0_.7, bf16[256,1024]{1,0:T(8,128)(2,1)} %refs_1_.10), custom_call_target="tpu_custom_call" | custom-call | flops 268435456 | bytes 1310720 | tf_op jit(solution)/shard_map/pallas_call | solution.py:592
  3.3 6.3 %all-to-all-start = ((bf16[16,128,128]{2,1,0:T(8,128)(2,1)}), bf16[16,128,128]{2,1,0:T(8,128)(2,1)S(1)}, u32[]{:S(2)}, u32[]{:S(2)}) async-start(bf16[16,128,128]{2,1,0:T(8,128)(2,1)} %shard_map.109), calls=%async_computation | async-start | bytes 1048576 | tf_op jit(solution)/shard_map/all_to_all | solution.py:641
  9.6 8.2 %shard_map.110 = (bf16[16,192,128]{2,1,0:T(8,128)(2,1)}, f32[8,64,128]{2,1,0:T(8,128)}, f32[64,128]{1,0:T(8,128)}, f32[64,128]{1,0:T(8,128)}) custom-call(bf16[8,64,256]{2,1,0:T(8,128)(2,1)} %refs_0_.7, bf16[8,64,256]{2,1,0:T(8,128)(2,1)} %refs_1_.8, bf16[256,1024]{1,0:T(8,128)(2,1)} %refs_1_.10, bf16[256,256]{1,0:T(8,128)(2,1)} %refs_3_.3, ...), custom_call_target="tpu_custom_call" | custom-call | flops 268435456 | bytes 4395008 | tf_op jit(solution)/shard_map/pallas_call | solution.py:592
  17.8 2.3 %all-to-all-done.refs_1_.refs_5_ = bf16[16,128,128]{2,1,0:T(8,128)(2,1)S(1)} async-done(((bf16[16,128,128]{2,1,0:T(8,128)(2,1)}), bf16[16,128,128]{2,1,0:T(8,128)(2,1)S(1)}, u32[]{:S(2)}, u32[]{:S(2)}) %all-to-all-start) | async-done | bytes 524320 | tf_op jit(solution)/shard_map/all_to_all | solution.py:641
  20.1 3.6 %all-to-all-start.1 = ((bf16[16,192,128]{2,1,0:T(8,128)(2,1)}), bf16[16,192,128]{2,1,0:T(8,128)(2,1)S(1)}, u32[]{:S(2)}, u32[]{:S(2)}) async-start(bf16[16,192,128]{2,1,0:T(8,128)(2,1)} %get-tuple-element.49), calls=%async_computation.1 | async-start | bytes 1572864 | tf_op jit(solution)/shard_map/all_to_all | solution.py:641
  26.7 2.7 %collective-permute-start.1 = (f32[128,512]{1,0:T(8,128)S(1)}, f32[128,512]{1,0:T(8,128)S(1)}, u32[]{:S(2)}, u32[]{:S(2)}) collective-permute-start(f32[128,512]{1,0:T(8,128)S(1)} %get-tuple-element.50), channel_id=1, source_target_pairs={{0,16},{8,24},{16,0},{24,8},{1,17},{9,25},{17,1},{25,9},{2,18},{10... | collective-permute-start | bytes 786440 | tf_op jit(solution)/shard_map/ppermute | solution.py:609
  29.4 9.3 %collective-permute-done.1.refs_2_ = f32[128,512]{1,0:T(8,128)S(1)} collective-permute-done((f32[128,512]{1,0:T(8,128)S(1)}, f32[128,512]{1,0:T(8,128)S(1)}, u32[]{:S(2)}, u32[]{:S(2)}) %collective-permute-start.1) | collective-permute-done | bytes 262176 | tf_op jit(solution)/shard_map/ppermute | solution.py:609
  38.7 4.0 %all-to-all-done.1.refs_1_.refs_5_ = bf16[16,192,128]{2,1,0:T(8,128)(2,1)S(1)} async-done(((bf16[16,192,128]{2,1,0:T(8,128)(2,1)}), bf16[16,192,128]{2,1,0:T(8,128)(2,1)S(1)}, u32[]{:S(2)}, u32[]{:S(2)}) %all-to-all-start.1) | async-done | bytes 786464 | tf_op jit(solution)/shard_map/all_to_all | solution.py:641
  46.0 6.9 %collective-permute-done.2.refs_4_ = bf16[8,64,128]{2,1,0:T(8,128)(2,1)S(1)} collective-permute-done((bf16[8,64,128]{2,1,0:T(8,128)(2,1)S(1)}, bf16[8,64,128]{2,1,0:T(8,128)(2,1)S(1)}, u32[]{:S(2)}, u32[]{:S(2)}) %collective-permute-start.2) | collective-permute-done | bytes 131104 | tf_op jit(solution)/shard_map/ppermute | solution.py:609
  53.8 2.9 %collective-permute-start.7 = (bf16[128,512]{1,0:T(8,128)(2,1)S(1)}, bf16[128,512]{1,0:T(8,128)(2,1)S(1)}, u32[]{:S(2)}, u32[]{:S(2)}) collective-permute-start(bf16[128,512]{1,0:T(8,128)(2,1)S(1)} %get-tuple-element.60), channel_id=1, source_target_pairs={{0,16},{8,24},{16,0},{24,8},{1,17},{9,25},{17,1},{25,9},{2,18},{10... | collective-permute-start | bytes 393224 | tf_op jit(solution)/shard_map/ppermute | solution.py:609
  56.8 7.7 %collective-permute-done.4.refs_2_ = bf16[128,512]{1,0:T(8,128)(2,1)S(1)} collective-permute-done((bf16[128,512]{1,0:T(8,128)(2,1)S(1)}, bf16[128,512]{1,0:T(8,128)(2,1)S(1)}, u32[]{:S(2)}, u32[]{:S(2)}) %collective-permute-start.4) | collective-permute-done | bytes 131104 | tf_op jit(solution)/shard_map/ppermute | solution.py:609
  64.5 2.7 %collective-permute-done.7.refs_2_ = bf16[128,512]{1,0:T(8,128)(2,1)S(1)} collective-permute-done((bf16[128,512]{1,0:T(8,128)(2,1)S(1)}, bf16[128,512]{1,0:T(8,128)(2,1)S(1)}, u32[]{:S(2)}, u32[]{:S(2)}) %collective-permute-start.7) | collective-permute-done | bytes 131104 | tf_op jit(solution)/shard_map/ppermute | solution.py:609
  67.3 1.8 %shard_map.115 = bf16[16,128,128]{2,1,0:T(8,128)(2,1)} custom-call(s32[3]{0:T(128)S(1)} %pad_add_fusion.refs_0_, bf16[128,512]{1,0:T(8,128)(2,1)S(1)} %get-tuple-element.57.refs_1_, bf16[128,512]{1,0:T(8,128)(2,1)S(1)} %collective-permute-done.4.refs_2_, bf16[128,512]{1,0:T(8,128)(2,1)S(1)} %collective-permute-done.5.refs_3_, ...), custom_call_target="tpu_custom_call" | custom-call | flops 268435456 | bytes 1835008 | tf_op jit(solution)/shard_map/pallas_call | solution.py:592
  69.1 3.6 %all-to-all-start.2 = ((bf16[16,128,128]{2,1,0:T(8,128)(2,1)}), bf16[16,128,128]{2,1,0:T(8,128)(2,1)S(1)}, u32[]{:S(2)}, u32[]{:S(2)}) async-start(bf16[16,128,128]{2,1,0:T(8,128)(2,1)} %shard_map.115), calls=%async_computation.2 | async-start | bytes 1048576 | tf_op jit(solution)/shard_map/all_to_all | solution.py:641
  73.7 8.3 %collective-permute-done.8.refs_2_ = bf16[128,512]{1,0:T(8,128)(2,1)S(1)} collective-permute-done((bf16[128,512]{1,0:T(8,128)(2,1)S(1)}, bf16[128,512]{1,0:T(8,128)(2,1)S(1)}, u32[]{:S(2)}, u32[]{:S(2)}) %collective-permute-start.8) | collective-permute-done | bytes 131104 | tf_op jit(solution)/shard_map/ppermute | solution.py:609
  83.4 1.9 %shard_map.117 = bf16[16,160,128]{2,1,0:T(8,128)(2,1)} custom-call(s32[3]{0:T(128)S(1)} %pad_add_fusion.refs_0_, bf16[128,512]{1,0:T(8,128)(2,1)S(1)} %shard_map.116.refs_1_, bf16[128,512]{1,0:T(8,128)(2,1)S(1)} %collective-permute-done.8.refs_2_, bf16[128,512]{1,0:T(8,128)(2,1)S(1)} %collective-permute-done.9.refs_3_, ...), custom_call_target="tpu_custom_call" | custom-call | flops 268435456 | bytes 1703936 | tf_op jit(solution)/shard_map/pallas_call | solution.py:592
  86.0 5.4 %all-to-all-start.3 = ((bf16[16,160,128]{2,1,0:T(8,128)(2,1)}), bf16[16,160,128]{2,1,0:T(8,128)(2,1)S(1)}, u32[]{:S(2)}, u32[]{:S(2)}) async-start(bf16[16,160,128]{2,1,0:T(8,128)(2,1)} %shard_map.117), calls=%async_computation.3 | async-start | bytes 1310720 | tf_op jit(solution)/shard_map/all_to_all | solution.py:641
  91.4 4.1 %shard_map.118 = (bf16[8,64,256]{2,1,0:T(8,128)(2,1)}, bf16[512,512]{1,0:T(8,128)(2,1)}, bf16[512,256]{1,0:T(8,128)(2,1)}, bf16[256,768]{1,0:T(8,128)(2,1)}) custom-call(bf16[8,64,256]{2,1,0:T(8,128)(2,1)} %refs_0_.7, bf16[8,64,256]{2,1,0:T(8,128)(2,1)} %refs_1_.8, bf16[256,1024]{1,0:T(8,128)(2,1)} %refs_1_.10, bf16[256,256]{1,0:T(8,128)(2,1)} %refs_3_.3, ...), custom_call_target="tpu_custom_call" | custom-call | flops 469762048 | bytes 3145728 | tf_op jit(solution)/shard_map/pallas_call | solution.py:592
  95.6 7.8 %all-to-all-done.3.refs_0_.refs_2_ = bf16[16,160,128]{2,1,0:T(8,128)(2,1)S(1)} async-done(((bf16[16,160,128]{2,1,0:T(8,128)(2,1)}), bf16[16,160,128]{2,1,0:T(8,128)(2,1)S(1)}, u32[]{:S(2)}, u32[]{:S(2)}) %all-to-all-start.3) | async-done | bytes 655392 | tf_op jit(solution)/shard_map/all_to_all | solution.py:641
  109.5 2.5 %collective-permute-start.14 = (bf16[32,1408]{1,0:T(8,128)(2,1)S(1)}, bf16[32,1408]{1,0:T(8,128)(2,1)S(1)}, u32[]{:S(2)}, u32[]{:S(2)}) collective-permute-start(bf16[32,1408]{1,0:T(8,128)(2,1)S(1)} %get-tuple-element.76), channel_id=1, source_target_pairs={{0,6},{1,7},{2,4},{3,5},{4,2},{5,3},{6,0},{7,1},{8,14},{9,15},{10,... | collective-permute-start | bytes 270344 | tf_op jit(solution)/shard_map/ppermute | solution.py:609
  112.0 4.3 %shard_map.123 = bf16[64,128,128]{2,1,0:T(8,128)(2,1)} custom-call(bf16[16,160,128]{2,1,0:T(8,128)(2,1)S(1)} %all-to-all-done.3.refs_0_.refs_2_, bf16[64,128,128]{2,1,0:T(8,128)(2,1)S(1)} %copy-done, f32[8,128]{1,0:T(8,128)S(1)} %bitcast.8, f32[8,64,128]{2,1,0:T(8,128)S(1)} %copy-done.5, f32[64,128]{1,0:T(8,128)S(1)} %copy-done.7, f32[64,128]{1,0:T(8,128)S(1)} %copy-done.8), custom_call_target="tpu_custom_call" | custom-call | flops 268435456 | bytes 5181440 | tf_op jit(solution)/shard_map/pallas_call | solution.py:592
  117.0 4.0 %collective-permute-done.15 = bf16[32,1408]{1,0:T(8,128)(2,1)S(1)} collective-permute-done((bf16[32,1408]{1,0:T(8,128)(2,1)S(1)}, bf16[32,1408]{1,0:T(8,128)(2,1)S(1)}, u32[]{:S(2)}, u32[]{:S(2)}) %collective-permute-start.15) | collective-permute-done | bytes 90144 | tf_op jit(solution)/shard_map/ppermute | solution.py:609
  123.6 3.9 %collective-permute-done.16 = bf16[32,1408]{1,0:T(8,128)(2,1)S(1)} collective-permute-done((bf16[32,1408]{1,0:T(8,128)(2,1)S(1)}, bf16[32,1408]{1,0:T(8,128)(2,1)S(1)}, u32[]{:S(2)}, u32[]{:S(2)}) %collective-permute-start.16) | collective-permute-done | bytes 90144 | tf_op jit(solution)/shard_map/ppermute | solution.py:609
  127.5 9.3 %all-gather = bf16[256,1408]{1,0:T(8,128)(2,1)S(1)} all-gather(bf16[32,1408]{1,0:T(8,128)(2,1)S(1)} %add_convert_fusion), channel_id=2, replica_groups=mesh['seq'=4,'res'=8] {'res'}, dimensions={0}, use_global_device_ids=true | all-gather | bytes 811008 | tf_op jit(solution)/shard_map/all_gather | solution.py:769
  (61 shorter events, 20.9 us)
Async XLA Ops:
  3.3 16.9 %all-to-all-start = ((bf16[16,128,128]{2,1,0:T(8,128)(2,1)}), bf16[16,128,128]{2,1,0:T(8,128)(2,1)S(1)}, u32[]{:S(2)}, u32[]{:S(2)}) async-start(bf16[16,128,128]{2,1,0:T(8,128)(2,1)} %shard_map.109), calls=%async_computation | async-start | bytes 1048576 | tf_op jit(solution)/shard_map/all_to_all | solution.py:641
  20.1 22.6 %all-to-all-start.1 = ((bf16[16,192,128]{2,1,0:T(8,128)(2,1)}), bf16[16,192,128]{2,1,0:T(8,128)(2,1)S(1)}, u32[]{:S(2)}, u32[]{:S(2)}) async-start(bf16[16,192,128]{2,1,0:T(8,128)(2,1)} %get-tuple-element.49), calls=%async_computation.1 | async-start | bytes 1572864 | tf_op jit(solution)/shard_map/all_to_all | solution.py:641
  23.7 2.0 %collective-permute-start = (bf16[16,128,128]{2,1,0:T(8,128)(2,1)S(1)}, bf16[16,128,128]{2,1,0:T(8,128)(2,1)S(1)}, u32[]{:S(2)}, u32[]{:S(2)}) collective-permute-start(bf16[16,128,128]{2,1,0:T(8,128)(2,1)S(1)} %all-to-all-done.refs_1_.refs_5_), channel_id=1, source_target_pairs={{0,1},{1,0},{2,3},{3,2},{4,5},{5,4},{6,7},{7,6},{8,9},{9,8},{10,11... | collective-permute-start | bytes 1572872 | tf_op jit(solution)/shard_map/ppermute | solution.py:609
  26.7 12.0 %collective-permute-start.1 = (f32[128,512]{1,0:T(8,128)S(1)}, f32[128,512]{1,0:T(8,128)S(1)}, u32[]{:S(2)}, u32[]{:S(2)}) collective-permute-start(f32[128,512]{1,0:T(8,128)S(1)} %get-tuple-element.50), channel_id=1, source_target_pairs={{0,16},{8,24},{16,0},{24,8},{1,17},{9,25},{17,1},{25,9},{2,18},{10... | collective-permute-start | bytes 786440 | tf_op jit(solution)/shard_map/ppermute | solution.py:609
  42.7 2.3 %collective-permute-start.3 = (bf16[16,192,128]{2,1,0:T(8,128)(2,1)S(1)}, bf16[16,192,128]{2,1,0:T(8,128)(2,1)S(1)}, u32[]{:S(2)}, u32[]{:S(2)}) collective-permute-start(bf16[16,192,128]{2,1,0:T(8,128)(2,1)S(1)} %all-to-all-done.1.refs_1_.refs_5_), channel_id=1, source_target_pairs={{0,1},{1,0},{2,3},{3,2},{4,5},{5,4},{6,7},{7,6},{8,9},{9,8},{10,11... | collective-permute-start | bytes 2359304 | tf_op jit(solution)/shard_map/ppermute | solution.py:609
  43.3 9.7 %collective-permute-start.2 = (bf16[8,64,128]{2,1,0:T(8,128)(2,1)S(1)}, bf16[8,64,128]{2,1,0:T(8,128)(2,1)S(1)}, u32[]{:S(2)}, u32[]{:S(2)}) collective-permute-start(bf16[8,64,128]{2,1,0:T(8,128)(2,1)S(1)} %get-tuple-element.54), channel_id=1, source_target_pairs={{0,16},{8,24},{16,0},{24,8},{1,17},{9,25},{17,1},{25,9},{2,18},{10... | collective-permute-start | bytes 393224 | tf_op jit(solution)/shard_map/ppermute | solution.py:609
  53.8 10.7 %collective-permute-start.4 = (bf16[128,512]{1,0:T(8,128)(2,1)S(1)}, bf16[128,512]{1,0:T(8,128)(2,1)S(1)}, u32[]{:S(2)}, u32[]{:S(2)}) collective-permute-start(bf16[128,512]{1,0:T(8,128)(2,1)S(1)} %get-tuple-element.57.refs_1_), channel_id=1, source_target_pairs={{0,16},{8,24},{16,0},{24,8},{1,17},{9,25},{17,1},{25,9},{2,18},{10... | collective-permute-start | bytes 393224 | tf_op jit(solution)/shard_map/ppermute | solution.py:609
  53.8 13.3 %collective-permute-start.7 = (bf16[128,512]{1,0:T(8,128)(2,1)S(1)}, bf16[128,512]{1,0:T(8,128)(2,1)S(1)}, u32[]{:S(2)}, u32[]{:S(2)}) collective-permute-start(bf16[128,512]{1,0:T(8,128)(2,1)S(1)} %get-tuple-element.60), channel_id=1, source_target_pairs={{0,16},{8,24},{16,0},{24,8},{1,17},{9,25},{17,1},{25,9},{2,18},{10... | collective-permute-start | bytes 393224 | tf_op jit(solution)/shard_map/ppermute | solution.py:609
  56.8 10.5 %collective-permute-start.5 = (bf16[128,512]{1,0:T(8,128)(2,1)S(1)}, bf16[128,512]{1,0:T(8,128)(2,1)S(1)}, u32[]{:S(2)}, u32[]{:S(2)}) collective-permute-start(bf16[128,512]{1,0:T(8,128)(2,1)S(1)} %get-tuple-element.57.refs_1_), channel_id=1, source_target_pairs={{0,1},{1,0},{2,3},{3,2},{4,5},{5,4},{6,7},{7,6},{8,9},{9,8},{10,11... | collective-permute-start | bytes 393224 | tf_op jit(solution)/shard_map/ppermute | solution.py:609
  64.5 2.9 %collective-permute-start.6 = (bf16[128,512]{1,0:T(8,128)(2,1)S(1)}, bf16[128,512]{1,0:T(8,128)(2,1)S(1)}, u32[]{:S(2)}, u32[]{:S(2)}) collective-permute-start(bf16[128,512]{1,0:T(8,128)(2,1)S(1)} %collective-permute-done.4.refs_2_), channel_id=1, source_target_pairs={{0,1},{1,0},{2,3},{3,2},{4,5},{5,4},{6,7},{7,6},{8,9},{9,8},{10,11... | collective-permute-start | bytes 393224 | tf_op jit(solution)/shard_map/ppermute | solution.py:609
  69.1 16.9 %all-to-all-start.2 = ((bf16[16,128,128]{2,1,0:T(8,128)(2,1)}), bf16[16,128,128]{2,1,0:T(8,128)(2,1)S(1)}, u32[]{:S(2)}, u32[]{:S(2)}) async-start(bf16[16,128,128]{2,1,0:T(8,128)(2,1)} %shard_map.115), calls=%async_computation.2 | async-start | bytes 1048576 | tf_op jit(solution)/shard_map/all_to_all | solution.py:641
  72.7 30.7 %copy-start = (bf16[64,128,128]{2,1,0:T(8,128)(2,1)S(1)}, bf16[64,128,128]{2,1,0:T(8,128)(2,1)}, u32[]{:S(2)}) copy-start(bf16[64,128,128]{2,1,0:T(8,128)(2,1)} %refs_1_.11) | copy-start | bytes 6291460
  72.7 30.7 %copy-start.7 = (f32[64,128]{1,0:T(8,128)S(1)}, f32[64,128]{1,0:T(8,128)}, u32[]{:S(2)}) copy-start(f32[64,128]{1,0:T(8,128)} %get-tuple-element.67.refs_2_.refs_4_) | copy-start | bytes 98308
  72.8 30.6 %copy-start.8 = (f32[64,128]{1,0:T(8,128)S(1)}, f32[64,128]{1,0:T(8,128)}, u32[]{:S(2)}) copy-start(f32[64,128]{1,0:T(8,128)} %get-tuple-element.68.refs_3_.refs_5_) | copy-start | bytes 98308
  72.8 9.3 %collective-permute-start.8 = (bf16[128,512]{1,0:T(8,128)(2,1)S(1)}, bf16[128,512]{1,0:T(8,128)(2,1)S(1)}, u32[]{:S(2)}, u32[]{:S(2)}) collective-permute-start(bf16[128,512]{1,0:T(8,128)(2,1)S(1)} %shard_map.116.refs_1_), channel_id=1, source_target_pairs={{0,16},{8,24},{16,0},{24,8},{1,17},{9,25},{17,1},{25,9},{2,18},{10... | collective-permute-start | bytes 393224 | tf_op jit(solution)/shard_map/ppermute | solution.py:609
  73.6 8.5 %collective-permute-start.9 = (bf16[128,512]{1,0:T(8,128)(2,1)S(1)}, bf16[128,512]{1,0:T(8,128)(2,1)S(1)}, u32[]{:S(2)}, u32[]{:S(2)}) collective-permute-start(bf16[128,512]{1,0:T(8,128)(2,1)S(1)} %shard_map.116.refs_1_), channel_id=1, source_target_pairs={{0,1},{1,0},{2,3},{3,2},{4,5},{5,4},{6,7},{7,6},{8,9},{9,8},{10,11... | collective-permute-start | bytes 393224 | tf_op jit(solution)/shard_map/ppermute | solution.py:609
  82.0 1.3 collective-permute-start.10
  86.0 17.3 %all-to-all-start.3 = ((bf16[16,160,128]{2,1,0:T(8,128)(2,1)}), bf16[16,160,128]{2,1,0:T(8,128)(2,1)S(1)}, u32[]{:S(2)}, u32[]{:S(2)}) async-start(bf16[16,160,128]{2,1,0:T(8,128)(2,1)} %shard_map.117), calls=%async_computation.3 | async-start | bytes 1310720 | tf_op jit(solution)/shard_map/all_to_all | solution.py:641
  106.0 1.7 %collective-permute-start.11 = (bf16[4,32,1408]{2,1,0:T(8,128)(2,1)S(1)}, bf16[4,32,1408]{2,1,0:T(8,128)(2,1)S(1)}, u32[]{:S(2)}, u32[]{:S(2)}) collective-permute-start(bf16[4,32,1408]{2,1,0:T(8,128)(2,1)S(1)} %get-tuple-element.73), channel_id=1, source_target_pairs={{0,1},{1,0},{2,3},{3,2},{4,5},{5,4},{6,7},{7,6},{8,9},{9,8},{10,11... | collective-permute-start | bytes 1081352 | tf_op jit(solution)/shard_map/ppermute | solution.py:609
  108.4 7.9 %collective-permute-start.12 = (bf16[32,1408]{1,0:T(8,128)(2,1)S(1)}, bf16[32,1408]{1,0:T(8,128)(2,1)S(1)}, u32[]{:S(2)}, u32[]{:S(2)}) collective-permute-start(bf16[32,1408]{1,0:T(8,128)(2,1)S(1)} %get-tuple-element.74), channel_id=1, source_target_pairs={{0,2},{1,3},{2,0},{3,1},{4,6},{5,7},{6,4},{7,5},{8,10},{9,11},{10,... | collective-permute-start | bytes 270344 | tf_op jit(solution)/shard_map/ppermute | solution.py:609
  108.5 7.8 %collective-permute-start.13 = (bf16[32,1408]{1,0:T(8,128)(2,1)S(1)}, bf16[32,1408]{1,0:T(8,128)(2,1)S(1)}, u32[]{:S(2)}, u32[]{:S(2)}) collective-permute-start(bf16[32,1408]{1,0:T(8,128)(2,1)S(1)} %get-tuple-element.75), channel_id=1, source_target_pairs={{0,4},{1,5},{2,6},{3,7},{4,0},{5,1},{6,2},{7,3},{8,12},{9,13},{10,... | collective-permute-start | bytes 270344 | tf_op jit(solution)/shard_map/ppermute | solution.py:609
  109.5 6.8 %collective-permute-start.14 = (bf16[32,1408]{1,0:T(8,128)(2,1)S(1)}, bf16[32,1408]{1,0:T(8,128)(2,1)S(1)}, u32[]{:S(2)}, u32[]{:S(2)}) collective-permute-start(bf16[32,1408]{1,0:T(8,128)(2,1)S(1)} %get-tuple-element.76), channel_id=1, source_target_pairs={{0,6},{1,7},{2,4},{3,5},{4,2},{5,3},{6,0},{7,1},{8,14},{9,15},{10,... | collective-permute-start | bytes 270344 | tf_op jit(solution)/shard_map/ppermute | solution.py:609
  116.4 4.6 %collective-permute-start.15 = (bf16[32,1408]{1,0:T(8,128)(2,1)S(1)}, bf16[32,1408]{1,0:T(8,128)(2,1)S(1)}, u32[]{:S(2)}, u32[]{:S(2)}) collective-permute-start(bf16[32,1408]{1,0:T(8,128)(2,1)S(1)} %shard_map.124), channel_id=1, source_target_pairs={{0,8},{8,0},{16,24},{24,16},{1,9},{9,1},{17,25},{25,17},{2,10},{10... | collective-permute-start | bytes 270344 | tf_op jit(solution)/shard_map/ppermute | solution.py:609
  121.0 6.5 %collective-permute-start.16 = (bf16[32,1408]{1,0:T(8,128)(2,1)S(1)}, bf16[32,1408]{1,0:T(8,128)(2,1)S(1)}, u32[]{:S(2)}, u32[]{:S(2)}) collective-permute-start(bf16[32,1408]{1,0:T(8,128)(2,1)S(1)} %add_convert_fusion.1), channel_id=1, source_target_pairs={{0,16},{8,24},{16,0},{24,8},{1,17},{9,25},{17,1},{25,9},{2,18},{10... | collective-permute-start | bytes 270344 | tf_op jit(solution)/shard_map/ppermute | solution.py:609
  (8 other events, 72.3 us)

commit v13 on v9

--- a/solution.py
+++ b/solution.py
@@ -250,26 +250,37 @@
     arrive()
     columns, channels = pair_ref.shape[1], pair_ref.shape[2]
     weight = centred(weight_ref[...])
-    first = weight.astype(jnp.bfloat16)
-    second, third = two_terms(weight - first.astype(jnp.float32))
-    share = jnp.full((heads, channels), 1.0 / channels, jnp.bfloat16)
-    left = jnp.concatenate([first, second, third, share], axis=0)
-    average = jnp.full((channels, channels), 1.0 / channels, jnp.bfloat16)
+    first = weight.astype(jnp.bfloat16).astype(jnp.float32)
+    second, third = two_terms(weight - first)
+    share = jnp.full((heads, channels), 1.0 / channels, jnp.float32)
+    right = jnp.concatenate(
+        [
+            first, second.astype(jnp.float32), third.astype(jnp.float32), share,
+            jnp.zeros((channels - 4 * heads, channels), jnp.float32),
+        ],
+        axis=0,
+    ).T
+    row = lax.broadcasted_iota(jnp.int32, (channels, channels), 0)
+    column = lax.broadcasted_iota(jnp.int32, (channels, channels), 1)
+    less_mean = jnp.where(row == column, 1.0, 0.0) - 1.0 / channels
+    right = jnp.concatenate([less_mean, right], axis=1).astype(jnp.bfloat16)
+    shares = jnp.full((2 * channels, channels), 1.0 / channels, jnp.bfloat16)
     step_rows = 8
+    lane = lax.broadcasted_iota(jnp.int32, (step_rows * columns, channels), 1)
 
     def rows(step, carry):
         start = pl.multiple_of(step * step_rows, step_rows)
         entries = pair_ref[pl.ds(start, step_rows)].reshape(step_rows * columns, channels)
-        center = entries.astype(jnp.float32) - f32_dot(entries, average)
-        high, low = two_terms(center * center)
-        variance = f32_dot(share, high, NT) + f32_dot(share, low, NT)
-        spread = lax.rsqrt(variance + eps_norm)
-        raw = f32_dot(left, entries, NT)
-        bias = spread * (raw[:heads] + raw[heads : 2 * heads] + raw[2 * heads : 3 * heads])
+        both = f32_dot(entries, right)
+        center = both[:, :channels]
+        variance = f32_dot(jnp.concatenate(two_terms(center * center), axis=1), shares)
+        turned = jnp.where(lane < 4 * heads, both[:, channels:], variance).T
+        spread = lax.rsqrt(turned[4 * heads : 5 * heads] + eps_norm)
+        bias = spread * (turned[:heads] + turned[heads : 2 * heads] + turned[2 * heads : 3 * heads])
         for k in range(step_rows):
             lanes = slice(k * columns, (k + 1) * columns)
             bias_ref[:, start + k, :] = bias[:, lanes]
-            mean_ref[pl.ds(start + k, 1), :] = raw[3 * heads : 3 * heads + 1, lanes]
+            mean_ref[pl.ds(start + k, 1), :] = turned[3 * heads : 3 * heads + 1, lanes]
             spread_ref[pl.ds(start + k, 1), :] = spread[:1, lanes]
         return carry
 
@@ -532,6 +543,17 @@
     lax.fori_loop(0, pair_ref.shape[0] // 8, rows, 0)
 
 
+def output_kernel(parts_ref, combined_ref, out_weight_ref, pair_weight_ref):
+    width = combined_ref.shape[0]
+    rows = parts_ref.shape[1]
+    for h in range(parts_ref.shape[0]):
+        block = slice(h * rows, (h + 1) * rows)
+        part = parts_ref[h].astype(jnp.float32)
+        combined_ref[block, :] = part[:, : 4 * width]
+        out_weight_ref[block, :] = part[:, 4 * width : 5 * width]
+        pair_weight_ref[h : h + 1, :] = part[:1, 5 * width :]
+
+
 def call(kernel, outs, *args, scratch=(), place=None, flops=0, after=(), outside=0, late=0):
     whole, anywhere = pl.BlockSpec(memory_space=pltpu.VMEM), pl.BlockSpec(memory_space=pl.ANY)
     specs = [anywhere] * outside + [whole] * (len(args) - outside)
@@ -671,15 +693,17 @@
         return mine, far, swapped(mine, "res", 1), swapped(far, "res", 1)
 
     attended = products(with_near(probs, probs_far), value_blocks, 0, residues, False, 1.0)
-    attended, grad_other = lax.optimization_barrier((attended, grad_other))
+    attended, grad_sent = lax.optimization_barrier((attended, grad_sent))
     attended_blocks = across(attended)
+    grad_other = lax.optimization_barrier((attended, grad_other))[1]
     (grad_logits,) = call(
         softmax_gradient_kernel, [(quarter, bf16)], softmax_out, grad_mine, grad_other,
         flops=total * total,
     )
     grad_quarters = with_near(grad_logits, swapped(grad_logits, "seq", seq_half))
-    grad_quarters, attended_blocks = lax.optimization_barrier((grad_quarters, attended_blocks))
-    grad_blocks = across(products(grad_quarters, query_blocks, residues, 0, True, scale))
+    grad_sums = products(grad_quarters, query_blocks, residues, 0, True, scale)
+    grad_sums, attended_blocks = lax.optimization_barrier((grad_sums, attended_blocks))
+    grad_blocks = across(grad_sums)
 
     updated, value_gate, normed, attended_sums = call(
         attended_weight_kernel,
@@ -732,14 +756,18 @@
 
     part = added(part, swapped(part, "seq", 1))
     part = added(part, swapped(part, "seq", seq_half))
-    whole = lax.all_gather(part, "res", axis=0)
+    combined_gradient, output_gradient, pair_weight_gradient = call(
+        output_kernel,
+        [(wc.shape, f32), (wo.shape, f32), ((heads, channels), f32)],
+        lax.all_gather(part, "res", axis=0),
+    )
     return (
         updated,
         alignment_gradient,
         pair_gradient,
-        whole[:, :, : 4 * width].reshape(wc.shape).astype(f32),
-        whole[:, :, 4 * width : 5 * width].reshape(wo.shape).astype(f32),
-        whole[:, 0, 5 * width :].T.astype(f32),
+        combined_gradient,
+        output_gradient,
+        pair_weight_gradient.T,
     )
 
 

time: 141 us -> 142 us (level)
  starting transfers between devices: 33 us -> 38.3 us
  waiting for transfers between devices: 45.3 us -> 41.8 us
  other arithmetic: 2.57 us -> 0.13 us
  Pallas kernels: 29.8 us -> 31.3 us
    ppermute x16, starting transfers between devices: 16.7 us -> 20.6 us  [swapped(): lax.ppermute(mine, axis_name, [(a, a ^ distance) for a in range(size)])]
    all_to_all x3, waiting for transfers between devices: 10.5 us -> 7.83 us  [across(): lax.all_to_all(blocks, ('seq', 'res'), 0, 0, axis_index_groups=groups, ti...]
    convert_element_type x3 -> x0, other arithmetic: 2.45 us -> none  [the longest x1 1.12 us: head_body(): whole[:, :, :4 * width].reshape(wc.shape).astype(f32)]
    pallas_call x15 -> x16, Pallas kernels: 29.8 us -> 31.3 us  [call(): pl.pallas_call(wrapped, out_shape=shapes, in_specs=[pl.BlockSpec(memory_s...]
  transfers between devices with their start and end apart: 19 -> 19, of which waited for: 11 -> 11; matrix products, arithmetic and copies ran while one was open for 0% -> 0% of each run, Pallas kernels for 11% -> 12%
where the time goes in v13:
time: 142 us; the launch traced here: 141 us
  waiting for transfers between devices  41.8 us (29%)
  starting transfers between devices  38.3 us (27%)
  Pallas kernels  31.3 us (22%)
  blocking collectives  28.9 us (20%)
    ppermute x16, waiting for transfers between devices, swapped(): lax.ppermute(mine, axis_name, [(a, a ^ distance) for a in range(size)])  34 us
    pallas_call x16, Pallas kernels, call(): pl.pallas_call(wrapped, out_shape=shapes, in_specs=[pl.BlockSpec(memory_s...  31.3 us
    ppermute x16, starting transfers between devices, swapped(): lax.ppermute(mine, axis_name, [(a, a ^ distance) for a in range(size)])  20.6 us
    all_to_all x1, blocking collectives, across(): lax.all_to_all(blocks, ('seq', 'res'), 0, 0, axis_index_groups=groups, ti...  19.7 us
    all_to_all x3, starting transfers between devices, across(): lax.all_to_all(blocks, ('seq', 'res'), 0, 0, axis_index_groups=groups, ti...  17.7 us
    all_gather x1, blocking collectives, head_body(): lax.all_gather(part, 'res', axis=0)  9.25 us
    all_to_all x3, waiting for transfers between devices, across(): lax.all_to_all(blocks, ('seq', 'res'), 0, 0, axis_index_groups=groups, ti...  7.83 us
  transfers between devices with their start and end apart: 19, of which 11 were waited for; matrix products, arithmetic and copies ran while one was open for 0% of the time, Pallas kernels for 12%

profile of v13, /device:TPU:0, one launch (start us, length us, event | category | flops | bytes accessed | tf_op | source)
XLA Modules:
  0.0 141.3 jit_solution(6695958533596681360)
XLA Ops:
  0.6 8.4 %shard_map.109 = (bf16[16,192,128]{2,1,0:T(8,128)(2,1)}, f32[8,64,128]{2,1,0:T(8,128)}, f32[64,128]{1,0:T(8,128)}, f32[64,128]{1,0:T(8,128)}) custom-call(bf16[8,64,256]{2,1,0:T(8,128)(2,1)} %refs_0_.7, bf16[256,1024]{1,0:T(8,128)(2,1)} %refs_1_.10, bf16[64,128,128]{2,1,0:T(8,128)(2,1)} %refs_1_.11, f32[8,128]{1,0:T(8,128)} %bitcast.7), custom_call_target="tpu_custom_call" | custom-call | flops 268435456 | bytes 4001792 | tf_op jit(solution)/shard_map/pallas_call | solution.py:589
  9.1 19.7 %all_to_all.20.refs_1_.refs_5_ = bf16[16,192,128]{2,1,0:T(8,128)(2,1)S(1)} all-to-all(bf16[16,192,128]{2,1,0:T(8,128)(2,1)} %get-tuple-element.42), channel_id=1, replica_groups={{0,1,2,3,4,5,6,7,8,9,10,11,12,13,14,15},{16,17,18,19,20,21,22,23,24,25,..., dimensions={0} | all-to-all | bytes 1572864 | tf_op jit(solution)/shard_map/all_to_all | solution.py:638
  28.7 2.7 %shard_map.111 = bf16[16,128,128]{2,1,0:T(8,128)(2,1)} custom-call(bf16[8,64,256]{2,1,0:T(8,128)(2,1)} %refs_0_.7, bf16[8,64,256]{2,1,0:T(8,128)(2,1)} %refs_1_.8, bf16[256,1024]{1,0:T(8,128)(2,1)} %refs_1_.10, bf16[256,256]{1,0:T(8,128)(2,1)} %refs_3_.3), custom_call_target="tpu_custom_call" | custom-call | flops 268435456 | bytes 1703936 | tf_op jit(solution)/shard_map/pallas_call | solution.py:589
  32.6 3.6 %all-to-all-start.1 = ((bf16[16,128,128]{2,1,0:T(8,128)(2,1)}), bf16[16,128,128]{2,1,0:T(8,128)(2,1)S(1)}, u32[]{:S(2)}, u32[]{:S(2)}) async-start(bf16[16,128,128]{2,1,0:T(8,128)(2,1)} %shard_map.111), calls=%async_computation.1 | async-start | bytes 1048576 | tf_op jit(solution)/shard_map/all_to_all | solution.py:638
  36.2 2.7 %collective-permute-start.1 = (f32[128,512]{1,0:T(8,128)S(1)}, f32[128,512]{1,0:T(8,128)S(1)}, u32[]{:S(2)}, u32[]{:S(2)}) collective-permute-start(f32[128,512]{1,0:T(8,128)S(1)} %get-tuple-element.45), channel_id=1, source_target_pairs={{0,16},{8,24},{16,0},{24,8},{1,17},{9,25},{17,1},{25,9},{2,18},{10... | collective-permute-start | bytes 786440 | tf_op jit(solution)/shard_map/ppermute | solution.py:606
  38.8 9.5 %collective-permute-done.1.refs_1_ = f32[128,512]{1,0:T(8,128)S(1)} collective-permute-done((f32[128,512]{1,0:T(8,128)S(1)}, f32[128,512]{1,0:T(8,128)S(1)}, u32[]{:S(2)}, u32[]{:S(2)}) %collective-permute-start.1) | collective-permute-done | bytes 262176 | tf_op jit(solution)/shard_map/ppermute | solution.py:606
  48.6 3.5 %collective-permute-start.2 = (bf16[128,512]{1,0:T(8,128)(2,1)S(1)}, bf16[128,512]{1,0:T(8,128)(2,1)S(1)}, u32[]{:S(2)}, u32[]{:S(2)}) collective-permute-start(bf16[128,512]{1,0:T(8,128)(2,1)S(1)} %get-tuple-element.48.refs_1_), channel_id=1, source_target_pairs={{0,16},{8,24},{16,0},{24,8},{1,17},{9,25},{17,1},{25,9},{2,18},{10... | collective-permute-start | bytes 393224 | tf_op jit(solution)/shard_map/ppermute | solution.py:606
  52.1 3.4 %collective-permute-done.2.refs_2_ = bf16[128,512]{1,0:T(8,128)(2,1)S(1)} collective-permute-done((bf16[128,512]{1,0:T(8,128)(2,1)S(1)}, bf16[128,512]{1,0:T(8,128)(2,1)S(1)}, u32[]{:S(2)}, u32[]{:S(2)}) %collective-permute-start.2) | collective-permute-done | bytes 131104 | tf_op jit(solution)/shard_map/ppermute | solution.py:606
  57.8 1.8 %shard_map.114 = bf16[16,128,128]{2,1,0:T(8,128)(2,1)} custom-call(s32[3]{0:T(128)S(1)} %pad_add_fusion.refs_0_, bf16[128,512]{1,0:T(8,128)(2,1)S(1)} %get-tuple-element.48.refs_1_, bf16[128,512]{1,0:T(8,128)(2,1)S(1)} %collective-permute-done.2.refs_2_, bf16[128,512]{1,0:T(8,128)(2,1)S(1)} %collective-permute-done.4.refs_3_, ...), custom_call_target="tpu_custom_call" | custom-call | flops 268435456 | bytes 1572864 | tf_op jit(solution)/shard_map/pallas_call | solution.py:589
  60.6 7.0 %all-to-all-start.2 = ((bf16[16,128,128]{2,1,0:T(8,128)(2,1)}), bf16[16,128,128]{2,1,0:T(8,128)(2,1)S(1)}, u32[]{:S(2)}, u32[]{:S(2)}) async-start(bf16[16,128,128]{2,1,0:T(8,128)(2,1)} %shard_map.114), calls=%async_computation.2 | async-start | bytes 1048576 | tf_op jit(solution)/shard_map/all_to_all | solution.py:638
  67.6 3.2 %collective-permute-start.6 = (bf16[128,512]{1,0:T(8,128)(2,1)S(1)}, bf16[128,512]{1,0:T(8,128)(2,1)S(1)}, u32[]{:S(2)}, u32[]{:S(2)}) collective-permute-start(bf16[128,512]{1,0:T(8,128)(2,1)S(1)} %get-tuple-element.52), channel_id=1, source_target_pairs={{0,16},{8,24},{16,0},{24,8},{1,17},{9,25},{17,1},{25,9},{2,18},{10... | collective-permute-start | bytes 393224 | tf_op jit(solution)/shard_map/ppermute | solution.py:606
  70.8 6.3 %collective-permute-done.6.refs_2_ = bf16[128,512]{1,0:T(8,128)(2,1)S(1)} collective-permute-done((bf16[128,512]{1,0:T(8,128)(2,1)S(1)}, bf16[128,512]{1,0:T(8,128)(2,1)S(1)}, u32[]{:S(2)}, u32[]{:S(2)}) %collective-permute-start.6) | collective-permute-done | bytes 131104 | tf_op jit(solution)/shard_map/ppermute | solution.py:606
  77.3 3.5 %collective-permute-start.7 = (bf16[128,512]{1,0:T(8,128)(2,1)S(1)}, bf16[128,512]{1,0:T(8,128)(2,1)S(1)}, u32[]{:S(2)}, u32[]{:S(2)}) collective-permute-start(bf16[128,512]{1,0:T(8,128)(2,1)S(1)} %shard_map.115.refs_1_), channel_id=1, source_target_pairs={{0,16},{8,24},{16,0},{24,8},{1,17},{9,25},{17,1},{25,9},{2,18},{10... | collective-permute-start | bytes 393224 | tf_op jit(solution)/shard_map/ppermute | solution.py:606
  80.8 3.8 %collective-permute-done.7.refs_2_ = bf16[128,512]{1,0:T(8,128)(2,1)S(1)} collective-permute-done((bf16[128,512]{1,0:T(8,128)(2,1)S(1)}, bf16[128,512]{1,0:T(8,128)(2,1)S(1)}, u32[]{:S(2)}, u32[]{:S(2)}) %collective-permute-start.7) | collective-permute-done | bytes 131104 | tf_op jit(solution)/shard_map/ppermute | solution.py:606
  85.9 1.9 %shard_map.116 = bf16[16,160,128]{2,1,0:T(8,128)(2,1)} custom-call(s32[3]{0:T(128)S(1)} %pad_add_fusion.refs_0_, bf16[128,512]{1,0:T(8,128)(2,1)S(1)} %shard_map.115.refs_1_, bf16[128,512]{1,0:T(8,128)(2,1)S(1)} %collective-permute-done.7.refs_2_, bf16[128,512]{1,0:T(8,128)(2,1)S(1)} %collective-permute-done.8.refs_3_, ...), custom_call_target="tpu_custom_call" | custom-call | flops 268435456 | bytes 1966080 | tf_op jit(solution)/shard_map/pallas_call | solution.py:589
  87.8 7.1 %all-to-all-start.3 = ((bf16[16,160,128]{2,1,0:T(8,128)(2,1)}), bf16[16,160,128]{2,1,0:T(8,128)(2,1)S(1)}, u32[]{:S(2)}, u32[]{:S(2)}) async-start(bf16[16,160,128]{2,1,0:T(8,128)(2,1)} %shard_map.116), calls=%async_computation.3 | async-start | bytes 1310720 | tf_op jit(solution)/shard_map/all_to_all | solution.py:638
  94.9 4.1 %shard_map.117 = (bf16[8,64,256]{2,1,0:T(8,128)(2,1)}, bf16[512,512]{1,0:T(8,128)(2,1)}, bf16[512,256]{1,0:T(8,128)(2,1)}, bf16[256,768]{1,0:T(8,128)(2,1)}) custom-call(bf16[8,64,256]{2,1,0:T(8,128)(2,1)} %refs_0_.7, bf16[8,64,256]{2,1,0:T(8,128)(2,1)} %refs_1_.8, bf16[256,1024]{1,0:T(8,128)(2,1)} %refs_1_.10, bf16[256,256]{1,0:T(8,128)(2,1)} %refs_3_.3, ...), custom_call_target="tpu_custom_call" | custom-call | flops 469762048 | bytes 3145728 | tf_op jit(solution)/shard_map/pallas_call | solution.py:589
  99.0 7.8 %all-to-all-done.3.refs_0_.refs_2_ = bf16[16,160,128]{2,1,0:T(8,128)(2,1)S(1)} async-done(((bf16[16,160,128]{2,1,0:T(8,128)(2,1)}), bf16[16,160,128]{2,1,0:T(8,128)(2,1)S(1)}, u32[]{:S(2)}, u32[]{:S(2)}) %all-to-all-start.3) | async-done | bytes 655392 | tf_op jit(solution)/shard_map/all_to_all | solution.py:638
  113.0 2.5 %collective-permute-start.13 = (bf16[32,1408]{1,0:T(8,128)(2,1)S(1)}, bf16[32,1408]{1,0:T(8,128)(2,1)S(1)}, u32[]{:S(2)}, u32[]{:S(2)}) collective-permute-start(bf16[32,1408]{1,0:T(8,128)(2,1)S(1)} %get-tuple-element.68), channel_id=1, source_target_pairs={{0,6},{1,7},{2,4},{3,5},{4,2},{5,3},{6,0},{7,1},{8,14},{9,15},{10,... | collective-permute-start | bytes 270344 | tf_op jit(solution)/shard_map/ppermute | solution.py:606
  115.5 4.3 %shard_map.122 = bf16[64,128,128]{2,1,0:T(8,128)(2,1)} custom-call(bf16[16,160,128]{2,1,0:T(8,128)(2,1)S(1)} %all-to-all-done.3.refs_0_.refs_2_, bf16[64,128,128]{2,1,0:T(8,128)(2,1)S(1)} %copy-done, f32[8,128]{1,0:T(8,128)S(1)} %bitcast.8, f32[8,64,128]{2,1,0:T(8,128)S(1)} %copy-done.5, f32[64,128]{1,0:T(8,128)S(1)} %copy-done.7, f32[64,128]{1,0:T(8,128)S(1)} %copy-done.8), custom_call_target="tpu_custom_call" | custom-call | flops 268435456 | bytes 5181440 | tf_op jit(solution)/shard_map/pallas_call | solution.py:589
  120.5 4.0 %collective-permute-done.14 = bf16[32,1408]{1,0:T(8,128)(2,1)S(1)} collective-permute-done((bf16[32,1408]{1,0:T(8,128)(2,1)S(1)}, bf16[32,1408]{1,0:T(8,128)(2,1)S(1)}, u32[]{:S(2)}, u32[]{:S(2)}) %collective-permute-start.14) | collective-permute-done | bytes 90144 | tf_op jit(solution)/shard_map/ppermute | solution.py:606
  124.5 3.0 %collective-permute-start.15 = (bf16[32,1408]{1,0:T(8,128)(2,1)S(1)}, bf16[32,1408]{1,0:T(8,128)(2,1)S(1)}, u32[]{:S(2)}, u32[]{:S(2)}) collective-permute-start(bf16[32,1408]{1,0:T(8,128)(2,1)S(1)} %add_convert_fusion.1), channel_id=1, source_target_pairs={{0,16},{8,24},{16,0},{24,8},{1,17},{9,25},{17,1},{25,9},{2,18},{10... | collective-permute-start | bytes 270344 | tf_op jit(solution)/shard_map/ppermute | solution.py:606
  128.8 2.2 %collective-permute-done.15 = bf16[32,1408]{1,0:T(8,128)(2,1)S(1)} collective-permute-done((bf16[32,1408]{1,0:T(8,128)(2,1)S(1)}, bf16[32,1408]{1,0:T(8,128)(2,1)S(1)}, u32[]{:S(2)}, u32[]{:S(2)}) %collective-permute-start.15) | collective-permute-done | bytes 90144 | tf_op jit(solution)/shard_map/ppermute | solution.py:606
  131.0 9.3 %all-gather = bf16[256,1408]{1,0:T(8,128)(2,1)S(1)} all-gather(bf16[32,1408]{1,0:T(8,128)(2,1)S(1)} %add_convert_fusion), channel_id=2, replica_groups=mesh['seq'=4,'res'=8] {'res'}, dimensions={0}, use_global_device_ids=true | all-gather | bytes 811008 | tf_op jit(solution)/shard_map/all_gather | solution.py:762
  (57 shorter events, 15.3 us)
Async XLA Ops:
  28.7 2.8 %collective-permute-start = (bf16[16,192,128]{2,1,0:T(8,128)(2,1)S(1)}, bf16[16,192,128]{2,1,0:T(8,128)(2,1)S(1)}, u32[]{:S(2)}, u32[]{:S(2)}) collective-permute-start(bf16[16,192,128]{2,1,0:T(8,128)(2,1)S(1)} %all_to_all.20.refs_1_.refs_5_), channel_id=1, source_target_pairs={{0,1},{1,0},{2,3},{3,2},{4,5},{5,4},{6,7},{7,6},{8,9},{9,8},{10,11... | collective-permute-start | bytes 2359304 | tf_op jit(solution)/shard_map/ppermute | solution.py:606
  32.6 22.9 %all-to-all-start.1 = ((bf16[16,128,128]{2,1,0:T(8,128)(2,1)}), bf16[16,128,128]{2,1,0:T(8,128)(2,1)S(1)}, u32[]{:S(2)}, u32[]{:S(2)}) async-start(bf16[16,128,128]{2,1,0:T(8,128)(2,1)} %shard_map.111), calls=%async_computation.1 | async-start | bytes 1048576 | tf_op jit(solution)/shard_map/all_to_all | solution.py:638
  36.2 12.2 %collective-permute-start.1 = (f32[128,512]{1,0:T(8,128)S(1)}, f32[128,512]{1,0:T(8,128)S(1)}, u32[]{:S(2)}, u32[]{:S(2)}) collective-permute-start(f32[128,512]{1,0:T(8,128)S(1)} %get-tuple-element.45), channel_id=1, source_target_pairs={{0,16},{8,24},{16,0},{24,8},{1,17},{9,25},{17,1},{25,9},{2,18},{10... | collective-permute-start | bytes 786440 | tf_op jit(solution)/shard_map/ppermute | solution.py:606
  48.6 6.9 %collective-permute-start.2 = (bf16[128,512]{1,0:T(8,128)(2,1)S(1)}, bf16[128,512]{1,0:T(8,128)(2,1)S(1)}, u32[]{:S(2)}, u32[]{:S(2)}) collective-permute-start(bf16[128,512]{1,0:T(8,128)(2,1)S(1)} %get-tuple-element.48.refs_1_), channel_id=1, source_target_pairs={{0,16},{8,24},{16,0},{24,8},{1,17},{9,25},{17,1},{25,9},{2,18},{10... | collective-permute-start | bytes 393224 | tf_op jit(solution)/shard_map/ppermute | solution.py:606
  55.5 4.1 %collective-permute-start.3 = (bf16[16,128,128]{2,1,0:T(8,128)(2,1)S(1)}, bf16[16,128,128]{2,1,0:T(8,128)(2,1)S(1)}, u32[]{:S(2)}, u32[]{:S(2)}) collective-permute-start(bf16[16,128,128]{2,1,0:T(8,128)(2,1)S(1)} %all-to-all-done.1.refs_1_.refs_5_), channel_id=1, source_target_pairs={{0,1},{1,0},{2,3},{3,2},{4,5},{5,4},{6,7},{7,6},{8,9},{9,8},{10,11... | collective-permute-start | bytes 1572872 | tf_op jit(solution)/shard_map/ppermute | solution.py:606
  55.5 2.1 %collective-permute-start.4 = (bf16[128,512]{1,0:T(8,128)(2,1)S(1)}, bf16[128,512]{1,0:T(8,128)(2,1)S(1)}, u32[]{:S(2)}, u32[]{:S(2)}) collective-permute-start(bf16[128,512]{1,0:T(8,128)(2,1)S(1)} %get-tuple-element.48.refs_1_), channel_id=1, source_target_pairs={{0,1},{1,0},{2,3},{3,2},{4,5},{5,4},{6,7},{7,6},{8,9},{9,8},{10,11... | collective-permute-start | bytes 393224 | tf_op jit(solution)/shard_map/ppermute | solution.py:606
  56.0 1.8 %collective-permute-start.5 = (bf16[128,512]{1,0:T(8,128)(2,1)S(1)}, bf16[128,512]{1,0:T(8,128)(2,1)S(1)}, u32[]{:S(2)}, u32[]{:S(2)}) collective-permute-start(bf16[128,512]{1,0:T(8,128)(2,1)S(1)} %collective-permute-done.2.refs_2_), channel_id=1, source_target_pairs={{0,1},{1,0},{2,3},{3,2},{4,5},{5,4},{6,7},{7,6},{8,9},{9,8},{10,11... | collective-permute-start | bytes 393224 | tf_op jit(solution)/shard_map/ppermute | solution.py:606
  60.6 27.2 %all-to-all-start.2 = ((bf16[16,128,128]{2,1,0:T(8,128)(2,1)}), bf16[16,128,128]{2,1,0:T(8,128)(2,1)S(1)}, u32[]{:S(2)}, u32[]{:S(2)}) async-start(bf16[16,128,128]{2,1,0:T(8,128)(2,1)} %shard_map.114), calls=%async_computation.2 | async-start | bytes 1048576 | tf_op jit(solution)/shard_map/all_to_all | solution.py:638
  67.6 9.5 %collective-permute-start.6 = (bf16[128,512]{1,0:T(8,128)(2,1)S(1)}, bf16[128,512]{1,0:T(8,128)(2,1)S(1)}, u32[]{:S(2)}, u32[]{:S(2)}) collective-permute-start(bf16[128,512]{1,0:T(8,128)(2,1)S(1)} %get-tuple-element.52), channel_id=1, source_target_pairs={{0,16},{8,24},{16,0},{24,8},{1,17},{9,25},{17,1},{25,9},{2,18},{10... | collective-permute-start | bytes 393224 | tf_op jit(solution)/shard_map/ppermute | solution.py:606
  77.2 29.6 %copy-start = (bf16[64,128,128]{2,1,0:T(8,128)(2,1)S(1)}, bf16[64,128,128]{2,1,0:T(8,128)(2,1)}, u32[]{:S(2)}) copy-start(bf16[64,128,128]{2,1,0:T(8,128)(2,1)} %refs_1_.11) | copy-start | bytes 6291460
  77.2 29.6 %copy-start.7 = (f32[64,128]{1,0:T(8,128)S(1)}, f32[64,128]{1,0:T(8,128)}, u32[]{:S(2)}) copy-start(f32[64,128]{1,0:T(8,128)} %get-tuple-element.59.refs_2_.refs_4_) | copy-start | bytes 98308
  77.2 29.6 %copy-start.8 = (f32[64,128]{1,0:T(8,128)S(1)}, f32[64,128]{1,0:T(8,128)}, u32[]{:S(2)}) copy-start(f32[64,128]{1,0:T(8,128)} %get-tuple-element.60.refs_3_.refs_5_) | copy-start | bytes 98308
  77.3 7.3 %collective-permute-start.7 = (bf16[128,512]{1,0:T(8,128)(2,1)S(1)}, bf16[128,512]{1,0:T(8,128)(2,1)S(1)}, u32[]{:S(2)}, u32[]{:S(2)}) collective-permute-start(bf16[128,512]{1,0:T(8,128)(2,1)S(1)} %shard_map.115.refs_1_), channel_id=1, source_target_pairs={{0,16},{8,24},{16,0},{24,8},{1,17},{9,25},{17,1},{25,9},{2,18},{10... | collective-permute-start | bytes 393224 | tf_op jit(solution)/shard_map/ppermute | solution.py:606
  80.8 3.8 %collective-permute-start.8 = (bf16[128,512]{1,0:T(8,128)(2,1)S(1)}, bf16[128,512]{1,0:T(8,128)(2,1)S(1)}, u32[]{:S(2)}, u32[]{:S(2)}) collective-permute-start(bf16[128,512]{1,0:T(8,128)(2,1)S(1)} %shard_map.115.refs_1_), channel_id=1, source_target_pairs={{0,1},{1,0},{2,3},{3,2},{4,5},{5,4},{6,7},{7,6},{8,9},{9,8},{10,11... | collective-permute-start | bytes 393224 | tf_op jit(solution)/shard_map/ppermute | solution.py:606
  84.6 1.3 collective-permute-start.9
  87.8 19.1 %all-to-all-start.3 = ((bf16[16,160,128]{2,1,0:T(8,128)(2,1)}), bf16[16,160,128]{2,1,0:T(8,128)(2,1)S(1)}, u32[]{:S(2)}, u32[]{:S(2)}) async-start(bf16[16,160,128]{2,1,0:T(8,128)(2,1)} %shard_map.116), calls=%async_computation.3 | async-start | bytes 1310720 | tf_op jit(solution)/shard_map/all_to_all | solution.py:638
  109.5 1.7 %collective-permute-start.10 = (bf16[4,32,1408]{2,1,0:T(8,128)(2,1)S(1)}, bf16[4,32,1408]{2,1,0:T(8,128)(2,1)S(1)}, u32[]{:S(2)}, u32[]{:S(2)}) collective-permute-start(bf16[4,32,1408]{2,1,0:T(8,128)(2,1)S(1)} %get-tuple-element.65), channel_id=1, source_target_pairs={{0,1},{1,0},{2,3},{3,2},{4,5},{5,4},{6,7},{7,6},{8,9},{9,8},{10,11... | collective-permute-start | bytes 1081352 | tf_op jit(solution)/shard_map/ppermute | solution.py:606
  111.9 7.9 %collective-permute-start.11 = (bf16[32,1408]{1,0:T(8,128)(2,1)S(1)}, bf16[32,1408]{1,0:T(8,128)(2,1)S(1)}, u32[]{:S(2)}, u32[]{:S(2)}) collective-permute-start(bf16[32,1408]{1,0:T(8,128)(2,1)S(1)} %get-tuple-element.66), channel_id=1, source_target_pairs={{0,2},{1,3},{2,0},{3,1},{4,6},{5,7},{6,4},{7,5},{8,10},{9,11},{10,... | collective-permute-start | bytes 270344 | tf_op jit(solution)/shard_map/ppermute | solution.py:606
  112.0 7.8 %collective-permute-start.12 = (bf16[32,1408]{1,0:T(8,128)(2,1)S(1)}, bf16[32,1408]{1,0:T(8,128)(2,1)S(1)}, u32[]{:S(2)}, u32[]{:S(2)}) collective-permute-start(bf16[32,1408]{1,0:T(8,128)(2,1)S(1)} %get-tuple-element.67), channel_id=1, source_target_pairs={{0,4},{1,5},{2,6},{3,7},{4,0},{5,1},{6,2},{7,3},{8,12},{9,13},{10,... | collective-permute-start | bytes 270344 | tf_op jit(solution)/shard_map/ppermute | solution.py:606
  113.0 6.8 %collective-permute-start.13 = (bf16[32,1408]{1,0:T(8,128)(2,1)S(1)}, bf16[32,1408]{1,0:T(8,128)(2,1)S(1)}, u32[]{:S(2)}, u32[]{:S(2)}) collective-permute-start(bf16[32,1408]{1,0:T(8,128)(2,1)S(1)} %get-tuple-element.68), channel_id=1, source_target_pairs={{0,6},{1,7},{2,4},{3,5},{4,2},{5,3},{6,0},{7,1},{8,14},{9,15},{10,... | collective-permute-start | bytes 270344 | tf_op jit(solution)/shard_map/ppermute | solution.py:606
  115.5 12.0 %copy-start.1 = (bf16[256,1024]{1,0:T(8,128)(2,1)S(1)}, bf16[256,1024]{1,0:T(8,128)(2,1)}, u32[]{:S(2)}) copy-start(bf16[256,1024]{1,0:T(8,128)(2,1)} %refs_1_.10) | copy-start | bytes 1572868
  115.5 12.0 %copy-start.2 = (bf16[8,64,256]{2,1,0:T(8,128)(2,1)S(1)}, bf16[8,64,256]{2,1,0:T(8,128)(2,1)}, u32[]{:S(2)}) copy-start(bf16[8,64,256]{2,1,0:T(8,128)(2,1)} %refs_0_.7) | copy-start | bytes 786436
  119.9 4.6 %collective-permute-start.14 = (bf16[32,1408]{1,0:T(8,128)(2,1)S(1)}, bf16[32,1408]{1,0:T(8,128)(2,1)S(1)}, u32[]{:S(2)}, u32[]{:S(2)}) collective-permute-start(bf16[32,1408]{1,0:T(8,128)(2,1)S(1)} %shard_map.123), channel_id=1, source_target_pairs={{0,8},{8,0},{16,24},{24,16},{1,9},{9,1},{17,25},{25,17},{2,10},{10... | collective-permute-start | bytes 270344 | tf_op jit(solution)/shard_map/ppermute | solution.py:606
  124.5 6.5 %collective-permute-start.15 = (bf16[32,1408]{1,0:T(8,128)(2,1)S(1)}, bf16[32,1408]{1,0:T(8,128)(2,1)S(1)}, u32[]{:S(2)}, u32[]{:S(2)}) collective-permute-start(bf16[32,1408]{1,0:T(8,128)(2,1)S(1)} %add_convert_fusion.1), channel_id=1, source_target_pairs={{0,16},{8,24},{16,0},{24,8},{1,17},{9,25},{17,1},{25,9},{2,18},{10... | collective-permute-start | bytes 270344 | tf_op jit(solution)/shard_map/ppermute | solution.py:606
  (6 other events, 55.0 us)

commit v14 on v9

--- a/solution.py
+++ b/solution.py
@@ -532,6 +532,17 @@
     lax.fori_loop(0, pair_ref.shape[0] // 8, rows, 0)
 
 
+def output_kernel(parts_ref, combined_ref, out_weight_ref, pair_weight_ref):
+    width = combined_ref.shape[0]
+    rows = parts_ref.shape[1]
+    for h in range(parts_ref.shape[0]):
+        block = slice(h * rows, (h + 1) * rows)
+        part = parts_ref[h].astype(jnp.float32)
+        combined_ref[block, :] = part[:, : 4 * width]
+        out_weight_ref[block, :] = part[:, 4 * width : 5 * width]
+        pair_weight_ref[h : h + 1, :] = part[:1, 5 * width :]
+
+
 def call(kernel, outs, *args, scratch=(), place=None, flops=0, after=(), outside=0, late=0):
     whole, anywhere = pl.BlockSpec(memory_space=pltpu.VMEM), pl.BlockSpec(memory_space=pl.ANY)
     specs = [anywhere] * outside + [whole] * (len(args) - outside)
@@ -628,6 +639,13 @@
         flops=8 * tokens * width * width, outside=3, late=1,
     )
     query_blocks = across(query_blocks)
+    (value_blocks,) = call(
+        value_kernel, [((group, 2 * residues, LANES), bf16)], x, grad, wc, wo,
+        flops=8 * tokens * width * width, outside=4,
+    )
+    query_blocks, value_blocks = lax.optimization_barrier((query_blocks, value_blocks))
+    value_blocks = across(value_blocks)
+
     def scores(blocks, left_row, right_row, with_bias, kind):
         return call(
             functools.partial(score_kernel, residues, left_row, right_row, with_bias),
@@ -636,21 +654,15 @@
             place=place, flops=2 * total * total * width,
         )
 
-    (value_blocks,) = call(
-        value_kernel, [((group, 2 * residues, LANES), bf16)], x, grad, wc, wo,
-        flops=8 * tokens * width * width, outside=4,
-    )
     logit_mine, logit_sent = scores(query_blocks, 0, residues, True, f32)
-    value_blocks, logit_sent = lax.optimization_barrier((value_blocks, logit_sent))
     logit_other = swapped(logit_sent, "seq", seq_half)
-    value_blocks = across(value_blocks)
     quarter = (total // 4, total)
     softmax_out, probs = call(
         softmax_kernel, [(quarter, f32), (quarter, bf16)], logit_mine, logit_other,
         flops=total * total,
     )
+    value_blocks, probs = lax.optimization_barrier((value_blocks, probs))
     probs_far = swapped(probs, "seq", seq_half)
-    value_blocks, probs_far = lax.optimization_barrier((value_blocks, probs_far))
     grad_mine, grad_sent = scores(value_blocks, residues, 0, False, bf16)
     grad_other = swapped(grad_sent, "seq", seq_half)
 
@@ -678,8 +690,9 @@
         flops=total * total,
     )
     grad_quarters = with_near(grad_logits, swapped(grad_logits, "seq", seq_half))
-    grad_quarters, attended_blocks = lax.optimization_barrier((grad_quarters, attended_blocks))
-    grad_blocks = across(products(grad_quarters, query_blocks, residues, 0, True, scale))
+    grad_sums = products(grad_quarters, query_blocks, residues, 0, True, scale)
+    grad_sums, attended_blocks = lax.optimization_barrier((grad_sums, attended_blocks))
+    grad_blocks = across(grad_sums)
 
     updated, value_gate, normed, attended_sums = call(
         attended_weight_kernel,
@@ -720,26 +733,32 @@
         grad_blocks, pair_entries, pair_weight.T, bias, mean, spread,
         scratch=[share], flops=8 * tokens * width * width,
     )
-    received, pair_gradient = lax.optimization_barrier((received, pair_gradient))
-    (part,) = call(plane_sum_kernel, [((rows, columns), bf16)], own, *received)
     (alignment_gradient,) = call(
         alignment_kernel, [(x.shape, bf16)], x, wc, query_key, value_gate,
         flops=8 * tokens * width * width,
     )
+    received, alignment_gradient = lax.optimization_barrier((received, alignment_gradient))
+    (part,) = call(plane_sum_kernel, [((rows, columns), bf16)], own, *received)
 
     def added(mine, other):
         return (mine.astype(f32) + other.astype(f32)).astype(bf16)
 
     part = added(part, swapped(part, "seq", 1))
-    part = added(part, swapped(part, "seq", seq_half))
-    whole = lax.all_gather(part, "res", axis=0)
+    other_half = swapped(part, "seq", seq_half)
+    other_half, pair_gradient = lax.optimization_barrier((other_half, pair_gradient))
+    part = added(part, other_half)
+    combined_gradient, output_gradient, pair_weight_gradient = call(
+        output_kernel,
+        [(wc.shape, f32), (wo.shape, f32), ((heads, channels), f32)],
+        lax.all_gather(part, "res", axis=0),
+    )
     return (
         updated,
         alignment_gradient,
         pair_gradient,
-        whole[:, :, : 4 * width].reshape(wc.shape).astype(f32),
-        whole[:, :, 4 * width : 5 * width].reshape(wo.shape).astype(f32),
-        whole[:, 0, 5 * width :].T.astype(f32),
+        combined_gradient,
+        output_gradient,
+        pair_weight_gradient.T,
     )
 
 

time: 141 us -> 139 us (0.986)
  blocking collectives: 28.9 us -> 11.1 us
  waiting for transfers between devices: 45.3 us -> 63 us
  other arithmetic: 2.57 us -> 0.13 us
    all_to_all x1 -> x0, blocking collectives: 19.7 us -> none  [across(): lax.all_to_all(blocks, ('seq', 'res'), 0, 0, axis_index_groups=groups, ti...]
    all_to_all x3 -> x4, waiting for transfers between devices: 10.5 us -> 22.8 us  [across(): lax.all_to_all(blocks, ('seq', 'res'), 0, 0, axis_index_groups=groups, ti...]
    ppermute x16, starting transfers between devices: 16.7 us -> 10.7 us  [swapped(): lax.ppermute(mine, axis_name, [(a, a ^ distance) for a in range(size)])]
    ppermute x16, waiting for transfers between devices: 34.7 us -> 40.2 us  [swapped(): lax.ppermute(mine, axis_name, [(a, a ^ distance) for a in range(size)])]
    all_to_all x3 -> x4, starting transfers between devices: 16.4 us -> 21.3 us  [across(): lax.all_to_all(blocks, ('seq', 'res'), 0, 0, axis_index_groups=groups, ti...]
    convert_element_type x3 -> x0, other arithmetic: 2.45 us -> none  [the longest x1 1.12 us: head_body(): whole[:, :, :4 * width].reshape(wc.shape).astype(f32)]
    all_gather x1, blocking collectives: 9.25 us -> 11.1 us  [head_body(): lax.all_gather(part, 'res', axis=0)]
    pallas_call x15 -> x16, Pallas kernels: 29.8 us -> 30.9 us  [call(): pl.pallas_call(wrapped, out_shape=shapes, in_specs=[pl.BlockSpec(memory_s...]
  transfers between devices with their start and end apart: 19 -> 20, of which waited for: 11 -> 15; matrix products, arithmetic and copies ran while one was open for 0% -> 0% of each run, Pallas kernels for 11% -> 13%
where the time goes in v14:
time: 139 us; the launch traced here: 138 us
  waiting for transfers between devices  63 us (45%)
  starting transfers between devices  32 us (23%)
  Pallas kernels  30.9 us (22%)
  blocking collectives  11.1 us (8%)
    ppermute x16, waiting for transfers between devices, swapped(): lax.ppermute(mine, axis_name, [(a, a ^ distance) for a in range(size)])  40.2 us
    pallas_call x16, Pallas kernels, call(): pl.pallas_call(wrapped, out_shape=shapes, in_specs=[pl.BlockSpec(memory_s...  30.9 us
    all_to_all x4, waiting for transfers between devices, across(): lax.all_to_all(blocks, ('seq', 'res'), 0, 0, axis_index_groups=groups, ti...  22.8 us
    all_to_all x4, starting transfers between devices, across(): lax.all_to_all(blocks, ('seq', 'res'), 0, 0, axis_index_groups=groups, ti...  21.3 us
    all_gather x1, blocking collectives, head_body(): lax.all_gather(part, 'res', axis=0)  11.1 us
    ppermute x16, starting transfers between devices, swapped(): lax.ppermute(mine, axis_name, [(a, a ^ distance) for a in range(size)])  10.7 us
  transfers between devices with their start and end apart: 20, of which 15 were waited for; matrix products, arithmetic and copies ran while one was open for 0% of the time, Pallas kernels for 13%

profile of v14, /device:TPU:0, one launch (start us, length us, event | category | flops | bytes accessed | tf_op | source)
XLA Modules:
  0.0 138.2 jit_solution(498312218630565716)
XLA Ops:
  0.6 8.1 %shard_map.109 = (bf16[16,192,128]{2,1,0:T(8,128)(2,1)}, f32[8,64,128]{2,1,0:T(8,128)}, f32[64,128]{1,0:T(8,128)}, f32[64,128]{1,0:T(8,128)}) custom-call(bf16[8,64,256]{2,1,0:T(8,128)(2,1)} %refs_0_.7, bf16[256,1024]{1,0:T(8,128)(2,1)} %refs_1_.10, bf16[64,128,128]{2,1,0:T(8,128)(2,1)} %refs_1_.11, f32[8,128]{1,0:T(8,128)} %bitcast.7), custom_call_target="tpu_custom_call" | custom-call | flops 268435456 | bytes 4001792 | tf_op jit(solution)/shard_map/pallas_call | solution.py:578
  8.7 6.3 %all-to-all-start = ((bf16[16,192,128]{2,1,0:T(8,128)(2,1)}), bf16[16,192,128]{2,1,0:T(8,128)(2,1)S(1)}, u32[]{:S(2)}, u32[]{:S(2)}) async-start(bf16[16,192,128]{2,1,0:T(8,128)(2,1)} %get-tuple-element.44), calls=%async_computation | async-start | bytes 1572864 | tf_op jit(solution)/shard_map/all_to_all | solution.py:627
  15.0 2.7 %shard_map.110 = bf16[16,128,128]{2,1,0:T(8,128)(2,1)} custom-call(bf16[8,64,256]{2,1,0:T(8,128)(2,1)} %refs_0_.7, bf16[8,64,256]{2,1,0:T(8,128)(2,1)} %refs_1_.8, bf16[256,1024]{1,0:T(8,128)(2,1)} %refs_1_.10, bf16[256,256]{1,0:T(8,128)(2,1)} %refs_3_.3), custom_call_target="tpu_custom_call" | custom-call | flops 268435456 | bytes 1703936 | tf_op jit(solution)/shard_map/pallas_call | solution.py:578
  17.7 10.6 %all-to-all-done.refs_1_.refs_5_ = bf16[16,192,128]{2,1,0:T(8,128)(2,1)S(1)} async-done(((bf16[16,192,128]{2,1,0:T(8,128)(2,1)}), bf16[16,192,128]{2,1,0:T(8,128)(2,1)S(1)}, u32[]{:S(2)}, u32[]{:S(2)}) %all-to-all-start) | async-done | bytes 786464 | tf_op jit(solution)/shard_map/all_to_all | solution.py:627
  28.4 3.6 %all-to-all-start.1 = ((bf16[16,128,128]{2,1,0:T(8,128)(2,1)}), bf16[16,128,128]{2,1,0:T(8,128)(2,1)S(1)}, u32[]{:S(2)}, u32[]{:S(2)}) async-start(bf16[16,128,128]{2,1,0:T(8,128)(2,1)} %shard_map.110), calls=%async_computation.1 | async-start | bytes 1048576 | tf_op jit(solution)/shard_map/all_to_all | solution.py:627
  33.1 2.7 %collective-permute-start.1 = (f32[128,512]{1,0:T(8,128)S(1)}, f32[128,512]{1,0:T(8,128)S(1)}, u32[]{:S(2)}, u32[]{:S(2)}) collective-permute-start(f32[128,512]{1,0:T(8,128)S(1)} %get-tuple-element.47), channel_id=1, source_target_pairs={{0,16},{8,24},{16,0},{24,8},{1,17},{9,25},{17,1},{25,9},{2,18},{10... | collective-permute-start | bytes 786440 | tf_op jit(solution)/shard_map/ppermute | solution.py:595
  35.8 8.4 %collective-permute-done.1.refs_1_ = f32[128,512]{1,0:T(8,128)S(1)} collective-permute-done((f32[128,512]{1,0:T(8,128)S(1)}, f32[128,512]{1,0:T(8,128)S(1)}, u32[]{:S(2)}, u32[]{:S(2)}) %collective-permute-start.1) | collective-permute-done | bytes 262176 | tf_op jit(solution)/shard_map/ppermute | solution.py:595
  44.3 3.7 %all-to-all-done.1.refs_1_.refs_5_ = bf16[16,128,128]{2,1,0:T(8,128)(2,1)S(1)} async-done(((bf16[16,128,128]{2,1,0:T(8,128)(2,1)}), bf16[16,128,128]{2,1,0:T(8,128)(2,1)S(1)}, u32[]{:S(2)}, u32[]{:S(2)}) %all-to-all-start.1) | async-done | bytes 524320 | tf_op jit(solution)/shard_map/all_to_all | solution.py:627
  48.6 9.1 %collective-permute-done.3.refs_2_ = bf16[128,512]{1,0:T(8,128)(2,1)S(1)} collective-permute-done((bf16[128,512]{1,0:T(8,128)(2,1)S(1)}, bf16[128,512]{1,0:T(8,128)(2,1)S(1)}, u32[]{:S(2)}, u32[]{:S(2)}) %collective-permute-start.3) | collective-permute-done | bytes 131104 | tf_op jit(solution)/shard_map/ppermute | solution.py:595
  59.0 1.8 %shard_map.114 = bf16[16,128,128]{2,1,0:T(8,128)(2,1)} custom-call(s32[3]{0:T(128)S(1)} %pad_add_fusion.refs_0_, bf16[128,512]{1,0:T(8,128)(2,1)S(1)} %get-tuple-element.53.refs_1_, bf16[128,512]{1,0:T(8,128)(2,1)S(1)} %collective-permute-done.3.refs_2_, bf16[128,512]{1,0:T(8,128)(2,1)S(1)} %collective-permute-done.4.refs_3_, ...), custom_call_target="tpu_custom_call" | custom-call | flops 268435456 | bytes 1572864 | tf_op jit(solution)/shard_map/pallas_call | solution.py:578
  60.8 6.4 %collective-permute-done.6.refs_2_ = bf16[128,512]{1,0:T(8,128)(2,1)S(1)} collective-permute-done((bf16[128,512]{1,0:T(8,128)(2,1)S(1)}, bf16[128,512]{1,0:T(8,128)(2,1)S(1)}, u32[]{:S(2)}, u32[]{:S(2)}) %collective-permute-start.6) | collective-permute-done | bytes 131104 | tf_op jit(solution)/shard_map/ppermute | solution.py:595
  67.2 4.1 %all-to-all-start.2 = ((bf16[16,128,128]{2,1,0:T(8,128)(2,1)}), bf16[16,128,128]{2,1,0:T(8,128)(2,1)S(1)}, u32[]{:S(2)}, u32[]{:S(2)}) async-start(bf16[16,128,128]{2,1,0:T(8,128)(2,1)} %shard_map.114), calls=%async_computation.2 | async-start | bytes 1048576 | tf_op jit(solution)/shard_map/all_to_all | solution.py:627
  71.5 2.7 %collective-permute-start.7 = (bf16[128,512]{1,0:T(8,128)(2,1)S(1)}, bf16[128,512]{1,0:T(8,128)(2,1)S(1)}, u32[]{:S(2)}, u32[]{:S(2)}) collective-permute-start(bf16[128,512]{1,0:T(8,128)(2,1)S(1)} %shard_map.115.refs_1_), channel_id=1, source_target_pairs={{0,16},{8,24},{16,0},{24,8},{1,17},{9,25},{17,1},{25,9},{2,18},{10... | collective-permute-start | bytes 393224 | tf_op jit(solution)/shard_map/ppermute | solution.py:595
  74.4 6.4 %collective-permute-done.7.refs_2_ = bf16[128,512]{1,0:T(8,128)(2,1)S(1)} collective-permute-done((bf16[128,512]{1,0:T(8,128)(2,1)S(1)}, bf16[128,512]{1,0:T(8,128)(2,1)S(1)}, u32[]{:S(2)}, u32[]{:S(2)}) %collective-permute-start.7) | collective-permute-done | bytes 131104 | tf_op jit(solution)/shard_map/ppermute | solution.py:595
  82.1 1.9 %shard_map.116 = bf16[16,160,128]{2,1,0:T(8,128)(2,1)} custom-call(s32[3]{0:T(128)S(1)} %pad_add_fusion.refs_0_, bf16[128,512]{1,0:T(8,128)(2,1)S(1)} %shard_map.115.refs_1_, bf16[128,512]{1,0:T(8,128)(2,1)S(1)} %collective-permute-done.7.refs_2_, bf16[128,512]{1,0:T(8,128)(2,1)S(1)} %collective-permute-done.8.refs_3_, ...), custom_call_target="tpu_custom_call" | custom-call | flops 268435456 | bytes 1966080 | tf_op jit(solution)/shard_map/pallas_call | solution.py:578
  84.7 7.3 %all-to-all-start.3 = ((bf16[16,160,128]{2,1,0:T(8,128)(2,1)}), bf16[16,160,128]{2,1,0:T(8,128)(2,1)S(1)}, u32[]{:S(2)}, u32[]{:S(2)}) async-start(bf16[16,160,128]{2,1,0:T(8,128)(2,1)} %shard_map.116), calls=%async_computation.3 | async-start | bytes 1310720 | tf_op jit(solution)/shard_map/all_to_all | solution.py:627
  92.0 4.1 %shard_map.117 = (bf16[8,64,256]{2,1,0:T(8,128)(2,1)}, bf16[512,512]{1,0:T(8,128)(2,1)}, bf16[512,256]{1,0:T(8,128)(2,1)}, bf16[256,768]{1,0:T(8,128)(2,1)}) custom-call(bf16[8,64,256]{2,1,0:T(8,128)(2,1)} %refs_0_.7, bf16[8,64,256]{2,1,0:T(8,128)(2,1)} %refs_1_.8, bf16[256,1024]{1,0:T(8,128)(2,1)} %refs_1_.10, bf16[256,256]{1,0:T(8,128)(2,1)} %refs_3_.3, ...), custom_call_target="tpu_custom_call" | custom-call | flops 469762048 | bytes 3145728 | tf_op jit(solution)/shard_map/pallas_call | solution.py:578
  96.1 7.8 %all-to-all-done.3.refs_0_.refs_2_ = bf16[16,160,128]{2,1,0:T(8,128)(2,1)S(1)} async-done(((bf16[16,160,128]{2,1,0:T(8,128)(2,1)}), bf16[16,160,128]{2,1,0:T(8,128)(2,1)S(1)}, u32[]{:S(2)}, u32[]{:S(2)}) %all-to-all-start.3) | async-done | bytes 655392 | tf_op jit(solution)/shard_map/all_to_all | solution.py:627
  104.0 1.5 %shard_map.118.refs_3_ = f32[8,128]{1,0:T(8,128)S(1)} custom-call(bf16[16,160,128]{2,1,0:T(8,128)(2,1)S(1)} %all-to-all-done.3.refs_0_.refs_2_, bf16[64,128,128]{2,1,0:T(8,128)(2,1)S(1)} %copy-done, f32[64,128]{1,0:T(8,128)S(1)} %copy-done.7, f32[64,128]{1,0:T(8,128)S(1)} %copy-done.8), custom_call_target="tpu_custom_call" | custom-call | flops 134217728 | bytes 2822144 | tf_op jit(solution)/shard_map/pallas_call | solution.py:578
  106.7 1.7 %collective-permute-done.10.refs_2_ = bf16[4,32,1408]{2,1,0:T(8,128)(2,1)S(1)} collective-permute-done((bf16[4,32,1408]{2,1,0:T(8,128)(2,1)S(1)}, bf16[4,32,1408]{2,1,0:T(8,128)(2,1)S(1)}, u32[]{:S(2)}, u32[]{:S(2)}) %collective-permute-start.10) | collective-permute-done | bytes 360480 | tf_op jit(solution)/shard_map/ppermute | solution.py:595
  110.1 2.5 %collective-permute-start.13 = (bf16[32,1408]{1,0:T(8,128)(2,1)S(1)}, bf16[32,1408]{1,0:T(8,128)(2,1)S(1)}, u32[]{:S(2)}, u32[]{:S(2)}) collective-permute-start(bf16[32,1408]{1,0:T(8,128)(2,1)S(1)} %get-tuple-element.68), channel_id=1, source_target_pairs={{0,6},{1,7},{2,4},{3,5},{4,2},{5,3},{6,0},{7,1},{8,14},{9,15},{10,... | collective-permute-start | bytes 270344 | tf_op jit(solution)/shard_map/ppermute | solution.py:595
  116.7 3.7 %collective-permute-done.14 = bf16[32,1408]{1,0:T(8,128)(2,1)S(1)} collective-permute-done((bf16[32,1408]{1,0:T(8,128)(2,1)S(1)}, bf16[32,1408]{1,0:T(8,128)(2,1)S(1)}, u32[]{:S(2)}, u32[]{:S(2)}) %collective-permute-start.14) | collective-permute-done | bytes 90144 | tf_op jit(solution)/shard_map/ppermute | solution.py:595
  120.5 4.3 %shard_map.123 = bf16[64,128,128]{2,1,0:T(8,128)(2,1)} custom-call(bf16[16,160,128]{2,1,0:T(8,128)(2,1)S(1)} %all-to-all-done.3.refs_0_.refs_2_, bf16[64,128,128]{2,1,0:T(8,128)(2,1)S(1)} %copy-done, f32[8,128]{1,0:T(8,128)S(1)} %bitcast.8, f32[8,64,128]{2,1,0:T(8,128)S(1)} %copy-done.5, f32[64,128]{1,0:T(8,128)S(1)} %copy-done.7, f32[64,128]{1,0:T(8,128)S(1)} %copy-done.8), custom_call_target="tpu_custom_call" | custom-call | flops 268435456 | bytes 5181440 | tf_op jit(solution)/shard_map/pallas_call | solution.py:578
  125.9 11.1 %all-gather = bf16[256,1408]{1,0:T(8,128)(2,1)S(1)} all-gather(bf16[32,1408]{1,0:T(8,128)(2,1)S(1)} %add_convert_fusion), channel_id=2, replica_groups=mesh['seq'=4,'res'=8] {'res'}, dimensions={0}, use_global_device_ids=true | all-gather | bytes 811008 | tf_op jit(solution)/shard_map/all_gather | solution.py:753
  (58 shorter events, 14.9 us)
Async XLA Ops:
  8.7 19.7 %all-to-all-start = ((bf16[16,192,128]{2,1,0:T(8,128)(2,1)}), bf16[16,192,128]{2,1,0:T(8,128)(2,1)S(1)}, u32[]{:S(2)}, u32[]{:S(2)}) async-start(bf16[16,192,128]{2,1,0:T(8,128)(2,1)} %get-tuple-element.44), calls=%async_computation | async-start | bytes 1572864 | tf_op jit(solution)/shard_map/all_to_all | solution.py:627
  28.4 3.7 %collective-permute-start = (bf16[16,192,128]{2,1,0:T(8,128)(2,1)S(1)}, bf16[16,192,128]{2,1,0:T(8,128)(2,1)S(1)}, u32[]{:S(2)}, u32[]{:S(2)}) collective-permute-start(bf16[16,192,128]{2,1,0:T(8,128)(2,1)S(1)} %all-to-all-done.refs_1_.refs_5_), channel_id=1, source_target_pairs={{0,1},{1,0},{2,3},{3,2},{4,5},{5,4},{6,7},{7,6},{8,9},{9,8},{10,11... | collective-permute-start | bytes 2359304 | tf_op jit(solution)/shard_map/ppermute | solution.py:595
  28.4 19.7 %all-to-all-start.1 = ((bf16[16,128,128]{2,1,0:T(8,128)(2,1)}), bf16[16,128,128]{2,1,0:T(8,128)(2,1)S(1)}, u32[]{:S(2)}, u32[]{:S(2)}) async-start(bf16[16,128,128]{2,1,0:T(8,128)(2,1)} %shard_map.110), calls=%async_computation.1 | async-start | bytes 1048576 | tf_op jit(solution)/shard_map/all_to_all | solution.py:627
  33.1 11.0 %collective-permute-start.1 = (f32[128,512]{1,0:T(8,128)S(1)}, f32[128,512]{1,0:T(8,128)S(1)}, u32[]{:S(2)}, u32[]{:S(2)}) collective-permute-start(f32[128,512]{1,0:T(8,128)S(1)} %get-tuple-element.47), channel_id=1, source_target_pairs={{0,16},{8,24},{16,0},{24,8},{1,17},{9,25},{17,1},{25,9},{2,18},{10... | collective-permute-start | bytes 786440 | tf_op jit(solution)/shard_map/ppermute | solution.py:595
  48.1 9.6 %collective-permute-start.2 = (bf16[16,128,128]{2,1,0:T(8,128)(2,1)S(1)}, bf16[16,128,128]{2,1,0:T(8,128)(2,1)S(1)}, u32[]{:S(2)}, u32[]{:S(2)}) collective-permute-start(bf16[16,128,128]{2,1,0:T(8,128)(2,1)S(1)} %all-to-all-done.1.refs_1_.refs_5_), channel_id=1, source_target_pairs={{0,1},{1,0},{2,3},{3,2},{4,5},{5,4},{6,7},{7,6},{8,9},{9,8},{10,11... | collective-permute-start | bytes 1572872 | tf_op jit(solution)/shard_map/ppermute | solution.py:595
  48.1 9.6 %collective-permute-start.3 = (bf16[128,512]{1,0:T(8,128)(2,1)S(1)}, bf16[128,512]{1,0:T(8,128)(2,1)S(1)}, u32[]{:S(2)}, u32[]{:S(2)}) collective-permute-start(bf16[128,512]{1,0:T(8,128)(2,1)S(1)} %get-tuple-element.53.refs_1_), channel_id=1, source_target_pairs={{0,16},{8,24},{16,0},{24,8},{1,17},{9,25},{17,1},{25,9},{2,18},{10... | collective-permute-start | bytes 393224 | tf_op jit(solution)/shard_map/ppermute | solution.py:595
  48.1 10.7 %collective-permute-start.4 = (bf16[128,512]{1,0:T(8,128)(2,1)S(1)}, bf16[128,512]{1,0:T(8,128)(2,1)S(1)}, u32[]{:S(2)}, u32[]{:S(2)}) collective-permute-start(bf16[128,512]{1,0:T(8,128)(2,1)S(1)} %get-tuple-element.53.refs_1_), channel_id=1, source_target_pairs={{0,1},{1,0},{2,3},{3,2},{4,5},{5,4},{6,7},{7,6},{8,9},{9,8},{10,11... | collective-permute-start | bytes 393224 | tf_op jit(solution)/shard_map/ppermute | solution.py:595
  57.7 1.3 collective-permute-start.5
  58.7 8.5 %collective-permute-start.6 = (bf16[128,512]{1,0:T(8,128)(2,1)S(1)}, bf16[128,512]{1,0:T(8,128)(2,1)S(1)}, u32[]{:S(2)}, u32[]{:S(2)}) collective-permute-start(bf16[128,512]{1,0:T(8,128)(2,1)S(1)} %get-tuple-element.54), channel_id=1, source_target_pairs={{0,16},{8,24},{16,0},{24,8},{1,17},{9,25},{17,1},{25,9},{2,18},{10... | collective-permute-start | bytes 393224 | tf_op jit(solution)/shard_map/ppermute | solution.py:595
  67.2 17.5 %all-to-all-start.2 = ((bf16[16,128,128]{2,1,0:T(8,128)(2,1)}), bf16[16,128,128]{2,1,0:T(8,128)(2,1)S(1)}, u32[]{:S(2)}, u32[]{:S(2)}) async-start(bf16[16,128,128]{2,1,0:T(8,128)(2,1)} %shard_map.114), calls=%async_computation.2 | async-start | bytes 1048576 | tf_op jit(solution)/shard_map/all_to_all | solution.py:627
  71.5 32.5 %copy-start = (bf16[64,128,128]{2,1,0:T(8,128)(2,1)S(1)}, bf16[64,128,128]{2,1,0:T(8,128)(2,1)}, u32[]{:S(2)}) copy-start(bf16[64,128,128]{2,1,0:T(8,128)(2,1)} %refs_1_.11) | copy-start | bytes 6291460
  71.5 32.4 %copy-start.7 = (f32[64,128]{1,0:T(8,128)S(1)}, f32[64,128]{1,0:T(8,128)}, u32[]{:S(2)}) copy-start(f32[64,128]{1,0:T(8,128)} %get-tuple-element.61.refs_2_.refs_4_) | copy-start | bytes 98308
  71.5 32.4 %copy-start.8 = (f32[64,128]{1,0:T(8,128)S(1)}, f32[64,128]{1,0:T(8,128)}, u32[]{:S(2)}) copy-start(f32[64,128]{1,0:T(8,128)} %get-tuple-element.62.refs_3_.refs_5_) | copy-start | bytes 98308
  71.5 9.3 %collective-permute-start.7 = (bf16[128,512]{1,0:T(8,128)(2,1)S(1)}, bf16[128,512]{1,0:T(8,128)(2,1)S(1)}, u32[]{:S(2)}, u32[]{:S(2)}) collective-permute-start(bf16[128,512]{1,0:T(8,128)(2,1)S(1)} %shard_map.115.refs_1_), channel_id=1, source_target_pairs={{0,16},{8,24},{16,0},{24,8},{1,17},{9,25},{17,1},{25,9},{2,18},{10... | collective-permute-start | bytes 393224 | tf_op jit(solution)/shard_map/ppermute | solution.py:595
  74.2 6.6 %collective-permute-start.8 = (bf16[128,512]{1,0:T(8,128)(2,1)S(1)}, bf16[128,512]{1,0:T(8,128)(2,1)S(1)}, u32[]{:S(2)}, u32[]{:S(2)}) collective-permute-start(bf16[128,512]{1,0:T(8,128)(2,1)S(1)} %shard_map.115.refs_1_), channel_id=1, source_target_pairs={{0,1},{1,0},{2,3},{3,2},{4,5},{5,4},{6,7},{7,6},{8,9},{9,8},{10,11... | collective-permute-start | bytes 393224 | tf_op jit(solution)/shard_map/ppermute | solution.py:595
  80.8 1.3 collective-permute-start.9
  84.7 19.2 %all-to-all-start.3 = ((bf16[16,160,128]{2,1,0:T(8,128)(2,1)}), bf16[16,160,128]{2,1,0:T(8,128)(2,1)S(1)}, u32[]{:S(2)}, u32[]{:S(2)}) async-start(bf16[16,160,128]{2,1,0:T(8,128)(2,1)} %shard_map.116), calls=%async_computation.3 | async-start | bytes 1310720 | tf_op jit(solution)/shard_map/all_to_all | solution.py:627
  106.6 13.9 %copy-start.5 = (f32[8,64,128]{2,1,0:T(8,128)S(1)}, f32[8,64,128]{2,1,0:T(8,128)}, u32[]{:S(2)}) copy-start(f32[8,64,128]{2,1,0:T(8,128)} %get-tuple-element.76.refs_3_) | copy-start | bytes 786436
  106.6 1.7 %collective-permute-start.10 = (bf16[4,32,1408]{2,1,0:T(8,128)(2,1)S(1)}, bf16[4,32,1408]{2,1,0:T(8,128)(2,1)S(1)}, u32[]{:S(2)}, u32[]{:S(2)}) collective-permute-start(bf16[4,32,1408]{2,1,0:T(8,128)(2,1)S(1)} %get-tuple-element.65), channel_id=1, source_target_pairs={{0,1},{1,0},{2,3},{3,2},{4,5},{5,4},{6,7},{7,6},{8,9},{9,8},{10,11... | collective-permute-start | bytes 1081352 | tf_op jit(solution)/shard_map/ppermute | solution.py:595
  109.0 5.4 %collective-permute-start.11 = (bf16[32,1408]{1,0:T(8,128)(2,1)S(1)}, bf16[32,1408]{1,0:T(8,128)(2,1)S(1)}, u32[]{:S(2)}, u32[]{:S(2)}) collective-permute-start(bf16[32,1408]{1,0:T(8,128)(2,1)S(1)} %get-tuple-element.66), channel_id=1, source_target_pairs={{0,2},{1,3},{2,0},{3,1},{4,6},{5,7},{6,4},{7,5},{8,10},{9,11},{10,... | collective-permute-start | bytes 270344 | tf_op jit(solution)/shard_map/ppermute | solution.py:595
  109.1 6.7 %collective-permute-start.12 = (bf16[32,1408]{1,0:T(8,128)(2,1)S(1)}, bf16[32,1408]{1,0:T(8,128)(2,1)S(1)}, u32[]{:S(2)}, u32[]{:S(2)}) collective-permute-start(bf16[32,1408]{1,0:T(8,128)(2,1)S(1)} %get-tuple-element.67), channel_id=1, source_target_pairs={{0,4},{1,5},{2,6},{3,7},{4,0},{5,1},{6,2},{7,3},{8,12},{9,13},{10,... | collective-permute-start | bytes 270344 | tf_op jit(solution)/shard_map/ppermute | solution.py:595
  110.1 5.6 %collective-permute-start.13 = (bf16[32,1408]{1,0:T(8,128)(2,1)S(1)}, bf16[32,1408]{1,0:T(8,128)(2,1)S(1)}, u32[]{:S(2)}, u32[]{:S(2)}) collective-permute-start(bf16[32,1408]{1,0:T(8,128)(2,1)S(1)} %get-tuple-element.68), channel_id=1, source_target_pairs={{0,6},{1,7},{2,4},{3,5},{4,2},{5,3},{6,0},{7,1},{8,14},{9,15},{10,... | collective-permute-start | bytes 270344 | tf_op jit(solution)/shard_map/ppermute | solution.py:595
  115.8 4.6 %collective-permute-start.14 = (bf16[32,1408]{1,0:T(8,128)(2,1)S(1)}, bf16[32,1408]{1,0:T(8,128)(2,1)S(1)}, u32[]{:S(2)}, u32[]{:S(2)}) collective-permute-start(bf16[32,1408]{1,0:T(8,128)(2,1)S(1)} %shard_map.122), channel_id=1, source_target_pairs={{0,8},{8,0},{16,24},{24,16},{1,9},{9,1},{17,25},{25,17},{2,10},{10... | collective-permute-start | bytes 270344 | tf_op jit(solution)/shard_map/ppermute | solution.py:595
  120.4 5.5 %collective-permute-start.15 = (bf16[32,1408]{1,0:T(8,128)(2,1)S(1)}, bf16[32,1408]{1,0:T(8,128)(2,1)S(1)}, u32[]{:S(2)}, u32[]{:S(2)}) collective-permute-start(bf16[32,1408]{1,0:T(8,128)(2,1)S(1)} %add_convert_fusion.1), channel_id=1, source_target_pairs={{0,16},{8,24},{16,0},{24,8},{1,17},{9,25},{17,1},{25,9},{2,18},{10... | collective-permute-start | bytes 270344 | tf_op jit(solution)/shard_map/ppermute | solution.py:595
  (7 other events, 65.8 us)

commit v15 on v14

--- a/solution.py
+++ b/solution.py
@@ -255,7 +255,7 @@
     share = jnp.full((heads, channels), 1.0 / channels, jnp.bfloat16)
     left = jnp.concatenate([first, second, third, share], axis=0)
     average = jnp.full((channels, channels), 1.0 / channels, jnp.bfloat16)
-    step_rows = 8
+    step_rows = 16
 
     def rows(step, carry):
         start = pl.multiple_of(step * step_rows, step_rows)
@@ -408,7 +408,7 @@
 
 
 def query_weight_kernel(
-    place_ref, normed_ref, blocks_ref, pair_weight_ref, attended_sums_ref,
+    place_ref, normed_ref, blocks_ref, attended_sums_ref,
     projected_ref, keep_ref, send_ref, sums_ref,
 ):
     width = normed_ref.shape[1]
@@ -421,17 +421,10 @@
     sums_ref[:, : 2 * width] = f32_dot(normed_ref[...], projected_ref[...], TN).astype(
         jnp.bfloat16
     )
-    sums_ref[:, 2 * width : 5 * width] = attended_sums_ref[...]
-    heads, channels = pair_weight_ref.shape
-    rows = sums_ref.shape[0] // heads
-    first = lax.broadcasted_iota(jnp.int32, (rows, channels), 0) == 0
-    for h in range(heads):
-        row = jnp.broadcast_to(pair_weight_ref[h : h + 1], (rows, channels))
-        sums_ref[h * rows : (h + 1) * rows, 5 * width :] = jnp.where(first, row, 0.0).astype(
-            jnp.bfloat16
-        )
+    sums_ref[:, 2 * width :] = attended_sums_ref[...]
+    rows = keep_ref.shape[1]
     for which, ref in ((core, keep_ref), (1 - core, send_ref)):
-        for block in range(heads // 2):
+        for block in range(keep_ref.shape[0]):
             start = pl.multiple_of((2 * block + which) * rows, rows)
             ref[block] = sums_ref[pl.ds(start, rows), :]
 
@@ -444,11 +437,18 @@
         ref[...] = total.astype(ref.dtype)
 
 
-def plane_sum_kernel(own_ref, *refs):
+def plane_sum_kernel(own_ref, pair_weight_ref, *refs):
+    *received, out_ref = refs
     total = own_ref[...]
-    for ref in refs[:-1]:
+    for ref in received:
         total += ref[...].astype(jnp.float32)
-    refs[-1][...] = total.astype(refs[-1].dtype)
+    count = own_ref.shape[1]
+    heads = pair_weight_ref.shape[0]
+    out_ref[:, :count] = total.astype(out_ref.dtype)
+    rest = jnp.zeros((out_ref.shape[0] - heads, out_ref.shape[1] - count), jnp.float32)
+    out_ref[:, count:] = jnp.concatenate([pair_weight_ref[...], rest], axis=0).astype(
+        out_ref.dtype
+    )
 
 
 def pair_weight_kernel(blocks_ref, pair_ref, mean_ref, spread_ref, out_ref, share_ref):
@@ -540,7 +540,8 @@
         part = parts_ref[h].astype(jnp.float32)
         combined_ref[block, :] = part[:, : 4 * width]
         out_weight_ref[block, :] = part[:, 4 * width : 5 * width]
-        pair_weight_ref[h : h + 1, :] = part[:1, 5 * width :]
+        share = part[: pair_weight_ref.shape[0], 5 * width :]
+        pair_weight_ref[...] = share if h == 0 else pair_weight_ref[...] + share
 
 
 def call(kernel, outs, *args, scratch=(), place=None, flops=0, after=(), outside=0, late=0):
@@ -665,6 +666,7 @@
     probs_far = swapped(probs, "seq", seq_half)
     grad_mine, grad_sent = scores(value_blocks, residues, 0, False, bf16)
     grad_other = swapped(grad_sent, "seq", seq_half)
+    probs_far = lax.optimization_barrier((probs_far, grad_sent))[0]
 
     def products(quarters, blocks, first_row, second_row, with_share, factor):
         rows = 2 * residues + (residues // 2 if with_share else 0)
@@ -683,8 +685,8 @@
         return mine, far, swapped(mine, "res", 1), swapped(far, "res", 1)
 
     attended = products(with_near(probs, probs_far), value_blocks, 0, residues, False, 1.0)
-    attended, grad_other = lax.optimization_barrier((attended, grad_other))
     attended_blocks = across(attended)
+    grad_other = lax.optimization_barrier((attended, grad_other))[1]
     (grad_logits,) = call(
         softmax_gradient_kernel, [(quarter, bf16)], softmax_out, grad_mine, grad_other,
         flops=total * total,
@@ -706,18 +708,13 @@
         flops=14 * tokens * width * width, outside=4,
     )
     share = pltpu.VMEM((heads, residues, LANES), f32)
-    (pair_weight_part,) = call(
-        pair_weight_kernel, [((heads, channels), f32)],
-        grad_blocks, pair_entries, mean, spread,
-        scratch=[share], flops=4 * tokens * width * width,
-    )
-    columns = 5 * width + channels
+    columns = 5 * width
     rows = width // res_size
     part_rows = ((res_size // 2, rows, columns), bf16)
     query_key, keep, send = call(
         query_weight_kernel,
         [((tokens, 2 * width), bf16), part_rows, part_rows],
-        normed, grad_blocks, pair_weight_part, attended_sums,
+        normed, grad_blocks, attended_sums,
         scratch=[pltpu.VMEM((width, columns), bf16)],
         place=place, flops=4 * tokens * width * width,
     )
@@ -727,23 +724,32 @@
         keep, swapped(send, "res", 1), place=place,
     )
     received = [swapped(t, "res", 2 * flip) for flip, t in enumerate(sent, 1)]
+    (pair_weight_part,) = call(
+        pair_weight_kernel, [((heads, channels), f32)],
+        grad_blocks, pair_entries, mean, spread,
+        scratch=[share], flops=4 * tokens * width * width, after=(sent[0],),
+    )
     (pair_gradient,) = call(
         functools.partial(pair_kernel, 2 * residues),
         [(pair_entries.shape, bf16)],
         grad_blocks, pair_entries, pair_weight.T, bias, mean, spread,
         scratch=[share], flops=8 * tokens * width * width,
     )
+    received, pair_weight_part = lax.optimization_barrier((received, pair_weight_part))
+    (part,) = call(
+        plane_sum_kernel, [((rows, columns + channels), bf16)], own, pair_weight_part, *received
+    )
     (alignment_gradient,) = call(
         alignment_kernel, [(x.shape, bf16)], x, wc, query_key, value_gate,
         flops=8 * tokens * width * width,
     )
-    received, alignment_gradient = lax.optimization_barrier((received, alignment_gradient))
-    (part,) = call(plane_sum_kernel, [((rows, columns), bf16)], own, *received)
 
     def added(mine, other):
         return (mine.astype(f32) + other.astype(f32)).astype(bf16)
 
-    part = added(part, swapped(part, "seq", 1))
+    other_plane = swapped(part, "seq", 1)
+    other_plane, alignment_gradient = lax.optimization_barrier((other_plane, alignment_gradient))
+    part = added(part, other_plane)
     other_half = swapped(part, "seq", seq_half)
     other_half, pair_gradient = lax.optimization_barrier((other_half, pair_gradient))
     part = added(part, other_half)

time: 139 us -> 138 us (level)
  local copies, waits for them, and re-layouts: 0.11 us -> 1.99 us
  blocking collectives: 11.1 us -> 9.38 us
    ppermute x16, starting transfers between devices: 10.7 us -> 14.3 us  [swapped(): lax.ppermute(mine, axis_name, [(a, a ^ distance) for a in range(size)])]
    all_to_all x4, starting transfers between devices: 21.3 us -> 18.1 us  [across(): lax.all_to_all(blocks, ('seq', 'res'), 0, 0, axis_index_groups=groups, ti...]
    unnamed x22, local copies, waits for them, and re-layouts: 0.11 us -> 1.99 us
    all_gather x1, blocking collectives: 11.1 us -> 9.38 us  [head_body(): lax.all_gather(part, 'res', axis=0)]
where the time goes in v15:
time: 138 us; the launch traced here: 137 us
  waiting for transfers between devices  62.5 us (45%)
  starting transfers between devices  32.4 us (23%)
  Pallas kernels  29.9 us (22%)
  blocking collectives  9.38 us (7%)
  local copies, waits for them, and re-layouts  1.99 us (1%)
    ppermute x16, waiting for transfers between devices, swapped(): lax.ppermute(mine, axis_name, [(a, a ^ distance) for a in range(size)])  40.5 us
    pallas_call x16, Pallas kernels, call(): pl.pallas_call(wrapped, out_shape=shapes, in_specs=[pl.BlockSpec(memory_s...  29.9 us
    all_to_all x4, waiting for transfers between devices, across(): lax.all_to_all(blocks, ('seq', 'res'), 0, 0, axis_index_groups=groups, ti...  22 us
    all_to_all x4, starting transfers between devices, across(): lax.all_to_all(blocks, ('seq', 'res'), 0, 0, axis_index_groups=groups, ti...  18.1 us
    ppermute x16, starting transfers between devices, swapped(): lax.ppermute(mine, axis_name, [(a, a ^ distance) for a in range(size)])  14.3 us
    all_gather x1, blocking collectives, head_body(): lax.all_gather(part, 'res', axis=0)  9.38 us
  transfers between devices with their start and end apart: 20, of which 15 were waited for; matrix products, arithmetic and copies ran while one was open for 0% of the time, Pallas kernels for 13%

profile of v15, /device:TPU:0, one launch (start us, length us, event | category | flops | bytes accessed | tf_op | source)
XLA Modules:
  0.0 137.2 jit_solution(16398771755771986255)
XLA Ops:
  0.6 6.9 %shard_map.109 = (bf16[16,192,128]{2,1,0:T(8,128)(2,1)}, f32[8,64,128]{2,1,0:T(8,128)}, f32[64,128]{1,0:T(8,128)}, f32[64,128]{1,0:T(8,128)}) custom-call(bf16[8,64,256]{2,1,0:T(8,128)(2,1)} %refs_0_.7, bf16[256,1024]{1,0:T(8,128)(2,1)} %refs_1_.10, bf16[64,128,128]{2,1,0:T(8,128)(2,1)} %refs_1_.11, f32[8,128]{1,0:T(8,128)} %bitcast.7), custom_call_target="tpu_custom_call" | custom-call | flops 268435456 | bytes 4001792 | tf_op jit(solution)/shard_map/pallas_call | solution.py:579
  7.6 6.3 %all-to-all-start = ((bf16[16,192,128]{2,1,0:T(8,128)(2,1)}), bf16[16,192,128]{2,1,0:T(8,128)(2,1)S(1)}, u32[]{:S(2)}, u32[]{:S(2)}) async-start(bf16[16,192,128]{2,1,0:T(8,128)(2,1)} %get-tuple-element.46), calls=%async_computation | async-start | bytes 1572864 | tf_op jit(solution)/shard_map/all_to_all | solution.py:628
  13.9 2.7 %shard_map.110 = bf16[16,128,128]{2,1,0:T(8,128)(2,1)} custom-call(bf16[8,64,256]{2,1,0:T(8,128)(2,1)} %refs_0_.7, bf16[8,64,256]{2,1,0:T(8,128)(2,1)} %refs_1_.8, bf16[256,1024]{1,0:T(8,128)(2,1)} %refs_1_.10, bf16[256,256]{1,0:T(8,128)(2,1)} %refs_3_.3), custom_call_target="tpu_custom_call" | custom-call | flops 268435456 | bytes 1703936 | tf_op jit(solution)/shard_map/pallas_call | solution.py:579
  16.6 10.6 %all-to-all-done.refs_1_.refs_5_ = bf16[16,192,128]{2,1,0:T(8,128)(2,1)S(1)} async-done(((bf16[16,192,128]{2,1,0:T(8,128)(2,1)}), bf16[16,192,128]{2,1,0:T(8,128)(2,1)S(1)}, u32[]{:S(2)}, u32[]{:S(2)}) %all-to-all-start) | async-done | bytes 786464 | tf_op jit(solution)/shard_map/all_to_all | solution.py:628
  27.3 3.6 %all-to-all-start.1 = ((bf16[16,128,128]{2,1,0:T(8,128)(2,1)}), bf16[16,128,128]{2,1,0:T(8,128)(2,1)S(1)}, u32[]{:S(2)}, u32[]{:S(2)}) async-start(bf16[16,128,128]{2,1,0:T(8,128)(2,1)} %shard_map.110), calls=%async_computation.1 | async-start | bytes 1048576 | tf_op jit(solution)/shard_map/all_to_all | solution.py:628
  32.0 2.7 %collective-permute-start.1 = (f32[128,512]{1,0:T(8,128)S(1)}, f32[128,512]{1,0:T(8,128)S(1)}, u32[]{:S(2)}, u32[]{:S(2)}) collective-permute-start(f32[128,512]{1,0:T(8,128)S(1)} %get-tuple-element.49), channel_id=1, source_target_pairs={{0,16},{8,24},{16,0},{24,8},{1,17},{9,25},{17,1},{25,9},{2,18},{10... | collective-permute-start | bytes 786440 | tf_op jit(solution)/shard_map/ppermute | solution.py:596
  34.6 8.4 %collective-permute-done.1.refs_1_ = f32[128,512]{1,0:T(8,128)S(1)} collective-permute-done((f32[128,512]{1,0:T(8,128)S(1)}, f32[128,512]{1,0:T(8,128)S(1)}, u32[]{:S(2)}, u32[]{:S(2)}) %collective-permute-start.1) | collective-permute-done | bytes 262176 | tf_op jit(solution)/shard_map/ppermute | solution.py:596
  43.2 3.7 %all-to-all-done.1.refs_1_.refs_5_ = bf16[16,128,128]{2,1,0:T(8,128)(2,1)S(1)} async-done(((bf16[16,128,128]{2,1,0:T(8,128)(2,1)}), bf16[16,128,128]{2,1,0:T(8,128)(2,1)S(1)}, u32[]{:S(2)}, u32[]{:S(2)}) %all-to-all-start.1) | async-done | bytes 524320 | tf_op jit(solution)/shard_map/all_to_all | solution.py:628
  49.9 6.7 %collective-permute-done.3.refs_2_ = bf16[128,512]{1,0:T(8,128)(2,1)S(1)} collective-permute-done((bf16[128,512]{1,0:T(8,128)(2,1)S(1)}, bf16[128,512]{1,0:T(8,128)(2,1)S(1)}, u32[]{:S(2)}, u32[]{:S(2)}) %collective-permute-start.3) | collective-permute-done | bytes 131104 | tf_op jit(solution)/shard_map/ppermute | solution.py:596
  57.9 1.8 %shard_map.114 = bf16[16,128,128]{2,1,0:T(8,128)(2,1)} custom-call(s32[3]{0:T(128)S(1)} %pad_add_fusion.refs_0_, bf16[128,512]{1,0:T(8,128)(2,1)S(1)} %get-tuple-element.55.refs_1_, bf16[128,512]{1,0:T(8,128)(2,1)S(1)} %collective-permute-done.3.refs_2_, bf16[128,512]{1,0:T(8,128)(2,1)S(1)} %collective-permute-done.4.refs_3_, ...), custom_call_target="tpu_custom_call" | custom-call | flops 268435456 | bytes 1572864 | tf_op jit(solution)/shard_map/pallas_call | solution.py:579
  59.7 4.4 %all-to-all-start.2 = ((bf16[16,128,128]{2,1,0:T(8,128)(2,1)}), bf16[16,128,128]{2,1,0:T(8,128)(2,1)S(1)}, u32[]{:S(2)}, u32[]{:S(2)}) async-start(bf16[16,128,128]{2,1,0:T(8,128)(2,1)} %shard_map.114), calls=%async_computation.2 | async-start | bytes 1048576 | tf_op jit(solution)/shard_map/all_to_all | solution.py:628
  65.4 8.2 %collective-permute-done.6.refs_2_ = bf16[128,512]{1,0:T(8,128)(2,1)S(1)} collective-permute-done((bf16[128,512]{1,0:T(8,128)(2,1)S(1)}, bf16[128,512]{1,0:T(8,128)(2,1)S(1)}, u32[]{:S(2)}, u32[]{:S(2)}) %collective-permute-start.6) | collective-permute-done | bytes 131104 | tf_op jit(solution)/shard_map/ppermute | solution.py:596
  73.7 3.4 %collective-permute-start.7 = (bf16[128,512]{1,0:T(8,128)(2,1)S(1)}, bf16[128,512]{1,0:T(8,128)(2,1)S(1)}, u32[]{:S(2)}, u32[]{:S(2)}) collective-permute-start(bf16[128,512]{1,0:T(8,128)(2,1)S(1)} %shard_map.115.refs_1_), channel_id=1, source_target_pairs={{0,16},{8,24},{16,0},{24,8},{1,17},{9,25},{17,1},{25,9},{2,18},{10... | collective-permute-start | bytes 393224 | tf_op jit(solution)/shard_map/ppermute | solution.py:596
  77.2 6.4 %collective-permute-done.7.refs_2_ = bf16[128,512]{1,0:T(8,128)(2,1)S(1)} collective-permute-done((bf16[128,512]{1,0:T(8,128)(2,1)S(1)}, bf16[128,512]{1,0:T(8,128)(2,1)S(1)}, u32[]{:S(2)}, u32[]{:S(2)}) %collective-permute-start.7) | collective-permute-done | bytes 131104 | tf_op jit(solution)/shard_map/ppermute | solution.py:596
  84.9 1.9 %shard_map.116 = bf16[16,160,128]{2,1,0:T(8,128)(2,1)} custom-call(s32[3]{0:T(128)S(1)} %pad_add_fusion.refs_0_, bf16[128,512]{1,0:T(8,128)(2,1)S(1)} %shard_map.115.refs_1_, bf16[128,512]{1,0:T(8,128)(2,1)S(1)} %collective-permute-done.7.refs_2_, bf16[128,512]{1,0:T(8,128)(2,1)S(1)} %collective-permute-done.8.refs_3_, ...), custom_call_target="tpu_custom_call" | custom-call | flops 268435456 | bytes 1966080 | tf_op jit(solution)/shard_map/pallas_call | solution.py:579
  86.8 3.8 %all-to-all-start.3 = ((bf16[16,160,128]{2,1,0:T(8,128)(2,1)}), bf16[16,160,128]{2,1,0:T(8,128)(2,1)S(1)}, u32[]{:S(2)}, u32[]{:S(2)}) async-start(bf16[16,160,128]{2,1,0:T(8,128)(2,1)} %shard_map.116), calls=%async_computation.3 | async-start | bytes 1310720 | tf_op jit(solution)/shard_map/all_to_all | solution.py:628
  90.6 4.2 %shard_map.117 = (bf16[8,64,256]{2,1,0:T(8,128)(2,1)}, bf16[512,512]{1,0:T(8,128)(2,1)}, bf16[512,256]{1,0:T(8,128)(2,1)}, bf16[256,768]{1,0:T(8,128)(2,1)}) custom-call(bf16[8,64,256]{2,1,0:T(8,128)(2,1)} %refs_0_.7, bf16[8,64,256]{2,1,0:T(8,128)(2,1)} %refs_1_.8, bf16[256,1024]{1,0:T(8,128)(2,1)} %refs_1_.10, bf16[256,256]{1,0:T(8,128)(2,1)} %refs_3_.3, ...), custom_call_target="tpu_custom_call" | custom-call | flops 469762048 | bytes 3145728 | tf_op jit(solution)/shard_map/pallas_call | solution.py:579
  94.9 7.7 %all-to-all-done.3.refs_2_.refs_0_ = bf16[16,160,128]{2,1,0:T(8,128)(2,1)S(1)} async-done(((bf16[16,160,128]{2,1,0:T(8,128)(2,1)}), bf16[16,160,128]{2,1,0:T(8,128)(2,1)S(1)}, u32[]{:S(2)}, u32[]{:S(2)}) %all-to-all-start.3) | async-done | bytes 655392 | tf_op jit(solution)/shard_map/all_to_all | solution.py:628
  105.7 1.6 %collective-permute-done.10.refs_2_ = bf16[4,32,1280]{2,1,0:T(8,128)(2,1)S(1)} collective-permute-done((bf16[4,32,1280]{2,1,0:T(8,128)(2,1)S(1)}, bf16[4,32,1280]{2,1,0:T(8,128)(2,1)S(1)}, u32[]{:S(2)}, u32[]{:S(2)}) %collective-permute-start.10) | collective-permute-done | bytes 327712 | tf_op jit(solution)/shard_map/ppermute | solution.py:596
  109.0 2.5 %collective-permute-start.11 = (bf16[32,1280]{1,0:T(8,128)(2,1)S(1)}, bf16[32,1280]{1,0:T(8,128)(2,1)S(1)}, u32[]{:S(2)}, u32[]{:S(2)}) collective-permute-start(bf16[32,1280]{1,0:T(8,128)(2,1)S(1)} %get-tuple-element.67.refs_4_), channel_id=1, source_target_pairs={{0,2},{1,3},{2,0},{3,1},{4,6},{5,7},{6,4},{7,5},{8,10},{9,11},{10,... | collective-permute-start | bytes 245768 | tf_op jit(solution)/shard_map/ppermute | solution.py:596
  117.4 2.7 %collective-permute-done.14 = bf16[32,1408]{1,0:T(8,128)(2,1)S(1)} collective-permute-done((bf16[32,1408]{1,0:T(8,128)(2,1)S(1)}, bf16[32,1408]{1,0:T(8,128)(2,1)S(1)}, u32[]{:S(2)}, u32[]{:S(2)}) %collective-permute-start.14) | collective-permute-done | bytes 90144 | tf_op jit(solution)/shard_map/ppermute | solution.py:596
  120.1 2.2 %collective-permute-start.15 = (bf16[32,1408]{1,0:T(8,128)(2,1)S(1)}, bf16[32,1408]{1,0:T(8,128)(2,1)S(1)}, u32[]{:S(2)}, u32[]{:S(2)}) collective-permute-start(bf16[32,1408]{1,0:T(8,128)(2,1)S(1)} %add_convert_fusion.1), channel_id=1, source_target_pairs={{0,16},{8,24},{16,0},{24,8},{1,17},{9,25},{17,1},{25,9},{2,18},{10... | collective-permute-start | bytes 270344 | tf_op jit(solution)/shard_map/ppermute | solution.py:596
  122.3 4.3 %shard_map.123 = bf16[64,128,128]{2,1,0:T(8,128)(2,1)} custom-call(bf16[16,160,128]{2,1,0:T(8,128)(2,1)S(1)} %all-to-all-done.3.refs_2_.refs_0_, bf16[64,128,128]{2,1,0:T(8,128)(2,1)S(1)} %copy-done, f32[8,128]{1,0:T(8,128)S(1)} %bitcast.8, f32[8,64,128]{2,1,0:T(8,128)S(1)} %copy-done.5, f32[64,128]{1,0:T(8,128)S(1)} %copy-done.7, f32[64,128]{1,0:T(8,128)S(1)} %copy-done.8), custom_call_target="tpu_custom_call" | custom-call | flops 268435456 | bytes 5181440 | tf_op jit(solution)/shard_map/pallas_call | solution.py:579
  126.7 9.4 %all-gather = bf16[256,1408]{1,0:T(8,128)(2,1)S(1)} all-gather(bf16[32,1408]{1,0:T(8,128)(2,1)S(1)} %add_convert_fusion), channel_id=2, replica_groups=mesh['seq'=4,'res'=8] {'res'}, dimensions={0}, use_global_device_ids=true | all-gather | bytes 811008 | tf_op jit(solution)/shard_map/all_gather | solution.py:759
  (58 shorter events, 20.1 us)
Async XLA Ops:
  7.6 19.7 %all-to-all-start = ((bf16[16,192,128]{2,1,0:T(8,128)(2,1)}), bf16[16,192,128]{2,1,0:T(8,128)(2,1)S(1)}, u32[]{:S(2)}, u32[]{:S(2)}) async-start(bf16[16,192,128]{2,1,0:T(8,128)(2,1)} %get-tuple-element.46), calls=%async_computation | async-start | bytes 1572864 | tf_op jit(solution)/shard_map/all_to_all | solution.py:628
  27.2 3.7 %collective-permute-start = (bf16[16,192,128]{2,1,0:T(8,128)(2,1)S(1)}, bf16[16,192,128]{2,1,0:T(8,128)(2,1)S(1)}, u32[]{:S(2)}, u32[]{:S(2)}) collective-permute-start(bf16[16,192,128]{2,1,0:T(8,128)(2,1)S(1)} %all-to-all-done.refs_1_.refs_5_), channel_id=1, source_target_pairs={{0,1},{1,0},{2,3},{3,2},{4,5},{5,4},{6,7},{7,6},{8,9},{9,8},{10,11... | collective-permute-start | bytes 2359304 | tf_op jit(solution)/shard_map/ppermute | solution.py:596
  27.3 19.7 %all-to-all-start.1 = ((bf16[16,128,128]{2,1,0:T(8,128)(2,1)}), bf16[16,128,128]{2,1,0:T(8,128)(2,1)S(1)}, u32[]{:S(2)}, u32[]{:S(2)}) async-start(bf16[16,128,128]{2,1,0:T(8,128)(2,1)} %shard_map.110), calls=%async_computation.1 | async-start | bytes 1048576 | tf_op jit(solution)/shard_map/all_to_all | solution.py:628
  32.0 11.0 %collective-permute-start.1 = (f32[128,512]{1,0:T(8,128)S(1)}, f32[128,512]{1,0:T(8,128)S(1)}, u32[]{:S(2)}, u32[]{:S(2)}) collective-permute-start(f32[128,512]{1,0:T(8,128)S(1)} %get-tuple-element.49), channel_id=1, source_target_pairs={{0,16},{8,24},{16,0},{24,8},{1,17},{9,25},{17,1},{25,9},{2,18},{10... | collective-permute-start | bytes 786440 | tf_op jit(solution)/shard_map/ppermute | solution.py:596
  46.9 1.9 %collective-permute-start.2 = (bf16[16,128,128]{2,1,0:T(8,128)(2,1)S(1)}, bf16[16,128,128]{2,1,0:T(8,128)(2,1)S(1)}, u32[]{:S(2)}, u32[]{:S(2)}) collective-permute-start(bf16[16,128,128]{2,1,0:T(8,128)(2,1)S(1)} %all-to-all-done.1.refs_1_.refs_5_), channel_id=1, source_target_pairs={{0,1},{1,0},{2,3},{3,2},{4,5},{5,4},{6,7},{7,6},{8,9},{9,8},{10,11... | collective-permute-start | bytes 1572872 | tf_op jit(solution)/shard_map/ppermute | solution.py:596
  46.9 9.6 %collective-permute-start.3 = (bf16[128,512]{1,0:T(8,128)(2,1)S(1)}, bf16[128,512]{1,0:T(8,128)(2,1)S(1)}, u32[]{:S(2)}, u32[]{:S(2)}) collective-permute-start(bf16[128,512]{1,0:T(8,128)(2,1)S(1)} %get-tuple-element.55.refs_1_), channel_id=1, source_target_pairs={{0,16},{8,24},{16,0},{24,8},{1,17},{9,25},{17,1},{25,9},{2,18},{10... | collective-permute-start | bytes 393224 | tf_op jit(solution)/shard_map/ppermute | solution.py:596
  46.9 9.6 %collective-permute-start.4 = (bf16[128,512]{1,0:T(8,128)(2,1)S(1)}, bf16[128,512]{1,0:T(8,128)(2,1)S(1)}, u32[]{:S(2)}, u32[]{:S(2)}) collective-permute-start(bf16[128,512]{1,0:T(8,128)(2,1)S(1)} %get-tuple-element.55.refs_1_), channel_id=1, source_target_pairs={{0,1},{1,0},{2,3},{3,2},{4,5},{5,4},{6,7},{7,6},{8,9},{9,8},{10,11... | collective-permute-start | bytes 393224 | tf_op jit(solution)/shard_map/ppermute | solution.py:596
  56.6 1.3 collective-permute-start.5
  59.7 27.1 %all-to-all-start.2 = ((bf16[16,128,128]{2,1,0:T(8,128)(2,1)}), bf16[16,128,128]{2,1,0:T(8,128)(2,1)S(1)}, u32[]{:S(2)}, u32[]{:S(2)}) async-start(bf16[16,128,128]{2,1,0:T(8,128)(2,1)} %shard_map.114), calls=%async_computation.2 | async-start | bytes 1048576 | tf_op jit(solution)/shard_map/all_to_all | solution.py:628
  64.2 9.4 %collective-permute-start.6 = (bf16[128,512]{1,0:T(8,128)(2,1)S(1)}, bf16[128,512]{1,0:T(8,128)(2,1)S(1)}, u32[]{:S(2)}, u32[]{:S(2)}) collective-permute-start(bf16[128,512]{1,0:T(8,128)(2,1)S(1)} %get-tuple-element.56), channel_id=1, source_target_pairs={{0,16},{8,24},{16,0},{24,8},{1,17},{9,25},{17,1},{25,9},{2,18},{10... | collective-permute-start | bytes 393224 | tf_op jit(solution)/shard_map/ppermute | solution.py:596
  73.7 9.8 %collective-permute-start.7 = (bf16[128,512]{1,0:T(8,128)(2,1)S(1)}, bf16[128,512]{1,0:T(8,128)(2,1)S(1)}, u32[]{:S(2)}, u32[]{:S(2)}) collective-permute-start(bf16[128,512]{1,0:T(8,128)(2,1)S(1)} %shard_map.115.refs_1_), channel_id=1, source_target_pairs={{0,16},{8,24},{16,0},{24,8},{1,17},{9,25},{17,1},{25,9},{2,18},{10... | collective-permute-start | bytes 393224 | tf_op jit(solution)/shard_map/ppermute | solution.py:596
  77.2 6.4 %collective-permute-start.8 = (bf16[128,512]{1,0:T(8,128)(2,1)S(1)}, bf16[128,512]{1,0:T(8,128)(2,1)S(1)}, u32[]{:S(2)}, u32[]{:S(2)}) collective-permute-start(bf16[128,512]{1,0:T(8,128)(2,1)S(1)} %shard_map.115.refs_1_), channel_id=1, source_target_pairs={{0,1},{1,0},{2,3},{3,2},{4,5},{5,4},{6,7},{7,6},{8,9},{9,8},{10,11... | collective-permute-start | bytes 393224 | tf_op jit(solution)/shard_map/ppermute | solution.py:596
  83.6 1.3 collective-permute-start.9
  86.8 24.7 %copy-start.7 = (f32[64,128]{1,0:T(8,128)S(1)}, f32[64,128]{1,0:T(8,128)}, u32[]{:S(2)}) copy-start(f32[64,128]{1,0:T(8,128)} %get-tuple-element.70.refs_2_.refs_4_) | copy-start | bytes 98308
  86.8 24.7 %copy-start.8 = (f32[64,128]{1,0:T(8,128)S(1)}, f32[64,128]{1,0:T(8,128)}, u32[]{:S(2)}) copy-start(f32[64,128]{1,0:T(8,128)} %get-tuple-element.71.refs_3_.refs_5_) | copy-start | bytes 98308
  86.8 15.8 %all-to-all-start.3 = ((bf16[16,160,128]{2,1,0:T(8,128)(2,1)}), bf16[16,160,128]{2,1,0:T(8,128)(2,1)S(1)}, u32[]{:S(2)}, u32[]{:S(2)}) async-start(bf16[16,160,128]{2,1,0:T(8,128)(2,1)} %shard_map.116), calls=%async_computation.3 | async-start | bytes 1310720 | tf_op jit(solution)/shard_map/all_to_all | solution.py:628
  90.6 20.9 %copy-start = (bf16[64,128,128]{2,1,0:T(8,128)(2,1)S(1)}, bf16[64,128,128]{2,1,0:T(8,128)(2,1)}, u32[]{:S(2)}) copy-start(bf16[64,128,128]{2,1,0:T(8,128)(2,1)} %refs_1_.11) | copy-start | bytes 6291460
  105.6 10.5 %copy-start.1 = (bf16[256,1024]{1,0:T(8,128)(2,1)S(1)}, bf16[256,1024]{1,0:T(8,128)(2,1)}, u32[]{:S(2)}) copy-start(bf16[256,1024]{1,0:T(8,128)(2,1)} %refs_1_.10) | copy-start | bytes 1572868
  105.6 1.7 %collective-permute-start.10 = (bf16[4,32,1280]{2,1,0:T(8,128)(2,1)S(1)}, bf16[4,32,1280]{2,1,0:T(8,128)(2,1)S(1)}, u32[]{:S(2)}, u32[]{:S(2)}) collective-permute-start(bf16[4,32,1280]{2,1,0:T(8,128)(2,1)S(1)} %get-tuple-element.65), channel_id=1, source_target_pairs={{0,1},{1,0},{2,3},{3,2},{4,5},{5,4},{6,7},{7,6},{8,9},{9,8},{10,11... | collective-permute-start | bytes 983048 | tf_op jit(solution)/shard_map/ppermute | solution.py:596
  107.9 6.2 %collective-permute-start.12 = (bf16[32,1280]{1,0:T(8,128)(2,1)S(1)}, bf16[32,1280]{1,0:T(8,128)(2,1)S(1)}, u32[]{:S(2)}, u32[]{:S(2)}) collective-permute-start(bf16[32,1280]{1,0:T(8,128)(2,1)S(1)} %get-tuple-element.68), channel_id=1, source_target_pairs={{0,4},{1,5},{2,6},{3,7},{4,0},{5,1},{6,2},{7,3},{8,12},{9,13},{10,... | collective-permute-start | bytes 245768 | tf_op jit(solution)/shard_map/ppermute | solution.py:596
  108.0 6.3 %collective-permute-start.13 = (bf16[32,1280]{1,0:T(8,128)(2,1)S(1)}, bf16[32,1280]{1,0:T(8,128)(2,1)S(1)}, u32[]{:S(2)}, u32[]{:S(2)}) collective-permute-start(bf16[32,1280]{1,0:T(8,128)(2,1)S(1)} %get-tuple-element.69), channel_id=1, source_target_pairs={{0,6},{1,7},{2,4},{3,5},{4,2},{5,3},{6,0},{7,1},{8,14},{9,15},{10,... | collective-permute-start | bytes 245768 | tf_op jit(solution)/shard_map/ppermute | solution.py:596
  109.0 6.4 %collective-permute-start.11 = (bf16[32,1280]{1,0:T(8,128)(2,1)S(1)}, bf16[32,1280]{1,0:T(8,128)(2,1)S(1)}, u32[]{:S(2)}, u32[]{:S(2)}) collective-permute-start(bf16[32,1280]{1,0:T(8,128)(2,1)S(1)} %get-tuple-element.67.refs_4_), channel_id=1, source_target_pairs={{0,2},{1,3},{2,0},{3,1},{4,6},{5,7},{6,4},{7,5},{8,10},{9,11},{10,... | collective-permute-start | bytes 245768 | tf_op jit(solution)/shard_map/ppermute | solution.py:596
  115.5 4.6 %collective-permute-start.14 = (bf16[32,1408]{1,0:T(8,128)(2,1)S(1)}, bf16[32,1408]{1,0:T(8,128)(2,1)S(1)}, u32[]{:S(2)}, u32[]{:S(2)}) collective-permute-start(bf16[32,1408]{1,0:T(8,128)(2,1)S(1)} %shard_map.121), channel_id=1, source_target_pairs={{0,8},{8,0},{16,24},{24,16},{1,9},{9,1},{17,25},{25,17},{2,10},{10... | collective-permute-start | bytes 270344 | tf_op jit(solution)/shard_map/ppermute | solution.py:596
  120.1 6.6 %collective-permute-start.15 = (bf16[32,1408]{1,0:T(8,128)(2,1)S(1)}, bf16[32,1408]{1,0:T(8,128)(2,1)S(1)}, u32[]{:S(2)}, u32[]{:S(2)}) collective-permute-start(bf16[32,1408]{1,0:T(8,128)(2,1)S(1)} %add_convert_fusion.1), channel_id=1, source_target_pairs={{0,16},{8,24},{16,0},{24,8},{1,17},{9,25},{17,1},{25,9},{2,18},{10... | collective-permute-start | bytes 270344 | tf_op jit(solution)/shard_map/ppermute | solution.py:596
  (7 other events, 45.5 us)

commit v16 on v15

--- a/solution.py
+++ b/solution.py
@@ -255,7 +255,7 @@
     share = jnp.full((heads, channels), 1.0 / channels, jnp.bfloat16)
     left = jnp.concatenate([first, second, third, share], axis=0)
     average = jnp.full((channels, channels), 1.0 / channels, jnp.bfloat16)
-    step_rows = 16
+    step_rows = 32
 
     def rows(step, carry):
         start = pl.multiple_of(step * step_rows, step_rows)
@@ -408,7 +408,7 @@
 
 
 def query_weight_kernel(
-    place_ref, normed_ref, blocks_ref, attended_sums_ref,
+    arrive, place_ref, normed_ref, attended_sums_ref, blocks_ref,
     projected_ref, keep_ref, send_ref, sums_ref,
 ):
     width = normed_ref.shape[1]
@@ -418,6 +418,7 @@
         projected_ref[:, t * width : (t + 1) * width] = unpack_heads(
             blocks_ref, t * residues, residues, tiles
         ).astype(jnp.bfloat16)
+    arrive()
     sums_ref[:, : 2 * width] = f32_dot(normed_ref[...], projected_ref[...], TN).astype(
         jnp.bfloat16
     )
@@ -666,7 +667,7 @@
     probs_far = swapped(probs, "seq", seq_half)
     grad_mine, grad_sent = scores(value_blocks, residues, 0, False, bf16)
     grad_other = swapped(grad_sent, "seq", seq_half)
-    probs_far = lax.optimization_barrier((probs_far, grad_sent))[0]
+    probs_far, grad_other = lax.optimization_barrier((probs_far, grad_other))
 
     def products(quarters, blocks, first_row, second_row, with_share, factor):
         rows = 2 * residues + (residues // 2 if with_share else 0)
@@ -714,9 +715,9 @@
     query_key, keep, send = call(
         query_weight_kernel,
         [((tokens, 2 * width), bf16), part_rows, part_rows],
-        normed, grad_blocks, attended_sums,
+        normed, attended_sums, grad_blocks,
         scratch=[pltpu.VMEM((width, columns), bf16)],
-        place=place, flops=4 * tokens * width * width,
+        place=place, flops=4 * tokens * width * width, outside=2, late=2,
     )
     own, *sent = call(
         core_sum_kernel,

time: 138 us -> 139 us (level)
  starting transfers between devices: 32.4 us -> 30.4 us
  Pallas kernels: 29.9 us -> 31.7 us
  local copies, waits for them, and re-layouts: 1.99 us -> 3.78 us
    ppermute x16, starting transfers between devices: 14.3 us -> 10.3 us  [swapped(): lax.ppermute(mine, axis_name, [(a, a ^ distance) for a in range(size)])]
    all_to_all x4, starting transfers between devices: 18.1 us -> 20.1 us  [across(): lax.all_to_all(blocks, ('seq', 'res'), 0, 0, axis_index_groups=groups, ti...]
    pallas_call x16, Pallas kernels: 29.9 us -> 31.7 us  [call(): pl.pallas_call(wrapped, out_shape=shapes, in_specs=[pl.BlockSpec(memory_s...]
    unnamed x22 -> x32, local copies, waits for them, and re-layouts: 1.99 us -> 3.78 us
  transfers between devices with their start and end apart: 20 -> 20, of which waited for: 15 -> 17; matrix products, arithmetic and copies ran while one was open for 0% -> 0% of each run, Pallas kernels for 13% -> 13%
where the time goes in v16:
time: 139 us; the launch traced here: 138 us
  waiting for transfers between devices  61.8 us (44%)
  Pallas kernels  31.7 us (23%)
  starting transfers between devices  30.4 us (22%)
  blocking collectives  9.35 us (7%)
  local copies, waits for them, and re-layouts  3.78 us (3%)
    ppermute x16, waiting for transfers between devices, swapped(): lax.ppermute(mine, axis_name, [(a, a ^ distance) for a in range(size)])  39.1 us
    pallas_call x16, Pallas kernels, call(): pl.pallas_call(wrapped, out_shape=shapes, in_specs=[pl.BlockSpec(memory_s...  31.7 us
    all_to_all x4, waiting for transfers between devices, across(): lax.all_to_all(blocks, ('seq', 'res'), 0, 0, axis_index_groups=groups, ti...  22.7 us
    all_to_all x4, starting transfers between devices, across(): lax.all_to_all(blocks, ('seq', 'res'), 0, 0, axis_index_groups=groups, ti...  20.1 us
    ppermute x16, starting transfers between devices, swapped(): lax.ppermute(mine, axis_name, [(a, a ^ distance) for a in range(size)])  10.3 us
    all_gather x1, blocking collectives, head_body(): lax.all_gather(part, 'res', axis=0)  9.35 us
    unnamed x32, local copies, waits for them, and re-layouts  3.78 us
  transfers between devices with their start and end apart: 20, of which 17 were waited for; matrix products, arithmetic and copies ran while one was open for 0% of the time, Pallas kernels for 13%

profile of v16, /device:TPU:0, one launch (start us, length us, event | category | flops | bytes accessed | tf_op | source)
XLA Modules:
  0.0 138.1 jit_solution(3834295212548100229)
XLA Ops:
  0.6 6.4 %shard_map.109 = (bf16[16,192,128]{2,1,0:T(8,128)(2,1)}, f32[8,64,128]{2,1,0:T(8,128)}, f32[64,128]{1,0:T(8,128)}, f32[64,128]{1,0:T(8,128)}) custom-call(bf16[8,64,256]{2,1,0:T(8,128)(2,1)} %refs_0_.7, bf16[256,1024]{1,0:T(8,128)(2,1)} %refs_1_.10, bf16[64,128,128]{2,1,0:T(8,128)(2,1)} %refs_1_.11, f32[8,128]{1,0:T(8,128)} %bitcast.7), custom_call_target="tpu_custom_call" | custom-call | flops 268435456 | bytes 4001792 | tf_op jit(solution)/shard_map/pallas_call | solution.py:580
  7.1 6.3 %all-to-all-start = ((bf16[16,192,128]{2,1,0:T(8,128)(2,1)}), bf16[16,192,128]{2,1,0:T(8,128)(2,1)S(1)}, u32[]{:S(2)}, u32[]{:S(2)}) async-start(bf16[16,192,128]{2,1,0:T(8,128)(2,1)} %get-tuple-element.47), calls=%async_computation | async-start | bytes 1572864 | tf_op jit(solution)/shard_map/all_to_all | solution.py:629
  13.4 2.7 %shard_map.110 = bf16[16,128,128]{2,1,0:T(8,128)(2,1)} custom-call(bf16[8,64,256]{2,1,0:T(8,128)(2,1)} %refs_0_.7, bf16[8,64,256]{2,1,0:T(8,128)(2,1)} %refs_1_.8, bf16[256,1024]{1,0:T(8,128)(2,1)} %refs_1_.10, bf16[256,256]{1,0:T(8,128)(2,1)} %refs_3_.3), custom_call_target="tpu_custom_call" | custom-call | flops 268435456 | bytes 1703936 | tf_op jit(solution)/shard_map/pallas_call | solution.py:580
  16.1 10.6 %all-to-all-done.refs_1_.refs_5_ = bf16[16,192,128]{2,1,0:T(8,128)(2,1)S(1)} async-done(((bf16[16,192,128]{2,1,0:T(8,128)(2,1)}), bf16[16,192,128]{2,1,0:T(8,128)(2,1)S(1)}, u32[]{:S(2)}, u32[]{:S(2)}) %all-to-all-start) | async-done | bytes 786464 | tf_op jit(solution)/shard_map/all_to_all | solution.py:629
  26.7 3.6 %all-to-all-start.1 = ((bf16[16,128,128]{2,1,0:T(8,128)(2,1)}), bf16[16,128,128]{2,1,0:T(8,128)(2,1)S(1)}, u32[]{:S(2)}, u32[]{:S(2)}) async-start(bf16[16,128,128]{2,1,0:T(8,128)(2,1)} %shard_map.110), calls=%async_computation.1 | async-start | bytes 1048576 | tf_op jit(solution)/shard_map/all_to_all | solution.py:629
  31.5 2.7 %collective-permute-start.1 = (f32[128,512]{1,0:T(8,128)S(1)}, f32[128,512]{1,0:T(8,128)S(1)}, u32[]{:S(2)}, u32[]{:S(2)}) collective-permute-start(f32[128,512]{1,0:T(8,128)S(1)} %get-tuple-element.50), channel_id=1, source_target_pairs={{0,16},{8,24},{16,0},{24,8},{1,17},{9,25},{17,1},{25,9},{2,18},{10... | collective-permute-start | bytes 786440 | tf_op jit(solution)/shard_map/ppermute | solution.py:597
  34.1 8.4 %collective-permute-done.1.refs_1_ = f32[128,512]{1,0:T(8,128)S(1)} collective-permute-done((f32[128,512]{1,0:T(8,128)S(1)}, f32[128,512]{1,0:T(8,128)S(1)}, u32[]{:S(2)}, u32[]{:S(2)}) %collective-permute-start.1) | collective-permute-done | bytes 262176 | tf_op jit(solution)/shard_map/ppermute | solution.py:597
  42.7 3.7 %all-to-all-done.1.refs_1_.refs_5_ = bf16[16,128,128]{2,1,0:T(8,128)(2,1)S(1)} async-done(((bf16[16,128,128]{2,1,0:T(8,128)(2,1)}), bf16[16,128,128]{2,1,0:T(8,128)(2,1)S(1)}, u32[]{:S(2)}, u32[]{:S(2)}) %all-to-all-start.1) | async-done | bytes 524320 | tf_op jit(solution)/shard_map/all_to_all | solution.py:629
  46.4 1.9 %collective-permute-done.2.refs_2_ = bf16[16,128,128]{2,1,0:T(8,128)(2,1)S(1)} collective-permute-done((bf16[16,128,128]{2,1,0:T(8,128)(2,1)S(1)}, bf16[16,128,128]{2,1,0:T(8,128)(2,1)S(1)}, u32[]{:S(2)}, u32[]{:S(2)}) %collective-permute-start.2) | collective-permute-done | bytes 524320 | tf_op jit(solution)/shard_map/ppermute | solution.py:597
  50.4 8.8 %collective-permute-done.3.refs_2_ = bf16[128,512]{1,0:T(8,128)(2,1)S(1)} collective-permute-done((bf16[128,512]{1,0:T(8,128)(2,1)S(1)}, bf16[128,512]{1,0:T(8,128)(2,1)S(1)}, u32[]{:S(2)}, u32[]{:S(2)}) %collective-permute-start.3) | collective-permute-done | bytes 131104 | tf_op jit(solution)/shard_map/ppermute | solution.py:597
  59.2 2.4 %collective-permute-done.4.refs_2_ = bf16[128,512]{1,0:T(8,128)(2,1)S(1)} collective-permute-done((bf16[128,512]{1,0:T(8,128)(2,1)S(1)}, bf16[128,512]{1,0:T(8,128)(2,1)S(1)}, u32[]{:S(2)}, u32[]{:S(2)}) %collective-permute-start.4) | collective-permute-done | bytes 131104 | tf_op jit(solution)/shard_map/ppermute | solution.py:597
  63.0 1.8 %shard_map.114 = bf16[16,128,128]{2,1,0:T(8,128)(2,1)} custom-call(s32[3]{0:T(128)S(1)} %pad_add_fusion.refs_0_, bf16[128,512]{1,0:T(8,128)(2,1)S(1)} %get-tuple-element.56.refs_1_, bf16[128,512]{1,0:T(8,128)(2,1)S(1)} %collective-permute-done.3.refs_2_, bf16[128,512]{1,0:T(8,128)(2,1)S(1)} %collective-permute-done.5.refs_3_, ...), custom_call_target="tpu_custom_call" | custom-call | flops 268435456 | bytes 1572864 | tf_op jit(solution)/shard_map/pallas_call | solution.py:580
  64.8 4.4 %all-to-all-start.2 = ((bf16[16,128,128]{2,1,0:T(8,128)(2,1)}), bf16[16,128,128]{2,1,0:T(8,128)(2,1)S(1)}, u32[]{:S(2)}, u32[]{:S(2)}) async-start(bf16[16,128,128]{2,1,0:T(8,128)(2,1)} %shard_map.114), calls=%async_computation.2 | async-start | bytes 1048576 | tf_op jit(solution)/shard_map/all_to_all | solution.py:629
  70.8 7.9 %collective-permute-done.7.refs_2_ = bf16[128,512]{1,0:T(8,128)(2,1)S(1)} collective-permute-done((bf16[128,512]{1,0:T(8,128)(2,1)S(1)}, bf16[128,512]{1,0:T(8,128)(2,1)S(1)}, u32[]{:S(2)}, u32[]{:S(2)}) %collective-permute-start.7) | collective-permute-done | bytes 131104 | tf_op jit(solution)/shard_map/ppermute | solution.py:597
  80.1 1.9 %shard_map.116 = bf16[16,160,128]{2,1,0:T(8,128)(2,1)} custom-call(s32[3]{0:T(128)S(1)} %pad_add_fusion.refs_0_, bf16[128,512]{1,0:T(8,128)(2,1)S(1)} %shard_map.115.refs_1_, bf16[128,512]{1,0:T(8,128)(2,1)S(1)} %collective-permute-done.7.refs_2_, bf16[128,512]{1,0:T(8,128)(2,1)S(1)} %collective-permute-done.8.refs_3_, ...), custom_call_target="tpu_custom_call" | custom-call | flops 268435456 | bytes 1966080 | tf_op jit(solution)/shard_map/pallas_call | solution.py:580
  83.4 5.8 %all-to-all-start.3 = ((bf16[16,160,128]{2,1,0:T(8,128)(2,1)}), bf16[16,160,128]{2,1,0:T(8,128)(2,1)S(1)}, u32[]{:S(2)}, u32[]{:S(2)}) async-start(bf16[16,160,128]{2,1,0:T(8,128)(2,1)} %shard_map.116), calls=%async_computation.3 | async-start | bytes 1310720 | tf_op jit(solution)/shard_map/all_to_all | solution.py:629
  89.3 4.2 %shard_map.117 = (bf16[8,64,256]{2,1,0:T(8,128)(2,1)}, bf16[512,512]{1,0:T(8,128)(2,1)}, bf16[512,256]{1,0:T(8,128)(2,1)}, bf16[256,768]{1,0:T(8,128)(2,1)}) custom-call(bf16[8,64,256]{2,1,0:T(8,128)(2,1)} %refs_0_.7, bf16[8,64,256]{2,1,0:T(8,128)(2,1)} %refs_1_.8, bf16[256,1024]{1,0:T(8,128)(2,1)} %refs_1_.10, bf16[256,256]{1,0:T(8,128)(2,1)} %refs_3_.3, ...), custom_call_target="tpu_custom_call" | custom-call | flops 469762048 | bytes 3145728 | tf_op jit(solution)/shard_map/pallas_call | solution.py:580
  93.5 7.7 %all-to-all-done.3.refs_3_.refs_0_ = bf16[16,160,128]{2,1,0:T(8,128)(2,1)S(1)} async-done(((bf16[16,160,128]{2,1,0:T(8,128)(2,1)}), bf16[16,160,128]{2,1,0:T(8,128)(2,1)S(1)}, u32[]{:S(2)}, u32[]{:S(2)}) %all-to-all-start.3) | async-done | bytes 655392 | tf_op jit(solution)/shard_map/all_to_all | solution.py:629
  102.0 3.5 %shard_map.118 = (bf16[512,512]{1,0:T(8,128)(2,1)}, bf16[4,32,1280]{2,1,0:T(8,128)(2,1)}, bf16[4,32,1280]{2,1,0:T(8,128)(2,1)}) custom-call(s32[3]{0:T(128)} %copy-done.12, bf16[512,256]{1,0:T(8,128)(2,1)} %get-tuple-element.63.refs_1_, bf16[256,768]{1,0:T(8,128)(2,1)} %get-tuple-element.64.refs_2_, bf16[16,160,128]{2,1,0:T(8,128)(2,1)} %copy-done.1), custom_call_target="tpu_custom_call" | custom-call | flops 134217728 | bytes 2490368 | tf_op jit(solution)/shard_map/pallas_call | solution.py:580
  105.6 1.8 %collective-permute-done.10.refs_2_ = bf16[4,32,1280]{2,1,0:T(8,128)(2,1)S(1)} collective-permute-done((bf16[4,32,1280]{2,1,0:T(8,128)(2,1)}, bf16[4,32,1280]{2,1,0:T(8,128)(2,1)S(1)}, u32[]{:S(2)}, u32[]{:S(2)}) %collective-permute-start.10) | collective-permute-done | bytes 327712 | tf_op jit(solution)/shard_map/ppermute | solution.py:597
  110.1 2.5 %collective-permute-start.11 = (bf16[32,1280]{1,0:T(8,128)(2,1)S(1)}, bf16[32,1280]{1,0:T(8,128)(2,1)S(1)}, u32[]{:S(2)}, u32[]{:S(2)}) collective-permute-start(bf16[32,1280]{1,0:T(8,128)(2,1)S(1)} %get-tuple-element.69.refs_4_), channel_id=1, source_target_pairs={{0,2},{1,3},{2,0},{3,1},{4,6},{5,7},{6,4},{7,5},{8,10},{9,11},{10,... | collective-permute-start | bytes 245768 | tf_op jit(solution)/shard_map/ppermute | solution.py:597
  118.5 2.7 %collective-permute-done.14 = bf16[32,1408]{1,0:T(8,128)(2,1)S(1)} collective-permute-done((bf16[32,1408]{1,0:T(8,128)(2,1)S(1)}, bf16[32,1408]{1,0:T(8,128)(2,1)S(1)}, u32[]{:S(2)}, u32[]{:S(2)}) %collective-permute-start.14) | collective-permute-done | bytes 90144 | tf_op jit(solution)/shard_map/ppermute | solution.py:597
  122.1 4.3 %shard_map.123 = bf16[64,128,128]{2,1,0:T(8,128)(2,1)} custom-call(bf16[16,160,128]{2,1,0:T(8,128)(2,1)S(1)} %copy-done.3, bf16[64,128,128]{2,1,0:T(8,128)(2,1)S(1)} %copy-done, f32[8,128]{1,0:T(8,128)S(1)} %bitcast.8, f32[8,64,128]{2,1,0:T(8,128)S(1)} %copy-done.9, f32[64,128]{1,0:T(8,128)S(1)} %copy-done.10, f32[64,128]{1,0:T(8,128)S(1)} %copy-done.11), custom_call_target="tpu_custom_call" | custom-call | flops 268435456 | bytes 5181440 | tf_op jit(solution)/shard_map/pallas_call | solution.py:580
  127.7 9.3 %all-gather = bf16[256,1408]{1,0:T(8,128)(2,1)S(1)} all-gather(bf16[32,1408]{1,0:T(8,128)(2,1)S(1)} %add_convert_fusion), channel_id=2, replica_groups=mesh['seq'=4,'res'=8] {'res'}, dimensions={0}, use_global_device_ids=true | all-gather | bytes 811008 | tf_op jit(solution)/shard_map/all_gather | solution.py:760
  (68 shorter events, 21.8 us)
Async XLA Ops:
  7.1 19.7 %all-to-all-start = ((bf16[16,192,128]{2,1,0:T(8,128)(2,1)}), bf16[16,192,128]{2,1,0:T(8,128)(2,1)S(1)}, u32[]{:S(2)}, u32[]{:S(2)}) async-start(bf16[16,192,128]{2,1,0:T(8,128)(2,1)} %get-tuple-element.47), calls=%async_computation | async-start | bytes 1572864 | tf_op jit(solution)/shard_map/all_to_all | solution.py:629
  26.7 3.7 %collective-permute-start = (bf16[16,192,128]{2,1,0:T(8,128)(2,1)S(1)}, bf16[16,192,128]{2,1,0:T(8,128)(2,1)S(1)}, u32[]{:S(2)}, u32[]{:S(2)}) collective-permute-start(bf16[16,192,128]{2,1,0:T(8,128)(2,1)S(1)} %all-to-all-done.refs_1_.refs_5_), channel_id=1, source_target_pairs={{0,1},{1,0},{2,3},{3,2},{4,5},{5,4},{6,7},{7,6},{8,9},{9,8},{10,11... | collective-permute-start | bytes 2359304 | tf_op jit(solution)/shard_map/ppermute | solution.py:597
  26.7 19.7 %all-to-all-start.1 = ((bf16[16,128,128]{2,1,0:T(8,128)(2,1)}), bf16[16,128,128]{2,1,0:T(8,128)(2,1)S(1)}, u32[]{:S(2)}, u32[]{:S(2)}) async-start(bf16[16,128,128]{2,1,0:T(8,128)(2,1)} %shard_map.110), calls=%async_computation.1 | async-start | bytes 1048576 | tf_op jit(solution)/shard_map/all_to_all | solution.py:629
  30.4 49.6 %copy-start.12 = (s32[3]{0:T(128)}, s32[3]{0:T(128)S(1)}, u32[]{:S(2)}) copy-start(s32[3]{0:T(128)S(1)} %pad_add_fusion.refs_0_) | copy-start | bytes 40
  31.5 11.0 %collective-permute-start.1 = (f32[128,512]{1,0:T(8,128)S(1)}, f32[128,512]{1,0:T(8,128)S(1)}, u32[]{:S(2)}, u32[]{:S(2)}) collective-permute-start(f32[128,512]{1,0:T(8,128)S(1)} %get-tuple-element.50), channel_id=1, source_target_pairs={{0,16},{8,24},{16,0},{24,8},{1,17},{9,25},{17,1},{25,9},{2,18},{10... | collective-permute-start | bytes 786440 | tf_op jit(solution)/shard_map/ppermute | solution.py:597
  46.4 1.9 %collective-permute-start.2 = (bf16[16,128,128]{2,1,0:T(8,128)(2,1)S(1)}, bf16[16,128,128]{2,1,0:T(8,128)(2,1)S(1)}, u32[]{:S(2)}, u32[]{:S(2)}) collective-permute-start(bf16[16,128,128]{2,1,0:T(8,128)(2,1)S(1)} %all-to-all-done.1.refs_1_.refs_5_), channel_id=1, source_target_pairs={{0,1},{1,0},{2,3},{3,2},{4,5},{5,4},{6,7},{7,6},{8,9},{9,8},{10,11... | collective-permute-start | bytes 1572872 | tf_op jit(solution)/shard_map/ppermute | solution.py:597
  46.4 12.8 %collective-permute-start.3 = (bf16[128,512]{1,0:T(8,128)(2,1)S(1)}, bf16[128,512]{1,0:T(8,128)(2,1)S(1)}, u32[]{:S(2)}, u32[]{:S(2)}) collective-permute-start(bf16[128,512]{1,0:T(8,128)(2,1)S(1)} %get-tuple-element.56.refs_1_), channel_id=1, source_target_pairs={{0,16},{8,24},{16,0},{24,8},{1,17},{9,25},{17,1},{25,9},{2,18},{10... | collective-permute-start | bytes 393224 | tf_op jit(solution)/shard_map/ppermute | solution.py:597
  49.4 12.3 %collective-permute-start.4 = (bf16[128,512]{1,0:T(8,128)(2,1)S(1)}, bf16[128,512]{1,0:T(8,128)(2,1)S(1)}, u32[]{:S(2)}, u32[]{:S(2)}) collective-permute-start(bf16[128,512]{1,0:T(8,128)(2,1)S(1)} %get-tuple-element.57), channel_id=1, source_target_pairs={{0,16},{8,24},{16,0},{24,8},{1,17},{9,25},{17,1},{25,9},{2,18},{10... | collective-permute-start | bytes 393224 | tf_op jit(solution)/shard_map/ppermute | solution.py:597
  50.4 11.2 %collective-permute-start.5 = (bf16[128,512]{1,0:T(8,128)(2,1)S(1)}, bf16[128,512]{1,0:T(8,128)(2,1)S(1)}, u32[]{:S(2)}, u32[]{:S(2)}) collective-permute-start(bf16[128,512]{1,0:T(8,128)(2,1)S(1)} %get-tuple-element.56.refs_1_), channel_id=1, source_target_pairs={{0,1},{1,0},{2,3},{3,2},{4,5},{5,4},{6,7},{7,6},{8,9},{9,8},{10,11... | collective-permute-start | bytes 393224 | tf_op jit(solution)/shard_map/ppermute | solution.py:597
  61.7 1.3 collective-permute-start.6
  64.8 17.8 %all-to-all-start.2 = ((bf16[16,128,128]{2,1,0:T(8,128)(2,1)}), bf16[16,128,128]{2,1,0:T(8,128)(2,1)S(1)}, u32[]{:S(2)}, u32[]{:S(2)}) async-start(bf16[16,128,128]{2,1,0:T(8,128)(2,1)} %shard_map.114), calls=%async_computation.2 | async-start | bytes 1048576 | tf_op jit(solution)/shard_map/all_to_all | solution.py:629
  69.4 9.3 %collective-permute-start.7 = (bf16[128,512]{1,0:T(8,128)(2,1)S(1)}, bf16[128,512]{1,0:T(8,128)(2,1)S(1)}, u32[]{:S(2)}, u32[]{:S(2)}) collective-permute-start(bf16[128,512]{1,0:T(8,128)(2,1)S(1)} %shard_map.115.refs_1_), channel_id=1, source_target_pairs={{0,16},{8,24},{16,0},{24,8},{1,17},{9,25},{17,1},{25,9},{2,18},{10... | collective-permute-start | bytes 393224 | tf_op jit(solution)/shard_map/ppermute | solution.py:597
  70.6 8.1 %collective-permute-start.8 = (bf16[128,512]{1,0:T(8,128)(2,1)S(1)}, bf16[128,512]{1,0:T(8,128)(2,1)S(1)}, u32[]{:S(2)}, u32[]{:S(2)}) collective-permute-start(bf16[128,512]{1,0:T(8,128)(2,1)S(1)} %shard_map.115.refs_1_), channel_id=1, source_target_pairs={{0,1},{1,0},{2,3},{3,2},{4,5},{5,4},{6,7},{7,6},{8,9},{9,8},{10,11... | collective-permute-start | bytes 393224 | tf_op jit(solution)/shard_map/ppermute | solution.py:597
  78.7 1.3 collective-permute-start.9
  81.9 25.5 %copy-start.13 = (s32[3]{0:T(128)S(1)}, s32[3]{0:T(128)}, u32[]{:S(2)}) copy-start(s32[3]{0:T(128)} %copy-done.12) | copy-start | bytes 40
  83.4 17.7 %all-to-all-start.3 = ((bf16[16,160,128]{2,1,0:T(8,128)(2,1)}), bf16[16,160,128]{2,1,0:T(8,128)(2,1)S(1)}, u32[]{:S(2)}, u32[]{:S(2)}) async-start(bf16[16,160,128]{2,1,0:T(8,128)(2,1)} %shard_map.116), calls=%async_computation.3 | async-start | bytes 1310720 | tf_op jit(solution)/shard_map/all_to_all | solution.py:629
  89.2 23.3 %copy-start = (bf16[64,128,128]{2,1,0:T(8,128)(2,1)S(1)}, bf16[64,128,128]{2,1,0:T(8,128)(2,1)}, u32[]{:S(2)}) copy-start(bf16[64,128,128]{2,1,0:T(8,128)(2,1)} %refs_1_.11) | copy-start | bytes 6291460
  89.2 23.3 %copy-start.10 = (f32[64,128]{1,0:T(8,128)S(1)}, f32[64,128]{1,0:T(8,128)}, u32[]{:S(2)}) copy-start(f32[64,128]{1,0:T(8,128)} %get-tuple-element.72.refs_2_.refs_4_) | copy-start | bytes 98308
  105.5 1.9 %collective-permute-start.10 = (bf16[4,32,1280]{2,1,0:T(8,128)(2,1)}, bf16[4,32,1280]{2,1,0:T(8,128)(2,1)S(1)}, u32[]{:S(2)}, u32[]{:S(2)}) collective-permute-start(bf16[4,32,1280]{2,1,0:T(8,128)(2,1)} %get-tuple-element.67), channel_id=1, source_target_pairs={{0,1},{1,0},{2,3},{3,2},{4,5},{5,4},{6,7},{7,6},{8,9},{9,8},{10,11... | collective-permute-start | bytes 983048 | tf_op jit(solution)/shard_map/ppermute | solution.py:597
  109.0 6.2 %collective-permute-start.12 = (bf16[32,1280]{1,0:T(8,128)(2,1)S(1)}, bf16[32,1280]{1,0:T(8,128)(2,1)S(1)}, u32[]{:S(2)}, u32[]{:S(2)}) collective-permute-start(bf16[32,1280]{1,0:T(8,128)(2,1)S(1)} %get-tuple-element.70), channel_id=1, source_target_pairs={{0,4},{1,5},{2,6},{3,7},{4,0},{5,1},{6,2},{7,3},{8,12},{9,13},{10,... | collective-permute-start | bytes 245768 | tf_op jit(solution)/shard_map/ppermute | solution.py:597
  109.1 6.3 %collective-permute-start.13 = (bf16[32,1280]{1,0:T(8,128)(2,1)S(1)}, bf16[32,1280]{1,0:T(8,128)(2,1)S(1)}, u32[]{:S(2)}, u32[]{:S(2)}) collective-permute-start(bf16[32,1280]{1,0:T(8,128)(2,1)S(1)} %get-tuple-element.71), channel_id=1, source_target_pairs={{0,6},{1,7},{2,4},{3,5},{4,2},{5,3},{6,0},{7,1},{8,14},{9,15},{10,... | collective-permute-start | bytes 245768 | tf_op jit(solution)/shard_map/ppermute | solution.py:597
  110.1 6.4 %collective-permute-start.11 = (bf16[32,1280]{1,0:T(8,128)(2,1)S(1)}, bf16[32,1280]{1,0:T(8,128)(2,1)S(1)}, u32[]{:S(2)}, u32[]{:S(2)}) collective-permute-start(bf16[32,1280]{1,0:T(8,128)(2,1)S(1)} %get-tuple-element.69.refs_4_), channel_id=1, source_target_pairs={{0,2},{1,3},{2,0},{3,1},{4,6},{5,7},{6,4},{7,5},{8,10},{9,11},{10,... | collective-permute-start | bytes 245768 | tf_op jit(solution)/shard_map/ppermute | solution.py:597
  116.5 4.6 %collective-permute-start.14 = (bf16[32,1408]{1,0:T(8,128)(2,1)S(1)}, bf16[32,1408]{1,0:T(8,128)(2,1)S(1)}, u32[]{:S(2)}, u32[]{:S(2)}) collective-permute-start(bf16[32,1408]{1,0:T(8,128)(2,1)S(1)} %shard_map.121), channel_id=1, source_target_pairs={{0,8},{8,0},{16,24},{24,16},{1,9},{9,1},{17,25},{25,17},{2,10},{10... | collective-permute-start | bytes 270344 | tf_op jit(solution)/shard_map/ppermute | solution.py:597
  121.2 6.5 %collective-permute-start.15 = (bf16[32,1408]{1,0:T(8,128)(2,1)S(1)}, bf16[32,1408]{1,0:T(8,128)(2,1)S(1)}, u32[]{:S(2)}, u32[]{:S(2)}) collective-permute-start(bf16[32,1408]{1,0:T(8,128)(2,1)S(1)} %add_convert_fusion.1), channel_id=1, source_target_pairs={{0,16},{8,24},{16,0},{24,8},{1,17},{9,25},{17,1},{25,9},{2,18},{10... | collective-permute-start | bytes 270344 | tf_op jit(solution)/shard_map/ppermute | solution.py:597
  (12 other events, 93.4 us)

commit v17 on v16

--- a/solution.py
+++ b/solution.py
@@ -255,7 +255,7 @@
     share = jnp.full((heads, channels), 1.0 / channels, jnp.bfloat16)
     left = jnp.concatenate([first, second, third, share], axis=0)
     average = jnp.full((channels, channels), 1.0 / channels, jnp.bfloat16)
-    step_rows = 32
+    step_rows = 64
 
     def rows(step, carry):
         start = pl.multiple_of(step * step_rows, step_rows)
@@ -545,7 +545,7 @@
         pair_weight_ref[...] = share if h == 0 else pair_weight_ref[...] + share
 
 
-def call(kernel, outs, *args, scratch=(), place=None, flops=0, after=(), outside=0, late=0):
+def call(kernel, outs, *args, scratch=(), place=None, flops=0, after=(), outside=0, late=0, limit=None):
     whole, anywhere = pl.BlockSpec(memory_space=pltpu.VMEM), pl.BlockSpec(memory_space=pl.ANY)
     specs = [anywhere] * outside + [whole] * (len(args) - outside)
     ahead = () if place is None else (place,)
@@ -586,7 +586,7 @@
         out_specs=[whole] * len(shapes),
         scratch_shapes=[*scratch, *held],
         compiler_params=pltpu.CompilerParams(
-            vmem_limit_bytes=ARGUMENT_VMEM_LIMIT if outside else VMEM_LIMIT
+            vmem_limit_bytes=limit or (ARGUMENT_VMEM_LIMIT if outside else VMEM_LIMIT)
         ),
         cost_estimate=pl.CostEstimate(flops=flops, bytes_accessed=moved, transcendentals=0),
     )(*ahead, *args, *after)
@@ -663,11 +663,10 @@
         softmax_kernel, [(quarter, f32), (quarter, bf16)], logit_mine, logit_other,
         flops=total * total,
     )
-    value_blocks, probs = lax.optimization_barrier((value_blocks, probs))
     probs_far = swapped(probs, "seq", seq_half)
+    value_blocks, probs_far = lax.optimization_barrier((value_blocks, probs_far))
     grad_mine, grad_sent = scores(value_blocks, residues, 0, False, bf16)
     grad_other = swapped(grad_sent, "seq", seq_half)
-    probs_far, grad_other = lax.optimization_barrier((probs_far, grad_other))
 
     def products(quarters, blocks, first_row, second_row, with_share, factor):
         rows = 2 * residues + (residues // 2 if with_share else 0)
@@ -686,8 +685,8 @@
         return mine, far, swapped(mine, "res", 1), swapped(far, "res", 1)
 
     attended = products(with_near(probs, probs_far), value_blocks, 0, residues, False, 1.0)
+    attended, grad_other = lax.optimization_barrier((attended, grad_other))
     attended_blocks = across(attended)
-    grad_other = lax.optimization_barrier((attended, grad_other))[1]
     (grad_logits,) = call(
         softmax_gradient_kernel, [(quarter, bf16)], softmax_out, grad_mine, grad_other,
         flops=total * total,
@@ -717,7 +716,7 @@
         [((tokens, 2 * width), bf16), part_rows, part_rows],
         normed, attended_sums, grad_blocks,
         scratch=[pltpu.VMEM((width, columns), bf16)],
-        place=place, flops=4 * tokens * width * width, outside=2, late=2,
+        place=place, flops=4 * tokens * width * width, outside=2, late=2, limit=VMEM_LIMIT,
     )
     own, *sent = call(
         core_sum_kernel,

time: 139 us -> 138 us (level)
  starting transfers between devices: 30.4 us -> 43.8 us
  waiting for transfers between devices: 61.8 us -> 51.2 us
  Pallas kernels: 31.7 us -> 29.4 us
  local copies, waits for them, and re-layouts: 3.78 us -> 1.99 us
    all_to_all x4, starting transfers between devices: 20.1 us -> 27.7 us  [across(): lax.all_to_all(blocks, ('seq', 'res'), 0, 0, axis_index_groups=groups, ti...]
    ppermute x16, waiting for transfers between devices: 39.1 us -> 32 us  [swapped(): lax.ppermute(mine, axis_name, [(a, a ^ distance) for a in range(size)])]
    ppermute x16, starting transfers between devices: 10.3 us -> 16.1 us  [swapped(): lax.ppermute(mine, axis_name, [(a, a ^ distance) for a in range(size)])]
    all_to_all x4, waiting for transfers between devices: 22.7 us -> 19.2 us  [across(): lax.all_to_all(blocks, ('seq', 'res'), 0, 0, axis_index_groups=groups, ti...]
    pallas_call x16, Pallas kernels: 31.7 us -> 29.4 us  [call(): pl.pallas_call(wrapped, out_shape=shapes, in_specs=[pl.BlockSpec(memory_s...]
    unnamed x32 -> x22, local copies, waits for them, and re-layouts: 3.78 us -> 1.99 us
  transfers between devices with their start and end apart: 20 -> 20, of which waited for: 17 -> 16; matrix products, arithmetic and copies ran while one was open for 0% -> 0% of each run, Pallas kernels for 13% -> 15%
where the time goes in v17:
time: 138 us; the launch traced here: 137 us
  waiting for transfers between devices  51.2 us (37%)
  starting transfers between devices  43.8 us (32%)
  Pallas kernels  29.4 us (21%)
  blocking collectives  9.35 us (7%)
  local copies, waits for them, and re-layouts  1.99 us (1%)
    ppermute x16, waiting for transfers between devices, swapped(): lax.ppermute(mine, axis_name, [(a, a ^ distance) for a in range(size)])  32 us
    pallas_call x16, Pallas kernels, call(): pl.pallas_call(wrapped, out_shape=shapes, in_specs=[pl.BlockSpec(memory_s...  29.4 us
    all_to_all x4, starting transfers between devices, across(): lax.all_to_all(blocks, ('seq', 'res'), 0, 0, axis_index_groups=groups, ti...  27.7 us
    all_to_all x4, waiting for transfers between devices, across(): lax.all_to_all(blocks, ('seq', 'res'), 0, 0, axis_index_groups=groups, ti...  19.2 us
    ppermute x16, starting transfers between devices, swapped(): lax.ppermute(mine, axis_name, [(a, a ^ distance) for a in range(size)])  16.1 us
    all_gather x1, blocking collectives, head_body(): lax.all_gather(part, 'res', axis=0)  9.35 us
  transfers between devices with their start and end apart: 20, of which 16 were waited for; matrix products, arithmetic and copies ran while one was open for 0% of the time, Pallas kernels for 15%

profile of v17, /device:TPU:0, one launch (start us, length us, event | category | flops | bytes accessed | tf_op | source)
XLA Modules:
  0.0 136.8 jit_solution(1643859418852466215)
XLA Ops:
  0.6 6.1 %shard_map.109 = (bf16[16,192,128]{2,1,0:T(8,128)(2,1)}, f32[8,64,128]{2,1,0:T(8,128)}, f32[64,128]{1,0:T(8,128)}, f32[64,128]{1,0:T(8,128)}) custom-call(bf16[8,64,256]{2,1,0:T(8,128)(2,1)} %refs_0_.7, bf16[256,1024]{1,0:T(8,128)(2,1)} %refs_1_.10, bf16[64,128,128]{2,1,0:T(8,128)(2,1)} %refs_1_.11, f32[8,128]{1,0:T(8,128)} %bitcast.7), custom_call_target="tpu_custom_call" | custom-call | flops 268435456 | bytes 4001792 | tf_op jit(solution)/shard_map/pallas_call | solution.py:580
  6.8 6.3 %all-to-all-start = ((bf16[16,192,128]{2,1,0:T(8,128)(2,1)}), bf16[16,192,128]{2,1,0:T(8,128)(2,1)S(1)}, u32[]{:S(2)}, u32[]{:S(2)}) async-start(bf16[16,192,128]{2,1,0:T(8,128)(2,1)} %get-tuple-element.46), calls=%async_computation | async-start | bytes 1572864 | tf_op jit(solution)/shard_map/all_to_all | solution.py:629
  13.1 2.7 %shard_map.110 = bf16[16,128,128]{2,1,0:T(8,128)(2,1)} custom-call(bf16[8,64,256]{2,1,0:T(8,128)(2,1)} %refs_0_.7, bf16[8,64,256]{2,1,0:T(8,128)(2,1)} %refs_1_.8, bf16[256,1024]{1,0:T(8,128)(2,1)} %refs_1_.10, bf16[256,256]{1,0:T(8,128)(2,1)} %refs_3_.3), custom_call_target="tpu_custom_call" | custom-call | flops 268435456 | bytes 1703936 | tf_op jit(solution)/shard_map/pallas_call | solution.py:580
  15.8 10.6 %all-to-all-done.refs_1_.refs_5_ = bf16[16,192,128]{2,1,0:T(8,128)(2,1)S(1)} async-done(((bf16[16,192,128]{2,1,0:T(8,128)(2,1)}), bf16[16,192,128]{2,1,0:T(8,128)(2,1)S(1)}, u32[]{:S(2)}, u32[]{:S(2)}) %all-to-all-start) | async-done | bytes 786464 | tf_op jit(solution)/shard_map/all_to_all | solution.py:629
  26.4 3.6 %all-to-all-start.1 = ((bf16[16,128,128]{2,1,0:T(8,128)(2,1)}), bf16[16,128,128]{2,1,0:T(8,128)(2,1)S(1)}, u32[]{:S(2)}, u32[]{:S(2)}) async-start(bf16[16,128,128]{2,1,0:T(8,128)(2,1)} %shard_map.110), calls=%async_computation.1 | async-start | bytes 1048576 | tf_op jit(solution)/shard_map/all_to_all | solution.py:629
  31.2 2.7 %collective-permute-start.1 = (f32[128,512]{1,0:T(8,128)S(1)}, f32[128,512]{1,0:T(8,128)S(1)}, u32[]{:S(2)}, u32[]{:S(2)}) collective-permute-start(f32[128,512]{1,0:T(8,128)S(1)} %get-tuple-element.49), channel_id=1, source_target_pairs={{0,16},{8,24},{16,0},{24,8},{1,17},{9,25},{17,1},{25,9},{2,18},{10... | collective-permute-start | bytes 786440 | tf_op jit(solution)/shard_map/ppermute | solution.py:597
  33.8 8.4 %collective-permute-done.1.refs_1_ = f32[128,512]{1,0:T(8,128)S(1)} collective-permute-done((f32[128,512]{1,0:T(8,128)S(1)}, f32[128,512]{1,0:T(8,128)S(1)}, u32[]{:S(2)}, u32[]{:S(2)}) %collective-permute-start.1) | collective-permute-done | bytes 262176 | tf_op jit(solution)/shard_map/ppermute | solution.py:597
  42.4 3.5 %collective-permute-start.2 = (bf16[128,512]{1,0:T(8,128)(2,1)S(1)}, bf16[128,512]{1,0:T(8,128)(2,1)S(1)}, u32[]{:S(2)}, u32[]{:S(2)}) collective-permute-start(bf16[128,512]{1,0:T(8,128)(2,1)S(1)} %get-tuple-element.52.refs_1_), channel_id=1, source_target_pairs={{0,16},{8,24},{16,0},{24,8},{1,17},{9,25},{17,1},{25,9},{2,18},{10... | collective-permute-start | bytes 393224 | tf_op jit(solution)/shard_map/ppermute | solution.py:597
  46.1 3.2 %collective-permute-done.2.refs_2_ = bf16[128,512]{1,0:T(8,128)(2,1)S(1)} collective-permute-done((bf16[128,512]{1,0:T(8,128)(2,1)S(1)}, bf16[128,512]{1,0:T(8,128)(2,1)S(1)}, u32[]{:S(2)}, u32[]{:S(2)}) %collective-permute-start.2) | collective-permute-done | bytes 131104 | tf_op jit(solution)/shard_map/ppermute | solution.py:597
  52.3 2.7 %collective-permute-start.6 = (bf16[128,512]{1,0:T(8,128)(2,1)S(1)}, bf16[128,512]{1,0:T(8,128)(2,1)S(1)}, u32[]{:S(2)}, u32[]{:S(2)}) collective-permute-start(bf16[128,512]{1,0:T(8,128)(2,1)S(1)} %get-tuple-element.56), channel_id=1, source_target_pairs={{0,16},{8,24},{16,0},{24,8},{1,17},{9,25},{17,1},{25,9},{2,18},{10... | collective-permute-start | bytes 393224 | tf_op jit(solution)/shard_map/ppermute | solution.py:597
  55.0 1.8 %shard_map.114 = bf16[16,128,128]{2,1,0:T(8,128)(2,1)} custom-call(s32[3]{0:T(128)S(1)} %pad_add_fusion.refs_0_, bf16[128,512]{1,0:T(8,128)(2,1)S(1)} %get-tuple-element.52.refs_1_, bf16[128,512]{1,0:T(8,128)(2,1)S(1)} %collective-permute-done.2.refs_2_, bf16[128,512]{1,0:T(8,128)(2,1)S(1)} %collective-permute-done.4.refs_3_, ...), custom_call_target="tpu_custom_call" | custom-call | flops 268435456 | bytes 1572864 | tf_op jit(solution)/shard_map/pallas_call | solution.py:580
  56.8 2.0 %collective-permute-done.6.refs_2_ = bf16[128,512]{1,0:T(8,128)(2,1)S(1)} collective-permute-done((bf16[128,512]{1,0:T(8,128)(2,1)S(1)}, bf16[128,512]{1,0:T(8,128)(2,1)S(1)}, u32[]{:S(2)}, u32[]{:S(2)}) %collective-permute-start.6) | collective-permute-done | bytes 131104 | tf_op jit(solution)/shard_map/ppermute | solution.py:597
  58.8 10.9 %all-to-all-start.2 = ((bf16[16,128,128]{2,1,0:T(8,128)(2,1)}), bf16[16,128,128]{2,1,0:T(8,128)(2,1)S(1)}, u32[]{:S(2)}, u32[]{:S(2)}) async-start(bf16[16,128,128]{2,1,0:T(8,128)(2,1)} %shard_map.114), calls=%async_computation.2 | async-start | bytes 1048576 | tf_op jit(solution)/shard_map/all_to_all | solution.py:629
  69.9 2.2 %collective-permute-start.7 = (bf16[128,512]{1,0:T(8,128)(2,1)S(1)}, bf16[128,512]{1,0:T(8,128)(2,1)S(1)}, u32[]{:S(2)}, u32[]{:S(2)}) collective-permute-start(bf16[128,512]{1,0:T(8,128)(2,1)S(1)} %shard_map.115.refs_1_), channel_id=1, source_target_pairs={{0,16},{8,24},{16,0},{24,8},{1,17},{9,25},{17,1},{25,9},{2,18},{10... | collective-permute-start | bytes 393224 | tf_op jit(solution)/shard_map/ppermute | solution.py:597
  72.2 6.9 %collective-permute-done.7.refs_2_ = bf16[128,512]{1,0:T(8,128)(2,1)S(1)} collective-permute-done((bf16[128,512]{1,0:T(8,128)(2,1)S(1)}, bf16[128,512]{1,0:T(8,128)(2,1)S(1)}, u32[]{:S(2)}, u32[]{:S(2)}) %collective-permute-start.7) | collective-permute-done | bytes 131104 | tf_op jit(solution)/shard_map/ppermute | solution.py:597
  80.5 1.9 %shard_map.116 = bf16[16,160,128]{2,1,0:T(8,128)(2,1)} custom-call(s32[3]{0:T(128)S(1)} %pad_add_fusion.refs_0_, bf16[128,512]{1,0:T(8,128)(2,1)S(1)} %shard_map.115.refs_1_, bf16[128,512]{1,0:T(8,128)(2,1)S(1)} %collective-permute-done.7.refs_2_, bf16[128,512]{1,0:T(8,128)(2,1)S(1)} %collective-permute-done.8.refs_3_, ...), custom_call_target="tpu_custom_call" | custom-call | flops 268435456 | bytes 1966080 | tf_op jit(solution)/shard_map/pallas_call | solution.py:580
  83.1 6.9 %all-to-all-start.3 = ((bf16[16,160,128]{2,1,0:T(8,128)(2,1)}), bf16[16,160,128]{2,1,0:T(8,128)(2,1)S(1)}, u32[]{:S(2)}, u32[]{:S(2)}) async-start(bf16[16,160,128]{2,1,0:T(8,128)(2,1)} %shard_map.116), calls=%async_computation.3 | async-start | bytes 1310720 | tf_op jit(solution)/shard_map/all_to_all | solution.py:629
  90.1 4.2 %shard_map.117 = (bf16[8,64,256]{2,1,0:T(8,128)(2,1)}, bf16[512,512]{1,0:T(8,128)(2,1)}, bf16[512,256]{1,0:T(8,128)(2,1)}, bf16[256,768]{1,0:T(8,128)(2,1)}) custom-call(bf16[8,64,256]{2,1,0:T(8,128)(2,1)} %refs_0_.7, bf16[8,64,256]{2,1,0:T(8,128)(2,1)} %refs_1_.8, bf16[256,1024]{1,0:T(8,128)(2,1)} %refs_1_.10, bf16[256,256]{1,0:T(8,128)(2,1)} %refs_3_.3, ...), custom_call_target="tpu_custom_call" | custom-call | flops 469762048 | bytes 3145728 | tf_op jit(solution)/shard_map/pallas_call | solution.py:580
  94.3 7.7 %all-to-all-done.3.refs_3_.refs_0_ = bf16[16,160,128]{2,1,0:T(8,128)(2,1)S(1)} async-done(((bf16[16,160,128]{2,1,0:T(8,128)(2,1)}), bf16[16,160,128]{2,1,0:T(8,128)(2,1)S(1)}, u32[]{:S(2)}, u32[]{:S(2)}) %all-to-all-start.3) | async-done | bytes 655392 | tf_op jit(solution)/shard_map/all_to_all | solution.py:629
  108.8 2.5 %collective-permute-start.11 = (bf16[32,1280]{1,0:T(8,128)(2,1)S(1)}, bf16[32,1280]{1,0:T(8,128)(2,1)S(1)}, u32[]{:S(2)}, u32[]{:S(2)}) collective-permute-start(bf16[32,1280]{1,0:T(8,128)(2,1)S(1)} %get-tuple-element.67.refs_4_), channel_id=1, source_target_pairs={{0,2},{1,3},{2,0},{3,1},{4,6},{5,7},{6,4},{7,5},{8,10},{9,11},{10,... | collective-permute-start | bytes 245768 | tf_op jit(solution)/shard_map/ppermute | solution.py:597
  117.2 2.7 %collective-permute-done.14 = bf16[32,1408]{1,0:T(8,128)(2,1)S(1)} collective-permute-done((bf16[32,1408]{1,0:T(8,128)(2,1)S(1)}, bf16[32,1408]{1,0:T(8,128)(2,1)S(1)}, u32[]{:S(2)}, u32[]{:S(2)}) %collective-permute-start.14) | collective-permute-done | bytes 90144 | tf_op jit(solution)/shard_map/ppermute | solution.py:597
  120.0 4.3 %shard_map.123 = bf16[64,128,128]{2,1,0:T(8,128)(2,1)} custom-call(bf16[16,160,128]{2,1,0:T(8,128)(2,1)S(1)} %all-to-all-done.3.refs_3_.refs_0_, bf16[64,128,128]{2,1,0:T(8,128)(2,1)S(1)} %copy-done, f32[8,128]{1,0:T(8,128)S(1)} %bitcast.8, f32[8,64,128]{2,1,0:T(8,128)S(1)} %copy-done.5, f32[64,128]{1,0:T(8,128)S(1)} %copy-done.7, f32[64,128]{1,0:T(8,128)S(1)} %copy-done.8), custom_call_target="tpu_custom_call" | custom-call | flops 268435456 | bytes 5181440 | tf_op jit(solution)/shard_map/pallas_call | solution.py:580
  124.3 2.0 %collective-permute-done.15 = bf16[32,1408]{1,0:T(8,128)(2,1)S(1)} collective-permute-done((bf16[32,1408]{1,0:T(8,128)(2,1)S(1)}, bf16[32,1408]{1,0:T(8,128)(2,1)S(1)}, u32[]{:S(2)}, u32[]{:S(2)}) %collective-permute-start.15) | collective-permute-done | bytes 90144 | tf_op jit(solution)/shard_map/ppermute | solution.py:597
  126.4 9.3 %all-gather = bf16[256,1408]{1,0:T(8,128)(2,1)S(1)} all-gather(bf16[32,1408]{1,0:T(8,128)(2,1)S(1)} %add_convert_fusion), channel_id=2, replica_groups=mesh['seq'=4,'res'=8] {'res'}, dimensions={0}, use_global_device_ids=true | all-gather | bytes 811008 | tf_op jit(solution)/shard_map/all_gather | solution.py:759
  (58 shorter events, 20.6 us)
Async XLA Ops:
  6.8 19.7 %all-to-all-start = ((bf16[16,192,128]{2,1,0:T(8,128)(2,1)}), bf16[16,192,128]{2,1,0:T(8,128)(2,1)S(1)}, u32[]{:S(2)}, u32[]{:S(2)}) async-start(bf16[16,192,128]{2,1,0:T(8,128)(2,1)} %get-tuple-element.46), calls=%async_computation | async-start | bytes 1572864 | tf_op jit(solution)/shard_map/all_to_all | solution.py:629
  26.4 3.7 %collective-permute-start = (bf16[16,192,128]{2,1,0:T(8,128)(2,1)S(1)}, bf16[16,192,128]{2,1,0:T(8,128)(2,1)S(1)}, u32[]{:S(2)}, u32[]{:S(2)}) collective-permute-start(bf16[16,192,128]{2,1,0:T(8,128)(2,1)S(1)} %all-to-all-done.refs_1_.refs_5_), channel_id=1, source_target_pairs={{0,1},{1,0},{2,3},{3,2},{4,5},{5,4},{6,7},{7,6},{8,9},{9,8},{10,11... | collective-permute-start | bytes 2359304 | tf_op jit(solution)/shard_map/ppermute | solution.py:597
  26.4 19.7 %all-to-all-start.1 = ((bf16[16,128,128]{2,1,0:T(8,128)(2,1)}), bf16[16,128,128]{2,1,0:T(8,128)(2,1)S(1)}, u32[]{:S(2)}, u32[]{:S(2)}) async-start(bf16[16,128,128]{2,1,0:T(8,128)(2,1)} %shard_map.110), calls=%async_computation.1 | async-start | bytes 1048576 | tf_op jit(solution)/shard_map/all_to_all | solution.py:629
  31.2 11.0 %collective-permute-start.1 = (f32[128,512]{1,0:T(8,128)S(1)}, f32[128,512]{1,0:T(8,128)S(1)}, u32[]{:S(2)}, u32[]{:S(2)}) collective-permute-start(f32[128,512]{1,0:T(8,128)S(1)} %get-tuple-element.49), channel_id=1, source_target_pairs={{0,16},{8,24},{16,0},{24,8},{1,17},{9,25},{17,1},{25,9},{2,18},{10... | collective-permute-start | bytes 786440 | tf_op jit(solution)/shard_map/ppermute | solution.py:597
  42.4 6.9 %collective-permute-start.2 = (bf16[128,512]{1,0:T(8,128)(2,1)S(1)}, bf16[128,512]{1,0:T(8,128)(2,1)S(1)}, u32[]{:S(2)}, u32[]{:S(2)}) collective-permute-start(bf16[128,512]{1,0:T(8,128)(2,1)S(1)} %get-tuple-element.52.refs_1_), channel_id=1, source_target_pairs={{0,16},{8,24},{16,0},{24,8},{1,17},{9,25},{17,1},{25,9},{2,18},{10... | collective-permute-start | bytes 393224 | tf_op jit(solution)/shard_map/ppermute | solution.py:597
  49.4 1.9 %collective-permute-start.3 = (bf16[16,128,128]{2,1,0:T(8,128)(2,1)S(1)}, bf16[16,128,128]{2,1,0:T(8,128)(2,1)S(1)}, u32[]{:S(2)}, u32[]{:S(2)}) collective-permute-start(bf16[16,128,128]{2,1,0:T(8,128)(2,1)S(1)} %all-to-all-done.1.refs_1_.refs_5_), channel_id=1, source_target_pairs={{0,1},{1,0},{2,3},{3,2},{4,5},{5,4},{6,7},{7,6},{8,9},{9,8},{10,11... | collective-permute-start | bytes 1572872 | tf_op jit(solution)/shard_map/ppermute | solution.py:597
  49.4 5.6 %collective-permute-start.4 = (bf16[128,512]{1,0:T(8,128)(2,1)S(1)}, bf16[128,512]{1,0:T(8,128)(2,1)S(1)}, u32[]{:S(2)}, u32[]{:S(2)}) collective-permute-start(bf16[128,512]{1,0:T(8,128)(2,1)S(1)} %get-tuple-element.52.refs_1_), channel_id=1, source_target_pairs={{0,1},{1,0},{2,3},{3,2},{4,5},{5,4},{6,7},{7,6},{8,9},{9,8},{10,11... | collective-permute-start | bytes 393224 | tf_op jit(solution)/shard_map/ppermute | solution.py:597
  49.9 5.1 %collective-permute-start.5 = (bf16[128,512]{1,0:T(8,128)(2,1)S(1)}, bf16[128,512]{1,0:T(8,128)(2,1)S(1)}, u32[]{:S(2)}, u32[]{:S(2)}) collective-permute-start(bf16[128,512]{1,0:T(8,128)(2,1)S(1)} %collective-permute-done.2.refs_2_), channel_id=1, source_target_pairs={{0,1},{1,0},{2,3},{3,2},{4,5},{5,4},{6,7},{7,6},{8,9},{9,8},{10,11... | collective-permute-start | bytes 393224 | tf_op jit(solution)/shard_map/ppermute | solution.py:597
  52.3 6.5 %collective-permute-start.6 = (bf16[128,512]{1,0:T(8,128)(2,1)S(1)}, bf16[128,512]{1,0:T(8,128)(2,1)S(1)}, u32[]{:S(2)}, u32[]{:S(2)}) collective-permute-start(bf16[128,512]{1,0:T(8,128)(2,1)S(1)} %get-tuple-element.56), channel_id=1, source_target_pairs={{0,16},{8,24},{16,0},{24,8},{1,17},{9,25},{17,1},{25,9},{2,18},{10... | collective-permute-start | bytes 393224 | tf_op jit(solution)/shard_map/ppermute | solution.py:597
  58.8 24.3 %all-to-all-start.2 = ((bf16[16,128,128]{2,1,0:T(8,128)(2,1)}), bf16[16,128,128]{2,1,0:T(8,128)(2,1)S(1)}, u32[]{:S(2)}, u32[]{:S(2)}) async-start(bf16[16,128,128]{2,1,0:T(8,128)(2,1)} %shard_map.114), calls=%async_computation.2 | async-start | bytes 1048576 | tf_op jit(solution)/shard_map/all_to_all | solution.py:629
  69.9 9.3 %collective-permute-start.7 = (bf16[128,512]{1,0:T(8,128)(2,1)S(1)}, bf16[128,512]{1,0:T(8,128)(2,1)S(1)}, u32[]{:S(2)}, u32[]{:S(2)}) collective-permute-start(bf16[128,512]{1,0:T(8,128)(2,1)S(1)} %shard_map.115.refs_1_), channel_id=1, source_target_pairs={{0,16},{8,24},{16,0},{24,8},{1,17},{9,25},{17,1},{25,9},{2,18},{10... | collective-permute-start | bytes 393224 | tf_op jit(solution)/shard_map/ppermute | solution.py:597
  72.1 7.1 %collective-permute-start.8 = (bf16[128,512]{1,0:T(8,128)(2,1)S(1)}, bf16[128,512]{1,0:T(8,128)(2,1)S(1)}, u32[]{:S(2)}, u32[]{:S(2)}) collective-permute-start(bf16[128,512]{1,0:T(8,128)(2,1)S(1)} %shard_map.115.refs_1_), channel_id=1, source_target_pairs={{0,1},{1,0},{2,3},{3,2},{4,5},{5,4},{6,7},{7,6},{8,9},{9,8},{10,11... | collective-permute-start | bytes 393224 | tf_op jit(solution)/shard_map/ppermute | solution.py:597
  79.2 1.3 collective-permute-start.9
  83.1 28.2 %copy-start.7 = (f32[64,128]{1,0:T(8,128)S(1)}, f32[64,128]{1,0:T(8,128)}, u32[]{:S(2)}) copy-start(f32[64,128]{1,0:T(8,128)} %get-tuple-element.70.refs_2_.refs_4_) | copy-start | bytes 98308
  83.1 28.2 %copy-start.8 = (f32[64,128]{1,0:T(8,128)S(1)}, f32[64,128]{1,0:T(8,128)}, u32[]{:S(2)}) copy-start(f32[64,128]{1,0:T(8,128)} %get-tuple-element.71.refs_3_.refs_5_) | copy-start | bytes 98308
  83.1 18.9 %all-to-all-start.3 = ((bf16[16,160,128]{2,1,0:T(8,128)(2,1)}), bf16[16,160,128]{2,1,0:T(8,128)(2,1)S(1)}, u32[]{:S(2)}, u32[]{:S(2)}) async-start(bf16[16,160,128]{2,1,0:T(8,128)(2,1)} %shard_map.116), calls=%async_computation.3 | async-start | bytes 1310720 | tf_op jit(solution)/shard_map/all_to_all | solution.py:629
  90.1 21.2 %copy-start = (bf16[64,128,128]{2,1,0:T(8,128)(2,1)S(1)}, bf16[64,128,128]{2,1,0:T(8,128)(2,1)}, u32[]{:S(2)}) copy-start(bf16[64,128,128]{2,1,0:T(8,128)(2,1)} %refs_1_.11) | copy-start | bytes 6291460
  105.4 10.5 %copy-start.1 = (bf16[256,1024]{1,0:T(8,128)(2,1)S(1)}, bf16[256,1024]{1,0:T(8,128)(2,1)}, u32[]{:S(2)}) copy-start(bf16[256,1024]{1,0:T(8,128)(2,1)} %refs_1_.10) | copy-start | bytes 1572868
  105.4 1.7 %collective-permute-start.10 = (bf16[4,32,1280]{2,1,0:T(8,128)(2,1)S(1)}, bf16[4,32,1280]{2,1,0:T(8,128)(2,1)S(1)}, u32[]{:S(2)}, u32[]{:S(2)}) collective-permute-start(bf16[4,32,1280]{2,1,0:T(8,128)(2,1)S(1)} %get-tuple-element.65), channel_id=1, source_target_pairs={{0,1},{1,0},{2,3},{3,2},{4,5},{5,4},{6,7},{7,6},{8,9},{9,8},{10,11... | collective-permute-start | bytes 983048 | tf_op jit(solution)/shard_map/ppermute | solution.py:597
  107.7 6.2 %collective-permute-start.12 = (bf16[32,1280]{1,0:T(8,128)(2,1)S(1)}, bf16[32,1280]{1,0:T(8,128)(2,1)S(1)}, u32[]{:S(2)}, u32[]{:S(2)}) collective-permute-start(bf16[32,1280]{1,0:T(8,128)(2,1)S(1)} %get-tuple-element.68), channel_id=1, source_target_pairs={{0,4},{1,5},{2,6},{3,7},{4,0},{5,1},{6,2},{7,3},{8,12},{9,13},{10,... | collective-permute-start | bytes 245768 | tf_op jit(solution)/shard_map/ppermute | solution.py:597
  107.8 6.3 %collective-permute-start.13 = (bf16[32,1280]{1,0:T(8,128)(2,1)S(1)}, bf16[32,1280]{1,0:T(8,128)(2,1)S(1)}, u32[]{:S(2)}, u32[]{:S(2)}) collective-permute-start(bf16[32,1280]{1,0:T(8,128)(2,1)S(1)} %get-tuple-element.69), channel_id=1, source_target_pairs={{0,6},{1,7},{2,4},{3,5},{4,2},{5,3},{6,0},{7,1},{8,14},{9,15},{10,... | collective-permute-start | bytes 245768 | tf_op jit(solution)/shard_map/ppermute | solution.py:597
  108.8 6.4 %collective-permute-start.11 = (bf16[32,1280]{1,0:T(8,128)(2,1)S(1)}, bf16[32,1280]{1,0:T(8,128)(2,1)S(1)}, u32[]{:S(2)}, u32[]{:S(2)}) collective-permute-start(bf16[32,1280]{1,0:T(8,128)(2,1)S(1)} %get-tuple-element.67.refs_4_), channel_id=1, source_target_pairs={{0,2},{1,3},{2,0},{3,1},{4,6},{5,7},{6,4},{7,5},{8,10},{9,11},{10,... | collective-permute-start | bytes 245768 | tf_op jit(solution)/shard_map/ppermute | solution.py:597
  115.3 4.6 %collective-permute-start.14 = (bf16[32,1408]{1,0:T(8,128)(2,1)S(1)}, bf16[32,1408]{1,0:T(8,128)(2,1)S(1)}, u32[]{:S(2)}, u32[]{:S(2)}) collective-permute-start(bf16[32,1408]{1,0:T(8,128)(2,1)S(1)} %shard_map.121), channel_id=1, source_target_pairs={{0,8},{8,0},{16,24},{24,16},{1,9},{9,1},{17,25},{25,17},{2,10},{10... | collective-permute-start | bytes 270344 | tf_op jit(solution)/shard_map/ppermute | solution.py:597
  119.9 6.5 %collective-permute-start.15 = (bf16[32,1408]{1,0:T(8,128)(2,1)S(1)}, bf16[32,1408]{1,0:T(8,128)(2,1)S(1)}, u32[]{:S(2)}, u32[]{:S(2)}) collective-permute-start(bf16[32,1408]{1,0:T(8,128)(2,1)S(1)} %add_convert_fusion.1), channel_id=1, source_target_pairs={{0,16},{8,24},{16,0},{24,8},{1,17},{9,25},{17,1},{25,9},{2,18},{10... | collective-permute-start | bytes 270344 | tf_op jit(solution)/shard_map/ppermute | solution.py:597
  (7 other events, 44.4 us)

commit v18 on v16

--- a/solution.py
+++ b/solution.py
@@ -255,7 +255,7 @@
     share = jnp.full((heads, channels), 1.0 / channels, jnp.bfloat16)
     left = jnp.concatenate([first, second, third, share], axis=0)
     average = jnp.full((channels, channels), 1.0 / channels, jnp.bfloat16)
-    step_rows = 32
+    step_rows = 64
 
     def rows(step, carry):
         start = pl.multiple_of(step * step_rows, step_rows)
@@ -335,11 +335,38 @@
     low_ref[...] = softmax_out.astype(jnp.bfloat16)
 
 
-def softmax_gradient_kernel(softmax_ref, grad_ref, other_ref, out_ref):
-    softmax_out = softmax_ref[...]
-    grad_probs = grad_ref[...] + other_ref[...].astype(jnp.float32)
-    row_dot = jnp.sum(softmax_out * grad_probs, axis=-1, keepdims=True)
-    out_ref[...] = (softmax_out * (grad_probs - row_dot)).astype(jnp.bfloat16)
+def grad_score_kernel(
+    residues, left_row, right_row, place_ref, own_ref, other_ref, full_ref, sent_ref
+):
+    core = place_ref[0]
+    count = own_ref.shape[0] // 2
+    part = residues // 2
+    right = jnp.concatenate(
+        [lanes_of(own_ref, right_row, residues), lanes_of(other_ref, right_row, residues)], axis=1
+    )
+    rows = pl.ds(pl.multiple_of(left_row + core * part, part), part)
+    left = [
+        jnp.concatenate(
+            [r[p * count + k, rows, :] for r in (own_ref, other_ref) for p in range(2)], axis=1
+        )
+        for k in range(count)
+    ]
+    terms = f32_dot(jnp.concatenate(left, axis=0), right, NT)
+    full_ref[...] = terms
+    sent_ref[...] = terms.astype(jnp.bfloat16)
+
+
+def softmax_gradient_kernel(
+    place_ref, softmax_ref, far_ref, grad_ref, other_ref, out_ref, out_far_ref
+):
+    half = place_ref[1]
+    count = softmax_ref.shape[0]
+    for which, probs, ref in ((half, softmax_ref, out_ref), (1 - half, far_ref, out_far_ref)):
+        rows = pl.ds(pl.multiple_of(which * count, count), count)
+        softmax_out = probs[...].astype(jnp.float32)
+        grad_probs = grad_ref[rows, :] + other_ref[rows, :].astype(jnp.float32)
+        row_dot = jnp.sum(softmax_out * grad_probs, axis=-1, keepdims=True)
+        ref[...] = (softmax_out * (grad_probs - row_dot)).astype(jnp.bfloat16)
 
 
 def product_kernel(
@@ -408,7 +435,7 @@
 
 
 def query_weight_kernel(
-    arrive, place_ref, normed_ref, attended_sums_ref, blocks_ref,
+    place_ref, normed_ref, attended_sums_ref, blocks_ref,
     projected_ref, keep_ref, send_ref, sums_ref,
 ):
     width = normed_ref.shape[1]
@@ -418,7 +445,6 @@
         projected_ref[:, t * width : (t + 1) * width] = unpack_heads(
             blocks_ref, t * residues, residues, tiles
         ).astype(jnp.bfloat16)
-    arrive()
     sums_ref[:, : 2 * width] = f32_dot(normed_ref[...], projected_ref[...], TN).astype(
         jnp.bfloat16
     )
@@ -629,6 +655,11 @@
         return lax.all_to_all(blocks, ("seq", "res"), 0, 0, axis_index_groups=groups, tiled=True)
 
     x, grad, wc, wo = alignment_rows, updated_gradient, combined_weight, output_weight
+    (value_blocks,) = call(
+        value_kernel, [((group, 2 * residues, LANES), bf16)], x, grad, wc, wo,
+        flops=8 * tokens * width * width, outside=4,
+    )
+    value_blocks = across(value_blocks)
     query_blocks, bias, mean, spread = call(
         functools.partial(query_kernel, scale),
         [
@@ -640,60 +671,53 @@
         x, wc, pair_entries, pair_weight.T,
         flops=8 * tokens * width * width, outside=3, late=1,
     )
+    value_blocks, query_blocks = lax.optimization_barrier((value_blocks, query_blocks))
     query_blocks = across(query_blocks)
-    (value_blocks,) = call(
-        value_kernel, [((group, 2 * residues, LANES), bf16)], x, grad, wc, wo,
-        flops=8 * tokens * width * width, outside=4,
-    )
-    query_blocks, value_blocks = lax.optimization_barrier((query_blocks, value_blocks))
-    value_blocks = across(value_blocks)
-
-    def scores(blocks, left_row, right_row, with_bias, kind):
-        return call(
-            functools.partial(score_kernel, residues, left_row, right_row, with_bias),
-            [((total // 4, total), f32), ((total // 4, total), kind)],
-            blocks, swapped(blocks, "res", 1),
-            place=place, flops=2 * total * total * width,
-        )
-
-    logit_mine, logit_sent = scores(query_blocks, 0, residues, True, f32)
-    logit_other = swapped(logit_sent, "seq", seq_half)
-    quarter = (total // 4, total)
+
+    quarter, half_rows = (total // 4, total), (total // 2, total)
+    grad_full, grad_sent = call(
+        functools.partial(grad_score_kernel, residues, residues, 0),
+        [(half_rows, f32), (half_rows, bf16)],
+        value_blocks, swapped(value_blocks, "res", 1),
+        place=place, flops=2 * total * total * width,
+    )
+    grad_other = swapped(grad_sent, "seq", seq_half)
+    query_blocks, grad_other = lax.optimization_barrier((query_blocks, grad_other))
+    logit_mine, logit_sent = call(
+        functools.partial(score_kernel, residues, 0, residues, True),
+        [(quarter, f32), (quarter, f32)],
+        query_blocks, swapped(query_blocks, "res", 1),
+        place=place, flops=2 * total * total * width,
+    )
     softmax_out, probs = call(
-        softmax_kernel, [(quarter, f32), (quarter, bf16)], logit_mine, logit_other,
+        softmax_kernel, [(quarter, f32), (quarter, bf16)],
+        logit_mine, swapped(logit_sent, "seq", seq_half),
         flops=total * total,
     )
-    value_blocks, probs = lax.optimization_barrier((value_blocks, probs))
-    probs_far = swapped(probs, "seq", seq_half)
-    grad_mine, grad_sent = scores(value_blocks, residues, 0, False, bf16)
-    grad_other = swapped(grad_sent, "seq", seq_half)
-    probs_far, grad_other = lax.optimization_barrier((probs_far, grad_other))
-
-    def products(quarters, blocks, first_row, second_row, with_share, factor):
+
+    def products(mine, far, blocks, first_row, second_row, with_share, factor):
         rows = 2 * residues + (residues // 2 if with_share else 0)
         (out,) = call(
             functools.partial(
                 product_kernel, residues, factor, first_row, second_row, with_share
             ),
             [((group, rows, LANES), bf16)],
-            *quarters, blocks,
+            mine, far, swapped(mine, "res", 1), swapped(far, "res", 1), blocks,
             scratch=[pltpu.VMEM((total, total), bf16)],
             place=place, flops=4 * total * total * width,
         )
         return out
 
-    def with_near(mine, far):
-        return mine, far, swapped(mine, "res", 1), swapped(far, "res", 1)
-
-    attended = products(with_near(probs, probs_far), value_blocks, 0, residues, False, 1.0)
+    probs_far = swapped(probs, "seq", seq_half)
+    attended = products(probs, probs_far, value_blocks, 0, residues, False, 1.0)
     attended_blocks = across(attended)
-    grad_other = lax.optimization_barrier((attended, grad_other))[1]
-    (grad_logits,) = call(
-        softmax_gradient_kernel, [(quarter, bf16)], softmax_out, grad_mine, grad_other,
-        flops=total * total,
-    )
-    grad_quarters = with_near(grad_logits, swapped(grad_logits, "seq", seq_half))
-    grad_sums = products(grad_quarters, query_blocks, residues, 0, True, scale)
+    softmax_out = lax.optimization_barrier((attended, softmax_out))[1]
+    grad_logits, grad_far = call(
+        softmax_gradient_kernel, [(quarter, bf16), (quarter, bf16)],
+        softmax_out, probs_far, grad_full, grad_other,
+        place=place, flops=total * total,
+    )
+    grad_sums = products(grad_logits, grad_far, query_blocks, residues, 0, True, scale)
     grad_sums, attended_blocks = lax.optimization_barrier((grad_sums, attended_blocks))
     grad_blocks = across(grad_sums)
 
@@ -712,12 +736,17 @@
     columns = 5 * width
     rows = width // res_size
     part_rows = ((res_size // 2, rows, columns), bf16)
+    (pair_weight_part,) = call(
+        pair_weight_kernel, [((heads, channels), f32)],
+        grad_blocks, pair_entries, mean, spread,
+        scratch=[share], flops=4 * tokens * width * width,
+    )
     query_key, keep, send = call(
         query_weight_kernel,
         [((tokens, 2 * width), bf16), part_rows, part_rows],
         normed, attended_sums, grad_blocks,
         scratch=[pltpu.VMEM((width, columns), bf16)],
-        place=place, flops=4 * tokens * width * width, outside=2, late=2,
+        place=place, flops=4 * tokens * width * width, after=(pair_weight_part,),
     )
     own, *sent = call(
         core_sum_kernel,
@@ -725,31 +754,24 @@
         keep, swapped(send, "res", 1), place=place,
     )
     received = [swapped(t, "res", 2 * flip) for flip, t in enumerate(sent, 1)]
-    (pair_weight_part,) = call(
-        pair_weight_kernel, [((heads, channels), f32)],
-        grad_blocks, pair_entries, mean, spread,
-        scratch=[share], flops=4 * tokens * width * width, after=(sent[0],),
-    )
     (pair_gradient,) = call(
         functools.partial(pair_kernel, 2 * residues),
         [(pair_entries.shape, bf16)],
         grad_blocks, pair_entries, pair_weight.T, bias, mean, spread,
         scratch=[share], flops=8 * tokens * width * width,
     )
-    received, pair_weight_part = lax.optimization_barrier((received, pair_weight_part))
-    (part,) = call(
-        plane_sum_kernel, [((rows, columns + channels), bf16)], own, pair_weight_part, *received
-    )
     (alignment_gradient,) = call(
         alignment_kernel, [(x.shape, bf16)], x, wc, query_key, value_gate,
         flops=8 * tokens * width * width,
     )
-
+    received, alignment_gradient = lax.optimization_barrier((received, alignment_gradient))
+    (part,) = call(
+        plane_sum_kernel, [((rows, columns + channels), bf16)], own, pair_weight_part, *received
+    )
     def added(mine, other):
         return (mine.astype(f32) + other.astype(f32)).astype(bf16)
 
     other_plane = swapped(part, "seq", 1)
-    other_plane, alignment_gradient = lax.optimization_barrier((other_plane, alignment_gradient))
     part = added(part, other_plane)
     other_half = swapped(part, "seq", seq_half)
     other_half, pair_gradient = lax.optimization_barrier((other_half, pair_gradient))

time: 139 us -> 137 us (0.986)
  waiting for transfers between devices: 61.8 us -> 69.2 us
  starting transfers between devices: 30.4 us -> 26.5 us
  local copies, waits for them, and re-layouts: 3.78 us -> 0.1 us
  Pallas kernels: 31.7 us -> 29.3 us
    ppermute x16 -> x15, waiting for transfers between devices: 39.1 us -> 46.8 us  [swapped(): lax.ppermute(mine, axis_name, [(a, a ^ distance) for a in range(size)])]
    unnamed x32 -> x20, local copies, waits for them, and re-layouts: 3.78 us -> 0.1 us
    pallas_call x16, Pallas kernels: 31.7 us -> 29.3 us  [call(): pl.pallas_call(wrapped, out_shape=shapes, in_specs=[pl.BlockSpec(memory_s...]
    all_to_all x4, starting transfers between devices: 20.1 us -> 17.8 us  [across(): lax.all_to_all(blocks, ('seq', 'res'), 0, 0, axis_index_groups=groups, ti...]
    ppermute x16 -> x15, starting transfers between devices: 10.3 us -> 8.7 us  [swapped(): lax.ppermute(mine, axis_name, [(a, a ^ distance) for a in range(size)])]
  transfers between devices with their start and end apart: 20 -> 19, of which waited for: 17 -> 18; matrix products, arithmetic and copies ran while one was open for 0% -> 0% of each run, Pallas kernels for 13% -> 14%
where the time goes in v18:
time: 137 us; the launch traced here: 136 us
  waiting for transfers between devices  69.2 us (51%)
  Pallas kernels  29.3 us (21%)
  starting transfers between devices  26.5 us (19%)
  blocking collectives  10.1 us (7%)
    ppermute x15, waiting for transfers between devices, swapped(): lax.ppermute(mine, axis_name, [(a, a ^ distance) for a in range(size)])  46.8 us
    pallas_call x16, Pallas kernels, call(): pl.pallas_call(wrapped, out_shape=shapes, in_specs=[pl.BlockSpec(memory_s...  29.3 us
    all_to_all x4, waiting for transfers between devices, across(): lax.all_to_all(blocks, ('seq', 'res'), 0, 0, axis_index_groups=groups, ti...  22.5 us
    all_to_all x4, starting transfers between devices, across(): lax.all_to_all(blocks, ('seq', 'res'), 0, 0, axis_index_groups=groups, ti...  17.8 us
    all_gather x1, blocking collectives, head_body(): lax.all_gather(part, 'res', axis=0)  10.1 us
    ppermute x15, starting transfers between devices, swapped(): lax.ppermute(mine, axis_name, [(a, a ^ distance) for a in range(size)])  8.7 us
  transfers between devices with their start and end apart: 19, of which 18 were waited for; matrix products, arithmetic and copies ran while one was open for 0% of the time, Pallas kernels for 14%

profile of v18, /device:TPU:0, one launch (start us, length us, event | category | flops | bytes accessed | tf_op | source)
XLA Modules:
  0.0 136.3 jit_solution(7087642935452694658)
XLA Ops:
  0.6 2.7 %shard_map.109 = bf16[16,128,128]{2,1,0:T(8,128)(2,1)} custom-call(bf16[8,64,256]{2,1,0:T(8,128)(2,1)} %refs_0_.7, bf16[8,64,256]{2,1,0:T(8,128)(2,1)} %refs_1_.8, bf16[256,1024]{1,0:T(8,128)(2,1)} %refs_1_.10, bf16[256,256]{1,0:T(8,128)(2,1)} %refs_3_.3), custom_call_target="tpu_custom_call" | custom-call | flops 268435456 | bytes 1703936 | tf_op jit(solution)/shard_map/pallas_call | solution.py:606
  3.4 6.3 %all-to-all-start = ((bf16[16,128,128]{2,1,0:T(8,128)(2,1)}), bf16[16,128,128]{2,1,0:T(8,128)(2,1)S(1)}, u32[]{:S(2)}, u32[]{:S(2)}) async-start(bf16[16,128,128]{2,1,0:T(8,128)(2,1)} %shard_map.109), calls=%async_computation | async-start | bytes 1048576 | tf_op jit(solution)/shard_map/all_to_all | solution.py:655
  9.7 6.1 %shard_map.110 = (bf16[16,192,128]{2,1,0:T(8,128)(2,1)}, f32[8,64,128]{2,1,0:T(8,128)}, f32[64,128]{1,0:T(8,128)}, f32[64,128]{1,0:T(8,128)}) custom-call(bf16[8,64,256]{2,1,0:T(8,128)(2,1)} %refs_0_.7, bf16[256,1024]{1,0:T(8,128)(2,1)} %refs_1_.10, bf16[64,128,128]{2,1,0:T(8,128)(2,1)} %refs_1_.11, f32[8,128]{1,0:T(8,128)} %bitcast.7), custom_call_target="tpu_custom_call" | custom-call | flops 268435456 | bytes 4001792 | tf_op jit(solution)/shard_map/pallas_call | solution.py:606
  15.8 4.4 %all-to-all-done.refs_1_.refs_5_ = bf16[16,128,128]{2,1,0:T(8,128)(2,1)S(1)} async-done(((bf16[16,128,128]{2,1,0:T(8,128)(2,1)}), bf16[16,128,128]{2,1,0:T(8,128)(2,1)S(1)}, u32[]{:S(2)}, u32[]{:S(2)}) %all-to-all-start) | async-done | bytes 524320 | tf_op jit(solution)/shard_map/all_to_all | solution.py:655
  20.2 3.6 %all-to-all-start.1 = ((bf16[16,192,128]{2,1,0:T(8,128)(2,1)}), bf16[16,192,128]{2,1,0:T(8,128)(2,1)S(1)}, u32[]{:S(2)}, u32[]{:S(2)}) async-start(bf16[16,192,128]{2,1,0:T(8,128)(2,1)} %get-tuple-element.46), calls=%async_computation.1 | async-start | bytes 1572864 | tf_op jit(solution)/shard_map/all_to_all | solution.py:655
  26.7 2.7 %collective-permute-start.1 = (bf16[256,512]{1,0:T(8,128)(2,1)S(1)}, bf16[256,512]{1,0:T(8,128)(2,1)S(1)}, u32[]{:S(2)}, u32[]{:S(2)}) collective-permute-start(bf16[256,512]{1,0:T(8,128)(2,1)S(1)} %get-tuple-element.48), channel_id=1, source_target_pairs={{0,16},{8,24},{16,0},{24,8},{1,17},{9,25},{17,1},{25,9},{2,18},{10... | collective-permute-start | bytes 786440 | tf_op jit(solution)/shard_map/ppermute | solution.py:623
  29.4 9.5 %collective-permute-done.1.refs_4_ = bf16[256,512]{1,0:T(8,128)(2,1)S(1)} collective-permute-done((bf16[256,512]{1,0:T(8,128)(2,1)S(1)}, bf16[256,512]{1,0:T(8,128)(2,1)S(1)}, u32[]{:S(2)}, u32[]{:S(2)}) %collective-permute-start.1) | collective-permute-done | bytes 262176 | tf_op jit(solution)/shard_map/ppermute | solution.py:623
  38.8 4.0 %all-to-all-done.1.refs_1_.refs_5_ = bf16[16,192,128]{2,1,0:T(8,128)(2,1)S(1)} async-done(((bf16[16,192,128]{2,1,0:T(8,128)(2,1)}), bf16[16,192,128]{2,1,0:T(8,128)(2,1)S(1)}, u32[]{:S(2)}, u32[]{:S(2)}) %all-to-all-start.1) | async-done | bytes 786464 | tf_op jit(solution)/shard_map/all_to_all | solution.py:655
  42.8 2.3 %collective-permute-done.2.refs_2_ = bf16[16,192,128]{2,1,0:T(8,128)(2,1)S(1)} collective-permute-done((bf16[16,192,128]{2,1,0:T(8,128)(2,1)S(1)}, bf16[16,192,128]{2,1,0:T(8,128)(2,1)S(1)}, u32[]{:S(2)}, u32[]{:S(2)}) %collective-permute-start.2) | collective-permute-done | bytes 786464 | tf_op jit(solution)/shard_map/ppermute | solution.py:623
  46.2 14.9 %collective-permute-done.3.refs_1_ = f32[128,512]{1,0:T(8,128)S(1)} collective-permute-done((f32[128,512]{1,0:T(8,128)S(1)}, f32[128,512]{1,0:T(8,128)S(1)}, u32[]{:S(2)}, u32[]{:S(2)}) %collective-permute-start.3) | collective-permute-done | bytes 262176 | tf_op jit(solution)/shard_map/ppermute | solution.py:623
  61.4 7.6 %collective-permute-done.4.refs_2_ = bf16[128,512]{1,0:T(8,128)(2,1)S(1)} collective-permute-done((bf16[128,512]{1,0:T(8,128)(2,1)S(1)}, bf16[128,512]{1,0:T(8,128)(2,1)S(1)}, u32[]{:S(2)}, u32[]{:S(2)}) %collective-permute-start.4) | collective-permute-done | bytes 131104 | tf_op jit(solution)/shard_map/ppermute | solution.py:623
  70.4 1.8 %shard_map.114 = bf16[16,128,128]{2,1,0:T(8,128)(2,1)} custom-call(s32[3]{0:T(128)S(1)} %pad_add_fusion.refs_0_, bf16[128,512]{1,0:T(8,128)(2,1)S(1)} %get-tuple-element.52.refs_1_, bf16[128,512]{1,0:T(8,128)(2,1)S(1)} %collective-permute-done.4.refs_2_, bf16[128,512]{1,0:T(8,128)(2,1)S(1)} %collective-permute-done.5.refs_3_, ...), custom_call_target="tpu_custom_call" | custom-call | flops 268435456 | bytes 1572864 | tf_op jit(solution)/shard_map/pallas_call | solution.py:606
  72.2 4.2 %all-to-all-start.2 = ((bf16[16,128,128]{2,1,0:T(8,128)(2,1)}), bf16[16,128,128]{2,1,0:T(8,128)(2,1)}, u32[]{:S(2)}, u32[]{:S(2)}) async-start(bf16[16,128,128]{2,1,0:T(8,128)(2,1)} %shard_map.114), calls=%async_computation.2 | async-start | bytes 1048576 | tf_op jit(solution)/shard_map/all_to_all | solution.py:655
  78.8 1.9 %shard_map.116 = bf16[16,160,128]{2,1,0:T(8,128)(2,1)} custom-call(s32[3]{0:T(128)S(1)} %pad_add_fusion.refs_0_, bf16[128,512]{1,0:T(8,128)(2,1)S(1)} %get-tuple-element.57.refs_1_, bf16[128,512]{1,0:T(8,128)(2,1)S(1)} %get-tuple-element.58.refs_2_, bf16[128,512]{1,0:T(8,128)(2,1)S(1)} %collective-permute-done.7.refs_3_, ...), custom_call_target="tpu_custom_call" | custom-call | flops 268435456 | bytes 1966080 | tf_op jit(solution)/shard_map/pallas_call | solution.py:606
  80.7 6.3 %all-to-all-done.2.refs_4_ = bf16[16,128,128]{2,1,0:T(8,128)(2,1)} async-done(((bf16[16,128,128]{2,1,0:T(8,128)(2,1)}), bf16[16,128,128]{2,1,0:T(8,128)(2,1)}, u32[]{:S(2)}, u32[]{:S(2)}) %all-to-all-start.2) | async-done | bytes 524320 | tf_op jit(solution)/shard_map/all_to_all | solution.py:655
  87.0 3.6 %all-to-all-start.3 = ((bf16[16,160,128]{2,1,0:T(8,128)(2,1)}), bf16[16,160,128]{2,1,0:T(8,128)(2,1)S(1)}, u32[]{:S(2)}, u32[]{:S(2)}) async-start(bf16[16,160,128]{2,1,0:T(8,128)(2,1)} %shard_map.116), calls=%async_computation.3 | async-start | bytes 1310720 | tf_op jit(solution)/shard_map/all_to_all | solution.py:655
  90.6 4.1 %shard_map.117 = (bf16[8,64,256]{2,1,0:T(8,128)(2,1)}, bf16[512,512]{1,0:T(8,128)(2,1)}, bf16[512,256]{1,0:T(8,128)(2,1)}, bf16[256,768]{1,0:T(8,128)(2,1)}) custom-call(bf16[8,64,256]{2,1,0:T(8,128)(2,1)} %refs_0_.7, bf16[8,64,256]{2,1,0:T(8,128)(2,1)} %refs_1_.8, bf16[256,1024]{1,0:T(8,128)(2,1)} %refs_1_.10, bf16[256,256]{1,0:T(8,128)(2,1)} %refs_3_.3, ...), custom_call_target="tpu_custom_call" | custom-call | flops 469762048 | bytes 3145728 | tf_op jit(solution)/shard_map/pallas_call | solution.py:606
  94.7 7.8 %all-to-all-done.3.refs_0_.refs_3_ = bf16[16,160,128]{2,1,0:T(8,128)(2,1)S(1)} async-done(((bf16[16,160,128]{2,1,0:T(8,128)(2,1)}), bf16[16,160,128]{2,1,0:T(8,128)(2,1)S(1)}, u32[]{:S(2)}, u32[]{:S(2)}) %all-to-all-start.3) | async-done | bytes 655392 | tf_op jit(solution)/shard_map/all_to_all | solution.py:655
  105.3 1.6 %collective-permute-done.9.refs_2_ = bf16[4,32,1280]{2,1,0:T(8,128)(2,1)S(1)} collective-permute-done((bf16[4,32,1280]{2,1,0:T(8,128)(2,1)S(1)}, bf16[4,32,1280]{2,1,0:T(8,128)(2,1)S(1)}, u32[]{:S(2)}, u32[]{:S(2)}) %collective-permute-start.9) | collective-permute-done | bytes 327712 | tf_op jit(solution)/shard_map/ppermute | solution.py:623
  108.6 2.5 %collective-permute-start.12 = (bf16[32,1280]{1,0:T(8,128)(2,1)S(1)}, bf16[32,1280]{1,0:T(8,128)(2,1)S(1)}, u32[]{:S(2)}, u32[]{:S(2)}) collective-permute-start(bf16[32,1280]{1,0:T(8,128)(2,1)S(1)} %get-tuple-element.70), channel_id=1, source_target_pairs={{0,6},{1,7},{2,4},{3,5},{4,2},{5,3},{6,0},{7,1},{8,14},{9,15},{10,... | collective-permute-start | bytes 245768 | tf_op jit(solution)/shard_map/ppermute | solution.py:623
  115.0 3.6 %collective-permute-done.13 = bf16[32,1408]{1,0:T(8,128)(2,1)S(1)} collective-permute-done((bf16[32,1408]{1,0:T(8,128)(2,1)S(1)}, bf16[32,1408]{1,0:T(8,128)(2,1)S(1)}, u32[]{:S(2)}, u32[]{:S(2)}) %collective-permute-start.13) | collective-permute-done | bytes 90144 | tf_op jit(solution)/shard_map/ppermute | solution.py:623
  118.9 4.3 %shard_map.123 = bf16[64,128,128]{2,1,0:T(8,128)(2,1)} custom-call(bf16[16,160,128]{2,1,0:T(8,128)(2,1)S(1)} %all-to-all-done.3.refs_0_.refs_3_, bf16[64,128,128]{2,1,0:T(8,128)(2,1)S(1)} %copy-done, f32[8,128]{1,0:T(8,128)S(1)} %bitcast.8, f32[8,64,128]{2,1,0:T(8,128)S(1)} %copy-done.5, f32[64,128]{1,0:T(8,128)S(1)} %copy-done.7, f32[64,128]{1,0:T(8,128)S(1)} %copy-done.8), custom_call_target="tpu_custom_call" | custom-call | flops 268435456 | bytes 5181440 | tf_op jit(solution)/shard_map/pallas_call | solution.py:606
  123.2 1.8 %collective-permute-done.14 = bf16[32,1408]{1,0:T(8,128)(2,1)S(1)} collective-permute-done((bf16[32,1408]{1,0:T(8,128)(2,1)S(1)}, bf16[32,1408]{1,0:T(8,128)(2,1)S(1)}, u32[]{:S(2)}, u32[]{:S(2)}) %collective-permute-start.14) | collective-permute-done | bytes 90144 | tf_op jit(solution)/shard_map/ppermute | solution.py:623
  125.1 10.1 %all-gather = bf16[256,1408]{1,0:T(8,128)(2,1)S(1)} all-gather(bf16[32,1408]{1,0:T(8,128)(2,1)S(1)} %add_convert_fusion), channel_id=2, replica_groups=mesh['seq'=4,'res'=8] {'res'}, dimensions={0}, use_global_device_ids=true | all-gather | bytes 811008 | tf_op jit(solution)/shard_map/all_gather | solution.py:782
  (54 shorter events, 17.7 us)
Async XLA Ops:
  3.4 16.9 %all-to-all-start = ((bf16[16,128,128]{2,1,0:T(8,128)(2,1)}), bf16[16,128,128]{2,1,0:T(8,128)(2,1)S(1)}, u32[]{:S(2)}, u32[]{:S(2)}) async-start(bf16[16,128,128]{2,1,0:T(8,128)(2,1)} %shard_map.109), calls=%async_computation | async-start | bytes 1048576 | tf_op jit(solution)/shard_map/all_to_all | solution.py:655
  20.2 22.6 %all-to-all-start.1 = ((bf16[16,192,128]{2,1,0:T(8,128)(2,1)}), bf16[16,192,128]{2,1,0:T(8,128)(2,1)S(1)}, u32[]{:S(2)}, u32[]{:S(2)}) async-start(bf16[16,192,128]{2,1,0:T(8,128)(2,1)} %get-tuple-element.46), calls=%async_computation.1 | async-start | bytes 1572864 | tf_op jit(solution)/shard_map/all_to_all | solution.py:655
  23.8 2.0 %collective-permute-start = (bf16[16,128,128]{2,1,0:T(8,128)(2,1)S(1)}, bf16[16,128,128]{2,1,0:T(8,128)(2,1)S(1)}, u32[]{:S(2)}, u32[]{:S(2)}) collective-permute-start(bf16[16,128,128]{2,1,0:T(8,128)(2,1)S(1)} %all-to-all-done.refs_1_.refs_5_), channel_id=1, source_target_pairs={{0,1},{1,0},{2,3},{3,2},{4,5},{5,4},{6,7},{7,6},{8,9},{9,8},{10,11... | collective-permute-start | bytes 1572872 | tf_op jit(solution)/shard_map/ppermute | solution.py:623
  26.7 12.1 %collective-permute-start.1 = (bf16[256,512]{1,0:T(8,128)(2,1)S(1)}, bf16[256,512]{1,0:T(8,128)(2,1)S(1)}, u32[]{:S(2)}, u32[]{:S(2)}) collective-permute-start(bf16[256,512]{1,0:T(8,128)(2,1)S(1)} %get-tuple-element.48), channel_id=1, source_target_pairs={{0,16},{8,24},{16,0},{24,8},{1,17},{9,25},{17,1},{25,9},{2,18},{10... | collective-permute-start | bytes 786440 | tf_op jit(solution)/shard_map/ppermute | solution.py:623
  42.8 2.3 %collective-permute-start.2 = (bf16[16,192,128]{2,1,0:T(8,128)(2,1)S(1)}, bf16[16,192,128]{2,1,0:T(8,128)(2,1)S(1)}, u32[]{:S(2)}, u32[]{:S(2)}) collective-permute-start(bf16[16,192,128]{2,1,0:T(8,128)(2,1)S(1)} %all-to-all-done.1.refs_1_.refs_5_), channel_id=1, source_target_pairs={{0,1},{1,0},{2,3},{3,2},{4,5},{5,4},{6,7},{7,6},{8,9},{9,8},{10,11... | collective-permute-start | bytes 2359304 | tf_op jit(solution)/shard_map/ppermute | solution.py:623
  46.1 14.9 %collective-permute-start.3 = (f32[128,512]{1,0:T(8,128)S(1)}, f32[128,512]{1,0:T(8,128)S(1)}, u32[]{:S(2)}, u32[]{:S(2)}) collective-permute-start(f32[128,512]{1,0:T(8,128)S(1)} %get-tuple-element.51), channel_id=1, source_target_pairs={{0,16},{8,24},{16,0},{24,8},{1,17},{9,25},{17,1},{25,9},{2,18},{10... | collective-permute-start | bytes 786440 | tf_op jit(solution)/shard_map/ppermute | solution.py:623
  61.2 7.8 %collective-permute-start.4 = (bf16[128,512]{1,0:T(8,128)(2,1)S(1)}, bf16[128,512]{1,0:T(8,128)(2,1)S(1)}, u32[]{:S(2)}, u32[]{:S(2)}) collective-permute-start(bf16[128,512]{1,0:T(8,128)(2,1)S(1)} %get-tuple-element.52.refs_1_), channel_id=1, source_target_pairs={{0,16},{8,24},{16,0},{24,8},{1,17},{9,25},{17,1},{25,9},{2,18},{10... | collective-permute-start | bytes 393224 | tf_op jit(solution)/shard_map/ppermute | solution.py:623
  61.3 7.7 %collective-permute-start.5 = (bf16[128,512]{1,0:T(8,128)(2,1)S(1)}, bf16[128,512]{1,0:T(8,128)(2,1)S(1)}, u32[]{:S(2)}, u32[]{:S(2)}) collective-permute-start(bf16[128,512]{1,0:T(8,128)(2,1)S(1)} %get-tuple-element.52.refs_1_), channel_id=1, source_target_pairs={{0,1},{1,0},{2,3},{3,2},{4,5},{5,4},{6,7},{7,6},{8,9},{9,8},{10,11... | collective-permute-start | bytes 393224 | tf_op jit(solution)/shard_map/ppermute | solution.py:623
  69.0 1.3 collective-permute-start.6
  72.2 14.8 %all-to-all-start.2 = ((bf16[16,128,128]{2,1,0:T(8,128)(2,1)}), bf16[16,128,128]{2,1,0:T(8,128)(2,1)}, u32[]{:S(2)}, u32[]{:S(2)}) async-start(bf16[16,128,128]{2,1,0:T(8,128)(2,1)} %shard_map.114), calls=%async_computation.2 | async-start | bytes 1048576 | tf_op jit(solution)/shard_map/all_to_all | solution.py:655
  77.1 1.4 %collective-permute-start.7 = (bf16[128,512]{1,0:T(8,128)(2,1)S(1)}, bf16[128,512]{1,0:T(8,128)(2,1)S(1)}, u32[]{:S(2)}, u32[]{:S(2)}) collective-permute-start(bf16[128,512]{1,0:T(8,128)(2,1)S(1)} %get-tuple-element.57.refs_1_), channel_id=1, source_target_pairs={{0,1},{1,0},{2,3},{3,2},{4,5},{5,4},{6,7},{7,6},{8,9},{9,8},{10,11... | collective-permute-start | bytes 393224 | tf_op jit(solution)/shard_map/ppermute | solution.py:623
  77.4 25.1 %copy-start = (bf16[64,128,128]{2,1,0:T(8,128)(2,1)S(1)}, bf16[64,128,128]{2,1,0:T(8,128)(2,1)}, u32[]{:S(2)}) copy-start(bf16[64,128,128]{2,1,0:T(8,128)(2,1)} %refs_1_.11) | copy-start | bytes 6291460
  77.4 25.1 %copy-start.7 = (f32[64,128]{1,0:T(8,128)S(1)}, f32[64,128]{1,0:T(8,128)}, u32[]{:S(2)}) copy-start(f32[64,128]{1,0:T(8,128)} %get-tuple-element.64.refs_2_.refs_4_) | copy-start | bytes 98308
  77.4 25.1 %copy-start.8 = (f32[64,128]{1,0:T(8,128)S(1)}, f32[64,128]{1,0:T(8,128)}, u32[]{:S(2)}) copy-start(f32[64,128]{1,0:T(8,128)} %get-tuple-element.65.refs_3_.refs_5_) | copy-start | bytes 98308
  77.4 1.3 collective-permute-start.8
  87.0 15.5 %all-to-all-start.3 = ((bf16[16,160,128]{2,1,0:T(8,128)(2,1)}), bf16[16,160,128]{2,1,0:T(8,128)(2,1)S(1)}, u32[]{:S(2)}, u32[]{:S(2)}) async-start(bf16[16,160,128]{2,1,0:T(8,128)(2,1)} %shard_map.116), calls=%async_computation.3 | async-start | bytes 1310720 | tf_op jit(solution)/shard_map/all_to_all | solution.py:655
  105.2 13.7 %copy-start.5 = (f32[8,64,128]{2,1,0:T(8,128)S(1)}, f32[8,64,128]{2,1,0:T(8,128)}, u32[]{:S(2)}) copy-start(f32[8,64,128]{2,1,0:T(8,128)} %get-tuple-element.78.refs_3_) | copy-start | bytes 786436
  105.2 13.7 %copy-start.9 = (f32[128,8]{0,1:T(8,128)S(1)}, f32[128,8]{0,1:T(8,128)}, u32[]{:S(2)}) copy-start(f32[128,8]{0,1:T(8,128)} %param.10) | copy-start | bytes 12292
  105.2 1.7 %collective-permute-start.9 = (bf16[4,32,1280]{2,1,0:T(8,128)(2,1)S(1)}, bf16[4,32,1280]{2,1,0:T(8,128)(2,1)S(1)}, u32[]{:S(2)}, u32[]{:S(2)}) collective-permute-start(bf16[4,32,1280]{2,1,0:T(8,128)(2,1)S(1)} %get-tuple-element.67), channel_id=1, source_target_pairs={{0,1},{1,0},{2,3},{3,2},{4,5},{5,4},{6,7},{7,6},{8,9},{9,8},{10,11... | collective-permute-start | bytes 983048 | tf_op jit(solution)/shard_map/ppermute | solution.py:623
  107.5 5.1 %collective-permute-start.10 = (bf16[32,1280]{1,0:T(8,128)(2,1)S(1)}, bf16[32,1280]{1,0:T(8,128)(2,1)S(1)}, u32[]{:S(2)}, u32[]{:S(2)}) collective-permute-start(bf16[32,1280]{1,0:T(8,128)(2,1)S(1)} %get-tuple-element.68), channel_id=1, source_target_pairs={{0,2},{1,3},{2,0},{3,1},{4,6},{5,7},{6,4},{7,5},{8,10},{9,11},{10,... | collective-permute-start | bytes 245768 | tf_op jit(solution)/shard_map/ppermute | solution.py:623
  107.6 5.4 %collective-permute-start.11 = (bf16[32,1280]{1,0:T(8,128)(2,1)S(1)}, bf16[32,1280]{1,0:T(8,128)(2,1)S(1)}, u32[]{:S(2)}, u32[]{:S(2)}) collective-permute-start(bf16[32,1280]{1,0:T(8,128)(2,1)S(1)} %get-tuple-element.69), channel_id=1, source_target_pairs={{0,4},{1,5},{2,6},{3,7},{4,0},{5,1},{6,2},{7,3},{8,12},{9,13},{10,... | collective-permute-start | bytes 245768 | tf_op jit(solution)/shard_map/ppermute | solution.py:623
  108.6 5.3 %collective-permute-start.12 = (bf16[32,1280]{1,0:T(8,128)(2,1)S(1)}, bf16[32,1280]{1,0:T(8,128)(2,1)S(1)}, u32[]{:S(2)}, u32[]{:S(2)}) collective-permute-start(bf16[32,1280]{1,0:T(8,128)(2,1)S(1)} %get-tuple-element.70), channel_id=1, source_target_pairs={{0,6},{1,7},{2,4},{3,5},{4,2},{5,3},{6,0},{7,1},{8,14},{9,15},{10,... | collective-permute-start | bytes 245768 | tf_op jit(solution)/shard_map/ppermute | solution.py:623
  113.9 4.6 %collective-permute-start.13 = (bf16[32,1408]{1,0:T(8,128)(2,1)S(1)}, bf16[32,1408]{1,0:T(8,128)(2,1)S(1)}, u32[]{:S(2)}, u32[]{:S(2)}) collective-permute-start(bf16[32,1408]{1,0:T(8,128)(2,1)S(1)} %shard_map.122), channel_id=1, source_target_pairs={{0,8},{8,0},{16,24},{24,16},{1,9},{9,1},{17,25},{25,17},{2,10},{10... | collective-permute-start | bytes 270344 | tf_op jit(solution)/shard_map/ppermute | solution.py:623
  118.6 6.5 %collective-permute-start.14 = (bf16[32,1408]{1,0:T(8,128)(2,1)S(1)}, bf16[32,1408]{1,0:T(8,128)(2,1)S(1)}, u32[]{:S(2)}, u32[]{:S(2)}) collective-permute-start(bf16[32,1408]{1,0:T(8,128)(2,1)S(1)} %add_convert_fusion.1), channel_id=1, source_target_pairs={{0,16},{8,24},{16,0},{24,8},{1,17},{9,25},{17,1},{25,9},{2,18},{10... | collective-permute-start | bytes 270344 | tf_op jit(solution)/shard_map/ppermute | solution.py:623
  (5 other events, 44.3 us)

commit v19 on v18

--- a/solution.py
+++ b/solution.py
@@ -224,28 +224,29 @@
     return 1.0 / (1.0 + jnp.exp(-logits))
 
 
-def value_kernel(x_ref, grad_ref, wc_ref, wo_ref, out_ref):
+def query_kernel(scale, x_ref, wc_ref, out_ref):
     residues, width = x_ref.shape[1], x_ref.shape[2]
+    normed = normalized(x_ref)[0].astype(jnp.bfloat16)
+    pack_heads(out_ref, 0, f32_dot(normed, wc_ref[:, :width]) * scale, residues)
+    pack_heads(out_ref, residues, f32_dot(normed, wc_ref[:, width : 2 * width]), residues)
+
+
+def centred(weight):
+    return weight - jnp.mean(weight, axis=1, keepdims=True)
+
+
+def value_kernel(
+    arrive, x_ref, grad_ref, wc_ref, wo_ref, pair_ref, weight_ref,
+    out_ref, bias_ref, mean_ref, spread_ref,
+):
+    residues, width = x_ref.shape[1], x_ref.shape[2]
+    heads = weight_ref.shape[0]
     normed = normalized(x_ref)[0].astype(jnp.bfloat16)
     values = f32_dot(normed, wc_ref[:, 2 * width : 3 * width])
     gate = gate_of(f32_dot(normed, wc_ref[:, 3 * width :]))
     grad_gated = f32_dot(grad_ref[...].reshape(-1, width), wo_ref[...], NT)
     pack_heads(out_ref, 0, values, residues)
     pack_heads(out_ref, residues, grad_gated * gate, residues)
-
-
-def centred(weight):
-    return weight - jnp.mean(weight, axis=1, keepdims=True)
-
-
-def query_kernel(
-    scale, arrive, x_ref, wc_ref, pair_ref, weight_ref, out_ref, bias_ref, mean_ref, spread_ref
-):
-    residues, width = x_ref.shape[1], x_ref.shape[2]
-    heads = weight_ref.shape[0]
-    normed = normalized(x_ref)[0].astype(jnp.bfloat16)
-    pack_heads(out_ref, 0, f32_dot(normed, wc_ref[:, :width]) * scale, residues)
-    pack_heads(out_ref, residues, f32_dot(normed, wc_ref[:, width : 2 * width]), residues)
 
     arrive()
     columns, channels = pair_ref.shape[1], pair_ref.shape[2]
@@ -292,7 +293,7 @@
 
 
 def score_kernel(
-    residues, left_row, right_row, with_bias, place_ref, own_ref, other_ref, mine_ref, sent_ref
+    residues, left_row, right_row, place_ref, own_ref, other_ref, mine_ref, sent_ref
 ):
     core, half = place_ref[0], place_ref[1]
     count = own_ref.shape[0] // 2
@@ -316,19 +317,32 @@
                 )
             )
         ref[...] = f32_dot(jnp.concatenate(left, axis=0), right, NT).astype(ref.dtype)
-        if with_bias:
-            for p in range(2):
-                columns = pl.ds(pl.multiple_of((half * 2 + p) * LANES, LANES), LANES)
-                for k in range(count // 2):
-                    block = p * count + which * (count // 2) + k
-                    high = own_ref[block, 2 * residues : 2 * residues + part, :]
-                    low = own_ref[block, 2 * residues + part : 3 * residues, :]
-                    bias = high.astype(jnp.float32) + low.astype(jnp.float32)
-                    ref[k * part : (k + 1) * part, columns] += bias
-
-
-def softmax_kernel(logit_ref, other_ref, out_ref, low_ref):
-    logits = logit_ref[...] + other_ref[...]
+
+
+def bias_kernel(row, place_ref, blocks_ref, mine_ref, sent_ref):
+    half = place_ref[1]
+    count = blocks_ref.shape[0] // 2
+    for which, ref in ((half, mine_ref), (1 - half, sent_ref)):
+        for p in range(2):
+            for k in range(count // 2):
+                block = p * count + which * (count // 2) + k
+                ref[p * (count // 2) + k] = blocks_ref[block, row:, :]
+
+
+def softmax_kernel(
+    place_ref, logit_ref, other_ref, bias_ref, bias_other_ref, out_ref, low_ref
+):
+    half = place_ref[1]
+    count, part = bias_ref.shape[0] // 2, bias_ref.shape[1] // 2
+    out_ref[...] = logit_ref[...] + other_ref[...]
+    for which, ref in ((half, bias_ref), (1 - half, bias_other_ref)):
+        for p in range(2):
+            columns = pl.ds(pl.multiple_of((which * 2 + p) * LANES, LANES), LANES)
+            for k in range(count):
+                high = ref[p * count + k, :part, :].astype(jnp.float32)
+                low = ref[p * count + k, part:, :].astype(jnp.float32)
+                out_ref[k * part : (k + 1) * part, columns] += high + low
+    logits = out_ref[...]
     lifted = jnp.exp(logits - jnp.max(logits, axis=-1, keepdims=True))
     softmax_out = lifted / jnp.sum(lifted, axis=-1, keepdims=True)
     out_ref[...] = softmax_out
@@ -655,26 +669,40 @@
         return lax.all_to_all(blocks, ("seq", "res"), 0, 0, axis_index_groups=groups, tiled=True)
 
     x, grad, wc, wo = alignment_rows, updated_gradient, combined_weight, output_weight
-    (value_blocks,) = call(
-        value_kernel, [((group, 2 * residues, LANES), bf16)], x, grad, wc, wo,
-        flops=8 * tokens * width * width, outside=4,
-    )
-    value_blocks = across(value_blocks)
-    query_blocks, bias, mean, spread = call(
-        functools.partial(query_kernel, scale),
+    (query_blocks,) = call(
+        functools.partial(query_kernel, scale), [((group, 2 * residues, LANES), bf16)], x, wc,
+        flops=8 * tokens * width * width, outside=2,
+    )
+    query_blocks = across(query_blocks)
+    value_blocks, bias, mean, spread = call(
+        value_kernel,
         [
             ((group, 3 * residues, LANES), bf16),
             ((heads, residues, LANES), f32),
             ((residues, LANES), f32),
             ((residues, LANES), f32),
         ],
-        x, wc, pair_entries, pair_weight.T,
-        flops=8 * tokens * width * width, outside=3, late=1,
-    )
-    value_blocks, query_blocks = lax.optimization_barrier((value_blocks, query_blocks))
-    query_blocks = across(query_blocks)
+        x, grad, wc, wo, pair_entries, pair_weight.T,
+        flops=8 * tokens * width * width, outside=5, late=1,
+    )
+    query_blocks, value_blocks = lax.optimization_barrier((query_blocks, value_blocks))
+    value_blocks = across(value_blocks)
 
     quarter, half_rows = (total // 4, total), (total // 2, total)
+    logit_mine, logit_sent = call(
+        functools.partial(score_kernel, residues, 0, residues),
+        [(quarter, f32), (quarter, f32)],
+        query_blocks, swapped(query_blocks, "res", 1),
+        place=place, flops=2 * total * total * width,
+    )
+    logit_other = swapped(logit_sent, "seq", seq_half)
+    value_blocks, logit_other = lax.optimization_barrier((value_blocks, logit_other))
+    bias_half = ((group // 2, residues, LANES), bf16)
+    bias_mine, bias_sent = call(
+        functools.partial(bias_kernel, 2 * residues), [bias_half, bias_half], value_blocks,
+        place=place,
+    )
+    bias_other = swapped(bias_sent, "seq", seq_half)
     grad_full, grad_sent = call(
         functools.partial(grad_score_kernel, residues, residues, 0),
         [(half_rows, f32), (half_rows, bf16)],
@@ -682,17 +710,11 @@
         place=place, flops=2 * total * total * width,
     )
     grad_other = swapped(grad_sent, "seq", seq_half)
-    query_blocks, grad_other = lax.optimization_barrier((query_blocks, grad_other))
-    logit_mine, logit_sent = call(
-        functools.partial(score_kernel, residues, 0, residues, True),
-        [(quarter, f32), (quarter, f32)],
-        query_blocks, swapped(query_blocks, "res", 1),
-        place=place, flops=2 * total * total * width,
-    )
+    bias_other, grad_full = lax.optimization_barrier((bias_other, grad_full))
     softmax_out, probs = call(
         softmax_kernel, [(quarter, f32), (quarter, bf16)],
-        logit_mine, swapped(logit_sent, "seq", seq_half),
-        flops=total * total,
+        logit_mine, logit_other, bias_mine, bias_other,
+        place=place, flops=total * total,
     )
 
     def products(mine, far, blocks, first_row, second_row, with_share, factor):

time: 137 us -> 139 us (1.015)
    all_to_all x4, waiting for transfers between devices: 22.5 us -> 16 us  [across(): lax.all_to_all(blocks, ('seq', 'res'), 0, 0, axis_index_groups=groups, ti...]
    ppermute x15 -> x16, waiting for transfers between devices: 46.8 us -> 52.8 us  [swapped(): lax.ppermute(mine, axis_name, [(a, a ^ distance) for a in range(size)])]
    pallas_call x16 -> x17, Pallas kernels: 29.3 us -> 30.6 us  [call(): pl.pallas_call(wrapped, out_shape=shapes, in_specs=[pl.BlockSpec(memory_s...]
    ppermute x15 -> x16, starting transfers between devices: 8.7 us -> 9.06 us  [swapped(): lax.ppermute(mine, axis_name, [(a, a ^ distance) for a in range(size)])]
  transfers between devices with their start and end apart: 19 -> 20, of which waited for: 18 -> 18; matrix products, arithmetic and copies ran while one was open for 0% -> 0% of each run, Pallas kernels for 14% -> 15%
where the time goes in v19:
time: 139 us; the launch traced here: 138 us
  waiting for transfers between devices  68.9 us (50%)
  Pallas kernels  30.6 us (22%)
  starting transfers between devices  27.2 us (20%)
  blocking collectives  10.1 us (7%)
    ppermute x16, waiting for transfers between devices, swapped(): lax.ppermute(mine, axis_name, [(a, a ^ distance) for a in range(size)])  52.8 us
    pallas_call x17, Pallas kernels, call(): pl.pallas_call(wrapped, out_shape=shapes, in_specs=[pl.BlockSpec(memory_s...  30.6 us
    all_to_all x4, starting transfers between devices, across(): lax.all_to_all(blocks, ('seq', 'res'), 0, 0, axis_index_groups=groups, ti...  18.1 us
    all_to_all x4, waiting for transfers between devices, across(): lax.all_to_all(blocks, ('seq', 'res'), 0, 0, axis_index_groups=groups, ti...  16 us
    all_gather x1, blocking collectives, head_body(): lax.all_gather(part, 'res', axis=0)  10.1 us
    ppermute x16, starting transfers between devices, swapped(): lax.ppermute(mine, axis_name, [(a, a ^ distance) for a in range(size)])  9.06 us
  transfers between devices with their start and end apart: 20, of which 18 were waited for; matrix products, arithmetic and copies ran while one was open for 0% of the time, Pallas kernels for 15%

profile of v19, /device:TPU:0, one launch (start us, length us, event | category | flops | bytes accessed | tf_op | source)
XLA Modules:
  0.0 137.9 jit_solution(9105298361370352484)
XLA Ops:
  0.6 2.6 %shard_map.109 = bf16[16,128,128]{2,1,0:T(8,128)(2,1)} custom-call(bf16[8,64,256]{2,1,0:T(8,128)(2,1)} %refs_0_.7, bf16[256,1024]{1,0:T(8,128)(2,1)} %refs_1_.10), custom_call_target="tpu_custom_call" | custom-call | flops 268435456 | bytes 1310720 | tf_op jit(solution)/shard_map/pallas_call | solution.py:620
  3.3 6.3 %all-to-all-start = ((bf16[16,128,128]{2,1,0:T(8,128)(2,1)}), bf16[16,128,128]{2,1,0:T(8,128)(2,1)S(1)}, u32[]{:S(2)}, u32[]{:S(2)}) async-start(bf16[16,128,128]{2,1,0:T(8,128)(2,1)} %shard_map.109), calls=%async_computation | async-start | bytes 1048576 | tf_op jit(solution)/shard_map/all_to_all | solution.py:669
  9.6 6.3 %shard_map.110 = (bf16[16,192,128]{2,1,0:T(8,128)(2,1)}, f32[8,64,128]{2,1,0:T(8,128)}, f32[64,128]{1,0:T(8,128)}, f32[64,128]{1,0:T(8,128)}) custom-call(bf16[8,64,256]{2,1,0:T(8,128)(2,1)} %refs_0_.7, bf16[8,64,256]{2,1,0:T(8,128)(2,1)} %refs_1_.8, bf16[256,1024]{1,0:T(8,128)(2,1)} %refs_1_.10, bf16[256,256]{1,0:T(8,128)(2,1)} %refs_3_.3, ...), custom_call_target="tpu_custom_call" | custom-call | flops 268435456 | bytes 4395008 | tf_op jit(solution)/shard_map/pallas_call | solution.py:620
  15.9 4.2 %all-to-all-done.refs_1_.refs_5_ = bf16[16,128,128]{2,1,0:T(8,128)(2,1)S(1)} async-done(((bf16[16,128,128]{2,1,0:T(8,128)(2,1)}), bf16[16,128,128]{2,1,0:T(8,128)(2,1)S(1)}, u32[]{:S(2)}, u32[]{:S(2)}) %all-to-all-start) | async-done | bytes 524320 | tf_op jit(solution)/shard_map/all_to_all | solution.py:669
  20.1 3.6 %all-to-all-start.1 = ((bf16[16,192,128]{2,1,0:T(8,128)(2,1)}), bf16[16,192,128]{2,1,0:T(8,128)(2,1)S(1)}, u32[]{:S(2)}, u32[]{:S(2)}) async-start(bf16[16,192,128]{2,1,0:T(8,128)(2,1)} %get-tuple-element.52), calls=%async_computation.1 | async-start | bytes 1572864 | tf_op jit(solution)/shard_map/all_to_all | solution.py:669
  26.7 2.7 %collective-permute-start.1 = (f32[128,512]{1,0:T(8,128)S(1)}, f32[128,512]{1,0:T(8,128)S(1)}, u32[]{:S(2)}, u32[]{:S(2)}) collective-permute-start(f32[128,512]{1,0:T(8,128)S(1)} %get-tuple-element.53), channel_id=1, source_target_pairs={{0,16},{8,24},{16,0},{24,8},{1,17},{9,25},{17,1},{25,9},{2,18},{10... | collective-permute-start | bytes 786440 | tf_op jit(solution)/shard_map/ppermute | solution.py:637
  29.4 9.3 %collective-permute-done.1.refs_2_ = f32[128,512]{1,0:T(8,128)S(1)} collective-permute-done((f32[128,512]{1,0:T(8,128)S(1)}, f32[128,512]{1,0:T(8,128)S(1)}, u32[]{:S(2)}, u32[]{:S(2)}) %collective-permute-start.1) | collective-permute-done | bytes 262176 | tf_op jit(solution)/shard_map/ppermute | solution.py:637
  38.7 4.0 %all-to-all-done.1.refs_1_.refs_5_ = bf16[16,192,128]{2,1,0:T(8,128)(2,1)S(1)} async-done(((bf16[16,192,128]{2,1,0:T(8,128)(2,1)}), bf16[16,192,128]{2,1,0:T(8,128)(2,1)S(1)}, u32[]{:S(2)}, u32[]{:S(2)}) %all-to-all-start.1) | async-done | bytes 786464 | tf_op jit(solution)/shard_map/all_to_all | solution.py:669
  43.3 1.6 %collective-permute-done.3.refs_2_ = bf16[16,192,128]{2,1,0:T(8,128)(2,1)S(1)} collective-permute-done((bf16[16,192,128]{2,1,0:T(8,128)(2,1)S(1)}, bf16[16,192,128]{2,1,0:T(8,128)(2,1)S(1)}, u32[]{:S(2)}, u32[]{:S(2)}) %collective-permute-start.3) | collective-permute-done | bytes 786464 | tf_op jit(solution)/shard_map/ppermute | solution.py:637
  45.9 7.1 %collective-permute-done.2.refs_4_ = bf16[8,64,128]{2,1,0:T(8,128)(2,1)S(1)} collective-permute-done((bf16[8,64,128]{2,1,0:T(8,128)(2,1)S(1)}, bf16[8,64,128]{2,1,0:T(8,128)(2,1)S(1)}, u32[]{:S(2)}, u32[]{:S(2)}) %collective-permute-start.2) | collective-permute-done | bytes 131104 | tf_op jit(solution)/shard_map/ppermute | solution.py:637
  53.9 7.6 %collective-permute-done.4.refs_2_ = bf16[128,512]{1,0:T(8,128)(2,1)S(1)} collective-permute-done((bf16[128,512]{1,0:T(8,128)(2,1)S(1)}, bf16[128,512]{1,0:T(8,128)(2,1)S(1)}, u32[]{:S(2)}, u32[]{:S(2)}) %collective-permute-start.4) | collective-permute-done | bytes 131104 | tf_op jit(solution)/shard_map/ppermute | solution.py:637
  62.9 1.8 %shard_map.115 = bf16[16,128,128]{2,1,0:T(8,128)(2,1)} custom-call(s32[3]{0:T(128)S(1)} %pad_add_fusion.refs_0_, bf16[128,512]{1,0:T(8,128)(2,1)S(1)} %get-tuple-element.60.refs_1_, bf16[128,512]{1,0:T(8,128)(2,1)S(1)} %collective-permute-done.4.refs_2_, bf16[128,512]{1,0:T(8,128)(2,1)S(1)} %collective-permute-done.5.refs_3_, ...), custom_call_target="tpu_custom_call" | custom-call | flops 268435456 | bytes 1835008 | tf_op jit(solution)/shard_map/pallas_call | solution.py:620
  64.7 4.2 %all-to-all-start.2 = ((bf16[16,128,128]{2,1,0:T(8,128)(2,1)}), bf16[16,128,128]{2,1,0:T(8,128)(2,1)}, u32[]{:S(2)}, u32[]{:S(2)}) async-start(bf16[16,128,128]{2,1,0:T(8,128)(2,1)} %shard_map.115), calls=%async_computation.2 | async-start | bytes 1048576 | tf_op jit(solution)/shard_map/all_to_all | solution.py:669
  69.2 14.8 %collective-permute-done.7.refs_4_ = bf16[256,512]{1,0:T(8,128)(2,1)S(1)} collective-permute-done((bf16[256,512]{1,0:T(8,128)(2,1)S(1)}, bf16[256,512]{1,0:T(8,128)(2,1)S(1)}, u32[]{:S(2)}, u32[]{:S(2)}) %collective-permute-start.7) | collective-permute-done | bytes 262176 | tf_op jit(solution)/shard_map/ppermute | solution.py:637
  86.3 1.9 %shard_map.117 = bf16[16,160,128]{2,1,0:T(8,128)(2,1)} custom-call(s32[3]{0:T(128)S(1)} %pad_add_fusion.refs_0_, bf16[128,512]{1,0:T(8,128)(2,1)S(1)} %get-tuple-element.65.refs_1_, bf16[128,512]{1,0:T(8,128)(2,1)S(1)} %get-tuple-element.66.refs_2_, bf16[128,512]{1,0:T(8,128)(2,1)S(1)} %collective-permute-done.8.refs_3_, ...), custom_call_target="tpu_custom_call" | custom-call | flops 268435456 | bytes 1703936 | tf_op jit(solution)/shard_map/pallas_call | solution.py:620
  88.2 4.0 %all-to-all-start.3 = ((bf16[16,160,128]{2,1,0:T(8,128)(2,1)}), bf16[16,160,128]{2,1,0:T(8,128)(2,1)S(1)}, u32[]{:S(2)}, u32[]{:S(2)}) async-start(bf16[16,160,128]{2,1,0:T(8,128)(2,1)} %shard_map.117), calls=%async_computation.3 | async-start | bytes 1310720 | tf_op jit(solution)/shard_map/all_to_all | solution.py:669
  92.2 4.1 %shard_map.118 = (bf16[8,64,256]{2,1,0:T(8,128)(2,1)}, bf16[512,512]{1,0:T(8,128)(2,1)}, bf16[512,256]{1,0:T(8,128)(2,1)}, bf16[256,768]{1,0:T(8,128)(2,1)}) custom-call(bf16[8,64,256]{2,1,0:T(8,128)(2,1)} %refs_0_.7, bf16[8,64,256]{2,1,0:T(8,128)(2,1)} %refs_1_.8, bf16[256,1024]{1,0:T(8,128)(2,1)} %refs_1_.10, bf16[256,256]{1,0:T(8,128)(2,1)} %refs_3_.3, ...), custom_call_target="tpu_custom_call" | custom-call | flops 469762048 | bytes 3145728 | tf_op jit(solution)/shard_map/pallas_call | solution.py:620
  96.3 7.8 %all-to-all-done.3.refs_0_.refs_3_ = bf16[16,160,128]{2,1,0:T(8,128)(2,1)S(1)} async-done(((bf16[16,160,128]{2,1,0:T(8,128)(2,1)}), bf16[16,160,128]{2,1,0:T(8,128)(2,1)S(1)}, u32[]{:S(2)}, u32[]{:S(2)}) %all-to-all-start.3) | async-done | bytes 655392 | tf_op jit(solution)/shard_map/all_to_all | solution.py:669
  106.9 1.6 %collective-permute-done.10.refs_2_ = bf16[4,32,1280]{2,1,0:T(8,128)(2,1)S(1)} collective-permute-done((bf16[4,32,1280]{2,1,0:T(8,128)(2,1)S(1)}, bf16[4,32,1280]{2,1,0:T(8,128)(2,1)S(1)}, u32[]{:S(2)}, u32[]{:S(2)}) %collective-permute-start.10) | collective-permute-done | bytes 327712 | tf_op jit(solution)/shard_map/ppermute | solution.py:637
  110.2 2.5 %collective-permute-start.13 = (bf16[32,1280]{1,0:T(8,128)(2,1)S(1)}, bf16[32,1280]{1,0:T(8,128)(2,1)S(1)}, u32[]{:S(2)}, u32[]{:S(2)}) collective-permute-start(bf16[32,1280]{1,0:T(8,128)(2,1)S(1)} %get-tuple-element.78), channel_id=1, source_target_pairs={{0,6},{1,7},{2,4},{3,5},{4,2},{5,3},{6,0},{7,1},{8,14},{9,15},{10,... | collective-permute-start | bytes 245768 | tf_op jit(solution)/shard_map/ppermute | solution.py:637
  116.6 3.6 %collective-permute-done.14 = bf16[32,1408]{1,0:T(8,128)(2,1)S(1)} collective-permute-done((bf16[32,1408]{1,0:T(8,128)(2,1)S(1)}, bf16[32,1408]{1,0:T(8,128)(2,1)S(1)}, u32[]{:S(2)}, u32[]{:S(2)}) %collective-permute-start.14) | collective-permute-done | bytes 90144 | tf_op jit(solution)/shard_map/ppermute | solution.py:637
  120.7 4.3 %shard_map.124 = bf16[64,128,128]{2,1,0:T(8,128)(2,1)} custom-call(bf16[16,160,128]{2,1,0:T(8,128)(2,1)S(1)} %all-to-all-done.3.refs_0_.refs_3_, bf16[64,128,128]{2,1,0:T(8,128)(2,1)S(1)} %copy-done, f32[8,128]{1,0:T(8,128)S(1)} %bitcast.8, f32[8,64,128]{2,1,0:T(8,128)S(1)} %copy-done.5, f32[64,128]{1,0:T(8,128)S(1)} %copy-done.7, f32[64,128]{1,0:T(8,128)S(1)} %copy-done.8), custom_call_target="tpu_custom_call" | custom-call | flops 268435456 | bytes 5181440 | tf_op jit(solution)/shard_map/pallas_call | solution.py:620
  125.1 1.6 %collective-permute-done.15 = bf16[32,1408]{1,0:T(8,128)(2,1)S(1)} collective-permute-done((bf16[32,1408]{1,0:T(8,128)(2,1)S(1)}, bf16[32,1408]{1,0:T(8,128)(2,1)S(1)}, u32[]{:S(2)}, u32[]{:S(2)}) %collective-permute-start.15) | collective-permute-done | bytes 90144 | tf_op jit(solution)/shard_map/ppermute | solution.py:637
  126.7 10.1 %all-gather = bf16[256,1408]{1,0:T(8,128)(2,1)S(1)} all-gather(bf16[32,1408]{1,0:T(8,128)(2,1)S(1)} %add_convert_fusion), channel_id=2, replica_groups=mesh['seq'=4,'res'=8] {'res'}, dimensions={0}, use_global_device_ids=true | all-gather | bytes 811008 | tf_op jit(solution)/shard_map/all_gather | solution.py:804
  (57 shorter events, 19.2 us)
Async XLA Ops:
  3.3 16.9 %all-to-all-start = ((bf16[16,128,128]{2,1,0:T(8,128)(2,1)}), bf16[16,128,128]{2,1,0:T(8,128)(2,1)S(1)}, u32[]{:S(2)}, u32[]{:S(2)}) async-start(bf16[16,128,128]{2,1,0:T(8,128)(2,1)} %shard_map.109), calls=%async_computation | async-start | bytes 1048576 | tf_op jit(solution)/shard_map/all_to_all | solution.py:669
  20.1 22.6 %all-to-all-start.1 = ((bf16[16,192,128]{2,1,0:T(8,128)(2,1)}), bf16[16,192,128]{2,1,0:T(8,128)(2,1)S(1)}, u32[]{:S(2)}, u32[]{:S(2)}) async-start(bf16[16,192,128]{2,1,0:T(8,128)(2,1)} %get-tuple-element.52), calls=%async_computation.1 | async-start | bytes 1572864 | tf_op jit(solution)/shard_map/all_to_all | solution.py:669
  23.7 2.0 %collective-permute-start = (bf16[16,128,128]{2,1,0:T(8,128)(2,1)S(1)}, bf16[16,128,128]{2,1,0:T(8,128)(2,1)S(1)}, u32[]{:S(2)}, u32[]{:S(2)}) collective-permute-start(bf16[16,128,128]{2,1,0:T(8,128)(2,1)S(1)} %all-to-all-done.refs_1_.refs_5_), channel_id=1, source_target_pairs={{0,1},{1,0},{2,3},{3,2},{4,5},{5,4},{6,7},{7,6},{8,9},{9,8},{10,11... | collective-permute-start | bytes 1572872 | tf_op jit(solution)/shard_map/ppermute | solution.py:637
  26.7 12.0 %collective-permute-start.1 = (f32[128,512]{1,0:T(8,128)S(1)}, f32[128,512]{1,0:T(8,128)S(1)}, u32[]{:S(2)}, u32[]{:S(2)}) collective-permute-start(f32[128,512]{1,0:T(8,128)S(1)} %get-tuple-element.53), channel_id=1, source_target_pairs={{0,16},{8,24},{16,0},{24,8},{1,17},{9,25},{17,1},{25,9},{2,18},{10... | collective-permute-start | bytes 786440 | tf_op jit(solution)/shard_map/ppermute | solution.py:637
  42.7 2.3 %collective-permute-start.3 = (bf16[16,192,128]{2,1,0:T(8,128)(2,1)S(1)}, bf16[16,192,128]{2,1,0:T(8,128)(2,1)S(1)}, u32[]{:S(2)}, u32[]{:S(2)}) collective-permute-start(bf16[16,192,128]{2,1,0:T(8,128)(2,1)S(1)} %all-to-all-done.1.refs_1_.refs_5_), channel_id=1, source_target_pairs={{0,1},{1,0},{2,3},{3,2},{4,5},{5,4},{6,7},{7,6},{8,9},{9,8},{10,11... | collective-permute-start | bytes 2359304 | tf_op jit(solution)/shard_map/ppermute | solution.py:637
  43.3 9.7 %collective-permute-start.2 = (bf16[8,64,128]{2,1,0:T(8,128)(2,1)S(1)}, bf16[8,64,128]{2,1,0:T(8,128)(2,1)S(1)}, u32[]{:S(2)}, u32[]{:S(2)}) collective-permute-start(bf16[8,64,128]{2,1,0:T(8,128)(2,1)S(1)} %get-tuple-element.57), channel_id=1, source_target_pairs={{0,16},{8,24},{16,0},{24,8},{1,17},{9,25},{17,1},{25,9},{2,18},{10... | collective-permute-start | bytes 393224 | tf_op jit(solution)/shard_map/ppermute | solution.py:637
  53.8 7.8 %collective-permute-start.4 = (bf16[128,512]{1,0:T(8,128)(2,1)S(1)}, bf16[128,512]{1,0:T(8,128)(2,1)S(1)}, u32[]{:S(2)}, u32[]{:S(2)}) collective-permute-start(bf16[128,512]{1,0:T(8,128)(2,1)S(1)} %get-tuple-element.60.refs_1_), channel_id=1, source_target_pairs={{0,16},{8,24},{16,0},{24,8},{1,17},{9,25},{17,1},{25,9},{2,18},{10... | collective-permute-start | bytes 393224 | tf_op jit(solution)/shard_map/ppermute | solution.py:637
  53.8 7.7 %collective-permute-start.5 = (bf16[128,512]{1,0:T(8,128)(2,1)S(1)}, bf16[128,512]{1,0:T(8,128)(2,1)S(1)}, u32[]{:S(2)}, u32[]{:S(2)}) collective-permute-start(bf16[128,512]{1,0:T(8,128)(2,1)S(1)} %get-tuple-element.60.refs_1_), channel_id=1, source_target_pairs={{0,1},{1,0},{2,3},{3,2},{4,5},{5,4},{6,7},{7,6},{8,9},{9,8},{10,11... | collective-permute-start | bytes 393224 | tf_op jit(solution)/shard_map/ppermute | solution.py:637
  61.6 1.3 collective-permute-start.6
  64.7 23.5 %all-to-all-start.2 = ((bf16[16,128,128]{2,1,0:T(8,128)(2,1)}), bf16[16,128,128]{2,1,0:T(8,128)(2,1)}, u32[]{:S(2)}, u32[]{:S(2)}) async-start(bf16[16,128,128]{2,1,0:T(8,128)(2,1)} %shard_map.115), calls=%async_computation.2 | async-start | bytes 1048576 | tf_op jit(solution)/shard_map/all_to_all | solution.py:669
  69.0 15.0 %collective-permute-start.7 = (bf16[256,512]{1,0:T(8,128)(2,1)S(1)}, bf16[256,512]{1,0:T(8,128)(2,1)S(1)}, u32[]{:S(2)}, u32[]{:S(2)}) collective-permute-start(bf16[256,512]{1,0:T(8,128)(2,1)S(1)} %get-tuple-element.64), channel_id=1, source_target_pairs={{0,16},{8,24},{16,0},{24,8},{1,17},{9,25},{17,1},{25,9},{2,18},{10... | collective-permute-start | bytes 786440 | tf_op jit(solution)/shard_map/ppermute | solution.py:637
  84.7 1.4 %collective-permute-start.8 = (bf16[128,512]{1,0:T(8,128)(2,1)S(1)}, bf16[128,512]{1,0:T(8,128)(2,1)S(1)}, u32[]{:S(2)}, u32[]{:S(2)}) collective-permute-start(bf16[128,512]{1,0:T(8,128)(2,1)S(1)} %get-tuple-element.65.refs_1_), channel_id=1, source_target_pairs={{0,1},{1,0},{2,3},{3,2},{4,5},{5,4},{6,7},{7,6},{8,9},{9,8},{10,11... | collective-permute-start | bytes 393224 | tf_op jit(solution)/shard_map/ppermute | solution.py:637
  84.8 19.3 %copy-start = (bf16[64,128,128]{2,1,0:T(8,128)(2,1)S(1)}, bf16[64,128,128]{2,1,0:T(8,128)(2,1)}, u32[]{:S(2)}) copy-start(bf16[64,128,128]{2,1,0:T(8,128)(2,1)} %refs_1_.11) | copy-start | bytes 6291460
  84.8 19.3 %copy-start.7 = (f32[64,128]{1,0:T(8,128)S(1)}, f32[64,128]{1,0:T(8,128)}, u32[]{:S(2)}) copy-start(f32[64,128]{1,0:T(8,128)} %get-tuple-element.72.refs_2_.refs_4_) | copy-start | bytes 98308
  84.8 19.3 %copy-start.8 = (f32[64,128]{1,0:T(8,128)S(1)}, f32[64,128]{1,0:T(8,128)}, u32[]{:S(2)}) copy-start(f32[64,128]{1,0:T(8,128)} %get-tuple-element.73.refs_3_.refs_5_) | copy-start | bytes 98308
  84.8 1.5 %collective-permute-start.9 = (bf16[128,512]{1,0:T(8,128)(2,1)S(1)}, bf16[128,512]{1,0:T(8,128)(2,1)S(1)}, u32[]{:S(2)}, u32[]{:S(2)}) collective-permute-start(bf16[128,512]{1,0:T(8,128)(2,1)S(1)} %get-tuple-element.66.refs_2_), channel_id=1, source_target_pairs={{0,1},{1,0},{2,3},{3,2},{4,5},{5,4},{6,7},{7,6},{8,9},{9,8},{10,11... | collective-permute-start | bytes 393224 | tf_op jit(solution)/shard_map/ppermute | solution.py:637
  88.2 15.9 %all-to-all-start.3 = ((bf16[16,160,128]{2,1,0:T(8,128)(2,1)}), bf16[16,160,128]{2,1,0:T(8,128)(2,1)S(1)}, u32[]{:S(2)}, u32[]{:S(2)}) async-start(bf16[16,160,128]{2,1,0:T(8,128)(2,1)} %shard_map.117), calls=%async_computation.3 | async-start | bytes 1310720 | tf_op jit(solution)/shard_map/all_to_all | solution.py:669
  106.8 14.0 %copy-start.5 = (f32[8,64,128]{2,1,0:T(8,128)S(1)}, f32[8,64,128]{2,1,0:T(8,128)}, u32[]{:S(2)}) copy-start(f32[8,64,128]{2,1,0:T(8,128)} %get-tuple-element.86.refs_3_) | copy-start | bytes 786436
  106.8 1.7 %collective-permute-start.10 = (bf16[4,32,1280]{2,1,0:T(8,128)(2,1)S(1)}, bf16[4,32,1280]{2,1,0:T(8,128)(2,1)S(1)}, u32[]{:S(2)}, u32[]{:S(2)}) collective-permute-start(bf16[4,32,1280]{2,1,0:T(8,128)(2,1)S(1)} %get-tuple-element.75), channel_id=1, source_target_pairs={{0,1},{1,0},{2,3},{3,2},{4,5},{5,4},{6,7},{7,6},{8,9},{9,8},{10,11... | collective-permute-start | bytes 983048 | tf_op jit(solution)/shard_map/ppermute | solution.py:637
  109.1 5.1 %collective-permute-start.11 = (bf16[32,1280]{1,0:T(8,128)(2,1)S(1)}, bf16[32,1280]{1,0:T(8,128)(2,1)S(1)}, u32[]{:S(2)}, u32[]{:S(2)}) collective-permute-start(bf16[32,1280]{1,0:T(8,128)(2,1)S(1)} %get-tuple-element.76), channel_id=1, source_target_pairs={{0,2},{1,3},{2,0},{3,1},{4,6},{5,7},{6,4},{7,5},{8,10},{9,11},{10,... | collective-permute-start | bytes 245768 | tf_op jit(solution)/shard_map/ppermute | solution.py:637
  109.2 5.4 %collective-permute-start.12 = (bf16[32,1280]{1,0:T(8,128)(2,1)S(1)}, bf16[32,1280]{1,0:T(8,128)(2,1)S(1)}, u32[]{:S(2)}, u32[]{:S(2)}) collective-permute-start(bf16[32,1280]{1,0:T(8,128)(2,1)S(1)} %get-tuple-element.77), channel_id=1, source_target_pairs={{0,4},{1,5},{2,6},{3,7},{4,0},{5,1},{6,2},{7,3},{8,12},{9,13},{10,... | collective-permute-start | bytes 245768 | tf_op jit(solution)/shard_map/ppermute | solution.py:637
  110.2 5.3 %collective-permute-start.13 = (bf16[32,1280]{1,0:T(8,128)(2,1)S(1)}, bf16[32,1280]{1,0:T(8,128)(2,1)S(1)}, u32[]{:S(2)}, u32[]{:S(2)}) collective-permute-start(bf16[32,1280]{1,0:T(8,128)(2,1)S(1)} %get-tuple-element.78), channel_id=1, source_target_pairs={{0,6},{1,7},{2,4},{3,5},{4,2},{5,3},{6,0},{7,1},{8,14},{9,15},{10,... | collective-permute-start | bytes 245768 | tf_op jit(solution)/shard_map/ppermute | solution.py:637
  115.6 4.6 %collective-permute-start.14 = (bf16[32,1408]{1,0:T(8,128)(2,1)S(1)}, bf16[32,1408]{1,0:T(8,128)(2,1)S(1)}, u32[]{:S(2)}, u32[]{:S(2)}) collective-permute-start(bf16[32,1408]{1,0:T(8,128)(2,1)S(1)} %shard_map.123), channel_id=1, source_target_pairs={{0,8},{8,0},{16,24},{24,16},{1,9},{9,1},{17,25},{25,17},{2,10},{10... | collective-permute-start | bytes 270344 | tf_op jit(solution)/shard_map/ppermute | solution.py:637
  120.2 6.5 %collective-permute-start.15 = (bf16[32,1408]{1,0:T(8,128)(2,1)S(1)}, bf16[32,1408]{1,0:T(8,128)(2,1)S(1)}, u32[]{:S(2)}, u32[]{:S(2)}) collective-permute-start(bf16[32,1408]{1,0:T(8,128)(2,1)S(1)} %add_convert_fusion.1), channel_id=1, source_target_pairs={{0,16},{8,24},{16,0},{24,8},{1,17},{9,25},{17,1},{25,9},{2,18},{10... | collective-permute-start | bytes 270344 | tf_op jit(solution)/shard_map/ppermute | solution.py:637
  (6 other events, 58.4 us)

commit v20 on v18

--- a/solution.py
+++ b/solution.py
@@ -559,16 +559,23 @@
     lax.fori_loop(0, pair_ref.shape[0] // 8, rows, 0)
 
 
-def output_kernel(parts_ref, combined_ref, out_weight_ref, pair_weight_ref):
+def output_kernel(place_ref, *refs):
+    *parts, combined_ref, out_weight_ref, pair_weight_ref, shares_ref = refs
+    core, chip = place_ref[0], place_ref[2]
     width = combined_ref.shape[0]
-    rows = parts_ref.shape[1]
-    for h in range(parts_ref.shape[0]):
-        block = slice(h * rows, (h + 1) * rows)
-        part = parts_ref[h].astype(jnp.float32)
+    rows = parts[0].shape[0]
+    heads = pair_weight_ref.shape[0]
+    for k, ref in enumerate(parts):
+        owner = jnp.bitwise_xor(chip, k // 2) * 2 + jnp.bitwise_xor(core, k % 2)
+        block = pl.ds(pl.multiple_of(owner * rows, rows), rows)
+        part = ref[...].astype(jnp.float32)
         combined_ref[block, :] = part[:, : 4 * width]
         out_weight_ref[block, :] = part[:, 4 * width : 5 * width]
-        share = part[: pair_weight_ref.shape[0], 5 * width :]
-        pair_weight_ref[...] = share if h == 0 else pair_weight_ref[...] + share
+        shares_ref[owner] = part[:heads, 5 * width :]
+    total = shares_ref[0]
+    for k in range(1, len(parts)):
+        total += shares_ref[k]
+    pair_weight_ref[...] = total
 
 
 def call(kernel, outs, *args, scratch=(), place=None, flops=0, after=(), outside=0, late=0):
@@ -776,10 +783,14 @@
     other_half = swapped(part, "seq", seq_half)
     other_half, pair_gradient = lax.optimization_barrier((other_half, pair_gradient))
     part = added(part, other_half)
+    chips = [part] + [swapped(part, "res", 2 * flip) for flip in range(1, res_size // 2)]
+    parts = [t for chip in chips for t in (chip, swapped(chip, "res", 1))]
     combined_gradient, output_gradient, pair_weight_gradient = call(
         output_kernel,
         [(wc.shape, f32), (wo.shape, f32), ((heads, channels), f32)],
-        lax.all_gather(part, "res", axis=0),
+        *parts,
+        scratch=[pltpu.VMEM((len(parts), heads, channels), f32)],
+        place=place,
     )
     return (
         updated,

time: 137 us -> 136 us (level)
  blocking collectives: 10.1 us -> 0 us
  starting transfers between devices: 26.5 us -> 31.1 us
  waiting for transfers between devices: 69.2 us -> 73.1 us
    all_gather x1 -> x0, blocking collectives: 10.1 us -> none  [head_body(): lax.all_gather(part, 'res', axis=0)]
    ppermute x15 -> x22, starting transfers between devices: 8.7 us -> 13.4 us  [swapped(): lax.ppermute(mine, axis_name, [(a, a ^ distance) for a in range(size)])]
    ppermute x15 -> x22, waiting for transfers between devices: 46.8 us -> 50.6 us  [swapped(): lax.ppermute(mine, axis_name, [(a, a ^ distance) for a in range(size)])]
  transfers between devices with their start and end apart: 19 -> 26, of which waited for: 18 -> 22; matrix products, arithmetic and copies ran while one was open for 0% -> 0% of each run, Pallas kernels for 14% -> 14%
where the time goes in v20:
time: 136 us; the launch traced here: 135 us
  waiting for transfers between devices  73.1 us (54%)
  starting transfers between devices  31.1 us (23%)
  Pallas kernels  29.9 us (22%)
    ppermute x22, waiting for transfers between devices, swapped(): lax.ppermute(mine, axis_name, [(a, a ^ distance) for a in range(size)])  50.6 us
    pallas_call x16, Pallas kernels, call(): pl.pallas_call(wrapped, out_shape=shapes, in_specs=[pl.BlockSpec(memory_s...  29.9 us
    all_to_all x4, waiting for transfers between devices, across(): lax.all_to_all(blocks, ('seq', 'res'), 0, 0, axis_index_groups=groups, ti...  22.5 us
    all_to_all x4, starting transfers between devices, across(): lax.all_to_all(blocks, ('seq', 'res'), 0, 0, axis_index_groups=groups, ti...  17.8 us
    ppermute x22, starting transfers between devices, swapped(): lax.ppermute(mine, axis_name, [(a, a ^ distance) for a in range(size)])  13.4 us
  transfers between devices with their start and end apart: 26, of which 22 were waited for; matrix products, arithmetic and copies ran while one was open for 0% of the time, Pallas kernels for 14%

profile of v20, /device:TPU:0, one launch (start us, length us, event | category | flops | bytes accessed | tf_op | source)
XLA Modules:
  0.0 135.2 jit_solution(11816168679725545208)
XLA Ops:
  0.6 2.7 %shard_map.109 = bf16[16,128,128]{2,1,0:T(8,128)(2,1)} custom-call(bf16[8,64,256]{2,1,0:T(8,128)(2,1)} %refs_0_.7, bf16[8,64,256]{2,1,0:T(8,128)(2,1)} %refs_1_.8, bf16[256,1024]{1,0:T(8,128)(2,1)} %refs_1_.10, bf16[256,256]{1,0:T(8,128)(2,1)} %refs_3_.3), custom_call_target="tpu_custom_call" | custom-call | flops 268435456 | bytes 1703936 | tf_op jit(solution)/shard_map/pallas_call | solution.py:613
  3.4 6.3 %all-to-all-start = ((bf16[16,128,128]{2,1,0:T(8,128)(2,1)}), bf16[16,128,128]{2,1,0:T(8,128)(2,1)S(1)}, u32[]{:S(2)}, u32[]{:S(2)}) async-start(bf16[16,128,128]{2,1,0:T(8,128)(2,1)} %shard_map.109), calls=%async_computation | async-start | bytes 1048576 | tf_op jit(solution)/shard_map/all_to_all | solution.py:662
  9.7 6.1 %shard_map.110 = (bf16[16,192,128]{2,1,0:T(8,128)(2,1)}, f32[8,64,128]{2,1,0:T(8,128)}, f32[64,128]{1,0:T(8,128)}, f32[64,128]{1,0:T(8,128)}) custom-call(bf16[8,64,256]{2,1,0:T(8,128)(2,1)} %refs_0_.7, bf16[256,1024]{1,0:T(8,128)(2,1)} %refs_1_.10, bf16[64,128,128]{2,1,0:T(8,128)(2,1)} %refs_1_.11, f32[8,128]{1,0:T(8,128)} %bitcast.5), custom_call_target="tpu_custom_call" | custom-call | flops 268435456 | bytes 4001792 | tf_op jit(solution)/shard_map/pallas_call | solution.py:613
  15.8 4.4 %all-to-all-done.refs_1_.refs_5_ = bf16[16,128,128]{2,1,0:T(8,128)(2,1)S(1)} async-done(((bf16[16,128,128]{2,1,0:T(8,128)(2,1)}), bf16[16,128,128]{2,1,0:T(8,128)(2,1)S(1)}, u32[]{:S(2)}, u32[]{:S(2)}) %all-to-all-start) | async-done | bytes 524320 | tf_op jit(solution)/shard_map/all_to_all | solution.py:662
  20.2 3.6 %all-to-all-start.1 = ((bf16[16,192,128]{2,1,0:T(8,128)(2,1)}), bf16[16,192,128]{2,1,0:T(8,128)(2,1)S(1)}, u32[]{:S(2)}, u32[]{:S(2)}) async-start(bf16[16,192,128]{2,1,0:T(8,128)(2,1)} %get-tuple-element.46), calls=%async_computation.1 | async-start | bytes 1572864 | tf_op jit(solution)/shard_map/all_to_all | solution.py:662
  26.7 2.7 %collective-permute-start.1 = (bf16[256,512]{1,0:T(8,128)(2,1)S(1)}, bf16[256,512]{1,0:T(8,128)(2,1)S(1)}, u32[]{:S(2)}, u32[]{:S(2)}) collective-permute-start(bf16[256,512]{1,0:T(8,128)(2,1)S(1)} %get-tuple-element.48), channel_id=1, source_target_pairs={{0,16},{8,24},{16,0},{24,8},{1,17},{9,25},{17,1},{25,9},{2,18},{10... | collective-permute-start | bytes 786440 | tf_op jit(solution)/shard_map/ppermute | solution.py:630
  29.4 9.5 %collective-permute-done.1.refs_4_ = bf16[256,512]{1,0:T(8,128)(2,1)S(1)} collective-permute-done((bf16[256,512]{1,0:T(8,128)(2,1)S(1)}, bf16[256,512]{1,0:T(8,128)(2,1)S(1)}, u32[]{:S(2)}, u32[]{:S(2)}) %collective-permute-start.1) | collective-permute-done | bytes 262176 | tf_op jit(solution)/shard_map/ppermute | solution.py:630
  38.8 4.0 %all-to-all-done.1.refs_1_.refs_5_ = bf16[16,192,128]{2,1,0:T(8,128)(2,1)S(1)} async-done(((bf16[16,192,128]{2,1,0:T(8,128)(2,1)}), bf16[16,192,128]{2,1,0:T(8,128)(2,1)S(1)}, u32[]{:S(2)}, u32[]{:S(2)}) %all-to-all-start.1) | async-done | bytes 786464 | tf_op jit(solution)/shard_map/all_to_all | solution.py:662
  42.8 2.3 %collective-permute-done.2.refs_2_ = bf16[16,192,128]{2,1,0:T(8,128)(2,1)S(1)} collective-permute-done((bf16[16,192,128]{2,1,0:T(8,128)(2,1)S(1)}, bf16[16,192,128]{2,1,0:T(8,128)(2,1)S(1)}, u32[]{:S(2)}, u32[]{:S(2)}) %collective-permute-start.2) | collective-permute-done | bytes 786464 | tf_op jit(solution)/shard_map/ppermute | solution.py:630
  46.2 14.9 %collective-permute-done.3.refs_1_ = f32[128,512]{1,0:T(8,128)S(1)} collective-permute-done((f32[128,512]{1,0:T(8,128)S(1)}, f32[128,512]{1,0:T(8,128)S(1)}, u32[]{:S(2)}, u32[]{:S(2)}) %collective-permute-start.3) | collective-permute-done | bytes 262176 | tf_op jit(solution)/shard_map/ppermute | solution.py:630
  61.4 7.6 %collective-permute-done.4.refs_2_ = bf16[128,512]{1,0:T(8,128)(2,1)S(1)} collective-permute-done((bf16[128,512]{1,0:T(8,128)(2,1)S(1)}, bf16[128,512]{1,0:T(8,128)(2,1)S(1)}, u32[]{:S(2)}, u32[]{:S(2)}) %collective-permute-start.4) | collective-permute-done | bytes 131104 | tf_op jit(solution)/shard_map/ppermute | solution.py:630
  70.4 1.8 %shard_map.114 = bf16[16,128,128]{2,1,0:T(8,128)(2,1)} custom-call(s32[3]{0:T(128)S(1)} %pad_add_fusion.refs_0_, bf16[128,512]{1,0:T(8,128)(2,1)S(1)} %get-tuple-element.52.refs_1_, bf16[128,512]{1,0:T(8,128)(2,1)S(1)} %collective-permute-done.4.refs_2_, bf16[128,512]{1,0:T(8,128)(2,1)S(1)} %collective-permute-done.5.refs_3_, ...), custom_call_target="tpu_custom_call" | custom-call | flops 268435456 | bytes 1572864 | tf_op jit(solution)/shard_map/pallas_call | solution.py:613
  72.2 4.2 %all-to-all-start.2 = ((bf16[16,128,128]{2,1,0:T(8,128)(2,1)}), bf16[16,128,128]{2,1,0:T(8,128)(2,1)}, u32[]{:S(2)}, u32[]{:S(2)}) async-start(bf16[16,128,128]{2,1,0:T(8,128)(2,1)} %shard_map.114), calls=%async_computation.2 | async-start | bytes 1048576 | tf_op jit(solution)/shard_map/all_to_all | solution.py:662
  78.8 1.9 %shard_map.116 = bf16[16,160,128]{2,1,0:T(8,128)(2,1)} custom-call(s32[3]{0:T(128)S(1)} %pad_add_fusion.refs_0_, bf16[128,512]{1,0:T(8,128)(2,1)S(1)} %get-tuple-element.57.refs_1_, bf16[128,512]{1,0:T(8,128)(2,1)S(1)} %get-tuple-element.58.refs_2_, bf16[128,512]{1,0:T(8,128)(2,1)S(1)} %collective-permute-done.7.refs_3_, ...), custom_call_target="tpu_custom_call" | custom-call | flops 268435456 | bytes 1966080 | tf_op jit(solution)/shard_map/pallas_call | solution.py:613
  80.7 6.3 %all-to-all-done.2.refs_4_ = bf16[16,128,128]{2,1,0:T(8,128)(2,1)} async-done(((bf16[16,128,128]{2,1,0:T(8,128)(2,1)}), bf16[16,128,128]{2,1,0:T(8,128)(2,1)}, u32[]{:S(2)}, u32[]{:S(2)}) %all-to-all-start.2) | async-done | bytes 524320 | tf_op jit(solution)/shard_map/all_to_all | solution.py:662
  87.0 3.6 %all-to-all-start.3 = ((bf16[16,160,128]{2,1,0:T(8,128)(2,1)}), bf16[16,160,128]{2,1,0:T(8,128)(2,1)S(1)}, u32[]{:S(2)}, u32[]{:S(2)}) async-start(bf16[16,160,128]{2,1,0:T(8,128)(2,1)} %shard_map.116), calls=%async_computation.3 | async-start | bytes 1310720 | tf_op jit(solution)/shard_map/all_to_all | solution.py:662
  90.6 4.1 %shard_map.117 = (bf16[8,64,256]{2,1,0:T(8,128)(2,1)}, bf16[512,512]{1,0:T(8,128)(2,1)}, bf16[512,256]{1,0:T(8,128)(2,1)}, bf16[256,768]{1,0:T(8,128)(2,1)}) custom-call(bf16[8,64,256]{2,1,0:T(8,128)(2,1)} %refs_0_.7, bf16[8,64,256]{2,1,0:T(8,128)(2,1)} %refs_1_.8, bf16[256,1024]{1,0:T(8,128)(2,1)} %refs_1_.10, bf16[256,256]{1,0:T(8,128)(2,1)} %refs_3_.3, ...), custom_call_target="tpu_custom_call" | custom-call | flops 469762048 | bytes 3145728 | tf_op jit(solution)/shard_map/pallas_call | solution.py:613
  94.7 7.8 %all-to-all-done.3.refs_0_.refs_3_ = bf16[16,160,128]{2,1,0:T(8,128)(2,1)S(1)} async-done(((bf16[16,160,128]{2,1,0:T(8,128)(2,1)}), bf16[16,160,128]{2,1,0:T(8,128)(2,1)S(1)}, u32[]{:S(2)}, u32[]{:S(2)}) %all-to-all-start.3) | async-done | bytes 655392 | tf_op jit(solution)/shard_map/all_to_all | solution.py:662
  108.6 2.5 %collective-permute-start.12 = (bf16[32,1280]{1,0:T(8,128)(2,1)S(1)}, bf16[32,1280]{1,0:T(8,128)(2,1)S(1)}, u32[]{:S(2)}, u32[]{:S(2)}) collective-permute-start(bf16[32,1280]{1,0:T(8,128)(2,1)S(1)} %get-tuple-element.70), channel_id=1, source_target_pairs={{0,6},{1,7},{2,4},{3,5},{4,2},{5,3},{6,0},{7,1},{8,14},{9,15},{10,... | collective-permute-start | bytes 245768 | tf_op jit(solution)/shard_map/ppermute | solution.py:630
  115.0 3.6 %collective-permute-done.13 = bf16[32,1408]{1,0:T(8,128)(2,1)S(1)} collective-permute-done((bf16[32,1408]{1,0:T(8,128)(2,1)S(1)}, bf16[32,1408]{1,0:T(8,128)(2,1)S(1)}, u32[]{:S(2)}, u32[]{:S(2)}) %collective-permute-start.13) | collective-permute-done | bytes 90144 | tf_op jit(solution)/shard_map/ppermute | solution.py:630
  118.9 4.3 %shard_map.123 = bf16[64,128,128]{2,1,0:T(8,128)(2,1)} custom-call(bf16[16,160,128]{2,1,0:T(8,128)(2,1)S(1)} %all-to-all-done.3.refs_0_.refs_3_, bf16[64,128,128]{2,1,0:T(8,128)(2,1)S(1)} %copy-done, f32[8,128]{1,0:T(8,128)S(1)} %bitcast.6, f32[8,64,128]{2,1,0:T(8,128)S(1)} %copy-done.5, f32[64,128]{1,0:T(8,128)S(1)} %copy-done.7, f32[64,128]{1,0:T(8,128)S(1)} %copy-done.8), custom_call_target="tpu_custom_call" | custom-call | flops 268435456 | bytes 5181440 | tf_op jit(solution)/shard_map/pallas_call | solution.py:613
  124.1 3.5 %collective-permute-start.20 = (bf16[32,1408]{1,0:T(8,128)(2,1)S(1)}, bf16[32,1408]{1,0:T(8,128)(2,1)S(1)}, u32[]{:S(2)}, u32[]{:S(2)}) collective-permute-start(bf16[32,1408]{1,0:T(8,128)(2,1)S(1)} %add_convert_fusion.refs_1_), channel_id=1, source_target_pairs={{0,6},{1,7},{2,4},{3,5},{4,2},{5,3},{6,0},{7,1},{8,14},{9,15},{10,... | collective-permute-start | bytes 270344 | tf_op jit(solution)/shard_map/ppermute | solution.py:630
  128.3 1.9 %collective-permute-done.20.refs_7_ = bf16[32,1408]{1,0:T(8,128)(2,1)S(1)} collective-permute-done((bf16[32,1408]{1,0:T(8,128)(2,1)S(1)}, bf16[32,1408]{1,0:T(8,128)(2,1)S(1)}, u32[]{:S(2)}, u32[]{:S(2)}) %collective-permute-start.20) | collective-permute-done | bytes 90144 | tf_op jit(solution)/shard_map/ppermute | solution.py:630
  130.1 2.0 %collective-permute-done.18.refs_5_ = bf16[32,1408]{1,0:T(8,128)(2,1)S(1)} collective-permute-done((bf16[32,1408]{1,0:T(8,128)(2,1)S(1)}, bf16[32,1408]{1,0:T(8,128)(2,1)S(1)}, u32[]{:S(2)}, u32[]{:S(2)}) %collective-permute-start.18) | collective-permute-done | bytes 90144 | tf_op jit(solution)/shard_map/ppermute | solution.py:630
  (67 shorter events, 22.8 us)
Async XLA Ops:
  3.4 16.9 %all-to-all-start = ((bf16[16,128,128]{2,1,0:T(8,128)(2,1)}), bf16[16,128,128]{2,1,0:T(8,128)(2,1)S(1)}, u32[]{:S(2)}, u32[]{:S(2)}) async-start(bf16[16,128,128]{2,1,0:T(8,128)(2,1)} %shard_map.109), calls=%async_computation | async-start | bytes 1048576 | tf_op jit(solution)/shard_map/all_to_all | solution.py:662
  20.2 22.6 %all-to-all-start.1 = ((bf16[16,192,128]{2,1,0:T(8,128)(2,1)}), bf16[16,192,128]{2,1,0:T(8,128)(2,1)S(1)}, u32[]{:S(2)}, u32[]{:S(2)}) async-start(bf16[16,192,128]{2,1,0:T(8,128)(2,1)} %get-tuple-element.46), calls=%async_computation.1 | async-start | bytes 1572864 | tf_op jit(solution)/shard_map/all_to_all | solution.py:662
  23.8 2.0 %collective-permute-start = (bf16[16,128,128]{2,1,0:T(8,128)(2,1)S(1)}, bf16[16,128,128]{2,1,0:T(8,128)(2,1)S(1)}, u32[]{:S(2)}, u32[]{:S(2)}) collective-permute-start(bf16[16,128,128]{2,1,0:T(8,128)(2,1)S(1)} %all-to-all-done.refs_1_.refs_5_), channel_id=1, source_target_pairs={{0,1},{1,0},{2,3},{3,2},{4,5},{5,4},{6,7},{7,6},{8,9},{9,8},{10,11... | collective-permute-start | bytes 1572872 | tf_op jit(solution)/shard_map/ppermute | solution.py:630
  26.7 12.1 %collective-permute-start.1 = (bf16[256,512]{1,0:T(8,128)(2,1)S(1)}, bf16[256,512]{1,0:T(8,128)(2,1)S(1)}, u32[]{:S(2)}, u32[]{:S(2)}) collective-permute-start(bf16[256,512]{1,0:T(8,128)(2,1)S(1)} %get-tuple-element.48), channel_id=1, source_target_pairs={{0,16},{8,24},{16,0},{24,8},{1,17},{9,25},{17,1},{25,9},{2,18},{10... | collective-permute-start | bytes 786440 | tf_op jit(solution)/shard_map/ppermute | solution.py:630
  42.8 2.3 %collective-permute-start.2 = (bf16[16,192,128]{2,1,0:T(8,128)(2,1)S(1)}, bf16[16,192,128]{2,1,0:T(8,128)(2,1)S(1)}, u32[]{:S(2)}, u32[]{:S(2)}) collective-permute-start(bf16[16,192,128]{2,1,0:T(8,128)(2,1)S(1)} %all-to-all-done.1.refs_1_.refs_5_), channel_id=1, source_target_pairs={{0,1},{1,0},{2,3},{3,2},{4,5},{5,4},{6,7},{7,6},{8,9},{9,8},{10,11... | collective-permute-start | bytes 2359304 | tf_op jit(solution)/shard_map/ppermute | solution.py:630
  46.1 14.9 %collective-permute-start.3 = (f32[128,512]{1,0:T(8,128)S(1)}, f32[128,512]{1,0:T(8,128)S(1)}, u32[]{:S(2)}, u32[]{:S(2)}) collective-permute-start(f32[128,512]{1,0:T(8,128)S(1)} %get-tuple-element.51), channel_id=1, source_target_pairs={{0,16},{8,24},{16,0},{24,8},{1,17},{9,25},{17,1},{25,9},{2,18},{10... | collective-permute-start | bytes 786440 | tf_op jit(solution)/shard_map/ppermute | solution.py:630
  61.2 7.8 %collective-permute-start.4 = (bf16[128,512]{1,0:T(8,128)(2,1)S(1)}, bf16[128,512]{1,0:T(8,128)(2,1)S(1)}, u32[]{:S(2)}, u32[]{:S(2)}) collective-permute-start(bf16[128,512]{1,0:T(8,128)(2,1)S(1)} %get-tuple-element.52.refs_1_), channel_id=1, source_target_pairs={{0,16},{8,24},{16,0},{24,8},{1,17},{9,25},{17,1},{25,9},{2,18},{10... | collective-permute-start | bytes 393224 | tf_op jit(solution)/shard_map/ppermute | solution.py:630
  61.3 7.7 %collective-permute-start.5 = (bf16[128,512]{1,0:T(8,128)(2,1)S(1)}, bf16[128,512]{1,0:T(8,128)(2,1)S(1)}, u32[]{:S(2)}, u32[]{:S(2)}) collective-permute-start(bf16[128,512]{1,0:T(8,128)(2,1)S(1)} %get-tuple-element.52.refs_1_), channel_id=1, source_target_pairs={{0,1},{1,0},{2,3},{3,2},{4,5},{5,4},{6,7},{7,6},{8,9},{9,8},{10,11... | collective-permute-start | bytes 393224 | tf_op jit(solution)/shard_map/ppermute | solution.py:630
  69.0 1.3 collective-permute-start.6
  72.2 14.8 %all-to-all-start.2 = ((bf16[16,128,128]{2,1,0:T(8,128)(2,1)}), bf16[16,128,128]{2,1,0:T(8,128)(2,1)}, u32[]{:S(2)}, u32[]{:S(2)}) async-start(bf16[16,128,128]{2,1,0:T(8,128)(2,1)} %shard_map.114), calls=%async_computation.2 | async-start | bytes 1048576 | tf_op jit(solution)/shard_map/all_to_all | solution.py:662
  77.1 1.4 %collective-permute-start.7 = (bf16[128,512]{1,0:T(8,128)(2,1)S(1)}, bf16[128,512]{1,0:T(8,128)(2,1)S(1)}, u32[]{:S(2)}, u32[]{:S(2)}) collective-permute-start(bf16[128,512]{1,0:T(8,128)(2,1)S(1)} %get-tuple-element.57.refs_1_), channel_id=1, source_target_pairs={{0,1},{1,0},{2,3},{3,2},{4,5},{5,4},{6,7},{7,6},{8,9},{9,8},{10,11... | collective-permute-start | bytes 393224 | tf_op jit(solution)/shard_map/ppermute | solution.py:630
  87.0 15.5 %all-to-all-start.3 = ((bf16[16,160,128]{2,1,0:T(8,128)(2,1)}), bf16[16,160,128]{2,1,0:T(8,128)(2,1)S(1)}, u32[]{:S(2)}, u32[]{:S(2)}) async-start(bf16[16,160,128]{2,1,0:T(8,128)(2,1)} %shard_map.116), calls=%async_computation.3 | async-start | bytes 1310720 | tf_op jit(solution)/shard_map/all_to_all | solution.py:662
  105.2 1.7 %collective-permute-start.9 = (bf16[4,32,1280]{2,1,0:T(8,128)(2,1)S(1)}, bf16[4,32,1280]{2,1,0:T(8,128)(2,1)S(1)}, u32[]{:S(2)}, u32[]{:S(2)}) collective-permute-start(bf16[4,32,1280]{2,1,0:T(8,128)(2,1)S(1)} %get-tuple-element.67), channel_id=1, source_target_pairs={{0,1},{1,0},{2,3},{3,2},{4,5},{5,4},{6,7},{7,6},{8,9},{9,8},{10,11... | collective-permute-start | bytes 983048 | tf_op jit(solution)/shard_map/ppermute | solution.py:630
  107.5 5.1 %collective-permute-start.10 = (bf16[32,1280]{1,0:T(8,128)(2,1)S(1)}, bf16[32,1280]{1,0:T(8,128)(2,1)S(1)}, u32[]{:S(2)}, u32[]{:S(2)}) collective-permute-start(bf16[32,1280]{1,0:T(8,128)(2,1)S(1)} %get-tuple-element.68), channel_id=1, source_target_pairs={{0,2},{1,3},{2,0},{3,1},{4,6},{5,7},{6,4},{7,5},{8,10},{9,11},{10,... | collective-permute-start | bytes 245768 | tf_op jit(solution)/shard_map/ppermute | solution.py:630
  107.6 5.4 %collective-permute-start.11 = (bf16[32,1280]{1,0:T(8,128)(2,1)S(1)}, bf16[32,1280]{1,0:T(8,128)(2,1)S(1)}, u32[]{:S(2)}, u32[]{:S(2)}) collective-permute-start(bf16[32,1280]{1,0:T(8,128)(2,1)S(1)} %get-tuple-element.69), channel_id=1, source_target_pairs={{0,4},{1,5},{2,6},{3,7},{4,0},{5,1},{6,2},{7,3},{8,12},{9,13},{10,... | collective-permute-start | bytes 245768 | tf_op jit(solution)/shard_map/ppermute | solution.py:630
  108.6 5.3 %collective-permute-start.12 = (bf16[32,1280]{1,0:T(8,128)(2,1)S(1)}, bf16[32,1280]{1,0:T(8,128)(2,1)S(1)}, u32[]{:S(2)}, u32[]{:S(2)}) collective-permute-start(bf16[32,1280]{1,0:T(8,128)(2,1)S(1)} %get-tuple-element.70), channel_id=1, source_target_pairs={{0,6},{1,7},{2,4},{3,5},{4,2},{5,3},{6,0},{7,1},{8,14},{9,15},{10,... | collective-permute-start | bytes 245768 | tf_op jit(solution)/shard_map/ppermute | solution.py:630
  113.9 4.6 %collective-permute-start.13 = (bf16[32,1408]{1,0:T(8,128)(2,1)S(1)}, bf16[32,1408]{1,0:T(8,128)(2,1)S(1)}, u32[]{:S(2)}, u32[]{:S(2)}) collective-permute-start(bf16[32,1408]{1,0:T(8,128)(2,1)S(1)} %shard_map.122), channel_id=1, source_target_pairs={{0,8},{8,0},{16,24},{24,16},{1,9},{9,1},{17,25},{25,17},{2,10},{10... | collective-permute-start | bytes 270344 | tf_op jit(solution)/shard_map/ppermute | solution.py:630
  118.6 5.5 %collective-permute-start.14 = (bf16[32,1408]{1,0:T(8,128)(2,1)S(1)}, bf16[32,1408]{1,0:T(8,128)(2,1)S(1)}, u32[]{:S(2)}, u32[]{:S(2)}) collective-permute-start(bf16[32,1408]{1,0:T(8,128)(2,1)S(1)} %add_convert_fusion.1), channel_id=1, source_target_pairs={{0,16},{8,24},{16,0},{24,8},{1,17},{9,25},{17,1},{25,9},{2,18},{10... | collective-permute-start | bytes 270344 | tf_op jit(solution)/shard_map/ppermute | solution.py:630
  124.1 6.0 %collective-permute-start.20 = (bf16[32,1408]{1,0:T(8,128)(2,1)S(1)}, bf16[32,1408]{1,0:T(8,128)(2,1)S(1)}, u32[]{:S(2)}, u32[]{:S(2)}) collective-permute-start(bf16[32,1408]{1,0:T(8,128)(2,1)S(1)} %add_convert_fusion.refs_1_), channel_id=1, source_target_pairs={{0,6},{1,7},{2,4},{3,5},{4,2},{5,3},{6,0},{7,1},{8,14},{9,15},{10,... | collective-permute-start | bytes 270344 | tf_op jit(solution)/shard_map/ppermute | solution.py:630
  127.6 4.5 %collective-permute-start.18 = (bf16[32,1408]{1,0:T(8,128)(2,1)S(1)}, bf16[32,1408]{1,0:T(8,128)(2,1)S(1)}, u32[]{:S(2)}, u32[]{:S(2)}) collective-permute-start(bf16[32,1408]{1,0:T(8,128)(2,1)S(1)} %add_convert_fusion.refs_1_), channel_id=1, source_target_pairs={{0,4},{1,5},{2,6},{3,7},{4,0},{5,1},{6,2},{7,3},{8,12},{9,13},{10,... | collective-permute-start | bytes 270344 | tf_op jit(solution)/shard_map/ppermute | solution.py:630
  127.6 4.5 %collective-permute-start.16 = (bf16[32,1408]{1,0:T(8,128)(2,1)S(1)}, bf16[32,1408]{1,0:T(8,128)(2,1)S(1)}, u32[]{:S(2)}, u32[]{:S(2)}) collective-permute-start(bf16[32,1408]{1,0:T(8,128)(2,1)S(1)} %add_convert_fusion.refs_1_), channel_id=1, source_target_pairs={{0,2},{1,3},{2,0},{3,1},{4,6},{5,7},{6,4},{7,5},{8,10},{9,11},{10,... | collective-permute-start | bytes 270344 | tf_op jit(solution)/shard_map/ppermute | solution.py:630
  128.3 4.4 %collective-permute-start.15 = (bf16[32,1408]{1,0:T(8,128)(2,1)S(1)}, bf16[32,1408]{1,0:T(8,128)(2,1)S(1)}, u32[]{:S(2)}, u32[]{:S(2)}) collective-permute-start(bf16[32,1408]{1,0:T(8,128)(2,1)S(1)} %add_convert_fusion.refs_1_), channel_id=1, source_target_pairs={{0,1},{1,0},{2,3},{3,2},{4,5},{5,4},{6,7},{7,6},{8,9},{9,8},{10,11... | collective-permute-start | bytes 270344 | tf_op jit(solution)/shard_map/ppermute | solution.py:630
  130.1 2.5 %collective-permute-start.21 = (bf16[32,1408]{1,0:T(8,128)(2,1)S(1)}, bf16[32,1408]{1,0:T(8,128)(2,1)S(1)}, u32[]{:S(2)}, u32[]{:S(2)}) collective-permute-start(bf16[32,1408]{1,0:T(8,128)(2,1)S(1)} %collective-permute-done.20.refs_7_), channel_id=1, source_target_pairs={{0,1},{1,0},{2,3},{3,2},{4,5},{5,4},{6,7},{7,6},{8,9},{9,8},{10,11... | collective-permute-start | bytes 270344 | tf_op jit(solution)/shard_map/ppermute | solution.py:630
  132.2 1.4 %collective-permute-start.17 = (bf16[32,1408]{1,0:T(8,128)(2,1)S(1)}, bf16[32,1408]{1,0:T(8,128)(2,1)S(1)}, u32[]{:S(2)}, u32[]{:S(2)}) collective-permute-start(bf16[32,1408]{1,0:T(8,128)(2,1)S(1)} %collective-permute-done.16.refs_3_), channel_id=1, source_target_pairs={{0,1},{1,0},{2,3},{3,2},{4,5},{5,4},{6,7},{7,6},{8,9},{9,8},{10,11... | collective-permute-start | bytes 270344 | tf_op jit(solution)/shard_map/ppermute | solution.py:630
  (12 other events, 149.6 us)

commit v21 on v19

--- a/solution.py
+++ b/solution.py
@@ -349,9 +349,7 @@
     low_ref[...] = softmax_out.astype(jnp.bfloat16)
 
 
-def grad_score_kernel(
-    residues, left_row, right_row, place_ref, own_ref, other_ref, full_ref, sent_ref
-):
+def grad_score_kernel(residues, left_row, right_row, place_ref, own_ref, other_ref, out_ref):
     core = place_ref[0]
     count = own_ref.shape[0] // 2
     part = residues // 2
@@ -365,20 +363,16 @@
         )
         for k in range(count)
     ]
-    terms = f32_dot(jnp.concatenate(left, axis=0), right, NT)
-    full_ref[...] = terms
-    sent_ref[...] = terms.astype(jnp.bfloat16)
-
-
-def softmax_gradient_kernel(
-    place_ref, softmax_ref, far_ref, grad_ref, other_ref, out_ref, out_far_ref
-):
+    out_ref[...] = f32_dot(jnp.concatenate(left, axis=0), right, NT).astype(jnp.bfloat16)
+
+
+def softmax_gradient_kernel(place_ref, softmax_ref, far_ref, grad_ref, out_ref, out_far_ref):
     half = place_ref[1]
     count = softmax_ref.shape[0]
     for which, probs, ref in ((half, softmax_ref, out_ref), (1 - half, far_ref, out_far_ref)):
         rows = pl.ds(pl.multiple_of(which * count, count), count)
         softmax_out = probs[...].astype(jnp.float32)
-        grad_probs = grad_ref[rows, :] + other_ref[rows, :].astype(jnp.float32)
+        grad_probs = grad_ref[rows, :].astype(jnp.float32)
         row_dot = jnp.sum(softmax_out * grad_probs, axis=-1, keepdims=True)
         ref[...] = (softmax_out * (grad_probs - row_dot)).astype(jnp.bfloat16)
 
@@ -573,16 +567,23 @@
     lax.fori_loop(0, pair_ref.shape[0] // 8, rows, 0)
 
 
-def output_kernel(parts_ref, combined_ref, out_weight_ref, pair_weight_ref):
+def output_kernel(place_ref, *refs):
+    *parts, combined_ref, out_weight_ref, pair_weight_ref, shares_ref = refs
+    core, chip = place_ref[0], place_ref[2]
     width = combined_ref.shape[0]
-    rows = parts_ref.shape[1]
-    for h in range(parts_ref.shape[0]):
-        block = slice(h * rows, (h + 1) * rows)
-        part = parts_ref[h].astype(jnp.float32)
+    rows = parts[0].shape[0]
+    heads = pair_weight_ref.shape[0]
+    for k, ref in enumerate(parts):
+        owner = jnp.bitwise_xor(chip, k // 2) * 2 + jnp.bitwise_xor(core, k % 2)
+        block = pl.ds(pl.multiple_of(owner * rows, rows), rows)
+        part = ref[...].astype(jnp.float32)
         combined_ref[block, :] = part[:, : 4 * width]
         out_weight_ref[block, :] = part[:, 4 * width : 5 * width]
-        share = part[: pair_weight_ref.shape[0], 5 * width :]
-        pair_weight_ref[...] = share if h == 0 else pair_weight_ref[...] + share
+        shares_ref[owner] = part[:heads, 5 * width :]
+    total = shares_ref[0]
+    for k in range(1, len(parts)):
+        total += shares_ref[k]
+    pair_weight_ref[...] = total
 
 
 def call(kernel, outs, *args, scratch=(), place=None, flops=0, after=(), outside=0, late=0):
@@ -688,7 +689,7 @@
     query_blocks, value_blocks = lax.optimization_barrier((query_blocks, value_blocks))
     value_blocks = across(value_blocks)
 
-    quarter, half_rows = (total // 4, total), (total // 2, total)
+    quarter = (total // 4, total)
     logit_mine, logit_sent = call(
         functools.partial(score_kernel, residues, 0, residues),
         [(quarter, f32), (quarter, f32)],
@@ -703,14 +704,14 @@
         place=place,
     )
     bias_other = swapped(bias_sent, "seq", seq_half)
-    grad_full, grad_sent = call(
-        functools.partial(grad_score_kernel, residues, residues, 0),
-        [(half_rows, f32), (half_rows, bf16)],
+    (grad_terms,) = call(
+        functools.partial(grad_score_kernel, residues, residues, 0), [((total // 2, total), bf16)],
         value_blocks, swapped(value_blocks, "res", 1),
         place=place, flops=2 * total * total * width,
     )
-    grad_other = swapped(grad_sent, "seq", seq_half)
-    bias_other, grad_full = lax.optimization_barrier((bias_other, grad_full))
+    halves = [[k, k + seq_half] for k in range(seq_half)]
+    grad_probs = lax.psum(grad_terms, "seq", axis_index_groups=halves)
+    bias_other, grad_terms = lax.optimization_barrier((bias_other, grad_terms))
     softmax_out, probs = call(
         softmax_kernel, [(quarter, f32), (quarter, bf16)],
         logit_mine, logit_other, bias_mine, bias_other,
@@ -736,7 +737,7 @@
     softmax_out = lax.optimization_barrier((attended, softmax_out))[1]
     grad_logits, grad_far = call(
         softmax_gradient_kernel, [(quarter, bf16), (quarter, bf16)],
-        softmax_out, probs_far, grad_full, grad_other,
+        softmax_out, probs_far, grad_probs,
         place=place, flops=total * total,
     )
     grad_sums = products(grad_logits, grad_far, query_blocks, residues, 0, True, scale)
@@ -798,10 +799,14 @@
     other_half = swapped(part, "seq", seq_half)
     other_half, pair_gradient = lax.optimization_barrier((other_half, pair_gradient))
     part = added(part, other_half)
+    chips = [part] + [swapped(part, "res", 2 * flip) for flip in range(1, res_size // 2)]
+    parts = [t for chip in chips for t in (chip, swapped(chip, "res", 1))]
     combined_gradient, output_gradient, pair_weight_gradient = call(
         output_kernel,
         [(wc.shape, f32), (wo.shape, f32), ((heads, channels), f32)],
-        lax.all_gather(part, "res", axis=0),
+        *parts,
+        scratch=[pltpu.VMEM((len(parts), heads, channels), f32)],
+        place=place,
     )
     return (
         updated,

time: 139 us -> 170 us (1.22)
  waiting for transfers between devices: 68.9 us -> 91.2 us
  between operations: 0.91 us -> 14.3 us
  blocking collectives: 10.1 us -> 0 us
  starting transfers between devices: 27.2 us -> 30.6 us
    psum x0 -> x1, waiting for transfers between devices: none -> 32.7 us  [head_body(): grad_probs = lax.psum(grad_terms, 'seq', axis_index_groups=halves)]
    ppermute x16 -> x22, waiting for transfers between devices: 52.8 us -> 41.9 us  [swapped(): lax.ppermute(mine, axis_name, [(a, a ^ distance) for a in range(size)])]
    all_gather x1 -> x0, blocking collectives: 10.1 us -> none  [head_body(): lax.all_gather(part, 'res', axis=0)]
    ppermute x16 -> x22, starting transfers between devices: 9.06 us -> 13.3 us  [swapped(): lax.ppermute(mine, axis_name, [(a, a ^ distance) for a in range(size)])]
  transfers between devices with their start and end apart: 20 -> 27, of which waited for: 18 -> 23; matrix products, arithmetic and copies ran while one was open for 0% -> 0% of each run, Pallas kernels for 15% -> 13%
where the time goes in v21:
time: 170 us; the launch traced here: 169 us
  waiting for transfers between devices  91.2 us (54%)
  Pallas kernels  31.9 us (19%)
  starting transfers between devices  30.6 us (18%)
  between operations  14.3 us (8%)
    ppermute x22, waiting for transfers between devices, swapped(): lax.ppermute(mine, axis_name, [(a, a ^ distance) for a in range(size)])  41.9 us
    psum x1, waiting for transfers between devices, head_body(): grad_probs = lax.psum(grad_terms, 'seq', axis_index_groups=halves)  32.7 us
    pallas_call x17, Pallas kernels, call(): pl.pallas_call(wrapped, out_shape=shapes, in_specs=[pl.BlockSpec(memory_s...  31.9 us
    all_to_all x4, starting transfers between devices, across(): lax.all_to_all(blocks, ('seq', 'res'), 0, 0, axis_index_groups=groups, ti...  17.2 us
    all_to_all x4, waiting for transfers between devices, across(): lax.all_to_all(blocks, ('seq', 'res'), 0, 0, axis_index_groups=groups, ti...  16 us
    ppermute x22, starting transfers between devices, swapped(): lax.ppermute(mine, axis_name, [(a, a ^ distance) for a in range(size)])  13.3 us
  transfers between devices with their start and end apart: 27, of which 23 were waited for; matrix products, arithmetic and copies ran while one was open for 0% of the time, Pallas kernels for 13%

profile of v21, /device:TPU:0, one launch (start us, length us, event | category | flops | bytes accessed | tf_op | source)
XLA Modules:
  0.0 169.2 jit_solution(13424301324620311316)
XLA Ops:
  7.2 2.6 %shard_map.109 = bf16[16,128,128]{2,1,0:T(8,128)(2,1)} custom-call(bf16[8,64,256]{2,1,0:T(8,128)(2,1)} %refs_0_.7, bf16[256,1024]{1,0:T(8,128)(2,1)} %refs_1_.10), custom_call_target="tpu_custom_call" | custom-call | flops 268435456 | bytes 1310720 | tf_op jit(solution)/shard_map/pallas_call | solution.py:621
  9.8 6.3 %all-to-all-start = ((bf16[16,128,128]{2,1,0:T(8,128)(2,1)}), bf16[16,128,128]{2,1,0:T(8,128)(2,1)S(1)}, u32[]{:S(2)}, u32[]{:S(2)}) async-start(bf16[16,128,128]{2,1,0:T(8,128)(2,1)} %shard_map.109), calls=%async_computation | async-start | bytes 1048576 | tf_op jit(solution)/shard_map/all_to_all | solution.py:670
  16.1 6.3 %shard_map.110 = (bf16[16,192,128]{2,1,0:T(8,128)(2,1)}, f32[8,64,128]{2,1,0:T(8,128)}, f32[64,128]{1,0:T(8,128)}, f32[64,128]{1,0:T(8,128)}) custom-call(bf16[8,64,256]{2,1,0:T(8,128)(2,1)} %refs_0_.7, bf16[8,64,256]{2,1,0:T(8,128)(2,1)} %refs_1_.8, bf16[256,1024]{1,0:T(8,128)(2,1)} %refs_1_.10, bf16[256,256]{1,0:T(8,128)(2,1)} %refs_3_.3, ...), custom_call_target="tpu_custom_call" | custom-call | flops 268435456 | bytes 4395008 | tf_op jit(solution)/shard_map/pallas_call | solution.py:621
  22.4 4.2 %all-to-all-done.refs_1_.refs_5_ = bf16[16,128,128]{2,1,0:T(8,128)(2,1)S(1)} async-done(((bf16[16,128,128]{2,1,0:T(8,128)(2,1)}), bf16[16,128,128]{2,1,0:T(8,128)(2,1)S(1)}, u32[]{:S(2)}, u32[]{:S(2)}) %all-to-all-start) | async-done | bytes 524320 | tf_op jit(solution)/shard_map/all_to_all | solution.py:670
  26.7 3.6 %all-to-all-start.1 = ((bf16[16,192,128]{2,1,0:T(8,128)(2,1)}), bf16[16,192,128]{2,1,0:T(8,128)(2,1)S(1)}, u32[]{:S(2)}, u32[]{:S(2)}) async-start(bf16[16,192,128]{2,1,0:T(8,128)(2,1)} %get-tuple-element.49), calls=%async_computation.1 | async-start | bytes 1572864 | tf_op jit(solution)/shard_map/all_to_all | solution.py:670
  33.3 2.7 %collective-permute-start.1 = (f32[128,512]{1,0:T(8,128)S(1)}, f32[128,512]{1,0:T(8,128)S(1)}, u32[]{:S(2)}, u32[]{:S(2)}) collective-permute-start(f32[128,512]{1,0:T(8,128)S(1)} %get-tuple-element.50), channel_id=1, source_target_pairs={{0,16},{8,24},{16,0},{24,8},{1,17},{9,25},{17,1},{25,9},{2,18},{10... | collective-permute-start | bytes 786440 | tf_op jit(solution)/shard_map/ppermute | solution.py:638
  35.9 9.3 %collective-permute-done.1.refs_2_ = f32[128,512]{1,0:T(8,128)S(1)} collective-permute-done((f32[128,512]{1,0:T(8,128)S(1)}, f32[128,512]{1,0:T(8,128)S(1)}, u32[]{:S(2)}, u32[]{:S(2)}) %collective-permute-start.1) | collective-permute-done | bytes 262176 | tf_op jit(solution)/shard_map/ppermute | solution.py:638
  45.3 4.0 %all-to-all-done.1.refs_1_.refs_5_ = bf16[16,192,128]{2,1,0:T(8,128)(2,1)S(1)} async-done(((bf16[16,192,128]{2,1,0:T(8,128)(2,1)}), bf16[16,192,128]{2,1,0:T(8,128)(2,1)S(1)}, u32[]{:S(2)}, u32[]{:S(2)}) %all-to-all-start.1) | async-done | bytes 786464 | tf_op jit(solution)/shard_map/all_to_all | solution.py:670
  49.9 1.6 collective-permute-done.3.refs_2_
  53.1 6.4 %collective-permute-done.2.refs_4_ = bf16[8,64,128]{2,1,0:T(8,128)(2,1)S(1)} collective-permute-done((bf16[8,64,128]{2,1,0:T(8,128)(2,1)S(1)}, bf16[8,64,128]{2,1,0:T(8,128)(2,1)S(1)}, u32[]{:S(2)}, u32[]{:S(2)}) %collective-permute-start.2) | collective-permute-done | bytes 131104 | tf_op jit(solution)/shard_map/ppermute | solution.py:638
  60.5 7.6 %collective-permute-done.4.refs_2_ = bf16[128,512]{1,0:T(8,128)(2,1)S(1)} collective-permute-done((bf16[128,512]{1,0:T(8,128)(2,1)S(1)}, bf16[128,512]{1,0:T(8,128)(2,1)S(1)}, u32[]{:S(2)}, u32[]{:S(2)}) %collective-permute-start.4) | collective-permute-done | bytes 131104 | tf_op jit(solution)/shard_map/ppermute | solution.py:638
  69.4 1.8 %shard_map.115 = bf16[16,128,128]{2,1,0:T(8,128)(2,1)} custom-call(s32[3]{0:T(128)S(1)} %pad_add_fusion.refs_0_, bf16[128,512]{1,0:T(8,128)(2,1)S(1)} %get-tuple-element.56.refs_1_, bf16[128,512]{1,0:T(8,128)(2,1)S(1)} %collective-permute-done.4.refs_2_, bf16[128,512]{1,0:T(8,128)(2,1)S(1)} %collective-permute-done.5.refs_3_, ...), custom_call_target="tpu_custom_call" | custom-call | flops 268435456 | bytes 1835008 | tf_op jit(solution)/shard_map/pallas_call | solution.py:621
  71.3 3.6 %all-to-all-start.2 = ((bf16[16,128,128]{2,1,0:T(8,128)(2,1)}), bf16[16,128,128]{2,1,0:T(8,128)(2,1)S(1)}, u32[]{:S(2)}, u32[]{:S(2)}) async-start(bf16[16,128,128]{2,1,0:T(8,128)(2,1)} %shard_map.115), calls=%async_computation.2 | async-start | bytes 1048576 | tf_op jit(solution)/shard_map/all_to_all | solution.py:670
  75.6 32.7 %all-reduce.2.cloned.1.call-done.refs_3_ = bf16[256,512]{1,0:T(8,128)(2,1)} async-done(((bf16[256,512]{1,0:T(8,128)(2,1)}), bf16[256,512]{1,0:T(8,128)(2,1)}) %all-reduce.2.cloned.1.call-update) | async-done | bytes 262160 | tf_op jit(solution)/shard_map/psum | solution.py:713
  111.5 1.9 %shard_map.117 = bf16[16,160,128]{2,1,0:T(8,128)(2,1)} custom-call(s32[3]{0:T(128)S(1)} %pad_add_fusion.refs_0_, bf16[128,512]{1,0:T(8,128)(2,1)S(1)} %get-tuple-element.59.refs_1_, bf16[128,512]{1,0:T(8,128)(2,1)S(1)} %get-tuple-element.60.refs_2_, bf16[128,512]{1,0:T(8,128)(2,1)S(1)} %collective-permute-done.7.refs_3_, ...), custom_call_target="tpu_custom_call" | custom-call | flops 268435456 | bytes 1703936 | tf_op jit(solution)/shard_map/pallas_call | solution.py:621
  113.4 3.8 %all-to-all-start.3 = ((bf16[16,160,128]{2,1,0:T(8,128)(2,1)}), bf16[16,160,128]{2,1,0:T(8,128)(2,1)S(1)}, u32[]{:S(2)}, u32[]{:S(2)}) async-start(bf16[16,160,128]{2,1,0:T(8,128)(2,1)} %shard_map.117), calls=%async_computation.3 | async-start | bytes 1310720 | tf_op jit(solution)/shard_map/all_to_all | solution.py:670
  117.2 4.1 %shard_map.118 = (bf16[8,64,256]{2,1,0:T(8,128)(2,1)}, bf16[512,512]{1,0:T(8,128)(2,1)}, bf16[512,256]{1,0:T(8,128)(2,1)}, bf16[256,768]{1,0:T(8,128)(2,1)}) custom-call(bf16[8,64,256]{2,1,0:T(8,128)(2,1)} %refs_0_.7, bf16[8,64,256]{2,1,0:T(8,128)(2,1)} %refs_1_.8, bf16[256,1024]{1,0:T(8,128)(2,1)} %refs_1_.10, bf16[256,256]{1,0:T(8,128)(2,1)} %refs_3_.3, ...), custom_call_target="tpu_custom_call" | custom-call | flops 469762048 | bytes 3145728 | tf_op jit(solution)/shard_map/pallas_call | solution.py:621
  121.3 7.8 %all-to-all-done.3.refs_0_.refs_3_ = bf16[16,160,128]{2,1,0:T(8,128)(2,1)S(1)} async-done(((bf16[16,160,128]{2,1,0:T(8,128)(2,1)}), bf16[16,160,128]{2,1,0:T(8,128)(2,1)S(1)}, u32[]{:S(2)}, u32[]{:S(2)}) %all-to-all-start.3) | async-done | bytes 655392 | tf_op jit(solution)/shard_map/all_to_all | solution.py:670
  135.2 2.5 %collective-permute-start.12 = (bf16[32,1280]{1,0:T(8,128)(2,1)S(1)}, bf16[32,1280]{1,0:T(8,128)(2,1)S(1)}, u32[]{:S(2)}, u32[]{:S(2)}) collective-permute-start(bf16[32,1280]{1,0:T(8,128)(2,1)S(1)} %get-tuple-element.72), channel_id=1, source_target_pairs={{0,6},{1,7},{2,4},{3,5},{4,2},{5,3},{6,0},{7,1},{8,14},{9,15},{10,... | collective-permute-start | bytes 245768 | tf_op jit(solution)/shard_map/ppermute | solution.py:638
  141.6 3.6 %collective-permute-done.13 = bf16[32,1408]{1,0:T(8,128)(2,1)S(1)} collective-permute-done((bf16[32,1408]{1,0:T(8,128)(2,1)S(1)}, bf16[32,1408]{1,0:T(8,128)(2,1)S(1)}, u32[]{:S(2)}, u32[]{:S(2)}) %collective-permute-start.13) | collective-permute-done | bytes 90144 | tf_op jit(solution)/shard_map/ppermute | solution.py:638
  146.6 4.3 %shard_map.124 = bf16[64,128,128]{2,1,0:T(8,128)(2,1)} custom-call(bf16[16,160,128]{2,1,0:T(8,128)(2,1)S(1)} %all-to-all-done.3.refs_0_.refs_3_, bf16[64,128,128]{2,1,0:T(8,128)(2,1)S(1)} %copy-done, f32[8,128]{1,0:T(8,128)S(1)} %bitcast.6, f32[8,64,128]{2,1,0:T(8,128)S(1)} %copy-done.5, f32[64,128]{1,0:T(8,128)S(1)} %copy-done.8, f32[64,128]{1,0:T(8,128)S(1)} %copy-done.9), custom_call_target="tpu_custom_call" | custom-call | flops 268435456 | bytes 5181440 | tf_op jit(solution)/shard_map/pallas_call | solution.py:621
  151.7 2.5 %collective-permute-start.20 = (bf16[32,1408]{1,0:T(8,128)(2,1)S(1)}, bf16[32,1408]{1,0:T(8,128)(2,1)S(1)}, u32[]{:S(2)}, u32[]{:S(2)}) collective-permute-start(bf16[32,1408]{1,0:T(8,128)(2,1)S(1)} %add_convert_fusion.refs_1_), channel_id=1, source_target_pairs={{0,6},{1,7},{2,4},{3,5},{4,2},{5,3},{6,0},{7,1},{8,14},{9,15},{10,... | collective-permute-start | bytes 270344 | tf_op jit(solution)/shard_map/ppermute | solution.py:638
  155.3 1.9 %collective-permute-done.20.refs_7_ = bf16[32,1408]{1,0:T(8,128)(2,1)S(1)} collective-permute-done((bf16[32,1408]{1,0:T(8,128)(2,1)S(1)}, bf16[32,1408]{1,0:T(8,128)(2,1)S(1)}, u32[]{:S(2)}, u32[]{:S(2)}) %collective-permute-start.20) | collective-permute-done | bytes 90144 | tf_op jit(solution)/shard_map/ppermute | solution.py:638
  160.7 1.6 shard_map.125
  (75 shorter events, 28.1 us)
Async XLA Ops:
  9.8 16.9 %all-to-all-start = ((bf16[16,128,128]{2,1,0:T(8,128)(2,1)}), bf16[16,128,128]{2,1,0:T(8,128)(2,1)S(1)}, u32[]{:S(2)}, u32[]{:S(2)}) async-start(bf16[16,128,128]{2,1,0:T(8,128)(2,1)} %shard_map.109), calls=%async_computation | async-start | bytes 1048576 | tf_op jit(solution)/shard_map/all_to_all | solution.py:670
  26.7 22.6 %all-to-all-start.1 = ((bf16[16,192,128]{2,1,0:T(8,128)(2,1)}), bf16[16,192,128]{2,1,0:T(8,128)(2,1)S(1)}, u32[]{:S(2)}, u32[]{:S(2)}) async-start(bf16[16,192,128]{2,1,0:T(8,128)(2,1)} %get-tuple-element.49), calls=%async_computation.1 | async-start | bytes 1572864 | tf_op jit(solution)/shard_map/all_to_all | solution.py:670
  30.3 2.0 %collective-permute-start = (bf16[16,128,128]{2,1,0:T(8,128)(2,1)S(1)}, bf16[16,128,128]{2,1,0:T(8,128)(2,1)S(1)}, u32[]{:S(2)}, u32[]{:S(2)}) collective-permute-start(bf16[16,128,128]{2,1,0:T(8,128)(2,1)S(1)} %all-to-all-done.refs_1_.refs_5_), channel_id=1, source_target_pairs={{0,1},{1,0},{2,3},{3,2},{4,5},{5,4},{6,7},{7,6},{8,9},{9,8},{10,11... | collective-permute-start | bytes 1572872 | tf_op jit(solution)/shard_map/ppermute | solution.py:638
  33.3 12.0 %collective-permute-start.1 = (f32[128,512]{1,0:T(8,128)S(1)}, f32[128,512]{1,0:T(8,128)S(1)}, u32[]{:S(2)}, u32[]{:S(2)}) collective-permute-start(f32[128,512]{1,0:T(8,128)S(1)} %get-tuple-element.50), channel_id=1, source_target_pairs={{0,16},{8,24},{16,0},{24,8},{1,17},{9,25},{17,1},{25,9},{2,18},{10... | collective-permute-start | bytes 786440 | tf_op jit(solution)/shard_map/ppermute | solution.py:638
  49.2 2.3 %collective-permute-start.3 = (bf16[16,192,128]{2,1,0:T(8,128)(2,1)S(1)}, bf16[16,192,128]{2,1,0:T(8,128)(2,1)S(1)}, u32[]{:S(2)}, u32[]{:S(2)}) collective-permute-start(bf16[16,192,128]{2,1,0:T(8,128)(2,1)S(1)} %all-to-all-done.1.refs_1_.refs_5_), channel_id=1, source_target_pairs={{0,1},{1,0},{2,3},{3,2},{4,5},{5,4},{6,7},{7,6},{8,9},{9,8},{10,11... | collective-permute-start | bytes 2359304 | tf_op jit(solution)/shard_map/ppermute | solution.py:638
  49.8 9.7 %collective-permute-start.2 = (bf16[8,64,128]{2,1,0:T(8,128)(2,1)S(1)}, bf16[8,64,128]{2,1,0:T(8,128)(2,1)S(1)}, u32[]{:S(2)}, u32[]{:S(2)}) collective-permute-start(bf16[8,64,128]{2,1,0:T(8,128)(2,1)S(1)} %get-tuple-element.54), channel_id=1, source_target_pairs={{0,16},{8,24},{16,0},{24,8},{1,17},{9,25},{17,1},{25,9},{2,18},{10... | collective-permute-start | bytes 393224 | tf_op jit(solution)/shard_map/ppermute | solution.py:638
  60.3 7.8 %collective-permute-start.4 = (bf16[128,512]{1,0:T(8,128)(2,1)S(1)}, bf16[128,512]{1,0:T(8,128)(2,1)S(1)}, u32[]{:S(2)}, u32[]{:S(2)}) collective-permute-start(bf16[128,512]{1,0:T(8,128)(2,1)S(1)} %get-tuple-element.56.refs_1_), channel_id=1, source_target_pairs={{0,16},{8,24},{16,0},{24,8},{1,17},{9,25},{17,1},{25,9},{2,18},{10... | collective-permute-start | bytes 393224 | tf_op jit(solution)/shard_map/ppermute | solution.py:638
  60.4 7.7 %collective-permute-start.5 = (bf16[128,512]{1,0:T(8,128)(2,1)S(1)}, bf16[128,512]{1,0:T(8,128)(2,1)S(1)}, u32[]{:S(2)}, u32[]{:S(2)}) collective-permute-start(bf16[128,512]{1,0:T(8,128)(2,1)S(1)} %get-tuple-element.56.refs_1_), channel_id=1, source_target_pairs={{0,1},{1,0},{2,3},{3,2},{4,5},{5,4},{6,7},{7,6},{8,9},{9,8},{10,11... | collective-permute-start | bytes 393224 | tf_op jit(solution)/shard_map/ppermute | solution.py:638
  71.3 42.1 %all-to-all-start.2 = ((bf16[16,128,128]{2,1,0:T(8,128)(2,1)}), bf16[16,128,128]{2,1,0:T(8,128)(2,1)S(1)}, u32[]{:S(2)}, u32[]{:S(2)}) async-start(bf16[16,128,128]{2,1,0:T(8,128)(2,1)} %shard_map.115), calls=%async_computation.2 | async-start | bytes 1048576 | tf_op jit(solution)/shard_map/all_to_all | solution.py:670
  74.8 33.4 %all-reduce.2.cloned.1.call-start = ((), (), s32[]{:S(2)}) async-start(), calls=%async_computation.4 | async-start | bytes 524288 | tf_op jit(solution)/shard_map/psum | solution.py:713
  109.9 1.4 collective-permute-start.7
  110.0 1.5 collective-permute-start.8
  113.4 15.7 %all-to-all-start.3 = ((bf16[16,160,128]{2,1,0:T(8,128)(2,1)}), bf16[16,160,128]{2,1,0:T(8,128)(2,1)S(1)}, u32[]{:S(2)}, u32[]{:S(2)}) async-start(bf16[16,160,128]{2,1,0:T(8,128)(2,1)} %shard_map.117), calls=%async_computation.3 | async-start | bytes 1310720 | tf_op jit(solution)/shard_map/all_to_all | solution.py:670
  131.8 1.7 %collective-permute-start.9 = (bf16[4,32,1280]{2,1,0:T(8,128)(2,1)S(1)}, bf16[4,32,1280]{2,1,0:T(8,128)(2,1)S(1)}, u32[]{:S(2)}, u32[]{:S(2)}) collective-permute-start(bf16[4,32,1280]{2,1,0:T(8,128)(2,1)S(1)} %get-tuple-element.69), channel_id=1, source_target_pairs={{0,1},{1,0},{2,3},{3,2},{4,5},{5,4},{6,7},{7,6},{8,9},{9,8},{10,11... | collective-permute-start | bytes 983048 | tf_op jit(solution)/shard_map/ppermute | solution.py:638
  134.1 5.1 %collective-permute-start.10 = (bf16[32,1280]{1,0:T(8,128)(2,1)S(1)}, bf16[32,1280]{1,0:T(8,128)(2,1)S(1)}, u32[]{:S(2)}, u32[]{:S(2)}) collective-permute-start(bf16[32,1280]{1,0:T(8,128)(2,1)S(1)} %get-tuple-element.70), channel_id=1, source_target_pairs={{0,2},{1,3},{2,0},{3,1},{4,6},{5,7},{6,4},{7,5},{8,10},{9,11},{10,... | collective-permute-start | bytes 245768 | tf_op jit(solution)/shard_map/ppermute | solution.py:638
  134.2 5.4 %collective-permute-start.11 = (bf16[32,1280]{1,0:T(8,128)(2,1)S(1)}, bf16[32,1280]{1,0:T(8,128)(2,1)S(1)}, u32[]{:S(2)}, u32[]{:S(2)}) collective-permute-start(bf16[32,1280]{1,0:T(8,128)(2,1)S(1)} %get-tuple-element.71), channel_id=1, source_target_pairs={{0,4},{1,5},{2,6},{3,7},{4,0},{5,1},{6,2},{7,3},{8,12},{9,13},{10,... | collective-permute-start | bytes 245768 | tf_op jit(solution)/shard_map/ppermute | solution.py:638
  135.2 5.3 %collective-permute-start.12 = (bf16[32,1280]{1,0:T(8,128)(2,1)S(1)}, bf16[32,1280]{1,0:T(8,128)(2,1)S(1)}, u32[]{:S(2)}, u32[]{:S(2)}) collective-permute-start(bf16[32,1280]{1,0:T(8,128)(2,1)S(1)} %get-tuple-element.72), channel_id=1, source_target_pairs={{0,6},{1,7},{2,4},{3,5},{4,2},{5,3},{6,0},{7,1},{8,14},{9,15},{10,... | collective-permute-start | bytes 245768 | tf_op jit(solution)/shard_map/ppermute | solution.py:638
  140.6 4.6 %collective-permute-start.13 = (bf16[32,1408]{1,0:T(8,128)(2,1)S(1)}, bf16[32,1408]{1,0:T(8,128)(2,1)S(1)}, u32[]{:S(2)}, u32[]{:S(2)}) collective-permute-start(bf16[32,1408]{1,0:T(8,128)(2,1)S(1)} %shard_map.123), channel_id=1, source_target_pairs={{0,8},{8,0},{16,24},{24,16},{1,9},{9,1},{17,25},{25,17},{2,10},{10... | collective-permute-start | bytes 270344 | tf_op jit(solution)/shard_map/ppermute | solution.py:638
  145.2 6.5 %collective-permute-start.14 = (bf16[32,1408]{1,0:T(8,128)(2,1)S(1)}, bf16[32,1408]{1,0:T(8,128)(2,1)S(1)}, u32[]{:S(2)}, u32[]{:S(2)}) collective-permute-start(bf16[32,1408]{1,0:T(8,128)(2,1)S(1)} %add_convert_fusion.1), channel_id=1, source_target_pairs={{0,16},{8,24},{16,0},{24,8},{1,17},{9,25},{17,1},{25,9},{2,18},{10... | collective-permute-start | bytes 270344 | tf_op jit(solution)/shard_map/ppermute | solution.py:638
  151.7 5.5 %collective-permute-start.20 = (bf16[32,1408]{1,0:T(8,128)(2,1)S(1)}, bf16[32,1408]{1,0:T(8,128)(2,1)S(1)}, u32[]{:S(2)}, u32[]{:S(2)}) collective-permute-start(bf16[32,1408]{1,0:T(8,128)(2,1)S(1)} %add_convert_fusion.refs_1_), channel_id=1, source_target_pairs={{0,6},{1,7},{2,4},{3,5},{4,2},{5,3},{6,0},{7,1},{8,14},{9,15},{10,... | collective-permute-start | bytes 270344 | tf_op jit(solution)/shard_map/ppermute | solution.py:638
  154.2 4.5 %collective-permute-start.18 = (bf16[32,1408]{1,0:T(8,128)(2,1)S(1)}, bf16[32,1408]{1,0:T(8,128)(2,1)S(1)}, u32[]{:S(2)}, u32[]{:S(2)}) collective-permute-start(bf16[32,1408]{1,0:T(8,128)(2,1)S(1)} %add_convert_fusion.refs_1_), channel_id=1, source_target_pairs={{0,4},{1,5},{2,6},{3,7},{4,0},{5,1},{6,2},{7,3},{8,12},{9,13},{10,... | collective-permute-start | bytes 270344 | tf_op jit(solution)/shard_map/ppermute | solution.py:638
  154.9 4.5 %collective-permute-start.16 = (bf16[32,1408]{1,0:T(8,128)(2,1)S(1)}, bf16[32,1408]{1,0:T(8,128)(2,1)S(1)}, u32[]{:S(2)}, u32[]{:S(2)}) collective-permute-start(bf16[32,1408]{1,0:T(8,128)(2,1)S(1)} %add_convert_fusion.refs_1_), channel_id=1, source_target_pairs={{0,2},{1,3},{2,0},{3,1},{4,6},{5,7},{6,4},{7,5},{8,10},{9,11},{10,... | collective-permute-start | bytes 270344 | tf_op jit(solution)/shard_map/ppermute | solution.py:638
  155.3 4.2 %collective-permute-start.15 = (bf16[32,1408]{1,0:T(8,128)(2,1)S(1)}, bf16[32,1408]{1,0:T(8,128)(2,1)S(1)}, u32[]{:S(2)}, u32[]{:S(2)}) collective-permute-start(bf16[32,1408]{1,0:T(8,128)(2,1)S(1)} %add_convert_fusion.refs_1_), channel_id=1, source_target_pairs={{0,1},{1,0},{2,3},{3,2},{4,5},{5,4},{6,7},{7,6},{8,9},{9,8},{10,11... | collective-permute-start | bytes 270344 | tf_op jit(solution)/shard_map/ppermute | solution.py:638
  157.2 2.2 %collective-permute-start.21 = (bf16[32,1408]{1,0:T(8,128)(2,1)S(1)}, bf16[32,1408]{1,0:T(8,128)(2,1)S(1)}, u32[]{:S(2)}, u32[]{:S(2)}) collective-permute-start(bf16[32,1408]{1,0:T(8,128)(2,1)S(1)} %collective-permute-done.20.refs_7_), channel_id=1, source_target_pairs={{0,1},{1,0},{2,3},{3,2},{4,5},{5,4},{6,7},{7,6},{8,9},{9,8},{10,11... | collective-permute-start | bytes 270344 | tf_op jit(solution)/shard_map/ppermute | solution.py:638
  (15 other events, 140.1 us)
Sparse Core Ops, SparseCore 0:
  78.6 29.6 all-reduce.1

commit v22 on v20

--- a/solution.py
+++ b/solution.py
@@ -292,7 +292,7 @@
 
 
 def score_kernel(
-    residues, left_row, right_row, with_bias, place_ref, own_ref, other_ref, mine_ref, sent_ref
+    residues, left_row, right_row, sent, place_ref, own_ref, other_ref, out_ref
 ):
     core, half = place_ref[0], place_ref[1]
     count = own_ref.shape[0] // 2
@@ -300,31 +300,30 @@
     right = jnp.concatenate(
         [lanes_of(own_ref, right_row, residues), lanes_of(other_ref, right_row, residues)], axis=1
     )
-    for which, ref in ((half, mine_ref), (1 - half, sent_ref)):
-        left = []
+    which = 1 - half if sent else half
+    left = []
+    for k in range(count // 2):
+        block = which * (count // 2) + k
+        rows = pl.ds(pl.multiple_of(left_row + core * part, part), part)
+        left.append(
+            jnp.concatenate(
+                [
+                    r[p * count + block, rows, :]
+                    for r in (own_ref, other_ref)
+                    for p in range(2)
+                ],
+                axis=1,
+            )
+        )
+    out_ref[...] = f32_dot(jnp.concatenate(left, axis=0), right, NT)
+    for p in range(2):
+        columns = pl.ds(pl.multiple_of((half * 2 + p) * LANES, LANES), LANES)
         for k in range(count // 2):
-            block = which * (count // 2) + k
-            rows = pl.ds(pl.multiple_of(left_row + core * part, part), part)
-            left.append(
-                jnp.concatenate(
-                    [
-                        r[p * count + block, rows, :]
-                        for r in (own_ref, other_ref)
-                        for p in range(2)
-                    ],
-                    axis=1,
-                )
-            )
-        ref[...] = f32_dot(jnp.concatenate(left, axis=0), right, NT).astype(ref.dtype)
-        if with_bias:
-            for p in range(2):
-                columns = pl.ds(pl.multiple_of((half * 2 + p) * LANES, LANES), LANES)
-                for k in range(count // 2):
-                    block = p * count + which * (count // 2) + k
-                    high = own_ref[block, 2 * residues : 2 * residues + part, :]
-                    low = own_ref[block, 2 * residues + part : 3 * residues, :]
-                    bias = high.astype(jnp.float32) + low.astype(jnp.float32)
-                    ref[k * part : (k + 1) * part, columns] += bias
+            block = p * count + which * (count // 2) + k
+            high = own_ref[block, 2 * residues : 2 * residues + part, :]
+            low = own_ref[block, 2 * residues + part : 3 * residues, :]
+            bias = high.astype(jnp.float32) + low.astype(jnp.float32)
+            out_ref[k * part : (k + 1) * part, columns] += bias
 
 
 def softmax_kernel(logit_ref, other_ref, out_ref, low_ref):
@@ -413,8 +412,17 @@
     )
 
 
+def split_rows(core, sums_ref, keep_ref, send_ref):
+    rows = keep_ref.shape[1]
+    for which, ref in ((core, keep_ref), (1 - core, send_ref)):
+        for block in range(keep_ref.shape[0]):
+            start = pl.multiple_of((2 * block + which) * rows, rows)
+            ref[block] = sums_ref[pl.ds(start, rows), :]
+
+
 def attended_weight_kernel(
-    x_ref, grad_ref, wc_ref, wo_ref, blocks_ref, updated_ref, projected_ref, normed_ref, sums_ref
+    place_ref, x_ref, grad_ref, wc_ref, wo_ref, blocks_ref,
+    updated_ref, projected_ref, normed_ref, keep_ref, send_ref, sums_ref,
 ):
     residues, width = x_ref.shape[1], x_ref.shape[2]
     tiles = width // LANES
@@ -432,28 +440,20 @@
     projected_ref[:, width:] = (grad_gated * attended * gate * (1.0 - gate)).astype(jnp.bfloat16)
     sums_ref[:, : 2 * width] = f32_dot(normed, projected_ref[...], TN).astype(jnp.bfloat16)
     sums_ref[:, 2 * width :] = f32_dot(gated, grad, TN).astype(jnp.bfloat16)
+    split_rows(place_ref[0], sums_ref, keep_ref, send_ref)
 
 
 def query_weight_kernel(
-    place_ref, normed_ref, attended_sums_ref, blocks_ref,
-    projected_ref, keep_ref, send_ref, sums_ref,
+    place_ref, normed_ref, blocks_ref, projected_ref, keep_ref, send_ref, sums_ref
 ):
     width = normed_ref.shape[1]
     tiles, residues = width // LANES, (blocks_ref.shape[1] * 2) // 5
-    core = place_ref[0]
     for t in range(2):
         projected_ref[:, t * width : (t + 1) * width] = unpack_heads(
             blocks_ref, t * residues, residues, tiles
         ).astype(jnp.bfloat16)
-    sums_ref[:, : 2 * width] = f32_dot(normed_ref[...], projected_ref[...], TN).astype(
-        jnp.bfloat16
-    )
-    sums_ref[:, 2 * width :] = attended_sums_ref[...]
-    rows = keep_ref.shape[1]
-    for which, ref in ((core, keep_ref), (1 - core, send_ref)):
-        for block in range(keep_ref.shape[0]):
-            start = pl.multiple_of((2 * block + which) * rows, rows)
-            ref[block] = sums_ref[pl.ds(start, rows), :]
+    sums_ref[...] = f32_dot(normed_ref[...], projected_ref[...], TN).astype(jnp.bfloat16)
+    split_rows(place_ref[0], sums_ref, keep_ref, send_ref)
 
 
 def core_sum_kernel(place_ref, keep_ref, other_ref, own_ref, *send_refs):
@@ -464,7 +464,14 @@
         ref[...] = total.astype(ref.dtype)
 
 
-def plane_sum_kernel(own_ref, pair_weight_ref, *refs):
+def plane_sum_kernel(own_ref, *refs):
+    total = own_ref[...]
+    for ref in refs[:-1]:
+        total += ref[...].astype(jnp.float32)
+    refs[-1][...] = total.astype(refs[-1].dtype)
+
+
+def plane_pair_sum_kernel(own_ref, pair_weight_ref, *refs):
     *received, out_ref = refs
     total = own_ref[...]
     for ref in received:
@@ -476,6 +483,16 @@
     out_ref[:, count:] = jnp.concatenate([pair_weight_ref[...], rest], axis=0).astype(
         out_ref.dtype
     )
+
+
+def join_kernel(query_ref, query_other_ref, value_ref, value_other_ref, out_ref):
+    query = query_ref[...].astype(jnp.float32) + query_other_ref[...].astype(jnp.float32)
+    value = value_ref[...].astype(jnp.float32) + value_other_ref[...].astype(jnp.float32)
+    channels = query.shape[1] + value.shape[1] - out_ref.shape[1] + LANES
+    count = query.shape[1] - channels
+    out_ref[:, :count] = query[:, :count].astype(out_ref.dtype)
+    out_ref[:, count : count + value.shape[1]] = value.astype(out_ref.dtype)
+    out_ref[:, count + value.shape[1] :] = query[:, count:].astype(out_ref.dtype)
 
 
 def pair_weight_kernel(blocks_ref, pair_ref, mean_ref, spread_ref, out_ref, share_ref):
@@ -690,12 +707,16 @@
     )
     grad_other = swapped(grad_sent, "seq", seq_half)
     query_blocks, grad_other = lax.optimization_barrier((query_blocks, grad_other))
-    logit_mine, logit_sent = call(
-        functools.partial(score_kernel, residues, 0, residues, True),
-        [(quarter, f32), (quarter, f32)],
-        query_blocks, swapped(query_blocks, "res", 1),
-        place=place, flops=2 * total * total * width,
-    )
+    query_other = swapped(query_blocks, "res", 1)
+
+    def scores(sent):
+        return call(
+            functools.partial(score_kernel, residues, 0, residues, sent), [(quarter, f32)],
+            query_blocks, query_other,
+            place=place, flops=total * total * width,
+        )[0]
+
+    logit_sent, logit_mine = scores(True), scores(False)
     softmax_out, probs = call(
         softmax_kernel, [(quarter, f32), (quarter, bf16)],
         logit_mine, swapped(logit_sent, "seq", seq_half),
@@ -728,21 +749,34 @@
     grad_sums, attended_blocks = lax.optimization_barrier((grad_sums, attended_blocks))
     grad_blocks = across(grad_sums)
 
-    updated, value_gate, normed, attended_sums = call(
+    rows = width // res_size
+
+    def part_rows(columns):
+        return [((res_size // 2, rows, columns), bf16)] * 2
+
+    def chip_sums(keep, send):
+        columns = keep.shape[2]
+        own, *sent = call(
+            core_sum_kernel,
+            [((rows, columns), f32)] + [((rows, columns), bf16)] * 3,
+            keep, swapped(send, "res", 1), place=place,
+        )
+        return own, [swapped(t, "res", 2 * flip) for flip, t in enumerate(sent, 1)]
+
+    updated, value_gate, normed, keep, send = call(
         attended_weight_kernel,
-        [
-            (x.shape, bf16),
-            ((tokens, 2 * width), bf16),
-            ((tokens, width), bf16),
-            ((width, 3 * width), bf16),
-        ],
+        [(x.shape, bf16), ((tokens, 2 * width), bf16), ((tokens, width), bf16)]
+        + part_rows(3 * width),
         x, grad, wc, wo, attended_blocks,
-        flops=14 * tokens * width * width, outside=4,
+        scratch=[pltpu.VMEM((width, 3 * width), bf16)],
+        place=place, flops=14 * tokens * width * width, outside=4,
+    )
+    value_own, value_received = chip_sums(keep, send)
+    grad_blocks, value_received = lax.optimization_barrier((grad_blocks, value_received))
+    (value_part,) = call(
+        plane_sum_kernel, [((rows, 3 * width), bf16)], value_own, *value_received
     )
     share = pltpu.VMEM((heads, residues, LANES), f32)
-    columns = 5 * width
-    rows = width // res_size
-    part_rows = ((res_size // 2, rows, columns), bf16)
     (pair_weight_part,) = call(
         pair_weight_kernel, [((heads, channels), f32)],
         grad_blocks, pair_entries, mean, spread,
@@ -750,17 +784,12 @@
     )
     query_key, keep, send = call(
         query_weight_kernel,
-        [((tokens, 2 * width), bf16), part_rows, part_rows],
-        normed, attended_sums, grad_blocks,
-        scratch=[pltpu.VMEM((width, columns), bf16)],
+        [((tokens, 2 * width), bf16)] + part_rows(2 * width),
+        normed, grad_blocks,
+        scratch=[pltpu.VMEM((width, 2 * width), bf16)],
         place=place, flops=4 * tokens * width * width, after=(pair_weight_part,),
     )
-    own, *sent = call(
-        core_sum_kernel,
-        [((rows, columns), f32)] + [((rows, columns), bf16)] * 3,
-        keep, swapped(send, "res", 1), place=place,
-    )
-    received = [swapped(t, "res", 2 * flip) for flip, t in enumerate(sent, 1)]
+    query_own, query_received = chip_sums(keep, send)
     (pair_gradient,) = call(
         functools.partial(pair_kernel, 2 * residues),
         [(pair_entries.shape, bf16)],
@@ -771,18 +800,26 @@
         alignment_kernel, [(x.shape, bf16)], x, wc, query_key, value_gate,
         flops=8 * tokens * width * width,
     )
-    received, alignment_gradient = lax.optimization_barrier((received, alignment_gradient))
-    (part,) = call(
-        plane_sum_kernel, [((rows, columns + channels), bf16)], own, pair_weight_part, *received
-    )
+    query_received, alignment_gradient = lax.optimization_barrier(
+        (query_received, alignment_gradient)
+    )
+    (query_part,) = call(
+        plane_pair_sum_kernel, [((rows, 2 * width + channels), bf16)],
+        query_own, pair_weight_part, *query_received,
+    )
+
     def added(mine, other):
         return (mine.astype(f32) + other.astype(f32)).astype(bf16)
 
-    other_plane = swapped(part, "seq", 1)
-    part = added(part, other_plane)
-    other_half = swapped(part, "seq", seq_half)
-    other_half, pair_gradient = lax.optimization_barrier((other_half, pair_gradient))
-    part = added(part, other_half)
+    value_part = added(value_part, swapped(value_part, "seq", 1))
+    value_other = swapped(value_part, "seq", seq_half)
+    query_part = added(query_part, swapped(query_part, "seq", 1))
+    query_other = swapped(query_part, "seq", seq_half)
+    query_other, pair_gradient = lax.optimization_barrier((query_other, pair_gradient))
+    (part,) = call(
+        join_kernel, [((rows, 5 * width + channels), bf16)],
+        query_part, query_other, value_part, value_other,
+    )
     chips = [part] + [swapped(part, "res", 2 * flip) for flip in range(1, res_size // 2)]
     parts = [t for chip in chips for t in (chip, swapped(chip, "res", 1))]
     combined_gradient, output_gradient, pair_weight_gradient = call(

time: 136 us -> 137 us (level)
  waiting for transfers between devices: 73.1 us -> 66.4 us
  starting transfers between devices: 31.1 us -> 36.6 us
    all_to_all x4, waiting for transfers between devices: 22.5 us -> 14.6 us  [across(): lax.all_to_all(blocks, ('seq', 'res'), 0, 0, axis_index_groups=groups, ti...]
    ppermute x22 -> x28, starting transfers between devices: 13.4 us -> 19.5 us  [swapped(): lax.ppermute(mine, axis_name, [(a, a ^ distance) for a in range(size)])]
    pallas_call x16 -> x20, Pallas kernels: 29.9 us -> 31.1 us  [call(): pl.pallas_call(wrapped, out_shape=shapes, in_specs=[pl.BlockSpec(memory_s...]
    ppermute x22 -> x28, waiting for transfers between devices: 50.6 us -> 51.8 us  [swapped(): lax.ppermute(mine, axis_name, [(a, a ^ distance) for a in range(size)])]
  transfers between devices with their start and end apart: 26 -> 32, of which waited for: 22 -> 22; matrix products, arithmetic and copies ran while one was open for 0% -> 0% of each run, Pallas kernels for 14% -> 16%
where the time goes in v22:
time: 137 us; the launch traced here: 136 us
  waiting for transfers between devices  66.4 us (48%)
  starting transfers between devices  36.6 us (27%)
  Pallas kernels  31.1 us (23%)
    ppermute x28, waiting for transfers between devices, swapped(): lax.ppermute(mine, axis_name, [(a, a ^ distance) for a in range(size)])  51.8 us
    pallas_call x20, Pallas kernels, call(): pl.pallas_call(wrapped, out_shape=shapes, in_specs=[pl.BlockSpec(memory_s...  31.1 us
    ppermute x28, starting transfers between devices, swapped(): lax.ppermute(mine, axis_name, [(a, a ^ distance) for a in range(size)])  19.5 us
    all_to_all x4, starting transfers between devices, across(): lax.all_to_all(blocks, ('seq', 'res'), 0, 0, axis_index_groups=groups, ti...  17.1 us
    all_to_all x4, waiting for transfers between devices, across(): lax.all_to_all(blocks, ('seq', 'res'), 0, 0, axis_index_groups=groups, ti...  14.6 us
  transfers between devices with their start and end apart: 32, of which 22 were waited for; matrix products, arithmetic and copies ran while one was open for 0% of the time, Pallas kernels for 16%

profile of v22, /device:TPU:0, one launch (start us, length us, event | category | flops | bytes accessed | tf_op | source)
XLA Modules:
  0.0 136.2 jit_solution(815968655029096419)
XLA Ops:
  0.6 2.7 %shard_map.109 = bf16[16,128,128]{2,1,0:T(8,128)(2,1)} custom-call(bf16[8,64,256]{2,1,0:T(8,128)(2,1)} %refs_0_.5, bf16[8,64,256]{2,1,0:T(8,128)(2,1)} %refs_2_.5, bf16[256,1024]{1,0:T(8,128)(2,1)} %refs_1_.10, bf16[256,256]{1,0:T(8,128)(2,1)} %refs_4_.1), custom_call_target="tpu_custom_call" | custom-call | flops 268435456 | bytes 1703936 | tf_op jit(solution)/shard_map/pallas_call | solution.py:630
  3.4 6.3 %all-to-all-start = ((bf16[16,128,128]{2,1,0:T(8,128)(2,1)}), bf16[16,128,128]{2,1,0:T(8,128)(2,1)S(1)}, u32[]{:S(2)}, u32[]{:S(2)}) async-start(bf16[16,128,128]{2,1,0:T(8,128)(2,1)} %shard_map.109), calls=%async_computation | async-start | bytes 1048576 | tf_op jit(solution)/shard_map/all_to_all | solution.py:679
  9.7 6.1 %shard_map.110 = (bf16[16,192,128]{2,1,0:T(8,128)(2,1)}, f32[8,64,128]{2,1,0:T(8,128)}, f32[64,128]{1,0:T(8,128)}, f32[64,128]{1,0:T(8,128)}) custom-call(bf16[8,64,256]{2,1,0:T(8,128)(2,1)} %refs_0_.5, bf16[256,1024]{1,0:T(8,128)(2,1)} %refs_1_.10, bf16[64,128,128]{2,1,0:T(8,128)(2,1)} %refs_1_.11, f32[8,128]{1,0:T(8,128)} %bitcast.5), custom_call_target="tpu_custom_call" | custom-call | flops 268435456 | bytes 4001792 | tf_op jit(solution)/shard_map/pallas_call | solution.py:630
  15.8 4.4 %all-to-all-done.refs_1_.refs_5_ = bf16[16,128,128]{2,1,0:T(8,128)(2,1)S(1)} async-done(((bf16[16,128,128]{2,1,0:T(8,128)(2,1)}), bf16[16,128,128]{2,1,0:T(8,128)(2,1)S(1)}, u32[]{:S(2)}, u32[]{:S(2)}) %all-to-all-start) | async-done | bytes 524320 | tf_op jit(solution)/shard_map/all_to_all | solution.py:679
  20.2 3.6 %all-to-all-start.1 = ((bf16[16,192,128]{2,1,0:T(8,128)(2,1)}), bf16[16,192,128]{2,1,0:T(8,128)(2,1)S(1)}, u32[]{:S(2)}, u32[]{:S(2)}) async-start(bf16[16,192,128]{2,1,0:T(8,128)(2,1)} %get-tuple-element.53), calls=%async_computation.1 | async-start | bytes 1572864 | tf_op jit(solution)/shard_map/all_to_all | solution.py:679
  26.7 2.7 %collective-permute-start.1 = (bf16[256,512]{1,0:T(8,128)(2,1)S(1)}, bf16[256,512]{1,0:T(8,128)(2,1)S(1)}, u32[]{:S(2)}, u32[]{:S(2)}) collective-permute-start(bf16[256,512]{1,0:T(8,128)(2,1)S(1)} %get-tuple-element.55), channel_id=1, source_target_pairs={{0,16},{8,24},{16,0},{24,8},{1,17},{9,25},{17,1},{25,9},{2,18},{10... | collective-permute-start | bytes 786440 | tf_op jit(solution)/shard_map/ppermute | solution.py:647
  29.4 9.5 %collective-permute-done.1.refs_4_ = bf16[256,512]{1,0:T(8,128)(2,1)S(1)} collective-permute-done((bf16[256,512]{1,0:T(8,128)(2,1)S(1)}, bf16[256,512]{1,0:T(8,128)(2,1)S(1)}, u32[]{:S(2)}, u32[]{:S(2)}) %collective-permute-start.1) | collective-permute-done | bytes 262176 | tf_op jit(solution)/shard_map/ppermute | solution.py:647
  38.8 4.0 %all-to-all-done.1.refs_1_.refs_5_ = bf16[16,192,128]{2,1,0:T(8,128)(2,1)S(1)} async-done(((bf16[16,192,128]{2,1,0:T(8,128)(2,1)}), bf16[16,192,128]{2,1,0:T(8,128)(2,1)S(1)}, u32[]{:S(2)}, u32[]{:S(2)}) %all-to-all-start.1) | async-done | bytes 786464 | tf_op jit(solution)/shard_map/all_to_all | solution.py:679
  42.8 2.3 %collective-permute-done.2.refs_2_ = bf16[16,192,128]{2,1,0:T(8,128)(2,1)S(1)} collective-permute-done((bf16[16,192,128]{2,1,0:T(8,128)(2,1)S(1)}, bf16[16,192,128]{2,1,0:T(8,128)(2,1)S(1)}, u32[]{:S(2)}, u32[]{:S(2)}) %collective-permute-start.2) | collective-permute-done | bytes 786464 | tf_op jit(solution)/shard_map/ppermute | solution.py:647
  46.9 14.0 %collective-permute-done.3.refs_1_ = f32[128,512]{1,0:T(8,128)S(1)} collective-permute-done((f32[128,512]{1,0:T(8,128)S(1)}, f32[128,512]{1,0:T(8,128)S(1)}, u32[]{:S(2)}, u32[]{:S(2)}) %collective-permute-start.3) | collective-permute-done | bytes 262176 | tf_op jit(solution)/shard_map/ppermute | solution.py:647
  61.2 7.6 %collective-permute-done.4.refs_2_ = bf16[128,512]{1,0:T(8,128)(2,1)S(1)} collective-permute-done((bf16[128,512]{1,0:T(8,128)(2,1)S(1)}, bf16[128,512]{1,0:T(8,128)(2,1)S(1)}, u32[]{:S(2)}, u32[]{:S(2)}) %collective-permute-start.4) | collective-permute-done | bytes 131104 | tf_op jit(solution)/shard_map/ppermute | solution.py:647
  70.2 1.8 %shard_map.115 = bf16[16,128,128]{2,1,0:T(8,128)(2,1)} custom-call(s32[3]{0:T(128)S(1)} %pad_add_fusion.refs_0_, bf16[128,512]{1,0:T(8,128)(2,1)S(1)} %get-tuple-element.57.refs_1_, bf16[128,512]{1,0:T(8,128)(2,1)S(1)} %collective-permute-done.4.refs_2_, bf16[128,512]{1,0:T(8,128)(2,1)S(1)} %collective-permute-done.5.refs_3_, ...), custom_call_target="tpu_custom_call" | custom-call | flops 268435456 | bytes 1572864 | tf_op jit(solution)/shard_map/pallas_call | solution.py:630
  72.0 3.6 %all-to-all-start.2 = ((bf16[16,128,128]{2,1,0:T(8,128)(2,1)}), bf16[16,128,128]{2,1,0:T(8,128)(2,1)S(1)}, u32[]{:S(2)}, u32[]{:S(2)}) async-start(bf16[16,128,128]{2,1,0:T(8,128)(2,1)} %shard_map.115), calls=%async_computation.2 | async-start | bytes 1048576 | tf_op jit(solution)/shard_map/all_to_all | solution.py:679
  78.0 1.9 %shard_map.117 = bf16[16,160,128]{2,1,0:T(8,128)(2,1)} custom-call(s32[3]{0:T(128)S(1)} %pad_add_fusion.refs_0_, bf16[128,512]{1,0:T(8,128)(2,1)S(1)} %get-tuple-element.62.refs_1_, bf16[128,512]{1,0:T(8,128)(2,1)S(1)} %get-tuple-element.63.refs_2_, bf16[128,512]{1,0:T(8,128)(2,1)S(1)} %collective-permute-done.7.refs_3_, ...), custom_call_target="tpu_custom_call" | custom-call | flops 268435456 | bytes 1966080 | tf_op jit(solution)/shard_map/pallas_call | solution.py:630
  79.9 6.2 %all-to-all-done.2.refs_5_ = bf16[16,128,128]{2,1,0:T(8,128)(2,1)S(1)} async-done(((bf16[16,128,128]{2,1,0:T(8,128)(2,1)}), bf16[16,128,128]{2,1,0:T(8,128)(2,1)S(1)}, u32[]{:S(2)}, u32[]{:S(2)}) %all-to-all-start.2) | async-done | bytes 524320 | tf_op jit(solution)/shard_map/all_to_all | solution.py:679
  86.1 3.6 %all-to-all-start.3 = ((bf16[16,160,128]{2,1,0:T(8,128)(2,1)}), bf16[16,160,128]{2,1,0:T(8,128)(2,1)S(1)}, u32[]{:S(2)}, u32[]{:S(2)}) async-start(bf16[16,160,128]{2,1,0:T(8,128)(2,1)} %shard_map.117), calls=%async_computation.3 | async-start | bytes 1310720 | tf_op jit(solution)/shard_map/all_to_all | solution.py:679
  89.7 4.1 %shard_map.118 = (bf16[8,64,256]{2,1,0:T(8,128)(2,1)}, bf16[512,512]{1,0:T(8,128)(2,1)}, bf16[512,256]{1,0:T(8,128)(2,1)}, bf16[4,32,768]{2,1,0:T(8,128)(2,1)}, bf16[4,32,768]{2,1,0:T(8,128)(2,1)}) custom-call(s32[3]{0:T(128)} %copy-done.9, bf16[8,64,256]{2,1,0:T(8,128)(2,1)} %refs_0_.5, bf16[8,64,256]{2,1,0:T(8,128)(2,1)} %refs_2_.5, ...), custom_call_target="tpu_custom_call" | custom-call | flops 469762048 | bytes 3145728 | tf_op jit(solution)/shard_map/pallas_call | solution.py:630
  97.1 1.9 %collective-permute-start.10 = (bf16[32,768]{1,0:T(8,128)(2,1)S(1)}, bf16[32,768]{1,0:T(8,128)(2,1)S(1)}, u32[]{:S(2)}, u32[]{:S(2)}) collective-permute-start(bf16[32,768]{1,0:T(8,128)(2,1)S(1)} %get-tuple-element.70), channel_id=1, source_target_pairs={{0,2},{1,3},{2,0},{3,1},{4,6},{5,7},{6,4},{7,5},{8,10},{9,11},{10,... | collective-permute-start | bytes 147464 | tf_op jit(solution)/shard_map/ppermute | solution.py:647
  103.0 2.4 %collective-permute-done.12.refs_3_ = bf16[32,768]{1,0:T(8,128)(2,1)S(1)} collective-permute-done((bf16[32,768]{1,0:T(8,128)(2,1)S(1)}, bf16[32,768]{1,0:T(8,128)(2,1)S(1)}, u32[]{:S(2)}, u32[]{:S(2)}) %collective-permute-start.12) | collective-permute-done | bytes 49184 | tf_op jit(solution)/shard_map/ppermute | solution.py:647
  111.5 2.4 %collective-permute-start.16 = (bf16[32,512]{1,0:T(8,128)(2,1)S(1)}, bf16[32,512]{1,0:T(8,128)(2,1)S(1)}, u32[]{:S(2)}, u32[]{:S(2)}) collective-permute-start(bf16[32,512]{1,0:T(8,128)(2,1)S(1)} %get-tuple-element.80), channel_id=1, source_target_pairs={{0,6},{1,7},{2,4},{3,5},{4,2},{5,3},{6,0},{7,1},{8,14},{9,15},{10,... | collective-permute-start | bytes 98312 | tf_op jit(solution)/shard_map/ppermute | solution.py:647
  118.5 1.9 %collective-permute-done.17 = bf16[32,640]{1,0:T(8,128)(2,1)S(1)} collective-permute-done((bf16[32,640]{1,0:T(8,128)(2,1)S(1)}, bf16[32,640]{1,0:T(8,128)(2,1)S(1)}, u32[]{:S(2)}, u32[]{:S(2)}) %collective-permute-start.17) | collective-permute-done | bytes 40992 | tf_op jit(solution)/shard_map/ppermute | solution.py:647
  121.4 4.3 %shard_map.125 = bf16[64,128,128]{2,1,0:T(8,128)(2,1)} custom-call(bf16[16,160,128]{2,1,0:T(8,128)(2,1)S(1)} %all-to-all-done.3.refs_0_.refs_2_, bf16[64,128,128]{2,1,0:T(8,128)(2,1)S(1)} %copy-done, f32[8,128]{1,0:T(8,128)S(1)} %bitcast.6, f32[8,64,128]{2,1,0:T(8,128)S(1)} %copy-done.4, f32[64,128]{1,0:T(8,128)S(1)} %copy-done.7, f32[64,128]{1,0:T(8,128)S(1)} %copy-done.8), custom_call_target="tpu_custom_call" | custom-call | flops 268435456 | bytes 5181440 | tf_op jit(solution)/shard_map/pallas_call | solution.py:630
  125.7 2.4 %collective-permute-start.26 = (bf16[32,1408]{1,0:T(8,128)(2,1)S(1)}, bf16[32,1408]{1,0:T(8,128)(2,1)S(1)}, u32[]{:S(2)}, u32[]{:S(2)}) collective-permute-start(bf16[32,1408]{1,0:T(8,128)(2,1)S(1)} %shard_map.127.refs_1_), channel_id=1, source_target_pairs={{0,6},{1,7},{2,4},{3,5},{4,2},{5,3},{6,0},{7,1},{8,14},{9,15},{10,... | collective-permute-start | bytes 270344 | tf_op jit(solution)/shard_map/ppermute | solution.py:647
  129.3 1.9 %collective-permute-done.26.refs_7_ = bf16[32,1408]{1,0:T(8,128)(2,1)S(1)} collective-permute-done((bf16[32,1408]{1,0:T(8,128)(2,1)S(1)}, bf16[32,1408]{1,0:T(8,128)(2,1)S(1)}, u32[]{:S(2)}, u32[]{:S(2)}) %collective-permute-start.26) | collective-permute-done | bytes 90144 | tf_op jit(solution)/shard_map/ppermute | solution.py:647
  (89 shorter events, 33.8 us)
Async XLA Ops:
  3.4 16.9 %all-to-all-start = ((bf16[16,128,128]{2,1,0:T(8,128)(2,1)}), bf16[16,128,128]{2,1,0:T(8,128)(2,1)S(1)}, u32[]{:S(2)}, u32[]{:S(2)}) async-start(bf16[16,128,128]{2,1,0:T(8,128)(2,1)} %shard_map.109), calls=%async_computation | async-start | bytes 1048576 | tf_op jit(solution)/shard_map/all_to_all | solution.py:679
  20.2 22.6 %all-to-all-start.1 = ((bf16[16,192,128]{2,1,0:T(8,128)(2,1)}), bf16[16,192,128]{2,1,0:T(8,128)(2,1)S(1)}, u32[]{:S(2)}, u32[]{:S(2)}) async-start(bf16[16,192,128]{2,1,0:T(8,128)(2,1)} %get-tuple-element.53), calls=%async_computation.1 | async-start | bytes 1572864 | tf_op jit(solution)/shard_map/all_to_all | solution.py:679
  26.7 12.1 %collective-permute-start.1 = (bf16[256,512]{1,0:T(8,128)(2,1)S(1)}, bf16[256,512]{1,0:T(8,128)(2,1)S(1)}, u32[]{:S(2)}, u32[]{:S(2)}) collective-permute-start(bf16[256,512]{1,0:T(8,128)(2,1)S(1)} %get-tuple-element.55), channel_id=1, source_target_pairs={{0,16},{8,24},{16,0},{24,8},{1,17},{9,25},{17,1},{25,9},{2,18},{10... | collective-permute-start | bytes 786440 | tf_op jit(solution)/shard_map/ppermute | solution.py:647
  42.8 2.3 %collective-permute-start.2 = (bf16[16,192,128]{2,1,0:T(8,128)(2,1)S(1)}, bf16[16,192,128]{2,1,0:T(8,128)(2,1)S(1)}, u32[]{:S(2)}, u32[]{:S(2)}) collective-permute-start(bf16[16,192,128]{2,1,0:T(8,128)(2,1)S(1)} %all-to-all-done.1.refs_1_.refs_5_), channel_id=1, source_target_pairs={{0,1},{1,0},{2,3},{3,2},{4,5},{5,4},{6,7},{7,6},{8,9},{9,8},{10,11... | collective-permute-start | bytes 2359304 | tf_op jit(solution)/shard_map/ppermute | solution.py:647
  45.9 14.9 %collective-permute-start.3 = (f32[128,512]{1,0:T(8,128)S(1)}, f32[128,512]{1,0:T(8,128)S(1)}, u32[]{:S(2)}, u32[]{:S(2)}) collective-permute-start(f32[128,512]{1,0:T(8,128)S(1)} %shard_map.113), channel_id=1, source_target_pairs={{0,16},{8,24},{16,0},{24,8},{1,17},{9,25},{17,1},{25,9},{2,18},{10... | collective-permute-start | bytes 786440 | tf_op jit(solution)/shard_map/ppermute | solution.py:647
  61.1 7.8 %collective-permute-start.4 = (bf16[128,512]{1,0:T(8,128)(2,1)S(1)}, bf16[128,512]{1,0:T(8,128)(2,1)S(1)}, u32[]{:S(2)}, u32[]{:S(2)}) collective-permute-start(bf16[128,512]{1,0:T(8,128)(2,1)S(1)} %get-tuple-element.57.refs_1_), channel_id=1, source_target_pairs={{0,16},{8,24},{16,0},{24,8},{1,17},{9,25},{17,1},{25,9},{2,18},{10... | collective-permute-start | bytes 393224 | tf_op jit(solution)/shard_map/ppermute | solution.py:647
  61.2 7.7 %collective-permute-start.5 = (bf16[128,512]{1,0:T(8,128)(2,1)S(1)}, bf16[128,512]{1,0:T(8,128)(2,1)S(1)}, u32[]{:S(2)}, u32[]{:S(2)}) collective-permute-start(bf16[128,512]{1,0:T(8,128)(2,1)S(1)} %get-tuple-element.57.refs_1_), channel_id=1, source_target_pairs={{0,1},{1,0},{2,3},{3,2},{4,5},{5,4},{6,7},{7,6},{8,9},{9,8},{10,11... | collective-permute-start | bytes 393224 | tf_op jit(solution)/shard_map/ppermute | solution.py:647
  72.0 14.1 %all-to-all-start.2 = ((bf16[16,128,128]{2,1,0:T(8,128)(2,1)}), bf16[16,128,128]{2,1,0:T(8,128)(2,1)S(1)}, u32[]{:S(2)}, u32[]{:S(2)}) async-start(bf16[16,128,128]{2,1,0:T(8,128)(2,1)} %shard_map.115), calls=%async_computation.2 | async-start | bytes 1048576 | tf_op jit(solution)/shard_map/all_to_all | solution.py:679
  86.1 19.3 %all-to-all-start.3 = ((bf16[16,160,128]{2,1,0:T(8,128)(2,1)}), bf16[16,160,128]{2,1,0:T(8,128)(2,1)S(1)}, u32[]{:S(2)}, u32[]{:S(2)}) async-start(bf16[16,160,128]{2,1,0:T(8,128)(2,1)} %shard_map.117), calls=%async_computation.3 | async-start | bytes 1310720 | tf_op jit(solution)/shard_map/all_to_all | solution.py:679
  97.1 4.2 %collective-permute-start.10 = (bf16[32,768]{1,0:T(8,128)(2,1)S(1)}, bf16[32,768]{1,0:T(8,128)(2,1)S(1)}, u32[]{:S(2)}, u32[]{:S(2)}) collective-permute-start(bf16[32,768]{1,0:T(8,128)(2,1)S(1)} %get-tuple-element.70), channel_id=1, source_target_pairs={{0,2},{1,3},{2,0},{3,1},{4,6},{5,7},{6,4},{7,5},{8,10},{9,11},{10,... | collective-permute-start | bytes 147464 | tf_op jit(solution)/shard_map/ppermute | solution.py:647
  98.9 4.1 %collective-permute-start.11 = (bf16[32,768]{1,0:T(8,128)(2,1)S(1)}, bf16[32,768]{1,0:T(8,128)(2,1)S(1)}, u32[]{:S(2)}, u32[]{:S(2)}) collective-permute-start(bf16[32,768]{1,0:T(8,128)(2,1)S(1)} %get-tuple-element.71), channel_id=1, source_target_pairs={{0,4},{1,5},{2,6},{3,7},{4,0},{5,1},{6,2},{7,3},{8,12},{9,13},{10,... | collective-permute-start | bytes 147464 | tf_op jit(solution)/shard_map/ppermute | solution.py:647
  100.4 5.0 %collective-permute-start.12 = (bf16[32,768]{1,0:T(8,128)(2,1)S(1)}, bf16[32,768]{1,0:T(8,128)(2,1)S(1)}, u32[]{:S(2)}, u32[]{:S(2)}) collective-permute-start(bf16[32,768]{1,0:T(8,128)(2,1)S(1)} %get-tuple-element.72), channel_id=1, source_target_pairs={{0,6},{1,7},{2,4},{3,5},{4,2},{5,3},{6,0},{7,1},{8,14},{9,15},{10,... | collective-permute-start | bytes 147464 | tf_op jit(solution)/shard_map/ppermute | solution.py:647
  108.2 9.5 %collective-permute-start.19 = (bf16[32,768]{1,0:T(8,128)(2,1)S(1)}, bf16[32,768]{1,0:T(8,128)(2,1)S(1)}, u32[]{:S(2)}, u32[]{:S(2)}) collective-permute-start(bf16[32,768]{1,0:T(8,128)(2,1)S(1)} %shard_map.126), channel_id=1, source_target_pairs={{0,8},{8,0},{16,24},{24,16},{1,9},{9,1},{17,25},{25,17},{2,10},{10... | collective-permute-start | bytes 147464 | tf_op jit(solution)/shard_map/ppermute | solution.py:647
  110.3 4.8 %collective-permute-start.14 = (bf16[32,512]{1,0:T(8,128)(2,1)S(1)}, bf16[32,512]{1,0:T(8,128)(2,1)S(1)}, u32[]{:S(2)}, u32[]{:S(2)}) collective-permute-start(bf16[32,512]{1,0:T(8,128)(2,1)S(1)} %get-tuple-element.78), channel_id=1, source_target_pairs={{0,2},{1,3},{2,0},{3,1},{4,6},{5,7},{6,4},{7,5},{8,10},{9,11},{10,... | collective-permute-start | bytes 98312 | tf_op jit(solution)/shard_map/ppermute | solution.py:647
  111.0 4.3 %collective-permute-start.15 = (bf16[32,512]{1,0:T(8,128)(2,1)S(1)}, bf16[32,512]{1,0:T(8,128)(2,1)S(1)}, u32[]{:S(2)}, u32[]{:S(2)}) collective-permute-start(bf16[32,512]{1,0:T(8,128)(2,1)S(1)} %get-tuple-element.79), channel_id=1, source_target_pairs={{0,4},{1,5},{2,6},{3,7},{4,0},{5,1},{6,2},{7,3},{8,12},{9,13},{10,... | collective-permute-start | bytes 98312 | tf_op jit(solution)/shard_map/ppermute | solution.py:647
  111.5 4.8 %collective-permute-start.16 = (bf16[32,512]{1,0:T(8,128)(2,1)S(1)}, bf16[32,512]{1,0:T(8,128)(2,1)S(1)}, u32[]{:S(2)}, u32[]{:S(2)}) collective-permute-start(bf16[32,512]{1,0:T(8,128)(2,1)S(1)} %get-tuple-element.80), channel_id=1, source_target_pairs={{0,6},{1,7},{2,4},{3,5},{4,2},{5,3},{6,0},{7,1},{8,14},{9,15},{10,... | collective-permute-start | bytes 98312 | tf_op jit(solution)/shard_map/ppermute | solution.py:647
  116.3 4.1 %collective-permute-start.17 = (bf16[32,640]{1,0:T(8,128)(2,1)S(1)}, bf16[32,640]{1,0:T(8,128)(2,1)S(1)}, u32[]{:S(2)}, u32[]{:S(2)}) collective-permute-start(bf16[32,640]{1,0:T(8,128)(2,1)S(1)} %shard_map.124), channel_id=1, source_target_pairs={{0,8},{8,0},{16,24},{24,16},{1,9},{9,1},{17,25},{25,17},{2,10},{10... | collective-permute-start | bytes 122888 | tf_op jit(solution)/shard_map/ppermute | solution.py:647
  117.6 8.1 %collective-permute-start.20 = (bf16[32,768]{1,0:T(8,128)(2,1)S(1)}, bf16[32,768]{1,0:T(8,128)(2,1)S(1)}, u32[]{:S(2)}, u32[]{:S(2)}) collective-permute-start(bf16[32,768]{1,0:T(8,128)(2,1)S(1)} %add_convert_fusion.refs_2_), channel_id=1, source_target_pairs={{0,16},{8,24},{16,0},{24,8},{1,17},{9,25},{17,1},{25,9},{2,18},{10... | collective-permute-start | bytes 147464 | tf_op jit(solution)/shard_map/ppermute | solution.py:647
  120.5 5.2 %collective-permute-start.18 = (bf16[32,640]{1,0:T(8,128)(2,1)S(1)}, bf16[32,640]{1,0:T(8,128)(2,1)S(1)}, u32[]{:S(2)}, u32[]{:S(2)}) collective-permute-start(bf16[32,640]{1,0:T(8,128)(2,1)S(1)} %add_convert_fusion.1.refs_0_), channel_id=1, source_target_pairs={{0,16},{8,24},{16,0},{24,8},{1,17},{9,25},{17,1},{25,9},{2,18},{10... | collective-permute-start | bytes 122888 | tf_op jit(solution)/shard_map/ppermute | solution.py:647
  125.7 5.5 %collective-permute-start.26 = (bf16[32,1408]{1,0:T(8,128)(2,1)S(1)}, bf16[32,1408]{1,0:T(8,128)(2,1)S(1)}, u32[]{:S(2)}, u32[]{:S(2)}) collective-permute-start(bf16[32,1408]{1,0:T(8,128)(2,1)S(1)} %shard_map.127.refs_1_), channel_id=1, source_target_pairs={{0,6},{1,7},{2,4},{3,5},{4,2},{5,3},{6,0},{7,1},{8,14},{9,15},{10,... | collective-permute-start | bytes 270344 | tf_op jit(solution)/shard_map/ppermute | solution.py:647
  128.1 4.5 %collective-permute-start.24 = (bf16[32,1408]{1,0:T(8,128)(2,1)S(1)}, bf16[32,1408]{1,0:T(8,128)(2,1)S(1)}, u32[]{:S(2)}, u32[]{:S(2)}) collective-permute-start(bf16[32,1408]{1,0:T(8,128)(2,1)S(1)} %shard_map.127.refs_1_), channel_id=1, source_target_pairs={{0,4},{1,5},{2,6},{3,7},{4,0},{5,1},{6,2},{7,3},{8,12},{9,13},{10,... | collective-permute-start | bytes 270344 | tf_op jit(solution)/shard_map/ppermute | solution.py:647
  128.7 4.5 %collective-permute-start.22 = (bf16[32,1408]{1,0:T(8,128)(2,1)S(1)}, bf16[32,1408]{1,0:T(8,128)(2,1)S(1)}, u32[]{:S(2)}, u32[]{:S(2)}) collective-permute-start(bf16[32,1408]{1,0:T(8,128)(2,1)S(1)} %shard_map.127.refs_1_), channel_id=1, source_target_pairs={{0,2},{1,3},{2,0},{3,1},{4,6},{5,7},{6,4},{7,5},{8,10},{9,11},{10,... | collective-permute-start | bytes 270344 | tf_op jit(solution)/shard_map/ppermute | solution.py:647
  129.3 4.0 %collective-permute-start.21 = (bf16[32,1408]{1,0:T(8,128)(2,1)S(1)}, bf16[32,1408]{1,0:T(8,128)(2,1)S(1)}, u32[]{:S(2)}, u32[]{:S(2)}) collective-permute-start(bf16[32,1408]{1,0:T(8,128)(2,1)S(1)} %shard_map.127.refs_1_), channel_id=1, source_target_pairs={{0,1},{1,0},{2,3},{3,2},{4,5},{5,4},{6,7},{7,6},{8,9},{9,8},{10,11... | collective-permute-start | bytes 270344 | tf_op jit(solution)/shard_map/ppermute | solution.py:647
  131.2 2.1 %collective-permute-start.27 = (bf16[32,1408]{1,0:T(8,128)(2,1)S(1)}, bf16[32,1408]{1,0:T(8,128)(2,1)S(1)}, u32[]{:S(2)}, u32[]{:S(2)}) collective-permute-start(bf16[32,1408]{1,0:T(8,128)(2,1)S(1)} %collective-permute-done.26.refs_7_), channel_id=1, source_target_pairs={{0,1},{1,0},{2,3},{3,2},{4,5},{5,4},{6,7},{7,6},{8,9},{9,8},{10,11... | collective-permute-start | bytes 270344 | tf_op jit(solution)/shard_map/ppermute | solution.py:647
  (21 other events, 230.1 us)

commit v23 on v20

--- a/solution.py
+++ b/solution.py
@@ -292,7 +292,7 @@
 
 
 def score_kernel(
-    residues, left_row, right_row, with_bias, place_ref, own_ref, other_ref, mine_ref, sent_ref
+    residues, left_row, right_row, sent, with_bias, place_ref, own_ref, other_ref, out_ref
 ):
     core, half = place_ref[0], place_ref[1]
     count = own_ref.shape[0] // 2
@@ -300,73 +300,41 @@
     right = jnp.concatenate(
         [lanes_of(own_ref, right_row, residues), lanes_of(other_ref, right_row, residues)], axis=1
     )
-    for which, ref in ((half, mine_ref), (1 - half, sent_ref)):
-        left = []
+    which = 1 - half if sent else half
+    left = []
+    for k in range(count // 2):
+        block = which * (count // 2) + k
+        rows = pl.ds(pl.multiple_of(left_row + core * part, part), part)
+        left.append(
+            jnp.concatenate(
+                [
+                    r[p * count + block, rows, :]
+                    for r in (own_ref, other_ref)
+                    for p in range(2)
+                ],
+                axis=1,
+            )
+        )
+    terms = f32_dot(jnp.concatenate(left, axis=0), right, NT)
+    out_ref[...] = terms.astype(out_ref.dtype)
+    for p in range(2 if with_bias else 0):
+        columns = pl.ds(pl.multiple_of((half * 2 + p) * LANES, LANES), LANES)
         for k in range(count // 2):
-            block = which * (count // 2) + k
-            rows = pl.ds(pl.multiple_of(left_row + core * part, part), part)
-            left.append(
-                jnp.concatenate(
-                    [
-                        r[p * count + block, rows, :]
-                        for r in (own_ref, other_ref)
-                        for p in range(2)
-                    ],
-                    axis=1,
-                )
-            )
-        ref[...] = f32_dot(jnp.concatenate(left, axis=0), right, NT).astype(ref.dtype)
-        if with_bias:
-            for p in range(2):
-                columns = pl.ds(pl.multiple_of((half * 2 + p) * LANES, LANES), LANES)
-                for k in range(count // 2):
-                    block = p * count + which * (count // 2) + k
-                    high = own_ref[block, 2 * residues : 2 * residues + part, :]
-                    low = own_ref[block, 2 * residues + part : 3 * residues, :]
-                    bias = high.astype(jnp.float32) + low.astype(jnp.float32)
-                    ref[k * part : (k + 1) * part, columns] += bias
-
-
-def softmax_kernel(logit_ref, other_ref, out_ref, low_ref):
-    logits = logit_ref[...] + other_ref[...]
+            block = p * count + which * (count // 2) + k
+            high = own_ref[block, 2 * residues : 2 * residues + part, :]
+            low = own_ref[block, 2 * residues + part : 3 * residues, :]
+            bias = high.astype(jnp.float32) + low.astype(jnp.float32)
+            out_ref[k * part : (k + 1) * part, columns] += bias
+
+
+def softmax_kernel(logit_ref, logit_other_ref, grad_ref, grad_other_ref, out_ref, low_ref):
+    logits = logit_ref[...] + logit_other_ref[...]
     lifted = jnp.exp(logits - jnp.max(logits, axis=-1, keepdims=True))
     softmax_out = lifted / jnp.sum(lifted, axis=-1, keepdims=True)
-    out_ref[...] = softmax_out
     low_ref[...] = softmax_out.astype(jnp.bfloat16)
-
-
-def grad_score_kernel(
-    residues, left_row, right_row, place_ref, own_ref, other_ref, full_ref, sent_ref
-):
-    core = place_ref[0]
-    count = own_ref.shape[0] // 2
-    part = residues // 2
-    right = jnp.concatenate(
-        [lanes_of(own_ref, right_row, residues), lanes_of(other_ref, right_row, residues)], axis=1
-    )
-    rows = pl.ds(pl.multiple_of(left_row + core * part, part), part)
-    left = [
-        jnp.concatenate(
-            [r[p * count + k, rows, :] for r in (own_ref, other_ref) for p in range(2)], axis=1
-        )
-        for k in range(count)
-    ]
-    terms = f32_dot(jnp.concatenate(left, axis=0), right, NT)
-    full_ref[...] = terms
-    sent_ref[...] = terms.astype(jnp.bfloat16)
-
-
-def softmax_gradient_kernel(
-    place_ref, softmax_ref, far_ref, grad_ref, other_ref, out_ref, out_far_ref
-):
-    half = place_ref[1]
-    count = softmax_ref.shape[0]
-    for which, probs, ref in ((half, softmax_ref, out_ref), (1 - half, far_ref, out_far_ref)):
-        rows = pl.ds(pl.multiple_of(which * count, count), count)
-        softmax_out = probs[...].astype(jnp.float32)
-        grad_probs = grad_ref[rows, :] + other_ref[rows, :].astype(jnp.float32)
-        row_dot = jnp.sum(softmax_out * grad_probs, axis=-1, keepdims=True)
-        ref[...] = (softmax_out * (grad_probs - row_dot)).astype(jnp.bfloat16)
+    grad_probs = grad_ref[...] + grad_other_ref[...].astype(jnp.float32)
+    row_dot = jnp.sum(softmax_out * grad_probs, axis=-1, keepdims=True)
+    out_ref[...] = (softmax_out * (grad_probs - row_dot)).astype(jnp.bfloat16)
 
 
 def product_kernel(
@@ -681,24 +649,27 @@
     value_blocks, query_blocks = lax.optimization_barrier((value_blocks, query_blocks))
     query_blocks = across(query_blocks)
 
-    quarter, half_rows = (total // 4, total), (total // 2, total)
-    grad_full, grad_sent = call(
-        functools.partial(grad_score_kernel, residues, residues, 0),
-        [(half_rows, f32), (half_rows, bf16)],
-        value_blocks, swapped(value_blocks, "res", 1),
-        place=place, flops=2 * total * total * width,
-    )
+    quarter = (total // 4, total)
+
+    def scores(blocks, other, left_row, right_row, sent, with_bias, kind):
+        return call(
+            functools.partial(score_kernel, residues, left_row, right_row, sent, with_bias),
+            [(quarter, kind)],
+            blocks, other,
+            place=place, flops=total * total * width,
+        )[0]
+
+    value_other = swapped(value_blocks, "res", 1)
+    grad_sent = scores(value_blocks, value_other, residues, 0, True, False, bf16)
+    grad_mine = scores(value_blocks, value_other, residues, 0, False, False, f32)
     grad_other = swapped(grad_sent, "seq", seq_half)
     query_blocks, grad_other = lax.optimization_barrier((query_blocks, grad_other))
-    logit_mine, logit_sent = call(
-        functools.partial(score_kernel, residues, 0, residues, True),
-        [(quarter, f32), (quarter, f32)],
-        query_blocks, swapped(query_blocks, "res", 1),
-        place=place, flops=2 * total * total * width,
-    )
-    softmax_out, probs = call(
-        softmax_kernel, [(quarter, f32), (quarter, bf16)],
-        logit_mine, swapped(logit_sent, "seq", seq_half),
+    query_other = swapped(query_blocks, "res", 1)
+    logit_sent = scores(query_blocks, query_other, 0, residues, True, True, f32)
+    logit_mine = scores(query_blocks, query_other, 0, residues, False, True, f32)
+    grad_logits, probs = call(
+        softmax_kernel, [(quarter, bf16), (quarter, bf16)],
+        logit_mine, swapped(logit_sent, "seq", seq_half), grad_mine, grad_other,
         flops=total * total,
     )
 
@@ -716,14 +687,9 @@
         return out
 
     probs_far = swapped(probs, "seq", seq_half)
+    grad_far = swapped(grad_logits, "seq", seq_half)
     attended = products(probs, probs_far, value_blocks, 0, residues, False, 1.0)
     attended_blocks = across(attended)
-    softmax_out = lax.optimization_barrier((attended, softmax_out))[1]
-    grad_logits, grad_far = call(
-        softmax_gradient_kernel, [(quarter, bf16), (quarter, bf16)],
-        softmax_out, probs_far, grad_full, grad_other,
-        place=place, flops=total * total,
-    )
     grad_sums = products(grad_logits, grad_far, query_blocks, residues, 0, True, scale)
     grad_sums, attended_blocks = lax.optimization_barrier((grad_sums, attended_blocks))
     grad_blocks = across(grad_sums)

time: 136 us -> 138 us (1.015)
  starting transfers between devices: 31.1 us -> 32.7 us
    all_to_all x4, waiting for transfers between devices: 22.5 us -> 17.1 us  [across(): lax.all_to_all(blocks, ('seq', 'res'), 0, 0, axis_index_groups=groups, ti...]
    ppermute x22 -> x23, waiting for transfers between devices: 50.6 us -> 55.1 us  [swapped(): lax.ppermute(mine, axis_name, [(a, a ^ distance) for a in range(size)])]
    pallas_call x16 -> x17, Pallas kernels: 29.9 us -> 30.8 us  [call(): pl.pallas_call(wrapped, out_shape=shapes, in_specs=[pl.BlockSpec(memory_s...]
    ppermute x22 -> x23, starting transfers between devices: 13.4 us -> 13.8 us  [swapped(): lax.ppermute(mine, axis_name, [(a, a ^ distance) for a in range(size)])]
  transfers between devices with their start and end apart: 26 -> 27, of which waited for: 22 -> 23; matrix products, arithmetic and copies ran while one was open for 0% -> 0% of each run, Pallas kernels for 14% -> 15%
where the time goes in v23:
time: 138 us; the launch traced here: 137 us
  waiting for transfers between devices  72.2 us (52%)
  starting transfers between devices  32.7 us (24%)
  Pallas kernels  30.8 us (22%)
    ppermute x23, waiting for transfers between devices, swapped(): lax.ppermute(mine, axis_name, [(a, a ^ distance) for a in range(size)])  55.1 us
    pallas_call x17, Pallas kernels, call(): pl.pallas_call(wrapped, out_shape=shapes, in_specs=[pl.BlockSpec(memory_s...  30.8 us
    all_to_all x4, starting transfers between devices, across(): lax.all_to_all(blocks, ('seq', 'res'), 0, 0, axis_index_groups=groups, ti...  18.9 us
    all_to_all x4, waiting for transfers between devices, across(): lax.all_to_all(blocks, ('seq', 'res'), 0, 0, axis_index_groups=groups, ti...  17.1 us
    ppermute x23, starting transfers between devices, swapped(): lax.ppermute(mine, axis_name, [(a, a ^ distance) for a in range(size)])  13.8 us
  transfers between devices with their start and end apart: 27, of which 23 were waited for; matrix products, arithmetic and copies ran while one was open for 0% of the time, Pallas kernels for 15%

profile of v23, /device:TPU:0, one launch (start us, length us, event | category | flops | bytes accessed | tf_op | source)
XLA Modules:
  0.0 136.8 jit_solution(2933854520354053106)
XLA Ops:
  0.6 2.7 %shard_map.109 = bf16[16,128,128]{2,1,0:T(8,128)(2,1)} custom-call(bf16[8,64,256]{2,1,0:T(8,128)(2,1)} %refs_0_.7, bf16[8,64,256]{2,1,0:T(8,128)(2,1)} %refs_1_.8, bf16[256,1024]{1,0:T(8,128)(2,1)} %refs_1_.10, bf16[256,256]{1,0:T(8,128)(2,1)} %refs_3_.3), custom_call_target="tpu_custom_call" | custom-call | flops 268435456 | bytes 1703936 | tf_op jit(solution)/shard_map/pallas_call | solution.py:581
  3.4 6.3 %all-to-all-start = ((bf16[16,128,128]{2,1,0:T(8,128)(2,1)}), bf16[16,128,128]{2,1,0:T(8,128)(2,1)S(1)}, u32[]{:S(2)}, u32[]{:S(2)}) async-start(bf16[16,128,128]{2,1,0:T(8,128)(2,1)} %shard_map.109), calls=%async_computation | async-start | bytes 1048576 | tf_op jit(solution)/shard_map/all_to_all | solution.py:630
  9.7 6.1 %shard_map.110 = (bf16[16,192,128]{2,1,0:T(8,128)(2,1)}, f32[8,64,128]{2,1,0:T(8,128)}, f32[64,128]{1,0:T(8,128)}, f32[64,128]{1,0:T(8,128)}) custom-call(bf16[8,64,256]{2,1,0:T(8,128)(2,1)} %refs_0_.7, bf16[256,1024]{1,0:T(8,128)(2,1)} %refs_1_.10, bf16[64,128,128]{2,1,0:T(8,128)(2,1)} %refs_1_.11, f32[8,128]{1,0:T(8,128)} %bitcast.5), custom_call_target="tpu_custom_call" | custom-call | flops 268435456 | bytes 4001792 | tf_op jit(solution)/shard_map/pallas_call | solution.py:581
  15.8 4.4 %all-to-all-done.refs_1_.refs_5_ = bf16[16,128,128]{2,1,0:T(8,128)(2,1)S(1)} async-done(((bf16[16,128,128]{2,1,0:T(8,128)(2,1)}), bf16[16,128,128]{2,1,0:T(8,128)(2,1)S(1)}, u32[]{:S(2)}, u32[]{:S(2)}) %all-to-all-start) | async-done | bytes 524320 | tf_op jit(solution)/shard_map/all_to_all | solution.py:630
  20.2 3.6 %all-to-all-start.1 = ((bf16[16,192,128]{2,1,0:T(8,128)(2,1)}), bf16[16,192,128]{2,1,0:T(8,128)(2,1)S(1)}, u32[]{:S(2)}, u32[]{:S(2)}) async-start(bf16[16,192,128]{2,1,0:T(8,128)(2,1)} %get-tuple-element.39), calls=%async_computation.1 | async-start | bytes 1572864 | tf_op jit(solution)/shard_map/all_to_all | solution.py:630
  26.7 2.7 %collective-permute-start.1 = (bf16[128,512]{1,0:T(8,128)(2,1)S(1)}, bf16[128,512]{1,0:T(8,128)(2,1)S(1)}, u32[]{:S(2)}, u32[]{:S(2)}) collective-permute-start(bf16[128,512]{1,0:T(8,128)(2,1)S(1)} %shard_map.111), channel_id=1, source_target_pairs={{0,16},{8,24},{16,0},{24,8},{1,17},{9,25},{17,1},{25,9},{2,18},{10... | collective-permute-start | bytes 393224 | tf_op jit(solution)/shard_map/ppermute | solution.py:598
  29.3 6.6 %collective-permute-done.1.refs_3_ = bf16[128,512]{1,0:T(8,128)(2,1)S(1)} collective-permute-done((bf16[128,512]{1,0:T(8,128)(2,1)S(1)}, bf16[128,512]{1,0:T(8,128)(2,1)S(1)}, u32[]{:S(2)}, u32[]{:S(2)}) %collective-permute-start.1) | collective-permute-done | bytes 131104 | tf_op jit(solution)/shard_map/ppermute | solution.py:598
  36.0 4.0 %all-to-all-done.1.refs_1_.refs_5_ = bf16[16,192,128]{2,1,0:T(8,128)(2,1)S(1)} async-done(((bf16[16,192,128]{2,1,0:T(8,128)(2,1)}), bf16[16,192,128]{2,1,0:T(8,128)(2,1)S(1)}, u32[]{:S(2)}, u32[]{:S(2)}) %all-to-all-start.1) | async-done | bytes 786464 | tf_op jit(solution)/shard_map/all_to_all | solution.py:630
  40.0 2.3 %collective-permute-done.2.refs_2_ = bf16[16,192,128]{2,1,0:T(8,128)(2,1)S(1)} collective-permute-done((bf16[16,192,128]{2,1,0:T(8,128)(2,1)S(1)}, bf16[16,192,128]{2,1,0:T(8,128)(2,1)S(1)}, u32[]{:S(2)}, u32[]{:S(2)}) %collective-permute-start.2) | collective-permute-done | bytes 786464 | tf_op jit(solution)/shard_map/ppermute | solution.py:598
  45.2 12.9 %collective-permute-done.3.refs_1_ = f32[128,512]{1,0:T(8,128)S(1)} collective-permute-done((f32[128,512]{1,0:T(8,128)S(1)}, f32[128,512]{1,0:T(8,128)S(1)}, u32[]{:S(2)}, u32[]{:S(2)}) %collective-permute-start.3) | collective-permute-done | bytes 262176 | tf_op jit(solution)/shard_map/ppermute | solution.py:598
  58.5 7.6 %collective-permute-done.7.refs_2_ = bf16[128,512]{1,0:T(8,128)(2,1)S(1)} collective-permute-done((bf16[128,512]{1,0:T(8,128)(2,1)S(1)}, bf16[128,512]{1,0:T(8,128)(2,1)S(1)}, u32[]{:S(2)}, u32[]{:S(2)}) %collective-permute-start.7) | collective-permute-done | bytes 131104 | tf_op jit(solution)/shard_map/ppermute | solution.py:598
  67.5 1.8 %shard_map.117 = bf16[16,128,128]{2,1,0:T(8,128)(2,1)} custom-call(s32[3]{0:T(128)S(1)} %pad_add_fusion.refs_0_, bf16[128,512]{1,0:T(8,128)(2,1)S(1)} %get-tuple-element.44.refs_1_, bf16[128,512]{1,0:T(8,128)(2,1)S(1)} %collective-permute-done.7.refs_2_, bf16[128,512]{1,0:T(8,128)(2,1)S(1)} %collective-permute-done.8.refs_3_, ...), custom_call_target="tpu_custom_call" | custom-call | flops 268435456 | bytes 1572864 | tf_op jit(solution)/shard_map/pallas_call | solution.py:581
  69.3 4.2 %all-to-all-start.2 = ((bf16[16,128,128]{2,1,0:T(8,128)(2,1)}), bf16[16,128,128]{2,1,0:T(8,128)(2,1)}, u32[]{:S(2)}, u32[]{:S(2)}) async-start(bf16[16,128,128]{2,1,0:T(8,128)(2,1)} %shard_map.117), calls=%async_computation.2 | async-start | bytes 1048576 | tf_op jit(solution)/shard_map/all_to_all | solution.py:630
  73.9 8.9 %collective-permute-done.4.refs_2_ = bf16[128,512]{1,0:T(8,128)(2,1)S(1)} collective-permute-done((bf16[128,512]{1,0:T(8,128)(2,1)S(1)}, bf16[128,512]{1,0:T(8,128)(2,1)S(1)}, u32[]{:S(2)}, u32[]{:S(2)}) %collective-permute-start.4) | collective-permute-done | bytes 131104 | tf_op jit(solution)/shard_map/ppermute | solution.py:598
  84.1 1.9 %shard_map.116 = bf16[16,160,128]{2,1,0:T(8,128)(2,1)} custom-call(s32[3]{0:T(128)S(1)} %pad_add_fusion.refs_0_, bf16[128,512]{1,0:T(8,128)(2,1)S(1)} %get-tuple-element.43.refs_1_, bf16[128,512]{1,0:T(8,128)(2,1)S(1)} %collective-permute-done.4.refs_2_, bf16[128,512]{1,0:T(8,128)(2,1)S(1)} %collective-permute-done.5.refs_3_, ...), custom_call_target="tpu_custom_call" | custom-call | flops 268435456 | bytes 1966080 | tf_op jit(solution)/shard_map/pallas_call | solution.py:581
  86.9 4.7 %all-to-all-start.3 = ((bf16[16,160,128]{2,1,0:T(8,128)(2,1)}), bf16[16,160,128]{2,1,0:T(8,128)(2,1)S(1)}, u32[]{:S(2)}, u32[]{:S(2)}) async-start(bf16[16,160,128]{2,1,0:T(8,128)(2,1)} %shard_map.116), calls=%async_computation.3 | async-start | bytes 1310720 | tf_op jit(solution)/shard_map/all_to_all | solution.py:630
  91.7 4.1 %shard_map.118 = (bf16[8,64,256]{2,1,0:T(8,128)(2,1)}, bf16[512,512]{1,0:T(8,128)(2,1)}, bf16[512,256]{1,0:T(8,128)(2,1)}, bf16[256,768]{1,0:T(8,128)(2,1)}) custom-call(bf16[8,64,256]{2,1,0:T(8,128)(2,1)} %refs_0_.7, bf16[8,64,256]{2,1,0:T(8,128)(2,1)} %refs_1_.8, bf16[256,1024]{1,0:T(8,128)(2,1)} %refs_1_.10, bf16[256,256]{1,0:T(8,128)(2,1)} %refs_3_.3, ...), custom_call_target="tpu_custom_call" | custom-call | flops 469762048 | bytes 3145728 | tf_op jit(solution)/shard_map/pallas_call | solution.py:581
  95.8 7.8 %all-to-all-done.3.refs_0_.refs_3_ = bf16[16,160,128]{2,1,0:T(8,128)(2,1)S(1)} async-done(((bf16[16,160,128]{2,1,0:T(8,128)(2,1)}), bf16[16,160,128]{2,1,0:T(8,128)(2,1)S(1)}, u32[]{:S(2)}, u32[]{:S(2)}) %all-to-all-start.3) | async-done | bytes 655392 | tf_op jit(solution)/shard_map/all_to_all | solution.py:630
  109.7 2.5 %collective-permute-start.13 = (bf16[32,1280]{1,0:T(8,128)(2,1)S(1)}, bf16[32,1280]{1,0:T(8,128)(2,1)S(1)}, u32[]{:S(2)}, u32[]{:S(2)}) collective-permute-start(bf16[32,1280]{1,0:T(8,128)(2,1)S(1)} %get-tuple-element.56), channel_id=1, source_target_pairs={{0,6},{1,7},{2,4},{3,5},{4,2},{5,3},{6,0},{7,1},{8,14},{9,15},{10,... | collective-permute-start | bytes 245768 | tf_op jit(solution)/shard_map/ppermute | solution.py:598
  116.1 3.6 %collective-permute-done.14 = bf16[32,1408]{1,0:T(8,128)(2,1)S(1)} collective-permute-done((bf16[32,1408]{1,0:T(8,128)(2,1)S(1)}, bf16[32,1408]{1,0:T(8,128)(2,1)S(1)}, u32[]{:S(2)}, u32[]{:S(2)}) %collective-permute-start.14) | collective-permute-done | bytes 90144 | tf_op jit(solution)/shard_map/ppermute | solution.py:598
  119.7 1.8 %collective-permute-start.15 = (bf16[32,1408]{1,0:T(8,128)(2,1)S(1)}, bf16[32,1408]{1,0:T(8,128)(2,1)S(1)}, u32[]{:S(2)}, u32[]{:S(2)}) collective-permute-start(bf16[32,1408]{1,0:T(8,128)(2,1)S(1)} %add_convert_fusion.1), channel_id=1, source_target_pairs={{0,16},{8,24},{16,0},{24,8},{1,17},{9,25},{17,1},{25,9},{2,18},{10... | collective-permute-start | bytes 270344 | tf_op jit(solution)/shard_map/ppermute | solution.py:598
  121.5 4.3 %shard_map.124 = bf16[64,128,128]{2,1,0:T(8,128)(2,1)} custom-call(bf16[16,160,128]{2,1,0:T(8,128)(2,1)S(1)} %all-to-all-done.3.refs_0_.refs_3_, bf16[64,128,128]{2,1,0:T(8,128)(2,1)S(1)} %copy-done, f32[8,128]{1,0:T(8,128)S(1)} %bitcast.6, f32[8,64,128]{2,1,0:T(8,128)S(1)} %copy-done.5, f32[64,128]{1,0:T(8,128)S(1)} %copy-done.7, f32[64,128]{1,0:T(8,128)S(1)} %copy-done.8), custom_call_target="tpu_custom_call" | custom-call | flops 268435456 | bytes 5181440 | tf_op jit(solution)/shard_map/pallas_call | solution.py:581
  126.2 2.6 %collective-permute-start.21 = (bf16[32,1408]{1,0:T(8,128)(2,1)S(1)}, bf16[32,1408]{1,0:T(8,128)(2,1)S(1)}, u32[]{:S(2)}, u32[]{:S(2)}) collective-permute-start(bf16[32,1408]{1,0:T(8,128)(2,1)S(1)} %add_convert_fusion.refs_1_), channel_id=1, source_target_pairs={{0,6},{1,7},{2,4},{3,5},{4,2},{5,3},{6,0},{7,1},{8,14},{9,15},{10,... | collective-permute-start | bytes 270344 | tf_op jit(solution)/shard_map/ppermute | solution.py:598
  129.7 1.9 %collective-permute-done.21.refs_7_ = bf16[32,1408]{1,0:T(8,128)(2,1)S(1)} collective-permute-done((bf16[32,1408]{1,0:T(8,128)(2,1)S(1)}, bf16[32,1408]{1,0:T(8,128)(2,1)S(1)}, u32[]{:S(2)}, u32[]{:S(2)}) %collective-permute-start.21) | collective-permute-done | bytes 90144 | tf_op jit(solution)/shard_map/ppermute | solution.py:598
  (70 shorter events, 26.6 us)
Async XLA Ops:
  3.4 16.9 %all-to-all-start = ((bf16[16,128,128]{2,1,0:T(8,128)(2,1)}), bf16[16,128,128]{2,1,0:T(8,128)(2,1)S(1)}, u32[]{:S(2)}, u32[]{:S(2)}) async-start(bf16[16,128,128]{2,1,0:T(8,128)(2,1)} %shard_map.109), calls=%async_computation | async-start | bytes 1048576 | tf_op jit(solution)/shard_map/all_to_all | solution.py:630
  20.2 19.8 %all-to-all-start.1 = ((bf16[16,192,128]{2,1,0:T(8,128)(2,1)}), bf16[16,192,128]{2,1,0:T(8,128)(2,1)S(1)}, u32[]{:S(2)}, u32[]{:S(2)}) async-start(bf16[16,192,128]{2,1,0:T(8,128)(2,1)} %get-tuple-element.39), calls=%async_computation.1 | async-start | bytes 1572864 | tf_op jit(solution)/shard_map/all_to_all | solution.py:630
  23.8 2.0 %collective-permute-start = (bf16[16,128,128]{2,1,0:T(8,128)(2,1)S(1)}, bf16[16,128,128]{2,1,0:T(8,128)(2,1)S(1)}, u32[]{:S(2)}, u32[]{:S(2)}) collective-permute-start(bf16[16,128,128]{2,1,0:T(8,128)(2,1)S(1)} %all-to-all-done.refs_1_.refs_5_), channel_id=1, source_target_pairs={{0,1},{1,0},{2,3},{3,2},{4,5},{5,4},{6,7},{7,6},{8,9},{9,8},{10,11... | collective-permute-start | bytes 1572872 | tf_op jit(solution)/shard_map/ppermute | solution.py:598
  26.7 9.3 %collective-permute-start.1 = (bf16[128,512]{1,0:T(8,128)(2,1)S(1)}, bf16[128,512]{1,0:T(8,128)(2,1)S(1)}, u32[]{:S(2)}, u32[]{:S(2)}) collective-permute-start(bf16[128,512]{1,0:T(8,128)(2,1)S(1)} %shard_map.111), channel_id=1, source_target_pairs={{0,16},{8,24},{16,0},{24,8},{1,17},{9,25},{17,1},{25,9},{2,18},{10... | collective-permute-start | bytes 393224 | tf_op jit(solution)/shard_map/ppermute | solution.py:598
  40.0 2.3 %collective-permute-start.2 = (bf16[16,192,128]{2,1,0:T(8,128)(2,1)S(1)}, bf16[16,192,128]{2,1,0:T(8,128)(2,1)S(1)}, u32[]{:S(2)}, u32[]{:S(2)}) collective-permute-start(bf16[16,192,128]{2,1,0:T(8,128)(2,1)S(1)} %all-to-all-done.1.refs_1_.refs_5_), channel_id=1, source_target_pairs={{0,1},{1,0},{2,3},{3,2},{4,5},{5,4},{6,7},{7,6},{8,9},{9,8},{10,11... | collective-permute-start | bytes 2359304 | tf_op jit(solution)/shard_map/ppermute | solution.py:598
  43.1 14.9 %collective-permute-start.3 = (f32[128,512]{1,0:T(8,128)S(1)}, f32[128,512]{1,0:T(8,128)S(1)}, u32[]{:S(2)}, u32[]{:S(2)}) collective-permute-start(f32[128,512]{1,0:T(8,128)S(1)} %shard_map.113), channel_id=1, source_target_pairs={{0,16},{8,24},{16,0},{24,8},{1,17},{9,25},{17,1},{25,9},{2,18},{10... | collective-permute-start | bytes 786440 | tf_op jit(solution)/shard_map/ppermute | solution.py:598
  58.4 7.8 %collective-permute-start.7 = (bf16[128,512]{1,0:T(8,128)(2,1)S(1)}, bf16[128,512]{1,0:T(8,128)(2,1)S(1)}, u32[]{:S(2)}, u32[]{:S(2)}) collective-permute-start(bf16[128,512]{1,0:T(8,128)(2,1)S(1)} %get-tuple-element.44.refs_1_), channel_id=1, source_target_pairs={{0,16},{8,24},{16,0},{24,8},{1,17},{9,25},{17,1},{25,9},{2,18},{10... | collective-permute-start | bytes 393224 | tf_op jit(solution)/shard_map/ppermute | solution.py:598
  58.4 7.7 %collective-permute-start.8 = (bf16[128,512]{1,0:T(8,128)(2,1)S(1)}, bf16[128,512]{1,0:T(8,128)(2,1)S(1)}, u32[]{:S(2)}, u32[]{:S(2)}) collective-permute-start(bf16[128,512]{1,0:T(8,128)(2,1)S(1)} %get-tuple-element.44.refs_1_), channel_id=1, source_target_pairs={{0,1},{1,0},{2,3},{3,2},{4,5},{5,4},{6,7},{7,6},{8,9},{9,8},{10,11... | collective-permute-start | bytes 393224 | tf_op jit(solution)/shard_map/ppermute | solution.py:598
  66.1 1.3 collective-permute-start.9
  69.3 17.6 %all-to-all-start.2 = ((bf16[16,128,128]{2,1,0:T(8,128)(2,1)}), bf16[16,128,128]{2,1,0:T(8,128)(2,1)}, u32[]{:S(2)}, u32[]{:S(2)}) async-start(bf16[16,128,128]{2,1,0:T(8,128)(2,1)} %shard_map.117), calls=%async_computation.2 | async-start | bytes 1048576 | tf_op jit(solution)/shard_map/all_to_all | solution.py:630
  73.6 9.2 %collective-permute-start.4 = (bf16[128,512]{1,0:T(8,128)(2,1)S(1)}, bf16[128,512]{1,0:T(8,128)(2,1)S(1)}, u32[]{:S(2)}, u32[]{:S(2)}) collective-permute-start(bf16[128,512]{1,0:T(8,128)(2,1)S(1)} %get-tuple-element.43.refs_1_), channel_id=1, source_target_pairs={{0,16},{8,24},{16,0},{24,8},{1,17},{9,25},{17,1},{25,9},{2,18},{10... | collective-permute-start | bytes 393224 | tf_op jit(solution)/shard_map/ppermute | solution.py:598
  73.8 9.0 %collective-permute-start.5 = (bf16[128,512]{1,0:T(8,128)(2,1)S(1)}, bf16[128,512]{1,0:T(8,128)(2,1)S(1)}, u32[]{:S(2)}, u32[]{:S(2)}) collective-permute-start(bf16[128,512]{1,0:T(8,128)(2,1)S(1)} %get-tuple-element.43.refs_1_), channel_id=1, source_target_pairs={{0,1},{1,0},{2,3},{3,2},{4,5},{5,4},{6,7},{7,6},{8,9},{9,8},{10,11... | collective-permute-start | bytes 393224 | tf_op jit(solution)/shard_map/ppermute | solution.py:598
  86.9 16.7 %all-to-all-start.3 = ((bf16[16,160,128]{2,1,0:T(8,128)(2,1)}), bf16[16,160,128]{2,1,0:T(8,128)(2,1)S(1)}, u32[]{:S(2)}, u32[]{:S(2)}) async-start(bf16[16,160,128]{2,1,0:T(8,128)(2,1)} %shard_map.116), calls=%async_computation.3 | async-start | bytes 1310720 | tf_op jit(solution)/shard_map/all_to_all | solution.py:630
  106.3 1.7 %collective-permute-start.10 = (bf16[4,32,1280]{2,1,0:T(8,128)(2,1)S(1)}, bf16[4,32,1280]{2,1,0:T(8,128)(2,1)S(1)}, u32[]{:S(2)}, u32[]{:S(2)}) collective-permute-start(bf16[4,32,1280]{2,1,0:T(8,128)(2,1)S(1)} %get-tuple-element.53), channel_id=1, source_target_pairs={{0,1},{1,0},{2,3},{3,2},{4,5},{5,4},{6,7},{7,6},{8,9},{9,8},{10,11... | collective-permute-start | bytes 983048 | tf_op jit(solution)/shard_map/ppermute | solution.py:598
  108.6 5.1 %collective-permute-start.11 = (bf16[32,1280]{1,0:T(8,128)(2,1)S(1)}, bf16[32,1280]{1,0:T(8,128)(2,1)S(1)}, u32[]{:S(2)}, u32[]{:S(2)}) collective-permute-start(bf16[32,1280]{1,0:T(8,128)(2,1)S(1)} %get-tuple-element.54), channel_id=1, source_target_pairs={{0,2},{1,3},{2,0},{3,1},{4,6},{5,7},{6,4},{7,5},{8,10},{9,11},{10,... | collective-permute-start | bytes 245768 | tf_op jit(solution)/shard_map/ppermute | solution.py:598
  108.7 5.4 %collective-permute-start.12 = (bf16[32,1280]{1,0:T(8,128)(2,1)S(1)}, bf16[32,1280]{1,0:T(8,128)(2,1)S(1)}, u32[]{:S(2)}, u32[]{:S(2)}) collective-permute-start(bf16[32,1280]{1,0:T(8,128)(2,1)S(1)} %get-tuple-element.55), channel_id=1, source_target_pairs={{0,4},{1,5},{2,6},{3,7},{4,0},{5,1},{6,2},{7,3},{8,12},{9,13},{10,... | collective-permute-start | bytes 245768 | tf_op jit(solution)/shard_map/ppermute | solution.py:598
  109.7 5.3 %collective-permute-start.13 = (bf16[32,1280]{1,0:T(8,128)(2,1)S(1)}, bf16[32,1280]{1,0:T(8,128)(2,1)S(1)}, u32[]{:S(2)}, u32[]{:S(2)}) collective-permute-start(bf16[32,1280]{1,0:T(8,128)(2,1)S(1)} %get-tuple-element.56), channel_id=1, source_target_pairs={{0,6},{1,7},{2,4},{3,5},{4,2},{5,3},{6,0},{7,1},{8,14},{9,15},{10,... | collective-permute-start | bytes 245768 | tf_op jit(solution)/shard_map/ppermute | solution.py:598
  115.1 4.6 %collective-permute-start.14 = (bf16[32,1408]{1,0:T(8,128)(2,1)S(1)}, bf16[32,1408]{1,0:T(8,128)(2,1)S(1)}, u32[]{:S(2)}, u32[]{:S(2)}) collective-permute-start(bf16[32,1408]{1,0:T(8,128)(2,1)S(1)} %shard_map.123), channel_id=1, source_target_pairs={{0,8},{8,0},{16,24},{24,16},{1,9},{9,1},{17,25},{25,17},{2,10},{10... | collective-permute-start | bytes 270344 | tf_op jit(solution)/shard_map/ppermute | solution.py:598
  119.7 6.5 %collective-permute-start.15 = (bf16[32,1408]{1,0:T(8,128)(2,1)S(1)}, bf16[32,1408]{1,0:T(8,128)(2,1)S(1)}, u32[]{:S(2)}, u32[]{:S(2)}) collective-permute-start(bf16[32,1408]{1,0:T(8,128)(2,1)S(1)} %add_convert_fusion.1), channel_id=1, source_target_pairs={{0,16},{8,24},{16,0},{24,8},{1,17},{9,25},{17,1},{25,9},{2,18},{10... | collective-permute-start | bytes 270344 | tf_op jit(solution)/shard_map/ppermute | solution.py:598
  126.2 5.5 %collective-permute-start.21 = (bf16[32,1408]{1,0:T(8,128)(2,1)S(1)}, bf16[32,1408]{1,0:T(8,128)(2,1)S(1)}, u32[]{:S(2)}, u32[]{:S(2)}) collective-permute-start(bf16[32,1408]{1,0:T(8,128)(2,1)S(1)} %add_convert_fusion.refs_1_), channel_id=1, source_target_pairs={{0,6},{1,7},{2,4},{3,5},{4,2},{5,3},{6,0},{7,1},{8,14},{9,15},{10,... | collective-permute-start | bytes 270344 | tf_op jit(solution)/shard_map/ppermute | solution.py:598
  128.8 4.5 %collective-permute-start.19 = (bf16[32,1408]{1,0:T(8,128)(2,1)S(1)}, bf16[32,1408]{1,0:T(8,128)(2,1)S(1)}, u32[]{:S(2)}, u32[]{:S(2)}) collective-permute-start(bf16[32,1408]{1,0:T(8,128)(2,1)S(1)} %add_convert_fusion.refs_1_), channel_id=1, source_target_pairs={{0,4},{1,5},{2,6},{3,7},{4,0},{5,1},{6,2},{7,3},{8,12},{9,13},{10,... | collective-permute-start | bytes 270344 | tf_op jit(solution)/shard_map/ppermute | solution.py:598
  129.4 4.5 %collective-permute-start.17 = (bf16[32,1408]{1,0:T(8,128)(2,1)S(1)}, bf16[32,1408]{1,0:T(8,128)(2,1)S(1)}, u32[]{:S(2)}, u32[]{:S(2)}) collective-permute-start(bf16[32,1408]{1,0:T(8,128)(2,1)S(1)} %add_convert_fusion.refs_1_), channel_id=1, source_target_pairs={{0,2},{1,3},{2,0},{3,1},{4,6},{5,7},{6,4},{7,5},{8,10},{9,11},{10,... | collective-permute-start | bytes 270344 | tf_op jit(solution)/shard_map/ppermute | solution.py:598
  129.7 4.2 %collective-permute-start.16 = (bf16[32,1408]{1,0:T(8,128)(2,1)S(1)}, bf16[32,1408]{1,0:T(8,128)(2,1)S(1)}, u32[]{:S(2)}, u32[]{:S(2)}) collective-permute-start(bf16[32,1408]{1,0:T(8,128)(2,1)S(1)} %add_convert_fusion.refs_1_), channel_id=1, source_target_pairs={{0,1},{1,0},{2,3},{3,2},{4,5},{5,4},{6,7},{7,6},{8,9},{9,8},{10,11... | collective-permute-start | bytes 270344 | tf_op jit(solution)/shard_map/ppermute | solution.py:598
  131.7 2.2 %collective-permute-start.22 = (bf16[32,1408]{1,0:T(8,128)(2,1)S(1)}, bf16[32,1408]{1,0:T(8,128)(2,1)S(1)}, u32[]{:S(2)}, u32[]{:S(2)}) collective-permute-start(bf16[32,1408]{1,0:T(8,128)(2,1)S(1)} %collective-permute-done.21.refs_7_), channel_id=1, source_target_pairs={{0,1},{1,0},{2,3},{3,2},{4,5},{5,4},{6,7},{7,6},{8,9},{9,8},{10,11... | collective-permute-start | bytes 270344 | tf_op jit(solution)/shard_map/ppermute | solution.py:598
  (13 other events, 169.0 us)

commit v24 on v20

--- a/solution.py
+++ b/solution.py
@@ -292,7 +292,7 @@
 
 
 def score_kernel(
-    residues, left_row, right_row, with_bias, place_ref, own_ref, other_ref, mine_ref, sent_ref
+    residues, left_row, right_row, sent, place_ref, own_ref, other_ref, out_ref
 ):
     core, half = place_ref[0], place_ref[1]
     count = own_ref.shape[0] // 2
@@ -300,31 +300,30 @@
     right = jnp.concatenate(
         [lanes_of(own_ref, right_row, residues), lanes_of(other_ref, right_row, residues)], axis=1
     )
-    for which, ref in ((half, mine_ref), (1 - half, sent_ref)):
-        left = []
+    which = 1 - half if sent else half
+    left = []
+    for k in range(count // 2):
+        block = which * (count // 2) + k
+        rows = pl.ds(pl.multiple_of(left_row + core * part, part), part)
+        left.append(
+            jnp.concatenate(
+                [
+                    r[p * count + block, rows, :]
+                    for r in (own_ref, other_ref)
+                    for p in range(2)
+                ],
+                axis=1,
+            )
+        )
+    out_ref[...] = f32_dot(jnp.concatenate(left, axis=0), right, NT)
+    for p in range(2):
+        columns = pl.ds(pl.multiple_of((half * 2 + p) * LANES, LANES), LANES)
         for k in range(count // 2):
-            block = which * (count // 2) + k
-            rows = pl.ds(pl.multiple_of(left_row + core * part, part), part)
-            left.append(
-                jnp.concatenate(
-                    [
-                        r[p * count + block, rows, :]
-                        for r in (own_ref, other_ref)
-                        for p in range(2)
-                    ],
-                    axis=1,
-                )
-            )
-        ref[...] = f32_dot(jnp.concatenate(left, axis=0), right, NT).astype(ref.dtype)
-        if with_bias:
-            for p in range(2):
-                columns = pl.ds(pl.multiple_of((half * 2 + p) * LANES, LANES), LANES)
-                for k in range(count // 2):
-                    block = p * count + which * (count // 2) + k
-                    high = own_ref[block, 2 * residues : 2 * residues + part, :]
-                    low = own_ref[block, 2 * residues + part : 3 * residues, :]
-                    bias = high.astype(jnp.float32) + low.astype(jnp.float32)
-                    ref[k * part : (k + 1) * part, columns] += bias
+            block = p * count + which * (count // 2) + k
+            high = own_ref[block, 2 * residues : 2 * residues + part, :]
+            low = own_ref[block, 2 * residues + part : 3 * residues, :]
+            bias = high.astype(jnp.float32) + low.astype(jnp.float32)
+            out_ref[k * part : (k + 1) * part, columns] += bias
 
 
 def softmax_kernel(logit_ref, other_ref, out_ref, low_ref):
@@ -690,12 +689,16 @@
     )
     grad_other = swapped(grad_sent, "seq", seq_half)
     query_blocks, grad_other = lax.optimization_barrier((query_blocks, grad_other))
-    logit_mine, logit_sent = call(
-        functools.partial(score_kernel, residues, 0, residues, True),
-        [(quarter, f32), (quarter, f32)],
-        query_blocks, swapped(query_blocks, "res", 1),
-        place=place, flops=2 * total * total * width,
-    )
+    query_other = swapped(query_blocks, "res", 1)
+
+    def scores(sent):
+        return call(
+            functools.partial(score_kernel, residues, 0, residues, sent), [(quarter, f32)],
+            query_blocks, query_other,
+            place=place, flops=total * total * width,
+        )[0]
+
+    logit_sent, logit_mine = scores(True), scores(False)
     softmax_out, probs = call(
         softmax_kernel, [(quarter, f32), (quarter, bf16)],
         logit_mine, swapped(logit_sent, "seq", seq_half),
@@ -783,7 +786,8 @@
     other_half = swapped(part, "seq", seq_half)
     other_half, pair_gradient = lax.optimization_barrier((other_half, pair_gradient))
     part = added(part, other_half)
-    chips = [part] + [swapped(part, "res", 2 * flip) for flip in range(1, res_size // 2)]
+    beside = swapped(part, "res", 2)
+    chips = [part, beside, swapped(part, "res", 4), swapped(beside, "res", 4)]
     parts = [t for chip in chips for t in (chip, swapped(chip, "res", 1))]
     combined_gradient, output_gradient, pair_weight_gradient = call(
         output_kernel,

time: 136 us -> 137 us (level)
  starting transfers between devices: 31.1 us -> 33.4 us
  waiting for transfers between devices: 73.1 us -> 71.1 us
    ppermute x22, starting transfers between devices: 13.4 us -> 15.7 us  [swapped(): lax.ppermute(mine, axis_name, [(a, a ^ distance) for a in range(size)])]
    ppermute x22, waiting for transfers between devices: 50.6 us -> 48.7 us  [swapped(): lax.ppermute(mine, axis_name, [(a, a ^ distance) for a in range(size)])]
    pallas_call x16 -> x17, Pallas kernels: 29.9 us -> 30.6 us  [call(): pl.pallas_call(wrapped, out_shape=shapes, in_specs=[pl.BlockSpec(memory_s...]
  transfers between devices with their start and end apart: 26 -> 26, of which waited for: 22 -> 21; matrix products, arithmetic and copies ran while one was open for 0% -> 0% of each run, Pallas kernels for 14% -> 15%
where the time goes in v24:
time: 137 us; the launch traced here: 136 us
  waiting for transfers between devices  71.1 us (52%)
  starting transfers between devices  33.4 us (24%)
  Pallas kernels  30.6 us (22%)
    ppermute x22, waiting for transfers between devices, swapped(): lax.ppermute(mine, axis_name, [(a, a ^ distance) for a in range(size)])  48.7 us
    pallas_call x17, Pallas kernels, call(): pl.pallas_call(wrapped, out_shape=shapes, in_specs=[pl.BlockSpec(memory_s...  30.6 us
    all_to_all x4, waiting for transfers between devices, across(): lax.all_to_all(blocks, ('seq', 'res'), 0, 0, axis_index_groups=groups, ti...  22.5 us
    all_to_all x4, starting transfers between devices, across(): lax.all_to_all(blocks, ('seq', 'res'), 0, 0, axis_index_groups=groups, ti...  17.7 us
    ppermute x22, starting transfers between devices, swapped(): lax.ppermute(mine, axis_name, [(a, a ^ distance) for a in range(size)])  15.7 us
  transfers between devices with their start and end apart: 26, of which 21 were waited for; matrix products, arithmetic and copies ran while one was open for 0% of the time, Pallas kernels for 15%

profile of v24, /device:TPU:0, one launch (start us, length us, event | category | flops | bytes accessed | tf_op | source)
XLA Modules:
  0.0 136.3 jit_solution(11111132540544564214)
XLA Ops:
  0.6 2.7 %shard_map.109 = bf16[16,128,128]{2,1,0:T(8,128)(2,1)} custom-call(bf16[8,64,256]{2,1,0:T(8,128)(2,1)} %refs_0_.7, bf16[8,64,256]{2,1,0:T(8,128)(2,1)} %refs_1_.8, bf16[256,1024]{1,0:T(8,128)(2,1)} %refs_1_.10, bf16[256,256]{1,0:T(8,128)(2,1)} %refs_3_.3), custom_call_target="tpu_custom_call" | custom-call | flops 268435456 | bytes 1703936 | tf_op jit(solution)/shard_map/pallas_call | solution.py:612
  3.4 6.3 %all-to-all-start = ((bf16[16,128,128]{2,1,0:T(8,128)(2,1)}), bf16[16,128,128]{2,1,0:T(8,128)(2,1)S(1)}, u32[]{:S(2)}, u32[]{:S(2)}) async-start(bf16[16,128,128]{2,1,0:T(8,128)(2,1)} %shard_map.109), calls=%async_computation | async-start | bytes 1048576 | tf_op jit(solution)/shard_map/all_to_all | solution.py:661
  9.7 6.1 %shard_map.110 = (bf16[16,192,128]{2,1,0:T(8,128)(2,1)}, f32[8,64,128]{2,1,0:T(8,128)}, f32[64,128]{1,0:T(8,128)}, f32[64,128]{1,0:T(8,128)}) custom-call(bf16[8,64,256]{2,1,0:T(8,128)(2,1)} %refs_0_.7, bf16[256,1024]{1,0:T(8,128)(2,1)} %refs_1_.10, bf16[64,128,128]{2,1,0:T(8,128)(2,1)} %refs_1_.11, f32[8,128]{1,0:T(8,128)} %bitcast.5), custom_call_target="tpu_custom_call" | custom-call | flops 268435456 | bytes 4001792 | tf_op jit(solution)/shard_map/pallas_call | solution.py:612
  15.8 4.4 %all-to-all-done.refs_1_.refs_5_ = bf16[16,128,128]{2,1,0:T(8,128)(2,1)S(1)} async-done(((bf16[16,128,128]{2,1,0:T(8,128)(2,1)}), bf16[16,128,128]{2,1,0:T(8,128)(2,1)S(1)}, u32[]{:S(2)}, u32[]{:S(2)}) %all-to-all-start) | async-done | bytes 524320 | tf_op jit(solution)/shard_map/all_to_all | solution.py:661
  20.2 3.6 %all-to-all-start.1 = ((bf16[16,192,128]{2,1,0:T(8,128)(2,1)}), bf16[16,192,128]{2,1,0:T(8,128)(2,1)S(1)}, u32[]{:S(2)}, u32[]{:S(2)}) async-start(bf16[16,192,128]{2,1,0:T(8,128)(2,1)} %get-tuple-element.44), calls=%async_computation.1 | async-start | bytes 1572864 | tf_op jit(solution)/shard_map/all_to_all | solution.py:661
  26.7 2.7 %collective-permute-start.1 = (bf16[256,512]{1,0:T(8,128)(2,1)S(1)}, bf16[256,512]{1,0:T(8,128)(2,1)S(1)}, u32[]{:S(2)}, u32[]{:S(2)}) collective-permute-start(bf16[256,512]{1,0:T(8,128)(2,1)S(1)} %get-tuple-element.46), channel_id=1, source_target_pairs={{0,16},{8,24},{16,0},{24,8},{1,17},{9,25},{17,1},{25,9},{2,18},{10... | collective-permute-start | bytes 786440 | tf_op jit(solution)/shard_map/ppermute | solution.py:629
  29.4 9.5 %collective-permute-done.1.refs_4_ = bf16[256,512]{1,0:T(8,128)(2,1)S(1)} collective-permute-done((bf16[256,512]{1,0:T(8,128)(2,1)S(1)}, bf16[256,512]{1,0:T(8,128)(2,1)S(1)}, u32[]{:S(2)}, u32[]{:S(2)}) %collective-permute-start.1) | collective-permute-done | bytes 262176 | tf_op jit(solution)/shard_map/ppermute | solution.py:629
  38.8 4.0 %all-to-all-done.1.refs_1_.refs_5_ = bf16[16,192,128]{2,1,0:T(8,128)(2,1)S(1)} async-done(((bf16[16,192,128]{2,1,0:T(8,128)(2,1)}), bf16[16,192,128]{2,1,0:T(8,128)(2,1)S(1)}, u32[]{:S(2)}, u32[]{:S(2)}) %all-to-all-start.1) | async-done | bytes 786464 | tf_op jit(solution)/shard_map/all_to_all | solution.py:661
  42.8 2.3 %collective-permute-done.2.refs_2_ = bf16[16,192,128]{2,1,0:T(8,128)(2,1)S(1)} collective-permute-done((bf16[16,192,128]{2,1,0:T(8,128)(2,1)S(1)}, bf16[16,192,128]{2,1,0:T(8,128)(2,1)S(1)}, u32[]{:S(2)}, u32[]{:S(2)}) %collective-permute-start.2) | collective-permute-done | bytes 786464 | tf_op jit(solution)/shard_map/ppermute | solution.py:629
  46.9 14.0 %collective-permute-done.3.refs_1_ = f32[128,512]{1,0:T(8,128)S(1)} collective-permute-done((f32[128,512]{1,0:T(8,128)S(1)}, f32[128,512]{1,0:T(8,128)S(1)}, u32[]{:S(2)}, u32[]{:S(2)}) %collective-permute-start.3) | collective-permute-done | bytes 262176 | tf_op jit(solution)/shard_map/ppermute | solution.py:629
  61.2 7.6 %collective-permute-done.4.refs_2_ = bf16[128,512]{1,0:T(8,128)(2,1)S(1)} collective-permute-done((bf16[128,512]{1,0:T(8,128)(2,1)S(1)}, bf16[128,512]{1,0:T(8,128)(2,1)S(1)}, u32[]{:S(2)}, u32[]{:S(2)}) %collective-permute-start.4) | collective-permute-done | bytes 131104 | tf_op jit(solution)/shard_map/ppermute | solution.py:629
  70.2 1.8 %shard_map.115 = bf16[16,128,128]{2,1,0:T(8,128)(2,1)} custom-call(s32[3]{0:T(128)S(1)} %pad_add_fusion.refs_0_, bf16[128,512]{1,0:T(8,128)(2,1)S(1)} %get-tuple-element.48.refs_1_, bf16[128,512]{1,0:T(8,128)(2,1)S(1)} %collective-permute-done.4.refs_2_, bf16[128,512]{1,0:T(8,128)(2,1)S(1)} %collective-permute-done.5.refs_3_, ...), custom_call_target="tpu_custom_call" | custom-call | flops 268435456 | bytes 1572864 | tf_op jit(solution)/shard_map/pallas_call | solution.py:612
  72.0 4.2 %all-to-all-start.2 = ((bf16[16,128,128]{2,1,0:T(8,128)(2,1)}), bf16[16,128,128]{2,1,0:T(8,128)(2,1)}, u32[]{:S(2)}, u32[]{:S(2)}) async-start(bf16[16,128,128]{2,1,0:T(8,128)(2,1)} %shard_map.115), calls=%async_computation.2 | async-start | bytes 1048576 | tf_op jit(solution)/shard_map/all_to_all | solution.py:661
  78.6 1.9 %shard_map.117 = bf16[16,160,128]{2,1,0:T(8,128)(2,1)} custom-call(s32[3]{0:T(128)S(1)} %pad_add_fusion.refs_0_, bf16[128,512]{1,0:T(8,128)(2,1)S(1)} %get-tuple-element.53.refs_1_, bf16[128,512]{1,0:T(8,128)(2,1)S(1)} %get-tuple-element.54.refs_2_, bf16[128,512]{1,0:T(8,128)(2,1)S(1)} %collective-permute-done.7.refs_3_, ...), custom_call_target="tpu_custom_call" | custom-call | flops 268435456 | bytes 1966080 | tf_op jit(solution)/shard_map/pallas_call | solution.py:612
  80.5 6.3 %all-to-all-done.2.refs_4_ = bf16[16,128,128]{2,1,0:T(8,128)(2,1)} async-done(((bf16[16,128,128]{2,1,0:T(8,128)(2,1)}), bf16[16,128,128]{2,1,0:T(8,128)(2,1)}, u32[]{:S(2)}, u32[]{:S(2)}) %all-to-all-start.2) | async-done | bytes 524320 | tf_op jit(solution)/shard_map/all_to_all | solution.py:661
  86.8 3.6 %all-to-all-start.3 = ((bf16[16,160,128]{2,1,0:T(8,128)(2,1)}), bf16[16,160,128]{2,1,0:T(8,128)(2,1)S(1)}, u32[]{:S(2)}, u32[]{:S(2)}) async-start(bf16[16,160,128]{2,1,0:T(8,128)(2,1)} %shard_map.117), calls=%async_computation.3 | async-start | bytes 1310720 | tf_op jit(solution)/shard_map/all_to_all | solution.py:661
  90.4 4.1 %shard_map.118 = (bf16[8,64,256]{2,1,0:T(8,128)(2,1)}, bf16[512,512]{1,0:T(8,128)(2,1)}, bf16[512,256]{1,0:T(8,128)(2,1)}, bf16[256,768]{1,0:T(8,128)(2,1)}) custom-call(bf16[8,64,256]{2,1,0:T(8,128)(2,1)} %refs_0_.7, bf16[8,64,256]{2,1,0:T(8,128)(2,1)} %refs_1_.8, bf16[256,1024]{1,0:T(8,128)(2,1)} %refs_1_.10, bf16[256,256]{1,0:T(8,128)(2,1)} %refs_3_.3, ...), custom_call_target="tpu_custom_call" | custom-call | flops 469762048 | bytes 3145728 | tf_op jit(solution)/shard_map/pallas_call | solution.py:612
  94.5 7.8 %all-to-all-done.3.refs_0_.refs_3_ = bf16[16,160,128]{2,1,0:T(8,128)(2,1)S(1)} async-done(((bf16[16,160,128]{2,1,0:T(8,128)(2,1)}), bf16[16,160,128]{2,1,0:T(8,128)(2,1)S(1)}, u32[]{:S(2)}, u32[]{:S(2)}) %all-to-all-start.3) | async-done | bytes 655392 | tf_op jit(solution)/shard_map/all_to_all | solution.py:661
  108.4 2.5 %collective-permute-start.12 = (bf16[32,1280]{1,0:T(8,128)(2,1)S(1)}, bf16[32,1280]{1,0:T(8,128)(2,1)S(1)}, u32[]{:S(2)}, u32[]{:S(2)}) collective-permute-start(bf16[32,1280]{1,0:T(8,128)(2,1)S(1)} %get-tuple-element.66), channel_id=1, source_target_pairs={{0,6},{1,7},{2,4},{3,5},{4,2},{5,3},{6,0},{7,1},{8,14},{9,15},{10,... | collective-permute-start | bytes 245768 | tf_op jit(solution)/shard_map/ppermute | solution.py:629
  114.8 3.5 %collective-permute-done.13 = bf16[32,1408]{1,0:T(8,128)(2,1)S(1)} collective-permute-done((bf16[32,1408]{1,0:T(8,128)(2,1)S(1)}, bf16[32,1408]{1,0:T(8,128)(2,1)S(1)}, u32[]{:S(2)}, u32[]{:S(2)}) %collective-permute-start.13) | collective-permute-done | bytes 90144 | tf_op jit(solution)/shard_map/ppermute | solution.py:629
  118.7 4.3 %shard_map.124 = bf16[64,128,128]{2,1,0:T(8,128)(2,1)} custom-call(bf16[16,160,128]{2,1,0:T(8,128)(2,1)S(1)} %all-to-all-done.3.refs_0_.refs_3_, bf16[64,128,128]{2,1,0:T(8,128)(2,1)S(1)} %copy-done, f32[8,128]{1,0:T(8,128)S(1)} %bitcast.6, f32[8,64,128]{2,1,0:T(8,128)S(1)} %copy-done.5, f32[64,128]{1,0:T(8,128)S(1)} %copy-done.7, f32[64,128]{1,0:T(8,128)S(1)} %copy-done.8), custom_call_target="tpu_custom_call" | custom-call | flops 268435456 | bytes 5181440 | tf_op jit(solution)/shard_map/pallas_call | solution.py:612
  125.7 2.3 %collective-permute-start.18 = (bf16[32,1408]{1,0:T(8,128)(2,1)S(1)}, bf16[32,1408]{1,0:T(8,128)(2,1)S(1)}, u32[]{:S(2)}, u32[]{:S(2)}) collective-permute-start(bf16[32,1408]{1,0:T(8,128)(2,1)S(1)} %add_convert_fusion.refs_1_), channel_id=1, source_target_pairs={{0,4},{1,5},{2,6},{3,7},{4,0},{5,1},{6,2},{7,3},{8,12},{9,13},{10,... | collective-permute-start | bytes 270344 | tf_op jit(solution)/shard_map/ppermute | solution.py:629
  128.5 2.3 %collective-permute-start.20 = (bf16[32,1408]{1,0:T(8,128)(2,1)S(1)}, bf16[32,1408]{1,0:T(8,128)(2,1)S(1)}, u32[]{:S(2)}, u32[]{:S(2)}) collective-permute-start(bf16[32,1408]{1,0:T(8,128)(2,1)S(1)} %collective-permute-done.16.refs_3_), channel_id=1, source_target_pairs={{0,4},{1,5},{2,6},{3,7},{4,0},{5,1},{6,2},{7,3},{8,12},{9,13},{10,... | collective-permute-start | bytes 270344 | tf_op jit(solution)/shard_map/ppermute | solution.py:629
  131.4 2.0 %collective-permute-done.20.refs_7_ = bf16[32,1408]{1,0:T(8,128)(2,1)S(1)} collective-permute-done((bf16[32,1408]{1,0:T(8,128)(2,1)S(1)}, bf16[32,1408]{1,0:T(8,128)(2,1)S(1)}, u32[]{:S(2)}, u32[]{:S(2)}) %collective-permute-start.20) | collective-permute-done | bytes 90144 | tf_op jit(solution)/shard_map/ppermute | solution.py:629
  (68 shorter events, 25.5 us)
Async XLA Ops:
  3.4 16.9 %all-to-all-start = ((bf16[16,128,128]{2,1,0:T(8,128)(2,1)}), bf16[16,128,128]{2,1,0:T(8,128)(2,1)S(1)}, u32[]{:S(2)}, u32[]{:S(2)}) async-start(bf16[16,128,128]{2,1,0:T(8,128)(2,1)} %shard_map.109), calls=%async_computation | async-start | bytes 1048576 | tf_op jit(solution)/shard_map/all_to_all | solution.py:661
  20.2 22.6 %all-to-all-start.1 = ((bf16[16,192,128]{2,1,0:T(8,128)(2,1)}), bf16[16,192,128]{2,1,0:T(8,128)(2,1)S(1)}, u32[]{:S(2)}, u32[]{:S(2)}) async-start(bf16[16,192,128]{2,1,0:T(8,128)(2,1)} %get-tuple-element.44), calls=%async_computation.1 | async-start | bytes 1572864 | tf_op jit(solution)/shard_map/all_to_all | solution.py:661
  23.8 2.0 %collective-permute-start = (bf16[16,128,128]{2,1,0:T(8,128)(2,1)S(1)}, bf16[16,128,128]{2,1,0:T(8,128)(2,1)S(1)}, u32[]{:S(2)}, u32[]{:S(2)}) collective-permute-start(bf16[16,128,128]{2,1,0:T(8,128)(2,1)S(1)} %all-to-all-done.refs_1_.refs_5_), channel_id=1, source_target_pairs={{0,1},{1,0},{2,3},{3,2},{4,5},{5,4},{6,7},{7,6},{8,9},{9,8},{10,11... | collective-permute-start | bytes 1572872 | tf_op jit(solution)/shard_map/ppermute | solution.py:629
  26.7 12.1 %collective-permute-start.1 = (bf16[256,512]{1,0:T(8,128)(2,1)S(1)}, bf16[256,512]{1,0:T(8,128)(2,1)S(1)}, u32[]{:S(2)}, u32[]{:S(2)}) collective-permute-start(bf16[256,512]{1,0:T(8,128)(2,1)S(1)} %get-tuple-element.46), channel_id=1, source_target_pairs={{0,16},{8,24},{16,0},{24,8},{1,17},{9,25},{17,1},{25,9},{2,18},{10... | collective-permute-start | bytes 786440 | tf_op jit(solution)/shard_map/ppermute | solution.py:629
  42.8 2.3 %collective-permute-start.2 = (bf16[16,192,128]{2,1,0:T(8,128)(2,1)S(1)}, bf16[16,192,128]{2,1,0:T(8,128)(2,1)S(1)}, u32[]{:S(2)}, u32[]{:S(2)}) collective-permute-start(bf16[16,192,128]{2,1,0:T(8,128)(2,1)S(1)} %all-to-all-done.1.refs_1_.refs_5_), channel_id=1, source_target_pairs={{0,1},{1,0},{2,3},{3,2},{4,5},{5,4},{6,7},{7,6},{8,9},{9,8},{10,11... | collective-permute-start | bytes 2359304 | tf_op jit(solution)/shard_map/ppermute | solution.py:629
  45.9 14.9 %collective-permute-start.3 = (f32[128,512]{1,0:T(8,128)S(1)}, f32[128,512]{1,0:T(8,128)S(1)}, u32[]{:S(2)}, u32[]{:S(2)}) collective-permute-start(f32[128,512]{1,0:T(8,128)S(1)} %shard_map.113), channel_id=1, source_target_pairs={{0,16},{8,24},{16,0},{24,8},{1,17},{9,25},{17,1},{25,9},{2,18},{10... | collective-permute-start | bytes 786440 | tf_op jit(solution)/shard_map/ppermute | solution.py:629
  61.1 7.8 %collective-permute-start.4 = (bf16[128,512]{1,0:T(8,128)(2,1)S(1)}, bf16[128,512]{1,0:T(8,128)(2,1)S(1)}, u32[]{:S(2)}, u32[]{:S(2)}) collective-permute-start(bf16[128,512]{1,0:T(8,128)(2,1)S(1)} %get-tuple-element.48.refs_1_), channel_id=1, source_target_pairs={{0,16},{8,24},{16,0},{24,8},{1,17},{9,25},{17,1},{25,9},{2,18},{10... | collective-permute-start | bytes 393224 | tf_op jit(solution)/shard_map/ppermute | solution.py:629
  61.2 7.7 %collective-permute-start.5 = (bf16[128,512]{1,0:T(8,128)(2,1)S(1)}, bf16[128,512]{1,0:T(8,128)(2,1)S(1)}, u32[]{:S(2)}, u32[]{:S(2)}) collective-permute-start(bf16[128,512]{1,0:T(8,128)(2,1)S(1)} %get-tuple-element.48.refs_1_), channel_id=1, source_target_pairs={{0,1},{1,0},{2,3},{3,2},{4,5},{5,4},{6,7},{7,6},{8,9},{9,8},{10,11... | collective-permute-start | bytes 393224 | tf_op jit(solution)/shard_map/ppermute | solution.py:629
  68.8 1.3 collective-permute-start.6
  72.0 14.8 %all-to-all-start.2 = ((bf16[16,128,128]{2,1,0:T(8,128)(2,1)}), bf16[16,128,128]{2,1,0:T(8,128)(2,1)}, u32[]{:S(2)}, u32[]{:S(2)}) async-start(bf16[16,128,128]{2,1,0:T(8,128)(2,1)} %shard_map.115), calls=%async_computation.2 | async-start | bytes 1048576 | tf_op jit(solution)/shard_map/all_to_all | solution.py:661
  77.0 1.4 %collective-permute-start.7 = (bf16[128,512]{1,0:T(8,128)(2,1)S(1)}, bf16[128,512]{1,0:T(8,128)(2,1)S(1)}, u32[]{:S(2)}, u32[]{:S(2)}) collective-permute-start(bf16[128,512]{1,0:T(8,128)(2,1)S(1)} %get-tuple-element.53.refs_1_), channel_id=1, source_target_pairs={{0,1},{1,0},{2,3},{3,2},{4,5},{5,4},{6,7},{7,6},{8,9},{9,8},{10,11... | collective-permute-start | bytes 393224 | tf_op jit(solution)/shard_map/ppermute | solution.py:629
  86.8 15.5 %all-to-all-start.3 = ((bf16[16,160,128]{2,1,0:T(8,128)(2,1)}), bf16[16,160,128]{2,1,0:T(8,128)(2,1)S(1)}, u32[]{:S(2)}, u32[]{:S(2)}) async-start(bf16[16,160,128]{2,1,0:T(8,128)(2,1)} %shard_map.117), calls=%async_computation.3 | async-start | bytes 1310720 | tf_op jit(solution)/shard_map/all_to_all | solution.py:661
  105.0 1.7 %collective-permute-start.9 = (bf16[4,32,1280]{2,1,0:T(8,128)(2,1)S(1)}, bf16[4,32,1280]{2,1,0:T(8,128)(2,1)S(1)}, u32[]{:S(2)}, u32[]{:S(2)}) collective-permute-start(bf16[4,32,1280]{2,1,0:T(8,128)(2,1)S(1)} %get-tuple-element.63), channel_id=1, source_target_pairs={{0,1},{1,0},{2,3},{3,2},{4,5},{5,4},{6,7},{7,6},{8,9},{9,8},{10,11... | collective-permute-start | bytes 983048 | tf_op jit(solution)/shard_map/ppermute | solution.py:629
  107.3 5.1 %collective-permute-start.10 = (bf16[32,1280]{1,0:T(8,128)(2,1)S(1)}, bf16[32,1280]{1,0:T(8,128)(2,1)S(1)}, u32[]{:S(2)}, u32[]{:S(2)}) collective-permute-start(bf16[32,1280]{1,0:T(8,128)(2,1)S(1)} %get-tuple-element.64), channel_id=1, source_target_pairs={{0,2},{1,3},{2,0},{3,1},{4,6},{5,7},{6,4},{7,5},{8,10},{9,11},{10,... | collective-permute-start | bytes 245768 | tf_op jit(solution)/shard_map/ppermute | solution.py:629
  107.4 5.4 %collective-permute-start.11 = (bf16[32,1280]{1,0:T(8,128)(2,1)S(1)}, bf16[32,1280]{1,0:T(8,128)(2,1)S(1)}, u32[]{:S(2)}, u32[]{:S(2)}) collective-permute-start(bf16[32,1280]{1,0:T(8,128)(2,1)S(1)} %get-tuple-element.65), channel_id=1, source_target_pairs={{0,4},{1,5},{2,6},{3,7},{4,0},{5,1},{6,2},{7,3},{8,12},{9,13},{10,... | collective-permute-start | bytes 245768 | tf_op jit(solution)/shard_map/ppermute | solution.py:629
  108.4 5.3 %collective-permute-start.12 = (bf16[32,1280]{1,0:T(8,128)(2,1)S(1)}, bf16[32,1280]{1,0:T(8,128)(2,1)S(1)}, u32[]{:S(2)}, u32[]{:S(2)}) collective-permute-start(bf16[32,1280]{1,0:T(8,128)(2,1)S(1)} %get-tuple-element.66), channel_id=1, source_target_pairs={{0,6},{1,7},{2,4},{3,5},{4,2},{5,3},{6,0},{7,1},{8,14},{9,15},{10,... | collective-permute-start | bytes 245768 | tf_op jit(solution)/shard_map/ppermute | solution.py:629
  113.8 4.6 %collective-permute-start.13 = (bf16[32,1408]{1,0:T(8,128)(2,1)S(1)}, bf16[32,1408]{1,0:T(8,128)(2,1)S(1)}, u32[]{:S(2)}, u32[]{:S(2)}) collective-permute-start(bf16[32,1408]{1,0:T(8,128)(2,1)S(1)} %shard_map.123), channel_id=1, source_target_pairs={{0,8},{8,0},{16,24},{24,16},{1,9},{9,1},{17,25},{25,17},{2,10},{10... | collective-permute-start | bytes 270344 | tf_op jit(solution)/shard_map/ppermute | solution.py:629
  118.4 5.5 %collective-permute-start.14 = (bf16[32,1408]{1,0:T(8,128)(2,1)S(1)}, bf16[32,1408]{1,0:T(8,128)(2,1)S(1)}, u32[]{:S(2)}, u32[]{:S(2)}) collective-permute-start(bf16[32,1408]{1,0:T(8,128)(2,1)S(1)} %add_convert_fusion.1), channel_id=1, source_target_pairs={{0,16},{8,24},{16,0},{24,8},{1,17},{9,25},{17,1},{25,9},{2,18},{10... | collective-permute-start | bytes 270344 | tf_op jit(solution)/shard_map/ppermute | solution.py:629
  123.9 4.6 %collective-permute-start.16 = (bf16[32,1408]{1,0:T(8,128)(2,1)S(1)}, bf16[32,1408]{1,0:T(8,128)(2,1)S(1)}, u32[]{:S(2)}, u32[]{:S(2)}) collective-permute-start(bf16[32,1408]{1,0:T(8,128)(2,1)S(1)} %add_convert_fusion.refs_1_), channel_id=1, source_target_pairs={{0,2},{1,3},{2,0},{3,1},{4,6},{5,7},{6,4},{7,5},{8,10},{9,11},{10,... | collective-permute-start | bytes 270344 | tf_op jit(solution)/shard_map/ppermute | solution.py:629
  125.7 5.7 %collective-permute-start.18 = (bf16[32,1408]{1,0:T(8,128)(2,1)S(1)}, bf16[32,1408]{1,0:T(8,128)(2,1)S(1)}, u32[]{:S(2)}, u32[]{:S(2)}) collective-permute-start(bf16[32,1408]{1,0:T(8,128)(2,1)S(1)} %add_convert_fusion.refs_1_), channel_id=1, source_target_pairs={{0,4},{1,5},{2,6},{3,7},{4,0},{5,1},{6,2},{7,3},{8,12},{9,13},{10,... | collective-permute-start | bytes 270344 | tf_op jit(solution)/shard_map/ppermute | solution.py:629
  128.5 4.8 %collective-permute-start.20 = (bf16[32,1408]{1,0:T(8,128)(2,1)S(1)}, bf16[32,1408]{1,0:T(8,128)(2,1)S(1)}, u32[]{:S(2)}, u32[]{:S(2)}) collective-permute-start(bf16[32,1408]{1,0:T(8,128)(2,1)S(1)} %collective-permute-done.16.refs_3_), channel_id=1, source_target_pairs={{0,4},{1,5},{2,6},{3,7},{4,0},{5,1},{6,2},{7,3},{8,12},{9,13},{10,... | collective-permute-start | bytes 270344 | tf_op jit(solution)/shard_map/ppermute | solution.py:629
  130.8 2.5 %collective-permute-start.15 = (bf16[32,1408]{1,0:T(8,128)(2,1)S(1)}, bf16[32,1408]{1,0:T(8,128)(2,1)S(1)}, u32[]{:S(2)}, u32[]{:S(2)}) collective-permute-start(bf16[32,1408]{1,0:T(8,128)(2,1)S(1)} %add_convert_fusion.refs_1_), channel_id=1, source_target_pairs={{0,1},{1,0},{2,3},{3,2},{4,5},{5,4},{6,7},{7,6},{8,9},{9,8},{10,11... | collective-permute-start | bytes 270344 | tf_op jit(solution)/shard_map/ppermute | solution.py:629
  130.8 2.5 %collective-permute-start.17 = (bf16[32,1408]{1,0:T(8,128)(2,1)S(1)}, bf16[32,1408]{1,0:T(8,128)(2,1)S(1)}, u32[]{:S(2)}, u32[]{:S(2)}) collective-permute-start(bf16[32,1408]{1,0:T(8,128)(2,1)S(1)} %collective-permute-done.16.refs_3_), channel_id=1, source_target_pairs={{0,1},{1,0},{2,3},{3,2},{4,5},{5,4},{6,7},{7,6},{8,9},{9,8},{10,11... | collective-permute-start | bytes 270344 | tf_op jit(solution)/shard_map/ppermute | solution.py:629
  131.4 2.0 %collective-permute-start.19 = (bf16[32,1408]{1,0:T(8,128)(2,1)S(1)}, bf16[32,1408]{1,0:T(8,128)(2,1)S(1)}, u32[]{:S(2)}, u32[]{:S(2)}) collective-permute-start(bf16[32,1408]{1,0:T(8,128)(2,1)S(1)} %collective-permute-done.18.refs_5_), channel_id=1, source_target_pairs={{0,1},{1,0},{2,3},{3,2},{4,5},{5,4},{6,7},{7,6},{8,9},{9,8},{10,11... | collective-permute-start | bytes 270344 | tf_op jit(solution)/shard_map/ppermute | solution.py:629
  (12 other events, 149.6 us)

commit v25 on v20

--- a/solution.py
+++ b/solution.py
@@ -224,9 +224,10 @@
     return 1.0 / (1.0 + jnp.exp(-logits))
 
 
-def value_kernel(x_ref, grad_ref, wc_ref, wo_ref, out_ref):
+def value_kernel(arrive, x_ref, grad_ref, wc_ref, wo_ref, out_ref):
     residues, width = x_ref.shape[1], x_ref.shape[2]
     normed = normalized(x_ref)[0].astype(jnp.bfloat16)
+    arrive()
     values = f32_dot(normed, wc_ref[:, 2 * width : 3 * width])
     gate = gate_of(f32_dot(normed, wc_ref[:, 3 * width :]))
     grad_gated = f32_dot(grad_ref[...].reshape(-1, width), wo_ref[...], NT)
@@ -482,20 +483,24 @@
     heads, part = share_ref.shape[0], pair_ref.shape[0] // 2
     share_ref[...] = share_of(blocks_ref, blocks_ref.shape[1] - part, part, heads)
 
+    columns, channels = pair_ref.shape[1], pair_ref.shape[2]
+    step_rows = 16
+
     def rows(step, carry):
         total, shift = carry
-        for k in range(8):
-            i = step * 8 + k
-            scaled = share_ref[:, i, :] * spread_ref[pl.ds(i, 1), :]
-            high, low = two_terms(scaled)
-            total += f32_dot(jnp.concatenate([high, low], axis=0), pair_ref[i])
+        start = pl.multiple_of(step * step_rows, step_rows)
+        left = []
+        for k in range(step_rows):
+            i = start + k
+            high, low = two_terms(share_ref[:, i, :] * spread_ref[pl.ds(i, 1), :])
+            left.append(jnp.concatenate([high, low], axis=0))
             shift += (high.astype(jnp.float32) + low.astype(jnp.float32)) * mean_ref[pl.ds(i, 1), :]
-        return total, shift
-
-    channels = pair_ref.shape[2]
+        entries = pair_ref[pl.ds(start, step_rows)].reshape(step_rows * columns, channels)
+        return total + f32_dot(jnp.concatenate(left, axis=1), entries), shift
+
     total, shift = lax.fori_loop(
         0,
-        pair_ref.shape[0] // 8,
+        pair_ref.shape[0] // step_rows,
         rows,
         (jnp.zeros((2 * heads, channels), jnp.float32), jnp.zeros((heads, LANES), jnp.float32)),
     )
@@ -664,7 +669,7 @@
     x, grad, wc, wo = alignment_rows, updated_gradient, combined_weight, output_weight
     (value_blocks,) = call(
         value_kernel, [((group, 2 * residues, LANES), bf16)], x, grad, wc, wo,
-        flops=8 * tokens * width * width, outside=4,
+        flops=8 * tokens * width * width, outside=4, late=3,
     )
     value_blocks = across(value_blocks)
     query_blocks, bias, mean, spread = call(

time: 136 us -> 135 us (level)
  no operation moved by 1% of the time
where the time goes in v25:
time: 135 us; the launch traced here: 134 us
  waiting for transfers between devices  73.1 us (54%)
  starting transfers between devices  31.2 us (23%)
  Pallas kernels  29.2 us (22%)
    ppermute x22, waiting for transfers between devices, swapped(): lax.ppermute(mine, axis_name, [(a, a ^ distance) for a in range(size)])  50.6 us
    pallas_call x16, Pallas kernels, call(): pl.pallas_call(wrapped, out_shape=shapes, in_specs=[pl.BlockSpec(memory_s...  29.2 us
    all_to_all x4, waiting for transfers between devices, across(): lax.all_to_all(blocks, ('seq', 'res'), 0, 0, axis_index_groups=groups, ti...  22.5 us
    all_to_all x4, starting transfers between devices, across(): lax.all_to_all(blocks, ('seq', 'res'), 0, 0, axis_index_groups=groups, ti...  17.8 us
    ppermute x22, starting transfers between devices, swapped(): lax.ppermute(mine, axis_name, [(a, a ^ distance) for a in range(size)])  13.4 us
  transfers between devices with their start and end apart: 26, of which 22 were waited for; matrix products, arithmetic and copies ran while one was open for 0% of the time, Pallas kernels for 14%

profile of v25, /device:TPU:0, one launch (start us, length us, event | category | flops | bytes accessed | tf_op | source)
XLA Modules:
  0.0 134.5 jit_solution(8968455733590572922)
XLA Ops:
  0.6 2.6 %shard_map.109 = bf16[16,128,128]{2,1,0:T(8,128)(2,1)} custom-call(bf16[8,64,256]{2,1,0:T(8,128)(2,1)} %refs_0_.7, bf16[8,64,256]{2,1,0:T(8,128)(2,1)} %refs_1_.8, bf16[256,1024]{1,0:T(8,128)(2,1)} %refs_1_.10, bf16[256,256]{1,0:T(8,128)(2,1)} %refs_3_.3), custom_call_target="tpu_custom_call" | custom-call | flops 268435456 | bytes 1703936 | tf_op jit(solution)/shard_map/pallas_call | solution.py:618
  3.2 6.3 %all-to-all-start = ((bf16[16,128,128]{2,1,0:T(8,128)(2,1)}), bf16[16,128,128]{2,1,0:T(8,128)(2,1)S(1)}, u32[]{:S(2)}, u32[]{:S(2)}) async-start(bf16[16,128,128]{2,1,0:T(8,128)(2,1)} %shard_map.109), calls=%async_computation | async-start | bytes 1048576 | tf_op jit(solution)/shard_map/all_to_all | solution.py:667
  9.5 6.1 %shard_map.110 = (bf16[16,192,128]{2,1,0:T(8,128)(2,1)}, f32[8,64,128]{2,1,0:T(8,128)}, f32[64,128]{1,0:T(8,128)}, f32[64,128]{1,0:T(8,128)}) custom-call(bf16[8,64,256]{2,1,0:T(8,128)(2,1)} %refs_0_.7, bf16[256,1024]{1,0:T(8,128)(2,1)} %refs_1_.10, bf16[64,128,128]{2,1,0:T(8,128)(2,1)} %refs_1_.11, f32[8,128]{1,0:T(8,128)} %bitcast.5), custom_call_target="tpu_custom_call" | custom-call | flops 268435456 | bytes 4001792 | tf_op jit(solution)/shard_map/pallas_call | solution.py:618
  15.7 4.4 %all-to-all-done.refs_1_.refs_5_ = bf16[16,128,128]{2,1,0:T(8,128)(2,1)S(1)} async-done(((bf16[16,128,128]{2,1,0:T(8,128)(2,1)}), bf16[16,128,128]{2,1,0:T(8,128)(2,1)S(1)}, u32[]{:S(2)}, u32[]{:S(2)}) %all-to-all-start) | async-done | bytes 524320 | tf_op jit(solution)/shard_map/all_to_all | solution.py:667
  20.1 3.6 %all-to-all-start.1 = ((bf16[16,192,128]{2,1,0:T(8,128)(2,1)}), bf16[16,192,128]{2,1,0:T(8,128)(2,1)S(1)}, u32[]{:S(2)}, u32[]{:S(2)}) async-start(bf16[16,192,128]{2,1,0:T(8,128)(2,1)} %get-tuple-element.46), calls=%async_computation.1 | async-start | bytes 1572864 | tf_op jit(solution)/shard_map/all_to_all | solution.py:667
  26.6 2.7 %collective-permute-start.1 = (bf16[256,512]{1,0:T(8,128)(2,1)S(1)}, bf16[256,512]{1,0:T(8,128)(2,1)S(1)}, u32[]{:S(2)}, u32[]{:S(2)}) collective-permute-start(bf16[256,512]{1,0:T(8,128)(2,1)S(1)} %get-tuple-element.48), channel_id=1, source_target_pairs={{0,16},{8,24},{16,0},{24,8},{1,17},{9,25},{17,1},{25,9},{2,18},{10... | collective-permute-start | bytes 786440 | tf_op jit(solution)/shard_map/ppermute | solution.py:635
  29.2 9.5 %collective-permute-done.1.refs_4_ = bf16[256,512]{1,0:T(8,128)(2,1)S(1)} collective-permute-done((bf16[256,512]{1,0:T(8,128)(2,1)S(1)}, bf16[256,512]{1,0:T(8,128)(2,1)S(1)}, u32[]{:S(2)}, u32[]{:S(2)}) %collective-permute-start.1) | collective-permute-done | bytes 262176 | tf_op jit(solution)/shard_map/ppermute | solution.py:635
  38.7 4.0 %all-to-all-done.1.refs_1_.refs_5_ = bf16[16,192,128]{2,1,0:T(8,128)(2,1)S(1)} async-done(((bf16[16,192,128]{2,1,0:T(8,128)(2,1)}), bf16[16,192,128]{2,1,0:T(8,128)(2,1)S(1)}, u32[]{:S(2)}, u32[]{:S(2)}) %all-to-all-start.1) | async-done | bytes 786464 | tf_op jit(solution)/shard_map/all_to_all | solution.py:667
  42.6 2.3 %collective-permute-done.2.refs_2_ = bf16[16,192,128]{2,1,0:T(8,128)(2,1)S(1)} collective-permute-done((bf16[16,192,128]{2,1,0:T(8,128)(2,1)S(1)}, bf16[16,192,128]{2,1,0:T(8,128)(2,1)S(1)}, u32[]{:S(2)}, u32[]{:S(2)}) %collective-permute-start.2) | collective-permute-done | bytes 786464 | tf_op jit(solution)/shard_map/ppermute | solution.py:635
  46.0 14.9 %collective-permute-done.3.refs_1_ = f32[128,512]{1,0:T(8,128)S(1)} collective-permute-done((f32[128,512]{1,0:T(8,128)S(1)}, f32[128,512]{1,0:T(8,128)S(1)}, u32[]{:S(2)}, u32[]{:S(2)}) %collective-permute-start.3) | collective-permute-done | bytes 262176 | tf_op jit(solution)/shard_map/ppermute | solution.py:635
  61.3 7.6 %collective-permute-done.4.refs_2_ = bf16[128,512]{1,0:T(8,128)(2,1)S(1)} collective-permute-done((bf16[128,512]{1,0:T(8,128)(2,1)S(1)}, bf16[128,512]{1,0:T(8,128)(2,1)S(1)}, u32[]{:S(2)}, u32[]{:S(2)}) %collective-permute-start.4) | collective-permute-done | bytes 131104 | tf_op jit(solution)/shard_map/ppermute | solution.py:635
  70.2 1.8 %shard_map.114 = bf16[16,128,128]{2,1,0:T(8,128)(2,1)} custom-call(s32[3]{0:T(128)S(1)} %pad_add_fusion.refs_0_, bf16[128,512]{1,0:T(8,128)(2,1)S(1)} %get-tuple-element.52.refs_1_, bf16[128,512]{1,0:T(8,128)(2,1)S(1)} %collective-permute-done.4.refs_2_, bf16[128,512]{1,0:T(8,128)(2,1)S(1)} %collective-permute-done.5.refs_3_, ...), custom_call_target="tpu_custom_call" | custom-call | flops 268435456 | bytes 1572864 | tf_op jit(solution)/shard_map/pallas_call | solution.py:618
  72.0 4.2 %all-to-all-start.2 = ((bf16[16,128,128]{2,1,0:T(8,128)(2,1)}), bf16[16,128,128]{2,1,0:T(8,128)(2,1)}, u32[]{:S(2)}, u32[]{:S(2)}) async-start(bf16[16,128,128]{2,1,0:T(8,128)(2,1)} %shard_map.114), calls=%async_computation.2 | async-start | bytes 1048576 | tf_op jit(solution)/shard_map/all_to_all | solution.py:667
  78.6 1.9 %shard_map.116 = bf16[16,160,128]{2,1,0:T(8,128)(2,1)} custom-call(s32[3]{0:T(128)S(1)} %pad_add_fusion.refs_0_, bf16[128,512]{1,0:T(8,128)(2,1)S(1)} %get-tuple-element.57.refs_1_, bf16[128,512]{1,0:T(8,128)(2,1)S(1)} %get-tuple-element.58.refs_2_, bf16[128,512]{1,0:T(8,128)(2,1)S(1)} %collective-permute-done.7.refs_3_, ...), custom_call_target="tpu_custom_call" | custom-call | flops 268435456 | bytes 1966080 | tf_op jit(solution)/shard_map/pallas_call | solution.py:618
  80.5 6.3 %all-to-all-done.2.refs_4_ = bf16[16,128,128]{2,1,0:T(8,128)(2,1)} async-done(((bf16[16,128,128]{2,1,0:T(8,128)(2,1)}), bf16[16,128,128]{2,1,0:T(8,128)(2,1)}, u32[]{:S(2)}, u32[]{:S(2)}) %all-to-all-start.2) | async-done | bytes 524320 | tf_op jit(solution)/shard_map/all_to_all | solution.py:667
  86.8 3.6 %all-to-all-start.3 = ((bf16[16,160,128]{2,1,0:T(8,128)(2,1)}), bf16[16,160,128]{2,1,0:T(8,128)(2,1)S(1)}, u32[]{:S(2)}, u32[]{:S(2)}) async-start(bf16[16,160,128]{2,1,0:T(8,128)(2,1)} %shard_map.116), calls=%async_computation.3 | async-start | bytes 1310720 | tf_op jit(solution)/shard_map/all_to_all | solution.py:667
  90.5 4.1 %shard_map.117 = (bf16[8,64,256]{2,1,0:T(8,128)(2,1)}, bf16[512,512]{1,0:T(8,128)(2,1)}, bf16[512,256]{1,0:T(8,128)(2,1)}, bf16[256,768]{1,0:T(8,128)(2,1)}) custom-call(bf16[8,64,256]{2,1,0:T(8,128)(2,1)} %refs_0_.7, bf16[8,64,256]{2,1,0:T(8,128)(2,1)} %refs_1_.8, bf16[256,1024]{1,0:T(8,128)(2,1)} %refs_1_.10, bf16[256,256]{1,0:T(8,128)(2,1)} %refs_3_.3, ...), custom_call_target="tpu_custom_call" | custom-call | flops 469762048 | bytes 3145728 | tf_op jit(solution)/shard_map/pallas_call | solution.py:618
  94.6 7.8 %all-to-all-done.3.refs_0_.refs_3_ = bf16[16,160,128]{2,1,0:T(8,128)(2,1)S(1)} async-done(((bf16[16,160,128]{2,1,0:T(8,128)(2,1)}), bf16[16,160,128]{2,1,0:T(8,128)(2,1)S(1)}, u32[]{:S(2)}, u32[]{:S(2)}) %all-to-all-start.3) | async-done | bytes 655392 | tf_op jit(solution)/shard_map/all_to_all | solution.py:667
  107.8 2.5 %collective-permute-start.12 = (bf16[32,1280]{1,0:T(8,128)(2,1)S(1)}, bf16[32,1280]{1,0:T(8,128)(2,1)S(1)}, u32[]{:S(2)}, u32[]{:S(2)}) collective-permute-start(bf16[32,1280]{1,0:T(8,128)(2,1)S(1)} %get-tuple-element.70), channel_id=1, source_target_pairs={{0,6},{1,7},{2,4},{3,5},{4,2},{5,3},{6,0},{7,1},{8,14},{9,15},{10,... | collective-permute-start | bytes 245768 | tf_op jit(solution)/shard_map/ppermute | solution.py:635
  114.3 3.5 %collective-permute-done.13 = bf16[32,1408]{1,0:T(8,128)(2,1)S(1)} collective-permute-done((bf16[32,1408]{1,0:T(8,128)(2,1)S(1)}, bf16[32,1408]{1,0:T(8,128)(2,1)S(1)}, u32[]{:S(2)}, u32[]{:S(2)}) %collective-permute-start.13) | collective-permute-done | bytes 90144 | tf_op jit(solution)/shard_map/ppermute | solution.py:635
  118.1 4.3 %shard_map.123 = bf16[64,128,128]{2,1,0:T(8,128)(2,1)} custom-call(bf16[16,160,128]{2,1,0:T(8,128)(2,1)S(1)} %all-to-all-done.3.refs_0_.refs_3_, bf16[64,128,128]{2,1,0:T(8,128)(2,1)S(1)} %copy-done, f32[8,128]{1,0:T(8,128)S(1)} %bitcast.6, f32[8,64,128]{2,1,0:T(8,128)S(1)} %copy-done.5, f32[64,128]{1,0:T(8,128)S(1)} %copy-done.7, f32[64,128]{1,0:T(8,128)S(1)} %copy-done.8), custom_call_target="tpu_custom_call" | custom-call | flops 268435456 | bytes 5181440 | tf_op jit(solution)/shard_map/pallas_call | solution.py:618
  123.4 3.5 %collective-permute-start.20 = (bf16[32,1408]{1,0:T(8,128)(2,1)S(1)}, bf16[32,1408]{1,0:T(8,128)(2,1)S(1)}, u32[]{:S(2)}, u32[]{:S(2)}) collective-permute-start(bf16[32,1408]{1,0:T(8,128)(2,1)S(1)} %add_convert_fusion.refs_1_), channel_id=1, source_target_pairs={{0,6},{1,7},{2,4},{3,5},{4,2},{5,3},{6,0},{7,1},{8,14},{9,15},{10,... | collective-permute-start | bytes 270344 | tf_op jit(solution)/shard_map/ppermute | solution.py:635
  127.5 1.9 %collective-permute-done.20.refs_7_ = bf16[32,1408]{1,0:T(8,128)(2,1)S(1)} collective-permute-done((bf16[32,1408]{1,0:T(8,128)(2,1)S(1)}, bf16[32,1408]{1,0:T(8,128)(2,1)S(1)}, u32[]{:S(2)}, u32[]{:S(2)}) %collective-permute-start.20) | collective-permute-done | bytes 90144 | tf_op jit(solution)/shard_map/ppermute | solution.py:635
  129.4 2.0 %collective-permute-done.18.refs_5_ = bf16[32,1408]{1,0:T(8,128)(2,1)S(1)} collective-permute-done((bf16[32,1408]{1,0:T(8,128)(2,1)S(1)}, bf16[32,1408]{1,0:T(8,128)(2,1)S(1)}, u32[]{:S(2)}, u32[]{:S(2)}) %collective-permute-start.18) | collective-permute-done | bytes 90144 | tf_op jit(solution)/shard_map/ppermute | solution.py:635
  (67 shorter events, 22.2 us)
Async XLA Ops:
  3.2 16.9 %all-to-all-start = ((bf16[16,128,128]{2,1,0:T(8,128)(2,1)}), bf16[16,128,128]{2,1,0:T(8,128)(2,1)S(1)}, u32[]{:S(2)}, u32[]{:S(2)}) async-start(bf16[16,128,128]{2,1,0:T(8,128)(2,1)} %shard_map.109), calls=%async_computation | async-start | bytes 1048576 | tf_op jit(solution)/shard_map/all_to_all | solution.py:667
  20.1 22.6 %all-to-all-start.1 = ((bf16[16,192,128]{2,1,0:T(8,128)(2,1)}), bf16[16,192,128]{2,1,0:T(8,128)(2,1)S(1)}, u32[]{:S(2)}, u32[]{:S(2)}) async-start(bf16[16,192,128]{2,1,0:T(8,128)(2,1)} %get-tuple-element.46), calls=%async_computation.1 | async-start | bytes 1572864 | tf_op jit(solution)/shard_map/all_to_all | solution.py:667
  23.7 2.0 %collective-permute-start = (bf16[16,128,128]{2,1,0:T(8,128)(2,1)S(1)}, bf16[16,128,128]{2,1,0:T(8,128)(2,1)S(1)}, u32[]{:S(2)}, u32[]{:S(2)}) collective-permute-start(bf16[16,128,128]{2,1,0:T(8,128)(2,1)S(1)} %all-to-all-done.refs_1_.refs_5_), channel_id=1, source_target_pairs={{0,1},{1,0},{2,3},{3,2},{4,5},{5,4},{6,7},{7,6},{8,9},{9,8},{10,11... | collective-permute-start | bytes 1572872 | tf_op jit(solution)/shard_map/ppermute | solution.py:635
  26.6 12.1 %collective-permute-start.1 = (bf16[256,512]{1,0:T(8,128)(2,1)S(1)}, bf16[256,512]{1,0:T(8,128)(2,1)S(1)}, u32[]{:S(2)}, u32[]{:S(2)}) collective-permute-start(bf16[256,512]{1,0:T(8,128)(2,1)S(1)} %get-tuple-element.48), channel_id=1, source_target_pairs={{0,16},{8,24},{16,0},{24,8},{1,17},{9,25},{17,1},{25,9},{2,18},{10... | collective-permute-start | bytes 786440 | tf_op jit(solution)/shard_map/ppermute | solution.py:635
  42.6 2.3 %collective-permute-start.2 = (bf16[16,192,128]{2,1,0:T(8,128)(2,1)S(1)}, bf16[16,192,128]{2,1,0:T(8,128)(2,1)S(1)}, u32[]{:S(2)}, u32[]{:S(2)}) collective-permute-start(bf16[16,192,128]{2,1,0:T(8,128)(2,1)S(1)} %all-to-all-done.1.refs_1_.refs_5_), channel_id=1, source_target_pairs={{0,1},{1,0},{2,3},{3,2},{4,5},{5,4},{6,7},{7,6},{8,9},{9,8},{10,11... | collective-permute-start | bytes 2359304 | tf_op jit(solution)/shard_map/ppermute | solution.py:635
  46.0 14.9 %collective-permute-start.3 = (f32[128,512]{1,0:T(8,128)S(1)}, f32[128,512]{1,0:T(8,128)S(1)}, u32[]{:S(2)}, u32[]{:S(2)}) collective-permute-start(f32[128,512]{1,0:T(8,128)S(1)} %get-tuple-element.51), channel_id=1, source_target_pairs={{0,16},{8,24},{16,0},{24,8},{1,17},{9,25},{17,1},{25,9},{2,18},{10... | collective-permute-start | bytes 786440 | tf_op jit(solution)/shard_map/ppermute | solution.py:635
  61.1 7.8 %collective-permute-start.4 = (bf16[128,512]{1,0:T(8,128)(2,1)S(1)}, bf16[128,512]{1,0:T(8,128)(2,1)S(1)}, u32[]{:S(2)}, u32[]{:S(2)}) collective-permute-start(bf16[128,512]{1,0:T(8,128)(2,1)S(1)} %get-tuple-element.52.refs_1_), channel_id=1, source_target_pairs={{0,16},{8,24},{16,0},{24,8},{1,17},{9,25},{17,1},{25,9},{2,18},{10... | collective-permute-start | bytes 393224 | tf_op jit(solution)/shard_map/ppermute | solution.py:635
  61.2 7.7 %collective-permute-start.5 = (bf16[128,512]{1,0:T(8,128)(2,1)S(1)}, bf16[128,512]{1,0:T(8,128)(2,1)S(1)}, u32[]{:S(2)}, u32[]{:S(2)}) collective-permute-start(bf16[128,512]{1,0:T(8,128)(2,1)S(1)} %get-tuple-element.52.refs_1_), channel_id=1, source_target_pairs={{0,1},{1,0},{2,3},{3,2},{4,5},{5,4},{6,7},{7,6},{8,9},{9,8},{10,11... | collective-permute-start | bytes 393224 | tf_op jit(solution)/shard_map/ppermute | solution.py:635
  68.9 1.3 %collective-permute-start.6 = (bf16[128,512]{1,0:T(8,128)(2,1)S(1)}, bf16[128,512]{1,0:T(8,128)(2,1)S(1)}, u32[]{:S(2)}, u32[]{:S(2)}) collective-permute-start(bf16[128,512]{1,0:T(8,128)(2,1)S(1)} %collective-permute-done.4.refs_2_), channel_id=1, source_target_pairs={{0,1},{1,0},{2,3},{3,2},{4,5},{5,4},{6,7},{7,6},{8,9},{9,8},{10,11... | collective-permute-start | bytes 393224 | tf_op jit(solution)/shard_map/ppermute | solution.py:635
  72.0 14.8 %all-to-all-start.2 = ((bf16[16,128,128]{2,1,0:T(8,128)(2,1)}), bf16[16,128,128]{2,1,0:T(8,128)(2,1)}, u32[]{:S(2)}, u32[]{:S(2)}) async-start(bf16[16,128,128]{2,1,0:T(8,128)(2,1)} %shard_map.114), calls=%async_computation.2 | async-start | bytes 1048576 | tf_op jit(solution)/shard_map/all_to_all | solution.py:667
  77.0 1.4 %collective-permute-start.7 = (bf16[128,512]{1,0:T(8,128)(2,1)S(1)}, bf16[128,512]{1,0:T(8,128)(2,1)S(1)}, u32[]{:S(2)}, u32[]{:S(2)}) collective-permute-start(bf16[128,512]{1,0:T(8,128)(2,1)S(1)} %get-tuple-element.57.refs_1_), channel_id=1, source_target_pairs={{0,1},{1,0},{2,3},{3,2},{4,5},{5,4},{6,7},{7,6},{8,9},{9,8},{10,11... | collective-permute-start | bytes 393224 | tf_op jit(solution)/shard_map/ppermute | solution.py:635
  86.8 15.5 %all-to-all-start.3 = ((bf16[16,160,128]{2,1,0:T(8,128)(2,1)}), bf16[16,160,128]{2,1,0:T(8,128)(2,1)S(1)}, u32[]{:S(2)}, u32[]{:S(2)}) async-start(bf16[16,160,128]{2,1,0:T(8,128)(2,1)} %shard_map.116), calls=%async_computation.3 | async-start | bytes 1310720 | tf_op jit(solution)/shard_map/all_to_all | solution.py:667
  104.4 1.7 %collective-permute-start.9 = (bf16[4,32,1280]{2,1,0:T(8,128)(2,1)S(1)}, bf16[4,32,1280]{2,1,0:T(8,128)(2,1)S(1)}, u32[]{:S(2)}, u32[]{:S(2)}) collective-permute-start(bf16[4,32,1280]{2,1,0:T(8,128)(2,1)S(1)} %get-tuple-element.67), channel_id=1, source_target_pairs={{0,1},{1,0},{2,3},{3,2},{4,5},{5,4},{6,7},{7,6},{8,9},{9,8},{10,11... | collective-permute-start | bytes 983048 | tf_op jit(solution)/shard_map/ppermute | solution.py:635
  106.8 5.1 %collective-permute-start.10 = (bf16[32,1280]{1,0:T(8,128)(2,1)S(1)}, bf16[32,1280]{1,0:T(8,128)(2,1)S(1)}, u32[]{:S(2)}, u32[]{:S(2)}) collective-permute-start(bf16[32,1280]{1,0:T(8,128)(2,1)S(1)} %get-tuple-element.68), channel_id=1, source_target_pairs={{0,2},{1,3},{2,0},{3,1},{4,6},{5,7},{6,4},{7,5},{8,10},{9,11},{10,... | collective-permute-start | bytes 245768 | tf_op jit(solution)/shard_map/ppermute | solution.py:635
  106.8 5.4 %collective-permute-start.11 = (bf16[32,1280]{1,0:T(8,128)(2,1)S(1)}, bf16[32,1280]{1,0:T(8,128)(2,1)S(1)}, u32[]{:S(2)}, u32[]{:S(2)}) collective-permute-start(bf16[32,1280]{1,0:T(8,128)(2,1)S(1)} %get-tuple-element.69), channel_id=1, source_target_pairs={{0,4},{1,5},{2,6},{3,7},{4,0},{5,1},{6,2},{7,3},{8,12},{9,13},{10,... | collective-permute-start | bytes 245768 | tf_op jit(solution)/shard_map/ppermute | solution.py:635
  107.8 5.3 %collective-permute-start.12 = (bf16[32,1280]{1,0:T(8,128)(2,1)S(1)}, bf16[32,1280]{1,0:T(8,128)(2,1)S(1)}, u32[]{:S(2)}, u32[]{:S(2)}) collective-permute-start(bf16[32,1280]{1,0:T(8,128)(2,1)S(1)} %get-tuple-element.70), channel_id=1, source_target_pairs={{0,6},{1,7},{2,4},{3,5},{4,2},{5,3},{6,0},{7,1},{8,14},{9,15},{10,... | collective-permute-start | bytes 245768 | tf_op jit(solution)/shard_map/ppermute | solution.py:635
  113.2 4.6 %collective-permute-start.13 = (bf16[32,1408]{1,0:T(8,128)(2,1)S(1)}, bf16[32,1408]{1,0:T(8,128)(2,1)S(1)}, u32[]{:S(2)}, u32[]{:S(2)}) collective-permute-start(bf16[32,1408]{1,0:T(8,128)(2,1)S(1)} %shard_map.122), channel_id=1, source_target_pairs={{0,8},{8,0},{16,24},{24,16},{1,9},{9,1},{17,25},{25,17},{2,10},{10... | collective-permute-start | bytes 270344 | tf_op jit(solution)/shard_map/ppermute | solution.py:635
  117.8 5.5 %collective-permute-start.14 = (bf16[32,1408]{1,0:T(8,128)(2,1)S(1)}, bf16[32,1408]{1,0:T(8,128)(2,1)S(1)}, u32[]{:S(2)}, u32[]{:S(2)}) collective-permute-start(bf16[32,1408]{1,0:T(8,128)(2,1)S(1)} %add_convert_fusion.1), channel_id=1, source_target_pairs={{0,16},{8,24},{16,0},{24,8},{1,17},{9,25},{17,1},{25,9},{2,18},{10... | collective-permute-start | bytes 270344 | tf_op jit(solution)/shard_map/ppermute | solution.py:635
  123.4 6.0 %collective-permute-start.20 = (bf16[32,1408]{1,0:T(8,128)(2,1)S(1)}, bf16[32,1408]{1,0:T(8,128)(2,1)S(1)}, u32[]{:S(2)}, u32[]{:S(2)}) collective-permute-start(bf16[32,1408]{1,0:T(8,128)(2,1)S(1)} %add_convert_fusion.refs_1_), channel_id=1, source_target_pairs={{0,6},{1,7},{2,4},{3,5},{4,2},{5,3},{6,0},{7,1},{8,14},{9,15},{10,... | collective-permute-start | bytes 270344 | tf_op jit(solution)/shard_map/ppermute | solution.py:635
  126.9 4.5 %collective-permute-start.18 = (bf16[32,1408]{1,0:T(8,128)(2,1)S(1)}, bf16[32,1408]{1,0:T(8,128)(2,1)S(1)}, u32[]{:S(2)}, u32[]{:S(2)}) collective-permute-start(bf16[32,1408]{1,0:T(8,128)(2,1)S(1)} %add_convert_fusion.refs_1_), channel_id=1, source_target_pairs={{0,4},{1,5},{2,6},{3,7},{4,0},{5,1},{6,2},{7,3},{8,12},{9,13},{10,... | collective-permute-start | bytes 270344 | tf_op jit(solution)/shard_map/ppermute | solution.py:635
  126.9 4.5 %collective-permute-start.16 = (bf16[32,1408]{1,0:T(8,128)(2,1)S(1)}, bf16[32,1408]{1,0:T(8,128)(2,1)S(1)}, u32[]{:S(2)}, u32[]{:S(2)}) collective-permute-start(bf16[32,1408]{1,0:T(8,128)(2,1)S(1)} %add_convert_fusion.refs_1_), channel_id=1, source_target_pairs={{0,2},{1,3},{2,0},{3,1},{4,6},{5,7},{6,4},{7,5},{8,10},{9,11},{10,... | collective-permute-start | bytes 270344 | tf_op jit(solution)/shard_map/ppermute | solution.py:635
  127.5 4.4 %collective-permute-start.15 = (bf16[32,1408]{1,0:T(8,128)(2,1)S(1)}, bf16[32,1408]{1,0:T(8,128)(2,1)S(1)}, u32[]{:S(2)}, u32[]{:S(2)}) collective-permute-start(bf16[32,1408]{1,0:T(8,128)(2,1)S(1)} %add_convert_fusion.refs_1_), channel_id=1, source_target_pairs={{0,1},{1,0},{2,3},{3,2},{4,5},{5,4},{6,7},{7,6},{8,9},{9,8},{10,11... | collective-permute-start | bytes 270344 | tf_op jit(solution)/shard_map/ppermute | solution.py:635
  129.4 2.5 %collective-permute-start.21 = (bf16[32,1408]{1,0:T(8,128)(2,1)S(1)}, bf16[32,1408]{1,0:T(8,128)(2,1)S(1)}, u32[]{:S(2)}, u32[]{:S(2)}) collective-permute-start(bf16[32,1408]{1,0:T(8,128)(2,1)S(1)} %collective-permute-done.20.refs_7_), channel_id=1, source_target_pairs={{0,1},{1,0},{2,3},{3,2},{4,5},{5,4},{6,7},{7,6},{8,9},{9,8},{10,11... | collective-permute-start | bytes 270344 | tf_op jit(solution)/shard_map/ppermute | solution.py:635
  131.4 1.4 %collective-permute-start.17 = (bf16[32,1408]{1,0:T(8,128)(2,1)S(1)}, bf16[32,1408]{1,0:T(8,128)(2,1)S(1)}, u32[]{:S(2)}, u32[]{:S(2)}) collective-permute-start(bf16[32,1408]{1,0:T(8,128)(2,1)S(1)} %collective-permute-done.16.refs_3_), channel_id=1, source_target_pairs={{0,1},{1,0},{2,3},{3,2},{4,5},{5,4},{6,7},{7,6},{8,9},{9,8},{10,11... | collective-permute-start | bytes 270344 | tf_op jit(solution)/shard_map/ppermute | solution.py:635
  (12 other events, 146.7 us)

commit v26 on v24

--- a/solution.py
+++ b/solution.py
@@ -224,9 +224,10 @@
     return 1.0 / (1.0 + jnp.exp(-logits))
 
 
-def value_kernel(x_ref, grad_ref, wc_ref, wo_ref, out_ref):
+def value_kernel(arrive, x_ref, grad_ref, wc_ref, wo_ref, out_ref):
     residues, width = x_ref.shape[1], x_ref.shape[2]
     normed = normalized(x_ref)[0].astype(jnp.bfloat16)
+    arrive()
     values = f32_dot(normed, wc_ref[:, 2 * width : 3 * width])
     gate = gate_of(f32_dot(normed, wc_ref[:, 3 * width :]))
     grad_gated = f32_dot(grad_ref[...].reshape(-1, width), wo_ref[...], NT)
@@ -481,20 +482,24 @@
     heads, part = share_ref.shape[0], pair_ref.shape[0] // 2
     share_ref[...] = share_of(blocks_ref, blocks_ref.shape[1] - part, part, heads)
 
+    columns, channels = pair_ref.shape[1], pair_ref.shape[2]
+    step_rows = 16
+
     def rows(step, carry):
         total, shift = carry
-        for k in range(8):
-            i = step * 8 + k
-            scaled = share_ref[:, i, :] * spread_ref[pl.ds(i, 1), :]
-            high, low = two_terms(scaled)
-            total += f32_dot(jnp.concatenate([high, low], axis=0), pair_ref[i])
+        start = pl.multiple_of(step * step_rows, step_rows)
+        left = []
+        for k in range(step_rows):
+            i = start + k
+            high, low = two_terms(share_ref[:, i, :] * spread_ref[pl.ds(i, 1), :])
+            left.append(jnp.concatenate([high, low], axis=0))
             shift += (high.astype(jnp.float32) + low.astype(jnp.float32)) * mean_ref[pl.ds(i, 1), :]
-        return total, shift
-
-    channels = pair_ref.shape[2]
+        entries = pair_ref[pl.ds(start, step_rows)].reshape(step_rows * columns, channels)
+        return total + f32_dot(jnp.concatenate(left, axis=1), entries), shift
+
     total, shift = lax.fori_loop(
         0,
-        pair_ref.shape[0] // 8,
+        pair_ref.shape[0] // step_rows,
         rows,
         (jnp.zeros((2 * heads, channels), jnp.float32), jnp.zeros((heads, LANES), jnp.float32)),
     )
@@ -663,7 +668,7 @@
     x, grad, wc, wo = alignment_rows, updated_gradient, combined_weight, output_weight
     (value_blocks,) = call(
         value_kernel, [((group, 2 * residues, LANES), bf16)], x, grad, wc, wo,
-        flops=8 * tokens * width * width, outside=4,
+        flops=8 * tokens * width * width, outside=4, late=3,
     )
     value_blocks = across(value_blocks)
     query_blocks, bias, mean, spread = call(
@@ -786,8 +791,7 @@
     other_half = swapped(part, "seq", seq_half)
     other_half, pair_gradient = lax.optimization_barrier((other_half, pair_gradient))
     part = added(part, other_half)
-    beside = swapped(part, "res", 2)
-    chips = [part, beside, swapped(part, "res", 4), swapped(beside, "res", 4)]
+    chips = [part] + [swapped(part, "res", 2 * flip) for flip in range(1, res_size // 2)]
     parts = [t for chip in chips for t in (chip, swapped(chip, "res", 1))]
     combined_gradient, output_gradient, pair_weight_gradient = call(
         output_kernel,

time: 137 us -> 135 us (0.985)
  starting transfers between devices: 33.4 us -> 31.2 us
    ppermute x22, starting transfers between devices: 15.7 us -> 13.4 us  [swapped(): lax.ppermute(mine, axis_name, [(a, a ^ distance) for a in range(size)])]
  transfers between devices with their start and end apart: 26 -> 26, of which waited for: 21 -> 22; matrix products, arithmetic and copies ran while one was open for 0% -> 0% of each run, Pallas kernels for 15% -> 15%
where the time goes in v26:
time: 135 us; the launch traced here: 134 us
  waiting for transfers between devices  72.2 us (53%)
  starting transfers between devices  31.2 us (23%)
  Pallas kernels  29.9 us (22%)
    ppermute x22, waiting for transfers between devices, swapped(): lax.ppermute(mine, axis_name, [(a, a ^ distance) for a in range(size)])  49.7 us
    pallas_call x17, Pallas kernels, call(): pl.pallas_call(wrapped, out_shape=shapes, in_specs=[pl.BlockSpec(memory_s...  29.9 us
    all_to_all x4, waiting for transfers between devices, across(): lax.all_to_all(blocks, ('seq', 'res'), 0, 0, axis_index_groups=groups, ti...  22.5 us
    all_to_all x4, starting transfers between devices, across(): lax.all_to_all(blocks, ('seq', 'res'), 0, 0, axis_index_groups=groups, ti...  17.7 us
    ppermute x22, starting transfers between devices, swapped(): lax.ppermute(mine, axis_name, [(a, a ^ distance) for a in range(size)])  13.4 us
  transfers between devices with their start and end apart: 26, of which 22 were waited for; matrix products, arithmetic and copies ran while one was open for 0% of the time, Pallas kernels for 15%

profile of v26, /device:TPU:0, one launch (start us, length us, event | category | flops | bytes accessed | tf_op | source)
XLA Modules:
  0.0 134.3 jit_solution(8289380878214071744)
XLA Ops:
  0.6 2.6 %shard_map.109 = bf16[16,128,128]{2,1,0:T(8,128)(2,1)} custom-call(bf16[8,64,256]{2,1,0:T(8,128)(2,1)} %refs_0_.7, bf16[8,64,256]{2,1,0:T(8,128)(2,1)} %refs_1_.8, bf16[256,1024]{1,0:T(8,128)(2,1)} %refs_1_.10, bf16[256,256]{1,0:T(8,128)(2,1)} %refs_3_.3), custom_call_target="tpu_custom_call" | custom-call | flops 268435456 | bytes 1703936 | tf_op jit(solution)/shard_map/pallas_call | solution.py:617
  3.2 6.3 %all-to-all-start = ((bf16[16,128,128]{2,1,0:T(8,128)(2,1)}), bf16[16,128,128]{2,1,0:T(8,128)(2,1)S(1)}, u32[]{:S(2)}, u32[]{:S(2)}) async-start(bf16[16,128,128]{2,1,0:T(8,128)(2,1)} %shard_map.109), calls=%async_computation | async-start | bytes 1048576 | tf_op jit(solution)/shard_map/all_to_all | solution.py:666
  9.5 6.1 %shard_map.110 = (bf16[16,192,128]{2,1,0:T(8,128)(2,1)}, f32[8,64,128]{2,1,0:T(8,128)}, f32[64,128]{1,0:T(8,128)}, f32[64,128]{1,0:T(8,128)}) custom-call(bf16[8,64,256]{2,1,0:T(8,128)(2,1)} %refs_0_.7, bf16[256,1024]{1,0:T(8,128)(2,1)} %refs_1_.10, bf16[64,128,128]{2,1,0:T(8,128)(2,1)} %refs_1_.11, f32[8,128]{1,0:T(8,128)} %bitcast.5), custom_call_target="tpu_custom_call" | custom-call | flops 268435456 | bytes 4001792 | tf_op jit(solution)/shard_map/pallas_call | solution.py:617
  15.7 4.4 %all-to-all-done.refs_1_.refs_5_ = bf16[16,128,128]{2,1,0:T(8,128)(2,1)S(1)} async-done(((bf16[16,128,128]{2,1,0:T(8,128)(2,1)}), bf16[16,128,128]{2,1,0:T(8,128)(2,1)S(1)}, u32[]{:S(2)}, u32[]{:S(2)}) %all-to-all-start) | async-done | bytes 524320 | tf_op jit(solution)/shard_map/all_to_all | solution.py:666
  20.1 3.6 %all-to-all-start.1 = ((bf16[16,192,128]{2,1,0:T(8,128)(2,1)}), bf16[16,192,128]{2,1,0:T(8,128)(2,1)S(1)}, u32[]{:S(2)}, u32[]{:S(2)}) async-start(bf16[16,192,128]{2,1,0:T(8,128)(2,1)} %get-tuple-element.44), calls=%async_computation.1 | async-start | bytes 1572864 | tf_op jit(solution)/shard_map/all_to_all | solution.py:666
  26.6 2.7 %collective-permute-start.1 = (bf16[256,512]{1,0:T(8,128)(2,1)S(1)}, bf16[256,512]{1,0:T(8,128)(2,1)S(1)}, u32[]{:S(2)}, u32[]{:S(2)}) collective-permute-start(bf16[256,512]{1,0:T(8,128)(2,1)S(1)} %get-tuple-element.46), channel_id=1, source_target_pairs={{0,16},{8,24},{16,0},{24,8},{1,17},{9,25},{17,1},{25,9},{2,18},{10... | collective-permute-start | bytes 786440 | tf_op jit(solution)/shard_map/ppermute | solution.py:634
  29.2 9.5 %collective-permute-done.1.refs_4_ = bf16[256,512]{1,0:T(8,128)(2,1)S(1)} collective-permute-done((bf16[256,512]{1,0:T(8,128)(2,1)S(1)}, bf16[256,512]{1,0:T(8,128)(2,1)S(1)}, u32[]{:S(2)}, u32[]{:S(2)}) %collective-permute-start.1) | collective-permute-done | bytes 262176 | tf_op jit(solution)/shard_map/ppermute | solution.py:634
  38.7 4.0 %all-to-all-done.1.refs_1_.refs_5_ = bf16[16,192,128]{2,1,0:T(8,128)(2,1)S(1)} async-done(((bf16[16,192,128]{2,1,0:T(8,128)(2,1)}), bf16[16,192,128]{2,1,0:T(8,128)(2,1)S(1)}, u32[]{:S(2)}, u32[]{:S(2)}) %all-to-all-start.1) | async-done | bytes 786464 | tf_op jit(solution)/shard_map/all_to_all | solution.py:666
  42.6 2.3 %collective-permute-done.2.refs_2_ = bf16[16,192,128]{2,1,0:T(8,128)(2,1)S(1)} collective-permute-done((bf16[16,192,128]{2,1,0:T(8,128)(2,1)S(1)}, bf16[16,192,128]{2,1,0:T(8,128)(2,1)S(1)}, u32[]{:S(2)}, u32[]{:S(2)}) %collective-permute-start.2) | collective-permute-done | bytes 786464 | tf_op jit(solution)/shard_map/ppermute | solution.py:634
  46.8 14.0 %collective-permute-done.3.refs_1_ = f32[128,512]{1,0:T(8,128)S(1)} collective-permute-done((f32[128,512]{1,0:T(8,128)S(1)}, f32[128,512]{1,0:T(8,128)S(1)}, u32[]{:S(2)}, u32[]{:S(2)}) %collective-permute-start.3) | collective-permute-done | bytes 262176 | tf_op jit(solution)/shard_map/ppermute | solution.py:634
  61.1 7.6 %collective-permute-done.4.refs_2_ = bf16[128,512]{1,0:T(8,128)(2,1)S(1)} collective-permute-done((bf16[128,512]{1,0:T(8,128)(2,1)S(1)}, bf16[128,512]{1,0:T(8,128)(2,1)S(1)}, u32[]{:S(2)}, u32[]{:S(2)}) %collective-permute-start.4) | collective-permute-done | bytes 131104 | tf_op jit(solution)/shard_map/ppermute | solution.py:634
  70.0 1.8 %shard_map.115 = bf16[16,128,128]{2,1,0:T(8,128)(2,1)} custom-call(s32[3]{0:T(128)S(1)} %pad_add_fusion.refs_0_, bf16[128,512]{1,0:T(8,128)(2,1)S(1)} %get-tuple-element.48.refs_1_, bf16[128,512]{1,0:T(8,128)(2,1)S(1)} %collective-permute-done.4.refs_2_, bf16[128,512]{1,0:T(8,128)(2,1)S(1)} %collective-permute-done.5.refs_3_, ...), custom_call_target="tpu_custom_call" | custom-call | flops 268435456 | bytes 1572864 | tf_op jit(solution)/shard_map/pallas_call | solution.py:617
  71.9 4.2 %all-to-all-start.2 = ((bf16[16,128,128]{2,1,0:T(8,128)(2,1)}), bf16[16,128,128]{2,1,0:T(8,128)(2,1)}, u32[]{:S(2)}, u32[]{:S(2)}) async-start(bf16[16,128,128]{2,1,0:T(8,128)(2,1)} %shard_map.115), calls=%async_computation.2 | async-start | bytes 1048576 | tf_op jit(solution)/shard_map/all_to_all | solution.py:666
  78.5 1.9 %shard_map.117 = bf16[16,160,128]{2,1,0:T(8,128)(2,1)} custom-call(s32[3]{0:T(128)S(1)} %pad_add_fusion.refs_0_, bf16[128,512]{1,0:T(8,128)(2,1)S(1)} %get-tuple-element.53.refs_1_, bf16[128,512]{1,0:T(8,128)(2,1)S(1)} %get-tuple-element.54.refs_2_, bf16[128,512]{1,0:T(8,128)(2,1)S(1)} %collective-permute-done.7.refs_3_, ...), custom_call_target="tpu_custom_call" | custom-call | flops 268435456 | bytes 1966080 | tf_op jit(solution)/shard_map/pallas_call | solution.py:617
  80.4 6.3 %all-to-all-done.2.refs_4_ = bf16[16,128,128]{2,1,0:T(8,128)(2,1)} async-done(((bf16[16,128,128]{2,1,0:T(8,128)(2,1)}), bf16[16,128,128]{2,1,0:T(8,128)(2,1)}, u32[]{:S(2)}, u32[]{:S(2)}) %all-to-all-start.2) | async-done | bytes 524320 | tf_op jit(solution)/shard_map/all_to_all | solution.py:666
  86.7 3.6 %all-to-all-start.3 = ((bf16[16,160,128]{2,1,0:T(8,128)(2,1)}), bf16[16,160,128]{2,1,0:T(8,128)(2,1)S(1)}, u32[]{:S(2)}, u32[]{:S(2)}) async-start(bf16[16,160,128]{2,1,0:T(8,128)(2,1)} %shard_map.117), calls=%async_computation.3 | async-start | bytes 1310720 | tf_op jit(solution)/shard_map/all_to_all | solution.py:666
  90.3 4.1 %shard_map.118 = (bf16[8,64,256]{2,1,0:T(8,128)(2,1)}, bf16[512,512]{1,0:T(8,128)(2,1)}, bf16[512,256]{1,0:T(8,128)(2,1)}, bf16[256,768]{1,0:T(8,128)(2,1)}) custom-call(bf16[8,64,256]{2,1,0:T(8,128)(2,1)} %refs_0_.7, bf16[8,64,256]{2,1,0:T(8,128)(2,1)} %refs_1_.8, bf16[256,1024]{1,0:T(8,128)(2,1)} %refs_1_.10, bf16[256,256]{1,0:T(8,128)(2,1)} %refs_3_.3, ...), custom_call_target="tpu_custom_call" | custom-call | flops 469762048 | bytes 3145728 | tf_op jit(solution)/shard_map/pallas_call | solution.py:617
  94.4 7.8 %all-to-all-done.3.refs_0_.refs_3_ = bf16[16,160,128]{2,1,0:T(8,128)(2,1)S(1)} async-done(((bf16[16,160,128]{2,1,0:T(8,128)(2,1)}), bf16[16,160,128]{2,1,0:T(8,128)(2,1)S(1)}, u32[]{:S(2)}, u32[]{:S(2)}) %all-to-all-start.3) | async-done | bytes 655392 | tf_op jit(solution)/shard_map/all_to_all | solution.py:666
  107.6 2.5 %collective-permute-start.12 = (bf16[32,1280]{1,0:T(8,128)(2,1)S(1)}, bf16[32,1280]{1,0:T(8,128)(2,1)S(1)}, u32[]{:S(2)}, u32[]{:S(2)}) collective-permute-start(bf16[32,1280]{1,0:T(8,128)(2,1)S(1)} %get-tuple-element.66), channel_id=1, source_target_pairs={{0,6},{1,7},{2,4},{3,5},{4,2},{5,3},{6,0},{7,1},{8,14},{9,15},{10,... | collective-permute-start | bytes 245768 | tf_op jit(solution)/shard_map/ppermute | solution.py:634
  114.1 3.5 %collective-permute-done.13 = bf16[32,1408]{1,0:T(8,128)(2,1)S(1)} collective-permute-done((bf16[32,1408]{1,0:T(8,128)(2,1)S(1)}, bf16[32,1408]{1,0:T(8,128)(2,1)S(1)}, u32[]{:S(2)}, u32[]{:S(2)}) %collective-permute-start.13) | collective-permute-done | bytes 90144 | tf_op jit(solution)/shard_map/ppermute | solution.py:634
  118.0 4.3 %shard_map.124 = bf16[64,128,128]{2,1,0:T(8,128)(2,1)} custom-call(bf16[16,160,128]{2,1,0:T(8,128)(2,1)S(1)} %all-to-all-done.3.refs_0_.refs_3_, bf16[64,128,128]{2,1,0:T(8,128)(2,1)S(1)} %copy-done, f32[8,128]{1,0:T(8,128)S(1)} %bitcast.6, f32[8,64,128]{2,1,0:T(8,128)S(1)} %copy-done.5, f32[64,128]{1,0:T(8,128)S(1)} %copy-done.7, f32[64,128]{1,0:T(8,128)S(1)} %copy-done.8), custom_call_target="tpu_custom_call" | custom-call | flops 268435456 | bytes 5181440 | tf_op jit(solution)/shard_map/pallas_call | solution.py:617
  123.2 3.5 %collective-permute-start.20 = (bf16[32,1408]{1,0:T(8,128)(2,1)S(1)}, bf16[32,1408]{1,0:T(8,128)(2,1)S(1)}, u32[]{:S(2)}, u32[]{:S(2)}) collective-permute-start(bf16[32,1408]{1,0:T(8,128)(2,1)S(1)} %add_convert_fusion.refs_1_), channel_id=1, source_target_pairs={{0,6},{1,7},{2,4},{3,5},{4,2},{5,3},{6,0},{7,1},{8,14},{9,15},{10,... | collective-permute-start | bytes 270344 | tf_op jit(solution)/shard_map/ppermute | solution.py:634
  127.4 1.9 %collective-permute-done.20.refs_7_ = bf16[32,1408]{1,0:T(8,128)(2,1)S(1)} collective-permute-done((bf16[32,1408]{1,0:T(8,128)(2,1)S(1)}, bf16[32,1408]{1,0:T(8,128)(2,1)S(1)}, u32[]{:S(2)}, u32[]{:S(2)}) %collective-permute-start.20) | collective-permute-done | bytes 90144 | tf_op jit(solution)/shard_map/ppermute | solution.py:634
  129.2 2.0 %collective-permute-done.18.refs_5_ = bf16[32,1408]{1,0:T(8,128)(2,1)S(1)} collective-permute-done((bf16[32,1408]{1,0:T(8,128)(2,1)S(1)}, bf16[32,1408]{1,0:T(8,128)(2,1)S(1)}, u32[]{:S(2)}, u32[]{:S(2)}) %collective-permute-start.18) | collective-permute-done | bytes 90144 | tf_op jit(solution)/shard_map/ppermute | solution.py:634
  (68 shorter events, 22.9 us)
Async XLA Ops:
  3.2 16.9 %all-to-all-start = ((bf16[16,128,128]{2,1,0:T(8,128)(2,1)}), bf16[16,128,128]{2,1,0:T(8,128)(2,1)S(1)}, u32[]{:S(2)}, u32[]{:S(2)}) async-start(bf16[16,128,128]{2,1,0:T(8,128)(2,1)} %shard_map.109), calls=%async_computation | async-start | bytes 1048576 | tf_op jit(solution)/shard_map/all_to_all | solution.py:666
  20.1 22.6 %all-to-all-start.1 = ((bf16[16,192,128]{2,1,0:T(8,128)(2,1)}), bf16[16,192,128]{2,1,0:T(8,128)(2,1)S(1)}, u32[]{:S(2)}, u32[]{:S(2)}) async-start(bf16[16,192,128]{2,1,0:T(8,128)(2,1)} %get-tuple-element.44), calls=%async_computation.1 | async-start | bytes 1572864 | tf_op jit(solution)/shard_map/all_to_all | solution.py:666
  23.7 2.0 %collective-permute-start = (bf16[16,128,128]{2,1,0:T(8,128)(2,1)S(1)}, bf16[16,128,128]{2,1,0:T(8,128)(2,1)S(1)}, u32[]{:S(2)}, u32[]{:S(2)}) collective-permute-start(bf16[16,128,128]{2,1,0:T(8,128)(2,1)S(1)} %all-to-all-done.refs_1_.refs_5_), channel_id=1, source_target_pairs={{0,1},{1,0},{2,3},{3,2},{4,5},{5,4},{6,7},{7,6},{8,9},{9,8},{10,11... | collective-permute-start | bytes 1572872 | tf_op jit(solution)/shard_map/ppermute | solution.py:634
  26.6 12.1 %collective-permute-start.1 = (bf16[256,512]{1,0:T(8,128)(2,1)S(1)}, bf16[256,512]{1,0:T(8,128)(2,1)S(1)}, u32[]{:S(2)}, u32[]{:S(2)}) collective-permute-start(bf16[256,512]{1,0:T(8,128)(2,1)S(1)} %get-tuple-element.46), channel_id=1, source_target_pairs={{0,16},{8,24},{16,0},{24,8},{1,17},{9,25},{17,1},{25,9},{2,18},{10... | collective-permute-start | bytes 786440 | tf_op jit(solution)/shard_map/ppermute | solution.py:634
  42.6 2.3 %collective-permute-start.2 = (bf16[16,192,128]{2,1,0:T(8,128)(2,1)S(1)}, bf16[16,192,128]{2,1,0:T(8,128)(2,1)S(1)}, u32[]{:S(2)}, u32[]{:S(2)}) collective-permute-start(bf16[16,192,128]{2,1,0:T(8,128)(2,1)S(1)} %all-to-all-done.1.refs_1_.refs_5_), channel_id=1, source_target_pairs={{0,1},{1,0},{2,3},{3,2},{4,5},{5,4},{6,7},{7,6},{8,9},{9,8},{10,11... | collective-permute-start | bytes 2359304 | tf_op jit(solution)/shard_map/ppermute | solution.py:634
  45.8 14.9 %collective-permute-start.3 = (f32[128,512]{1,0:T(8,128)S(1)}, f32[128,512]{1,0:T(8,128)S(1)}, u32[]{:S(2)}, u32[]{:S(2)}) collective-permute-start(f32[128,512]{1,0:T(8,128)S(1)} %shard_map.113), channel_id=1, source_target_pairs={{0,16},{8,24},{16,0},{24,8},{1,17},{9,25},{17,1},{25,9},{2,18},{10... | collective-permute-start | bytes 786440 | tf_op jit(solution)/shard_map/ppermute | solution.py:634
  60.9 7.8 %collective-permute-start.4 = (bf16[128,512]{1,0:T(8,128)(2,1)S(1)}, bf16[128,512]{1,0:T(8,128)(2,1)S(1)}, u32[]{:S(2)}, u32[]{:S(2)}) collective-permute-start(bf16[128,512]{1,0:T(8,128)(2,1)S(1)} %get-tuple-element.48.refs_1_), channel_id=1, source_target_pairs={{0,16},{8,24},{16,0},{24,8},{1,17},{9,25},{17,1},{25,9},{2,18},{10... | collective-permute-start | bytes 393224 | tf_op jit(solution)/shard_map/ppermute | solution.py:634
  61.0 7.7 %collective-permute-start.5 = (bf16[128,512]{1,0:T(8,128)(2,1)S(1)}, bf16[128,512]{1,0:T(8,128)(2,1)S(1)}, u32[]{:S(2)}, u32[]{:S(2)}) collective-permute-start(bf16[128,512]{1,0:T(8,128)(2,1)S(1)} %get-tuple-element.48.refs_1_), channel_id=1, source_target_pairs={{0,1},{1,0},{2,3},{3,2},{4,5},{5,4},{6,7},{7,6},{8,9},{9,8},{10,11... | collective-permute-start | bytes 393224 | tf_op jit(solution)/shard_map/ppermute | solution.py:634
  68.7 1.3 %collective-permute-start.6 = (bf16[128,512]{1,0:T(8,128)(2,1)S(1)}, bf16[128,512]{1,0:T(8,128)(2,1)S(1)}, u32[]{:S(2)}, u32[]{:S(2)}) collective-permute-start(bf16[128,512]{1,0:T(8,128)(2,1)S(1)} %collective-permute-done.4.refs_2_), channel_id=1, source_target_pairs={{0,1},{1,0},{2,3},{3,2},{4,5},{5,4},{6,7},{7,6},{8,9},{9,8},{10,11... | collective-permute-start | bytes 393224 | tf_op jit(solution)/shard_map/ppermute | solution.py:634
  71.9 14.8 %all-to-all-start.2 = ((bf16[16,128,128]{2,1,0:T(8,128)(2,1)}), bf16[16,128,128]{2,1,0:T(8,128)(2,1)}, u32[]{:S(2)}, u32[]{:S(2)}) async-start(bf16[16,128,128]{2,1,0:T(8,128)(2,1)} %shard_map.115), calls=%async_computation.2 | async-start | bytes 1048576 | tf_op jit(solution)/shard_map/all_to_all | solution.py:666
  76.8 1.4 %collective-permute-start.7 = (bf16[128,512]{1,0:T(8,128)(2,1)S(1)}, bf16[128,512]{1,0:T(8,128)(2,1)S(1)}, u32[]{:S(2)}, u32[]{:S(2)}) collective-permute-start(bf16[128,512]{1,0:T(8,128)(2,1)S(1)} %get-tuple-element.53.refs_1_), channel_id=1, source_target_pairs={{0,1},{1,0},{2,3},{3,2},{4,5},{5,4},{6,7},{7,6},{8,9},{9,8},{10,11... | collective-permute-start | bytes 393224 | tf_op jit(solution)/shard_map/ppermute | solution.py:634
  86.7 15.5 %all-to-all-start.3 = ((bf16[16,160,128]{2,1,0:T(8,128)(2,1)}), bf16[16,160,128]{2,1,0:T(8,128)(2,1)S(1)}, u32[]{:S(2)}, u32[]{:S(2)}) async-start(bf16[16,160,128]{2,1,0:T(8,128)(2,1)} %shard_map.117), calls=%async_computation.3 | async-start | bytes 1310720 | tf_op jit(solution)/shard_map/all_to_all | solution.py:666
  104.3 1.7 %collective-permute-start.9 = (bf16[4,32,1280]{2,1,0:T(8,128)(2,1)S(1)}, bf16[4,32,1280]{2,1,0:T(8,128)(2,1)S(1)}, u32[]{:S(2)}, u32[]{:S(2)}) collective-permute-start(bf16[4,32,1280]{2,1,0:T(8,128)(2,1)S(1)} %get-tuple-element.63), channel_id=1, source_target_pairs={{0,1},{1,0},{2,3},{3,2},{4,5},{5,4},{6,7},{7,6},{8,9},{9,8},{10,11... | collective-permute-start | bytes 983048 | tf_op jit(solution)/shard_map/ppermute | solution.py:634
  106.6 5.1 %collective-permute-start.10 = (bf16[32,1280]{1,0:T(8,128)(2,1)S(1)}, bf16[32,1280]{1,0:T(8,128)(2,1)S(1)}, u32[]{:S(2)}, u32[]{:S(2)}) collective-permute-start(bf16[32,1280]{1,0:T(8,128)(2,1)S(1)} %get-tuple-element.64), channel_id=1, source_target_pairs={{0,2},{1,3},{2,0},{3,1},{4,6},{5,7},{6,4},{7,5},{8,10},{9,11},{10,... | collective-permute-start | bytes 245768 | tf_op jit(solution)/shard_map/ppermute | solution.py:634
  106.7 5.4 %collective-permute-start.11 = (bf16[32,1280]{1,0:T(8,128)(2,1)S(1)}, bf16[32,1280]{1,0:T(8,128)(2,1)S(1)}, u32[]{:S(2)}, u32[]{:S(2)}) collective-permute-start(bf16[32,1280]{1,0:T(8,128)(2,1)S(1)} %get-tuple-element.65), channel_id=1, source_target_pairs={{0,4},{1,5},{2,6},{3,7},{4,0},{5,1},{6,2},{7,3},{8,12},{9,13},{10,... | collective-permute-start | bytes 245768 | tf_op jit(solution)/shard_map/ppermute | solution.py:634
  107.6 5.3 %collective-permute-start.12 = (bf16[32,1280]{1,0:T(8,128)(2,1)S(1)}, bf16[32,1280]{1,0:T(8,128)(2,1)S(1)}, u32[]{:S(2)}, u32[]{:S(2)}) collective-permute-start(bf16[32,1280]{1,0:T(8,128)(2,1)S(1)} %get-tuple-element.66), channel_id=1, source_target_pairs={{0,6},{1,7},{2,4},{3,5},{4,2},{5,3},{6,0},{7,1},{8,14},{9,15},{10,... | collective-permute-start | bytes 245768 | tf_op jit(solution)/shard_map/ppermute | solution.py:634
  113.0 4.6 %collective-permute-start.13 = (bf16[32,1408]{1,0:T(8,128)(2,1)S(1)}, bf16[32,1408]{1,0:T(8,128)(2,1)S(1)}, u32[]{:S(2)}, u32[]{:S(2)}) collective-permute-start(bf16[32,1408]{1,0:T(8,128)(2,1)S(1)} %shard_map.123), channel_id=1, source_target_pairs={{0,8},{8,0},{16,24},{24,16},{1,9},{9,1},{17,25},{25,17},{2,10},{10... | collective-permute-start | bytes 270344 | tf_op jit(solution)/shard_map/ppermute | solution.py:634
  117.6 5.5 %collective-permute-start.14 = (bf16[32,1408]{1,0:T(8,128)(2,1)S(1)}, bf16[32,1408]{1,0:T(8,128)(2,1)S(1)}, u32[]{:S(2)}, u32[]{:S(2)}) collective-permute-start(bf16[32,1408]{1,0:T(8,128)(2,1)S(1)} %add_convert_fusion.1), channel_id=1, source_target_pairs={{0,16},{8,24},{16,0},{24,8},{1,17},{9,25},{17,1},{25,9},{2,18},{10... | collective-permute-start | bytes 270344 | tf_op jit(solution)/shard_map/ppermute | solution.py:634
  123.2 6.0 %collective-permute-start.20 = (bf16[32,1408]{1,0:T(8,128)(2,1)S(1)}, bf16[32,1408]{1,0:T(8,128)(2,1)S(1)}, u32[]{:S(2)}, u32[]{:S(2)}) collective-permute-start(bf16[32,1408]{1,0:T(8,128)(2,1)S(1)} %add_convert_fusion.refs_1_), channel_id=1, source_target_pairs={{0,6},{1,7},{2,4},{3,5},{4,2},{5,3},{6,0},{7,1},{8,14},{9,15},{10,... | collective-permute-start | bytes 270344 | tf_op jit(solution)/shard_map/ppermute | solution.py:634
  126.7 4.5 %collective-permute-start.18 = (bf16[32,1408]{1,0:T(8,128)(2,1)S(1)}, bf16[32,1408]{1,0:T(8,128)(2,1)S(1)}, u32[]{:S(2)}, u32[]{:S(2)}) collective-permute-start(bf16[32,1408]{1,0:T(8,128)(2,1)S(1)} %add_convert_fusion.refs_1_), channel_id=1, source_target_pairs={{0,4},{1,5},{2,6},{3,7},{4,0},{5,1},{6,2},{7,3},{8,12},{9,13},{10,... | collective-permute-start | bytes 270344 | tf_op jit(solution)/shard_map/ppermute | solution.py:634
  126.7 4.5 %collective-permute-start.16 = (bf16[32,1408]{1,0:T(8,128)(2,1)S(1)}, bf16[32,1408]{1,0:T(8,128)(2,1)S(1)}, u32[]{:S(2)}, u32[]{:S(2)}) collective-permute-start(bf16[32,1408]{1,0:T(8,128)(2,1)S(1)} %add_convert_fusion.refs_1_), channel_id=1, source_target_pairs={{0,2},{1,3},{2,0},{3,1},{4,6},{5,7},{6,4},{7,5},{8,10},{9,11},{10,... | collective-permute-start | bytes 270344 | tf_op jit(solution)/shard_map/ppermute | solution.py:634
  127.3 4.4 %collective-permute-start.15 = (bf16[32,1408]{1,0:T(8,128)(2,1)S(1)}, bf16[32,1408]{1,0:T(8,128)(2,1)S(1)}, u32[]{:S(2)}, u32[]{:S(2)}) collective-permute-start(bf16[32,1408]{1,0:T(8,128)(2,1)S(1)} %add_convert_fusion.refs_1_), channel_id=1, source_target_pairs={{0,1},{1,0},{2,3},{3,2},{4,5},{5,4},{6,7},{7,6},{8,9},{9,8},{10,11... | collective-permute-start | bytes 270344 | tf_op jit(solution)/shard_map/ppermute | solution.py:634
  129.2 2.5 %collective-permute-start.21 = (bf16[32,1408]{1,0:T(8,128)(2,1)S(1)}, bf16[32,1408]{1,0:T(8,128)(2,1)S(1)}, u32[]{:S(2)}, u32[]{:S(2)}) collective-permute-start(bf16[32,1408]{1,0:T(8,128)(2,1)S(1)} %collective-permute-done.20.refs_7_), channel_id=1, source_target_pairs={{0,1},{1,0},{2,3},{3,2},{4,5},{5,4},{6,7},{7,6},{8,9},{9,8},{10,11... | collective-permute-start | bytes 270344 | tf_op jit(solution)/shard_map/ppermute | solution.py:634
  131.2 1.4 %collective-permute-start.17 = (bf16[32,1408]{1,0:T(8,128)(2,1)S(1)}, bf16[32,1408]{1,0:T(8,128)(2,1)S(1)}, u32[]{:S(2)}, u32[]{:S(2)}) collective-permute-start(bf16[32,1408]{1,0:T(8,128)(2,1)S(1)} %collective-permute-done.16.refs_3_), channel_id=1, source_target_pairs={{0,1},{1,0},{2,3},{3,2},{4,5},{5,4},{6,7},{7,6},{8,9},{9,8},{10,11... | collective-permute-start | bytes 270344 | tf_op jit(solution)/shard_map/ppermute | solution.py:634
  (12 other events, 146.7 us)
